TPU v7x, 32 devices: a whole 2x2x4 slice. The times are simulated.
32 devices in a mesh: dp: 8 (over z, y), tensor: 4 (over x, core).
Axes of the slice: x: 2, y: 2, z: 4, core: 2. Of those that a mesh axis runs over, the one named last changes fastest.
Arguments:
- tokens: bfloat16 [16384, 768], P('dp'), may hold values from -6 to 6
- lengths: int32 [16], P('dp'), may hold values from 256 to 1024, as said below
- span_starts: int32 [16, 64], P('dp'), may hold values from 0 to 1014, as said below
- query_weight: bfloat16 [768, 768], P(None, 'tensor'), may hold values from -0.3125 to 0.3125
- key_weight: bfloat16 [768, 768], P(None, 'tensor'), may hold values from -0.3125 to 0.3125
- value_weight: bfloat16 [768, 768], P(None, 'tensor'), may hold values from -0.21875 to 0.21875
- merge_weight: bfloat16 [768, 768], P('tensor'), may hold values from -0.75 to 0.75
- up_weight: bfloat16 [768, 3072], P(None, 'tensor'), may hold values from -0.21875 to 0.21875
- down_weight: bfloat16 [3072, 768], P('tensor'), may hold values from -0.15625 to 0.15625
- inner_gain: float32 [768], replicated, may hold values from 0.1 to 1.9
- inner_bias: float32 [768], replicated, may hold values from -3 to 3
- outer_gain: float32 [768], replicated, may hold values from 0.1 to 1.9
- outer_bias: float32 [768], replicated, may hold values from -3 to 3
- out_grad: bfloat16 [16384, 768], P('dp'), may hold values from -18 to 18
Outputs:
- layer_output: bfloat16 [16384, 768], P('dp')
- input_grad: bfloat16 [16384, 768], P('dp')
- query_grad: float32 [768, 768], P(None, 'tensor')
- key_grad: float32 [768, 768], P(None, 'tensor')
- value_grad: float32 [768, 768], P(None, 'tensor')
- merge_grad: float32 [768, 768], P('tensor')
- up_grad: float32 [768, 3072], P(None, 'tensor')
- down_grad: float32 [3072, 768], P('tensor')
- inner_gain_grad: float32 [768], replicated
- inner_bias_grad: float32 [768], replicated
- outer_gain_grad: float32 [768], replicated
- outer_bias_grad: float32 [768], replicated
Inputs may be any that keep to these rules, and one draw needn't show every extreme that they name: `lengths`: live frames of each utterance; in every draw some utterance has all 1024 and some has 256. `span_starts`: every span of 10 frames ends within its utterance's live frames; spans may intersect.
All inputs are finite; a program needn't handle non-finite values.
Results may differ from a plain program's by a relative error of at most 0.024.
The roundings to bfloat16 on the way count: a program that leaves them out, or rounds other values in their place, can miss the bound.
Values may be sent and summed in bfloat16 or wider, within the bound.
No kernel may reach another device: no remote copies, remote signals or barrier semaphores. Data moves between devices by JAX's collectives and lax.ppermute only.
A program may use at most 192 MiB of HBM per device.

v0:
```python
import functools

import jax
import jax.numpy as jnp
from jax import lax
from jax.experimental import pallas as pl
from jax.experimental.pallas import tpu as pltpu
from jax.sharding import PartitionSpec as P

HEAD_DIM = 64
SPAN = 10
EPS = 1e-05
LOG2E = 1.4426950408889634
KB = 256
VMEM = 16
RB = 128
HB = 256
BF = jnp.bfloat16
F32 = jnp.float32
MIB = 1 << 20


def nn(a, b):
    return lax.dot_general(a, b, (((1,), (0,)), ((), ())), preferred_element_type=F32)


def nt(a, b):
    return lax.dot_general(a, b, (((1,), (1,)), ((), ())), preferred_element_type=F32)


def tn(a, b):
    return lax.dot_general(a, b, (((0,), (0,)), ((), ())), preferred_element_type=F32)


def params(limit):
    return pltpu.CompilerParams(vmem_limit_bytes=limit * MIB)


def cost(flops):
    return pl.CostEstimate(flops=flops, bytes_accessed=1024, transcendentals=0)


def project_kernel(x_ref, wq_ref, wk_ref, wv_ref, q_ref, k_ref, v_ref):
    x = x_ref[...]
    for w_ref, o_ref in ((wq_ref, q_ref), (wk_ref, k_ref), (wv_ref, v_ref)):
        o_ref[:, :192] = nt(x, w_ref[...]).astype(BF)
        o_ref[:, 192:] = jnp.zeros((x.shape[0], HEAD_DIM), BF)


def project(tokens, wq, wk, wv):
    rows, d = tokens.shape
    block = 512
    return pl.pallas_call(
        project_kernel,
        grid=(rows // block,),
        in_specs=[pl.BlockSpec((block, d), lambda i: (i, 0))]
        + [pl.BlockSpec((192, d), lambda i: (0, 0))] * 3,
        out_specs=[pl.BlockSpec((block, 256), lambda i: (i, 0))] * 3,
        out_shape=[jax.ShapeDtypeStruct((rows, 256), BF)] * 3,
        compiler_params=params(VMEM),
        cost_estimate=cost(1000),
        name="project",
    )(tokens, wq, wk, wv)


def lane_parts(block):
    left = block[:, :128]
    lane = lax.broadcasted_iota(jnp.int32, left.shape, 1)
    zero = jnp.zeros_like(left)
    return (
        jnp.where(lane < HEAD_DIM, left, zero),
        jnp.where(lane >= HEAD_DIM, left, zero),
        block[:, 128:],
    )


TILE = (0, 0, 1)


def call(kernel, name, grid, meta, args, in_specs, out_specs, out_shape, scratch=(), limit=VMEM):
    return pl.pallas_call(
        kernel,
        grid_spec=pltpu.PrefetchScalarGridSpec(
            num_scalar_prefetch=1,
            grid=grid,
            in_specs=in_specs,
            out_specs=out_specs,
            scratch_shapes=scratch,
        ),
        out_shape=out_shape,
        compiler_params=params(limit),
        cost_estimate=cost(1000),
        name=name,
    )(meta, *args)


def fixed(*shape):
    return pl.BlockSpec(shape, lambda *_: (0,) * len(shape))


def like(shape, dtype):
    return jax.ShapeDtypeStruct(shape, dtype)


def forward_kernel(u, meta_ref, q_ref, k_ref, v_ref, own_ref, other_ref, o32_ref, lse_ref, s_ref):
    length = meta_ref[1 + u]
    step = pl.program_id(0)
    blocks = lax.div(length + KB - 1, KB)
    parts = lane_parts(q_ref[...] * jnp.asarray(0.125, BF))
    width = q_ref.shape[0]

    def first(kb, highest):
        start = pl.multiple_of(kb * KB, KB)
        rows = pl.ds(start, KB)
        live = start + lax.broadcasted_iota(jnp.int32, (KB, width), 0) < length
        out = []
        for h in range(3):
            tile = pl.ds(128 * TILE[h], 128)
            s = nt(k_ref[rows, tile], parts[h])
            s = jnp.where(live, s, -1e30)
            s_ref[h, rows, :] = s
            out.append(jnp.maximum(highest[h], jnp.max(s, axis=0, keepdims=True)))
        return tuple(out)

    floor = jnp.full((1, width), -1e30, F32)
    highest = lax.fori_loop(0, blocks, first, (floor,) * 3)

    def second(kb, carry):
        rows = pl.ds(pl.multiple_of(kb * KB, KB), KB)
        out = []
        for h in range(3):
            total, result = carry[h]
            p = jnp.exp2((s_ref[h, rows, :] - highest[h]) * LOG2E)
            total = total + jnp.sum(p, axis=0, keepdims=True)
            v = v_ref[rows, pl.ds(128 * TILE[h], 128)]
            result = result + tn(v, p.astype(BF))
            out.append((total, result))
        return tuple(out)

    init = ((jnp.zeros((1, width), F32), jnp.zeros((128, width), F32)),) * 3
    done = lax.fori_loop(0, blocks, second, init)
    outs = []
    for h in range(3):
        total, result = done[h]
        lo = HEAD_DIM * (h % 2)
        o = result[lo : lo + HEAD_DIM] / total
        o32_ref[0, pl.ds(h * HEAD_DIM, HEAD_DIM), :] = o
        lse_ref[0, pl.ds(h, 1), :] = highest[h] * LOG2E + jnp.log2(total)
        outs.append(o.astype(BF))
    whole = jnp.concatenate(outs, axis=0)
    for j, o_ref in enumerate((own_ref, other_ref)):

        @pl.when(step == j)
        def _():
            o_ref[...] = whole


def attend_forward(meta, q, k, v, u, frames):
    half = frames // 2
    return call(
        functools.partial(forward_kernel, u),
        "attend_forward",
        (2,),
        meta,
        (q, k, v),
        [
            pl.BlockSpec((half, 256), lambda i, m: (u * 2 + (i ^ m[0]), 0)),
            pl.BlockSpec((frames, 256), lambda i, m: (u, 0)),
            pl.BlockSpec((frames, 256), lambda i, m: (u, 0)),
        ],
        [
            fixed(192, half),
            fixed(192, half),
            pl.BlockSpec((1, 192, half), lambda i, m: (i, 0, 0)),
            pl.BlockSpec((1, 8, half), lambda i, m: (i, 0, 0)),
        ],
        [
            like((192, half), BF),
            like((192, half), BF),
            like((2, 192, half), F32),
            like((2, 8, half), F32),
        ],
        [pltpu.VMEM((3, frames, half), F32)],
    )


def backward_kernel(
    u, meta_ref, q_ref, k_ref, v_ref, d0_ref, d1_ref, o32_ref, lse_ref,
    dq_ref, dk_ref, dv_ref, kt_ref, dk_acc, dv_acc, do_ref,
):
    length = meta_ref[1 + u]
    blocks = lax.div(length + KB - 1, KB)
    step = pl.program_id(0)

    @pl.when(step == 0)
    def _():
        dk_acc[...] = jnp.zeros_like(dk_acc)
        dv_acc[...] = jnp.zeros_like(dv_acc)
        kt_ref[...] = jnp.transpose(k_ref[...])
        do_ref[...] = d0_ref[...]

    @pl.when(step == 1)
    def _():
        do_ref[...] = d1_ref[...]

    parts = lane_parts(q_ref[...] * jnp.asarray(0.125, BF))
    width = q_ref.shape[0]
    empty = jnp.zeros((HEAD_DIM, width), BF)
    head = [do_ref[pl.ds(h * HEAD_DIM, HEAD_DIM), :] for h in range(3)]
    grads = (
        jnp.concatenate([head[0], empty], axis=0),
        jnp.concatenate([empty, head[1]], axis=0),
        jnp.concatenate([head[2], empty], axis=0),
    )
    delta = [
        jnp.sum(
            head[h].astype(F32) * o32_ref[0, pl.ds(h * HEAD_DIM, HEAD_DIM), :], axis=0, keepdims=True
        )
        for h in range(3)
    ]
    lse = [lse_ref[0, pl.ds(h, 1), :] for h in range(3)]

    def body(kb, carry):
        start = pl.multiple_of(kb * KB, KB)
        rows = pl.ds(start, KB)
        live = start + lax.broadcasted_iota(jnp.int32, (KB, width), 0) < length
        out = []
        for h in range(3):
            tile = pl.ds(128 * TILE[h], 128)
            s = nt(k_ref[rows, tile], parts[h])
            s = jnp.where(live, s, -1e30)
            p = jnp.exp2(s * LOG2E - lse[h])
            dp = nn(v_ref[rows, tile], grads[h])
            ds = (p * (dp - delta[h])).astype(BF)
            dv_acc[rows, tile] += nt(p.astype(BF), grads[h])
            dk_acc[rows, tile] += nn(ds, parts[h])
            kt = kt_ref[pl.ds(h * HEAD_DIM, HEAD_DIM), rows]
            out.append(carry[h] + nn(kt, ds))
        return tuple(out)

    zero = jnp.zeros((HEAD_DIM, width), F32)
    done = lax.fori_loop(0, blocks, body, (zero,) * 3)
    full = jnp.concatenate(done + (zero,), axis=0) * 0.125
    dq_ref[...] = jnp.transpose(full).astype(BF)

    @pl.when(step == 1)
    def _():
        dk_ref[...] = dk_acc[...].astype(BF)
        dv_ref[...] = dv_acc[...].astype(BF)


def attend_backward(meta, q, k, v, own, other, o32, lse, u, frames):
    half = frames // 2
    return call(
        functools.partial(backward_kernel, u),
        "attend_backward",
        (2,),
        meta,
        (q, k, v, own, other, o32, lse),
        [
            pl.BlockSpec((half, 256), lambda i, m: (u * 2 + (i ^ m[0]), 0)),
            pl.BlockSpec((frames, 256), lambda i, m: (u, 0)),
            pl.BlockSpec((frames, 256), lambda i, m: (u, 0)),
            fixed(192, half),
            fixed(192, half),
            pl.BlockSpec((1, 192, half), lambda i, m: (i, 0, 0)),
            pl.BlockSpec((1, 8, half), lambda i, m: (i, 0, 0)),
        ],
        [
            pl.BlockSpec((half, 256), lambda i, m: (i ^ m[0], 0)),
            fixed(frames, 256),
            fixed(frames, 256),
        ],
        [like((frames, 256), BF)] * 3,
        [
            pltpu.VMEM((256, frames), BF),
            pltpu.VMEM((frames, 256), F32),
            pltpu.VMEM((frames, 256), F32),
            pltpu.VMEM((192, half), BF),
        ],
    )


def entry_kernel(meta_ref, x_ref, dq_ref, dk_ref, dv_ref, wq_ref, wk_ref, wv_ref, *refs):
    before_ref = refs[0] if len(refs) == 5 else None
    send_ref, keep_ref, sum_ref, acc = refs[-4:]
    step = pl.program_id(0)
    x = x_ref[...]
    total = jnp.zeros(x.shape, F32)
    for i, (g_ref, w_ref) in enumerate(((dq_ref, wq_ref), (dk_ref, wk_ref), (dv_ref, wv_ref))):
        rows = pl.ds(192 * i, 192)
        g = g_ref[:, :192]
        total = total + nn(g, w_ref[...])
        product = tn(g, x)

        @pl.when(step == 0)
        def _():
            acc[rows, :] = product if before_ref is None else product + before_ref[rows, :]

        @pl.when(step == 1)
        def _():
            sum_ref[rows, :] = (product + acc[rows, :]).astype(sum_ref.dtype)

    low = total.astype(BF)

    @pl.when(step == 0)
    def _():
        send_ref[...] = low

    @pl.when(step == 1)
    def _():
        keep_ref[...] = low


def entry_back(meta, tokens, grads, weights, before, u, frames, dtype):
    half = frames // 2
    d = tokens.shape[1]
    return call(
        entry_kernel,
        "entry_back",
        (2,),
        meta,
        (tokens, *grads, *weights, *before),
        [pl.BlockSpec((half, d), lambda i, m: (u * 2 + (1 - i ^ m[0]), 0))]
        + [pl.BlockSpec((half, 256), lambda i, m: (1 - i ^ m[0], 0))] * 3
        + [fixed(192, d)] * 3
        + [fixed(576, d)] * len(before),
        [fixed(half, d), fixed(half, d), fixed(576, d)],
        [like((half, d), BF), like((half, d), BF), like((576, d), dtype)],
        [pltpu.VMEM((576, d), F32)],
    )


def place_kernel(meta_ref, own_ref, other_ref, o_ref):
    for j, r_ref in enumerate((own_ref, other_ref)):

        @pl.when(pl.program_id(1) == j)
        def _():
            o_ref[...] = r_ref[0]


def place(meta, own, other):
    seqs, half, d = own.shape
    return call(
        place_kernel,
        "place",
        (seqs, 2),
        meta,
        (own, other),
        [pl.BlockSpec((1, half, d), lambda u, j, m: (u, 0, 0))] * 2,
        pl.BlockSpec((half, d), lambda u, j, m: (u * 2 + (j ^ m[0]), 0)),
        like((seqs * 2 * half, d), own.dtype),
    )


def normalise(values):
    average = jnp.mean(values, axis=-1, keepdims=True)
    centred = values - average
    spread = jnp.mean(centred * centred, axis=-1, keepdims=True)
    rstd = lax.rsqrt(spread + EPS)
    return centred * rstd, rstd


def gelu_pair(v):
    e = jnp.exp2(v * v * (-0.5 * LOG2E))
    t = 1.0 / (1.0 + (0.3275911 * 0.7071067811865476) * jnp.abs(v))
    poly = t * (0.5 * 0.254829592 + t * (0.5 * -0.284496736 + t * (0.5 * 1.421413741 + t * (0.5 * -1.453152027 + t * (0.5 * 1.061405429)))))
    tail = poly * e
    phi_cap = jnp.where(v >= 0, 1.0 - tail, tail)
    return v * phi_cap, phi_cap + v * (e * 0.3989422804014327)


def ahead_kernel(
    meta_ref, tok_ref, a0, a1, a2, a3, w0, w1, w2, w3, ua_ref, ub_ref, da_ref, db_ref, vec_ref,
    xhat_ref, rstd_ref, low_ref, act_ref, slope_ref, own_ref, sent_ref,
):
    gain, bias = vec_ref[0:1, :], vec_ref[1:2, :]
    hidden = ua_ref.shape[1]
    for r in range(tok_ref.shape[0] // RB):
        rows = pl.ds(r * RB, RB)
        branch = jnp.zeros((RB, tok_ref.shape[1]), F32)
        for a, w in ((a0, w0), (a1, w1), (a2, w2), (a3, w3)):
            branch = branch + tn(a[:, rows], w[...]).astype(BF).astype(F32)
        xhat, rstd = normalise(tok_ref[rows, :].astype(F32) + branch)
        xhat_ref[rows, :] = xhat
        rstd_ref[rows, :] = jnp.broadcast_to(rstd, (RB, rstd_ref.shape[1]))
        normed = xhat * gain + bias
        low = normed.astype(BF)
        low_ref[rows, :] = low
        sent = jnp.zeros(normed.shape, F32)
        for g, (up, down) in enumerate(((ua_ref, da_ref), (ub_ref, db_ref))):
            acts = []
            for c in range(hidden // HB):
                act, slope = gelu_pair(nn(low, up[:, c * HB : (c + 1) * HB]))
                columns = pl.ds(g * hidden + c * HB, HB)
                acts.append(act.astype(BF))
                act_ref[rows, columns] = acts[-1]
                slope_ref[rows, columns] = slope.astype(BF)
            sent = sent + nn(jnp.concatenate(acts, axis=1), down[...]).astype(BF).astype(F32)
        own_ref[rows, :] = normed + sent
        sent_ref[rows, :] = sent.astype(BF)


def ahead(meta, tokens, att, merge_w, up, down, vectors, u):
    half = att[0].shape[1]
    d, hidden = up[0].shape
    return call(
        ahead_kernel,
        "ahead",
        (1,),
        meta,
        (tokens, *att, *merge_w, *up, *down, vectors),
        [pl.BlockSpec((half, d), lambda i, m: (u * 2 + m[0], 0))]
        + [fixed(192, half)] * 4
        + [fixed(192, d)] * 4
        + [fixed(d, hidden)] * 2
        + [fixed(hidden, d)] * 2
        + [fixed(4, d)],
        [fixed(half, d), fixed(half, 128), fixed(half, d), fixed(half, 2 * hidden), fixed(half, 2 * hidden), fixed(half, d), fixed(half, d)],
        [
            like((half, d), F32),
            like((half, 128), F32),
            like((half, d), BF),
            like((half, 2 * hidden), BF),
            like((half, 2 * hidden), BF),
            like((half, d), F32),
            like((half, d), BF),
        ],
    )


def astern_kernel(seqs, u, meta_ref, own_ref, far_ref, grad_ref, span_ref, ua_ref, ub_ref, da_ref, db_ref, slope_ref, vec_ref, *refs):
    last = u == seqs - 1
    before = refs[: 4 * seqs - 2] if last else ()
    out_ref, g_ref, pre_ref, back_ref, sent_ref, small_ref = refs[len(before) : len(before) + 6]
    gain, bias = vec_ref[2:3, :], vec_ref[3:4, :]
    half, d = own_ref.shape
    hidden = ua_ref.shape[1]
    starts = span_ref[u : u + 1, :]
    gain_grad = jnp.zeros(gain.shape, F32)
    bias_grad = jnp.zeros(gain.shape, F32)
    for r in range(half // RB):
        rows = pl.ds(r * RB, RB)
        xhat, rstd = normalise(own_ref[rows, :] + far_ref[rows, :].astype(F32))
        out_ref[rows, :] = (xhat * gain + bias).astype(BF)
        frame = meta_ref[0] * half + r * RB + lax.broadcasted_iota(jnp.int32, (RB, starts.shape[1]), 0)
        inside = (frame >= starts) & (frame < starts + SPAN)
        weight = jnp.max(jnp.where(inside, 1.0, 0.0), axis=1, keepdims=True)
        cot = grad_ref[rows, :].astype(F32) * weight
        gain_grad = gain_grad + jnp.sum(cot * xhat, axis=0, keepdims=True)
        bias_grad = bias_grad + jnp.sum(cot, axis=0, keepdims=True)
        gy = cot * gain
        mean_gy = jnp.mean(gy, axis=-1, keepdims=True)
        mean_gx = jnp.mean(gy * xhat, axis=-1, keepdims=True)
        sum_grad = rstd * (gy - mean_gy - xhat * mean_gx)
        low = sum_grad.astype(BF)
        g_ref[rows, :] = low
        sent = jnp.zeros(sum_grad.shape, F32)
        for g, (up, down) in enumerate(((ua_ref, da_ref), (ub_ref, db_ref))):
            pres = []
            for c in range(hidden // HB):
                columns = pl.ds(g * hidden + c * HB, HB)
                slope = slope_ref[rows, columns].astype(F32)
                pres.append((nt(low, down[c * HB : (c + 1) * HB, :]) * slope).astype(BF))
                pre_ref[rows, columns] = pres[-1]
            sent = sent + nt(jnp.concatenate(pres, axis=1), up[...]).astype(BF).astype(F32)
        back_ref[rows, :] = sum_grad + sent
        sent_ref[rows, :] = sent.astype(BF)
    small_ref[0:1, :] = gain_grad
    small_ref[1:2, :] = bias_grad
    if last:
        acts, xs = before[:seqs], before[seqs : 2 * seqs]
        pres = (*before[2 * seqs : 3 * seqs - 1], pre_ref)
        gs = (*before[3 * seqs - 1 :], g_ref)
        dups, ddowns = refs[-4:-2], refs[-2:]
        for g in range(2):
            for c in range(hidden // HB):
                columns = pl.ds(g * hidden + c * HB, HB)
                block = pl.ds(c * HB, HB)
                dups[g][:, block] = sum(tn(x[...], p[:, columns]) for x, p in zip(xs, pres)).astype(BF)
                ddowns[g][block, :] = sum(tn(a[:, columns], h[...]) for a, h in zip(acts, gs)).astype(BF)


def astern(meta, own, far, grad, spans, up, down, slope, vectors, u, seqs, before):
    half, d = own.shape
    hidden = up[0].shape[1]
    rows = fixed(half, d)
    wide = fixed(half, 2 * hidden)
    extra = [] if not before else [wide] * seqs + [rows] * seqs + [wide] * (seqs - 1) + [rows] * (seqs - 1)
    grads = [] if not before else [(d, hidden)] * 2 + [(hidden, d)] * 2
    return call(
        functools.partial(astern_kernel, seqs, u),
        "astern",
        (1,),
        meta,
        (own, far, grad, spans, *up, *down, slope, vectors, *before),
        [rows] * 2
        + [pl.BlockSpec((half, d), lambda i, m: (u * 2 + m[0], 0)), fixed(*spans.shape)]
        + [fixed(d, hidden)] * 2
        + [fixed(hidden, d)] * 2
        + [wide, fixed(4, d)]
        + extra,
        [rows, rows, wide, rows, rows, fixed(2, d)] + [fixed(*shape) for shape in grads],
        [
            like((half, d), BF),
            like((half, d), BF),
            like((half, 2 * hidden), BF),
            like((half, d), F32),
            like((half, d), BF),
            like((2, d), F32),
        ]
        + [like(shape, BF) for shape in grads],
        limit=32 if before else VMEM,
    )


def inner_kernel(meta_ref, own_ref, far_ref, xhat_ref, rstd_ref, vec_ref, a0, a1, w0, w1, *refs):
    last = len(refs) == 11
    out_ref, g0, g1, m0, m1, small_ref = refs[-6:]
    grad = own_ref[...] + far_ref[...].astype(F32)
    xhat = xhat_ref[...]
    gain_grad = jnp.sum(grad * xhat, axis=0, keepdims=True)
    bias_grad = jnp.sum(grad, axis=0, keepdims=True)
    gy = grad * vec_ref[0:1, :]
    mean_gy = jnp.mean(gy, axis=-1, keepdims=True)
    mean_gx = jnp.mean(gy * xhat, axis=-1, keepdims=True)
    inner = rstd_ref[:, 0:1] * (gy - mean_gy - xhat * mean_gx)
    out_ref[...] = inner
    low = inner.astype(BF)
    g0[...] = nt(w0[...], low).astype(BF)
    g1[...] = nt(w1[...], low).astype(BF)
    small = jnp.concatenate([gain_grad, bias_grad], axis=0)
    small_ref[...] = small
    if last:
        before0, before1, before_small, outer0, outer1 = refs[:5]
        below = jnp.concatenate(
            [small + before_small[...], outer0[...] + outer1[...], jnp.zeros((60, small.shape[1]), F32)], axis=0
        ).astype(BF)
        for m, a, before in ((m0, a0, before0), (m1, a1, before1)):
            m[:192, :] = (nn(a[...], low) + before[...]).astype(BF)
            m[192:, :] = below
    else:
        m0[...] = nn(a0[...], low)
        m1[...] = nn(a1[...], low)


def inner_norm(meta, own, far, xhat, rstd, vectors, att, weights, before):
    rows, d = xhat.shape
    merge = like((256, d), BF) if before else like((192, d), F32)
    return call(
        inner_kernel,
        "inner_norm",
        (1,),
        meta,
        (own, far, xhat, rstd, vectors, *att, *weights, *before),
        [fixed(rows, d)] * 3
        + [fixed(rows, 128), fixed(4, d)]
        + [fixed(192, rows)] * 2
        + [fixed(192, d)] * 2
        + ([fixed(192, d)] * 2 + [fixed(2, d)] * 3 if before else []),
        [fixed(rows, d), fixed(192, rows), fixed(192, rows), fixed(*merge.shape), fixed(*merge.shape), fixed(2, d)],
        [like((rows, d), F32), like((192, rows), BF), like((192, rows), BF), merge, merge, like((2, d), F32)],
    )


def local(groups, tokens, lengths, span_starts, wq, wk, wv, wm, wu, wd, ig, ib, og, ob, out_grad):
    rows, d = tokens.shape
    seqs = lengths.shape[0]
    frames = rows // seqs
    half = frames // 2
    core = lax.axis_index("tensor") % 2
    place_dp = lax.axis_index("dp")
    bits = groups.bit_length() - 1

    def swap(value, k):
        return lax.ppermute(value, "tensor", [(i, i ^ k) for i in range(4)])

    def swap_dp(value, k):
        return lax.ppermute(value, "dp", [(i, i ^ k) for i in range(groups)])

    def add(a, b):
        return (a.astype(F32) + b.astype(F32)).astype(BF)

    def cut(array, index, count):
        size = array.shape[0] // count
        return lax.dynamic_slice_in_dim(array, index * size, size, 0)

    def pieces_of(array, stage):
        low_bit, width = stage
        count = 1 << width
        spot = (place_dp >> low_bit) & (count - 1)
        got = [swap_dp(cut(array, spot ^ j, count), j << low_bit) for j in range(1, count)]
        return [cut(array, spot, count)] + got

    def add_up(pieces):
        return sum(piece.astype(F32) for piece in pieces).astype(BF)

    def scatter(array, stage):
        return add_up(pieces_of(array, stage))

    def collect(array, stage):
        low_bit, width = stage
        count = 1 << width
        spot = (place_dp >> low_bit) & (count - 1)
        size = array.shape[0]
        whole = jnp.zeros((size * count, d), BF)
        pieces = [array] + [swap_dp(array, j << low_bit) for j in range(1, count)]
        for j in range(count):
            whole = lax.dynamic_update_slice_in_dim(whole, pieces[j], (spot ^ j) * size, 0)
        return whole

    scalars = jnp.concatenate([core.reshape(1), lengths])
    token = []

    def meta():
        return lax.optimization_barrier((scalars, *token))[0] if token else scalars

    def done(results, *others):
        token[:] = [results[-1], *others]
        return results

    merge_w = (wm, swap(wm, 1), swap(wm, 2), swap(wm, 3))
    up_w = (wu, swap(wu, 1))
    down_w = (wd, swap(wd, 1))
    vectors = jnp.stack([ig, ib, og, ob])
    qkv_w = (wq.T, wk.T, wv.T)

    q, k, v = project(tokens, *qkv_w)
    fwd, att = [], []
    for u in range(seqs):
        fwd.append(done(attend_forward(meta(), q, k, v, u, frames), *merge_w[1:], up_w[1], down_w[1]))
        own, other = fwd[u][:2]
        att.append((own, swap(other, 1), swap(own, 2), swap(other, 3)))
    front, far = [], []
    for u in range(seqs):
        front.append(done(ahead(meta(), tokens, att[u], merge_w, up_w, down_w, vectors, u)))
        far.append(swap(front[u][6], 2))
    back, far_grad = [], []
    for u in range(seqs):
        before = ()
        if u == seqs - 1:
            before = (*(f[3] for f in front), *(f[2] for f in front), *(b[2] for b in back), *(b[1] for b in back))
        back.append(
            done(astern(meta(), front[u][5], far[u], out_grad, span_starts, up_w, down_w, front[u][4], vectors, u, seqs, before))
        )
        far_grad.append(swap(back[u][4], 2))
    up_own, up_other, down_own, down_other = back[-1][6:]
    up_sum, down_sum = add(up_own, swap(up_other, 1)), add(down_own, swap(down_other, 1))
    token.extend([up_sum, down_sum])
    up_sum, down_sum = lax.psum((up_sum, down_sum), "dp")

    def inner_step(u, before):
        res = done(inner_norm(meta(), back[u][3], far_grad[u], front[u][0], front[u][1], vectors, att[u][:2], merge_w[:2], before))
        return res, (res[1], swap(res[2], 1))

    def attend_step(u, grads):
        return done(attend_backward(meta(), q, k, v, *grads, fwd[u][2], fwd[u][3], u, frames))

    def entry_step(u, grads, before, dtype):
        return done(entry_back(meta(), tokens, grads, qkv_w, before, u, frames, dtype))


    stages = [(0, 1)] + [(b, 2) for b in range(1, bits - 1, 2)] + ([(bits - 1, 1)] if bits % 2 == 0 else [])
    inner, near, crossed, total = [], [], [], ()
    for u in range(seqs):
        last = u == seqs - 1
        if u == 0:
            res, grads = inner_step(0, ())
            inner.append(res)
        dqkv = attend_step(u, grads)
        if not last:
            before = ()
            if u + 1 == seqs - 1:
                before = (inner[0][3], inner[0][4], inner[0][5], back[0][5], back[1][5])
            res, grads = inner_step(u + 1, before)
            inner.append(res)
            if u + 1 == seqs - 1:
                merge_pieces = pieces_of(add(res[3], swap(res[4], 1)), stages[0])
        if last:
            merge_part = add_up(lax.optimization_barrier((*merge_pieces, dqkv[0]))[:-1])
            token.extend(crossed)
        res = entry_step(u, dqkv, total, BF if last else F32)
        total = (res[2],)
        got = swap(res[0], 1)
        near.append(res[1].astype(F32) + got.astype(F32))
        crossed.append(swap(near[u].astype(BF), 2))
        token.append(got)
    back_steps = [(collect, stage) for stage in reversed(stages)]
    steps = [(scatter, stage) for stage in stages] + back_steps
    merge_sum, qkv_sum = merge_part, total[0]
    for ahead_step, step in zip(steps[1:] + [None], steps):
        qkv_sum = step[0](qkv_sum, step[1])
        if ahead_step:
            merge_sum = ahead_step[0](merge_sum, ahead_step[1])
            merge_sum, qkv_sum = lax.optimization_barrier((merge_sum, qkv_sum))

    ready = []
    for u in range(seqs):
        ready.append((inner[u][0] + (near[u] + crossed[u].astype(F32))).astype(BF))
    ready = jnp.stack(ready)
    out_rows = jnp.stack([b[0] for b in back])
    layer_output = place(meta(), out_rows, swap(out_rows, 1))
    input_grad = place(scalars, ready, swap(ready, 1))

    small = merge_sum[192:196].astype(F32)
    query_grad, key_grad, value_grad = (qkv_sum[192 * i : 192 * (i + 1)].astype(F32).T for i in range(3))
    return (
        layer_output,
        input_grad,
        query_grad,
        key_grad,
        value_grad,
        merge_sum[:192].astype(F32),
        up_sum.astype(F32),
        down_sum.astype(F32),
        small[0],
        small[1],
        small[2],
        small[3],
    )


def solution(mesh):
    in_specs = (
        P("dp", None),
        P("dp"),
        P("dp", None),
        P(None, "tensor"),
        P(None, "tensor"),
        P(None, "tensor"),
        P("tensor", None),
        P(None, "tensor"),
        P("tensor", None),
        P(),
        P(),
        P(),
        P(),
        P("dp", None),
    )
    out_specs = (
        P("dp", None),
        P("dp", None),
        P(None, "tensor"),
        P(None, "tensor"),
        P(None, "tensor"),
        P("tensor", None),
        P(None, "tensor"),
        P("tensor", None),
        P(),
        P(),
        P(),
        P(),
    )
    body = functools.partial(local, mesh.shape["dp"])
    return jax.shard_map(body, mesh=mesh, in_specs=in_specs, out_specs=out_specs, check_vma=False)
```

profile of v0, /device:TPU:0, one launch (start us, length us, event | category | flops | bytes accessed | tf_op | source)
XLA Modules:
  0.0 336.3 jit_solution(6017381513229210515)
XLA Ops:
  8.3 2.6 collective-permute-start.1
  10.9 1.9 copy-done
  15.7 3.2 project.1
  23.7 2.6 attend_forward.2
  27.4 1.7 collective-permute-start.7
  35.1 6.5 %attend_forward.3 = (bf16[192,512]{1,0:T(8,128)(2,1)S(1)}, bf16[192,512]{1,0:T(8,128)(2,1)S(1)}, f32[2,192,512]{2,1,0:T(8,128)S(1)}, f32[2,8,512]{2,1,0:T(8,128)S(1)}) custom-call(s32[3]{0:T(128)S(1)} %pad_add_fusion.meta_ref, bf16[2048,256]{1,0:T(8,128)(2,1)S(1)} %copy-done.11, bf16[2048,256]{1,0:T(8,128)(2,1)S(1)} %copy-done.16, ...), custom_call_target="tpu_custom_call" | custom-call | flops 1000 | bytes 1024 | tf_op jit(solution)/shard_map/attend_forward/pallas_call | solution.py:81
  42.6 1.7 collective-permute-start.9
  47.1 8.9 %ahead.2 = (f32[512,768]{1,0:T(8,128)S(1)}, f32[512,128]{1,0:T(8,128)S(1)}, bf16[512,768]{1,0:T(8,128)(2,1)S(1)}, bf16[512,1536]{1,0:T(8,128)(2,1)S(1)}, bf16[51...) custom-call(s32[3]{0:T(128)S(1)} %pad_add_fusion.meta_ref, ...), custom_call_target="tpu_custom_call" | custom-call | flops 1000 | bytes 1024 | tf_op jit(solution)/shard_map/ahead/pallas_call | solution.py:81
  58.7 1.7 collective-permute-start.11
  60.4 9.5 %ahead.3 = (f32[512,768]{1,0:T(8,128)S(1)}, f32[512,128]{1,0:T(8,128)S(1)}, bf16[512,768]{1,0:T(8,128)(2,1)S(1)}, bf16[512,1536]{1,0:T(8,128)(2,1)S(1)}, bf16[51...) custom-call(s32[3]{0:T(128)S(1)} %pad_add_fusion.meta_ref, ...), custom_call_target="tpu_custom_call" | custom-call | flops 1000 | bytes 1024 | tf_op jit(solution)/shard_map/ahead/pallas_call | solution.py:81
  71.4 7.7 %collective-permute-done.11.far_ref = bf16[512,768]{1,0:T(8,128)(2,1)S(1)} collective-permute-done((bf16[512,768]{1,0:T(8,128)(2,1)S(1)}, bf16[512,768]{1,0:T(8,128)(2,1)S(1)}, u32[]{:S(2)}, u32[]{:S(2)}) %collective-permute-start.11) | collective-permute-done | bytes 786464 | tf_op jit(solution)/shard_map/ppermute | solution.py:576
  79.1 7.8 %astern.2 = (bf16[512,768]{1,0:T(8,128)(2,1)S(1)}, bf16[512,768]{1,0:T(8,128)(2,1)S(1)}, bf16[512,1536]{1,0:T(8,128)(2,1)S(1)}, f32[512,768]{1,0:T(8,128)S(1)}, ...) custom-call(s32[3]{0:T(128)S(1)} %pad_add_fusion.meta_ref, f32[512,768]{1,0:T(8,128)S(1)} %get-tuple-element.108.own_ref, ...), custom_call_target="tpu_custom_call" | custom-call | flops 1000 | bytes 1024 | tf_op jit(solution)/shard_map/astern/pallas_call | solution.py:81
  89.1 6.1 %collective-permute-done.12.far_ref = bf16[512,768]{1,0:T(8,128)(2,1)S(1)} collective-permute-done((bf16[512,768]{1,0:T(8,128)(2,1)S(1)}, bf16[512,768]{1,0:T(8,128)(2,1)S(1)}, u32[]{:S(2)}, u32[]{:S(2)}) %collective-permute-start.12) | collective-permute-done | bytes 786464 | tf_op jit(solution)/shard_map/ppermute | solution.py:576
  95.2 15.0 %astern.3 = (bf16[512,768]{1,0:T(8,128)(2,1)S(1)}, bf16[512,768]{1,0:T(8,128)(2,1)}, bf16[512,1536]{1,0:T(8,128)(2,1)}, f32[512,768]{1,0:T(8,128)S(1)}, bf16[512...) custom-call(s32[3]{0:T(128)S(1)} %pad_add_fusion.meta_ref, ...), custom_call_target="tpu_custom_call" | custom-call | flops 1000 | bytes 1024 | tf_op jit(solution)/shard_map/astern/pallas_call | solution.py:81
  110.9 1.7 collective-permute-start.15
  116.3 14.4 %collective-permute-done.15.far_ref = bf16[512,768]{1,0:T(8,128)(2,1)} collective-permute-done((bf16[512,768]{1,0:T(8,128)(2,1)}, bf16[512,768]{1,0:T(8,128)(2,1)}, u32[]{:S(2)}, u32[]{:S(2)}) %collective-permute-start.15) | collective-permute-done | bytes 786464 | tf_op jit(solution)/shard_map/ppermute | solution.py:576
  136.4 3.7 %inner_norm.2 = (f32[512,768]{1,0:T(8,128)S(1)}, bf16[192,512]{1,0:T(8,128)(2,1)S(1)}, bf16[192,512]{1,0:T(8,128)(2,1)S(1)}, f32[192,768]{1,0:T(8,128)S(1)}, f32...) custom-call(s32[3]{0:T(128)S(1)} %pad_add_fusion.meta_ref, f32[512,768]{1,0:T(8,128)S(1)} %copy-done.53, ...), custom_call_target="tpu_custom_call" | custom-call | flops 1000 | bytes 1024 | tf_op jit(solution)/shard_map/inner_norm/pallas_call | solution.py:81
  141.3 1.7 collective-permute-start.18
  143.1 4.0 %attend_backward.2 = (bf16[1024,256]{1,0:T(8,128)(2,1)S(1)}, bf16[1024,256]{1,0:T(8,128)(2,1)S(1)}, bf16[1024,256]{1,0:T(8,128)(2,1)S(1)}) custom-call(s32[3]{0:T(128)S(1)} %pad_add_fusion.meta_ref, bf16[2048,256]{1,0:T(8,128)(2,1)S(1)} %copy-done.12, bf16[2048,256]{1,0:T(8,128)(2,1)S(1)} %copy-done.17, bf16[2048,256]{1,0:T(8,128)(2,1)S(1)} %copy-done.22, ...), custom_call_target="tpu_custom_call" | custom-call | flops 1000 | bytes 1024 | tf_op jit(solution)/shard_map/attend_backward/pallas_call | solution.py:81
  147.2 5.6 %entry_back.2 = (bf16[512,768]{1,0:T(8,128)(2,1)}, bf16[512,768]{1,0:T(8,128)(2,1)S(1)}, f32[576,768]{1,0:T(8,128)S(1)}) custom-call(s32[3]{0:T(128)S(1)} %pad_add_fusion.meta_ref, bf16[2048,768]{1,0:T(8,128)(2,1)S(1)} %copy-done.1, bf16[1024,256]{1,0:T(8,128)(2,1)S(1)} %get-tuple-element.134.dq_ref, bf16[1024,256]{1,0:T(8,128)(2,1)S(1)} %get-tuple-element.135.dk_ref, ...), custom_call_target="tpu_custom_call" | custom-call | flops 1000 | bytes 1024 | tf_op jit(solution)/shard_map/entry_back/pallas_call | solution.py:81
  155.1 6.1 %collective-permute-done.18.far_ref = bf16[512,768]{1,0:T(8,128)(2,1)S(1)} collective-permute-done((bf16[512,768]{1,0:T(8,128)(2,1)S(1)}, bf16[512,768]{1,0:T(8,128)(2,1)S(1)}, u32[]{:S(2)}, u32[]{:S(2)}) %collective-permute-start.18) | collective-permute-done | bytes 786464 | tf_op jit(solution)/shard_map/ppermute | solution.py:576
  161.3 4.0 %inner_norm.3 = (f32[512,768]{1,0:T(8,128)S(1)}, bf16[192,512]{1,0:T(8,128)(2,1)S(1)}, bf16[192,512]{1,0:T(8,128)(2,1)S(1)}, bf16[256,768]{1,0:T(8,128)(2,1)S(1)...) custom-call(s32[3]{0:T(128)S(1)} %pad_add_fusion.meta_ref, f32[512,768]{1,0:T(8,128)S(1)} %copy-done.51, ...), custom_call_target="tpu_custom_call" | custom-call | flops 1000 | bytes 1024 | tf_op jit(solution)/shard_map/inner_norm/pallas_call | solution.py:81
  169.0 2.4 fusion
  171.5 1.7 collective-permute-start.20
  175.1 5.6 %collective-permute-start.26 = (bf16[128,768]{1,0:T(8,128)(2,1)}, bf16[128,768]{1,0:T(8,128)(2,1)}, u32[]{:S(2)}, u32[]{:S(2)}) collective-permute-start(bf16[128,768]{1,0:T(8,128)(2,1)} %get-tuple-element.186), channel_id=1, source_target_pairs={{0,4},{4,0},{8,12},{12,8},{16,20},{20,16},{24,28},{28,24},{1,5},{5... | collective-permute-start | bytes 589832 | tf_op jit(solution)/shard_map/ppermute | solution.py:579
  180.7 2.7 pad_maximum_fusion.own_ref
  189.1 10.2 %attend_backward.3 = (bf16[1024,256]{1,0:T(8,128)(2,1)S(1)}, bf16[1024,256]{1,0:T(8,128)(2,1)S(1)}, bf16[1024,256]{1,0:T(8,128)(2,1)S(1)}) custom-call(s32[3]{0:T(128)S(1)} %pad_add_fusion.meta_ref, bf16[2048,256]{1,0:T(8,128)(2,1)S(1)} %copy-done.13, bf16[2048,256]{1,0:T(8,128)(2,1)S(1)} %copy-done.18, bf16[2048,256]{1,0:T(8,128)(2,1)S(1)} %copy-done.23, ...), custom_call_target="tpu_custom_call" | custom-call | flops 1000 | bytes 1024 | tf_op jit(solution)/shard_map/attend_backward/pallas_call | solution.py:81
  200.4 5.2 %collective-permute-start.28 = (bf16[32,768]{1,0:T(8,128)(2,1)S(1)}, bf16[32,768]{1,0:T(8,128)(2,1)S(1)}, u32[]{:S(2)}, u32[]{:S(2)}) collective-permute-start(bf16[32,768]{1,0:T(8,128)(2,1)S(1)} %get-tuple-element.190), channel_id=1, source_target_pairs={{0,16},{4,20},{8,24},{12,28},{16,0},{20,4},{24,8},{28,12},{1,17},{... | collective-permute-start | bytes 147464 | tf_op jit(solution)/shard_map/ppermute | solution.py:579
  207.0 4.6 %entry_back.3 = (bf16[512,768]{1,0:T(8,128)(2,1)S(1)}, bf16[512,768]{1,0:T(8,128)(2,1)S(1)}, bf16[576,768]{1,0:T(8,128)(2,1)S(1)}) custom-call(s32[3]{0:T(128)S(1)} %pad_add_fusion.meta_ref, bf16[2048,768]{1,0:T(8,128)(2,1)S(1)} %copy-done.1, bf16[1024,256]{1,0:T(8,128)(2,1)S(1)} %get-tuple-element.154.dq_ref, ...), custom_call_target="tpu_custom_call" | custom-call | flops 1000 | bytes 1024 | tf_op jit(solution)/shard_map/entry_back/pallas_call | solution.py:81
  214.6 1.8 fusion.2
  216.4 6.8 %collective-permute-done.30 = bf16[288,768]{1,0:T(8,128)(2,1)S(1)} collective-permute-done((bf16[288,768]{1,0:T(8,128)(2,1)S(1)}, bf16[288,768]{1,0:T(8,128)(2,1)S(1)}, u32[]{:S(2)}, u32[]{:S(2)}) %collective-permute-start.30) | collective-permute-done | bytes 442400 | tf_op jit(solution)/shard_map/ppermute | solution.py:579
  224.0 2.8 collective-permute-start.32
  229.7 3.0 collective-permute-start.35
  233.7 2.0 collective-permute-start.36
  235.7 3.6 %collective-permute-done.34 = bf16[72,768]{1,0:T(8,128)(2,1)S(1)} collective-permute-done((bf16[72,768]{1,0:T(8,128)(2,1)S(1)}, bf16[72,768]{1,0:T(8,128)(2,1)S(1)}, u32[]{:S(2)}, u32[]{:S(2)}) %collective-permute-start.34) | collective-permute-done | bytes 110624 | tf_op jit(solution)/shard_map/ppermute | solution.py:579
  239.3 5.6 %collective-permute-done.35 = bf16[72,768]{1,0:T(8,128)(2,1)S(1)} collective-permute-done((bf16[72,768]{1,0:T(8,128)(2,1)S(1)}, bf16[72,768]{1,0:T(8,128)(2,1)S(1)}, u32[]{:S(2)}, u32[]{:S(2)}) %collective-permute-start.35) | collective-permute-done | bytes 110624 | tf_op jit(solution)/shard_map/ppermute | solution.py:579
  245.7 2.5 collective-permute-start.38
  248.8 1.7 collective-permute-start.40
  252.0 1.6 constant_dynamic-update-slice_fusion.5
  253.6 50.0 %all-reduce.3.cloned.1.call-done = (bf16[768,768]{1,0:T(8,128)(2,1)}, bf16[768,768]{1,0:T(8,128)(2,1)}) async-done(((bf16[768,768]{1,0:T(8,128)(2,1)}, bf16[768,768]{1,0:T(8,128)(2,1)}), (bf16[768,768]{1,0:T(8,128)(2,1)}, bf16[768,768]{1,0:T(8,128)(2,1)})) %all-reduce.3.cloned.1.call-update) | async-done | bytes 2359312 | tf_op jit(solution)/shard_map/psum | solution.py:650
  303.6 2.9 convert_element_type.156
  306.5 1.6 convert_element_type.157
  309.6 1.5 constant_dynamic-update-slice_fusion.4
  311.1 1.5 constant_dynamic-update-slice_fusion.3
  312.7 1.5 constant_dynamic-update-slice_fusion.2
  317.9 5.1 %place.2 = bf16[2048,768]{1,0:T(8,128)(2,1)} custom-call(s32[3]{0:T(128)S(1)} %pad_add_fusion.meta_ref, bf16[2,512,768]{2,1,0:T(8,128)(2,1)} %pad_maximum_fusion.own_ref, bf16[2,512,768]{2,1,0:T(8,128)(2,1)} %collective-permute-done.22.other_ref), custom_call_target="tpu_custom_call" | custom-call | flops 1000 | bytes 1024 | tf_op jit(solution)/shard_map/place/pallas_call | solution.py:81
  323.1 1.9 collective-permute-done.41
  326.3 2.7 place.3
  (281 shorter events, 70.0 us)
Async XLA Ops:
  7.2 296.4 %all-reduce.3.cloned.1.call-start = ((), (), s32[]{:S(2)}) async-start(), calls=%async_computation | async-start | bytes 4718592 | tf_op jit(solution)/shard_map/psum | solution.py:650
  7.2 22.2 %collective-permute-start.3 = (bf16[768,768]{1,0:T(8,128)(2,1)}, bf16[768,768]{1,0:T(8,128)(2,1)S(1)}, u32[]{:S(2)}, u32[]{:S(2)}) collective-permute-start(bf16[768,768]{1,0:T(8,128)(2,1)} %ua_ref.7), channel_id=1, source_target_pairs={{0,1},{1,0},{2,3},{3,2},{4,5},{5,4},{6,7},{7,6},{8,9},{9,8},{10,11... | collective-permute-start | bytes 3538952 | tf_op jit(solution)/shard_map/ppermute | solution.py:576
  7.7 22.7 %collective-permute-start.4 = (bf16[768,768]{1,0:T(8,128)(2,1)}, bf16[768,768]{1,0:T(8,128)(2,1)S(1)}, u32[]{:S(2)}, u32[]{:S(2)}) collective-permute-start(bf16[768,768]{1,0:T(8,128)(2,1)} %da_ref.7), channel_id=1, source_target_pairs={{0,1},{1,0},{2,3},{3,2},{4,5},{5,4},{6,7},{7,6},{8,9},{9,8},{10,11... | collective-permute-start | bytes 3538952 | tf_op jit(solution)/shard_map/ppermute | solution.py:576
  7.8 19.4 %collective-permute-start = (bf16[192,768]{1,0:T(8,128)(2,1)}, bf16[192,768]{1,0:T(8,128)(2,1)}, u32[]{:S(2)}, u32[]{:S(2)}) collective-permute-start(bf16[192,768]{1,0:T(8,128)(2,1)} %w0.7), channel_id=1, source_target_pairs={{0,1},{1,0},{2,3},{3,2},{4,5},{5,4},{6,7},{7,6},{8,9},{9,8},{10,11... | collective-permute-start | bytes 884744 | tf_op jit(solution)/shard_map/ppermute | solution.py:576
  8.3 19.1 %collective-permute-start.1 = (bf16[192,768]{1,0:T(8,128)(2,1)}, bf16[192,768]{1,0:T(8,128)(2,1)}, u32[]{:S(2)}, u32[]{:S(2)}) collective-permute-start(bf16[192,768]{1,0:T(8,128)(2,1)} %w0.7), channel_id=1, source_target_pairs={{0,2},{1,3},{2,0},{3,1},{4,6},{5,7},{6,4},{7,5},{8,10},{9,11},{10,... | collective-permute-start | bytes 884744 | tf_op jit(solution)/shard_map/ppermute | solution.py:576
  10.8 18.3 %collective-permute-start.2 = (bf16[192,768]{1,0:T(8,128)(2,1)}, bf16[192,768]{1,0:T(8,128)(2,1)}, u32[]{:S(2)}, u32[]{:S(2)}) collective-permute-start(bf16[192,768]{1,0:T(8,128)(2,1)} %w0.7), channel_id=1, source_target_pairs={{0,3},{1,2},{2,1},{3,0},{4,7},{5,6},{6,5},{7,4},{8,11},{9,10},{10,... | collective-permute-start | bytes 884744 | tf_op jit(solution)/shard_map/ppermute | solution.py:576
  23.7 20.9 %copy-start.2 = (bf16[768,768]{1,0:T(8,128)(2,1)S(1)}, bf16[768,768]{1,0:T(8,128)(2,1)}, u32[]{:S(2)}) copy-start(bf16[768,768]{1,0:T(8,128)(2,1)} %ua_ref.7) | copy-start | bytes 3538948
  23.7 20.9 %copy-start.3 = (bf16[768,768]{1,0:T(8,128)(2,1)S(1)}, bf16[768,768]{1,0:T(8,128)(2,1)}, u32[]{:S(2)}) copy-start(bf16[768,768]{1,0:T(8,128)(2,1)} %da_ref.7) | copy-start | bytes 3538948
  23.7 20.9 %copy-start.25 = (bf16[192,768]{1,0:T(8,128)(2,1)S(1)}, bf16[192,768]{1,0:T(8,128)(2,1)}, u32[]{:S(2)}) copy-start(bf16[192,768]{1,0:T(8,128)(2,1)} %w0.7) | copy-start | bytes 884740
  27.2 17.1 %collective-permute-start.5 = (bf16[192,512]{1,0:T(8,128)(2,1)S(1)}, bf16[192,512]{1,0:T(8,128)(2,1)S(1)}, u32[]{:S(2)}, u32[]{:S(2)}) collective-permute-start(bf16[192,512]{1,0:T(8,128)(2,1)S(1)} %get-tuple-element.101), channel_id=1, source_target_pairs={{0,1},{1,0},{2,3},{3,2},{4,5},{5,4},{6,7},{7,6},{8,9},{9,8},{10,11... | collective-permute-start | bytes 589832 | tf_op jit(solution)/shard_map/ppermute | solution.py:576
  27.4 17.2 %collective-permute-start.7 = (bf16[192,512]{1,0:T(8,128)(2,1)S(1)}, bf16[192,512]{1,0:T(8,128)(2,1)S(1)}, u32[]{:S(2)}, u32[]{:S(2)}) collective-permute-start(bf16[192,512]{1,0:T(8,128)(2,1)S(1)} %get-tuple-element.101), channel_id=1, source_target_pairs={{0,3},{1,2},{2,1},{3,0},{4,7},{5,6},{6,5},{7,4},{8,11},{9,10},{10,... | collective-permute-start | bytes 589832 | tf_op jit(solution)/shard_map/ppermute | solution.py:576
  29.1 15.4 %collective-permute-start.6 = (bf16[192,512]{1,0:T(8,128)(2,1)S(1)}, bf16[192,512]{1,0:T(8,128)(2,1)S(1)}, u32[]{:S(2)}, u32[]{:S(2)}) collective-permute-start(bf16[192,512]{1,0:T(8,128)(2,1)S(1)} %get-tuple-element.100.a0), channel_id=1, source_target_pairs={{0,2},{1,3},{2,0},{3,1},{4,6},{5,7},{6,4},{7,5},{8,10},{9,11},{10,... | collective-permute-start | bytes 589832 | tf_op jit(solution)/shard_map/ppermute | solution.py:576
  42.5 17.8 %collective-permute-start.8 = (bf16[192,512]{1,0:T(8,128)(2,1)S(1)}, bf16[192,512]{1,0:T(8,128)(2,1)S(1)}, u32[]{:S(2)}, u32[]{:S(2)}) collective-permute-start(bf16[192,512]{1,0:T(8,128)(2,1)S(1)} %get-tuple-element.105), channel_id=1, source_target_pairs={{0,1},{1,0},{2,3},{3,2},{4,5},{5,4},{6,7},{7,6},{8,9},{9,8},{10,11... | collective-permute-start | bytes 589832 | tf_op jit(solution)/shard_map/ppermute | solution.py:576
  42.6 17.8 %collective-permute-start.9 = (bf16[192,512]{1,0:T(8,128)(2,1)S(1)}, bf16[192,512]{1,0:T(8,128)(2,1)S(1)}, u32[]{:S(2)}, u32[]{:S(2)}) collective-permute-start(bf16[192,512]{1,0:T(8,128)(2,1)S(1)} %get-tuple-element.104.a0), channel_id=1, source_target_pairs={{0,2},{1,3},{2,0},{3,1},{4,6},{5,7},{6,4},{7,5},{8,10},{9,11},{10,... | collective-permute-start | bytes 589832 | tf_op jit(solution)/shard_map/ppermute | solution.py:576
  44.3 16.1 %collective-permute-start.10 = (bf16[192,512]{1,0:T(8,128)(2,1)S(1)}, bf16[192,512]{1,0:T(8,128)(2,1)S(1)}, u32[]{:S(2)}, u32[]{:S(2)}) collective-permute-start(bf16[192,512]{1,0:T(8,128)(2,1)S(1)} %get-tuple-element.105), channel_id=1, source_target_pairs={{0,3},{1,2},{2,1},{3,0},{4,7},{5,6},{6,5},{7,4},{8,11},{9,10},{10,... | collective-permute-start | bytes 589832 | tf_op jit(solution)/shard_map/ppermute | solution.py:576
  58.7 20.4 %copy-start.78 = (s32[2,64]{1,0:T(2,128)S(1)}, s32[2,64]{1,0:T(2,128)}, u32[]{:S(2)}) copy-start(s32[2,64]{1,0:T(2,128)} %span_ref.3) | copy-start | bytes 1540
  58.7 20.4 %collective-permute-start.11 = (bf16[512,768]{1,0:T(8,128)(2,1)S(1)}, bf16[512,768]{1,0:T(8,128)(2,1)S(1)}, u32[]{:S(2)}, u32[]{:S(2)}) collective-permute-start(bf16[512,768]{1,0:T(8,128)(2,1)S(1)} %get-tuple-element.102), channel_id=1, source_target_pairs={{0,2},{1,3},{2,0},{3,1},{4,6},{5,7},{6,4},{7,5},{8,10},{9,11},{10,... | collective-permute-start | bytes 2359304 | tf_op jit(solution)/shard_map/ppermute | solution.py:576
  71.0 24.2 %collective-permute-start.12 = (bf16[512,768]{1,0:T(8,128)(2,1)S(1)}, bf16[512,768]{1,0:T(8,128)(2,1)S(1)}, u32[]{:S(2)}, u32[]{:S(2)}) collective-permute-start(bf16[512,768]{1,0:T(8,128)(2,1)S(1)} %get-tuple-element.106), channel_id=1, source_target_pairs={{0,2},{1,3},{2,0},{3,1},{4,6},{5,7},{6,4},{7,5},{8,10},{9,11},{10,... | collective-permute-start | bytes 2359304 | tf_op jit(solution)/shard_map/ppermute | solution.py:576
  110.3 2.9 collective-permute-start.14
  110.4 4.5 %collective-permute-start.13 = (bf16[768,768]{1,0:T(8,128)(2,1)S(1)}, bf16[768,768]{1,0:T(8,128)(2,1)S(1)}, u32[]{:S(2)}, u32[]{:S(2)}) collective-permute-start(bf16[768,768]{1,0:T(8,128)(2,1)S(1)} %get-tuple-element.122), channel_id=1, source_target_pairs={{0,1},{1,0},{2,3},{3,2},{4,5},{5,4},{6,7},{7,6},{8,9},{9,8},{10,11... | collective-permute-start | bytes 3538952 | tf_op jit(solution)/shard_map/ppermute | solution.py:576
  110.9 19.8 %collective-permute-start.15 = (bf16[512,768]{1,0:T(8,128)(2,1)}, bf16[512,768]{1,0:T(8,128)(2,1)}, u32[]{:S(2)}, u32[]{:S(2)}) collective-permute-start(bf16[512,768]{1,0:T(8,128)(2,1)} %get-tuple-element.126), channel_id=1, source_target_pairs={{0,2},{1,3},{2,0},{3,1},{4,6},{5,7},{6,4},{7,5},{8,10},{9,11},{10,... | collective-permute-start | bytes 2359304 | tf_op jit(solution)/shard_map/ppermute | solution.py:576
  141.3 1.8 collective-permute-start.16
  141.3 20.0 %collective-permute-start.18 = (bf16[512,768]{1,0:T(8,128)(2,1)S(1)}, bf16[512,768]{1,0:T(8,128)(2,1)S(1)}, u32[]{:S(2)}, u32[]{:S(2)}) collective-permute-start(bf16[512,768]{1,0:T(8,128)(2,1)S(1)} %copy-done.80), channel_id=1, source_target_pairs={{0,2},{1,3},{2,0},{3,1},{4,6},{5,7},{6,4},{7,5},{8,10},{9,11},{10,... | collective-permute-start | bytes 2359304 | tf_op jit(solution)/shard_map/ppermute | solution.py:576
  154.9 14.1 %collective-permute-start.17 = (bf16[512,768]{1,0:T(8,128)(2,1)}, bf16[512,768]{1,0:T(8,128)(2,1)}, u32[]{:S(2)}, u32[]{:S(2)}) collective-permute-start(bf16[512,768]{1,0:T(8,128)(2,1)} %get-tuple-element.138), channel_id=1, source_target_pairs={{0,1},{1,0},{2,3},{3,2},{4,5},{5,4},{6,7},{7,6},{8,9},{9,8},{10,11... | collective-permute-start | bytes 2359304 | tf_op jit(solution)/shard_map/ppermute | solution.py:576
  168.5 4.7 %collective-permute-start.25 = (bf16[256,768]{1,0:T(8,128)(2,1)}, bf16[256,768]{1,0:T(8,128)(2,1)}, u32[]{:S(2)}, u32[]{:S(2)}) collective-permute-start(bf16[256,768]{1,0:T(8,128)(2,1)} %get-tuple-element.165), channel_id=1, source_target_pairs={{0,1},{1,0},{2,3},{3,2},{4,5},{5,4},{6,7},{7,6},{8,9},{9,8},{10,11... | collective-permute-start | bytes 1179656 | tf_op jit(solution)/shard_map/ppermute | solution.py:576
  168.5 14.8 %collective-permute-start.19 = (bf16[192,512]{1,0:T(8,128)(2,1)}, bf16[192,512]{1,0:T(8,128)(2,1)}, u32[]{:S(2)}, u32[]{:S(2)}) collective-permute-start(bf16[192,512]{1,0:T(8,128)(2,1)} %copy-done.81), channel_id=1, source_target_pairs={{0,1},{1,0},{2,3},{3,2},{4,5},{5,4},{6,7},{7,6},{8,9},{9,8},{10,11... | collective-permute-start | bytes 589832 | tf_op jit(solution)/shard_map/ppermute | solution.py:576
  171.5 35.5 %collective-permute-start.20 = (bf16[512,768]{1,0:T(8,128)(2,1)}, bf16[512,768]{1,0:T(8,128)(2,1)}, u32[]{:S(2)}, u32[]{:S(2)}) collective-permute-start(bf16[512,768]{1,0:T(8,128)(2,1)} %fusion), channel_id=1, source_target_pairs={{0,2},{1,3},{2,0},{3,1},{4,6},{5,7},{6,4},{7,5},{8,10},{9,11},{10,... | collective-permute-start | bytes 2359304 | tf_op jit(solution)/shard_map/ppermute | solution.py:576
  175.1 24.2 %collective-permute-start.26 = (bf16[128,768]{1,0:T(8,128)(2,1)}, bf16[128,768]{1,0:T(8,128)(2,1)}, u32[]{:S(2)}, u32[]{:S(2)}) collective-permute-start(bf16[128,768]{1,0:T(8,128)(2,1)} %get-tuple-element.186), channel_id=1, source_target_pairs={{0,4},{4,0},{8,12},{12,8},{16,20},{20,16},{24,28},{28,24},{1,5},{5... | collective-permute-start | bytes 589832 | tf_op jit(solution)/shard_map/ppermute | solution.py:579
  183.3 134.6 %collective-permute-start.22 = (bf16[2,512,768]{2,1,0:T(8,128)(2,1)}, bf16[2,512,768]{2,1,0:T(8,128)(2,1)}, u32[]{:S(2)}, u32[]{:S(2)}) collective-permute-start(bf16[2,512,768]{2,1,0:T(8,128)(2,1)} %pad_maximum_fusion.own_ref), channel_id=1, source_target_pairs={{0,1},{1,0},{2,3},{3,2},{4,5},{5,4},{6,7},{7,6},{8,9},{9,8},{10,11... | collective-permute-start | bytes 4718600 | tf_op jit(solution)/shard_map/ppermute | solution.py:576
  200.3 12.7 %collective-permute-start.27 = (bf16[32,768]{1,0:T(8,128)(2,1)S(1)}, bf16[32,768]{1,0:T(8,128)(2,1)S(1)}, u32[]{:S(2)}, u32[]{:S(2)}) collective-permute-start(bf16[32,768]{1,0:T(8,128)(2,1)S(1)} %get-tuple-element.188), channel_id=1, source_target_pairs={{0,8},{4,12},{8,0},{12,4},{16,24},{20,28},{24,16},{28,20},{1,9},{5... | collective-permute-start | bytes 147464 | tf_op jit(solution)/shard_map/ppermute | solution.py:579
  200.4 12.7 %collective-permute-start.28 = (bf16[32,768]{1,0:T(8,128)(2,1)S(1)}, bf16[32,768]{1,0:T(8,128)(2,1)S(1)}, u32[]{:S(2)}, u32[]{:S(2)}) collective-permute-start(bf16[32,768]{1,0:T(8,128)(2,1)S(1)} %get-tuple-element.190), channel_id=1, source_target_pairs={{0,16},{4,20},{8,24},{12,28},{16,0},{20,4},{24,8},{28,12},{1,17},{... | collective-permute-start | bytes 147464 | tf_op jit(solution)/shard_map/ppermute | solution.py:579
  205.6 9.0 %collective-permute-start.29 = (bf16[32,768]{1,0:T(8,128)(2,1)S(1)}, bf16[32,768]{1,0:T(8,128)(2,1)S(1)}, u32[]{:S(2)}, u32[]{:S(2)}) collective-permute-start(bf16[32,768]{1,0:T(8,128)(2,1)S(1)} %get-tuple-element.189), channel_id=1, source_target_pairs={{0,24},{4,28},{8,16},{12,20},{16,8},{20,12},{24,0},{28,4},{1,25},{... | collective-permute-start | bytes 147464 | tf_op jit(solution)/shard_map/ppermute | solution.py:579
  211.7 11.5 %collective-permute-start.30 = (bf16[288,768]{1,0:T(8,128)(2,1)S(1)}, bf16[288,768]{1,0:T(8,128)(2,1)S(1)}, u32[]{:S(2)}, u32[]{:S(2)}) collective-permute-start(bf16[288,768]{1,0:T(8,128)(2,1)S(1)} %constant_dynamic-slice_fusion.3), channel_id=1, source_target_pairs={{0,4},{4,0},{8,12},{12,8},{16,20},{20,16},{24,28},{28,24},{1,5},{5... | collective-permute-start | bytes 1327112 | tf_op jit(solution)/shard_map/ppermute | solution.py:579
  213.1 14.7 %collective-permute-start.21 = (bf16[512,768]{1,0:T(8,128)(2,1)S(1)}, bf16[512,768]{1,0:T(8,128)(2,1)S(1)}, u32[]{:S(2)}, u32[]{:S(2)}) collective-permute-start(bf16[512,768]{1,0:T(8,128)(2,1)S(1)} %get-tuple-element.157), channel_id=1, source_target_pairs={{0,1},{1,0},{2,3},{3,2},{4,5},{5,4},{6,7},{7,6},{8,9},{9,8},{10,11... | collective-permute-start | bytes 2359304 | tf_op jit(solution)/shard_map/ppermute | solution.py:576
  223.3 4.9 %collective-permute-start.31 = (bf16[32,768]{1,0:T(8,128)(2,1)S(1)}, bf16[32,768]{1,0:T(8,128)(2,1)S(1)}, u32[]{:S(2)}, u32[]{:S(2)}) collective-permute-start(bf16[32,768]{1,0:T(8,128)(2,1)S(1)} %add_convert_fusion.8), channel_id=1, source_target_pairs={{0,8},{4,12},{8,0},{12,4},{16,24},{20,28},{24,16},{28,20},{1,9},{5... | collective-permute-start | bytes 147464 | tf_op jit(solution)/shard_map/ppermute | solution.py:579
  224.0 5.7 %collective-permute-start.32 = (bf16[32,768]{1,0:T(8,128)(2,1)S(1)}, bf16[32,768]{1,0:T(8,128)(2,1)S(1)}, u32[]{:S(2)}, u32[]{:S(2)}) collective-permute-start(bf16[32,768]{1,0:T(8,128)(2,1)S(1)} %add_convert_fusion.8), channel_id=1, source_target_pairs={{0,16},{4,20},{8,24},{12,28},{16,0},{20,4},{24,8},{28,12},{1,17},{... | collective-permute-start | bytes 147464 | tf_op jit(solution)/shard_map/ppermute | solution.py:579
  226.8 6.9 %collective-permute-start.33 = (bf16[32,768]{1,0:T(8,128)(2,1)S(1)}, bf16[32,768]{1,0:T(8,128)(2,1)S(1)}, u32[]{:S(2)}, u32[]{:S(2)}) collective-permute-start(bf16[32,768]{1,0:T(8,128)(2,1)S(1)} %add_convert_fusion.8), channel_id=1, source_target_pairs={{0,24},{4,28},{8,16},{12,20},{16,8},{20,12},{24,0},{28,4},{1,25},{... | collective-permute-start | bytes 147464 | tf_op jit(solution)/shard_map/ppermute | solution.py:579
  227.8 22.8 %copy-start.43 = (f32[512,768]{1,0:T(8,128)S(1)}, f32[512,768]{1,0:T(8,128)}, u32[]{:S(2)}) copy-start(f32[512,768]{1,0:T(8,128)} %copy-done.42) | copy-start | bytes 4718596
  228.0 22.5 %collective-permute-start.23 = (bf16[512,768]{1,0:T(8,128)(2,1)S(1)}, bf16[512,768]{1,0:T(8,128)(2,1)S(1)}, u32[]{:S(2)}, u32[]{:S(2)}) collective-permute-start(bf16[512,768]{1,0:T(8,128)(2,1)S(1)} %fusion.1), channel_id=1, source_target_pairs={{0,2},{1,3},{2,0},{3,1},{4,6},{5,7},{6,4},{7,5},{8,10},{9,11},{10,... | collective-permute-start | bytes 2359304 | tf_op jit(solution)/shard_map/ppermute | solution.py:576
  228.2 11.1 %collective-permute-start.34 = (bf16[72,768]{1,0:T(8,128)(2,1)S(1)}, bf16[72,768]{1,0:T(8,128)(2,1)S(1)}, u32[]{:S(2)}, u32[]{:S(2)}) collective-permute-start(bf16[72,768]{1,0:T(8,128)(2,1)S(1)} %get-tuple-element.183), channel_id=1, source_target_pairs={{0,8},{4,12},{8,0},{12,4},{16,24},{20,28},{24,16},{28,20},{1,9},{5... | collective-permute-start | bytes 331784 | tf_op jit(solution)/shard_map/ppermute | solution.py:579
  229.7 15.3 %collective-permute-start.35 = (bf16[72,768]{1,0:T(8,128)(2,1)S(1)}, bf16[72,768]{1,0:T(8,128)(2,1)S(1)}, u32[]{:S(2)}, u32[]{:S(2)}) collective-permute-start(bf16[72,768]{1,0:T(8,128)(2,1)S(1)} %get-tuple-element.185), channel_id=1, source_target_pairs={{0,16},{4,20},{8,24},{12,28},{16,0},{20,4},{24,8},{28,12},{1,17},{... | collective-permute-start | bytes 331784 | tf_op jit(solution)/shard_map/ppermute | solution.py:579
  233.7 11.2 %collective-permute-start.36 = (bf16[72,768]{1,0:T(8,128)(2,1)S(1)}, bf16[72,768]{1,0:T(8,128)(2,1)S(1)}, u32[]{:S(2)}, u32[]{:S(2)}) collective-permute-start(bf16[72,768]{1,0:T(8,128)(2,1)S(1)} %get-tuple-element.184), channel_id=1, source_target_pairs={{0,24},{4,28},{8,16},{12,20},{16,8},{20,12},{24,0},{28,4},{1,25},{... | collective-permute-start | bytes 331784 | tf_op jit(solution)/shard_map/ppermute | solution.py:579
  245.7 62.4 %collective-permute-start.38 = (bf16[72,768]{1,0:T(8,128)(2,1)}, bf16[72,768]{1,0:T(8,128)(2,1)}, u32[]{:S(2)}, u32[]{:S(2)}) collective-permute-start(bf16[72,768]{1,0:T(8,128)(2,1)} %add_convert_fusion.7), channel_id=1, source_target_pairs={{0,8},{4,12},{8,0},{12,4},{16,24},{20,28},{24,16},{28,20},{1,9},{5... | collective-permute-start | bytes 331784 | tf_op jit(solution)/shard_map/ppermute | solution.py:579
  248.1 63.0 %collective-permute-start.39 = (bf16[72,768]{1,0:T(8,128)(2,1)}, bf16[72,768]{1,0:T(8,128)(2,1)}, u32[]{:S(2)}, u32[]{:S(2)}) collective-permute-start(bf16[72,768]{1,0:T(8,128)(2,1)} %add_convert_fusion.7), channel_id=1, source_target_pairs={{0,16},{4,20},{8,24},{12,28},{16,0},{20,4},{24,8},{28,12},{1,17},{... | collective-permute-start | bytes 331784 | tf_op jit(solution)/shard_map/ppermute | solution.py:579
  248.8 63.9 %collective-permute-start.40 = (bf16[72,768]{1,0:T(8,128)(2,1)}, bf16[72,768]{1,0:T(8,128)(2,1)}, u32[]{:S(2)}, u32[]{:S(2)}) collective-permute-start(bf16[72,768]{1,0:T(8,128)(2,1)} %add_convert_fusion.7), channel_id=1, source_target_pairs={{0,24},{4,28},{8,16},{12,20},{16,8},{20,12},{24,0},{28,4},{1,25},{... | collective-permute-start | bytes 331784 | tf_op jit(solution)/shard_map/ppermute | solution.py:579
  251.2 75.1 %collective-permute-start.24 = (bf16[2,512,768]{2,1,0:T(8,128)(2,1)S(1)}, bf16[2,512,768]{2,1,0:T(8,128)(2,1)S(1)}, u32[]{:S(2)}, u32[]{:S(2)}) collective-permute-start(bf16[2,512,768]{2,1,0:T(8,128)(2,1)S(1)} %pad_maximum_fusion.1.own_ref), channel_id=1, source_target_pairs={{0,1},{1,0},{2,3},{3,2},{4,5},{5,4},{6,7},{7,6},{8,9},{9,8},{10,11... | collective-permute-start | bytes 4718600 | tf_op jit(solution)/shard_map/ppermute | solution.py:576
  308.1 6.1 %collective-permute-start.37 = (bf16[128,768]{1,0:T(8,128)(2,1)S(1)}, bf16[128,768]{1,0:T(8,128)(2,1)S(1)}, u32[]{:S(2)}, u32[]{:S(2)}) collective-permute-start(bf16[128,768]{1,0:T(8,128)(2,1)S(1)} %copy-done.84), channel_id=1, source_target_pairs={{0,4},{4,0},{8,12},{12,8},{16,20},{20,16},{24,28},{28,24},{1,5},{5... | collective-permute-start | bytes 589832 | tf_op jit(solution)/shard_map/ppermute | solution.py:579
  314.2 10.7 %collective-permute-start.41 = (bf16[288,768]{1,0:T(8,128)(2,1)}, bf16[288,768]{1,0:T(8,128)(2,1)S(1)}, u32[]{:S(2)}, u32[]{:S(2)}) collective-permute-start(bf16[288,768]{1,0:T(8,128)(2,1)} %constant_dynamic-update-slice_fusion.2), channel_id=1, source_target_pairs={{0,4},{4,0},{8,12},{12,8},{16,20},{20,16},{24,28},{28,24},{1,5},{5... | collective-permute-start | bytes 1327112 | tf_op jit(solution)/shard_map/ppermute | solution.py:579
  (86 other events, 507.5 us)
Sparse Core Ops, SparseCore 0:
  183.5 120.0 all-reduce.2
where the time goes:
time: 341 us; the launch traced here: 336 us
  waiting for transfers between devices  107 us (31%)
  Pallas kernels  93.6 us (27%)
  local copies, waits for them, and re-layouts  53.2 us (16%)
  starting transfers between devices  47 us (14%)
  other arithmetic  20 us (6%)
  between operations  15.3 us (4%)
    pallas_call x14, Pallas kernels, call(): pl.pallas_call(kernel, grid_spec=pltpu.PrefetchScalarGridSpec(num_scalar_...  90.4 us
    psum x1, waiting for transfers between devices, local(): up_sum, down_sum = lax.psum((up_sum, down_sum), 'dp')  50 us
    unnamed x182, local copies, waits for them, and re-layouts  43.5 us
    ppermute x26, waiting for transfers between devices, swap(): return lax.ppermute(value, 'tensor', [(i, i ^ k) for i in range(4)])  35.3 us
    ppermute x16, starting transfers between devices, swap_dp(): return lax.ppermute(value, 'dp', [(i, i ^ k) for i in range(groups)])  30.5 us
    ppermute x16, waiting for transfers between devices, swap_dp(): return lax.ppermute(value, 'dp', [(i, i ^ k) for i in range(groups)])  21.8 us
    ppermute x26, starting transfers between devices, swap(): return lax.ppermute(value, 'tensor', [(i, i ^ k) for i in range(4)])  16.5 us
    dynamic_update_slice x12, local copies, waits for them, and re-layouts, collect(): lax.dynamic_update_slice_in_dim(whole, pieces[j], (spot ^ j) * size, 0)  7.36 us
  transfers between devices with their start and end apart: 43, of which 14 were waited for; matrix products, arithmetic and copies ran while one was open for 9% of the time, Pallas kernels for 21%

commit v1 on v0

--- a/solution.py
+++ b/solution.py
@@ -36,8 +36,11 @@
     return pltpu.CompilerParams(vmem_limit_bytes=limit * MIB)
 
 
-def cost(flops):
-    return pl.CostEstimate(flops=flops, bytes_accessed=1024, transcendentals=0)
+def cost(micros):
+    return pl.CostEstimate(flops=int(micros * 1.1e9), bytes_accessed=1024, transcendentals=0)
+
+
+MICROS = {"attend_forward": 8, "attend_backward": 12, "entry_back": 5, "place": 3, "ahead": 9, "astern": 8, "inner_norm": 3}
 
 
 def project_kernel(x_ref, wq_ref, wk_ref, wv_ref, q_ref, k_ref, v_ref):
@@ -58,7 +61,7 @@
         out_specs=[pl.BlockSpec((block, 256), lambda i: (i, 0))] * 3,
         out_shape=[jax.ShapeDtypeStruct((rows, 256), BF)] * 3,
         compiler_params=params(VMEM),
-        cost_estimate=cost(1000),
+        cost_estimate=cost(3),
         name="project",
     )(tokens, wq, wk, wv)
 
@@ -89,7 +92,7 @@
         ),
         out_shape=out_shape,
         compiler_params=params(limit),
-        cost_estimate=cost(1000),
+        cost_estimate=cost(MICROS[name]),
         name=name,
     )(meta, *args)
 
@@ -331,25 +334,27 @@
     )
 
 
-def place_kernel(meta_ref, own_ref, other_ref, o_ref):
-    for j, r_ref in enumerate((own_ref, other_ref)):
-
-        @pl.when(pl.program_id(1) == j)
+def place_kernel(meta_ref, *refs):
+    o_ref = refs[-1]
+    for i, r_ref in enumerate(refs[:-1]):
+
+        @pl.when(pl.program_id(0) == i)
         def _():
-            o_ref[...] = r_ref[0]
+            o_ref[...] = r_ref[...]
 
 
 def place(meta, own, other):
-    seqs, half, d = own.shape
+    half, d = own[0].shape
+    count = 2 * len(own)
     return call(
         place_kernel,
         "place",
-        (seqs, 2),
+        (count,),
         meta,
-        (own, other),
-        [pl.BlockSpec((1, half, d), lambda u, j, m: (u, 0, 0))] * 2,
-        pl.BlockSpec((half, d), lambda u, j, m: (u * 2 + (j ^ m[0]), 0)),
-        like((seqs * 2 * half, d), own.dtype),
+        [block for pair in zip(own, other) for block in pair],
+        [fixed(half, d)] * count,
+        pl.BlockSpec((half, d), lambda i, m: (i ^ m[0], 0)),
+        like((count * half, d), own[0].dtype),
     )
 
 
@@ -585,29 +590,40 @@
         size = array.shape[0] // count
         return lax.dynamic_slice_in_dim(array, index * size, size, 0)
 
-    def pieces_of(array, stage):
-        low_bit, width = stage
-        count = 1 << width
-        spot = (place_dp >> low_bit) & (count - 1)
-        got = [swap_dp(cut(array, spot ^ j, count), j << low_bit) for j in range(1, count)]
-        return [cut(array, spot, count)] + got
-
-    def add_up(pieces):
-        return sum(piece.astype(F32) for piece in pieces).astype(BF)
-
-    def scatter(array, stage):
-        return add_up(pieces_of(array, stage))
-
-    def collect(array, stage):
-        low_bit, width = stage
-        count = 1 << width
-        spot = (place_dp >> low_bit) & (count - 1)
-        size = array.shape[0]
-        whole = jnp.zeros((size * count, d), BF)
-        pieces = [array] + [swap_dp(array, j << low_bit) for j in range(1, count)]
-        for j in range(count):
-            whole = lax.dynamic_update_slice_in_dim(whole, pieces[j], (spot ^ j) * size, 0)
-        return whole
+    class Chain:
+        def __init__(self, state, order):
+            self.state = state
+            self.steps = [(True, *stage) for stage in order] + [(False, *stage) for stage in reversed(order)]
+
+        def start(self):
+            if self.steps:
+                scatter, low_bit, width = self.steps[0]
+                count = 1 << width
+                spot = (place_dp >> low_bit) & (count - 1)
+                sent = [cut(self.state, spot ^ j, count) if scatter else self.state for j in range(1, count)]
+                got = [swap_dp(piece, j << low_bit) for j, piece in enumerate(sent, 1)]
+                self.pending = [cut(self.state, spot, count) if scatter else self.state] + got
+
+        def finish(self, *after):
+            if not self.steps:
+                return
+            scatter, low_bit, width = self.steps.pop(0)
+            pieces = self.pending
+            if after:
+                pieces = lax.optimization_barrier((*pieces, *after))[: len(pieces)]
+            count = 1 << width
+            spot = (place_dp >> low_bit) & (count - 1)
+            if scatter:
+                self.state = sum(piece.astype(F32) for piece in pieces).astype(BF)
+            elif count == 2:
+                one, two = pieces
+                self.state = jnp.concatenate([jnp.where(spot, two, one), jnp.where(spot, one, two)], axis=0)
+            else:
+                size = pieces[0].shape[0]
+                whole = jnp.zeros((size * count, d), BF)
+                for j in range(count):
+                    whole = lax.dynamic_update_slice_in_dim(whole, pieces[j], (spot ^ j) * size, 0)
+                self.state = whole
 
     scalars = jnp.concatenate([core.reshape(1), lengths])
     token = []
@@ -616,7 +632,7 @@
         return lax.optimization_barrier((scalars, *token))[0] if token else scalars
 
     def done(results, *others):
-        token[:] = [results[-1], *others]
+        token[:] = [results[0], *others]
         return results
 
     merge_w = (wm, swap(wm, 1), swap(wm, 2), swap(wm, 3))
@@ -643,11 +659,8 @@
         back.append(
             done(astern(meta(), front[u][5], far[u], out_grad, span_starts, up_w, down_w, front[u][4], vectors, u, seqs, before))
         )
-        far_grad.append(swap(back[u][4], 2))
-    up_own, up_other, down_own, down_other = back[-1][6:]
-    up_sum, down_sum = add(up_own, swap(up_other, 1)), add(down_own, swap(down_other, 1))
-    token.extend([up_sum, down_sum])
-    up_sum, down_sum = lax.psum((up_sum, down_sum), "dp")
+        if u == 0:
+            far_grad.append(swap(back[u][4], 2))
 
     def inner_step(u, before):
         res = done(inner_norm(meta(), back[u][3], far_grad[u], front[u][0], front[u][1], vectors, att[u][:2], merge_w[:2], before))
@@ -660,47 +673,71 @@
         return done(entry_back(meta(), tokens, grads, qkv_w, before, u, frames, dtype))
 
 
+    pairs = [(b, 1) for b in range(bits)]
     stages = [(0, 1)] + [(b, 2) for b in range(1, bits - 1, 2)] + ([(bits - 1, 1)] if bits % 2 == 0 else [])
-    inner, near, crossed, total = [], [], [], ()
+    inner, near, crossed, total, chains = [], [], [], (), []
+    out_rows = [b[0] for b in back]
+    out_other = [swap(r, 1) for r in out_rows]
+
+    def advance(result):
+        for chain in chains:
+            chain.finish(result)
+            token.append(chain.state)
+            chain.start()
+
     for u in range(seqs):
         last = u == seqs - 1
         if u == 0:
             res, grads = inner_step(0, ())
             inner.append(res)
+            later = lax.optimization_barrier((*back[-1][6:], back[-1][4], res[0]))
+            up_own, up_other, down_own, down_other, sent = later[:5]
+            far_grad.append(swap(sent, 2))
+            chains.append(Chain(add(down_own, swap(down_other, 1)), pairs))
+            chains.append(Chain(add(up_own, swap(up_other, 1)), pairs[1:2] + pairs[:1] + pairs[2:]))
+            for chain in chains:
+                token.append(chain.state)
+                chain.start()
+            token.extend(out_other)
         dqkv = attend_step(u, grads)
+        advance(dqkv[0])
         if not last:
             before = ()
             if u + 1 == seqs - 1:
                 before = (inner[0][3], inner[0][4], inner[0][5], back[0][5], back[1][5])
             res, grads = inner_step(u + 1, before)
             inner.append(res)
-            if u + 1 == seqs - 1:
-                merge_pieces = pieces_of(add(res[3], swap(res[4], 1)), stages[0])
-        if last:
-            merge_part = add_up(lax.optimization_barrier((*merge_pieces, dqkv[0]))[:-1])
+        else:
             token.extend(crossed)
-        res = entry_step(u, dqkv, total, BF if last else F32)
-        total = (res[2],)
-        got = swap(res[0], 1)
-        near.append(res[1].astype(F32) + got.astype(F32))
+        out = entry_step(u, dqkv, total, BF if last else F32)
+        total = (out[2],)
+        got = swap(out[0], 1)
+        near.append(out[1].astype(F32) + got.astype(F32))
         crossed.append(swap(near[u].astype(BF), 2))
         token.append(got)
-    back_steps = [(collect, stage) for stage in reversed(stages)]
-    steps = [(scatter, stage) for stage in stages] + back_steps
-    merge_sum, qkv_sum = merge_part, total[0]
-    for ahead_step, step in zip(steps[1:] + [None], steps):
-        qkv_sum = step[0](qkv_sum, step[1])
-        if ahead_step:
-            merge_sum = ahead_step[0](merge_sum, ahead_step[1])
-            merge_sum, qkv_sum = lax.optimization_barrier((merge_sum, qkv_sum))
-
-    ready = []
-    for u in range(seqs):
-        ready.append((inner[u][0] + (near[u] + crossed[u].astype(F32))).astype(BF))
-    ready = jnp.stack(ready)
-    out_rows = jnp.stack([b[0] for b in back])
-    layer_output = place(meta(), out_rows, swap(out_rows, 1))
-    input_grad = place(scalars, ready, swap(ready, 1))
+        if not last:
+            advance(out[0])
+            chains.append(Chain(add(res[3], swap(res[4], 1)), pairs))
+            token.append(chains[-1].state)
+            chains[-1].start()
+    chains.append(Chain(total[0], stages))
+    chains[-1].start()
+    beside = {0: (got,), 1: (crossed[-1],)}
+    rounds = 0
+    while any(chain.steps for chain in chains):
+        for chain in chains:
+            chain.finish(total[0])
+        states = tuple(chain.state for chain in chains)
+        states = lax.optimization_barrier(states + beside.get(rounds, ()))[: len(chains)]
+        for chain, state in zip(chains, states):
+            chain.state = state
+            chain.start()
+        rounds += 1
+    down_sum, up_sum, merge_sum, qkv_sum = (chain.state for chain in chains)
+
+    ready = [(inner[u][0] + (near[u] + crossed[u].astype(F32))).astype(BF) for u in range(seqs)]
+    layer_output = place(meta(), out_rows, out_other)
+    input_grad = place(scalars, ready, [swap(r, 1) for r in ready])
 
     small = merge_sum[192:196].astype(F32)
     query_grad, key_grad, value_grad = (qkv_sum[192 * i : 192 * (i + 1)].astype(F32).T for i in range(3))

time: 341 us -> 272 us (0.80)
  local copies, waits for them, and re-layouts: 53.2 us -> 16.6 us
  waiting for transfers between devices: 107 us -> 90.8 us
  between operations: 15.3 us -> 2.23 us
  other arithmetic: 20 us -> 12.5 us
  Pallas kernels: 93.6 us -> 97.1 us
    psum x1 -> x0, waiting for transfers between devices: 50 us -> none  [local(): up_sum, down_sum = lax.psum((up_sum, down_sum), 'dp')]
    ppermute x16 -> x26, waiting for transfers between devices: 21.8 us -> 59.4 us  [swap_dp(): return lax.ppermute(value, 'dp', [(i, i ^ k) for i in range(groups)])]
    unnamed x182 -> x130, local copies, waits for them, and re-layouts: 43.5 us -> 15.3 us
    dynamic_update_slice x12 -> x4, local copies, waits for them, and re-layouts: 7.36 us -> 0.06 us  [finish(): lax.dynamic_update_slice_in_dim(whole, pieces[j], (spot ^ j) * size, 0)]
    another operation x4 -> x0, other arithmetic: 5.02 us -> none  [the longest x1 2.66 us: local(): out_rows = jnp.stack([b[0] for b in back])]
    ppermute x26 -> x28, waiting for transfers between devices: 35.3 us -> 31.4 us  [swap(): return lax.ppermute(value, 'tensor', [(i, i ^ k) for i in range(4)])]
    pallas_call x14, Pallas kernels: 90.4 us -> 93.9 us  [call(): pl.pallas_call(kernel, grid_spec=pltpu.PrefetchScalarGridSpec(num_scalar_...]
    ppermute x16 -> x26, starting transfers between devices: 30.5 us -> 32 us  [swap_dp(): return lax.ppermute(value, 'dp', [(i, i ^ k) for i in range(groups)])]
  transfers between devices with their start and end apart: 43 -> 54, of which waited for: 14 -> 22; matrix products, arithmetic and copies ran while one was open for 9% -> 3% of each run, Pallas kernels for 21% -> 34%
where the time goes in v1:
time: 272 us; the launch traced here: 269 us
  Pallas kernels  97.1 us (36%)
  waiting for transfers between devices  90.8 us (33%)
  starting transfers between devices  49.3 us (18%)
  local copies, waits for them, and re-layouts  16.6 us (6%)
  other arithmetic  12.5 us (5%)
    pallas_call x14, Pallas kernels, call(): pl.pallas_call(kernel, grid_spec=pltpu.PrefetchScalarGridSpec(num_scalar_...  93.9 us
    ppermute x26, waiting for transfers between devices, swap_dp(): return lax.ppermute(value, 'dp', [(i, i ^ k) for i in range(groups)])  59.4 us
    ppermute x26, starting transfers between devices, swap_dp(): return lax.ppermute(value, 'dp', [(i, i ^ k) for i in range(groups)])  32 us
    ppermute x28, waiting for transfers between devices, swap(): return lax.ppermute(value, 'tensor', [(i, i ^ k) for i in range(4)])  31.4 us
    ppermute x28, starting transfers between devices, swap(): return lax.ppermute(value, 'tensor', [(i, i ^ k) for i in range(4)])  17.4 us
    unnamed x130, local copies, waits for them, and re-layouts  15.3 us
  transfers between devices with their start and end apart: 54, of which 22 were waited for; matrix products, arithmetic and copies ran while one was open for 3% of the time, Pallas kernels for 34%

profile of v1, /device:TPU:0, one launch (start us, length us, event | category | flops | bytes accessed | tf_op | source)
XLA Modules:
  0.0 268.6 jit_solution(6119871966390205261)
XLA Ops:
  1.2 2.6 collective-permute-start.1
  5.0 1.9 copy-done.2
  9.8 3.2 %project.1 = (bf16[2048,256]{1,0:T(8,128)(2,1)S(1)}, bf16[2048,256]{1,0:T(8,128)(2,1)S(1)}, bf16[2048,256]{1,0:T(8,128)(2,1)S(1)}) custom-call(bf16[2048,768]{1,0:T(8,128)(2,1)S(1)} %copy-done.2, bf16[192,768]{1,0:T(8,128)(2,1)S(1)} %bitcast.10, bf16[192,768]{1,0:T(8,128)(2,1)S(1)} %bitcast.13, bf16[192,768]{1,0:T(8,128)(2,1)S(1)} %bitcast.16), custom_call_target="tpu_custom_call" | custom-call | flops 3300000000 | bytes 1024 | tf_op jit(solution)/shard_map/project/pallas_call | solution.py:56
  13.1 7.7 %attend_forward.2 = (bf16[192,512]{1,0:T(8,128)(2,1)S(1)}, bf16[192,512]{1,0:T(8,128)(2,1)S(1)}, f32[2,192,512]{2,1,0:T(8,128)S(1)}, f32[2,8,512]{2,1,0:T(8,128)S(1)}) custom-call(s32[3]{0:T(128)S(1)} %pad_add_fusion.meta_ref, bf16[2048,256]{1,0:T(8,128)(2,1)S(1)} %get-tuple-element.159.q_ref, bf16[2048,256]{1,0:T(8,128)(2,1)S(1)} %get-tuple-element.160.k_ref, ...), custom_call_target="tpu_custom_call" | custom-call | flops 8800000000 | bytes 1024 | tf_op jit(solution)/shard_map/attend_forward/pallas_call | solution.py:84
  22.1 1.7 collective-permute-start.7
  24.2 4.8 %attend_forward.3 = (bf16[192,512]{1,0:T(8,128)(2,1)S(1)}, bf16[192,512]{1,0:T(8,128)(2,1)S(1)}, f32[2,192,512]{2,1,0:T(8,128)S(1)}, f32[2,8,512]{2,1,0:T(8,128)S(1)}) custom-call(s32[3]{0:T(128)S(1)} %pad_add_fusion.meta_ref, bf16[2048,256]{1,0:T(8,128)(2,1)S(1)} %get-tuple-element.159.q_ref, bf16[2048,256]{1,0:T(8,128)(2,1)S(1)} %get-tuple-element.160.k_ref, ...), custom_call_target="tpu_custom_call" | custom-call | flops 8800000000 | bytes 1024 | tf_op jit(solution)/shard_map/attend_forward/pallas_call | solution.py:84
  29.9 1.7 collective-permute-start.9
  31.7 2.3 collective-permute-done.6.a2
  34.9 8.9 %ahead.2 = (f32[512,768]{1,0:T(8,128)S(1)}, f32[512,128]{1,0:T(8,128)S(1)}, bf16[512,768]{1,0:T(8,128)(2,1)S(1)}, bf16[512,1536]{1,0:T(8,128)(2,1)S(1)}, bf16[51...) custom-call(s32[3]{0:T(128)S(1)} %pad_add_fusion.meta_ref, ...), custom_call_target="tpu_custom_call" | custom-call | flops 9900000256 | bytes 1024 | tf_op jit(solution)/shard_map/ahead/pallas_call | solution.py:84
  44.8 9.1 %ahead.3 = (f32[512,768]{1,0:T(8,128)S(1)}, f32[512,128]{1,0:T(8,128)S(1)}, bf16[512,768]{1,0:T(8,128)(2,1)S(1)}, bf16[512,1536]{1,0:T(8,128)(2,1)S(1)}, bf16[51...) custom-call(s32[3]{0:T(128)S(1)} %pad_add_fusion.meta_ref, ...), custom_call_target="tpu_custom_call" | custom-call | flops 9900000256 | bytes 1024 | tf_op jit(solution)/shard_map/ahead/pallas_call | solution.py:84
  56.3 8.1 %collective-permute-done.11.far_ref = bf16[512,768]{1,0:T(8,128)(2,1)S(1)} collective-permute-done((bf16[512,768]{1,0:T(8,128)(2,1)S(1)}, bf16[512,768]{1,0:T(8,128)(2,1)S(1)}, u32[]{:S(2)}, u32[]{:S(2)}) %collective-permute-start.11) | collective-permute-done | bytes 786464 | tf_op jit(solution)/shard_map/ppermute | solution.py:581
  64.4 7.9 %astern.2 = (bf16[512,768]{1,0:T(8,128)(2,1)S(1)}, bf16[512,768]{1,0:T(8,128)(2,1)S(1)}, bf16[512,1536]{1,0:T(8,128)(2,1)S(1)}, f32[512,768]{1,0:T(8,128)S(1)}, ...) custom-call(s32[3]{0:T(128)S(1)} %pad_add_fusion.meta_ref, f32[512,768]{1,0:T(8,128)S(1)} %get-tuple-element.172.own_ref, ...), custom_call_target="tpu_custom_call" | custom-call | flops 8800000000 | bytes 1024 | tf_op jit(solution)/shard_map/astern/pallas_call | solution.py:84
  74.2 7.0 %collective-permute-done.12.far_ref = bf16[512,768]{1,0:T(8,128)(2,1)S(1)} collective-permute-done((bf16[512,768]{1,0:T(8,128)(2,1)S(1)}, bf16[512,768]{1,0:T(8,128)(2,1)S(1)}, u32[]{:S(2)}, u32[]{:S(2)}) %collective-permute-start.12) | collective-permute-done | bytes 786464 | tf_op jit(solution)/shard_map/ppermute | solution.py:581
  82.5 16.1 %astern.3 = (bf16[512,768]{1,0:T(8,128)(2,1)}, bf16[512,768]{1,0:T(8,128)(2,1)}, bf16[512,1536]{1,0:T(8,128)(2,1)}, f32[512,768]{1,0:T(8,128)S(1)}, bf16[512,768...) custom-call(s32[3]{0:T(128)S(1)} %pad_add_fusion.meta_ref, ...), custom_call_target="tpu_custom_call" | custom-call | flops 8800000000 | bytes 1024 | tf_op jit(solution)/shard_map/astern/pallas_call | solution.py:84
  98.6 2.4 inner_norm.2
  105.7 1.6 collective-permute-done.15
  108.0 1.9 add_convert_fusion
  110.3 1.6 add_convert_fusion.1
  112.3 2.8 %collective-permute-start.20 = (bf16[384,768]{1,0:T(8,128)(2,1)S(1)}, bf16[384,768]{1,0:T(8,128)(2,1)S(1)}, u32[]{:S(2)}, u32[]{:S(2)}) collective-permute-start(bf16[384,768]{1,0:T(8,128)(2,1)S(1)} %get-tuple-element.314), channel_id=1, source_target_pairs={{0,8},{4,12},{8,0},{12,4},{16,24},{20,28},{24,16},{28,20},{1,9},{5... | collective-permute-start | bytes 1769480 | tf_op jit(solution)/shard_map/ppermute | solution.py:584
  115.2 11.1 %attend_backward.2 = (bf16[1024,256]{1,0:T(8,128)(2,1)S(1)}, bf16[1024,256]{1,0:T(8,128)(2,1)S(1)}, bf16[1024,256]{1,0:T(8,128)(2,1)S(1)}) custom-call(s32[3]{0:T(128)S(1)} %pad_add_fusion.meta_ref, bf16[2048,256]{1,0:T(8,128)(2,1)S(1)} %copy-done.36, bf16[2048,256]{1,0:T(8,128)(2,1)S(1)} %copy-done.38, bf16[2048,256]{1,0:T(8,128)(2,1)S(1)} %copy-done.40, ...), custom_call_target="tpu_custom_call" | custom-call | flops 13200000000 | bytes 1024 | tf_op jit(solution)/shard_map/attend_backward/pallas_call | solution.py:84
  130.4 3.1 %inner_norm.3 = (f32[512,768]{1,0:T(8,128)S(1)}, bf16[192,512]{1,0:T(8,128)(2,1)S(1)}, bf16[192,512]{1,0:T(8,128)(2,1)S(1)}, bf16[256,768]{1,0:T(8,128)(2,1)S(1)...) custom-call(s32[3]{0:T(128)S(1)} %pad_add_fusion.meta_ref, f32[512,768]{1,0:T(8,128)S(1)} %copy-done.30, ...), custom_call_target="tpu_custom_call" | custom-call | flops 3300000000 | bytes 1024 | tf_op jit(solution)/shard_map/inner_norm/pallas_call | solution.py:84
  133.5 1.8 collective-permute-start.24
  135.3 4.8 %entry_back.2 = (bf16[512,768]{1,0:T(8,128)(2,1)S(1)}, bf16[512,768]{1,0:T(8,128)(2,1)S(1)}, f32[576,768]{1,0:T(8,128)S(1)}) custom-call(s32[3]{0:T(128)S(1)} %pad_add_fusion.meta_ref, bf16[2048,768]{1,0:T(8,128)(2,1)S(1)} %copy-done.4, bf16[1024,256]{1,0:T(8,128)(2,1)S(1)} %get-tuple-element.206.dq_ref, bf16[1024,256]{1,0:T(8,128)(2,1)S(1)} %get-tuple-element.222.dk_ref, ...), custom_call_target="tpu_custom_call" | custom-call | flops 5500000256 | bytes 1024 | tf_op jit(solution)/shard_map/entry_back/pallas_call | solution.py:84
  140.7 1.8 collective-permute-start.23
  142.6 7.1 %collective-permute-done.23 = bf16[192,768]{1,0:T(8,128)(2,1)S(1)} collective-permute-done((bf16[192,768]{1,0:T(8,128)(2,1)S(1)}, bf16[192,768]{1,0:T(8,128)(2,1)S(1)}, u32[]{:S(2)}, u32[]{:S(2)}) %collective-permute-start.23) | collective-permute-done | bytes 294944 | tf_op jit(solution)/shard_map/ppermute | solution.py:584
  149.7 2.6 collective-permute-start.28
  156.2 6.4 %attend_backward.3 = (bf16[1024,256]{1,0:T(8,128)(2,1)S(1)}, bf16[1024,256]{1,0:T(8,128)(2,1)S(1)}, bf16[1024,256]{1,0:T(8,128)(2,1)S(1)}) custom-call(s32[3]{0:T(128)S(1)} %pad_add_fusion.meta_ref, bf16[2048,256]{1,0:T(8,128)(2,1)S(1)} %copy-done.36, bf16[2048,256]{1,0:T(8,128)(2,1)S(1)} %copy-done.38, bf16[2048,256]{1,0:T(8,128)(2,1)S(1)} %copy-done.40, ...), custom_call_target="tpu_custom_call" | custom-call | flops 13200000000 | bytes 1024 | tf_op jit(solution)/shard_map/attend_backward/pallas_call | solution.py:84
  163.3 1.8 collective-permute-done.27
  165.2 2.9 %collective-permute-start.37 = (bf16[64,768]{1,0:T(8,128)(2,1)S(1)}, bf16[64,768]{1,0:T(8,128)(2,1)S(1)}, u32[]{:S(2)}, u32[]{:S(2)}) collective-permute-start(bf16[64,768]{1,0:T(8,128)(2,1)S(1)} %get-tuple-element.351), channel_id=1, source_target_pairs={{0,8},{4,12},{8,0},{12,4},{16,24},{20,28},{24,16},{28,20},{1,9},{5... | collective-permute-start | bytes 294920 | tf_op jit(solution)/shard_map/ppermute | solution.py:584
  168.8 2.5 collective-permute-start.35
  172.8 4.6 %entry_back.3 = (bf16[512,768]{1,0:T(8,128)(2,1)S(1)}, bf16[512,768]{1,0:T(8,128)(2,1)S(1)}, bf16[576,768]{1,0:T(8,128)(2,1)S(1)}) custom-call(s32[3]{0:T(128)S(1)} %pad_add_fusion.meta_ref, bf16[2048,768]{1,0:T(8,128)(2,1)S(1)} %copy-done.4, bf16[1024,256]{1,0:T(8,128)(2,1)S(1)} %get-tuple-element.236.dq_ref, ...), custom_call_target="tpu_custom_call" | custom-call | flops 5500000256 | bytes 1024 | tf_op jit(solution)/shard_map/entry_back/pallas_call | solution.py:84
  178.0 1.7 collective-permute-done.36
  179.7 2.3 collective-permute-done.35
  182.6 4.8 %collective-permute-done.38 = bf16[288,768]{1,0:T(8,128)(2,1)S(1)} collective-permute-done((bf16[288,768]{1,0:T(8,128)(2,1)S(1)}, bf16[288,768]{1,0:T(8,128)(2,1)S(1)}, u32[]{:S(2)}, u32[]{:S(2)}) %collective-permute-start.38) | collective-permute-done | bytes 442400 | tf_op jit(solution)/shard_map/ppermute | solution.py:584
  187.8 2.5 collective-permute-start.43
  190.3 1.7 collective-permute-start.44
  194.1 6.1 %collective-permute-done.41 = bf16[32,768]{1,0:T(8,128)(2,1)S(1)} collective-permute-done((bf16[32,768]{1,0:T(8,128)(2,1)S(1)}, bf16[32,768]{1,0:T(8,128)(2,1)S(1)}, u32[]{:S(2)}, u32[]{:S(2)}) %collective-permute-start.41) | collective-permute-done | bytes 49184 | tf_op jit(solution)/shard_map/ppermute | solution.py:584
  201.8 5.8 %collective-permute-done.39 = bf16[192,768]{1,0:T(8,128)(2,1)S(1)} collective-permute-done((bf16[192,768]{1,0:T(8,128)(2,1)S(1)}, bf16[192,768]{1,0:T(8,128)(2,1)S(1)}, u32[]{:S(2)}, u32[]{:S(2)}) %collective-permute-start.39) | collective-permute-done | bytes 294944 | tf_op jit(solution)/shard_map/ppermute | solution.py:584
  207.8 10.4 %collective-permute-done.33 = bf16[512,768]{1,0:T(8,128)(2,1)S(1)} collective-permute-done((bf16[512,768]{1,0:T(8,128)(2,1)S(1)}, bf16[512,768]{1,0:T(8,128)(2,1)S(1)}, u32[]{:S(2)}, u32[]{:S(2)}) %collective-permute-start.33) | collective-permute-done | bytes 786464 | tf_op jit(solution)/shard_map/ppermute | solution.py:581
  218.3 1.7 collective-permute-start.48
  221.0 1.7 collective-permute-start.50
  225.8 6.5 %collective-permute-done.47 = bf16[32,768]{1,0:T(8,128)(2,1)S(1)} collective-permute-done((bf16[32,768]{1,0:T(8,128)(2,1)S(1)}, bf16[32,768]{1,0:T(8,128)(2,1)S(1)}, u32[]{:S(2)}, u32[]{:S(2)}) %collective-permute-start.47) | collective-permute-done | bytes 49184 | tf_op jit(solution)/shard_map/ppermute | solution.py:584
  233.0 7.9 %collective-permute-done.46 = bf16[384,768]{1,0:T(8,128)(2,1)S(1)} collective-permute-done((bf16[384,768]{1,0:T(8,128)(2,1)S(1)}, bf16[384,768]{1,0:T(8,128)(2,1)S(1)}, u32[]{:S(2)}, u32[]{:S(2)}) %collective-permute-start.46) | collective-permute-done | bytes 589856 | tf_op jit(solution)/shard_map/ppermute | solution.py:584
  240.9 4.8 %collective-permute-done.45 = bf16[384,768]{1,0:T(8,128)(2,1)S(1)} collective-permute-done((bf16[384,768]{1,0:T(8,128)(2,1)S(1)}, bf16[384,768]{1,0:T(8,128)(2,1)S(1)}, u32[]{:S(2)}, u32[]{:S(2)}) %collective-permute-start.45) | collective-permute-done | bytes 589856 | tf_op jit(solution)/shard_map/ppermute | solution.py:584
  247.0 4.3 %place.2 = bf16[2048,768]{1,0:T(8,128)(2,1)} custom-call(s32[3]{0:T(128)S(1)} %pad_add_fusion.meta_ref, bf16[512,768]{1,0:T(8,128)(2,1)S(1)} %get-tuple-element.175.refs_0_, bf16[512,768]{1,0:T(8,128)(2,1)} %collective-permute-done.16.refs_1_, bf16[512,768]{1,0:T(8,128)(2,1)} %get-tuple-element.186.refs_2_, bf16[512,768]{1,0:T(8,128)(2,1)} %collective-permute-done.17.refs_3_), custom_call_target="tpu_custom_call" | custom-call | flops 3300000000 | bytes 1024 | tf_op jit(solution)/shard_map/place/pallas_call | solution.py:84
  251.4 4.9 %collective-permute-done.52 = bf16[288,768]{1,0:T(8,128)(2,1)S(1)} collective-permute-done((bf16[288,768]{1,0:T(8,128)(2,1)S(1)}, bf16[288,768]{1,0:T(8,128)(2,1)S(1)}, u32[]{:S(2)}, u32[]{:S(2)}) %collective-permute-start.52) | collective-permute-done | bytes 442400 | tf_op jit(solution)/shard_map/ppermute | solution.py:584
  256.8 2.7 %place.3 = bf16[2048,768]{1,0:T(8,128)(2,1)} custom-call(s32[3]{0:T(128)S(1)} %pad_add_fusion.meta_ref, bf16[512,768]{1,0:T(8,128)(2,1)S(1)} %add_convert_fusion.3.refs_0_, bf16[512,768]{1,0:T(8,128)(2,1)S(1)} %collective-permute-done.32.refs_1_, bf16[512,768]{1,0:T(8,128)(2,1)S(1)} %add_convert_fusion.2.refs_2_, ...), custom_call_target="tpu_custom_call" | custom-call | flops 3300000000 | bytes 1024 | tf_op jit(solution)/shard_map/place/pallas_call | solution.py:84
  259.5 2.7 collective-permute-done.53
  (270 shorter events, 49.9 us)
Async XLA Ops:
  0.6 21.2 %collective-permute-start = (bf16[192,768]{1,0:T(8,128)(2,1)}, bf16[192,768]{1,0:T(8,128)(2,1)S(1)}, u32[]{:S(2)}, u32[]{:S(2)}) collective-permute-start(bf16[192,768]{1,0:T(8,128)(2,1)} %w0.7), channel_id=1, source_target_pairs={{0,1},{1,0},{2,3},{3,2},{4,5},{5,4},{6,7},{7,6},{8,9},{9,8},{10,11... | collective-permute-start | bytes 884744 | tf_op jit(solution)/shard_map/ppermute | solution.py:581
  1.2 20.9 %collective-permute-start.1 = (bf16[192,768]{1,0:T(8,128)(2,1)}, bf16[192,768]{1,0:T(8,128)(2,1)S(1)}, u32[]{:S(2)}, u32[]{:S(2)}) collective-permute-start(bf16[192,768]{1,0:T(8,128)(2,1)} %w0.7), channel_id=1, source_target_pairs={{0,2},{1,3},{2,0},{3,1},{4,6},{5,7},{6,4},{7,5},{8,10},{9,11},{10,... | collective-permute-start | bytes 884744 | tf_op jit(solution)/shard_map/ppermute | solution.py:581
  3.7 20.1 %collective-permute-start.2 = (bf16[192,768]{1,0:T(8,128)(2,1)}, bf16[192,768]{1,0:T(8,128)(2,1)S(1)}, u32[]{:S(2)}, u32[]{:S(2)}) collective-permute-start(bf16[192,768]{1,0:T(8,128)(2,1)} %w0.7), channel_id=1, source_target_pairs={{0,3},{1,2},{2,1},{3,0},{4,7},{5,6},{6,5},{7,4},{8,11},{9,10},{10,... | collective-permute-start | bytes 884744 | tf_op jit(solution)/shard_map/ppermute | solution.py:581
  3.8 20.4 %collective-permute-start.3 = (bf16[768,768]{1,0:T(8,128)(2,1)}, bf16[768,768]{1,0:T(8,128)(2,1)S(1)}, u32[]{:S(2)}, u32[]{:S(2)}) collective-permute-start(bf16[768,768]{1,0:T(8,128)(2,1)} %ua_ref.7), channel_id=1, source_target_pairs={{0,1},{1,0},{2,3},{3,2},{4,5},{5,4},{6,7},{7,6},{8,9},{9,8},{10,11... | collective-permute-start | bytes 3538952 | tf_op jit(solution)/shard_map/ppermute | solution.py:581
  3.9 20.2 %collective-permute-start.4 = (bf16[768,768]{1,0:T(8,128)(2,1)}, bf16[768,768]{1,0:T(8,128)(2,1)}, u32[]{:S(2)}, u32[]{:S(2)}) collective-permute-start(bf16[768,768]{1,0:T(8,128)(2,1)} %da_ref.7), channel_id=1, source_target_pairs={{0,1},{1,0},{2,3},{3,2},{4,5},{5,4},{6,7},{7,6},{8,9},{9,8},{10,11... | collective-permute-start | bytes 3538952 | tf_op jit(solution)/shard_map/ppermute | solution.py:581
  21.9 13.0 %collective-permute-start.5 = (bf16[192,512]{1,0:T(8,128)(2,1)S(1)}, bf16[192,512]{1,0:T(8,128)(2,1)S(1)}, u32[]{:S(2)}, u32[]{:S(2)}) collective-permute-start(bf16[192,512]{1,0:T(8,128)(2,1)S(1)} %get-tuple-element.166), channel_id=1, source_target_pairs={{0,1},{1,0},{2,3},{3,2},{4,5},{5,4},{6,7},{7,6},{8,9},{9,8},{10,11... | collective-permute-start | bytes 589832 | tf_op jit(solution)/shard_map/ppermute | solution.py:581
  22.1 12.8 %collective-permute-start.7 = (bf16[192,512]{1,0:T(8,128)(2,1)S(1)}, bf16[192,512]{1,0:T(8,128)(2,1)S(1)}, u32[]{:S(2)}, u32[]{:S(2)}) collective-permute-start(bf16[192,512]{1,0:T(8,128)(2,1)S(1)} %get-tuple-element.166), channel_id=1, source_target_pairs={{0,3},{1,2},{2,1},{3,0},{4,7},{5,6},{6,5},{7,4},{8,11},{9,10},{10,... | collective-permute-start | bytes 589832 | tf_op jit(solution)/shard_map/ppermute | solution.py:581
  23.8 10.2 %collective-permute-start.6 = (bf16[192,512]{1,0:T(8,128)(2,1)S(1)}, bf16[192,512]{1,0:T(8,128)(2,1)S(1)}, u32[]{:S(2)}, u32[]{:S(2)}) collective-permute-start(bf16[192,512]{1,0:T(8,128)(2,1)S(1)} %get-tuple-element.162.a0), channel_id=1, source_target_pairs={{0,2},{1,3},{2,0},{3,1},{4,6},{5,7},{6,4},{7,5},{8,10},{9,11},{10,... | collective-permute-start | bytes 589832 | tf_op jit(solution)/shard_map/ppermute | solution.py:581
  29.9 14.8 %collective-permute-start.9 = (bf16[192,512]{1,0:T(8,128)(2,1)S(1)}, bf16[192,512]{1,0:T(8,128)(2,1)S(1)}, u32[]{:S(2)}, u32[]{:S(2)}) collective-permute-start(bf16[192,512]{1,0:T(8,128)(2,1)S(1)} %get-tuple-element.164.a0), channel_id=1, source_target_pairs={{0,2},{1,3},{2,0},{3,1},{4,6},{5,7},{6,4},{7,5},{8,10},{9,11},{10,... | collective-permute-start | bytes 589832 | tf_op jit(solution)/shard_map/ppermute | solution.py:581
  31.7 13.1 %collective-permute-start.8 = (bf16[192,512]{1,0:T(8,128)(2,1)S(1)}, bf16[192,512]{1,0:T(8,128)(2,1)S(1)}, u32[]{:S(2)}, u32[]{:S(2)}) collective-permute-start(bf16[192,512]{1,0:T(8,128)(2,1)S(1)} %get-tuple-element.169), channel_id=1, source_target_pairs={{0,1},{1,0},{2,3},{3,2},{4,5},{5,4},{6,7},{7,6},{8,9},{9,8},{10,11... | collective-permute-start | bytes 589832 | tf_op jit(solution)/shard_map/ppermute | solution.py:581
  34.0 10.8 %collective-permute-start.10 = (bf16[192,512]{1,0:T(8,128)(2,1)S(1)}, bf16[192,512]{1,0:T(8,128)(2,1)S(1)}, u32[]{:S(2)}, u32[]{:S(2)}) collective-permute-start(bf16[192,512]{1,0:T(8,128)(2,1)S(1)} %get-tuple-element.169), channel_id=1, source_target_pairs={{0,3},{1,2},{2,1},{3,0},{4,7},{5,6},{6,5},{7,4},{8,11},{9,10},{10,... | collective-permute-start | bytes 589832 | tf_op jit(solution)/shard_map/ppermute | solution.py:581
  43.9 20.5 %collective-permute-start.11 = (bf16[512,768]{1,0:T(8,128)(2,1)S(1)}, bf16[512,768]{1,0:T(8,128)(2,1)S(1)}, u32[]{:S(2)}, u32[]{:S(2)}) collective-permute-start(bf16[512,768]{1,0:T(8,128)(2,1)S(1)} %get-tuple-element.173), channel_id=1, source_target_pairs={{0,2},{1,3},{2,0},{3,1},{4,6},{5,7},{6,4},{7,5},{8,10},{9,11},{10,... | collective-permute-start | bytes 2359304 | tf_op jit(solution)/shard_map/ppermute | solution.py:581
  55.0 26.1 %collective-permute-start.12 = (bf16[512,768]{1,0:T(8,128)(2,1)S(1)}, bf16[512,768]{1,0:T(8,128)(2,1)S(1)}, u32[]{:S(2)}, u32[]{:S(2)}) collective-permute-start(bf16[512,768]{1,0:T(8,128)(2,1)S(1)} %get-tuple-element.178), channel_id=1, source_target_pairs={{0,2},{1,3},{2,0},{3,1},{4,6},{5,7},{6,4},{7,5},{8,10},{9,11},{10,... | collective-permute-start | bytes 2359304 | tf_op jit(solution)/shard_map/ppermute | solution.py:581
  73.5 25.2 %collective-permute-start.13 = (bf16[512,768]{1,0:T(8,128)(2,1)S(1)}, bf16[512,768]{1,0:T(8,128)(2,1)S(1)}, u32[]{:S(2)}, u32[]{:S(2)}) collective-permute-start(bf16[512,768]{1,0:T(8,128)(2,1)S(1)} %get-tuple-element.189), channel_id=1, source_target_pairs={{0,2},{1,3},{2,0},{3,1},{4,6},{5,7},{6,4},{7,5},{8,10},{9,11},{10,... | collective-permute-start | bytes 2359304 | tf_op jit(solution)/shard_map/ppermute | solution.py:581
  104.7 7.4 %collective-permute-start.16 = (bf16[512,768]{1,0:T(8,128)(2,1)S(1)}, bf16[512,768]{1,0:T(8,128)(2,1)}, u32[]{:S(2)}, u32[]{:S(2)}) collective-permute-start(bf16[512,768]{1,0:T(8,128)(2,1)S(1)} %get-tuple-element.175.refs_0_), channel_id=1, source_target_pairs={{0,1},{1,0},{2,3},{3,2},{4,5},{5,4},{6,7},{7,6},{8,9},{9,8},{10,11... | collective-permute-start | bytes 2359304 | tf_op jit(solution)/shard_map/ppermute | solution.py:581
  105.2 9.9 %collective-permute-start.18 = (bf16[192,512]{1,0:T(8,128)(2,1)}, bf16[192,512]{1,0:T(8,128)(2,1)S(1)}, u32[]{:S(2)}, u32[]{:S(2)}) collective-permute-start(bf16[192,512]{1,0:T(8,128)(2,1)} %copy-done.25), channel_id=1, source_target_pairs={{0,1},{1,0},{2,3},{3,2},{4,5},{5,4},{6,7},{7,6},{8,9},{9,8},{10,11... | collective-permute-start | bytes 589832 | tf_op jit(solution)/shard_map/ppermute | solution.py:581
  107.2 21.6 %collective-permute-start.21 = (bf16[512,768]{1,0:T(8,128)(2,1)}, bf16[512,768]{1,0:T(8,128)(2,1)S(1)}, u32[]{:S(2)}, u32[]{:S(2)}) collective-permute-start(bf16[512,768]{1,0:T(8,128)(2,1)} %copy-done.9), channel_id=1, source_target_pairs={{0,2},{1,3},{2,0},{3,1},{4,6},{5,7},{6,4},{7,5},{8,10},{9,11},{10,... | collective-permute-start | bytes 2359304 | tf_op jit(solution)/shard_map/ppermute | solution.py:581
  112.1 15.4 %collective-permute-start.19 = (bf16[384,768]{1,0:T(8,128)(2,1)S(1)}, bf16[384,768]{1,0:T(8,128)(2,1)S(1)}, u32[]{:S(2)}, u32[]{:S(2)}) collective-permute-start(bf16[384,768]{1,0:T(8,128)(2,1)S(1)} %get-tuple-element.316), channel_id=1, source_target_pairs={{0,4},{4,0},{8,12},{12,8},{16,20},{20,16},{24,28},{28,24},{1,5},{5... | collective-permute-start | bytes 1769480 | tf_op jit(solution)/shard_map/ppermute | solution.py:584
  112.3 16.1 %collective-permute-start.20 = (bf16[384,768]{1,0:T(8,128)(2,1)S(1)}, bf16[384,768]{1,0:T(8,128)(2,1)S(1)}, u32[]{:S(2)}, u32[]{:S(2)}) collective-permute-start(bf16[384,768]{1,0:T(8,128)(2,1)S(1)} %get-tuple-element.314), channel_id=1, source_target_pairs={{0,8},{4,12},{8,0},{12,4},{16,24},{20,28},{24,16},{28,20},{1,9},{5... | collective-permute-start | bytes 1769480 | tf_op jit(solution)/shard_map/ppermute | solution.py:584
  133.5 9.0 %collective-permute-start.24 = (bf16[192,768]{1,0:T(8,128)(2,1)S(1)}, bf16[192,768]{1,0:T(8,128)(2,1)S(1)}, u32[]{:S(2)}, u32[]{:S(2)}) collective-permute-start(bf16[192,768]{1,0:T(8,128)(2,1)S(1)} %get-tuple-element.329), channel_id=1, source_target_pairs={{0,4},{4,0},{8,12},{12,8},{16,20},{20,16},{24,28},{28,24},{1,5},{5... | collective-permute-start | bytes 884744 | tf_op jit(solution)/shard_map/ppermute | solution.py:584
  140.0 14.4 %collective-permute-start.22 = (bf16[512,768]{1,0:T(8,128)(2,1)S(1)}, bf16[512,768]{1,0:T(8,128)(2,1)S(1)}, u32[]{:S(2)}, u32[]{:S(2)}) collective-permute-start(bf16[512,768]{1,0:T(8,128)(2,1)S(1)} %get-tuple-element.224), channel_id=1, source_target_pairs={{0,1},{1,0},{2,3},{3,2},{4,5},{5,4},{6,7},{7,6},{8,9},{9,8},{10,11... | collective-permute-start | bytes 2359304 | tf_op jit(solution)/shard_map/ppermute | solution.py:581
  140.1 12.7 %collective-permute-start.25 = (bf16[256,768]{1,0:T(8,128)(2,1)S(1)}, bf16[256,768]{1,0:T(8,128)(2,1)S(1)}, u32[]{:S(2)}, u32[]{:S(2)}) collective-permute-start(bf16[256,768]{1,0:T(8,128)(2,1)S(1)} %get-tuple-element.230), channel_id=1, source_target_pairs={{0,1},{1,0},{2,3},{3,2},{4,5},{5,4},{6,7},{7,6},{8,9},{9,8},{10,11... | collective-permute-start | bytes 1179656 | tf_op jit(solution)/shard_map/ppermute | solution.py:581
  140.7 9.1 %collective-permute-start.23 = (bf16[192,768]{1,0:T(8,128)(2,1)S(1)}, bf16[192,768]{1,0:T(8,128)(2,1)S(1)}, u32[]{:S(2)}, u32[]{:S(2)}) collective-permute-start(bf16[192,768]{1,0:T(8,128)(2,1)S(1)} %get-tuple-element.331), channel_id=1, source_target_pairs={{0,8},{4,12},{8,0},{12,4},{16,24},{20,28},{24,16},{28,20},{1,9},{5... | collective-permute-start | bytes 884744 | tf_op jit(solution)/shard_map/ppermute | solution.py:584
  142.5 13.7 %collective-permute-start.26 = (bf16[192,512]{1,0:T(8,128)(2,1)S(1)}, bf16[192,512]{1,0:T(8,128)(2,1)S(1)}, u32[]{:S(2)}, u32[]{:S(2)}) collective-permute-start(bf16[192,512]{1,0:T(8,128)(2,1)S(1)} %get-tuple-element.233), channel_id=1, source_target_pairs={{0,1},{1,0},{2,3},{3,2},{4,5},{5,4},{6,7},{7,6},{8,9},{9,8},{10,11... | collective-permute-start | bytes 589832 | tf_op jit(solution)/shard_map/ppermute | solution.py:581
  149.7 13.5 %collective-permute-start.28 = (bf16[96,768]{1,0:T(8,128)(2,1)S(1)}, bf16[96,768]{1,0:T(8,128)(2,1)S(1)}, u32[]{:S(2)}, u32[]{:S(2)}) collective-permute-start(bf16[96,768]{1,0:T(8,128)(2,1)S(1)} %get-tuple-element.345), channel_id=1, source_target_pairs={{0,16},{4,20},{8,24},{12,28},{16,0},{20,4},{24,8},{28,12},{1,17},{... | collective-permute-start | bytes 442376 | tf_op jit(solution)/shard_map/ppermute | solution.py:584
  152.4 12.7 %collective-permute-start.27 = (bf16[96,768]{1,0:T(8,128)(2,1)S(1)}, bf16[96,768]{1,0:T(8,128)(2,1)S(1)}, u32[]{:S(2)}, u32[]{:S(2)}) collective-permute-start(bf16[96,768]{1,0:T(8,128)(2,1)S(1)} %get-tuple-element.347), channel_id=1, source_target_pairs={{0,16},{4,20},{8,24},{12,28},{16,0},{20,4},{24,8},{28,12},{1,17},{... | collective-permute-start | bytes 442376 | tf_op jit(solution)/shard_map/ppermute | solution.py:584
  153.0 9.5 %collective-permute-start.29 = (bf16[128,768]{1,0:T(8,128)(2,1)S(1)}, bf16[128,768]{1,0:T(8,128)(2,1)S(1)}, u32[]{:S(2)}, u32[]{:S(2)}) collective-permute-start(bf16[128,768]{1,0:T(8,128)(2,1)S(1)} %get-tuple-element.339), channel_id=1, source_target_pairs={{0,4},{4,0},{8,12},{12,8},{16,20},{20,16},{24,28},{28,24},{1,5},{5... | collective-permute-start | bytes 589832 | tf_op jit(solution)/shard_map/ppermute | solution.py:584
  154.6 18.2 %collective-permute-start.30 = (bf16[512,768]{1,0:T(8,128)(2,1)S(1)}, bf16[512,768]{1,0:T(8,128)(2,1)S(1)}, u32[]{:S(2)}, u32[]{:S(2)}) collective-permute-start(bf16[512,768]{1,0:T(8,128)(2,1)S(1)} %fusion), channel_id=1, source_target_pairs={{0,2},{1,3},{2,0},{3,1},{4,6},{5,7},{6,4},{7,5},{8,10},{9,11},{10,... | collective-permute-start | bytes 2359304 | tf_op jit(solution)/shard_map/ppermute | solution.py:581
  165.2 12.8 %collective-permute-start.37 = (bf16[64,768]{1,0:T(8,128)(2,1)S(1)}, bf16[64,768]{1,0:T(8,128)(2,1)S(1)}, u32[]{:S(2)}, u32[]{:S(2)}) collective-permute-start(bf16[64,768]{1,0:T(8,128)(2,1)S(1)} %get-tuple-element.351), channel_id=1, source_target_pairs={{0,8},{4,12},{8,0},{12,4},{16,24},{20,28},{24,16},{28,20},{1,9},{5... | collective-permute-start | bytes 294920 | tf_op jit(solution)/shard_map/ppermute | solution.py:584
  168.2 11.5 %collective-permute-start.36 = (bf16[96,768]{1,0:T(8,128)(2,1)S(1)}, bf16[96,768]{1,0:T(8,128)(2,1)S(1)}, u32[]{:S(2)}, u32[]{:S(2)}) collective-permute-start(bf16[96,768]{1,0:T(8,128)(2,1)S(1)} %add_convert_fusion.11), channel_id=1, source_target_pairs={{0,16},{4,20},{8,24},{12,28},{16,0},{20,4},{24,8},{28,12},{1,17},{... | collective-permute-start | bytes 442376 | tf_op jit(solution)/shard_map/ppermute | solution.py:584
  168.8 13.2 %collective-permute-start.35 = (bf16[96,768]{1,0:T(8,128)(2,1)S(1)}, bf16[96,768]{1,0:T(8,128)(2,1)S(1)}, u32[]{:S(2)}, u32[]{:S(2)}) collective-permute-start(bf16[96,768]{1,0:T(8,128)(2,1)S(1)} %add_convert_fusion.12), channel_id=1, source_target_pairs={{0,16},{4,20},{8,24},{12,28},{16,0},{20,4},{24,8},{28,12},{1,17},{... | collective-permute-start | bytes 442376 | tf_op jit(solution)/shard_map/ppermute | solution.py:584
  177.5 9.9 %collective-permute-start.38 = (bf16[288,768]{1,0:T(8,128)(2,1)S(1)}, bf16[288,768]{1,0:T(8,128)(2,1)S(1)}, u32[]{:S(2)}, u32[]{:S(2)}) collective-permute-start(bf16[288,768]{1,0:T(8,128)(2,1)S(1)} %get-tuple-element.323), channel_id=1, source_target_pairs={{0,4},{4,0},{8,12},{12,8},{16,20},{20,16},{24,28},{28,24},{1,5},{5... | collective-permute-start | bytes 1327112 | tf_op jit(solution)/shard_map/ppermute | solution.py:584
  187.6 12.6 %collective-permute-start.42 = (bf16[72,768]{1,0:T(8,128)(2,1)S(1)}, bf16[72,768]{1,0:T(8,128)(2,1)S(1)}, u32[]{:S(2)}, u32[]{:S(2)}) collective-permute-start(bf16[72,768]{1,0:T(8,128)(2,1)S(1)} %get-tuple-element.335), channel_id=1, source_target_pairs={{0,8},{4,12},{8,0},{12,4},{16,24},{20,28},{24,16},{28,20},{1,9},{5... | collective-permute-start | bytes 331784 | tf_op jit(solution)/shard_map/ppermute | solution.py:584
  187.8 13.9 %collective-permute-start.43 = (bf16[72,768]{1,0:T(8,128)(2,1)S(1)}, bf16[72,768]{1,0:T(8,128)(2,1)S(1)}, u32[]{:S(2)}, u32[]{:S(2)}) collective-permute-start(bf16[72,768]{1,0:T(8,128)(2,1)S(1)} %get-tuple-element.334), channel_id=1, source_target_pairs={{0,16},{4,20},{8,24},{12,28},{16,0},{20,4},{24,8},{28,12},{1,17},{... | collective-permute-start | bytes 331784 | tf_op jit(solution)/shard_map/ppermute | solution.py:584
  190.3 11.4 %collective-permute-start.44 = (bf16[72,768]{1,0:T(8,128)(2,1)S(1)}, bf16[72,768]{1,0:T(8,128)(2,1)S(1)}, u32[]{:S(2)}, u32[]{:S(2)}) collective-permute-start(bf16[72,768]{1,0:T(8,128)(2,1)S(1)} %get-tuple-element.333), channel_id=1, source_target_pairs={{0,24},{4,28},{8,16},{12,20},{16,8},{20,12},{24,0},{28,4},{1,25},{... | collective-permute-start | bytes 331784 | tf_op jit(solution)/shard_map/ppermute | solution.py:584
  192.1 8.1 %collective-permute-start.41 = (bf16[32,768]{1,0:T(8,128)(2,1)S(1)}, bf16[32,768]{1,0:T(8,128)(2,1)S(1)}, u32[]{:S(2)}, u32[]{:S(2)}) collective-permute-start(bf16[32,768]{1,0:T(8,128)(2,1)S(1)} %get-tuple-element.355), channel_id=1, source_target_pairs={{0,16},{4,20},{8,24},{12,28},{16,0},{20,4},{24,8},{28,12},{1,17},{... | collective-permute-start | bytes 147464 | tf_op jit(solution)/shard_map/ppermute | solution.py:584
  193.6 8.2 %collective-permute-start.40 = (bf16[192,768]{1,0:T(8,128)(2,1)S(1)}, bf16[192,768]{1,0:T(8,128)(2,1)S(1)}, u32[]{:S(2)}, u32[]{:S(2)}) collective-permute-start(bf16[192,768]{1,0:T(8,128)(2,1)S(1)} %pad_maximum_fusion.7), channel_id=1, source_target_pairs={{0,4},{4,0},{8,12},{12,8},{16,20},{20,16},{24,28},{28,24},{1,5},{5... | collective-permute-start | bytes 884744 | tf_op jit(solution)/shard_map/ppermute | solution.py:584
  200.2 7.5 %collective-permute-start.39 = (bf16[192,768]{1,0:T(8,128)(2,1)S(1)}, bf16[192,768]{1,0:T(8,128)(2,1)S(1)}, u32[]{:S(2)}, u32[]{:S(2)}) collective-permute-start(bf16[192,768]{1,0:T(8,128)(2,1)S(1)} %pad_maximum_fusion.6), channel_id=1, source_target_pairs={{0,8},{4,12},{8,0},{12,4},{16,24},{20,28},{24,16},{28,20},{1,9},{5... | collective-permute-start | bytes 884744 | tf_op jit(solution)/shard_map/ppermute | solution.py:584
  200.2 18.0 %collective-permute-start.33 = (bf16[512,768]{1,0:T(8,128)(2,1)S(1)}, bf16[512,768]{1,0:T(8,128)(2,1)S(1)}, u32[]{:S(2)}, u32[]{:S(2)}) collective-permute-start(bf16[512,768]{1,0:T(8,128)(2,1)S(1)} %fusion.1), channel_id=1, source_target_pairs={{0,2},{1,3},{2,0},{3,1},{4,6},{5,7},{6,4},{7,5},{8,10},{9,11},{10,... | collective-permute-start | bytes 2359304 | tf_op jit(solution)/shard_map/ppermute | solution.py:581
  218.3 14.1 %collective-permute-start.48 = (bf16[72,768]{1,0:T(8,128)(2,1)S(1)}, bf16[72,768]{1,0:T(8,128)(2,1)S(1)}, u32[]{:S(2)}, u32[]{:S(2)}) collective-permute-start(bf16[72,768]{1,0:T(8,128)(2,1)S(1)} %add_convert_fusion.13), channel_id=1, source_target_pairs={{0,8},{4,12},{8,0},{12,4},{16,24},{20,28},{24,16},{28,20},{1,9},{5... | collective-permute-start | bytes 331784 | tf_op jit(solution)/shard_map/ppermute | solution.py:584
  220.0 12.4 %collective-permute-start.49 = (bf16[72,768]{1,0:T(8,128)(2,1)S(1)}, bf16[72,768]{1,0:T(8,128)(2,1)S(1)}, u32[]{:S(2)}, u32[]{:S(2)}) collective-permute-start(bf16[72,768]{1,0:T(8,128)(2,1)S(1)} %add_convert_fusion.13), channel_id=1, source_target_pairs={{0,16},{4,20},{8,24},{12,28},{16,0},{20,4},{24,8},{28,12},{1,17},{... | collective-permute-start | bytes 331784 | tf_op jit(solution)/shard_map/ppermute | solution.py:584
  221.0 11.9 %collective-permute-start.50 = (bf16[72,768]{1,0:T(8,128)(2,1)S(1)}, bf16[72,768]{1,0:T(8,128)(2,1)S(1)}, u32[]{:S(2)}, u32[]{:S(2)}) collective-permute-start(bf16[72,768]{1,0:T(8,128)(2,1)S(1)} %add_convert_fusion.13), channel_id=1, source_target_pairs={{0,24},{4,28},{8,16},{12,20},{16,8},{20,12},{24,0},{28,4},{1,25},{... | collective-permute-start | bytes 331784 | tf_op jit(solution)/shard_map/ppermute | solution.py:584
  222.6 9.6 %collective-permute-start.47 = (bf16[32,768]{1,0:T(8,128)(2,1)S(1)}, bf16[32,768]{1,0:T(8,128)(2,1)S(1)}, u32[]{:S(2)}, u32[]{:S(2)}) collective-permute-start(bf16[32,768]{1,0:T(8,128)(2,1)S(1)} %add_convert_fusion.15), channel_id=1, source_target_pairs={{0,16},{4,20},{8,24},{12,28},{16,0},{20,4},{24,8},{28,12},{1,17},{... | collective-permute-start | bytes 147464 | tf_op jit(solution)/shard_map/ppermute | solution.py:584
  224.2 16.7 %collective-permute-start.46 = (bf16[384,768]{1,0:T(8,128)(2,1)S(1)}, bf16[384,768]{1,0:T(8,128)(2,1)S(1)}, u32[]{:S(2)}, u32[]{:S(2)}) collective-permute-start(bf16[384,768]{1,0:T(8,128)(2,1)S(1)} %pad_maximum_fusion.4), channel_id=1, source_target_pairs={{0,8},{4,12},{8,0},{12,4},{16,24},{20,28},{24,16},{28,20},{1,9},{5... | collective-permute-start | bytes 1769480 | tf_op jit(solution)/shard_map/ppermute | solution.py:584
  232.3 13.5 %collective-permute-start.45 = (bf16[384,768]{1,0:T(8,128)(2,1)S(1)}, bf16[384,768]{1,0:T(8,128)(2,1)S(1)}, u32[]{:S(2)}, u32[]{:S(2)}) collective-permute-start(bf16[384,768]{1,0:T(8,128)(2,1)S(1)} %pad_maximum_fusion.3), channel_id=1, source_target_pairs={{0,4},{4,0},{8,12},{12,8},{16,20},{20,16},{24,28},{28,24},{1,5},{5... | collective-permute-start | bytes 1769480 | tf_op jit(solution)/shard_map/ppermute | solution.py:584
  232.3 24.5 %collective-permute-start.32 = (bf16[512,768]{1,0:T(8,128)(2,1)S(1)}, bf16[512,768]{1,0:T(8,128)(2,1)S(1)}, u32[]{:S(2)}, u32[]{:S(2)}) collective-permute-start(bf16[512,768]{1,0:T(8,128)(2,1)S(1)} %add_convert_fusion.3.refs_0_), channel_id=1, source_target_pairs={{0,1},{1,0},{2,3},{3,2},{4,5},{5,4},{6,7},{7,6},{8,9},{9,8},{10,11... | collective-permute-start | bytes 2359304 | tf_op jit(solution)/shard_map/ppermute | solution.py:581
  232.4 24.4 %collective-permute-start.34 = (bf16[512,768]{1,0:T(8,128)(2,1)S(1)}, bf16[512,768]{1,0:T(8,128)(2,1)S(1)}, u32[]{:S(2)}, u32[]{:S(2)}) collective-permute-start(bf16[512,768]{1,0:T(8,128)(2,1)S(1)} %add_convert_fusion.2.refs_2_), channel_id=1, source_target_pairs={{0,1},{1,0},{2,3},{3,2},{4,5},{5,4},{6,7},{7,6},{8,9},{9,8},{10,11... | collective-permute-start | bytes 2359304 | tf_op jit(solution)/shard_map/ppermute | solution.py:581
  246.1 10.2 %collective-permute-start.52 = (bf16[288,768]{1,0:T(8,128)(2,1)S(1)}, bf16[288,768]{1,0:T(8,128)(2,1)S(1)}, u32[]{:S(2)}, u32[]{:S(2)}) collective-permute-start(bf16[288,768]{1,0:T(8,128)(2,1)S(1)} %constant_dynamic-update-slice_fusion), channel_id=1, source_target_pairs={{0,4},{4,0},{8,12},{12,8},{16,20},{20,16},{24,28},{28,24},{1,5},{5... | collective-permute-start | bytes 1327112 | tf_op jit(solution)/shard_map/ppermute | solution.py:584
  (71 other events, 458.2 us)

commit v2 on v1

--- a/solution.py
+++ b/solution.py
@@ -40,7 +40,7 @@
     return pl.CostEstimate(flops=int(micros * 1.1e9), bytes_accessed=1024, transcendentals=0)
 
 
-MICROS = {"attend_forward": 8, "attend_backward": 12, "entry_back": 5, "place": 3, "ahead": 9, "astern": 8, "inner_norm": 3}
+MICROS = {"attend_forward": 8, "attend_backward": 12, "entry_back": 5, "place": 3, "ahead": 9, "astern": 10, "inner_norm": 3, "weight_grads": 5}
 
 
 def project_kernel(x_ref, wq_ref, wk_ref, wv_ref, q_ref, k_ref, v_ref):
@@ -60,7 +60,7 @@
         + [pl.BlockSpec((192, d), lambda i: (0, 0))] * 3,
         out_specs=[pl.BlockSpec((block, 256), lambda i: (i, 0))] * 3,
         out_shape=[jax.ShapeDtypeStruct((rows, 256), BF)] * 3,
-        compiler_params=params(VMEM),
+        compiler_params=params(48),
         cost_estimate=cost(3),
         name="project",
     )(tokens, wq, wk, wv)
@@ -434,9 +434,9 @@
     )
 
 
-def astern_kernel(seqs, u, meta_ref, own_ref, far_ref, grad_ref, span_ref, ua_ref, ub_ref, da_ref, db_ref, slope_ref, vec_ref, *refs):
-    last = u == seqs - 1
-    before = refs[: 4 * seqs - 2] if last else ()
+def astern_kernel(u, meta_ref, own_ref, far_ref, grad_ref, span_ref, ua_ref, ub_ref, da_ref, db_ref, slope_ref, vec_ref, *refs):
+    last = len(refs) > 6
+    before = refs[: len(refs) - 10] if last else ()
     out_ref, g_ref, pre_ref, back_ref, sent_ref, small_ref = refs[len(before) : len(before) + 6]
     gain, bias = vec_ref[2:3, :], vec_ref[3:4, :]
     half, d = own_ref.shape
@@ -474,27 +474,19 @@
     small_ref[0:1, :] = gain_grad
     small_ref[1:2, :] = bias_grad
     if last:
-        acts, xs = before[:seqs], before[seqs : 2 * seqs]
-        pres = (*before[2 * seqs : 3 * seqs - 1], pre_ref)
-        gs = (*before[3 * seqs - 1 :], g_ref)
-        dups, ddowns = refs[-4:-2], refs[-2:]
-        for g in range(2):
-            for c in range(hidden // HB):
-                columns = pl.ds(g * hidden + c * HB, HB)
-                block = pl.ds(c * HB, HB)
-                dups[g][:, block] = sum(tn(x[...], p[:, columns]) for x, p in zip(xs, pres)).astype(BF)
-                ddowns[g][block, :] = sum(tn(a[:, columns], h[...]) for a, h in zip(acts, gs)).astype(BF)
-
-
-def astern(meta, own, far, grad, spans, up, down, slope, vectors, u, seqs, before):
+        x_ref, act_ref = before[:2]
+        weight_sums(x_ref[...], g_ref[...], act_ref, pre_ref, before[2:], refs[-4:])
+
+
+def astern(meta, own, far, grad, spans, up, down, slope, vectors, u, before):
     half, d = own.shape
     hidden = up[0].shape[1]
     rows = fixed(half, d)
     wide = fixed(half, 2 * hidden)
-    extra = [] if not before else [wide] * seqs + [rows] * seqs + [wide] * (seqs - 1) + [rows] * (seqs - 1)
     grads = [] if not before else [(d, hidden)] * 2 + [(hidden, d)] * 2
+    extra = [] if not before else [rows, wide] + [fixed(*shape) for shape in grads[: len(before) - 2]]
     return call(
-        functools.partial(astern_kernel, seqs, u),
+        functools.partial(astern_kernel, u),
         "astern",
         (1,),
         meta,
@@ -515,7 +507,44 @@
             like((2, d), F32),
         ]
         + [like(shape, BF) for shape in grads],
-        limit=32 if before else VMEM,
+        limit=28 if before else VMEM,
+    )
+
+
+def weight_kernel(meta_ref, x_ref, g_ref, act_ref, pre_ref, *refs):
+    before, sums = refs[:-4], refs[-4:]
+    weight_sums(x_ref[...], g_ref[...], act_ref, pre_ref, before, sums)
+
+
+def weight_sums(x, g, act_ref, pre_ref, before, sums):
+    hidden = act_ref.shape[1] // 2
+    for i in range(2):
+        for c in range(hidden // HB):
+            columns = pl.ds(i * hidden + c * HB, HB)
+            block = pl.ds(c * HB, HB)
+            up = tn(x, pre_ref[:, columns])
+            down = tn(act_ref[:, columns], g)
+            if before:
+                up = up + before[i][:, block].astype(F32)
+                down = down + before[2 + i][block, :].astype(F32)
+            sums[i][:, block] = up.astype(BF)
+            sums[2 + i][block, :] = down.astype(BF)
+
+
+def weight_grads(meta, x, g, act, pre, before):
+    rows, d = x.shape
+    hidden = act.shape[1] // 2
+    shapes = [(d, hidden)] * 2 + [(hidden, d)] * 2
+    return call(
+        weight_kernel,
+        "weight_grads",
+        (1,),
+        meta,
+        (x, g, act, pre, *before),
+        [fixed(rows, d)] * 2 + [fixed(rows, 2 * hidden)] * 2 + [fixed(*shape) for shape in shapes[: len(before)]],
+        [fixed(*shape) for shape in shapes],
+        [like(shape, BF) for shape in shapes],
+        limit=24,
     )
 
 
@@ -590,9 +619,12 @@
         size = array.shape[0] // count
         return lax.dynamic_slice_in_dim(array, index * size, size, 0)
 
+    def total(pieces):
+        return sum(piece.astype(F32) for piece in pieces).astype(BF) if len(pieces) > 1 else pieces[0]
+
     class Chain:
-        def __init__(self, state, order):
-            self.state = state
+        def __init__(self, parts, order):
+            self.parts = parts
             self.steps = [(True, *stage) for stage in order] + [(False, *stage) for stage in reversed(order)]
 
         def start(self):
@@ -600,9 +632,9 @@
                 scatter, low_bit, width = self.steps[0]
                 count = 1 << width
                 spot = (place_dp >> low_bit) & (count - 1)
-                sent = [cut(self.state, spot ^ j, count) if scatter else self.state for j in range(1, count)]
-                got = [swap_dp(piece, j << low_bit) for j, piece in enumerate(sent, 1)]
-                self.pending = [cut(self.state, spot, count) if scatter else self.state] + got
+                pick = lambda j: [cut(part, spot ^ j, count) if scatter else part for part in self.parts]
+                got = [swap_dp(total(pick(j)), j << low_bit) for j in range(1, count)]
+                self.pending = pick(0) + got
 
         def finish(self, *after):
             if not self.steps:
@@ -614,7 +646,7 @@
             count = 1 << width
             spot = (place_dp >> low_bit) & (count - 1)
             if scatter:
-                self.state = sum(piece.astype(F32) for piece in pieces).astype(BF)
+                self.state = total(pieces)
             elif count == 2:
                 one, two = pieces
                 self.state = jnp.concatenate([jnp.where(spot, two, one), jnp.where(spot, one, two)], axis=0)
@@ -624,6 +656,7 @@
                 for j in range(count):
                     whole = lax.dynamic_update_slice_in_dim(whole, pieces[j], (spot ^ j) * size, 0)
                 self.state = whole
+            self.parts = (self.state,)
 
     scalars = jnp.concatenate([core.reshape(1), lengths])
     token = []
@@ -651,16 +684,15 @@
     for u in range(seqs):
         front.append(done(ahead(meta(), tokens, att[u], merge_w, up_w, down_w, vectors, u)))
         far.append(swap(front[u][6], 2))
-    back, far_grad = [], []
+    back, far_grad, sums = [], [], ()
     for u in range(seqs):
-        before = ()
-        if u == seqs - 1:
-            before = (*(f[3] for f in front), *(f[2] for f in front), *(b[2] for b in back), *(b[1] for b in back))
+        before = (front[u][2], front[u][3], *sums) if u == seqs - 1 else ()
         back.append(
-            done(astern(meta(), front[u][5], far[u], out_grad, span_starts, up_w, down_w, front[u][4], vectors, u, seqs, before))
+            done(astern(meta(), front[u][5], far[u], out_grad, span_starts, up_w, down_w, front[u][4], vectors, u, before))
         )
-        if u == 0:
+        if u < seqs - 1:
             far_grad.append(swap(back[u][4], 2))
+            sums = done(weight_grads(meta(), front[u][2], back[u][1], front[u][3], back[u][2], sums))
 
     def inner_step(u, before):
         res = done(inner_norm(meta(), back[u][3], far_grad[u], front[u][0], front[u][1], vectors, att[u][:2], merge_w[:2], before))
@@ -675,64 +707,80 @@
 
     pairs = [(b, 1) for b in range(bits)]
     stages = [(0, 1)] + [(b, 2) for b in range(1, bits - 1, 2)] + ([(bits - 1, 1)] if bits % 2 == 0 else [])
-    inner, near, crossed, total, chains = [], [], [], (), []
     out_rows = [b[0] for b in back]
     out_other = [swap(r, 1) for r in out_rows]
-
-    def advance(result):
-        for chain in chains:
-            chain.finish(result)
-            token.append(chain.state)
+    inner, near, crossed, so_far = [], [], [], ()
+    ffn, chains = [], []
+
+    def finish(group, *after):
+        for chain in group:
+            chain.finish(*after)
+        return [chain.state for chain in group]
+
+    def start(group):
+        for chain in group:
             chain.start()
+
+    def together(group, *others):
+        values = lax.optimization_barrier((*(chain.state for chain in group), *others))
+        for chain, value in zip(group, values):
+            chain.state, chain.parts = value, (value,)
+        return values[len(group) :]
 
     for u in range(seqs):
         last = u == seqs - 1
         if u == 0:
+            up_own, up_other, down_own, down_other = lax.optimization_barrier((*back[-1][6:], far_grad[0]))[:4]
+            ffn.append(Chain((down_own, swap(down_other, 1)), pairs))
+            ffn.append(Chain((up_own, swap(up_other, 1)), pairs[1:2] + pairs[:1] + pairs[2:]))
             res, grads = inner_step(0, ())
+            start(ffn)
             inner.append(res)
-            later = lax.optimization_barrier((*back[-1][6:], back[-1][4], res[0]))
-            up_own, up_other, down_own, down_other, sent = later[:5]
-            far_grad.append(swap(sent, 2))
-            chains.append(Chain(add(down_own, swap(down_other, 1)), pairs))
-            chains.append(Chain(add(up_own, swap(up_other, 1)), pairs[1:2] + pairs[:1] + pairs[2:]))
-            for chain in chains:
-                token.append(chain.state)
-                chain.start()
+            far_grad.append(swap(lax.optimization_barrier((back[-1][4], res[0]))[0], 2))
             token.extend(out_other)
         dqkv = attend_step(u, grads)
-        advance(dqkv[0])
+        token.extend(finish(ffn + chains, dqkv[0]))
+        start(ffn + chains)
         if not last:
             before = ()
             if u + 1 == seqs - 1:
                 before = (inner[0][3], inner[0][4], inner[0][5], back[0][5], back[1][5])
             res, grads = inner_step(u + 1, before)
             inner.append(res)
+            merge = Chain((res[3], swap(res[4], 1)), pairs)
+            token.extend([grads[1], merge.parts[1]])
+            merge.start()
         else:
             token.extend(crossed)
-        out = entry_step(u, dqkv, total, BF if last else F32)
-        total = (out[2],)
+        out = entry_step(u, dqkv, so_far, BF if last else F32)
+        so_far = (out[2],)
         got = swap(out[0], 1)
-        near.append(out[1].astype(F32) + got.astype(F32))
-        crossed.append(swap(near[u].astype(BF), 2))
-        token.append(got)
         if not last:
-            advance(out[0])
-            chains.append(Chain(add(res[3], swap(res[4], 1)), pairs))
-            token.append(chains[-1].state)
-            chains[-1].start()
-    chains.append(Chain(total[0], stages))
-    chains[-1].start()
-    beside = {0: (got,), 1: (crossed[-1],)}
-    rounds = 0
+            chains.append(merge)
+            finish(ffn + chains, out[0])
+            (got,) = together(ffn + chains, got)
+            start(ffn + chains)
+            token.extend([chain.state for chain in ffn + chains])
+            near.append(out[1].astype(F32) + got.astype(F32))
+            crossed.append(swap(near[u].astype(BF), 2))
+    qkv = Chain((so_far[0],), stages)
+    qkv.start()
+    finish(ffn + [merge], out[0])
+    together(ffn + [merge])
+    start(ffn + [merge])
+    near.append(out[1].astype(F32) + got.astype(F32))
+    chains = ffn + [merge, qkv]
+    finish(chains)
+    (arrived,) = together(chains, near[-1].astype(BF))
+    crossed.append(swap(arrived, 2))
+    start(chains)
+    finish(chains)
+    together(chains, crossed[-1])
+    start(chains)
     while any(chain.steps for chain in chains):
-        for chain in chains:
-            chain.finish(total[0])
-        states = tuple(chain.state for chain in chains)
-        states = lax.optimization_barrier(states + beside.get(rounds, ()))[: len(chains)]
-        for chain, state in zip(chains, states):
-            chain.state = state
-            chain.start()
-        rounds += 1
+        finish(chains)
+        together(chains)
+        start(chains)
     down_sum, up_sum, merge_sum, qkv_sum = (chain.state for chain in chains)
 
     ready = [(inner[u][0] + (near[u] + crossed[u].astype(F32))).astype(BF) for u in range(seqs)]

time: 272 us -> 281 us (1.033)
  local copies, waits for them, and re-layouts: 16.6 us -> 39.6 us
  waiting for transfers between devices: 90.8 us -> 68.4 us
  Pallas kernels: 97.1 us -> 104 us
    unnamed x130 -> x180, local copies, waits for them, and re-layouts: 15.3 us -> 32.7 us
    ppermute x28, waiting for transfers between devices: 31.4 us -> 16.7 us  [swap(): return lax.ppermute(value, 'tensor', [(i, i ^ k) for i in range(4)])]
    ppermute x26, waiting for transfers between devices: 59.4 us -> 51.7 us  [swap_dp(): return lax.ppermute(value, 'dp', [(i, i ^ k) for i in range(groups)])]
    dynamic_slice x11 -> x13, local copies, waits for them, and re-layouts: 0.5 us -> 6.17 us  [cut(): return lax.dynamic_slice_in_dim(array, index * size, size, 0)]
    pallas_call x14 -> x15, Pallas kernels: 93.9 us -> 99.2 us  [call(): pl.pallas_call(kernel, grid_spec=pltpu.PrefetchScalarGridSpec(num_scalar_...]
    convert_element_type x13 -> x15, other arithmetic: 4.38 us -> 6.47 us  [the longest x14 6.29 us: total(): sum((piece.astype(F32) for piece in pieces)).astype(BF)]
  transfers between devices with their start and end apart: 54 -> 54, of which waited for: 22 -> 19; matrix products, arithmetic and copies ran while one was open for 3% -> 8% of each run, Pallas kernels for 34% -> 35%
where the time goes in v2:
time: 281 us; the launch traced here: 278 us
  Pallas kernels  104 us (37%)
  waiting for transfers between devices  68.4 us (24%)
  starting transfers between devices  49.3 us (18%)
  local copies, waits for them, and re-layouts  39.6 us (14%)
  other arithmetic  14.4 us (5%)
    pallas_call x15, Pallas kernels, call(): pl.pallas_call(kernel, grid_spec=pltpu.PrefetchScalarGridSpec(num_scalar_...  99.2 us
    ppermute x26, waiting for transfers between devices, swap_dp(): return lax.ppermute(value, 'dp', [(i, i ^ k) for i in range(groups)])  51.7 us
    unnamed x180, local copies, waits for them, and re-layouts  32.7 us
    ppermute x26, starting transfers between devices, swap_dp(): return lax.ppermute(value, 'dp', [(i, i ^ k) for i in range(groups)])  32.7 us
    ppermute x28, waiting for transfers between devices, swap(): return lax.ppermute(value, 'tensor', [(i, i ^ k) for i in range(4)])  16.7 us
    ppermute x28, starting transfers between devices, swap(): return lax.ppermute(value, 'tensor', [(i, i ^ k) for i in range(4)])  16.6 us
    convert_element_type x14, other arithmetic, total(): sum((piece.astype(F32) for piece in pieces)).astype(BF)  6.29 us
    dynamic_slice x13, local copies, waits for them, and re-layouts, cut(): return lax.dynamic_slice_in_dim(array, index * size, size, 0)  6.17 us
  transfers between devices with their start and end apart: 54, of which 19 were waited for; matrix products, arithmetic and copies ran while one was open for 8% of the time, Pallas kernels for 35%

profile of v2, /device:TPU:0, one launch (start us, length us, event | category | flops | bytes accessed | tf_op | source)
XLA Modules:
  0.0 278.0 jit_solution(4503386020035202941)
XLA Ops:
  1.2 2.6 collective-permute-start.1
  7.9 4.7 %project.1 = (bf16[2048,256]{1,0:T(8,128)(2,1)S(1)}, bf16[2048,256]{1,0:T(8,128)(2,1)S(1)}, bf16[2048,256]{1,0:T(8,128)(2,1)S(1)}) custom-call(bf16[2048,768]{1,0:T(8,128)(2,1)} %x_ref.5, bf16[192,768]{1,0:T(8,128)(2,1)S(1)} %bitcast.10, bf16[192,768]{1,0:T(8,128)(2,1)S(1)} %bitcast.13, bf16[192,768]{1,0:T(8,128)(2,1)S(1)} %bitcast.16), custom_call_target="tpu_custom_call" | custom-call | flops 3300000000 | bytes 1024 | tf_op jit(solution)/shard_map/project/pallas_call | solution.py:56
  12.8 7.7 %attend_forward.2 = (bf16[192,512]{1,0:T(8,128)(2,1)S(1)}, bf16[192,512]{1,0:T(8,128)(2,1)S(1)}, f32[2,192,512]{2,1,0:T(8,128)S(1)}, f32[2,8,512]{2,1,0:T(8,128)S(1)}) custom-call(s32[3]{0:T(128)S(1)} %pad_add_fusion.meta_ref, bf16[2048,256]{1,0:T(8,128)(2,1)S(1)} %get-tuple-element.145.q_ref, bf16[2048,256]{1,0:T(8,128)(2,1)S(1)} %get-tuple-element.146.k_ref, ...), custom_call_target="tpu_custom_call" | custom-call | flops 8800000000 | bytes 1024 | tf_op jit(solution)/shard_map/attend_forward/pallas_call | solution.py:84
  21.7 1.7 collective-permute-start.7
  23.8 8.2 %attend_forward.3 = (bf16[192,512]{1,0:T(8,128)(2,1)S(1)}, bf16[192,512]{1,0:T(8,128)(2,1)S(1)}, f32[2,192,512]{2,1,0:T(8,128)S(1)}, f32[2,8,512]{2,1,0:T(8,128)S(1)}) custom-call(s32[3]{0:T(128)S(1)} %pad_add_fusion.meta_ref, bf16[2048,256]{1,0:T(8,128)(2,1)S(1)} %get-tuple-element.145.q_ref, bf16[2048,256]{1,0:T(8,128)(2,1)S(1)} %get-tuple-element.146.k_ref, ...), custom_call_target="tpu_custom_call" | custom-call | flops 8800000000 | bytes 1024 | tf_op jit(solution)/shard_map/attend_forward/pallas_call | solution.py:84
  33.0 1.7 collective-permute-start.9
  35.2 7.9 %ahead.2 = (f32[512,768]{1,0:T(8,128)S(1)}, f32[512,128]{1,0:T(8,128)S(1)}, bf16[512,768]{1,0:T(8,128)(2,1)S(1)}, bf16[512,1536]{1,0:T(8,128)(2,1)S(1)}, bf16[51...) custom-call(s32[3]{0:T(128)S(1)} %pad_add_fusion.meta_ref, ...), custom_call_target="tpu_custom_call" | custom-call | flops 9900000256 | bytes 1024 | tf_op jit(solution)/shard_map/ahead/pallas_call | solution.py:84
  44.3 1.7 collective-permute-start.11
  49.0 8.0 %ahead.3 = (f32[512,768]{1,0:T(8,128)S(1)}, f32[512,128]{1,0:T(8,128)S(1)}, bf16[512,768]{1,0:T(8,128)(2,1)S(1)}, bf16[512,1536]{1,0:T(8,128)(2,1)S(1)}, bf16[51...) custom-call(s32[3]{0:T(128)S(1)} %pad_add_fusion.meta_ref, ...), custom_call_target="tpu_custom_call" | custom-call | flops 9900000256 | bytes 1024 | tf_op jit(solution)/shard_map/ahead/pallas_call | solution.py:84
  57.7 7.0 %collective-permute-done.11.far_ref = bf16[512,768]{1,0:T(8,128)(2,1)S(1)} collective-permute-done((bf16[512,768]{1,0:T(8,128)(2,1)S(1)}, bf16[512,768]{1,0:T(8,128)(2,1)S(1)}, u32[]{:S(2)}, u32[]{:S(2)}) %collective-permute-start.11) | collective-permute-done | bytes 786464 | tf_op jit(solution)/shard_map/ppermute | solution.py:610
  64.7 7.2 %astern.2 = (bf16[512,768]{1,0:T(8,128)(2,1)}, bf16[512,768]{1,0:T(8,128)(2,1)S(1)}, bf16[512,1536]{1,0:T(8,128)(2,1)S(1)}, f32[512,768]{1,0:T(8,128)S(1)}, bf16...) custom-call(s32[3]{0:T(128)S(1)} %pad_add_fusion.meta_ref, f32[512,768]{1,0:T(8,128)S(1)} %get-tuple-element.158.own_ref, ...), custom_call_target="tpu_custom_call" | custom-call | flops 11000000512 | bytes 1024 | tf_op jit(solution)/shard_map/astern/pallas_call | solution.py:84
  73.1 3.2 %weight_grads.1 = (bf16[768,768]{1,0:T(8,128)(2,1)S(1)}, bf16[768,768]{1,0:T(8,128)(2,1)S(1)}, bf16[768,768]{1,0:T(8,128)(2,1)S(1)}, bf16[768,768]{1,0:T(8,128)(2,1)S(1)}) custom-call(s32[3]{0:T(128)S(1)} %pad_add_fusion.meta_ref, bf16[512,768]{1,0:T(8,128)(2,1)S(1)} %get-tuple-element.163.x_ref, bf16[512,768]{1,0:T(8,128)(2,1)S(1)} %get-tuple-element.164.g_ref, ...), custom_call_target="tpu_custom_call" | custom-call | flops 5500000256 | bytes 1024 | tf_op jit(solution)/shard_map/weight_grads/pallas_call | solution.py:84
  76.3 1.8 collective-permute-start.13
  78.1 3.4 %collective-permute-done.12.far_ref = bf16[512,768]{1,0:T(8,128)(2,1)S(1)} collective-permute-done((bf16[512,768]{1,0:T(8,128)(2,1)S(1)}, bf16[512,768]{1,0:T(8,128)(2,1)S(1)}, u32[]{:S(2)}, u32[]{:S(2)}) %collective-permute-start.12) | collective-permute-done | bytes 786464 | tf_op jit(solution)/shard_map/ppermute | solution.py:610
  82.2 12.3 %astern.3 = (bf16[512,768]{1,0:T(8,128)(2,1)}, bf16[512,768]{1,0:T(8,128)(2,1)}, bf16[512,1536]{1,0:T(8,128)(2,1)}, f32[512,768]{1,0:T(8,128)S(1)}, bf16[512,768...) custom-call(s32[3]{0:T(128)S(1)} %copy-done.42, ...), custom_call_target="tpu_custom_call" | custom-call | flops 11000000512 | bytes 1024 | tf_op jit(solution)/shard_map/astern/pallas_call | solution.py:84
  109.4 2.4 inner_norm.2
  111.8 1.8 collective-permute-start.21
  118.0 11.3 %attend_backward.2 = (bf16[1024,256]{1,0:T(8,128)(2,1)S(1)}, bf16[1024,256]{1,0:T(8,128)(2,1)S(1)}, bf16[1024,256]{1,0:T(8,128)(2,1)S(1)}) custom-call(s32[3]{0:T(128)S(1)} %copy-done.44, bf16[2048,256]{1,0:T(8,128)(2,1)S(1)} %copy-done.54, bf16[2048,256]{1,0:T(8,128)(2,1)S(1)} %copy-done.57, bf16[2048,256]{1,0:T(8,128)(2,1)S(1)} %copy-done.60, ...), custom_call_target="tpu_custom_call" | custom-call | flops 13200000000 | bytes 1024 | tf_op jit(solution)/shard_map/attend_backward/pallas_call | solution.py:84
  129.3 1.5 constant_dynamic-slice_fusion.18
  135.2 3.2 %inner_norm.3 = (f32[512,768]{1,0:T(8,128)S(1)}, bf16[192,512]{1,0:T(8,128)(2,1)S(1)}, bf16[192,512]{1,0:T(8,128)(2,1)S(1)}, bf16[256,768]{1,0:T(8,128)(2,1)S(1)...) custom-call(s32[3]{0:T(128)S(1)} %copy-done.44, f32[512,768]{1,0:T(8,128)S(1)} %copy-done.48, ...), custom_call_target="tpu_custom_call" | custom-call | flops 3300000000 | bytes 1024 | tf_op jit(solution)/shard_map/inner_norm/pallas_call | solution.py:84
  143.7 1.5 collective-permute-start.24
  153.5 4.5 %entry_back.2 = (bf16[512,768]{1,0:T(8,128)(2,1)S(1)}, bf16[512,768]{1,0:T(8,128)(2,1)S(1)}, f32[576,768]{1,0:T(8,128)S(1)}) custom-call(s32[3]{0:T(128)S(1)} %copy-done.44, bf16[2048,768]{1,0:T(8,128)(2,1)S(1)} %copy-done.4, bf16[1024,256]{1,0:T(8,128)(2,1)S(1)} %copy-done.69, bf16[1024,256]{1,0:T(8,128)(2,1)S(1)} %copy-done.71, ...), custom_call_target="tpu_custom_call" | custom-call | flops 5500000256 | bytes 1024 | tf_op jit(solution)/shard_map/entry_back/pallas_call | solution.py:84
  162.3 2.7 collective-permute-start.29
  165.3 11.1 %attend_backward.3 = (bf16[1024,256]{1,0:T(8,128)(2,1)S(1)}, bf16[1024,256]{1,0:T(8,128)(2,1)S(1)}, bf16[1024,256]{1,0:T(8,128)(2,1)S(1)}) custom-call(s32[3]{0:T(128)S(1)} %copy-done.44, bf16[2048,256]{1,0:T(8,128)(2,1)S(1)} %copy-done.55, bf16[2048,256]{1,0:T(8,128)(2,1)S(1)} %copy-done.58, bf16[2048,256]{1,0:T(8,128)(2,1)S(1)} %copy-done.61, ...), custom_call_target="tpu_custom_call" | custom-call | flops 13200000000 | bytes 1024 | tf_op jit(solution)/shard_map/attend_backward/pallas_call | solution.py:84
  176.5 2.6 collective-permute-done.28
  179.6 2.7 collective-permute-start.34
  182.3 4.9 %entry_back.3 = (bf16[512,768]{1,0:T(8,128)(2,1)S(1)}, bf16[512,768]{1,0:T(8,128)(2,1)S(1)}, bf16[576,768]{1,0:T(8,128)(2,1)S(1)}) custom-call(s32[3]{0:T(128)S(1)} %copy-done.44, bf16[2048,768]{1,0:T(8,128)(2,1)S(1)} %copy-done.4, bf16[1024,256]{1,0:T(8,128)(2,1)S(1)} %get-tuple-element.235.dq_ref, bf16[1024,256]{1,0:T(8,128)(2,1)S(1)} %get-tuple-element.245.dk_ref, ...), custom_call_target="tpu_custom_call" | custom-call | flops 5500000256 | bytes 1024 | tf_op jit(solution)/shard_map/entry_back/pallas_call | solution.py:84
  187.4 1.9 collective-permute-start.40
  189.3 1.7 collective-permute-done.35
  191.0 2.6 collective-permute-done.34
  195.2 2.2 collective-permute-start.37
  198.9 7.5 %collective-permute-done.38 = bf16[192,768]{1,0:T(8,128)(2,1)S(1)} collective-permute-done((bf16[192,768]{1,0:T(8,128)(2,1)S(1)}, bf16[192,768]{1,0:T(8,128)(2,1)S(1)}, u32[]{:S(2)}, u32[]{:S(2)}) %collective-permute-start.38) | collective-permute-done | bytes 294944 | tf_op jit(solution)/shard_map/ppermute | solution.py:613
  207.2 1.9 collective-permute-start.44
  209.3 2.9 %collective-permute-start.47 = (bf16[72,768]{1,0:T(8,128)(2,1)S(1)}, bf16[72,768]{1,0:T(8,128)(2,1)S(1)}, u32[]{:S(2)}, u32[]{:S(2)}) collective-permute-start(bf16[72,768]{1,0:T(8,128)(2,1)S(1)} %get-tuple-element.301), channel_id=1, source_target_pairs={{0,16},{4,20},{8,24},{12,28},{16,0},{20,4},{24,8},{28,12},{1,17},{... | collective-permute-start | bytes 331784 | tf_op jit(solution)/shard_map/ppermute | solution.py:613
  212.2 2.0 collective-permute-done.45
  214.1 2.4 collective-permute-start.48
  216.5 12.5 %collective-permute-done.46 = bf16[72,768]{1,0:T(8,128)(2,1)S(1)} collective-permute-done((bf16[72,768]{1,0:T(8,128)(2,1)S(1)}, bf16[72,768]{1,0:T(8,128)(2,1)S(1)}, u32[]{:S(2)}, u32[]{:S(2)}) %collective-permute-start.46) | collective-permute-done | bytes 110624 | tf_op jit(solution)/shard_map/ppermute | solution.py:613
  229.1 1.7 collective-permute-start.43
  232.3 10.9 %collective-permute-done.43 = bf16[384,768]{1,0:T(8,128)(2,1)S(1)} collective-permute-done((bf16[384,768]{1,0:T(8,128)(2,1)S(1)}, bf16[384,768]{1,0:T(8,128)(2,1)S(1)}, u32[]{:S(2)}, u32[]{:S(2)}) %collective-permute-start.43) | collective-permute-done | bytes 589856 | tf_op jit(solution)/shard_map/ppermute | solution.py:613
  243.3 5.2 %collective-permute-done.41 = bf16[512,768]{1,0:T(8,128)(2,1)S(1)} collective-permute-done((bf16[512,768]{1,0:T(8,128)(2,1)S(1)}, bf16[512,768]{1,0:T(8,128)(2,1)S(1)}, u32[]{:S(2)}, u32[]{:S(2)}) %collective-permute-start.41) | collective-permute-done | bytes 786464 | tf_op jit(solution)/shard_map/ppermute | solution.py:610
  249.6 3.0 %collective-permute-start.51 = (bf16[72,768]{1,0:T(8,128)(2,1)S(1)}, bf16[72,768]{1,0:T(8,128)(2,1)S(1)}, u32[]{:S(2)}, u32[]{:S(2)}) collective-permute-start(bf16[72,768]{1,0:T(8,128)(2,1)S(1)} %add_convert_fusion.13), channel_id=1, source_target_pairs={{0,16},{4,20},{8,24},{12,28},{16,0},{20,4},{24,8},{28,12},{1,17},{... | collective-permute-start | bytes 331784 | tf_op jit(solution)/shard_map/ppermute | solution.py:613
  253.5 2.2 collective-permute-done.50
  255.7 2.0 collective-permute-done.51
  260.7 4.6 %place.2 = bf16[2048,768]{1,0:T(8,128)(2,1)} custom-call(s32[3]{0:T(128)S(1)} %copy-done.44, bf16[512,768]{1,0:T(8,128)(2,1)} %get-tuple-element.161.refs_0_, bf16[512,768]{1,0:T(8,128)(2,1)} %collective-permute-done.14.refs_1_, bf16[512,768]{1,0:T(8,128)(2,1)} %get-tuple-element.177.refs_2_, bf16[512,768]{1,0:T(8,128)(2,1)} %collective-permute-done.15.refs_3_), custom_call_target="tpu_custom_call" | custom-call | flops 3300000000 | bytes 1024 | tf_op jit(solution)/shard_map/place/pallas_call | solution.py:84
  265.7 3.0 %collective-permute-done.53 = bf16[288,768]{1,0:T(8,128)(2,1)S(1)} collective-permute-done((bf16[288,768]{1,0:T(8,128)(2,1)S(1)}, bf16[288,768]{1,0:T(8,128)(2,1)S(1)}, u32[]{:S(2)}, u32[]{:S(2)}) %collective-permute-start.53) | collective-permute-done | bytes 442400 | tf_op jit(solution)/shard_map/ppermute | solution.py:613
  268.9 1.6 convert_element_type.244
  270.5 1.6 convert_element_type.245
  274.8 2.7 place.3
  (324 shorter events, 70.1 us)
Async XLA Ops:
  0.6 20.8 %collective-permute-start = (bf16[192,768]{1,0:T(8,128)(2,1)}, bf16[192,768]{1,0:T(8,128)(2,1)S(1)}, u32[]{:S(2)}, u32[]{:S(2)}) collective-permute-start(bf16[192,768]{1,0:T(8,128)(2,1)} %w0.7), channel_id=1, source_target_pairs={{0,1},{1,0},{2,3},{3,2},{4,5},{5,4},{6,7},{7,6},{8,9},{9,8},{10,11... | collective-permute-start | bytes 884744 | tf_op jit(solution)/shard_map/ppermute | solution.py:610
  1.2 20.5 %collective-permute-start.1 = (bf16[192,768]{1,0:T(8,128)(2,1)}, bf16[192,768]{1,0:T(8,128)(2,1)S(1)}, u32[]{:S(2)}, u32[]{:S(2)}) collective-permute-start(bf16[192,768]{1,0:T(8,128)(2,1)} %w0.7), channel_id=1, source_target_pairs={{0,2},{1,3},{2,0},{3,1},{4,6},{5,7},{6,4},{7,5},{8,10},{9,11},{10,... | collective-permute-start | bytes 884744 | tf_op jit(solution)/shard_map/ppermute | solution.py:610
  3.7 19.7 %collective-permute-start.2 = (bf16[192,768]{1,0:T(8,128)(2,1)}, bf16[192,768]{1,0:T(8,128)(2,1)S(1)}, u32[]{:S(2)}, u32[]{:S(2)}) collective-permute-start(bf16[192,768]{1,0:T(8,128)(2,1)} %w0.7), channel_id=1, source_target_pairs={{0,3},{1,2},{2,1},{3,0},{4,7},{5,6},{6,5},{7,4},{8,11},{9,10},{10,... | collective-permute-start | bytes 884744 | tf_op jit(solution)/shard_map/ppermute | solution.py:610
  3.8 20.0 %collective-permute-start.3 = (bf16[768,768]{1,0:T(8,128)(2,1)}, bf16[768,768]{1,0:T(8,128)(2,1)S(1)}, u32[]{:S(2)}, u32[]{:S(2)}) collective-permute-start(bf16[768,768]{1,0:T(8,128)(2,1)} %ua_ref.7), channel_id=1, source_target_pairs={{0,1},{1,0},{2,3},{3,2},{4,5},{5,4},{6,7},{7,6},{8,9},{9,8},{10,11... | collective-permute-start | bytes 3538952 | tf_op jit(solution)/shard_map/ppermute | solution.py:610
  3.9 19.9 %collective-permute-start.4 = (bf16[768,768]{1,0:T(8,128)(2,1)}, bf16[768,768]{1,0:T(8,128)(2,1)S(1)}, u32[]{:S(2)}, u32[]{:S(2)}) collective-permute-start(bf16[768,768]{1,0:T(8,128)(2,1)} %da_ref.7), channel_id=1, source_target_pairs={{0,1},{1,0},{2,3},{3,2},{4,5},{5,4},{6,7},{7,6},{8,9},{9,8},{10,11... | collective-permute-start | bytes 3538952 | tf_op jit(solution)/shard_map/ppermute | solution.py:610
  21.5 13.7 %collective-permute-start.5 = (bf16[192,512]{1,0:T(8,128)(2,1)S(1)}, bf16[192,512]{1,0:T(8,128)(2,1)S(1)}, u32[]{:S(2)}, u32[]{:S(2)}) collective-permute-start(bf16[192,512]{1,0:T(8,128)(2,1)S(1)} %get-tuple-element.152), channel_id=1, source_target_pairs={{0,1},{1,0},{2,3},{3,2},{4,5},{5,4},{6,7},{7,6},{8,9},{9,8},{10,11... | collective-permute-start | bytes 589832 | tf_op jit(solution)/shard_map/ppermute | solution.py:610
  21.7 13.5 %collective-permute-start.7 = (bf16[192,512]{1,0:T(8,128)(2,1)S(1)}, bf16[192,512]{1,0:T(8,128)(2,1)S(1)}, u32[]{:S(2)}, u32[]{:S(2)}) collective-permute-start(bf16[192,512]{1,0:T(8,128)(2,1)S(1)} %get-tuple-element.152), channel_id=1, source_target_pairs={{0,3},{1,2},{2,1},{3,0},{4,7},{5,6},{6,5},{7,4},{8,11},{9,10},{10,... | collective-permute-start | bytes 589832 | tf_op jit(solution)/shard_map/ppermute | solution.py:610
  23.4 11.3 %collective-permute-start.6 = (bf16[192,512]{1,0:T(8,128)(2,1)S(1)}, bf16[192,512]{1,0:T(8,128)(2,1)S(1)}, u32[]{:S(2)}, u32[]{:S(2)}) collective-permute-start(bf16[192,512]{1,0:T(8,128)(2,1)S(1)} %get-tuple-element.148.a0), channel_id=1, source_target_pairs={{0,2},{1,3},{2,0},{3,1},{4,6},{5,7},{6,4},{7,5},{8,10},{9,11},{10,... | collective-permute-start | bytes 589832 | tf_op jit(solution)/shard_map/ppermute | solution.py:610
  33.0 13.0 %collective-permute-start.9 = (bf16[192,512]{1,0:T(8,128)(2,1)S(1)}, bf16[192,512]{1,0:T(8,128)(2,1)S(1)}, u32[]{:S(2)}, u32[]{:S(2)}) collective-permute-start(bf16[192,512]{1,0:T(8,128)(2,1)S(1)} %get-tuple-element.150.a0), channel_id=1, source_target_pairs={{0,2},{1,3},{2,0},{3,1},{4,6},{5,7},{6,4},{7,5},{8,10},{9,11},{10,... | collective-permute-start | bytes 589832 | tf_op jit(solution)/shard_map/ppermute | solution.py:610
  34.7 11.3 %collective-permute-start.8 = (bf16[192,512]{1,0:T(8,128)(2,1)S(1)}, bf16[192,512]{1,0:T(8,128)(2,1)S(1)}, u32[]{:S(2)}, u32[]{:S(2)}) collective-permute-start(bf16[192,512]{1,0:T(8,128)(2,1)S(1)} %get-tuple-element.155), channel_id=1, source_target_pairs={{0,1},{1,0},{2,3},{3,2},{4,5},{5,4},{6,7},{7,6},{8,9},{9,8},{10,11... | collective-permute-start | bytes 589832 | tf_op jit(solution)/shard_map/ppermute | solution.py:610
  34.7 11.3 %collective-permute-start.10 = (bf16[192,512]{1,0:T(8,128)(2,1)S(1)}, bf16[192,512]{1,0:T(8,128)(2,1)S(1)}, u32[]{:S(2)}, u32[]{:S(2)}) collective-permute-start(bf16[192,512]{1,0:T(8,128)(2,1)S(1)} %get-tuple-element.155), channel_id=1, source_target_pairs={{0,3},{1,2},{2,1},{3,0},{4,7},{5,6},{6,5},{7,4},{8,11},{9,10},{10,... | collective-permute-start | bytes 589832 | tf_op jit(solution)/shard_map/ppermute | solution.py:610
  44.3 20.4 %collective-permute-start.11 = (bf16[512,768]{1,0:T(8,128)(2,1)S(1)}, bf16[512,768]{1,0:T(8,128)(2,1)S(1)}, u32[]{:S(2)}, u32[]{:S(2)}) collective-permute-start(bf16[512,768]{1,0:T(8,128)(2,1)S(1)} %get-tuple-element.159), channel_id=1, source_target_pairs={{0,2},{1,3},{2,0},{3,1},{4,6},{5,7},{6,4},{7,5},{8,10},{9,11},{10,... | collective-permute-start | bytes 2359304 | tf_op jit(solution)/shard_map/ppermute | solution.py:610
  57.1 24.4 %collective-permute-start.12 = (bf16[512,768]{1,0:T(8,128)(2,1)S(1)}, bf16[512,768]{1,0:T(8,128)(2,1)S(1)}, u32[]{:S(2)}, u32[]{:S(2)}) collective-permute-start(bf16[512,768]{1,0:T(8,128)(2,1)S(1)} %get-tuple-element.170), channel_id=1, source_target_pairs={{0,2},{1,3},{2,0},{3,1},{4,6},{5,7},{6,4},{7,5},{8,10},{9,11},{10,... | collective-permute-start | bytes 2359304 | tf_op jit(solution)/shard_map/ppermute | solution.py:610
  76.3 21.9 %collective-permute-start.13 = (bf16[512,768]{1,0:T(8,128)(2,1)S(1)}, bf16[512,768]{1,0:T(8,128)(2,1)S(1)}, u32[]{:S(2)}, u32[]{:S(2)}) collective-permute-start(bf16[512,768]{1,0:T(8,128)(2,1)S(1)} %get-tuple-element.180), channel_id=1, source_target_pairs={{0,2},{1,3},{2,0},{3,1},{4,6},{5,7},{6,4},{7,5},{8,10},{9,11},{10,... | collective-permute-start | bytes 2359304 | tf_op jit(solution)/shard_map/ppermute | solution.py:610
  99.1 14.7 %collective-permute-start.19 = (bf16[768,768]{1,0:T(8,128)(2,1)}, bf16[768,768]{1,0:T(8,128)(2,1)}, u32[]{:S(2)}, u32[]{:S(2)}) collective-permute-start(bf16[768,768]{1,0:T(8,128)(2,1)} %get-tuple-element.199), channel_id=1, source_target_pairs={{0,1},{1,0},{2,3},{3,2},{4,5},{5,4},{6,7},{7,6},{8,9},{9,8},{10,11... | collective-permute-start | bytes 3538952 | tf_op jit(solution)/shard_map/ppermute | solution.py:610
  99.1 16.2 %collective-permute-start.17 = (bf16[768,768]{1,0:T(8,128)(2,1)}, bf16[768,768]{1,0:T(8,128)(2,1)}, u32[]{:S(2)}, u32[]{:S(2)}) collective-permute-start(bf16[768,768]{1,0:T(8,128)(2,1)} %get-tuple-element.194), channel_id=1, source_target_pairs={{0,1},{1,0},{2,3},{3,2},{4,5},{5,4},{6,7},{7,6},{8,9},{9,8},{10,11... | collective-permute-start | bytes 3538952 | tf_op jit(solution)/shard_map/ppermute | solution.py:610
  99.6 14.1 %collective-permute-start.14 = (bf16[512,768]{1,0:T(8,128)(2,1)}, bf16[512,768]{1,0:T(8,128)(2,1)}, u32[]{:S(2)}, u32[]{:S(2)}) collective-permute-start(bf16[512,768]{1,0:T(8,128)(2,1)} %get-tuple-element.161.refs_0_), channel_id=1, source_target_pairs={{0,1},{1,0},{2,3},{3,2},{4,5},{5,4},{6,7},{7,6},{8,9},{9,8},{10,11... | collective-permute-start | bytes 2359304 | tf_op jit(solution)/shard_map/ppermute | solution.py:610
  99.6 14.2 %collective-permute-start.15 = (bf16[512,768]{1,0:T(8,128)(2,1)}, bf16[512,768]{1,0:T(8,128)(2,1)}, u32[]{:S(2)}, u32[]{:S(2)}) collective-permute-start(bf16[512,768]{1,0:T(8,128)(2,1)} %get-tuple-element.177.refs_2_), channel_id=1, source_target_pairs={{0,1},{1,0},{2,3},{3,2},{4,5},{5,4},{6,7},{7,6},{8,9},{9,8},{10,11... | collective-permute-start | bytes 2359304 | tf_op jit(solution)/shard_map/ppermute | solution.py:610
  111.8 22.7 %collective-permute-start.21 = (bf16[512,768]{1,0:T(8,128)(2,1)S(1)}, bf16[512,768]{1,0:T(8,128)(2,1)S(1)}, u32[]{:S(2)}, u32[]{:S(2)}) collective-permute-start(bf16[512,768]{1,0:T(8,128)(2,1)S(1)} %copy-done.8), channel_id=1, source_target_pairs={{0,2},{1,3},{2,0},{3,1},{4,6},{5,7},{6,4},{7,5},{8,10},{9,11},{10,... | collective-permute-start | bytes 2359304 | tf_op jit(solution)/shard_map/ppermute | solution.py:610
  115.2 16.8 %collective-permute-start.20 = (bf16[384,768]{1,0:T(8,128)(2,1)S(1)}, bf16[384,768]{1,0:T(8,128)(2,1)S(1)}, u32[]{:S(2)}, u32[]{:S(2)}) collective-permute-start(bf16[384,768]{1,0:T(8,128)(2,1)S(1)} %add_convert_fusion.3), channel_id=1, source_target_pairs={{0,8},{4,12},{8,0},{12,4},{16,24},{20,28},{24,16},{28,20},{1,9},{5... | collective-permute-start | bytes 1769480 | tf_op jit(solution)/shard_map/ppermute | solution.py:613
  116.6 15.8 %collective-permute-start.18 = (bf16[384,768]{1,0:T(8,128)(2,1)S(1)}, bf16[384,768]{1,0:T(8,128)(2,1)S(1)}, u32[]{:S(2)}, u32[]{:S(2)}) collective-permute-start(bf16[384,768]{1,0:T(8,128)(2,1)S(1)} %add_convert_fusion.5), channel_id=1, source_target_pairs={{0,4},{4,0},{8,12},{12,8},{16,20},{20,16},{24,28},{28,24},{1,5},{5... | collective-permute-start | bytes 1769480 | tf_op jit(solution)/shard_map/ppermute | solution.py:613
  139.8 7.7 %collective-permute-start.22 = (bf16[192,512]{1,0:T(8,128)(2,1)}, bf16[192,512]{1,0:T(8,128)(2,1)S(1)}, u32[]{:S(2)}, u32[]{:S(2)}) collective-permute-start(bf16[192,512]{1,0:T(8,128)(2,1)} %copy-done.37), channel_id=1, source_target_pairs={{0,1},{1,0},{2,3},{3,2},{4,5},{5,4},{6,7},{7,6},{8,9},{9,8},{10,11... | collective-permute-start | bytes 589832 | tf_op jit(solution)/shard_map/ppermute | solution.py:610
  141.5 17.5 %collective-permute-start.25 = (bf16[192,768]{1,0:T(8,128)(2,1)S(1)}, bf16[192,768]{1,0:T(8,128)(2,1)S(1)}, u32[]{:S(2)}, u32[]{:S(2)}) collective-permute-start(bf16[192,768]{1,0:T(8,128)(2,1)S(1)} %get-tuple-element.295), channel_id=1, source_target_pairs={{0,4},{4,0},{8,12},{12,8},{16,20},{20,16},{24,28},{28,24},{1,5},{5... | collective-permute-start | bytes 884744 | tf_op jit(solution)/shard_map/ppermute | solution.py:613
  143.7 15.4 %collective-permute-start.24 = (bf16[192,768]{1,0:T(8,128)(2,1)S(1)}, bf16[192,768]{1,0:T(8,128)(2,1)S(1)}, u32[]{:S(2)}, u32[]{:S(2)}) collective-permute-start(bf16[192,768]{1,0:T(8,128)(2,1)S(1)} %get-tuple-element.297), channel_id=1, source_target_pairs={{0,8},{4,12},{8,0},{12,4},{16,24},{20,28},{24,16},{28,20},{1,9},{5... | collective-permute-start | bytes 884744 | tf_op jit(solution)/shard_map/ppermute | solution.py:613
  146.2 13.1 %collective-permute-start.26 = (bf16[128,768]{1,0:T(8,128)(2,1)S(1)}, bf16[128,768]{1,0:T(8,128)(2,1)S(1)}, u32[]{:S(2)}, u32[]{:S(2)}) collective-permute-start(bf16[128,768]{1,0:T(8,128)(2,1)S(1)} %add_convert_fusion.10), channel_id=1, source_target_pairs={{0,4},{4,0},{8,12},{12,8},{16,20},{20,16},{24,28},{28,24},{1,5},{5... | collective-permute-start | bytes 589832 | tf_op jit(solution)/shard_map/ppermute | solution.py:613
  160.6 21.7 %collective-permute-start.31 = (bf16[512,768]{1,0:T(8,128)(2,1)S(1)}, bf16[512,768]{1,0:T(8,128)(2,1)S(1)}, u32[]{:S(2)}, u32[]{:S(2)}) collective-permute-start(bf16[512,768]{1,0:T(8,128)(2,1)S(1)} %fusion), channel_id=1, source_target_pairs={{0,2},{1,3},{2,0},{3,1},{4,6},{5,7},{6,4},{7,5},{8,10},{9,11},{10,... | collective-permute-start | bytes 2359304 | tf_op jit(solution)/shard_map/ppermute | solution.py:610
  161.1 15.3 %collective-permute-start.30 = (bf16[64,768]{1,0:T(8,128)(2,1)S(1)}, bf16[64,768]{1,0:T(8,128)(2,1)S(1)}, u32[]{:S(2)}, u32[]{:S(2)}) collective-permute-start(bf16[64,768]{1,0:T(8,128)(2,1)S(1)} %get-tuple-element.314), channel_id=1, source_target_pairs={{0,8},{4,12},{8,0},{12,4},{16,24},{20,28},{24,16},{28,20},{1,9},{5... | collective-permute-start | bytes 294920 | tf_op jit(solution)/shard_map/ppermute | solution.py:613
  162.3 14.2 %collective-permute-start.29 = (bf16[96,768]{1,0:T(8,128)(2,1)S(1)}, bf16[96,768]{1,0:T(8,128)(2,1)S(1)}, u32[]{:S(2)}, u32[]{:S(2)}) collective-permute-start(bf16[96,768]{1,0:T(8,128)(2,1)S(1)} %get-tuple-element.308), channel_id=1, source_target_pairs={{0,16},{4,20},{8,24},{12,28},{16,0},{20,4},{24,8},{28,12},{1,17},{... | collective-permute-start | bytes 442376 | tf_op jit(solution)/shard_map/ppermute | solution.py:613
  165.0 14.1 %collective-permute-start.28 = (bf16[96,768]{1,0:T(8,128)(2,1)S(1)}, bf16[96,768]{1,0:T(8,128)(2,1)S(1)}, u32[]{:S(2)}, u32[]{:S(2)}) collective-permute-start(bf16[96,768]{1,0:T(8,128)(2,1)S(1)} %get-tuple-element.310), channel_id=1, source_target_pairs={{0,16},{4,20},{8,24},{12,28},{16,0},{20,4},{24,8},{28,12},{1,17},{... | collective-permute-start | bytes 442376 | tf_op jit(solution)/shard_map/ppermute | solution.py:613
  176.4 12.8 %collective-permute-start.36 = (bf16[32,768]{1,0:T(8,128)(2,1)S(1)}, bf16[32,768]{1,0:T(8,128)(2,1)S(1)}, u32[]{:S(2)}, u32[]{:S(2)}) collective-permute-start(bf16[32,768]{1,0:T(8,128)(2,1)S(1)} %get-tuple-element.318), channel_id=1, source_target_pairs={{0,16},{4,20},{8,24},{12,28},{16,0},{20,4},{24,8},{28,12},{1,17},{... | collective-permute-start | bytes 147464 | tf_op jit(solution)/shard_map/ppermute | solution.py:613
  179.2 11.8 %collective-permute-start.35 = (bf16[96,768]{1,0:T(8,128)(2,1)S(1)}, bf16[96,768]{1,0:T(8,128)(2,1)S(1)}, u32[]{:S(2)}, u32[]{:S(2)}) collective-permute-start(bf16[96,768]{1,0:T(8,128)(2,1)S(1)} %add_convert_fusion.11), channel_id=1, source_target_pairs={{0,16},{4,20},{8,24},{12,28},{16,0},{20,4},{24,8},{28,12},{1,17},{... | collective-permute-start | bytes 442376 | tf_op jit(solution)/shard_map/ppermute | solution.py:613
  179.6 14.0 %collective-permute-start.34 = (bf16[96,768]{1,0:T(8,128)(2,1)S(1)}, bf16[96,768]{1,0:T(8,128)(2,1)S(1)}, u32[]{:S(2)}, u32[]{:S(2)}) collective-permute-start(bf16[96,768]{1,0:T(8,128)(2,1)S(1)} %add_convert_fusion.12), channel_id=1, source_target_pairs={{0,16},{4,20},{8,24},{12,28},{16,0},{20,4},{24,8},{28,12},{1,17},{... | collective-permute-start | bytes 442376 | tf_op jit(solution)/shard_map/ppermute | solution.py:613
  187.2 19.5 %collective-permute-start.33 = (bf16[512,768]{1,0:T(8,128)(2,1)S(1)}, bf16[512,768]{1,0:T(8,128)(2,1)S(1)}, u32[]{:S(2)}, u32[]{:S(2)}) collective-permute-start(bf16[512,768]{1,0:T(8,128)(2,1)S(1)} %get-tuple-element.248), channel_id=1, source_target_pairs={{0,1},{1,0},{2,3},{3,2},{4,5},{5,4},{6,7},{7,6},{8,9},{9,8},{10,11... | collective-permute-start | bytes 2359304 | tf_op jit(solution)/shard_map/ppermute | solution.py:610
  187.4 19.3 %collective-permute-start.40 = (bf16[288,768]{1,0:T(8,128)(2,1)S(1)}, bf16[288,768]{1,0:T(8,128)(2,1)S(1)}, u32[]{:S(2)}, u32[]{:S(2)}) collective-permute-start(bf16[288,768]{1,0:T(8,128)(2,1)S(1)} %constant_dynamic-slice_fusion.3), channel_id=1, source_target_pairs={{0,4},{4,0},{8,12},{12,8},{16,20},{20,16},{24,28},{28,24},{1,5},{5... | collective-permute-start | bytes 1327112 | tf_op jit(solution)/shard_map/ppermute | solution.py:613
  193.8 12.6 %collective-permute-start.38 = (bf16[192,768]{1,0:T(8,128)(2,1)S(1)}, bf16[192,768]{1,0:T(8,128)(2,1)S(1)}, u32[]{:S(2)}, u32[]{:S(2)}) collective-permute-start(bf16[192,768]{1,0:T(8,128)(2,1)S(1)} %pad_maximum_fusion.7), channel_id=1, source_target_pairs={{0,4},{4,0},{8,12},{12,8},{16,20},{20,16},{24,28},{28,24},{1,5},{5... | collective-permute-start | bytes 884744 | tf_op jit(solution)/shard_map/ppermute | solution.py:613
  195.2 11.3 %collective-permute-start.37 = (bf16[192,768]{1,0:T(8,128)(2,1)S(1)}, bf16[192,768]{1,0:T(8,128)(2,1)S(1)}, u32[]{:S(2)}, u32[]{:S(2)}) collective-permute-start(bf16[192,768]{1,0:T(8,128)(2,1)S(1)} %pad_maximum_fusion.6), channel_id=1, source_target_pairs={{0,8},{4,12},{8,0},{12,4},{16,24},{20,28},{24,16},{28,20},{1,9},{5... | collective-permute-start | bytes 884744 | tf_op jit(solution)/shard_map/ppermute | solution.py:613
  198.9 75.9 %collective-permute-start.32 = (bf16[512,768]{1,0:T(8,128)(2,1)S(1)}, bf16[512,768]{1,0:T(8,128)(2,1)S(1)}, u32[]{:S(2)}, u32[]{:S(2)}) collective-permute-start(bf16[512,768]{1,0:T(8,128)(2,1)S(1)} %add_convert_fusion.1.refs_0_), channel_id=1, source_target_pairs={{0,1},{1,0},{2,3},{3,2},{4,5},{5,4},{6,7},{7,6},{8,9},{9,8},{10,11... | collective-permute-start | bytes 2359304 | tf_op jit(solution)/shard_map/ppermute | solution.py:610
  207.2 24.9 %collective-permute-start.44 = (bf16[384,768]{1,0:T(8,128)(2,1)S(1)}, bf16[384,768]{1,0:T(8,128)(2,1)S(1)}, u32[]{:S(2)}, u32[]{:S(2)}) collective-permute-start(bf16[384,768]{1,0:T(8,128)(2,1)S(1)} %pad_maximum_fusion.4), channel_id=1, source_target_pairs={{0,8},{4,12},{8,0},{12,4},{16,24},{20,28},{24,16},{28,20},{1,9},{5... | collective-permute-start | bytes 1769480 | tf_op jit(solution)/shard_map/ppermute | solution.py:613
  209.1 20.0 %collective-permute-start.46 = (bf16[72,768]{1,0:T(8,128)(2,1)S(1)}, bf16[72,768]{1,0:T(8,128)(2,1)S(1)}, u32[]{:S(2)}, u32[]{:S(2)}) collective-permute-start(bf16[72,768]{1,0:T(8,128)(2,1)S(1)} %get-tuple-element.299), channel_id=1, source_target_pairs={{0,8},{4,12},{8,0},{12,4},{16,24},{20,28},{24,16},{28,20},{1,9},{5... | collective-permute-start | bytes 331784 | tf_op jit(solution)/shard_map/ppermute | solution.py:613
  209.3 21.5 %collective-permute-start.47 = (bf16[72,768]{1,0:T(8,128)(2,1)S(1)}, bf16[72,768]{1,0:T(8,128)(2,1)S(1)}, u32[]{:S(2)}, u32[]{:S(2)}) collective-permute-start(bf16[72,768]{1,0:T(8,128)(2,1)S(1)} %get-tuple-element.301), channel_id=1, source_target_pairs={{0,16},{4,20},{8,24},{12,28},{16,0},{20,4},{24,8},{28,12},{1,17},{... | collective-permute-start | bytes 331784 | tf_op jit(solution)/shard_map/ppermute | solution.py:613
  214.1 17.9 %collective-permute-start.48 = (bf16[72,768]{1,0:T(8,128)(2,1)S(1)}, bf16[72,768]{1,0:T(8,128)(2,1)S(1)}, u32[]{:S(2)}, u32[]{:S(2)}) collective-permute-start(bf16[72,768]{1,0:T(8,128)(2,1)S(1)} %get-tuple-element.300), channel_id=1, source_target_pairs={{0,24},{4,28},{8,16},{12,20},{16,8},{20,12},{24,0},{28,4},{1,25},{... | collective-permute-start | bytes 331784 | tf_op jit(solution)/shard_map/ppermute | solution.py:613
  229.1 14.0 %collective-permute-start.43 = (bf16[384,768]{1,0:T(8,128)(2,1)S(1)}, bf16[384,768]{1,0:T(8,128)(2,1)S(1)}, u32[]{:S(2)}, u32[]{:S(2)}) collective-permute-start(bf16[384,768]{1,0:T(8,128)(2,1)S(1)} %pad_maximum_fusion.3), channel_id=1, source_target_pairs={{0,4},{4,0},{8,12},{12,8},{16,20},{20,16},{24,28},{28,24},{1,5},{5... | collective-permute-start | bytes 1769480 | tf_op jit(solution)/shard_map/ppermute | solution.py:613
  230.8 17.7 %collective-permute-start.41 = (bf16[512,768]{1,0:T(8,128)(2,1)S(1)}, bf16[512,768]{1,0:T(8,128)(2,1)S(1)}, u32[]{:S(2)}, u32[]{:S(2)}) collective-permute-start(bf16[512,768]{1,0:T(8,128)(2,1)S(1)} %fusion.1), channel_id=1, source_target_pairs={{0,2},{1,3},{2,0},{3,1},{4,6},{5,7},{6,4},{7,5},{8,10},{9,11},{10,... | collective-permute-start | bytes 2359304 | tf_op jit(solution)/shard_map/ppermute | solution.py:610
  248.5 7.2 %collective-permute-start.50 = (bf16[72,768]{1,0:T(8,128)(2,1)S(1)}, bf16[72,768]{1,0:T(8,128)(2,1)S(1)}, u32[]{:S(2)}, u32[]{:S(2)}) collective-permute-start(bf16[72,768]{1,0:T(8,128)(2,1)S(1)} %add_convert_fusion.13), channel_id=1, source_target_pairs={{0,8},{4,12},{8,0},{12,4},{16,24},{20,28},{24,16},{28,20},{1,9},{5... | collective-permute-start | bytes 331784 | tf_op jit(solution)/shard_map/ppermute | solution.py:613
  249.6 8.1 %collective-permute-start.51 = (bf16[72,768]{1,0:T(8,128)(2,1)S(1)}, bf16[72,768]{1,0:T(8,128)(2,1)S(1)}, u32[]{:S(2)}, u32[]{:S(2)}) collective-permute-start(bf16[72,768]{1,0:T(8,128)(2,1)S(1)} %add_convert_fusion.13), channel_id=1, source_target_pairs={{0,16},{4,20},{8,24},{12,28},{16,0},{20,4},{24,8},{28,12},{1,17},{... | collective-permute-start | bytes 331784 | tf_op jit(solution)/shard_map/ppermute | solution.py:613
  252.9 7.3 %collective-permute-start.49 = (bf16[128,768]{1,0:T(8,128)(2,1)S(1)}, bf16[128,768]{1,0:T(8,128)(2,1)S(1)}, u32[]{:S(2)}, u32[]{:S(2)}) collective-permute-start(bf16[128,768]{1,0:T(8,128)(2,1)S(1)} %pad_maximum_fusion.8), channel_id=1, source_target_pairs={{0,4},{4,0},{8,12},{12,8},{16,20},{20,16},{24,28},{28,24},{1,5},{5... | collective-permute-start | bytes 589832 | tf_op jit(solution)/shard_map/ppermute | solution.py:613
  260.3 8.4 %collective-permute-start.53 = (bf16[288,768]{1,0:T(8,128)(2,1)S(1)}, bf16[288,768]{1,0:T(8,128)(2,1)S(1)}, u32[]{:S(2)}, u32[]{:S(2)}) collective-permute-start(bf16[288,768]{1,0:T(8,128)(2,1)S(1)} %constant_dynamic-update-slice_fusion.3), channel_id=1, source_target_pairs={{0,4},{4,0},{8,12},{12,8},{16,20},{20,16},{24,28},{28,24},{1,5},{5... | collective-permute-start | bytes 1327112 | tf_op jit(solution)/shard_map/ppermute | solution.py:613
  265.6 9.1 %collective-permute-start.42 = (bf16[512,768]{1,0:T(8,128)(2,1)S(1)}, bf16[512,768]{1,0:T(8,128)(2,1)S(1)}, u32[]{:S(2)}, u32[]{:S(2)}) collective-permute-start(bf16[512,768]{1,0:T(8,128)(2,1)S(1)} %add_convert_fusion.refs_2_), channel_id=1, source_target_pairs={{0,1},{1,0},{2,3},{3,2},{4,5},{5,4},{6,7},{7,6},{8,9},{9,8},{10,11... | collective-permute-start | bytes 2359304 | tf_op jit(solution)/shard_map/ppermute | solution.py:610
  (96 other events, 543.3 us)

commit v3 on v2

--- a/solution.py
+++ b/solution.py
@@ -40,30 +40,7 @@
     return pl.CostEstimate(flops=int(micros * 1.1e9), bytes_accessed=1024, transcendentals=0)
 
 
-MICROS = {"attend_forward": 8, "attend_backward": 12, "entry_back": 5, "place": 3, "ahead": 9, "astern": 10, "inner_norm": 3, "weight_grads": 5}
-
-
-def project_kernel(x_ref, wq_ref, wk_ref, wv_ref, q_ref, k_ref, v_ref):
-    x = x_ref[...]
-    for w_ref, o_ref in ((wq_ref, q_ref), (wk_ref, k_ref), (wv_ref, v_ref)):
-        o_ref[:, :192] = nt(x, w_ref[...]).astype(BF)
-        o_ref[:, 192:] = jnp.zeros((x.shape[0], HEAD_DIM), BF)
-
-
-def project(tokens, wq, wk, wv):
-    rows, d = tokens.shape
-    block = 512
-    return pl.pallas_call(
-        project_kernel,
-        grid=(rows // block,),
-        in_specs=[pl.BlockSpec((block, d), lambda i: (i, 0))]
-        + [pl.BlockSpec((192, d), lambda i: (0, 0))] * 3,
-        out_specs=[pl.BlockSpec((block, 256), lambda i: (i, 0))] * 3,
-        out_shape=[jax.ShapeDtypeStruct((rows, 256), BF)] * 3,
-        compiler_params=params(48),
-        cost_estimate=cost(3),
-        name="project",
-    )(tokens, wq, wk, wv)
+MICROS = {"project": 3, "attend_forward": 8, "attend_backward": 12, "entry_back": 5, "place": 3, "ahead": 9, "astern": 10, "inner_norm": 3, "weight_grads": 5}
 
 
 def lane_parts(block):
@@ -80,7 +57,16 @@
 TILE = (0, 0, 1)
 
 
-def call(kernel, name, grid, meta, args, in_specs, out_specs, out_shape, scratch=(), limit=VMEM):
+def call(kernel, name, grid, meta, args, in_specs, out_specs, out_shape, scratch=(), limit=VMEM, free=()):
+    def place_input(i, value):
+        large = value.size * value.dtype.itemsize > MIB // 4
+        return pltpu.with_memory_space_constraint(value, pltpu.HBM) if large and i not in free else value
+
+    def place_output(shape):
+        large = shape.size * shape.dtype.itemsize > MIB // 4
+        return pltpu.HBM(shape.shape, shape.dtype) if large else shape
+
+    single = not isinstance(out_shape, list)
     return pl.pallas_call(
         kernel,
         grid_spec=pltpu.PrefetchScalarGridSpec(
@@ -90,11 +76,11 @@
             out_specs=out_specs,
             scratch_shapes=scratch,
         ),
-        out_shape=out_shape,
+        out_shape=place_output(out_shape) if single else [place_output(shape) for shape in out_shape],
         compiler_params=params(limit),
         cost_estimate=cost(MICROS[name]),
         name=name,
-    )(meta, *args)
+    )(meta, *(place_input(i, value) for i, value in enumerate(args)))
 
 
 def fixed(*shape):
@@ -105,7 +91,29 @@
     return jax.ShapeDtypeStruct(shape, dtype)
 
 
-def forward_kernel(u, meta_ref, q_ref, k_ref, v_ref, own_ref, other_ref, o32_ref, lse_ref, s_ref):
+def project_kernel(meta_ref, x_ref, wq_ref, wk_ref, wv_ref, q_ref, k_ref, v_ref):
+    x = x_ref[...]
+    for w_ref, o_ref in ((wq_ref, q_ref), (wk_ref, k_ref), (wv_ref, v_ref)):
+        o_ref[:, :192] = nt(x, w_ref[...]).astype(BF)
+        o_ref[:, 192:] = jnp.zeros((x.shape[0], HEAD_DIM), BF)
+
+
+def project(meta, tokens, weights):
+    rows, d = tokens.shape
+    block = 512
+    return call(
+        project_kernel,
+        "project",
+        (rows // block,),
+        meta,
+        (tokens, *weights),
+        [pl.BlockSpec((block, d), lambda i, m: (i, 0))] + [fixed(192, d)] * 3,
+        [pl.BlockSpec((block, 256), lambda i, m: (i, 0))] * 3,
+        [like((rows, 256), BF)] * 3,
+    )
+
+
+def forward_kernel(u, meta_ref, q_ref, k_ref, v_ref, own_ref, other_ref, lse_ref, s_ref):
     length = meta_ref[1 + u]
     step = pl.program_id(0)
     blocks = lax.div(length + KB - 1, KB)
@@ -147,7 +155,6 @@
         total, result = done[h]
         lo = HEAD_DIM * (h % 2)
         o = result[lo : lo + HEAD_DIM] / total
-        o32_ref[0, pl.ds(h * HEAD_DIM, HEAD_DIM), :] = o
         lse_ref[0, pl.ds(h, 1), :] = highest[h] * LOG2E + jnp.log2(total)
         outs.append(o.astype(BF))
     whole = jnp.concatenate(outs, axis=0)
@@ -174,13 +181,11 @@
         [
             fixed(192, half),
             fixed(192, half),
-            pl.BlockSpec((1, 192, half), lambda i, m: (i, 0, 0)),
             pl.BlockSpec((1, 8, half), lambda i, m: (i, 0, 0)),
         ],
         [
             like((192, half), BF),
             like((192, half), BF),
-            like((2, 192, half), F32),
             like((2, 8, half), F32),
         ],
         [pltpu.VMEM((3, frames, half), F32)],
@@ -188,8 +193,8 @@
 
 
 def backward_kernel(
-    u, meta_ref, q_ref, k_ref, v_ref, d0_ref, d1_ref, o32_ref, lse_ref,
-    dq_ref, dk_ref, dv_ref, kt_ref, dk_acc, dv_acc, do_ref,
+    u, meta_ref, q_ref, k_ref, v_ref, d0_ref, d1_ref, o0_ref, o1_ref, lse_ref,
+    dq_ref, dk_ref, dv_ref, kt_ref, dk_acc, dv_acc, do_ref, o_ref,
 ):
     length = meta_ref[1 + u]
     blocks = lax.div(length + KB - 1, KB)
@@ -201,10 +206,12 @@
         dv_acc[...] = jnp.zeros_like(dv_acc)
         kt_ref[...] = jnp.transpose(k_ref[...])
         do_ref[...] = d0_ref[...]
+        o_ref[...] = o0_ref[...]
 
     @pl.when(step == 1)
     def _():
         do_ref[...] = d1_ref[...]
+        o_ref[...] = o1_ref[...]
 
     parts = lane_parts(q_ref[...] * jnp.asarray(0.125, BF))
     width = q_ref.shape[0]
@@ -217,7 +224,7 @@
     )
     delta = [
         jnp.sum(
-            head[h].astype(F32) * o32_ref[0, pl.ds(h * HEAD_DIM, HEAD_DIM), :], axis=0, keepdims=True
+            head[h].astype(F32) * o_ref[pl.ds(h * HEAD_DIM, HEAD_DIM), :].astype(F32), axis=0, keepdims=True
         )
         for h in range(3)
     ]
@@ -252,21 +259,22 @@
         dv_ref[...] = dv_acc[...].astype(BF)
 
 
-def attend_backward(meta, q, k, v, own, other, o32, lse, u, frames):
+def attend_backward(meta, q, k, v, grads, outs, lse, u, frames):
     half = frames // 2
     return call(
         functools.partial(backward_kernel, u),
         "attend_backward",
         (2,),
         meta,
-        (q, k, v, own, other, o32, lse),
+        (q, k, v, *grads, *outs, lse),
         [
             pl.BlockSpec((half, 256), lambda i, m: (u * 2 + (i ^ m[0]), 0)),
             pl.BlockSpec((frames, 256), lambda i, m: (u, 0)),
             pl.BlockSpec((frames, 256), lambda i, m: (u, 0)),
             fixed(192, half),
             fixed(192, half),
-            pl.BlockSpec((1, 192, half), lambda i, m: (i, 0, 0)),
+            fixed(192, half),
+            fixed(192, half),
             pl.BlockSpec((1, 8, half), lambda i, m: (i, 0, 0)),
         ],
         [
@@ -279,6 +287,7 @@
             pltpu.VMEM((256, frames), BF),
             pltpu.VMEM((frames, 256), F32),
             pltpu.VMEM((frames, 256), F32),
+            pltpu.VMEM((192, half), BF),
             pltpu.VMEM((192, half), BF),
         ],
     )
@@ -381,47 +390,50 @@
 ):
     gain, bias = vec_ref[0:1, :], vec_ref[1:2, :]
     hidden = ua_ref.shape[1]
-    for r in range(tok_ref.shape[0] // RB):
-        rows = pl.ds(r * RB, RB)
-        branch = jnp.zeros((RB, tok_ref.shape[1]), F32)
-        for a, w in ((a0, w0), (a1, w1), (a2, w2), (a3, w3)):
-            branch = branch + tn(a[:, rows], w[...]).astype(BF).astype(F32)
-        xhat, rstd = normalise(tok_ref[rows, :].astype(F32) + branch)
-        xhat_ref[rows, :] = xhat
-        rstd_ref[rows, :] = jnp.broadcast_to(rstd, (RB, rstd_ref.shape[1]))
-        normed = xhat * gain + bias
-        low = normed.astype(BF)
-        low_ref[rows, :] = low
-        sent = jnp.zeros(normed.shape, F32)
-        for g, (up, down) in enumerate(((ua_ref, da_ref), (ub_ref, db_ref))):
-            acts = []
-            for c in range(hidden // HB):
-                act, slope = gelu_pair(nn(low, up[:, c * HB : (c + 1) * HB]))
-                columns = pl.ds(g * hidden + c * HB, HB)
-                acts.append(act.astype(BF))
-                act_ref[rows, columns] = acts[-1]
-                slope_ref[rows, columns] = slope.astype(BF)
-            sent = sent + nn(jnp.concatenate(acts, axis=1), down[...]).astype(BF).astype(F32)
-        own_ref[rows, :] = normed + sent
-        sent_ref[rows, :] = sent.astype(BF)
+    branch = jnp.zeros(tok_ref.shape, F32)
+    for a, w in ((a0, w0), (a1, w1), (a2, w2), (a3, w3)):
+        branch = branch + tn(a[...], w[...]).astype(BF).astype(F32)
+    xhat, rstd = normalise(tok_ref[...].astype(F32) + branch)
+    xhat_ref[...] = xhat
+    rstd_ref[...] = jnp.broadcast_to(rstd, rstd_ref.shape)
+    normed = xhat * gain + bias
+    low = normed.astype(BF)
+    low_ref[...] = low
+    sent = jnp.zeros(normed.shape, F32)
+    for g, (up, down) in enumerate(((ua_ref, da_ref), (ub_ref, db_ref))):
+        acts = []
+        for c in range(hidden // HB):
+            act, slope = gelu_pair(nn(low, up[:, c * HB : (c + 1) * HB]))
+            columns = pl.ds(g * hidden + c * HB, HB)
+            acts.append(act.astype(BF))
+            act_ref[:, columns] = acts[-1]
+            slope_ref[:, columns] = slope.astype(BF)
+        sent = sent + nn(jnp.concatenate(acts, axis=1), down[...]).astype(BF).astype(F32)
+    own_ref[...] = normed + sent
+    sent_ref[...] = sent.astype(BF)
+
+
+def rows_of(width):
+    return pl.BlockSpec((RB, width), lambda i, m: (i, 0))
 
 
 def ahead(meta, tokens, att, merge_w, up, down, vectors, u):
     half = att[0].shape[1]
     d, hidden = up[0].shape
+    steps = half // RB
     return call(
         ahead_kernel,
         "ahead",
-        (1,),
+        (steps,),
         meta,
         (tokens, *att, *merge_w, *up, *down, vectors),
-        [pl.BlockSpec((half, d), lambda i, m: (u * 2 + m[0], 0))]
-        + [fixed(192, half)] * 4
+        [pl.BlockSpec((RB, d), lambda i, m: ((u * 2 + m[0]) * steps + i, 0))]
+        + [pl.BlockSpec((192, RB), lambda i, m: (0, i))] * 4
         + [fixed(192, d)] * 4
         + [fixed(d, hidden)] * 2
         + [fixed(hidden, d)] * 2
         + [fixed(4, d)],
-        [fixed(half, d), fixed(half, 128), fixed(half, d), fixed(half, 2 * hidden), fixed(half, 2 * hidden), fixed(half, d), fixed(half, d)],
+        [rows_of(d), rows_of(128), rows_of(d), rows_of(2 * hidden), rows_of(2 * hidden), rows_of(d), rows_of(d)],
         [
             like((half, d), F32),
             like((half, 128), F32),
@@ -431,89 +443,101 @@
             like((half, d), F32),
             like((half, d), BF),
         ],
+        limit=24,
+        free=range(5, 13),
     )
 
 
 def astern_kernel(u, meta_ref, own_ref, far_ref, grad_ref, span_ref, ua_ref, ub_ref, da_ref, db_ref, slope_ref, vec_ref, *refs):
-    last = len(refs) > 6
-    before = refs[: len(refs) - 10] if last else ()
+    last = len(refs) > 7
+    before = refs[: len(refs) - 12] if last else ()
     out_ref, g_ref, pre_ref, back_ref, sent_ref, small_ref = refs[len(before) : len(before) + 6]
+    step = pl.program_id(0)
     gain, bias = vec_ref[2:3, :], vec_ref[3:4, :]
-    half, d = own_ref.shape
     hidden = ua_ref.shape[1]
     starts = span_ref[u : u + 1, :]
-    gain_grad = jnp.zeros(gain.shape, F32)
-    bias_grad = jnp.zeros(gain.shape, F32)
-    for r in range(half // RB):
-        rows = pl.ds(r * RB, RB)
-        xhat, rstd = normalise(own_ref[rows, :] + far_ref[rows, :].astype(F32))
-        out_ref[rows, :] = (xhat * gain + bias).astype(BF)
-        frame = meta_ref[0] * half + r * RB + lax.broadcasted_iota(jnp.int32, (RB, starts.shape[1]), 0)
-        inside = (frame >= starts) & (frame < starts + SPAN)
-        weight = jnp.max(jnp.where(inside, 1.0, 0.0), axis=1, keepdims=True)
-        cot = grad_ref[rows, :].astype(F32) * weight
-        gain_grad = gain_grad + jnp.sum(cot * xhat, axis=0, keepdims=True)
-        bias_grad = bias_grad + jnp.sum(cot, axis=0, keepdims=True)
-        gy = cot * gain
-        mean_gy = jnp.mean(gy, axis=-1, keepdims=True)
-        mean_gx = jnp.mean(gy * xhat, axis=-1, keepdims=True)
-        sum_grad = rstd * (gy - mean_gy - xhat * mean_gx)
-        low = sum_grad.astype(BF)
-        g_ref[rows, :] = low
-        sent = jnp.zeros(sum_grad.shape, F32)
-        for g, (up, down) in enumerate(((ua_ref, da_ref), (ub_ref, db_ref))):
-            pres = []
-            for c in range(hidden // HB):
-                columns = pl.ds(g * hidden + c * HB, HB)
-                slope = slope_ref[rows, columns].astype(F32)
-                pres.append((nt(low, down[c * HB : (c + 1) * HB, :]) * slope).astype(BF))
-                pre_ref[rows, columns] = pres[-1]
-            sent = sent + nt(jnp.concatenate(pres, axis=1), up[...]).astype(BF).astype(F32)
-        back_ref[rows, :] = sum_grad + sent
-        sent_ref[rows, :] = sent.astype(BF)
-    small_ref[0:1, :] = gain_grad
-    small_ref[1:2, :] = bias_grad
+    xhat, rstd = normalise(own_ref[...] + far_ref[...].astype(F32))
+    out_ref[...] = (xhat * gain + bias).astype(BF)
+    first = (meta_ref[0] * pl.num_programs(0) + step) * RB
+    frame = first + lax.broadcasted_iota(jnp.int32, (RB, starts.shape[1]), 0)
+    inside = (frame >= starts) & (frame < starts + SPAN)
+    weight = jnp.max(jnp.where(inside, 1.0, 0.0), axis=1, keepdims=True)
+    cot = grad_ref[...].astype(F32) * weight
+    gain_grad = jnp.sum(cot * xhat, axis=0, keepdims=True)
+    bias_grad = jnp.sum(cot, axis=0, keepdims=True)
+    gy = cot * gain
+    mean_gy = jnp.mean(gy, axis=-1, keepdims=True)
+    mean_gx = jnp.mean(gy * xhat, axis=-1, keepdims=True)
+    sum_grad = rstd * (gy - mean_gy - xhat * mean_gx)
+    low = sum_grad.astype(BF)
+    g_ref[...] = low
+    sent = jnp.zeros(sum_grad.shape, F32)
+    pres = []
+    for g, (up, down) in enumerate(((ua_ref, da_ref), (ub_ref, db_ref))):
+        for c in range(hidden // HB):
+            columns = pl.ds(g * hidden + c * HB, HB)
+            slope = slope_ref[:, columns].astype(F32)
+            pres.append((nt(low, down[c * HB : (c + 1) * HB, :]) * slope).astype(BF))
+            pre_ref[:, columns] = pres[-1]
+        group = jnp.concatenate(pres[g * (hidden // HB) :], axis=1)
+        sent = sent + nt(group, up[...]).astype(BF).astype(F32)
+    back_ref[...] = sum_grad + sent
+    sent_ref[...] = sent.astype(BF)
+
+    @pl.when(step == 0)
+    def _():
+        small_ref[0:1, :] = gain_grad
+        small_ref[1:2, :] = bias_grad
+
+    @pl.when(step > 0)
+    def _():
+        small_ref[0:1, :] += gain_grad
+        small_ref[1:2, :] += bias_grad
+
     if last:
         x_ref, act_ref = before[:2]
-        weight_sums(x_ref[...], g_ref[...], act_ref, pre_ref, before[2:], refs[-4:])
+        all_g, all_pre = refs[-2:]
+        rows = pl.ds(pl.multiple_of(step * RB, RB), RB)
+        all_g[rows, :] = low
+        all_pre[rows, :] = jnp.concatenate(pres, axis=1)
+
+        @pl.when(step == pl.num_programs(0) - 1)
+        def _():
+            weight_sums(x_ref[...], all_g[...], act_ref, all_pre, before[2:], refs[-6:-2])
 
 
 def astern(meta, own, far, grad, spans, up, down, slope, vectors, u, before):
     half, d = own.shape
     hidden = up[0].shape[1]
-    rows = fixed(half, d)
-    wide = fixed(half, 2 * hidden)
+    steps = half // RB
+    wide = 2 * hidden
     grads = [] if not before else [(d, hidden)] * 2 + [(hidden, d)] * 2
-    extra = [] if not before else [rows, wide] + [fixed(*shape) for shape in grads[: len(before) - 2]]
+    extra = [] if not before else [fixed(half, d), fixed(half, wide)] + [fixed(*shape) for shape in grads[: len(before) - 2]]
     return call(
         functools.partial(astern_kernel, u),
         "astern",
-        (1,),
+        (steps,),
         meta,
         (own, far, grad, spans, *up, *down, slope, vectors, *before),
-        [rows] * 2
-        + [pl.BlockSpec((half, d), lambda i, m: (u * 2 + m[0], 0)), fixed(*spans.shape)]
+        [rows_of(d), rows_of(d), pl.BlockSpec((RB, d), lambda i, m: ((u * 2 + m[0]) * steps + i, 0)), fixed(*spans.shape)]
         + [fixed(d, hidden)] * 2
         + [fixed(hidden, d)] * 2
-        + [wide, fixed(4, d)]
+        + [rows_of(wide), fixed(4, d)]
         + extra,
-        [rows, rows, wide, rows, rows, fixed(2, d)] + [fixed(*shape) for shape in grads],
+        [rows_of(d), rows_of(d), rows_of(wide), rows_of(d), rows_of(d), fixed(2, d)] + [fixed(*shape) for shape in grads],
         [
             like((half, d), BF),
             like((half, d), BF),
-            like((half, 2 * hidden), BF),
+            like((half, wide), BF),
             like((half, d), F32),
             like((half, d), BF),
             like((2, d), F32),
         ]
         + [like(shape, BF) for shape in grads],
-        limit=28 if before else VMEM,
-    )
-
-
-def weight_kernel(meta_ref, x_ref, g_ref, act_ref, pre_ref, *refs):
-    before, sums = refs[:-4], refs[-4:]
-    weight_sums(x_ref[...], g_ref[...], act_ref, pre_ref, before, sums)
+        [pltpu.VMEM((half, d), BF), pltpu.VMEM((half, wide), BF)] if before else [pltpu.VMEM((8, 128), F32)],
+        limit=44 if before else 24,
+        free=(4, 5, 6, 7, *range(12, 16)),
+    )
 
 
 def weight_sums(x, g, act_ref, pre_ref, before, sums):
@@ -531,26 +555,49 @@
             sums[2 + i][block, :] = down.astype(BF)
 
 
+def weight_kernel(per, meta_ref, x_ref, g_ref, act_ref, pre_ref, *refs):
+    step = pl.program_id(0)
+    before, sums = refs[:-4], refs[-4:]
+    up = tn(x_ref[...], pre_ref[...])
+    down = tn(act_ref[...], g_ref[...])
+    for i in range(2):
+
+        @pl.when((step >= i * per) & (step < (i + 1) * per))
+        def _():
+            if before:
+                sums[i][...] = (up + before[i][...].astype(F32)).astype(BF)
+                sums[2 + i][...] = (down + before[2 + i][...].astype(F32)).astype(BF)
+            else:
+                sums[i][...] = up.astype(BF)
+                sums[2 + i][...] = down.astype(BF)
+
+
 def weight_grads(meta, x, g, act, pre, before):
     rows, d = x.shape
     hidden = act.shape[1] // 2
-    shapes = [(d, hidden)] * 2 + [(hidden, d)] * 2
+    per = hidden // HB
+
+    def at(group, i):
+        return jnp.minimum(i, per - 1) if group == 0 else jnp.maximum(i - per, 0)
+
+    blocks = [pl.BlockSpec((d, HB), lambda i, m, g=g: (0, at(g, i))) for g in range(2)]
+    blocks += [pl.BlockSpec((HB, d), lambda i, m, g=g: (at(g, i), 0)) for g in range(2)]
     return call(
-        weight_kernel,
+        functools.partial(weight_kernel, per),
         "weight_grads",
-        (1,),
+        (2 * per,),
         meta,
         (x, g, act, pre, *before),
-        [fixed(rows, d)] * 2 + [fixed(rows, 2 * hidden)] * 2 + [fixed(*shape) for shape in shapes[: len(before)]],
-        [fixed(*shape) for shape in shapes],
-        [like(shape, BF) for shape in shapes],
-        limit=24,
+        [fixed(rows, d)] * 2 + [pl.BlockSpec((rows, HB), lambda i, m: (0, i))] * 2 + blocks[: len(before)],
+        blocks,
+        [like((d, hidden), BF)] * 2 + [like((hidden, d), BF)] * 2,
     )
 
 
 def inner_kernel(meta_ref, own_ref, far_ref, xhat_ref, rstd_ref, vec_ref, a0, a1, w0, w1, *refs):
-    last = len(refs) == 11
-    out_ref, g0, g1, m0, m1, small_ref = refs[-6:]
+    last = len(refs) == 14
+    out_ref, g0, g1, m0, m1, small_ref, acc0, acc1, acc_small = refs[-9:]
+    step = pl.program_id(0)
     grad = own_ref[...] + far_ref[...].astype(F32)
     xhat = xhat_ref[...]
     gain_grad = jnp.sum(grad * xhat, axis=0, keepdims=True)
@@ -563,37 +610,62 @@
     low = inner.astype(BF)
     g0[...] = nt(w0[...], low).astype(BF)
     g1[...] = nt(w1[...], low).astype(BF)
-    small = jnp.concatenate([gain_grad, bias_grad], axis=0)
-    small_ref[...] = small
-    if last:
-        before0, before1, before_small, outer0, outer1 = refs[:5]
-        below = jnp.concatenate(
-            [small + before_small[...], outer0[...] + outer1[...], jnp.zeros((60, small.shape[1]), F32)], axis=0
-        ).astype(BF)
-        for m, a, before in ((m0, a0, before0), (m1, a1, before1)):
-            m[:192, :] = (nn(a[...], low) + before[...]).astype(BF)
-            m[192:, :] = below
-    else:
-        m0[...] = nn(a0[...], low)
-        m1[...] = nn(a1[...], low)
+    merge0, merge1 = nn(a0[...], low), nn(a1[...], low)
+
+    @pl.when(step == 0)
+    def _():
+        if last:
+            acc0[...] = merge0 + refs[0][...]
+            acc1[...] = merge1 + refs[1][...]
+            acc_small[0:1, :] = gain_grad + refs[2][0:1, :]
+            acc_small[1:2, :] = bias_grad + refs[2][1:2, :]
+        else:
+            acc0[...] = merge0
+            acc1[...] = merge1
+            acc_small[0:1, :] = gain_grad
+            acc_small[1:2, :] = bias_grad
+
+    @pl.when(step > 0)
+    def _():
+        acc0[...] += merge0
+        acc1[...] += merge1
+        acc_small[0:1, :] += gain_grad
+        acc_small[1:2, :] += bias_grad
+
+    @pl.when(step == pl.num_programs(0) - 1)
+    def _():
+        small = acc_small[0:2, :]
+        small_ref[...] = small
+        if last:
+            zeros = jnp.zeros((60, small.shape[1]), F32)
+            below = jnp.concatenate([small, refs[3][...] + refs[4][...], zeros], axis=0).astype(BF)
+            for m, acc in ((m0, acc0), (m1, acc1)):
+                m[:192, :] = acc[...].astype(BF)
+                m[192:, :] = below
+        else:
+            m0[...] = acc0[...]
+            m1[...] = acc1[...]
 
 
 def inner_norm(meta, own, far, xhat, rstd, vectors, att, weights, before):
     rows, d = xhat.shape
     merge = like((256, d), BF) if before else like((192, d), F32)
+    lanes = pl.BlockSpec((192, RB), lambda i, m: (0, i))
     return call(
         inner_kernel,
         "inner_norm",
-        (1,),
+        (rows // RB,),
         meta,
         (own, far, xhat, rstd, vectors, *att, *weights, *before),
-        [fixed(rows, d)] * 3
-        + [fixed(rows, 128), fixed(4, d)]
-        + [fixed(192, rows)] * 2
+        [rows_of(d)] * 3
+        + [rows_of(128), fixed(4, d)]
+        + [lanes] * 2
         + [fixed(192, d)] * 2
         + ([fixed(192, d)] * 2 + [fixed(2, d)] * 3 if before else []),
-        [fixed(rows, d), fixed(192, rows), fixed(192, rows), fixed(*merge.shape), fixed(*merge.shape), fixed(2, d)],
+        [rows_of(d), lanes, lanes, fixed(*merge.shape), fixed(*merge.shape), fixed(2, d)],
         [like((rows, d), F32), like((192, rows), BF), like((192, rows), BF), merge, merge, like((2, d), F32)],
+        [pltpu.VMEM((192, d), F32)] * 2 + [pltpu.VMEM((8, d), F32)],
+        free=(7, 8),
     )
 
 
@@ -623,39 +695,46 @@
         return sum(piece.astype(F32) for piece in pieces).astype(BF) if len(pieces) > 1 else pieces[0]
 
     class Chain:
-        def __init__(self, parts, order):
+        def __init__(self, parts, order, back=None):
             self.parts = parts
-            self.steps = [(True, *stage) for stage in order] + [(False, *stage) for stage in reversed(order)]
+            self.order = order
+            self.held = list(order)
+            self.steps = [(True, *stage) for stage in order] + [(False, *stage) for stage in back or reversed(order)]
 
         def start(self):
             if self.steps:
                 scatter, low_bit, width = self.steps[0]
                 count = 1 << width
                 spot = (place_dp >> low_bit) & (count - 1)
-                pick = lambda j: [cut(part, spot ^ j, count) if scatter else part for part in self.parts]
-                got = [swap_dp(total(pick(j)), j << low_bit) for j in range(1, count)]
-                self.pending = pick(0) + got
+                pick = lambda j: total([cut(part, spot ^ j, count) if scatter else part for part in self.parts])
+                self.pending = [swap_dp(pick(j), j << low_bit) for j in range(1, count)]
 
         def finish(self, *after):
             if not self.steps:
                 return
             scatter, low_bit, width = self.steps.pop(0)
-            pieces = self.pending
+            got = self.pending
             if after:
-                pieces = lax.optimization_barrier((*pieces, *after))[: len(pieces)]
+                got = list(lax.optimization_barrier((*got, *after))[: len(got)])
             count = 1 << width
             spot = (place_dp >> low_bit) & (count - 1)
             if scatter:
-                self.state = total(pieces)
-            elif count == 2:
-                one, two = pieces
-                self.state = jnp.concatenate([jnp.where(spot, two, one), jnp.where(spot, one, two)], axis=0)
+                self.state = total([cut(part, spot, count) for part in self.parts] + got)
+                if all(step[0] is False for step in self.steps):
+                    self.state = self.state.reshape((1,) * len(self.order) + self.state.shape)
             else:
-                size = pieces[0].shape[0]
-                whole = jnp.zeros((size * count, d), BF)
-                for j in range(count):
-                    whole = lax.dynamic_update_slice_in_dim(whole, pieces[j], (spot ^ j) * size, 0)
-                self.state = whole
+                axis = self.order.index((low_bit, width))
+                mine = self.parts[0]
+                if count == 2:
+                    halves = [jnp.where(spot, got[0], mine), jnp.where(spot, mine, got[0])]
+                    self.state = jnp.concatenate(halves, axis=axis)
+                else:
+                    whole = jnp.zeros(mine.shape[:axis] + (count,) + mine.shape[axis + 1 :], BF)
+                    for j, piece in enumerate([mine] + got):
+                        whole = lax.dynamic_update_slice_in_dim(whole, piece, spot ^ j, axis)
+                    self.state = whole
+                if not self.steps:
+                    self.state = self.state.reshape(-1, d)
             self.parts = (self.state,)
 
     scalars = jnp.concatenate([core.reshape(1), lengths])
@@ -674,7 +753,7 @@
     vectors = jnp.stack([ig, ib, og, ob])
     qkv_w = (wq.T, wk.T, wv.T)
 
-    q, k, v = project(tokens, *qkv_w)
+    q, k, v = project(scalars, tokens, qkv_w)
     fwd, att = [], []
     for u in range(seqs):
         fwd.append(done(attend_forward(meta(), q, k, v, u, frames), *merge_w[1:], up_w[1], down_w[1]))
@@ -699,7 +778,7 @@
         return res, (res[1], swap(res[2], 1))
 
     def attend_step(u, grads):
-        return done(attend_backward(meta(), q, k, v, *grads, fwd[u][2], fwd[u][3], u, frames))
+        return done(attend_backward(meta(), q, k, v, grads, fwd[u][:2], fwd[u][2], u, frames))
 
     def entry_step(u, grads, before, dtype):
         return done(entry_back(meta(), tokens, grads, qkv_w, before, u, frames, dtype))
@@ -732,7 +811,7 @@
         if u == 0:
             up_own, up_other, down_own, down_other = lax.optimization_barrier((*back[-1][6:], far_grad[0]))[:4]
             ffn.append(Chain((down_own, swap(down_other, 1)), pairs))
-            ffn.append(Chain((up_own, swap(up_other, 1)), pairs[1:2] + pairs[:1] + pairs[2:]))
+            ffn.append(Chain((up_own, swap(up_other, 1)), pairs[1:2] + pairs[:1] + pairs[2:], pairs[::-1]))
             res, grads = inner_step(0, ())
             start(ffn)
             inner.append(res)

time: 281 us -> 292 us (1.039)
  Pallas kernels: 104 us -> 136 us
  local copies, waits for them, and re-layouts: 39.6 us -> 17.6 us
  starting transfers between devices: 49.3 us -> 56.8 us
  waiting for transfers between devices: 68.4 us -> 63.9 us
    pallas_call x15 -> x16, Pallas kernels: 99.2 us -> 136 us  [call(): pl.pallas_call(kernel, grid_spec=pltpu.PrefetchScalarGridSpec(num_scalar_...]
    unnamed x180 -> x112, local copies, waits for them, and re-layouts: 32.7 us -> 14.3 us
    ppermute x28, waiting for transfers between devices: 16.7 us -> 8.39 us  [swap(): return lax.ppermute(value, 'tensor', [(i, i ^ k) for i in range(4)])]
    ppermute x26, starting transfers between devices: 32.7 us -> 40.9 us  [swap_dp(): return lax.ppermute(value, 'dp', [(i, i ^ k) for i in range(groups)])]
    pallas_call x1 -> x0, Pallas kernels: 4.75 us -> none  [project(): pl.pallas_call(project_kernel, grid=(rows // block,), in_specs=[pl.BlockS...]
    ppermute x26, waiting for transfers between devices: 51.7 us -> 55.5 us  [swap_dp(): return lax.ppermute(value, 'dp', [(i, i ^ k) for i in range(groups)])]
    dynamic_slice x13 -> x8, local copies, waits for them, and re-layouts: 6.17 us -> 2.6 us  [cut(): return lax.dynamic_slice_in_dim(array, index * size, size, 0)]
    convert_element_type x14 -> x9, other arithmetic: 6.29 us -> 4.36 us  [total(): sum((piece.astype(F32) for piece in pieces)).astype(BF)]
  transfers between devices with their start and end apart: 54 -> 54, of which waited for: 19 -> 15; matrix products, arithmetic and copies ran while one was open for 8% -> 5% of each run, Pallas kernels for 35% -> 43%
where the time goes in v3:
time: 292 us; the launch traced here: 289 us
  Pallas kernels  136 us (47%)
  waiting for transfers between devices  63.9 us (22%)
  starting transfers between devices  56.8 us (19%)
  local copies, waits for them, and re-layouts  17.6 us (6%)
  other arithmetic  12.8 us (4%)
    pallas_call x16, Pallas kernels, call(): pl.pallas_call(kernel, grid_spec=pltpu.PrefetchScalarGridSpec(num_scalar_...  136 us
    ppermute x26, waiting for transfers between devices, swap_dp(): return lax.ppermute(value, 'dp', [(i, i ^ k) for i in range(groups)])  55.5 us
    ppermute x26, starting transfers between devices, swap_dp(): return lax.ppermute(value, 'dp', [(i, i ^ k) for i in range(groups)])  40.9 us
    ppermute x28, starting transfers between devices, swap(): return lax.ppermute(value, 'tensor', [(i, i ^ k) for i in range(4)])  15.9 us
    unnamed x112, local copies, waits for them, and re-layouts  14.3 us
    ppermute x28, waiting for transfers between devices, swap(): return lax.ppermute(value, 'tensor', [(i, i ^ k) for i in range(4)])  8.39 us
  transfers between devices with their start and end apart: 54, of which 15 were waited for; matrix products, arithmetic and copies ran while one was open for 5% of the time, Pallas kernels for 43%

profile of v3, /device:TPU:0, one launch (start us, length us, event | category | flops | bytes accessed | tf_op | source)
XLA Modules:
  0.0 288.7 jit_solution(13345388077531739582)
XLA Ops:
  1.2 2.6 collective-permute-start.1
  5.0 6.6 %project.1 = (bf16[2048,256]{1,0:T(8,128)(2,1)}, bf16[2048,256]{1,0:T(8,128)(2,1)}, bf16[2048,256]{1,0:T(8,128)(2,1)}) custom-call(s32[3]{0:T(128)S(1)} %pad_add_fusion.meta_ref, bf16[2048,768]{1,0:T(8,128)(2,1)} %x_ref.5, bf16[192,768]{1,0:T(8,128)(2,1)} %bitcast.27, bf16[192,768]{1,0:T(8,128)(2,1)} %bitcast.30, bf16[192,768]{1,0:T(8,128)(2,1)} %bitcast.33), custom_call_target="tpu_custom_call" | custom-call | flops 3300000000 | bytes 1024 | tf_op jit(solution)/shard_map/project/pallas_call | solution.py:70
  11.6 3.9 %attend_forward.2 = (bf16[192,512]{1,0:T(8,128)(2,1)S(1)}, bf16[192,512]{1,0:T(8,128)(2,1)S(1)}, f32[2,8,512]{2,1,0:T(8,128)S(1)}) custom-call(s32[3]{0:T(128)S(1)} %pad_add_fusion.meta_ref, bf16[2048,256]{1,0:T(8,128)(2,1)} %get-tuple-element.129.q_ref, bf16[2048,256]{1,0:T(8,128)(2,1)} %get-tuple-element.130.k_ref, bf16[2048,256]{1,0:T(8,128)(2,1)} %get-tuple-element.131.v_ref), custom_call_target="tpu_custom_call" | custom-call | flops 8800000000 | bytes 1024 | tf_op jit(solution)/shard_map/attend_forward/pallas_call | solution.py:70
  16.4 1.7 collective-permute-start.7
  19.2 9.0 %attend_forward.3 = (bf16[192,512]{1,0:T(8,128)(2,1)S(1)}, bf16[192,512]{1,0:T(8,128)(2,1)S(1)}, f32[2,8,512]{2,1,0:T(8,128)S(1)}) custom-call(s32[3]{0:T(128)S(1)} %pad_add_fusion.meta_ref, bf16[2048,256]{1,0:T(8,128)(2,1)} %get-tuple-element.129.q_ref, bf16[2048,256]{1,0:T(8,128)(2,1)} %get-tuple-element.130.k_ref, bf16[2048,256]{1,0:T(8,128)(2,1)} %get-tuple-element.131.v_ref), custom_call_target="tpu_custom_call" | custom-call | flops 8800000000 | bytes 1024 | tf_op jit(solution)/shard_map/attend_forward/pallas_call | solution.py:70
  31.0 10.5 %ahead.2 = (f32[512,768]{1,0:T(8,128)}, f32[512,128]{1,0:T(8,128)S(1)}, bf16[512,768]{1,0:T(8,128)(2,1)}, bf16[512,1536]{1,0:T(8,128)(2,1)}, bf16[512,1536]{1,0:...) custom-call(s32[3]{0:T(128)S(1)} %pad_add_fusion.meta_ref, bf16[2048,768]{1,0:T(8,128)(2,1)} %x_ref.5, ...), custom_call_target="tpu_custom_call" | custom-call | flops 9900000256 | bytes 1024 | tf_op jit(solution)/shard_map/ahead/pallas_call | solution.py:70
  43.3 10.5 %ahead.3 = (f32[512,768]{1,0:T(8,128)}, f32[512,128]{1,0:T(8,128)S(1)}, bf16[512,768]{1,0:T(8,128)(2,1)}, bf16[512,1536]{1,0:T(8,128)(2,1)}, bf16[512,1536]{1,0:...) custom-call(s32[3]{0:T(128)S(1)} %pad_add_fusion.meta_ref, bf16[2048,768]{1,0:T(8,128)(2,1)} %x_ref.5, ...), custom_call_target="tpu_custom_call" | custom-call | flops 9900000256 | bytes 1024 | tf_op jit(solution)/shard_map/ahead/pallas_call | solution.py:70
  54.9 8.0 %collective-permute-done.11.far_ref = bf16[512,768]{1,0:T(8,128)(2,1)S(1)} collective-permute-done((bf16[512,768]{1,0:T(8,128)(2,1)}, bf16[512,768]{1,0:T(8,128)(2,1)S(1)}, u32[]{:S(2)}, u32[]{:S(2)}) %collective-permute-start.11) | collective-permute-done | bytes 786464 | tf_op jit(solution)/shard_map/ppermute | solution.py:682
  63.8 10.9 %astern.2 = (bf16[512,768]{1,0:T(8,128)(2,1)}, bf16[512,768]{1,0:T(8,128)(2,1)}, bf16[512,1536]{1,0:T(8,128)(2,1)}, f32[512,768]{1,0:T(8,128)}, bf16[512,768]{1,0:T(8,128)(2,1)}, /*index=5*/f32[2,768]{1,0:T(2,128)S(1)}) custom-call(s32[3]{0:T(128)S(1)} %pad_add_fusion.meta_ref, f32[512,768]{1,0:T(8,128)} %get-tuple-element.142.own_ref, ...), custom_call_target="tpu_custom_call" | custom-call | flops 11000000512 | bytes 1024 | tf_op jit(solution)/shard_map/astern/pallas_call | solution.py:70
  74.7 8.9 %weight_grads.1 = (bf16[768,768]{1,0:T(8,128)(2,1)}, bf16[768,768]{1,0:T(8,128)(2,1)}, bf16[768,768]{1,0:T(8,128)(2,1)}, bf16[768,768]{1,0:T(8,128)(2,1)}) custom-call(s32[3]{0:T(128)S(1)} %pad_add_fusion.meta_ref, bf16[512,768]{1,0:T(8,128)(2,1)} %get-tuple-element.147.x_ref, bf16[512,768]{1,0:T(8,128)(2,1)} %get-tuple-element.148.g_ref, ...), custom_call_target="tpu_custom_call" | custom-call | flops 5500000256 | bytes 1024 | tf_op jit(solution)/shard_map/weight_grads/pallas_call | solution.py:70
  90.7 16.5 %astern.3 = (bf16[512,768]{1,0:T(8,128)(2,1)}, bf16[512,768]{1,0:T(8,128)(2,1)}, bf16[512,1536]{1,0:T(8,128)(2,1)}, f32[512,768]{1,0:T(8,128)}, bf16[512,768]{1,...) custom-call(s32[3]{0:T(128)S(1)} %pad_add_fusion.meta_ref, ...), custom_call_target="tpu_custom_call" | custom-call | flops 11000000512 | bytes 1024 | tf_op jit(solution)/shard_map/astern/pallas_call | solution.py:70
  110.1 6.9 %inner_norm.2 = (f32[512,768]{1,0:T(8,128)}, bf16[192,512]{1,0:T(8,128)(2,1)S(1)}, bf16[192,512]{1,0:T(8,128)(2,1)S(1)}, f32[192,768]{1,0:T(8,128)}, f32[192,768]{1,0:T(8,128)}, /*index=5*/f32[2,768]{1,0:T(2,128)S(1)}) custom-call(s32[3]{0:T(128)S(1)} %pad_add_fusion.meta_ref, f32[512,768]{1,0:T(8,128)} %get-tuple-element.163.own_ref, ...), custom_call_target="tpu_custom_call" | custom-call | flops 3300000000 | bytes 1024 | tf_op jit(solution)/shard_map/inner_norm/pallas_call | solution.py:70
  119.4 3.9 %collective-permute-start.20 = (bf16[384,768]{1,0:T(8,128)(2,1)S(1)}, bf16[384,768]{1,0:T(8,128)(2,1)S(1)}, u32[]{:S(2)}, u32[]{:S(2)}) collective-permute-start(bf16[384,768]{1,0:T(8,128)(2,1)S(1)} %add_convert_fusion.3), channel_id=1, source_target_pairs={{0,8},{4,12},{8,0},{12,4},{16,24},{20,28},{24,16},{28,20},{1,9},{5... | collective-permute-start | bytes 1769480 | tf_op jit(solution)/shard_map/ppermute | solution.py:685
  123.5 3.6 %collective-permute-start.18 = (bf16[384,768]{1,0:T(8,128)(2,1)S(1)}, bf16[384,768]{1,0:T(8,128)(2,1)S(1)}, u32[]{:S(2)}, u32[]{:S(2)}) collective-permute-start(bf16[384,768]{1,0:T(8,128)(2,1)S(1)} %add_convert_fusion.5), channel_id=1, source_target_pairs={{0,4},{4,0},{8,12},{12,8},{16,20},{20,16},{24,28},{28,24},{1,5},{5... | collective-permute-start | bytes 1769480 | tf_op jit(solution)/shard_map/ppermute | solution.py:685
  127.0 6.3 %attend_backward.2 = (bf16[1024,256]{1,0:T(8,128)(2,1)}, bf16[1024,256]{1,0:T(8,128)(2,1)}, bf16[1024,256]{1,0:T(8,128)(2,1)}) custom-call(s32[3]{0:T(128)S(1)} %pad_add_fusion.meta_ref, bf16[2048,256]{1,0:T(8,128)(2,1)} %get-tuple-element.129.q_ref, bf16[2048,256]{1,0:T(8,128)(2,1)} %get-tuple-element.130.k_ref, ...), custom_call_target="tpu_custom_call" | custom-call | flops 13200000000 | bytes 1024 | tf_op jit(solution)/shard_map/attend_backward/pallas_call | solution.py:70
  133.4 3.9 %collective-permute-done.20 = bf16[384,768]{1,0:T(8,128)(2,1)S(1)} collective-permute-done((bf16[384,768]{1,0:T(8,128)(2,1)S(1)}, bf16[384,768]{1,0:T(8,128)(2,1)S(1)}, u32[]{:S(2)}, u32[]{:S(2)}) %collective-permute-start.20) | collective-permute-done | bytes 589856 | tf_op jit(solution)/shard_map/ppermute | solution.py:685
  137.3 3.4 %collective-permute-done.18 = bf16[384,768]{1,0:T(8,128)(2,1)S(1)} collective-permute-done((bf16[384,768]{1,0:T(8,128)(2,1)S(1)}, bf16[384,768]{1,0:T(8,128)(2,1)S(1)}, u32[]{:S(2)}, u32[]{:S(2)}) %collective-permute-start.18) | collective-permute-done | bytes 589856 | tf_op jit(solution)/shard_map/ppermute | solution.py:685
  143.2 7.3 %inner_norm.3 = (f32[512,768]{1,0:T(8,128)}, bf16[192,512]{1,0:T(8,128)(2,1)S(1)}, bf16[192,512]{1,0:T(8,128)(2,1)S(1)}, bf16[256,768]{1,0:T(8,128)(2,1)}, bf16[256,768]{1,0:T(8,128)(2,1)}, /*index=5*/f32[2,768]{1,0:T(2,128)}) custom-call(s32[3]{0:T(128)S(1)} %pad_add_fusion.meta_ref, f32[512,768]{1,0:T(8,128)} %get-tuple-element.183.own_ref, ...), custom_call_target="tpu_custom_call" | custom-call | flops 3300000000 | bytes 1024 | tf_op jit(solution)/shard_map/inner_norm/pallas_call | solution.py:70
  152.5 8.0 %entry_back.2 = (bf16[512,768]{1,0:T(8,128)(2,1)}, bf16[512,768]{1,0:T(8,128)(2,1)}, f32[576,768]{1,0:T(8,128)}) custom-call(s32[3]{0:T(128)S(1)} %pad_add_fusion.meta_ref, bf16[2048,768]{1,0:T(8,128)(2,1)} %x_ref.5, bf16[1024,256]{1,0:T(8,128)(2,1)} %get-tuple-element.171.dq_ref, bf16[1024,256]{1,0:T(8,128)(2,1)} %get-tuple-element.196.dk_ref, ...), custom_call_target="tpu_custom_call" | custom-call | flops 5500000256 | bytes 1024 | tf_op jit(solution)/shard_map/entry_back/pallas_call | solution.py:70
  161.4 1.8 collective-permute-start.25
  163.6 8.0 %collective-permute-done.25 = bf16[192,768]{1,0:T(8,128)(2,1)} collective-permute-done((bf16[192,768]{1,0:T(8,128)(2,1)}, bf16[192,768]{1,0:T(8,128)(2,1)}, u32[]{:S(2)}, u32[]{:S(2)}) %collective-permute-start.25) | collective-permute-done | bytes 294944 | tf_op jit(solution)/shard_map/ppermute | solution.py:685
  172.7 2.3 collective-permute-done.26
  177.5 2.4 collective-permute-start.29
  180.4 13.4 %attend_backward.3 = (bf16[1024,256]{1,0:T(8,128)(2,1)}, bf16[1024,256]{1,0:T(8,128)(2,1)}, bf16[1024,256]{1,0:T(8,128)(2,1)}) custom-call(s32[3]{0:T(128)S(1)} %pad_add_fusion.meta_ref, bf16[2048,256]{1,0:T(8,128)(2,1)} %get-tuple-element.129.q_ref, bf16[2048,256]{1,0:T(8,128)(2,1)} %get-tuple-element.130.k_ref, ...), custom_call_target="tpu_custom_call" | custom-call | flops 13200000000 | bytes 1024 | tf_op jit(solution)/shard_map/attend_backward/pallas_call | solution.py:70
  194.0 3.0 %collective-permute-start.35 = (bf16[1,1,1,96,768]{4,3,2,1,0:T(8,128)(2,1)S(1)}, bf16[1,1,1,96,768]{4,3,2,1,0:T(8,128)(2,1)S(1)}, u32[]{:S(2)}, u32[]{:S(2)}) collective-permute-start(bf16[1,1,1,96,768]{4,3,2,1,0:T(8,128)(2,1)S(1)} %fusion.3), channel_id=1, source_target_pairs={{0,16},{4,20},{8,24},{12,28},{16,0},{20,4},{24,8},{28,12},{1,17},{... | collective-permute-start | bytes 442376 | tf_op jit(solution)/shard_map/ppermute | solution.py:685
  197.1 8.3 %entry_back.3 = (bf16[512,768]{1,0:T(8,128)(2,1)}, bf16[512,768]{1,0:T(8,128)(2,1)}, bf16[576,768]{1,0:T(8,128)(2,1)}) custom-call(s32[3]{0:T(128)S(1)} %pad_add_fusion.meta_ref, bf16[2048,768]{1,0:T(8,128)(2,1)} %x_ref.5, bf16[1024,256]{1,0:T(8,128)(2,1)} %get-tuple-element.209.dq_ref, bf16[1024,256]{1,0:T(8,128)(2,1)} %get-tuple-element.216.dk_ref, ...), custom_call_target="tpu_custom_call" | custom-call | flops 5500000256 | bytes 1024 | tf_op jit(solution)/shard_map/entry_back/pallas_call | solution.py:70
  206.5 4.1 %collective-permute-start.40 = (bf16[288,768]{1,0:T(8,128)(2,1)S(1)}, bf16[288,768]{1,0:T(8,128)(2,1)S(1)}, u32[]{:S(2)}, u32[]{:S(2)}) collective-permute-start(bf16[288,768]{1,0:T(8,128)(2,1)S(1)} %constant_dynamic-slice_fusion.3), channel_id=1, source_target_pairs={{0,4},{4,0},{8,12},{12,8},{16,20},{20,16},{24,28},{28,24},{1,5},{5... | collective-permute-start | bytes 1327112 | tf_op jit(solution)/shard_map/ppermute | solution.py:685
  210.8 1.6 collective-permute-start.38
  213.3 3.3 %collective-permute-done.39 = bf16[1,1,1,32,768]{4,3,2,1,0:T(8,128)(2,1)S(1)} collective-permute-done((bf16[1,1,1,32,768]{4,3,2,1,0:T(8,128)(2,1)S(1)}, bf16[1,1,1,32,768]{4,3,2,1,0:T(8,128)(2,1)S(1)}, u32[]{:S(2)}, u32[]{:S(2)}) %collective-permute-start.39) | collective-permute-done | bytes 49184 | tf_op jit(solution)/shard_map/ppermute | solution.py:685
  216.7 5.1 %collective-permute-done.38 = bf16[1,1,2,96,768]{4,3,2,1,0:T(8,128)(2,1)S(1)} collective-permute-done((bf16[1,1,2,96,768]{4,3,2,1,0:T(8,128)(2,1)S(1)}, bf16[1,1,2,96,768]{4,3,2,1,0:T(8,128)(2,1)S(1)}, u32[]{:S(2)}, u32[]{:S(2)}) %collective-permute-start.38) | collective-permute-done | bytes 294944 | tf_op jit(solution)/shard_map/ppermute | solution.py:685
  221.9 5.5 %collective-permute-done.37 = bf16[1,1,2,96,768]{4,3,2,1,0:T(8,128)(2,1)S(1)} collective-permute-done((bf16[1,1,2,96,768]{4,3,2,1,0:T(8,128)(2,1)S(1)}, bf16[1,1,2,96,768]{4,3,2,1,0:T(8,128)(2,1)S(1)}, u32[]{:S(2)}, u32[]{:S(2)}) %collective-permute-start.37) | collective-permute-done | bytes 294944 | tf_op jit(solution)/shard_map/ppermute | solution.py:685
  229.0 2.6 collective-permute-start.44
  231.6 1.6 collective-permute-start.46
  234.7 1.6 collective-permute-start.48
  237.2 2.0 collective-permute-start.43
  239.1 4.0 %collective-permute-done.47 = bf16[72,768]{1,0:T(8,128)(2,1)S(1)} collective-permute-done((bf16[72,768]{1,0:T(8,128)(2,1)S(1)}, bf16[72,768]{1,0:T(8,128)(2,1)S(1)}, u32[]{:S(2)}, u32[]{:S(2)}) %collective-permute-start.47) | collective-permute-done | bytes 110624 | tf_op jit(solution)/shard_map/ppermute | solution.py:685
  243.7 2.2 collective-permute-done.44
  246.1 10.2 %collective-permute-done.43 = bf16[1,2,2,96,768]{4,3,2,1,0:T(8,128)(2,1)S(1)} collective-permute-done((bf16[1,2,2,96,768]{4,3,2,1,0:T(8,128)(2,1)S(1)}, bf16[1,2,2,96,768]{4,3,2,1,0:T(8,128)(2,1)S(1)}, u32[]{:S(2)}, u32[]{:S(2)}) %collective-permute-start.43) | collective-permute-done | bytes 589856 | tf_op jit(solution)/shard_map/ppermute | solution.py:685
  256.5 1.7 collective-permute-start.50
  258.3 2.5 collective-permute-start.51
  261.0 1.7 collective-permute-start.49
  262.8 5.0 %collective-permute-done.51 = bf16[1,1,72,768]{3,2,1,0:T(8,128)(2,1)S(1)} collective-permute-done((bf16[1,1,72,768]{3,2,1,0:T(8,128)(2,1)S(1)}, bf16[1,1,72,768]{3,2,1,0:T(8,128)(2,1)S(1)}, u32[]{:S(2)}, u32[]{:S(2)}) %collective-permute-start.51) | collective-permute-done | bytes 110624 | tf_op jit(solution)/shard_map/ppermute | solution.py:685
  268.0 1.6 collective-permute-start.53
  269.5 4.6 %place.2 = bf16[2048,768]{1,0:T(8,128)(2,1)} custom-call(s32[3]{0:T(128)S(1)} %pad_add_fusion.meta_ref, bf16[512,768]{1,0:T(8,128)(2,1)} %get-tuple-element.145.refs_0_, bf16[512,768]{1,0:T(8,128)(2,1)} %collective-permute-done.14.refs_1_, bf16[512,768]{1,0:T(8,128)(2,1)} %get-tuple-element.161.refs_2_, bf16[512,768]{1,0:T(8,128)(2,1)} %collective-permute-done.15.refs_3_), custom_call_target="tpu_custom_call" | custom-call | flops 3300000000 | bytes 1024 | tf_op jit(solution)/shard_map/place/pallas_call | solution.py:70
  274.5 1.8 collective-permute-done.53
  276.5 1.6 convert_element_type.244
  278.1 1.6 convert_element_type.245
  284.2 4.6 %place.3 = bf16[2048,768]{1,0:T(8,128)(2,1)} custom-call(s32[3]{0:T(128)S(1)} %pad_add_fusion.meta_ref, bf16[512,768]{1,0:T(8,128)(2,1)} %copy-done.41, bf16[512,768]{1,0:T(8,128)(2,1)} %copy-done.48, bf16[512,768]{1,0:T(8,128)(2,1)} %copy-done.42, bf16[512,768]{1,0:T(8,128)(2,1)} %copy-done.54), custom_call_target="tpu_custom_call" | custom-call | flops 3300000000 | bytes 1024 | tf_op jit(solution)/shard_map/place/pallas_call | solution.py:70
  (250 shorter events, 45.5 us)
Async XLA Ops:
  0.6 15.6 %collective-permute-start = (bf16[192,768]{1,0:T(8,128)(2,1)}, bf16[192,768]{1,0:T(8,128)(2,1)S(1)}, u32[]{:S(2)}, u32[]{:S(2)}) collective-permute-start(bf16[192,768]{1,0:T(8,128)(2,1)} %w0.7), channel_id=1, source_target_pairs={{0,1},{1,0},{2,3},{3,2},{4,5},{5,4},{6,7},{7,6},{8,9},{9,8},{10,11... | collective-permute-start | bytes 884744 | tf_op jit(solution)/shard_map/ppermute | solution.py:682
  1.2 15.3 %collective-permute-start.1 = (bf16[192,768]{1,0:T(8,128)(2,1)}, bf16[192,768]{1,0:T(8,128)(2,1)S(1)}, u32[]{:S(2)}, u32[]{:S(2)}) collective-permute-start(bf16[192,768]{1,0:T(8,128)(2,1)} %w0.7), channel_id=1, source_target_pairs={{0,2},{1,3},{2,0},{3,1},{4,6},{5,7},{6,4},{7,5},{8,10},{9,11},{10,... | collective-permute-start | bytes 884744 | tf_op jit(solution)/shard_map/ppermute | solution.py:682
  3.7 14.4 %collective-permute-start.2 = (bf16[192,768]{1,0:T(8,128)(2,1)}, bf16[192,768]{1,0:T(8,128)(2,1)S(1)}, u32[]{:S(2)}, u32[]{:S(2)}) collective-permute-start(bf16[192,768]{1,0:T(8,128)(2,1)} %w0.7), channel_id=1, source_target_pairs={{0,3},{1,2},{2,1},{3,0},{4,7},{5,6},{6,5},{7,4},{8,11},{9,10},{10,... | collective-permute-start | bytes 884744 | tf_op jit(solution)/shard_map/ppermute | solution.py:682
  3.8 15.4 %collective-permute-start.3 = (bf16[768,768]{1,0:T(8,128)(2,1)}, bf16[768,768]{1,0:T(8,128)(2,1)S(1)}, u32[]{:S(2)}, u32[]{:S(2)}) collective-permute-start(bf16[768,768]{1,0:T(8,128)(2,1)} %ua_ref.7), channel_id=1, source_target_pairs={{0,1},{1,0},{2,3},{3,2},{4,5},{5,4},{6,7},{7,6},{8,9},{9,8},{10,11... | collective-permute-start | bytes 3538952 | tf_op jit(solution)/shard_map/ppermute | solution.py:682
  3.9 15.2 %collective-permute-start.4 = (bf16[768,768]{1,0:T(8,128)(2,1)}, bf16[768,768]{1,0:T(8,128)(2,1)S(1)}, u32[]{:S(2)}, u32[]{:S(2)}) collective-permute-start(bf16[768,768]{1,0:T(8,128)(2,1)} %da_ref.7), channel_id=1, source_target_pairs={{0,1},{1,0},{2,3},{3,2},{4,5},{5,4},{6,7},{7,6},{8,9},{9,8},{10,11... | collective-permute-start | bytes 3538952 | tf_op jit(solution)/shard_map/ppermute | solution.py:682
  16.2 14.7 %collective-permute-start.5 = (bf16[192,512]{1,0:T(8,128)(2,1)S(1)}, bf16[192,512]{1,0:T(8,128)(2,1)S(1)}, u32[]{:S(2)}, u32[]{:S(2)}) collective-permute-start(bf16[192,512]{1,0:T(8,128)(2,1)S(1)} %get-tuple-element.136.o1_ref), channel_id=1, source_target_pairs={{0,1},{1,0},{2,3},{3,2},{4,5},{5,4},{6,7},{7,6},{8,9},{9,8},{10,11... | collective-permute-start | bytes 589832 | tf_op jit(solution)/shard_map/ppermute | solution.py:682
  16.4 14.5 %collective-permute-start.7 = (bf16[192,512]{1,0:T(8,128)(2,1)S(1)}, bf16[192,512]{1,0:T(8,128)(2,1)S(1)}, u32[]{:S(2)}, u32[]{:S(2)}) collective-permute-start(bf16[192,512]{1,0:T(8,128)(2,1)S(1)} %get-tuple-element.136.o1_ref), channel_id=1, source_target_pairs={{0,3},{1,2},{2,1},{3,0},{4,7},{5,6},{6,5},{7,4},{8,11},{9,10},{10,... | collective-permute-start | bytes 589832 | tf_op jit(solution)/shard_map/ppermute | solution.py:682
  18.2 11.9 %collective-permute-start.6 = (bf16[192,512]{1,0:T(8,128)(2,1)S(1)}, bf16[192,512]{1,0:T(8,128)(2,1)S(1)}, u32[]{:S(2)}, u32[]{:S(2)}) collective-permute-start(bf16[192,512]{1,0:T(8,128)(2,1)S(1)} %get-tuple-element.132.a0.o0_ref), channel_id=1, source_target_pairs={{0,2},{1,3},{2,0},{3,1},{4,6},{5,7},{6,4},{7,5},{8,10},{9,11},{10,... | collective-permute-start | bytes 589832 | tf_op jit(solution)/shard_map/ppermute | solution.py:682
  28.8 14.5 %collective-permute-start.10 = (bf16[192,512]{1,0:T(8,128)(2,1)S(1)}, bf16[192,512]{1,0:T(8,128)(2,1)S(1)}, u32[]{:S(2)}, u32[]{:S(2)}) collective-permute-start(bf16[192,512]{1,0:T(8,128)(2,1)S(1)} %get-tuple-element.139.o1_ref), channel_id=1, source_target_pairs={{0,3},{1,2},{2,1},{3,0},{4,7},{5,6},{6,5},{7,4},{8,11},{9,10},{10,... | collective-permute-start | bytes 589832 | tf_op jit(solution)/shard_map/ppermute | solution.py:682
  29.6 13.7 %collective-permute-start.8 = (bf16[192,512]{1,0:T(8,128)(2,1)S(1)}, bf16[192,512]{1,0:T(8,128)(2,1)S(1)}, u32[]{:S(2)}, u32[]{:S(2)}) collective-permute-start(bf16[192,512]{1,0:T(8,128)(2,1)S(1)} %get-tuple-element.139.o1_ref), channel_id=1, source_target_pairs={{0,1},{1,0},{2,3},{3,2},{4,5},{5,4},{6,7},{7,6},{8,9},{9,8},{10,11... | collective-permute-start | bytes 589832 | tf_op jit(solution)/shard_map/ppermute | solution.py:682
  30.0 13.3 %collective-permute-start.9 = (bf16[192,512]{1,0:T(8,128)(2,1)S(1)}, bf16[192,512]{1,0:T(8,128)(2,1)S(1)}, u32[]{:S(2)}, u32[]{:S(2)}) collective-permute-start(bf16[192,512]{1,0:T(8,128)(2,1)S(1)} %get-tuple-element.134.a0.o0_ref), channel_id=1, source_target_pairs={{0,2},{1,3},{2,0},{3,1},{4,6},{5,7},{6,4},{7,5},{8,10},{9,11},{10,... | collective-permute-start | bytes 589832 | tf_op jit(solution)/shard_map/ppermute | solution.py:682
  42.2 20.7 %collective-permute-start.11 = (bf16[512,768]{1,0:T(8,128)(2,1)}, bf16[512,768]{1,0:T(8,128)(2,1)S(1)}, u32[]{:S(2)}, u32[]{:S(2)}) collective-permute-start(bf16[512,768]{1,0:T(8,128)(2,1)} %get-tuple-element.143), channel_id=1, source_target_pairs={{0,2},{1,3},{2,0},{3,1},{4,6},{5,7},{6,4},{7,5},{8,10},{9,11},{10,... | collective-permute-start | bytes 2359304 | tf_op jit(solution)/shard_map/ppermute | solution.py:682
  53.8 30.9 %collective-permute-start.12 = (bf16[512,768]{1,0:T(8,128)(2,1)}, bf16[512,768]{1,0:T(8,128)(2,1)S(1)}, u32[]{:S(2)}, u32[]{:S(2)}) collective-permute-start(bf16[512,768]{1,0:T(8,128)(2,1)} %get-tuple-element.154), channel_id=1, source_target_pairs={{0,2},{1,3},{2,0},{3,1},{4,6},{5,7},{6,4},{7,5},{8,10},{9,11},{10,... | collective-permute-start | bytes 2359304 | tf_op jit(solution)/shard_map/ppermute | solution.py:682
  83.6 23.7 %collective-permute-start.13 = (bf16[512,768]{1,0:T(8,128)(2,1)S(1)}, bf16[512,768]{1,0:T(8,128)(2,1)S(1)}, u32[]{:S(2)}, u32[]{:S(2)}) collective-permute-start(bf16[512,768]{1,0:T(8,128)(2,1)S(1)} %copy-done.53), channel_id=1, source_target_pairs={{0,2},{1,3},{2,0},{3,1},{4,6},{5,7},{6,4},{7,5},{8,10},{9,11},{10,... | collective-permute-start | bytes 2359304 | tf_op jit(solution)/shard_map/ppermute | solution.py:682
  108.1 10.0 %collective-permute-start.19 = (bf16[768,768]{1,0:T(8,128)(2,1)}, bf16[768,768]{1,0:T(8,128)(2,1)}, u32[]{:S(2)}, u32[]{:S(2)}) collective-permute-start(bf16[768,768]{1,0:T(8,128)(2,1)} %get-tuple-element.180), channel_id=1, source_target_pairs={{0,1},{1,0},{2,3},{3,2},{4,5},{5,4},{6,7},{7,6},{8,9},{9,8},{10,11... | collective-permute-start | bytes 3538952 | tf_op jit(solution)/shard_map/ppermute | solution.py:682
  108.1 15.1 %collective-permute-start.17 = (bf16[768,768]{1,0:T(8,128)(2,1)}, bf16[768,768]{1,0:T(8,128)(2,1)S(1)}, u32[]{:S(2)}, u32[]{:S(2)}) collective-permute-start(bf16[768,768]{1,0:T(8,128)(2,1)} %get-tuple-element.177), channel_id=1, source_target_pairs={{0,1},{1,0},{2,3},{3,2},{4,5},{5,4},{6,7},{7,6},{8,9},{9,8},{10,11... | collective-permute-start | bytes 3538952 | tf_op jit(solution)/shard_map/ppermute | solution.py:682
  108.7 9.5 %collective-permute-start.14 = (bf16[512,768]{1,0:T(8,128)(2,1)}, bf16[512,768]{1,0:T(8,128)(2,1)}, u32[]{:S(2)}, u32[]{:S(2)}) collective-permute-start(bf16[512,768]{1,0:T(8,128)(2,1)} %get-tuple-element.145.refs_0_), channel_id=1, source_target_pairs={{0,1},{1,0},{2,3},{3,2},{4,5},{5,4},{6,7},{7,6},{8,9},{9,8},{10,11... | collective-permute-start | bytes 2359304 | tf_op jit(solution)/shard_map/ppermute | solution.py:682
  108.7 9.5 %collective-permute-start.15 = (bf16[512,768]{1,0:T(8,128)(2,1)}, bf16[512,768]{1,0:T(8,128)(2,1)}, u32[]{:S(2)}, u32[]{:S(2)}) collective-permute-start(bf16[512,768]{1,0:T(8,128)(2,1)} %get-tuple-element.161.refs_2_), channel_id=1, source_target_pairs={{0,1},{1,0},{2,3},{3,2},{4,5},{5,4},{6,7},{7,6},{8,9},{9,8},{10,11... | collective-permute-start | bytes 2359304 | tf_op jit(solution)/shard_map/ppermute | solution.py:682
  117.1 25.2 %collective-permute-start.21 = (bf16[512,768]{1,0:T(8,128)(2,1)S(1)}, bf16[512,768]{1,0:T(8,128)(2,1)S(1)}, u32[]{:S(2)}, u32[]{:S(2)}) collective-permute-start(bf16[512,768]{1,0:T(8,128)(2,1)S(1)} %copy-done.49), channel_id=1, source_target_pairs={{0,2},{1,3},{2,0},{3,1},{4,6},{5,7},{6,4},{7,5},{8,10},{9,11},{10,... | collective-permute-start | bytes 2359304 | tf_op jit(solution)/shard_map/ppermute | solution.py:682
  118.1 8.9 %collective-permute-start.16 = (bf16[192,512]{1,0:T(8,128)(2,1)S(1)}, bf16[192,512]{1,0:T(8,128)(2,1)S(1)}, u32[]{:S(2)}, u32[]{:S(2)}) collective-permute-start(bf16[192,512]{1,0:T(8,128)(2,1)S(1)} %get-tuple-element.169), channel_id=1, source_target_pairs={{0,1},{1,0},{2,3},{3,2},{4,5},{5,4},{6,7},{7,6},{8,9},{9,8},{10,11... | collective-permute-start | bytes 589832 | tf_op jit(solution)/shard_map/ppermute | solution.py:682
  119.4 17.9 %collective-permute-start.20 = (bf16[384,768]{1,0:T(8,128)(2,1)S(1)}, bf16[384,768]{1,0:T(8,128)(2,1)S(1)}, u32[]{:S(2)}, u32[]{:S(2)}) collective-permute-start(bf16[384,768]{1,0:T(8,128)(2,1)S(1)} %add_convert_fusion.3), channel_id=1, source_target_pairs={{0,8},{4,12},{8,0},{12,4},{16,24},{20,28},{24,16},{28,20},{1,9},{5... | collective-permute-start | bytes 1769480 | tf_op jit(solution)/shard_map/ppermute | solution.py:685
  123.5 17.3 %collective-permute-start.18 = (bf16[384,768]{1,0:T(8,128)(2,1)S(1)}, bf16[384,768]{1,0:T(8,128)(2,1)S(1)}, u32[]{:S(2)}, u32[]{:S(2)}) collective-permute-start(bf16[384,768]{1,0:T(8,128)(2,1)S(1)} %add_convert_fusion.5), channel_id=1, source_target_pairs={{0,4},{4,0},{8,12},{12,8},{16,20},{20,16},{24,28},{28,24},{1,5},{5... | collective-permute-start | bytes 1769480 | tf_op jit(solution)/shard_map/ppermute | solution.py:685
  151.8 11.8 %collective-permute-start.24 = (bf16[192,768]{1,0:T(8,128)(2,1)}, bf16[192,768]{1,0:T(8,128)(2,1)}, u32[]{:S(2)}, u32[]{:S(2)}) collective-permute-start(bf16[192,768]{1,0:T(8,128)(2,1)} %constant_dynamic-slice_fusion.9), channel_id=1, source_target_pairs={{0,8},{4,12},{8,0},{12,4},{16,24},{20,28},{24,16},{28,20},{1,9},{5... | collective-permute-start | bytes 884744 | tf_op jit(solution)/shard_map/ppermute | solution.py:685
  160.5 14.7 %collective-permute-start.27 = (bf16[512,768]{1,0:T(8,128)(2,1)}, bf16[512,768]{1,0:T(8,128)(2,1)S(1)}, u32[]{:S(2)}, u32[]{:S(2)}) collective-permute-start(bf16[512,768]{1,0:T(8,128)(2,1)} %get-tuple-element.198), channel_id=1, source_target_pairs={{0,1},{1,0},{2,3},{3,2},{4,5},{5,4},{6,7},{7,6},{8,9},{9,8},{10,11... | collective-permute-start | bytes 2359304 | tf_op jit(solution)/shard_map/ppermute | solution.py:682
  161.4 10.2 %collective-permute-start.25 = (bf16[192,768]{1,0:T(8,128)(2,1)}, bf16[192,768]{1,0:T(8,128)(2,1)}, u32[]{:S(2)}, u32[]{:S(2)}) collective-permute-start(bf16[192,768]{1,0:T(8,128)(2,1)} %constant_dynamic-slice_fusion.8), channel_id=1, source_target_pairs={{0,4},{4,0},{8,12},{12,8},{16,20},{20,16},{24,28},{28,24},{1,5},{5... | collective-permute-start | bytes 884744 | tf_op jit(solution)/shard_map/ppermute | solution.py:685
  163.2 11.9 %collective-permute-start.26 = (bf16[128,768]{1,0:T(8,128)(2,1)S(1)}, bf16[128,768]{1,0:T(8,128)(2,1)S(1)}, u32[]{:S(2)}, u32[]{:S(2)}) collective-permute-start(bf16[128,768]{1,0:T(8,128)(2,1)S(1)} %add_convert_fusion.10), channel_id=1, source_target_pairs={{0,4},{4,0},{8,12},{12,8},{16,20},{20,16},{24,28},{28,24},{1,5},{5... | collective-permute-start | bytes 589832 | tf_op jit(solution)/shard_map/ppermute | solution.py:685
  175.5 21.7 %collective-permute-start.31 = (bf16[512,768]{1,0:T(8,128)(2,1)S(1)}, bf16[512,768]{1,0:T(8,128)(2,1)S(1)}, u32[]{:S(2)}, u32[]{:S(2)}) collective-permute-start(bf16[512,768]{1,0:T(8,128)(2,1)S(1)} %fusion), channel_id=1, source_target_pairs={{0,2},{1,3},{2,0},{3,1},{4,6},{5,7},{6,4},{7,5},{8,10},{9,11},{10,... | collective-permute-start | bytes 2359304 | tf_op jit(solution)/shard_map/ppermute | solution.py:682
  176.1 17.7 %collective-permute-start.30 = (bf16[64,768]{1,0:T(8,128)(2,1)S(1)}, bf16[64,768]{1,0:T(8,128)(2,1)S(1)}, u32[]{:S(2)}, u32[]{:S(2)}) collective-permute-start(bf16[64,768]{1,0:T(8,128)(2,1)S(1)} %constant_dynamic-slice_fusion.5), channel_id=1, source_target_pairs={{0,8},{4,12},{8,0},{12,4},{16,24},{20,28},{24,16},{28,20},{1,9},{5... | collective-permute-start | bytes 294920 | tf_op jit(solution)/shard_map/ppermute | solution.py:685
  177.5 16.5 %collective-permute-start.29 = (bf16[96,768]{1,0:T(8,128)(2,1)S(1)}, bf16[96,768]{1,0:T(8,128)(2,1)S(1)}, u32[]{:S(2)}, u32[]{:S(2)}) collective-permute-start(bf16[96,768]{1,0:T(8,128)(2,1)S(1)} %constant_dynamic-slice_fusion.6), channel_id=1, source_target_pairs={{0,16},{4,20},{8,24},{12,28},{16,0},{20,4},{24,8},{28,12},{1,17},{... | collective-permute-start | bytes 442376 | tf_op jit(solution)/shard_map/ppermute | solution.py:685
  179.9 14.1 %collective-permute-start.28 = (bf16[96,768]{1,0:T(8,128)(2,1)S(1)}, bf16[96,768]{1,0:T(8,128)(2,1)S(1)}, u32[]{:S(2)}, u32[]{:S(2)}) collective-permute-start(bf16[96,768]{1,0:T(8,128)(2,1)S(1)} %constant_dynamic-slice_fusion.7), channel_id=1, source_target_pairs={{0,16},{4,20},{8,24},{12,28},{16,0},{20,4},{24,8},{28,12},{1,17},{... | collective-permute-start | bytes 442376 | tf_op jit(solution)/shard_map/ppermute | solution.py:685
  193.9 16.7 %collective-permute-start.36 = (bf16[32,768]{1,0:T(8,128)(2,1)S(1)}, bf16[32,768]{1,0:T(8,128)(2,1)S(1)}, u32[]{:S(2)}, u32[]{:S(2)}) collective-permute-start(bf16[32,768]{1,0:T(8,128)(2,1)S(1)} %constant_dynamic-slice_fusion.4), channel_id=1, source_target_pairs={{0,16},{4,20},{8,24},{12,28},{16,0},{20,4},{24,8},{28,12},{1,17},{... | collective-permute-start | bytes 147464 | tf_op jit(solution)/shard_map/ppermute | solution.py:685
  194.0 16.5 %collective-permute-start.35 = (bf16[1,1,1,96,768]{4,3,2,1,0:T(8,128)(2,1)S(1)}, bf16[1,1,1,96,768]{4,3,2,1,0:T(8,128)(2,1)S(1)}, u32[]{:S(2)}, u32[]{:S(2)}) collective-permute-start(bf16[1,1,1,96,768]{4,3,2,1,0:T(8,128)(2,1)S(1)} %fusion.3), channel_id=1, source_target_pairs={{0,16},{4,20},{8,24},{12,28},{16,0},{20,4},{24,8},{28,12},{1,17},{... | collective-permute-start | bytes 442376 | tf_op jit(solution)/shard_map/ppermute | solution.py:685
  197.0 13.5 %collective-permute-start.34 = (bf16[1,1,1,96,768]{4,3,2,1,0:T(8,128)(2,1)S(1)}, bf16[1,1,1,96,768]{4,3,2,1,0:T(8,128)(2,1)S(1)}, u32[]{:S(2)}, u32[]{:S(2)}) collective-permute-start(bf16[1,1,1,96,768]{4,3,2,1,0:T(8,128)(2,1)S(1)} %fusion.2), channel_id=1, source_target_pairs={{0,16},{4,20},{8,24},{12,28},{16,0},{20,4},{24,8},{28,12},{1,17},{... | collective-permute-start | bytes 442376 | tf_op jit(solution)/shard_map/ppermute | solution.py:685
  205.4 22.2 %collective-permute-start.33 = (bf16[512,768]{1,0:T(8,128)(2,1)}, bf16[512,768]{1,0:T(8,128)(2,1)S(1)}, u32[]{:S(2)}, u32[]{:S(2)}) collective-permute-start(bf16[512,768]{1,0:T(8,128)(2,1)} %get-tuple-element.219), channel_id=1, source_target_pairs={{0,1},{1,0},{2,3},{3,2},{4,5},{5,4},{6,7},{7,6},{8,9},{9,8},{10,11... | collective-permute-start | bytes 2359304 | tf_op jit(solution)/shard_map/ppermute | solution.py:682
  206.5 21.0 %collective-permute-start.40 = (bf16[288,768]{1,0:T(8,128)(2,1)S(1)}, bf16[288,768]{1,0:T(8,128)(2,1)S(1)}, u32[]{:S(2)}, u32[]{:S(2)}) collective-permute-start(bf16[288,768]{1,0:T(8,128)(2,1)S(1)} %constant_dynamic-slice_fusion.3), channel_id=1, source_target_pairs={{0,4},{4,0},{8,12},{12,8},{16,20},{20,16},{24,28},{28,24},{1,5},{5... | collective-permute-start | bytes 1327112 | tf_op jit(solution)/shard_map/ppermute | solution.py:685
  210.8 10.9 %collective-permute-start.38 = (bf16[1,1,2,96,768]{4,3,2,1,0:T(8,128)(2,1)S(1)}, bf16[1,1,2,96,768]{4,3,2,1,0:T(8,128)(2,1)S(1)}, u32[]{:S(2)}, u32[]{:S(2)}) collective-permute-start(bf16[1,1,2,96,768]{4,3,2,1,0:T(8,128)(2,1)S(1)} %pad_maximum_fusion.7), channel_id=1, source_target_pairs={{0,8},{4,12},{8,0},{12,4},{16,24},{20,28},{24,16},{28,20},{1,9},{5... | collective-permute-start | bytes 884744 | tf_op jit(solution)/shard_map/ppermute | solution.py:685
  212.4 14.9 %collective-permute-start.37 = (bf16[1,1,2,96,768]{4,3,2,1,0:T(8,128)(2,1)S(1)}, bf16[1,1,2,96,768]{4,3,2,1,0:T(8,128)(2,1)S(1)}, u32[]{:S(2)}, u32[]{:S(2)}) collective-permute-start(bf16[1,1,2,96,768]{4,3,2,1,0:T(8,128)(2,1)S(1)} %pad_maximum_fusion.6), channel_id=1, source_target_pairs={{0,8},{4,12},{8,0},{12,4},{16,24},{20,28},{24,16},{28,20},{1,9},{5... | collective-permute-start | bytes 884744 | tf_op jit(solution)/shard_map/ppermute | solution.py:685
  216.7 65.7 %collective-permute-start.32 = (bf16[512,768]{1,0:T(8,128)(2,1)S(1)}, bf16[512,768]{1,0:T(8,128)(2,1)S(1)}, u32[]{:S(2)}, u32[]{:S(2)}) collective-permute-start(bf16[512,768]{1,0:T(8,128)(2,1)S(1)} %add_convert_fusion.1.refs_0_), channel_id=1, source_target_pairs={{0,1},{1,0},{2,3},{3,2},{4,5},{5,4},{6,7},{7,6},{8,9},{9,8},{10,11... | collective-permute-start | bytes 2359304 | tf_op jit(solution)/shard_map/ppermute | solution.py:682
  229.0 16.8 %collective-permute-start.44 = (bf16[2,1,2,96,768]{4,3,2,1,0:T(8,128)(2,1)S(1)}, bf16[2,1,2,96,768]{4,3,2,1,0:T(8,128)(2,1)S(1)}, u32[]{:S(2)}, u32[]{:S(2)}) collective-permute-start(bf16[2,1,2,96,768]{4,3,2,1,0:T(8,128)(2,1)S(1)} %pad_maximum_fusion.4), channel_id=1, source_target_pairs={{0,4},{4,0},{8,12},{12,8},{16,20},{20,16},{24,28},{28,24},{1,5},{5... | collective-permute-start | bytes 1769480 | tf_op jit(solution)/shard_map/ppermute | solution.py:685
  233.2 9.9 %collective-permute-start.47 = (bf16[72,768]{1,0:T(8,128)(2,1)S(1)}, bf16[72,768]{1,0:T(8,128)(2,1)S(1)}, u32[]{:S(2)}, u32[]{:S(2)}) collective-permute-start(bf16[72,768]{1,0:T(8,128)(2,1)S(1)} %get-tuple-element.265), channel_id=1, source_target_pairs={{0,16},{4,20},{8,24},{12,28},{16,0},{20,4},{24,8},{28,12},{1,17},{... | collective-permute-start | bytes 331784 | tf_op jit(solution)/shard_map/ppermute | solution.py:685
  234.7 8.9 %collective-permute-start.48 = (bf16[72,768]{1,0:T(8,128)(2,1)S(1)}, bf16[72,768]{1,0:T(8,128)(2,1)S(1)}, u32[]{:S(2)}, u32[]{:S(2)}) collective-permute-start(bf16[72,768]{1,0:T(8,128)(2,1)S(1)} %get-tuple-element.264), channel_id=1, source_target_pairs={{0,24},{4,28},{8,16},{12,20},{16,8},{20,12},{24,0},{28,4},{1,25},{... | collective-permute-start | bytes 331784 | tf_op jit(solution)/shard_map/ppermute | solution.py:685
  237.2 19.1 %collective-permute-start.43 = (bf16[1,2,2,96,768]{4,3,2,1,0:T(8,128)(2,1)S(1)}, bf16[1,2,2,96,768]{4,3,2,1,0:T(8,128)(2,1)S(1)}, u32[]{:S(2)}, u32[]{:S(2)}) collective-permute-start(bf16[1,2,2,96,768]{4,3,2,1,0:T(8,128)(2,1)S(1)} %pad_maximum_fusion.3), channel_id=1, source_target_pairs={{0,4},{4,0},{8,12},{12,8},{16,20},{20,16},{24,28},{28,24},{1,5},{5... | collective-permute-start | bytes 1769480 | tf_op jit(solution)/shard_map/ppermute | solution.py:685
  243.1 13.4 %collective-permute-start.41 = (bf16[512,768]{1,0:T(8,128)(2,1)S(1)}, bf16[512,768]{1,0:T(8,128)(2,1)S(1)}, u32[]{:S(2)}, u32[]{:S(2)}) collective-permute-start(bf16[512,768]{1,0:T(8,128)(2,1)S(1)} %fusion.1), channel_id=1, source_target_pairs={{0,2},{1,3},{2,0},{3,1},{4,6},{5,7},{6,4},{7,5},{8,10},{9,11},{10,... | collective-permute-start | bytes 2359304 | tf_op jit(solution)/shard_map/ppermute | solution.py:682
  258.3 9.5 %collective-permute-start.51 = (bf16[1,1,72,768]{3,2,1,0:T(8,128)(2,1)S(1)}, bf16[1,1,72,768]{3,2,1,0:T(8,128)(2,1)S(1)}, u32[]{:S(2)}, u32[]{:S(2)}) collective-permute-start(bf16[1,1,72,768]{3,2,1,0:T(8,128)(2,1)S(1)} %fusion.4), channel_id=1, source_target_pairs={{0,16},{4,20},{8,24},{12,28},{16,0},{20,4},{24,8},{28,12},{1,17},{... | collective-permute-start | bytes 331784 | tf_op jit(solution)/shard_map/ppermute | solution.py:685
  260.7 7.1 %collective-permute-start.52 = (bf16[1,1,72,768]{3,2,1,0:T(8,128)(2,1)S(1)}, bf16[1,1,72,768]{3,2,1,0:T(8,128)(2,1)S(1)}, u32[]{:S(2)}, u32[]{:S(2)}) collective-permute-start(bf16[1,1,72,768]{3,2,1,0:T(8,128)(2,1)S(1)} %fusion.4), channel_id=1, source_target_pairs={{0,24},{4,28},{8,16},{12,20},{16,8},{20,12},{24,0},{28,4},{1,25},{... | collective-permute-start | bytes 331784 | tf_op jit(solution)/shard_map/ppermute | solution.py:685
  261.0 6.8 %collective-permute-start.49 = (bf16[1,2,2,32,768]{4,3,2,1,0:T(8,128)(2,1)S(1)}, bf16[1,2,2,32,768]{4,3,2,1,0:T(8,128)(2,1)S(1)}, u32[]{:S(2)}, u32[]{:S(2)}) collective-permute-start(bf16[1,2,2,32,768]{4,3,2,1,0:T(8,128)(2,1)S(1)} %pad_maximum_fusion.8), channel_id=1, source_target_pairs={{0,4},{4,0},{8,12},{12,8},{16,20},{20,16},{24,28},{28,24},{1,5},{5... | collective-permute-start | bytes 589832 | tf_op jit(solution)/shard_map/ppermute | solution.py:685
  268.0 8.4 %collective-permute-start.53 = (bf16[1,4,72,768]{3,2,1,0:T(8,128)(2,1)S(1)}, bf16[1,4,72,768]{3,2,1,0:T(8,128)(2,1)S(1)}, u32[]{:S(2)}, u32[]{:S(2)}) collective-permute-start(bf16[1,4,72,768]{3,2,1,0:T(8,128)(2,1)S(1)} %constant_dynamic-update-slice_fusion.3), channel_id=1, source_target_pairs={{0,4},{4,0},{8,12},{12,8},{16,20},{20,16},{24,28},{28,24},{1,5},{5... | collective-permute-start | bytes 1327112 | tf_op jit(solution)/shard_map/ppermute | solution.py:685
  274.4 8.0 %collective-permute-start.42 = (bf16[512,768]{1,0:T(8,128)(2,1)S(1)}, bf16[512,768]{1,0:T(8,128)(2,1)S(1)}, u32[]{:S(2)}, u32[]{:S(2)}) collective-permute-start(bf16[512,768]{1,0:T(8,128)(2,1)S(1)} %add_convert_fusion.refs_2_), channel_id=1, source_target_pairs={{0,1},{1,0},{2,3},{3,2},{4,5},{5,4},{6,7},{7,6},{8,9},{9,8},{10,11... | collective-permute-start | bytes 2359304 | tf_op jit(solution)/shard_map/ppermute | solution.py:682
  (62 other events, 392.1 us)

commit v4 on v2

--- a/solution.py
+++ b/solution.py
@@ -40,30 +40,7 @@
     return pl.CostEstimate(flops=int(micros * 1.1e9), bytes_accessed=1024, transcendentals=0)
 
 
-MICROS = {"attend_forward": 8, "attend_backward": 12, "entry_back": 5, "place": 3, "ahead": 9, "astern": 10, "inner_norm": 3, "weight_grads": 5}
-
-
-def project_kernel(x_ref, wq_ref, wk_ref, wv_ref, q_ref, k_ref, v_ref):
-    x = x_ref[...]
-    for w_ref, o_ref in ((wq_ref, q_ref), (wk_ref, k_ref), (wv_ref, v_ref)):
-        o_ref[:, :192] = nt(x, w_ref[...]).astype(BF)
-        o_ref[:, 192:] = jnp.zeros((x.shape[0], HEAD_DIM), BF)
-
-
-def project(tokens, wq, wk, wv):
-    rows, d = tokens.shape
-    block = 512
-    return pl.pallas_call(
-        project_kernel,
-        grid=(rows // block,),
-        in_specs=[pl.BlockSpec((block, d), lambda i: (i, 0))]
-        + [pl.BlockSpec((192, d), lambda i: (0, 0))] * 3,
-        out_specs=[pl.BlockSpec((block, 256), lambda i: (i, 0))] * 3,
-        out_shape=[jax.ShapeDtypeStruct((rows, 256), BF)] * 3,
-        compiler_params=params(48),
-        cost_estimate=cost(3),
-        name="project",
-    )(tokens, wq, wk, wv)
+MICROS = {"project": 3, "attend_forward": 8, "attend_backward": 12, "entry_back": 5, "place": 3, "ahead": 9, "astern": 10, "inner_norm": 3, "weight_grads": 5}
 
 
 def lane_parts(block):
@@ -80,7 +57,14 @@
 TILE = (0, 0, 1)
 
 
-def call(kernel, name, grid, meta, args, in_specs, out_specs, out_shape, scratch=(), limit=VMEM):
+def call(kernel, name, grid, meta, args, in_specs, out_specs, out_shape, scratch=(), limit=VMEM, hold=(), out=()):
+    args = list(args)
+    for i in hold:
+        space = pltpu.VMEM if i >= 0 else pltpu.HBM
+        spot = i if i >= 0 else -1 - i
+        args[spot] = pltpu.with_memory_space_constraint(args[spot], space)
+    if isinstance(out_shape, list):
+        out_shape = [pltpu.VMEM(o.shape, o.dtype) if i in out else o for i, o in enumerate(out_shape)]
     return pl.pallas_call(
         kernel,
         grid_spec=pltpu.PrefetchScalarGridSpec(
@@ -105,7 +89,31 @@
     return jax.ShapeDtypeStruct(shape, dtype)
 
 
-def forward_kernel(u, meta_ref, q_ref, k_ref, v_ref, own_ref, other_ref, o32_ref, lse_ref, s_ref):
+def project_kernel(meta_ref, x_ref, wq_ref, wk_ref, wv_ref, q_ref, k_ref, v_ref):
+    x = x_ref[...]
+    for w_ref, o_ref in ((wq_ref, q_ref), (wk_ref, k_ref), (wv_ref, v_ref)):
+        o_ref[:, :192] = nt(x, w_ref[...]).astype(BF)
+        o_ref[:, 192:] = jnp.zeros((x.shape[0], HEAD_DIM), BF)
+
+
+def project(meta, tokens, weights):
+    rows, d = tokens.shape
+    block = 256
+    return call(
+        project_kernel,
+        "project",
+        (rows // block,),
+        meta,
+        (tokens, *weights),
+        [pl.BlockSpec((block, d), lambda i, m: (i, 0))] + [fixed(192, d)] * 3,
+        [pl.BlockSpec((block, 256), lambda i, m: (i, 0))] * 3,
+        [like((rows, 256), BF)] * 3,
+        hold=(-1, -2, -3, -4),
+        out=(0, 1, 2),
+    )
+
+
+def forward_kernel(u, meta_ref, q_ref, k_ref, v_ref, own_ref, other_ref, lse_ref, s_ref):
     length = meta_ref[1 + u]
     step = pl.program_id(0)
     blocks = lax.div(length + KB - 1, KB)
@@ -147,7 +155,6 @@
         total, result = done[h]
         lo = HEAD_DIM * (h % 2)
         o = result[lo : lo + HEAD_DIM] / total
-        o32_ref[0, pl.ds(h * HEAD_DIM, HEAD_DIM), :] = o
         lse_ref[0, pl.ds(h, 1), :] = highest[h] * LOG2E + jnp.log2(total)
         outs.append(o.astype(BF))
     whole = jnp.concatenate(outs, axis=0)
@@ -174,22 +181,22 @@
         [
             fixed(192, half),
             fixed(192, half),
-            pl.BlockSpec((1, 192, half), lambda i, m: (i, 0, 0)),
             pl.BlockSpec((1, 8, half), lambda i, m: (i, 0, 0)),
         ],
         [
             like((192, half), BF),
             like((192, half), BF),
-            like((2, 192, half), F32),
             like((2, 8, half), F32),
         ],
         [pltpu.VMEM((3, frames, half), F32)],
+        hold=(0, 1, 2),
+        out=(2,),
     )
 
 
 def backward_kernel(
-    u, meta_ref, q_ref, k_ref, v_ref, d0_ref, d1_ref, o32_ref, lse_ref,
-    dq_ref, dk_ref, dv_ref, kt_ref, dk_acc, dv_acc, do_ref,
+    u, meta_ref, q_ref, k_ref, v_ref, d0_ref, d1_ref, o0_ref, o1_ref, lse_ref,
+    dq_ref, dk_ref, dv_ref, kt_ref, dk_acc, dv_acc, do_ref, o_ref,
 ):
     length = meta_ref[1 + u]
     blocks = lax.div(length + KB - 1, KB)
@@ -201,10 +208,12 @@
         dv_acc[...] = jnp.zeros_like(dv_acc)
         kt_ref[...] = jnp.transpose(k_ref[...])
         do_ref[...] = d0_ref[...]
+        o_ref[...] = o0_ref[...]
 
     @pl.when(step == 1)
     def _():
         do_ref[...] = d1_ref[...]
+        o_ref[...] = o1_ref[...]
 
     parts = lane_parts(q_ref[...] * jnp.asarray(0.125, BF))
     width = q_ref.shape[0]
@@ -217,7 +226,7 @@
     )
     delta = [
         jnp.sum(
-            head[h].astype(F32) * o32_ref[0, pl.ds(h * HEAD_DIM, HEAD_DIM), :], axis=0, keepdims=True
+            head[h].astype(F32) * o_ref[pl.ds(h * HEAD_DIM, HEAD_DIM), :].astype(F32), axis=0, keepdims=True
         )
         for h in range(3)
     ]
@@ -252,21 +261,22 @@
         dv_ref[...] = dv_acc[...].astype(BF)
 
 
-def attend_backward(meta, q, k, v, own, other, o32, lse, u, frames):
+def attend_backward(meta, q, k, v, grads, outs, lse, u, frames):
     half = frames // 2
     return call(
         functools.partial(backward_kernel, u),
         "attend_backward",
         (2,),
         meta,
-        (q, k, v, own, other, o32, lse),
+        (q, k, v, *grads, *outs, lse),
         [
             pl.BlockSpec((half, 256), lambda i, m: (u * 2 + (i ^ m[0]), 0)),
             pl.BlockSpec((frames, 256), lambda i, m: (u, 0)),
             pl.BlockSpec((frames, 256), lambda i, m: (u, 0)),
             fixed(192, half),
             fixed(192, half),
-            pl.BlockSpec((1, 192, half), lambda i, m: (i, 0, 0)),
+            fixed(192, half),
+            fixed(192, half),
             pl.BlockSpec((1, 8, half), lambda i, m: (i, 0, 0)),
         ],
         [
@@ -280,7 +290,10 @@
             pltpu.VMEM((frames, 256), F32),
             pltpu.VMEM((frames, 256), F32),
             pltpu.VMEM((192, half), BF),
+            pltpu.VMEM((192, half), BF),
         ],
+        hold=(0, 1, 2, 7),
+        out=(0, 1, 2),
     )
 
 
@@ -331,6 +344,7 @@
         [fixed(half, d), fixed(half, d), fixed(576, d)],
         [like((half, d), BF), like((half, d), BF), like((576, d), dtype)],
         [pltpu.VMEM((576, d), F32)],
+        hold=(-1, 1, 2, 3, -5, -6, -7),
     )
 
 
@@ -431,6 +445,8 @@
             like((half, d), F32),
             like((half, d), BF),
         ],
+        hold=(-1,),
+        out=(0, 1, 2, 3, 4, 5),
     )
 
 
@@ -507,7 +523,9 @@
             like((2, d), F32),
         ]
         + [like(shape, BF) for shape in grads],
-        limit=28 if before else VMEM,
+        limit=24 if before else VMEM,
+        hold=(0, -3, 8, *range(10, 10 + len(before))),
+        out=(3,) if before else (1, 2, 3),
     )
 
 
@@ -544,7 +562,8 @@
         [fixed(rows, d)] * 2 + [fixed(rows, 2 * hidden)] * 2 + [fixed(*shape) for shape in shapes[: len(before)]],
         [fixed(*shape) for shape in shapes],
         [like(shape, BF) for shape in shapes],
-        limit=24,
+        hold=(0, 1, 2, 3),
+        out=(0, 1, 2, 3),
     )
 
 
@@ -594,6 +613,7 @@
         + ([fixed(192, d)] * 2 + [fixed(2, d)] * 3 if before else []),
         [fixed(rows, d), fixed(192, rows), fixed(192, rows), fixed(*merge.shape), fixed(*merge.shape), fixed(2, d)],
         [like((rows, d), F32), like((192, rows), BF), like((192, rows), BF), merge, merge, like((2, d), F32)],
+        hold=(0, 2, 3),
     )
 
 
@@ -623,39 +643,46 @@
         return sum(piece.astype(F32) for piece in pieces).astype(BF) if len(pieces) > 1 else pieces[0]
 
     class Chain:
-        def __init__(self, parts, order):
+        def __init__(self, parts, order, back=None):
             self.parts = parts
-            self.steps = [(True, *stage) for stage in order] + [(False, *stage) for stage in reversed(order)]
+            self.order = order
+            self.held = list(order)
+            self.steps = [(True, *stage) for stage in order] + [(False, *stage) for stage in back or reversed(order)]
 
         def start(self):
             if self.steps:
                 scatter, low_bit, width = self.steps[0]
                 count = 1 << width
                 spot = (place_dp >> low_bit) & (count - 1)
-                pick = lambda j: [cut(part, spot ^ j, count) if scatter else part for part in self.parts]
-                got = [swap_dp(total(pick(j)), j << low_bit) for j in range(1, count)]
-                self.pending = pick(0) + got
+                pick = lambda j: total([cut(part, spot ^ j, count) if scatter else part for part in self.parts])
+                self.pending = [swap_dp(pick(j), j << low_bit) for j in range(1, count)]
 
         def finish(self, *after):
             if not self.steps:
                 return
             scatter, low_bit, width = self.steps.pop(0)
-            pieces = self.pending
+            got = self.pending
             if after:
-                pieces = lax.optimization_barrier((*pieces, *after))[: len(pieces)]
+                got = list(lax.optimization_barrier((*got, *after))[: len(got)])
             count = 1 << width
             spot = (place_dp >> low_bit) & (count - 1)
             if scatter:
-                self.state = total(pieces)
-            elif count == 2:
-                one, two = pieces
-                self.state = jnp.concatenate([jnp.where(spot, two, one), jnp.where(spot, one, two)], axis=0)
+                self.state = total([cut(part, spot, count) for part in self.parts] + got)
+                if all(step[0] is False for step in self.steps):
+                    self.state = self.state.reshape((1,) * len(self.order) + self.state.shape)
             else:
-                size = pieces[0].shape[0]
-                whole = jnp.zeros((size * count, d), BF)
-                for j in range(count):
-                    whole = lax.dynamic_update_slice_in_dim(whole, pieces[j], (spot ^ j) * size, 0)
-                self.state = whole
+                axis = self.order.index((low_bit, width))
+                mine = self.parts[0]
+                if count == 2:
+                    halves = [jnp.where(spot, got[0], mine), jnp.where(spot, mine, got[0])]
+                    self.state = jnp.concatenate(halves, axis=axis)
+                else:
+                    whole = jnp.zeros(mine.shape[:axis] + (count,) + mine.shape[axis + 1 :], BF)
+                    for j, piece in enumerate([mine] + got):
+                        whole = lax.dynamic_update_slice_in_dim(whole, piece, spot ^ j, axis)
+                    self.state = whole
+                if not self.steps:
+                    self.state = self.state.reshape(-1, d)
             self.parts = (self.state,)
 
     scalars = jnp.concatenate([core.reshape(1), lengths])
@@ -674,7 +701,7 @@
     vectors = jnp.stack([ig, ib, og, ob])
     qkv_w = (wq.T, wk.T, wv.T)
 
-    q, k, v = project(tokens, *qkv_w)
+    q, k, v = project(scalars, tokens, qkv_w)
     fwd, att = [], []
     for u in range(seqs):
         fwd.append(done(attend_forward(meta(), q, k, v, u, frames), *merge_w[1:], up_w[1], down_w[1]))
@@ -699,7 +726,7 @@
         return res, (res[1], swap(res[2], 1))
 
     def attend_step(u, grads):
-        return done(attend_backward(meta(), q, k, v, *grads, fwd[u][2], fwd[u][3], u, frames))
+        return done(attend_backward(meta(), q, k, v, grads, fwd[u][:2], fwd[u][2], u, frames))
 
     def entry_step(u, grads, before, dtype):
         return done(entry_back(meta(), tokens, grads, qkv_w, before, u, frames, dtype))
@@ -732,7 +759,7 @@
         if u == 0:
             up_own, up_other, down_own, down_other = lax.optimization_barrier((*back[-1][6:], far_grad[0]))[:4]
             ffn.append(Chain((down_own, swap(down_other, 1)), pairs))
-            ffn.append(Chain((up_own, swap(up_other, 1)), pairs[1:2] + pairs[:1] + pairs[2:]))
+            ffn.append(Chain((up_own, swap(up_other, 1)), pairs[1:2] + pairs[:1] + pairs[2:], pairs[::-1]))
             res, grads = inner_step(0, ())
             start(ffn)
             inner.append(res)

time: 281 us -> 286 us (1.018)
  local copies, waits for them, and re-layouts: 39.6 us -> 28.9 us
  other arithmetic: 14.4 us -> 21.5 us
  Pallas kernels: 104 us -> 108 us
    pallas_call x15 -> x16, Pallas kernels: 99.2 us -> 108 us  [call(): pl.pallas_call(kernel, grid_spec=pltpu.PrefetchScalarGridSpec(num_scalar_...]
    unnamed x180 -> x156, local copies, waits for them, and re-layouts: 32.7 us -> 25.6 us
    ppermute x26, waiting for transfers between devices: 51.7 us -> 57.3 us  [swap_dp(): return lax.ppermute(value, 'dp', [(i, i ^ k) for i in range(groups)])]
    pallas_call x1 -> x0, Pallas kernels: 4.75 us -> none  [project(): pl.pallas_call(project_kernel, grid=(rows // block,), in_specs=[pl.BlockS...]
    convert_element_type x14 -> x9, other arithmetic: 6.29 us -> 10.7 us  [total(): sum((piece.astype(F32) for piece in pieces)).astype(BF)]
    ppermute x28, waiting for transfers between devices: 16.7 us -> 12.7 us  [swap(): return lax.ppermute(value, 'tensor', [(i, i ^ k) for i in range(4)])]
    dynamic_slice x13 -> x8, local copies, waits for them, and re-layouts: 6.17 us -> 2.55 us  [cut(): return lax.dynamic_slice_in_dim(array, index * size, size, 0)]
  transfers between devices with their start and end apart: 54 -> 54, of which waited for: 19 -> 22; matrix products, arithmetic and copies ran while one was open for 8% -> 8% of each run, Pallas kernels for 35% -> 36%
where the time goes in v4:
time: 286 us; the launch traced here: 282 us
  Pallas kernels  108 us (38%)
  waiting for transfers between devices  69.9 us (24%)
  starting transfers between devices  51.2 us (18%)
  local copies, waits for them, and re-layouts  28.9 us (10%)
  other arithmetic  21.5 us (8%)
    pallas_call x16, Pallas kernels, call(): pl.pallas_call(kernel, grid_spec=pltpu.PrefetchScalarGridSpec(num_scalar_...  108 us
    ppermute x26, waiting for transfers between devices, swap_dp(): return lax.ppermute(value, 'dp', [(i, i ^ k) for i in range(groups)])  57.3 us
    ppermute x26, starting transfers between devices, swap_dp(): return lax.ppermute(value, 'dp', [(i, i ^ k) for i in range(groups)])  34.6 us
    unnamed x156, local copies, waits for them, and re-layouts  25.6 us
    ppermute x28, starting transfers between devices, swap(): return lax.ppermute(value, 'tensor', [(i, i ^ k) for i in range(4)])  16.6 us
    ppermute x28, waiting for transfers between devices, swap(): return lax.ppermute(value, 'tensor', [(i, i ^ k) for i in range(4)])  12.7 us
    convert_element_type x9, other arithmetic, total(): sum((piece.astype(F32) for piece in pieces)).astype(BF)  10.7 us
  transfers between devices with their start and end apart: 54, of which 22 were waited for; matrix products, arithmetic and copies ran while one was open for 8% of the time, Pallas kernels for 36%

profile of v4, /device:TPU:0, one launch (start us, length us, event | category | flops | bytes accessed | tf_op | source)
XLA Modules:
  0.0 282.1 jit_solution(11055106337878819397)
XLA Ops:
  1.2 2.6 collective-permute-start.1
  5.0 7.4 %project.1 = (bf16[2048,256]{1,0:T(8,128)(2,1)S(1)}, bf16[2048,256]{1,0:T(8,128)(2,1)S(1)}, bf16[2048,256]{1,0:T(8,128)(2,1)S(1)}) custom-call(s32[3]{0:T(128)S(1)} %pad_add_fusion.meta_ref, bf16[2048,768]{1,0:T(8,128)(2,1)} %x_ref.5, bf16[192,768]{1,0:T(8,128)(2,1)} %bitcast.27, bf16[192,768]{1,0:T(8,128)(2,1)} %bitcast.30, bf16[192,768]{1,0:T(8,128)(2,1)} %bitcast.33), custom_call_target="tpu_custom_call" | custom-call | flops 3300000000 | bytes 1024 | tf_op jit(solution)/shard_map/project/pallas_call | solution.py:68
  12.5 7.7 %attend_forward.2 = (bf16[192,512]{1,0:T(8,128)(2,1)S(1)}, bf16[192,512]{1,0:T(8,128)(2,1)S(1)}, f32[2,8,512]{2,1,0:T(8,128)S(1)}) custom-call(s32[3]{0:T(128)S(1)} %pad_add_fusion.meta_ref, bf16[2048,256]{1,0:T(8,128)(2,1)S(1)} %get-tuple-element.129.q_ref, bf16[2048,256]{1,0:T(8,128)(2,1)S(1)} %get-tuple-element.130.k_ref, ...), custom_call_target="tpu_custom_call" | custom-call | flops 8800000000 | bytes 1024 | tf_op jit(solution)/shard_map/attend_forward/pallas_call | solution.py:68
  20.6 1.7 collective-permute-start.7
  24.1 6.5 %attend_forward.3 = (bf16[192,512]{1,0:T(8,128)(2,1)S(1)}, bf16[192,512]{1,0:T(8,128)(2,1)S(1)}, f32[2,8,512]{2,1,0:T(8,128)S(1)}) custom-call(s32[3]{0:T(128)S(1)} %pad_add_fusion.meta_ref, bf16[2048,256]{1,0:T(8,128)(2,1)S(1)} %get-tuple-element.129.q_ref, bf16[2048,256]{1,0:T(8,128)(2,1)S(1)} %get-tuple-element.130.k_ref, ...), custom_call_target="tpu_custom_call" | custom-call | flops 8800000000 | bytes 1024 | tf_op jit(solution)/shard_map/attend_forward/pallas_call | solution.py:68
  34.0 9.0 %ahead.2 = (f32[512,768]{1,0:T(8,128)S(1)}, f32[512,128]{1,0:T(8,128)S(1)}, bf16[512,768]{1,0:T(8,128)(2,1)S(1)}, bf16[512,1536]{1,0:T(8,128)(2,1)S(1)}, bf16[51...) custom-call(s32[3]{0:T(128)S(1)} %pad_add_fusion.meta_ref, bf16[2048,768]{1,0:T(8,128)(2,1)} %x_ref.5, ...), custom_call_target="tpu_custom_call" | custom-call | flops 9900000256 | bytes 1024 | tf_op jit(solution)/shard_map/ahead/pallas_call | solution.py:68
  46.2 9.2 %ahead.3 = (f32[512,768]{1,0:T(8,128)S(1)}, f32[512,128]{1,0:T(8,128)S(1)}, bf16[512,768]{1,0:T(8,128)(2,1)S(1)}, bf16[512,1536]{1,0:T(8,128)(2,1)S(1)}, bf16[51...) custom-call(s32[3]{0:T(128)S(1)} %pad_add_fusion.meta_ref, bf16[2048,768]{1,0:T(8,128)(2,1)} %x_ref.5, ...), custom_call_target="tpu_custom_call" | custom-call | flops 9900000256 | bytes 1024 | tf_op jit(solution)/shard_map/ahead/pallas_call | solution.py:68
  58.6 7.4 %collective-permute-done.11.far_ref = bf16[512,768]{1,0:T(8,128)(2,1)S(1)} collective-permute-done((bf16[512,768]{1,0:T(8,128)(2,1)S(1)}, bf16[512,768]{1,0:T(8,128)(2,1)S(1)}, u32[]{:S(2)}, u32[]{:S(2)}) %collective-permute-start.11) | collective-permute-done | bytes 786464 | tf_op jit(solution)/shard_map/ppermute | solution.py:630
  66.0 8.0 %astern.2 = (bf16[512,768]{1,0:T(8,128)(2,1)S(1)}, bf16[512,768]{1,0:T(8,128)(2,1)S(1)}, bf16[512,1536]{1,0:T(8,128)(2,1)S(1)}, f32[512,768]{1,0:T(8,128)S(1)}, ...) custom-call(s32[3]{0:T(128)S(1)} %pad_add_fusion.meta_ref, f32[512,768]{1,0:T(8,128)S(1)} %get-tuple-element.142.own_ref, ...), custom_call_target="tpu_custom_call" | custom-call | flops 11000000512 | bytes 1024 | tf_op jit(solution)/shard_map/astern/pallas_call | solution.py:68
  75.1 3.2 %weight_grads.1 = (bf16[768,768]{1,0:T(8,128)(2,1)S(1)}, bf16[768,768]{1,0:T(8,128)(2,1)S(1)}, bf16[768,768]{1,0:T(8,128)(2,1)S(1)}, bf16[768,768]{1,0:T(8,128)(2,1)S(1)}) custom-call(s32[3]{0:T(128)S(1)} %pad_add_fusion.meta_ref, bf16[512,768]{1,0:T(8,128)(2,1)S(1)} %get-tuple-element.147.x_ref, bf16[512,768]{1,0:T(8,128)(2,1)S(1)} %get-tuple-element.148.g_ref, ...), custom_call_target="tpu_custom_call" | custom-call | flops 5500000256 | bytes 1024 | tf_op jit(solution)/shard_map/weight_grads/pallas_call | solution.py:68
  79.0 3.8 %collective-permute-done.12.far_ref = bf16[512,768]{1,0:T(8,128)(2,1)S(1)} collective-permute-done((bf16[512,768]{1,0:T(8,128)(2,1)S(1)}, bf16[512,768]{1,0:T(8,128)(2,1)S(1)}, u32[]{:S(2)}, u32[]{:S(2)}) %collective-permute-start.12) | collective-permute-done | bytes 786464 | tf_op jit(solution)/shard_map/ppermute | solution.py:630
  82.8 12.4 %astern.3 = (bf16[512,768]{1,0:T(8,128)(2,1)}, bf16[512,768]{1,0:T(8,128)(2,1)}, bf16[512,1536]{1,0:T(8,128)(2,1)}, f32[512,768]{1,0:T(8,128)S(1)}, bf16[512,768...) custom-call(s32[3]{0:T(128)S(1)} %pad_add_fusion.meta_ref, ...), custom_call_target="tpu_custom_call" | custom-call | flops 11000000512 | bytes 1024 | tf_op jit(solution)/shard_map/astern/pallas_call | solution.py:68
  107.9 2.4 inner_norm.2
  114.0 4.7 %collective-permute-start.18 = (bf16[384,768]{1,0:T(8,128)(2,1)S(1)}, bf16[384,768]{1,0:T(8,128)(2,1)S(1)}, u32[]{:S(2)}, u32[]{:S(2)}) collective-permute-start(bf16[384,768]{1,0:T(8,128)(2,1)S(1)} %add_convert_fusion.5), channel_id=1, source_target_pairs={{0,4},{4,0},{8,12},{12,8},{16,20},{20,16},{24,28},{28,24},{1,5},{5... | collective-permute-start | bytes 1769480 | tf_op jit(solution)/shard_map/ppermute | solution.py:633
  118.8 11.0 %attend_backward.2 = (bf16[1024,256]{1,0:T(8,128)(2,1)S(1)}, bf16[1024,256]{1,0:T(8,128)(2,1)S(1)}, bf16[1024,256]{1,0:T(8,128)(2,1)S(1)}) custom-call(s32[3]{0:T(128)S(1)} %pad_add_fusion.meta_ref, bf16[2048,256]{1,0:T(8,128)(2,1)S(1)} %copy-done.45, bf16[2048,256]{1,0:T(8,128)(2,1)S(1)} %copy-done.48, bf16[2048,256]{1,0:T(8,128)(2,1)S(1)} %copy-done.51, ...), custom_call_target="tpu_custom_call" | custom-call | flops 13200000000 | bytes 1024 | tf_op jit(solution)/shard_map/attend_backward/pallas_call | solution.py:68
  132.4 2.3 add_convert_fusion.2
  134.8 2.2 add_convert_fusion.4
  137.0 3.0 %inner_norm.3 = (f32[512,768]{1,0:T(8,128)S(1)}, bf16[192,512]{1,0:T(8,128)(2,1)S(1)}, bf16[192,512]{1,0:T(8,128)(2,1)S(1)}, bf16[256,768]{1,0:T(8,128)(2,1)S(1)...) custom-call(s32[3]{0:T(128)S(1)} %pad_add_fusion.meta_ref, f32[512,768]{1,0:T(8,128)S(1)} %copy-done.39, ...), custom_call_target="tpu_custom_call" | custom-call | flops 3300000000 | bytes 1024 | tf_op jit(solution)/shard_map/inner_norm/pallas_call | solution.py:68
  141.2 1.7 constant_dynamic-slice_fusion.9
  147.1 7.0 %entry_back.2 = (bf16[512,768]{1,0:T(8,128)(2,1)}, bf16[512,768]{1,0:T(8,128)(2,1)S(1)}, f32[576,768]{1,0:T(8,128)S(1)}) custom-call(s32[3]{0:T(128)S(1)} %pad_add_fusion.meta_ref, bf16[2048,768]{1,0:T(8,128)(2,1)} %x_ref.5, bf16[1024,256]{1,0:T(8,128)(2,1)S(1)} %copy-done.62, bf16[1024,256]{1,0:T(8,128)(2,1)S(1)} %copy-done.64, ...), custom_call_target="tpu_custom_call" | custom-call | flops 5500000256 | bytes 1024 | tf_op jit(solution)/shard_map/entry_back/pallas_call | solution.py:68
  156.1 1.7 collective-permute-start.25
  159.2 7.0 %collective-permute-done.25 = bf16[192,768]{1,0:T(8,128)(2,1)} collective-permute-done((bf16[192,768]{1,0:T(8,128)(2,1)}, bf16[192,768]{1,0:T(8,128)(2,1)}, u32[]{:S(2)}, u32[]{:S(2)}) %collective-permute-start.25) | collective-permute-done | bytes 294944 | tf_op jit(solution)/shard_map/ppermute | solution.py:633
  167.6 2.4 collective-permute-done.26
  173.2 1.7 collective-permute-start.30
  177.9 8.6 %attend_backward.3 = (bf16[1024,256]{1,0:T(8,128)(2,1)S(1)}, bf16[1024,256]{1,0:T(8,128)(2,1)S(1)}, bf16[1024,256]{1,0:T(8,128)(2,1)S(1)}) custom-call(s32[3]{0:T(128)S(1)} %pad_add_fusion.meta_ref, bf16[2048,256]{1,0:T(8,128)(2,1)S(1)} %copy-done.46, bf16[2048,256]{1,0:T(8,128)(2,1)S(1)} %copy-done.49, bf16[2048,256]{1,0:T(8,128)(2,1)S(1)} %copy-done.52, ...), custom_call_target="tpu_custom_call" | custom-call | flops 13200000000 | bytes 1024 | tf_op jit(solution)/shard_map/attend_backward/pallas_call | solution.py:68
  187.8 3.5 %collective-permute-done.28 = bf16[96,768]{1,0:T(8,128)(2,1)S(1)} collective-permute-done((bf16[96,768]{1,0:T(8,128)(2,1)S(1)}, bf16[96,768]{1,0:T(8,128)(2,1)S(1)}, u32[]{:S(2)}, u32[]{:S(2)}) %collective-permute-start.28) | collective-permute-done | bytes 147488 | tf_op jit(solution)/shard_map/ppermute | solution.py:633
  191.5 3.0 %collective-permute-start.34 = (bf16[1,1,1,96,768]{4,3,2,1,0:T(8,128)(2,1)S(1)}, bf16[1,1,1,96,768]{4,3,2,1,0:T(8,128)(2,1)S(1)}, u32[]{:S(2)}, u32[]{:S(2)}) collective-permute-start(bf16[1,1,1,96,768]{4,3,2,1,0:T(8,128)(2,1)S(1)} %fusion.2), channel_id=1, source_target_pairs={{0,16},{4,20},{8,24},{12,28},{16,0},{20,4},{24,8},{28,12},{1,17},{... | collective-permute-start | bytes 442376 | tf_op jit(solution)/shard_map/ppermute | solution.py:633
  194.4 6.1 %entry_back.3 = (bf16[512,768]{1,0:T(8,128)(2,1)S(1)}, bf16[512,768]{1,0:T(8,128)(2,1)S(1)}, bf16[576,768]{1,0:T(8,128)(2,1)S(1)}) custom-call(s32[3]{0:T(128)S(1)} %pad_add_fusion.meta_ref, bf16[2048,768]{1,0:T(8,128)(2,1)} %x_ref.5, bf16[1024,256]{1,0:T(8,128)(2,1)S(1)} %get-tuple-element.209.dq_ref, bf16[1024,256]{1,0:T(8,128)(2,1)S(1)} %get-tuple-element.216.dk_ref, ...), custom_call_target="tpu_custom_call" | custom-call | flops 5500000256 | bytes 1024 | tf_op jit(solution)/shard_map/entry_back/pallas_call | solution.py:68
  202.6 2.8 %collective-permute-done.34 = bf16[1,1,1,96,768]{4,3,2,1,0:T(8,128)(2,1)S(1)} collective-permute-done((bf16[1,1,1,96,768]{4,3,2,1,0:T(8,128)(2,1)S(1)}, bf16[1,1,1,96,768]{4,3,2,1,0:T(8,128)(2,1)S(1)}, u32[]{:S(2)}, u32[]{:S(2)}) %collective-permute-start.34) | collective-permute-done | bytes 147488 | tf_op jit(solution)/shard_map/ppermute | solution.py:633
  205.7 2.7 collective-permute-start.38
  208.4 1.6 add_convert_fusion.1.refs_0_
  210.8 6.1 %collective-permute-done.38 = bf16[1,1,2,96,768]{4,3,2,1,0:T(8,128)(2,1)S(1)} collective-permute-done((bf16[1,1,2,96,768]{4,3,2,1,0:T(8,128)(2,1)S(1)}, bf16[1,1,2,96,768]{4,3,2,1,0:T(8,128)(2,1)S(1)}, u32[]{:S(2)}, u32[]{:S(2)}) %collective-permute-start.38) | collective-permute-done | bytes 294944 | tf_op jit(solution)/shard_map/ppermute | solution.py:633
  216.9 5.3 %collective-permute-done.37 = bf16[1,1,2,96,768]{4,3,2,1,0:T(8,128)(2,1)S(1)} collective-permute-done((bf16[1,1,2,96,768]{4,3,2,1,0:T(8,128)(2,1)S(1)}, bf16[1,1,2,96,768]{4,3,2,1,0:T(8,128)(2,1)S(1)}, u32[]{:S(2)}, u32[]{:S(2)}) %collective-permute-start.37) | collective-permute-done | bytes 294944 | tf_op jit(solution)/shard_map/ppermute | solution.py:633
  223.4 1.6 collective-permute-start.44
  225.0 1.6 collective-permute-start.46
  228.2 1.7 collective-permute-start.48
  230.6 2.7 collective-permute-start.43
  233.3 3.2 %collective-permute-done.47 = bf16[72,768]{1,0:T(8,128)(2,1)S(1)} collective-permute-done((bf16[72,768]{1,0:T(8,128)(2,1)S(1)}, bf16[72,768]{1,0:T(8,128)(2,1)S(1)}, u32[]{:S(2)}, u32[]{:S(2)}) %collective-permute-start.47) | collective-permute-done | bytes 110624 | tf_op jit(solution)/shard_map/ppermute | solution.py:633
  238.1 1.6 collective-permute-done.44
  239.9 10.0 %collective-permute-done.43 = bf16[1,2,2,96,768]{4,3,2,1,0:T(8,128)(2,1)S(1)} collective-permute-done((bf16[1,2,2,96,768]{4,3,2,1,0:T(8,128)(2,1)S(1)}, bf16[1,2,2,96,768]{4,3,2,1,0:T(8,128)(2,1)S(1)}, u32[]{:S(2)}, u32[]{:S(2)}) %collective-permute-start.43) | collective-permute-done | bytes 589856 | tf_op jit(solution)/shard_map/ppermute | solution.py:633
  251.8 5.4 %collective-permute-start.51 = (bf16[1,1,72,768]{3,2,1,0:T(8,128)(2,1)S(1)}, bf16[1,1,72,768]{3,2,1,0:T(8,128)(2,1)S(1)}, u32[]{:S(2)}, u32[]{:S(2)}) collective-permute-start(bf16[1,1,72,768]{3,2,1,0:T(8,128)(2,1)S(1)} %fusion.4), channel_id=1, source_target_pairs={{0,16},{4,20},{8,24},{12,28},{16,0},{20,4},{24,8},{28,12},{1,17},{... | collective-permute-start | bytes 331784 | tf_op jit(solution)/shard_map/ppermute | solution.py:633
  257.3 4.9 %collective-permute-done.51 = bf16[1,1,72,768]{3,2,1,0:T(8,128)(2,1)S(1)} collective-permute-done((bf16[1,1,72,768]{3,2,1,0:T(8,128)(2,1)S(1)}, bf16[1,1,72,768]{3,2,1,0:T(8,128)(2,1)S(1)}, u32[]{:S(2)}, u32[]{:S(2)}) %collective-permute-start.51) | collective-permute-done | bytes 110624 | tf_op jit(solution)/shard_map/ppermute | solution.py:633
  262.2 1.6 collective-permute-done.52
  264.0 4.3 %place.2 = bf16[2048,768]{1,0:T(8,128)(2,1)} custom-call(s32[3]{0:T(128)S(1)} %pad_add_fusion.meta_ref, bf16[512,768]{1,0:T(8,128)(2,1)S(1)} %get-tuple-element.145.refs_0_, bf16[512,768]{1,0:T(8,128)(2,1)} %collective-permute-done.14.refs_1_, bf16[512,768]{1,0:T(8,128)(2,1)} %get-tuple-element.161.refs_2_, bf16[512,768]{1,0:T(8,128)(2,1)} %collective-permute-done.15.refs_3_), custom_call_target="tpu_custom_call" | custom-call | flops 3300000000 | bytes 1024 | tf_op jit(solution)/shard_map/place/pallas_call | solution.py:68
  268.8 4.1 %collective-permute-done.53 = bf16[1,4,72,768]{3,2,1,0:T(8,128)(2,1)S(1)} collective-permute-done((bf16[1,4,72,768]{3,2,1,0:T(8,128)(2,1)S(1)}, bf16[1,4,72,768]{3,2,1,0:T(8,128)(2,1)S(1)}, u32[]{:S(2)}, u32[]{:S(2)}) %collective-permute-start.53) | collective-permute-done | bytes 442400 | tf_op jit(solution)/shard_map/ppermute | solution.py:633
  273.1 1.6 convert_element_type.244
  274.6 1.6 convert_element_type.245
  278.9 2.7 place.3
  (294 shorter events, 65.8 us)
Async XLA Ops:
  0.6 19.7 %collective-permute-start = (bf16[192,768]{1,0:T(8,128)(2,1)}, bf16[192,768]{1,0:T(8,128)(2,1)S(1)}, u32[]{:S(2)}, u32[]{:S(2)}) collective-permute-start(bf16[192,768]{1,0:T(8,128)(2,1)} %w0.7), channel_id=1, source_target_pairs={{0,1},{1,0},{2,3},{3,2},{4,5},{5,4},{6,7},{7,6},{8,9},{9,8},{10,11... | collective-permute-start | bytes 884744 | tf_op jit(solution)/shard_map/ppermute | solution.py:630
  1.2 19.4 %collective-permute-start.1 = (bf16[192,768]{1,0:T(8,128)(2,1)}, bf16[192,768]{1,0:T(8,128)(2,1)S(1)}, u32[]{:S(2)}, u32[]{:S(2)}) collective-permute-start(bf16[192,768]{1,0:T(8,128)(2,1)} %w0.7), channel_id=1, source_target_pairs={{0,2},{1,3},{2,0},{3,1},{4,6},{5,7},{6,4},{7,5},{8,10},{9,11},{10,... | collective-permute-start | bytes 884744 | tf_op jit(solution)/shard_map/ppermute | solution.py:630
  3.7 19.2 %collective-permute-start.2 = (bf16[192,768]{1,0:T(8,128)(2,1)}, bf16[192,768]{1,0:T(8,128)(2,1)S(1)}, u32[]{:S(2)}, u32[]{:S(2)}) collective-permute-start(bf16[192,768]{1,0:T(8,128)(2,1)} %w0.7), channel_id=1, source_target_pairs={{0,3},{1,2},{2,1},{3,0},{4,7},{5,6},{6,5},{7,4},{8,11},{9,10},{10,... | collective-permute-start | bytes 884744 | tf_op jit(solution)/shard_map/ppermute | solution.py:630
  3.8 20.2 %collective-permute-start.3 = (bf16[768,768]{1,0:T(8,128)(2,1)}, bf16[768,768]{1,0:T(8,128)(2,1)S(1)}, u32[]{:S(2)}, u32[]{:S(2)}) collective-permute-start(bf16[768,768]{1,0:T(8,128)(2,1)} %ua_ref.7), channel_id=1, source_target_pairs={{0,1},{1,0},{2,3},{3,2},{4,5},{5,4},{6,7},{7,6},{8,9},{9,8},{10,11... | collective-permute-start | bytes 3538952 | tf_op jit(solution)/shard_map/ppermute | solution.py:630
  3.9 20.1 %collective-permute-start.4 = (bf16[768,768]{1,0:T(8,128)(2,1)}, bf16[768,768]{1,0:T(8,128)(2,1)S(1)}, u32[]{:S(2)}, u32[]{:S(2)}) collective-permute-start(bf16[768,768]{1,0:T(8,128)(2,1)} %da_ref.7), channel_id=1, source_target_pairs={{0,1},{1,0},{2,3},{3,2},{4,5},{5,4},{6,7},{7,6},{8,9},{9,8},{10,11... | collective-permute-start | bytes 3538952 | tf_op jit(solution)/shard_map/ppermute | solution.py:630
  20.4 13.6 %collective-permute-start.5 = (bf16[192,512]{1,0:T(8,128)(2,1)S(1)}, bf16[192,512]{1,0:T(8,128)(2,1)S(1)}, u32[]{:S(2)}, u32[]{:S(2)}) collective-permute-start(bf16[192,512]{1,0:T(8,128)(2,1)S(1)} %get-tuple-element.136.o1_ref), channel_id=1, source_target_pairs={{0,1},{1,0},{2,3},{3,2},{4,5},{5,4},{6,7},{7,6},{8,9},{9,8},{10,11... | collective-permute-start | bytes 589832 | tf_op jit(solution)/shard_map/ppermute | solution.py:630
  20.6 13.4 %collective-permute-start.7 = (bf16[192,512]{1,0:T(8,128)(2,1)S(1)}, bf16[192,512]{1,0:T(8,128)(2,1)S(1)}, u32[]{:S(2)}, u32[]{:S(2)}) collective-permute-start(bf16[192,512]{1,0:T(8,128)(2,1)S(1)} %get-tuple-element.136.o1_ref), channel_id=1, source_target_pairs={{0,3},{1,2},{2,1},{3,0},{4,7},{5,6},{6,5},{7,4},{8,11},{9,10},{10,... | collective-permute-start | bytes 589832 | tf_op jit(solution)/shard_map/ppermute | solution.py:630
  23.7 8.8 %collective-permute-start.6 = (bf16[192,512]{1,0:T(8,128)(2,1)S(1)}, bf16[192,512]{1,0:T(8,128)(2,1)S(1)}, u32[]{:S(2)}, u32[]{:S(2)}) collective-permute-start(bf16[192,512]{1,0:T(8,128)(2,1)S(1)} %get-tuple-element.132.a0.o0_ref), channel_id=1, source_target_pairs={{0,2},{1,3},{2,0},{3,1},{4,6},{5,7},{6,4},{7,5},{8,10},{9,11},{10,... | collective-permute-start | bytes 589832 | tf_op jit(solution)/shard_map/ppermute | solution.py:630
  30.6 15.6 %collective-permute-start.10 = (bf16[192,512]{1,0:T(8,128)(2,1)S(1)}, bf16[192,512]{1,0:T(8,128)(2,1)S(1)}, u32[]{:S(2)}, u32[]{:S(2)}) collective-permute-start(bf16[192,512]{1,0:T(8,128)(2,1)S(1)} %get-tuple-element.139.o1_ref), channel_id=1, source_target_pairs={{0,3},{1,2},{2,1},{3,0},{4,7},{5,6},{6,5},{7,4},{8,11},{9,10},{10,... | collective-permute-start | bytes 589832 | tf_op jit(solution)/shard_map/ppermute | solution.py:630
  32.1 14.1 %collective-permute-start.8 = (bf16[192,512]{1,0:T(8,128)(2,1)S(1)}, bf16[192,512]{1,0:T(8,128)(2,1)S(1)}, u32[]{:S(2)}, u32[]{:S(2)}) collective-permute-start(bf16[192,512]{1,0:T(8,128)(2,1)S(1)} %get-tuple-element.139.o1_ref), channel_id=1, source_target_pairs={{0,1},{1,0},{2,3},{3,2},{4,5},{5,4},{6,7},{7,6},{8,9},{9,8},{10,11... | collective-permute-start | bytes 589832 | tf_op jit(solution)/shard_map/ppermute | solution.py:630
  32.5 13.7 %collective-permute-start.9 = (bf16[192,512]{1,0:T(8,128)(2,1)S(1)}, bf16[192,512]{1,0:T(8,128)(2,1)S(1)}, u32[]{:S(2)}, u32[]{:S(2)}) collective-permute-start(bf16[192,512]{1,0:T(8,128)(2,1)S(1)} %get-tuple-element.134.a0.o0_ref), channel_id=1, source_target_pairs={{0,2},{1,3},{2,0},{3,1},{4,6},{5,7},{6,4},{7,5},{8,10},{9,11},{10,... | collective-permute-start | bytes 589832 | tf_op jit(solution)/shard_map/ppermute | solution.py:630
  45.5 20.5 %collective-permute-start.11 = (bf16[512,768]{1,0:T(8,128)(2,1)S(1)}, bf16[512,768]{1,0:T(8,128)(2,1)S(1)}, u32[]{:S(2)}, u32[]{:S(2)}) collective-permute-start(bf16[512,768]{1,0:T(8,128)(2,1)S(1)} %get-tuple-element.143), channel_id=1, source_target_pairs={{0,2},{1,3},{2,0},{3,1},{4,6},{5,7},{6,4},{7,5},{8,10},{9,11},{10,... | collective-permute-start | bytes 2359304 | tf_op jit(solution)/shard_map/ppermute | solution.py:630
  57.2 25.6 %collective-permute-start.12 = (bf16[512,768]{1,0:T(8,128)(2,1)S(1)}, bf16[512,768]{1,0:T(8,128)(2,1)S(1)}, u32[]{:S(2)}, u32[]{:S(2)}) collective-permute-start(bf16[512,768]{1,0:T(8,128)(2,1)S(1)} %get-tuple-element.154), channel_id=1, source_target_pairs={{0,2},{1,3},{2,0},{3,1},{4,6},{5,7},{6,4},{7,5},{8,10},{9,11},{10,... | collective-permute-start | bytes 2359304 | tf_op jit(solution)/shard_map/ppermute | solution.py:630
  78.4 19.9 %collective-permute-start.13 = (bf16[512,768]{1,0:T(8,128)(2,1)S(1)}, bf16[512,768]{1,0:T(8,128)(2,1)S(1)}, u32[]{:S(2)}, u32[]{:S(2)}) collective-permute-start(bf16[512,768]{1,0:T(8,128)(2,1)S(1)} %get-tuple-element.164), channel_id=1, source_target_pairs={{0,2},{1,3},{2,0},{3,1},{4,6},{5,7},{6,4},{7,5},{8,10},{9,11},{10,... | collective-permute-start | bytes 2359304 | tf_op jit(solution)/shard_map/ppermute | solution.py:630
  99.1 12.0 %collective-permute-start.19 = (bf16[768,768]{1,0:T(8,128)(2,1)}, bf16[768,768]{1,0:T(8,128)(2,1)}, u32[]{:S(2)}, u32[]{:S(2)}) collective-permute-start(bf16[768,768]{1,0:T(8,128)(2,1)} %get-tuple-element.180), channel_id=1, source_target_pairs={{0,1},{1,0},{2,3},{3,2},{4,5},{5,4},{6,7},{7,6},{8,9},{9,8},{10,11... | collective-permute-start | bytes 3538952 | tf_op jit(solution)/shard_map/ppermute | solution.py:630
  99.1 13.5 %collective-permute-start.17 = (bf16[768,768]{1,0:T(8,128)(2,1)}, bf16[768,768]{1,0:T(8,128)(2,1)}, u32[]{:S(2)}, u32[]{:S(2)}) collective-permute-start(bf16[768,768]{1,0:T(8,128)(2,1)} %get-tuple-element.177), channel_id=1, source_target_pairs={{0,1},{1,0},{2,3},{3,2},{4,5},{5,4},{6,7},{7,6},{8,9},{9,8},{10,11... | collective-permute-start | bytes 3538952 | tf_op jit(solution)/shard_map/ppermute | solution.py:630
  99.7 11.5 %collective-permute-start.14 = (bf16[512,768]{1,0:T(8,128)(2,1)S(1)}, bf16[512,768]{1,0:T(8,128)(2,1)}, u32[]{:S(2)}, u32[]{:S(2)}) collective-permute-start(bf16[512,768]{1,0:T(8,128)(2,1)S(1)} %get-tuple-element.145.refs_0_), channel_id=1, source_target_pairs={{0,1},{1,0},{2,3},{3,2},{4,5},{5,4},{6,7},{7,6},{8,9},{9,8},{10,11... | collective-permute-start | bytes 2359304 | tf_op jit(solution)/shard_map/ppermute | solution.py:630
  99.7 11.5 %collective-permute-start.15 = (bf16[512,768]{1,0:T(8,128)(2,1)}, bf16[512,768]{1,0:T(8,128)(2,1)}, u32[]{:S(2)}, u32[]{:S(2)}) collective-permute-start(bf16[512,768]{1,0:T(8,128)(2,1)} %get-tuple-element.161.refs_2_), channel_id=1, source_target_pairs={{0,1},{1,0},{2,3},{3,2},{4,5},{5,4},{6,7},{7,6},{8,9},{9,8},{10,11... | collective-permute-start | bytes 2359304 | tf_op jit(solution)/shard_map/ppermute | solution.py:630
  110.3 26.7 %collective-permute-start.21 = (bf16[512,768]{1,0:T(8,128)(2,1)S(1)}, bf16[512,768]{1,0:T(8,128)(2,1)S(1)}, u32[]{:S(2)}, u32[]{:S(2)}) collective-permute-start(bf16[512,768]{1,0:T(8,128)(2,1)S(1)} %copy-done.9), channel_id=1, source_target_pairs={{0,2},{1,3},{2,0},{3,1},{4,6},{5,7},{6,4},{7,5},{8,10},{9,11},{10,... | collective-permute-start | bytes 2359304 | tf_op jit(solution)/shard_map/ppermute | solution.py:630
  111.1 7.6 %collective-permute-start.16 = (bf16[192,512]{1,0:T(8,128)(2,1)S(1)}, bf16[192,512]{1,0:T(8,128)(2,1)S(1)}, u32[]{:S(2)}, u32[]{:S(2)}) collective-permute-start(bf16[192,512]{1,0:T(8,128)(2,1)S(1)} %get-tuple-element.169), channel_id=1, source_target_pairs={{0,1},{1,0},{2,3},{3,2},{4,5},{5,4},{6,7},{7,6},{8,9},{9,8},{10,11... | collective-permute-start | bytes 589832 | tf_op jit(solution)/shard_map/ppermute | solution.py:630
  112.6 18.8 %collective-permute-start.20 = (bf16[384,768]{1,0:T(8,128)(2,1)S(1)}, bf16[384,768]{1,0:T(8,128)(2,1)S(1)}, u32[]{:S(2)}, u32[]{:S(2)}) collective-permute-start(bf16[384,768]{1,0:T(8,128)(2,1)S(1)} %add_convert_fusion.3), channel_id=1, source_target_pairs={{0,8},{4,12},{8,0},{12,4},{16,24},{20,28},{24,16},{28,20},{1,9},{5... | collective-permute-start | bytes 1769480 | tf_op jit(solution)/shard_map/ppermute | solution.py:633
  114.0 18.5 %collective-permute-start.18 = (bf16[384,768]{1,0:T(8,128)(2,1)S(1)}, bf16[384,768]{1,0:T(8,128)(2,1)S(1)}, u32[]{:S(2)}, u32[]{:S(2)}) collective-permute-start(bf16[384,768]{1,0:T(8,128)(2,1)S(1)} %add_convert_fusion.5), channel_id=1, source_target_pairs={{0,4},{4,0},{8,12},{12,8},{16,20},{20,16},{24,28},{28,24},{1,5},{5... | collective-permute-start | bytes 1769480 | tf_op jit(solution)/shard_map/ppermute | solution.py:633
  142.9 16.2 %collective-permute-start.24 = (bf16[192,768]{1,0:T(8,128)(2,1)}, bf16[192,768]{1,0:T(8,128)(2,1)}, u32[]{:S(2)}, u32[]{:S(2)}) collective-permute-start(bf16[192,768]{1,0:T(8,128)(2,1)} %constant_dynamic-slice_fusion.9), channel_id=1, source_target_pairs={{0,8},{4,12},{8,0},{12,4},{16,24},{20,28},{24,16},{28,20},{1,9},{5... | collective-permute-start | bytes 884744 | tf_op jit(solution)/shard_map/ppermute | solution.py:633
  155.3 15.7 %collective-permute-start.27 = (bf16[512,768]{1,0:T(8,128)(2,1)}, bf16[512,768]{1,0:T(8,128)(2,1)}, u32[]{:S(2)}, u32[]{:S(2)}) collective-permute-start(bf16[512,768]{1,0:T(8,128)(2,1)} %get-tuple-element.198), channel_id=1, source_target_pairs={{0,1},{1,0},{2,3},{3,2},{4,5},{5,4},{6,7},{7,6},{8,9},{9,8},{10,11... | collective-permute-start | bytes 2359304 | tf_op jit(solution)/shard_map/ppermute | solution.py:630
  156.1 10.1 %collective-permute-start.25 = (bf16[192,768]{1,0:T(8,128)(2,1)}, bf16[192,768]{1,0:T(8,128)(2,1)}, u32[]{:S(2)}, u32[]{:S(2)}) collective-permute-start(bf16[192,768]{1,0:T(8,128)(2,1)} %constant_dynamic-slice_fusion.8), channel_id=1, source_target_pairs={{0,4},{4,0},{8,12},{12,8},{16,20},{20,16},{24,28},{28,24},{1,5},{5... | collective-permute-start | bytes 884744 | tf_op jit(solution)/shard_map/ppermute | solution.py:633
  158.8 11.1 %collective-permute-start.26 = (bf16[128,768]{1,0:T(8,128)(2,1)S(1)}, bf16[128,768]{1,0:T(8,128)(2,1)S(1)}, u32[]{:S(2)}, u32[]{:S(2)}) collective-permute-start(bf16[128,768]{1,0:T(8,128)(2,1)S(1)} %add_convert_fusion.10), channel_id=1, source_target_pairs={{0,4},{4,0},{8,12},{12,8},{16,20},{20,16},{24,28},{28,24},{1,5},{5... | collective-permute-start | bytes 589832 | tf_op jit(solution)/shard_map/ppermute | solution.py:633
  172.6 21.9 %collective-permute-start.31 = (bf16[512,768]{1,0:T(8,128)(2,1)S(1)}, bf16[512,768]{1,0:T(8,128)(2,1)S(1)}, u32[]{:S(2)}, u32[]{:S(2)}) collective-permute-start(bf16[512,768]{1,0:T(8,128)(2,1)S(1)} %fusion), channel_id=1, source_target_pairs={{0,2},{1,3},{2,0},{3,1},{4,6},{5,7},{6,4},{7,5},{8,10},{9,11},{10,... | collective-permute-start | bytes 2359304 | tf_op jit(solution)/shard_map/ppermute | solution.py:630
  173.2 13.4 %collective-permute-start.30 = (bf16[64,768]{1,0:T(8,128)(2,1)S(1)}, bf16[64,768]{1,0:T(8,128)(2,1)S(1)}, u32[]{:S(2)}, u32[]{:S(2)}) collective-permute-start(bf16[64,768]{1,0:T(8,128)(2,1)S(1)} %constant_dynamic-slice_fusion.5), channel_id=1, source_target_pairs={{0,8},{4,12},{8,0},{12,4},{16,24},{20,28},{24,16},{28,20},{1,9},{5... | collective-permute-start | bytes 294920 | tf_op jit(solution)/shard_map/ppermute | solution.py:633
  174.9 12.8 %collective-permute-start.29 = (bf16[96,768]{1,0:T(8,128)(2,1)S(1)}, bf16[96,768]{1,0:T(8,128)(2,1)S(1)}, u32[]{:S(2)}, u32[]{:S(2)}) collective-permute-start(bf16[96,768]{1,0:T(8,128)(2,1)S(1)} %constant_dynamic-slice_fusion.6), channel_id=1, source_target_pairs={{0,16},{4,20},{8,24},{12,28},{16,0},{20,4},{24,8},{28,12},{1,17},{... | collective-permute-start | bytes 442376 | tf_op jit(solution)/shard_map/ppermute | solution.py:633
  176.5 14.8 %collective-permute-start.28 = (bf16[96,768]{1,0:T(8,128)(2,1)S(1)}, bf16[96,768]{1,0:T(8,128)(2,1)S(1)}, u32[]{:S(2)}, u32[]{:S(2)}) collective-permute-start(bf16[96,768]{1,0:T(8,128)(2,1)S(1)} %constant_dynamic-slice_fusion.7), channel_id=1, source_target_pairs={{0,16},{4,20},{8,24},{12,28},{16,0},{20,4},{24,8},{28,12},{1,17},{... | collective-permute-start | bytes 442376 | tf_op jit(solution)/shard_map/ppermute | solution.py:633
  186.7 14.7 %collective-permute-start.36 = (bf16[32,768]{1,0:T(8,128)(2,1)S(1)}, bf16[32,768]{1,0:T(8,128)(2,1)S(1)}, u32[]{:S(2)}, u32[]{:S(2)}) collective-permute-start(bf16[32,768]{1,0:T(8,128)(2,1)S(1)} %constant_dynamic-slice_fusion.4), channel_id=1, source_target_pairs={{0,16},{4,20},{8,24},{12,28},{16,0},{20,4},{24,8},{28,12},{1,17},{... | collective-permute-start | bytes 147464 | tf_op jit(solution)/shard_map/ppermute | solution.py:633
  191.3 11.2 %collective-permute-start.35 = (bf16[1,1,1,96,768]{4,3,2,1,0:T(8,128)(2,1)S(1)}, bf16[1,1,1,96,768]{4,3,2,1,0:T(8,128)(2,1)S(1)}, u32[]{:S(2)}, u32[]{:S(2)}) collective-permute-start(bf16[1,1,1,96,768]{4,3,2,1,0:T(8,128)(2,1)S(1)} %fusion.3), channel_id=1, source_target_pairs={{0,16},{4,20},{8,24},{12,28},{16,0},{20,4},{24,8},{28,12},{1,17},{... | collective-permute-start | bytes 442376 | tf_op jit(solution)/shard_map/ppermute | solution.py:633
  191.5 13.9 %collective-permute-start.34 = (bf16[1,1,1,96,768]{4,3,2,1,0:T(8,128)(2,1)S(1)}, bf16[1,1,1,96,768]{4,3,2,1,0:T(8,128)(2,1)S(1)}, u32[]{:S(2)}, u32[]{:S(2)}) collective-permute-start(bf16[1,1,1,96,768]{4,3,2,1,0:T(8,128)(2,1)S(1)} %fusion.2), channel_id=1, source_target_pairs={{0,16},{4,20},{8,24},{12,28},{16,0},{20,4},{24,8},{28,12},{1,17},{... | collective-permute-start | bytes 442376 | tf_op jit(solution)/shard_map/ppermute | solution.py:633
  200.5 22.0 %collective-permute-start.33 = (bf16[512,768]{1,0:T(8,128)(2,1)S(1)}, bf16[512,768]{1,0:T(8,128)(2,1)S(1)}, u32[]{:S(2)}, u32[]{:S(2)}) collective-permute-start(bf16[512,768]{1,0:T(8,128)(2,1)S(1)} %get-tuple-element.219), channel_id=1, source_target_pairs={{0,1},{1,0},{2,3},{3,2},{4,5},{5,4},{6,7},{7,6},{8,9},{9,8},{10,11... | collective-permute-start | bytes 2359304 | tf_op jit(solution)/shard_map/ppermute | solution.py:630
  200.7 21.7 %collective-permute-start.40 = (bf16[288,768]{1,0:T(8,128)(2,1)S(1)}, bf16[288,768]{1,0:T(8,128)(2,1)S(1)}, u32[]{:S(2)}, u32[]{:S(2)}) collective-permute-start(bf16[288,768]{1,0:T(8,128)(2,1)S(1)} %constant_dynamic-slice_fusion.3), channel_id=1, source_target_pairs={{0,4},{4,0},{8,12},{12,8},{16,20},{20,16},{24,28},{28,24},{1,5},{5... | collective-permute-start | bytes 1327112 | tf_op jit(solution)/shard_map/ppermute | solution.py:633
  205.7 11.2 %collective-permute-start.38 = (bf16[1,1,2,96,768]{4,3,2,1,0:T(8,128)(2,1)S(1)}, bf16[1,1,2,96,768]{4,3,2,1,0:T(8,128)(2,1)S(1)}, u32[]{:S(2)}, u32[]{:S(2)}) collective-permute-start(bf16[1,1,2,96,768]{4,3,2,1,0:T(8,128)(2,1)S(1)} %pad_maximum_fusion.7), channel_id=1, source_target_pairs={{0,8},{4,12},{8,0},{12,4},{16,24},{20,28},{24,16},{28,20},{1,9},{5... | collective-permute-start | bytes 884744 | tf_op jit(solution)/shard_map/ppermute | solution.py:633
  208.4 13.8 %collective-permute-start.37 = (bf16[1,1,2,96,768]{4,3,2,1,0:T(8,128)(2,1)S(1)}, bf16[1,1,2,96,768]{4,3,2,1,0:T(8,128)(2,1)S(1)}, u32[]{:S(2)}, u32[]{:S(2)}) collective-permute-start(bf16[1,1,2,96,768]{4,3,2,1,0:T(8,128)(2,1)S(1)} %pad_maximum_fusion.6), channel_id=1, source_target_pairs={{0,8},{4,12},{8,0},{12,4},{16,24},{20,28},{24,16},{28,20},{1,9},{5... | collective-permute-start | bytes 884744 | tf_op jit(solution)/shard_map/ppermute | solution.py:633
  210.7 68.2 %collective-permute-start.32 = (bf16[512,768]{1,0:T(8,128)(2,1)S(1)}, bf16[512,768]{1,0:T(8,128)(2,1)S(1)}, u32[]{:S(2)}, u32[]{:S(2)}) collective-permute-start(bf16[512,768]{1,0:T(8,128)(2,1)S(1)} %add_convert_fusion.1.refs_0_), channel_id=1, source_target_pairs={{0,1},{1,0},{2,3},{3,2},{4,5},{5,4},{6,7},{7,6},{8,9},{9,8},{10,11... | collective-permute-start | bytes 2359304 | tf_op jit(solution)/shard_map/ppermute | solution.py:630
  223.4 16.3 %collective-permute-start.44 = (bf16[2,1,2,96,768]{4,3,2,1,0:T(8,128)(2,1)S(1)}, bf16[2,1,2,96,768]{4,3,2,1,0:T(8,128)(2,1)S(1)}, u32[]{:S(2)}, u32[]{:S(2)}) collective-permute-start(bf16[2,1,2,96,768]{4,3,2,1,0:T(8,128)(2,1)S(1)} %pad_maximum_fusion.4), channel_id=1, source_target_pairs={{0,4},{4,0},{8,12},{12,8},{16,20},{20,16},{24,28},{28,24},{1,5},{5... | collective-permute-start | bytes 1769480 | tf_op jit(solution)/shard_map/ppermute | solution.py:633
  226.6 9.9 %collective-permute-start.47 = (bf16[72,768]{1,0:T(8,128)(2,1)S(1)}, bf16[72,768]{1,0:T(8,128)(2,1)S(1)}, u32[]{:S(2)}, u32[]{:S(2)}) collective-permute-start(bf16[72,768]{1,0:T(8,128)(2,1)S(1)} %get-tuple-element.265), channel_id=1, source_target_pairs={{0,16},{4,20},{8,24},{12,28},{16,0},{20,4},{24,8},{28,12},{1,17},{... | collective-permute-start | bytes 331784 | tf_op jit(solution)/shard_map/ppermute | solution.py:633
  228.2 9.9 %collective-permute-start.48 = (bf16[72,768]{1,0:T(8,128)(2,1)S(1)}, bf16[72,768]{1,0:T(8,128)(2,1)S(1)}, u32[]{:S(2)}, u32[]{:S(2)}) collective-permute-start(bf16[72,768]{1,0:T(8,128)(2,1)S(1)} %get-tuple-element.264), channel_id=1, source_target_pairs={{0,24},{4,28},{8,16},{12,20},{16,8},{20,12},{24,0},{28,4},{1,25},{... | collective-permute-start | bytes 331784 | tf_op jit(solution)/shard_map/ppermute | solution.py:633
  230.6 19.3 %collective-permute-start.43 = (bf16[1,2,2,96,768]{4,3,2,1,0:T(8,128)(2,1)S(1)}, bf16[1,2,2,96,768]{4,3,2,1,0:T(8,128)(2,1)S(1)}, u32[]{:S(2)}, u32[]{:S(2)}) collective-permute-start(bf16[1,2,2,96,768]{4,3,2,1,0:T(8,128)(2,1)S(1)} %pad_maximum_fusion.3), channel_id=1, source_target_pairs={{0,4},{4,0},{8,12},{12,8},{16,20},{20,16},{24,28},{28,24},{1,5},{5... | collective-permute-start | bytes 1769480 | tf_op jit(solution)/shard_map/ppermute | solution.py:633
  236.5 14.6 %collective-permute-start.41 = (bf16[512,768]{1,0:T(8,128)(2,1)S(1)}, bf16[512,768]{1,0:T(8,128)(2,1)S(1)}, u32[]{:S(2)}, u32[]{:S(2)}) collective-permute-start(bf16[512,768]{1,0:T(8,128)(2,1)S(1)} %fusion.1), channel_id=1, source_target_pairs={{0,2},{1,3},{2,0},{3,1},{4,6},{5,7},{6,4},{7,5},{8,10},{9,11},{10,... | collective-permute-start | bytes 2359304 | tf_op jit(solution)/shard_map/ppermute | solution.py:630
  251.8 10.4 %collective-permute-start.51 = (bf16[1,1,72,768]{3,2,1,0:T(8,128)(2,1)S(1)}, bf16[1,1,72,768]{3,2,1,0:T(8,128)(2,1)S(1)}, u32[]{:S(2)}, u32[]{:S(2)}) collective-permute-start(bf16[1,1,72,768]{3,2,1,0:T(8,128)(2,1)S(1)} %fusion.4), channel_id=1, source_target_pairs={{0,16},{4,20},{8,24},{12,28},{16,0},{20,4},{24,8},{28,12},{1,17},{... | collective-permute-start | bytes 331784 | tf_op jit(solution)/shard_map/ppermute | solution.py:633
  257.2 6.7 %collective-permute-start.52 = (bf16[1,1,72,768]{3,2,1,0:T(8,128)(2,1)S(1)}, bf16[1,1,72,768]{3,2,1,0:T(8,128)(2,1)S(1)}, u32[]{:S(2)}, u32[]{:S(2)}) collective-permute-start(bf16[1,1,72,768]{3,2,1,0:T(8,128)(2,1)S(1)} %fusion.4), channel_id=1, source_target_pairs={{0,24},{4,28},{8,16},{12,20},{16,8},{20,12},{24,0},{28,4},{1,25},{... | collective-permute-start | bytes 331784 | tf_op jit(solution)/shard_map/ppermute | solution.py:633
  257.2 6.7 %collective-permute-start.49 = (bf16[1,2,2,32,768]{4,3,2,1,0:T(8,128)(2,1)S(1)}, bf16[1,2,2,32,768]{4,3,2,1,0:T(8,128)(2,1)S(1)}, u32[]{:S(2)}, u32[]{:S(2)}) collective-permute-start(bf16[1,2,2,32,768]{4,3,2,1,0:T(8,128)(2,1)S(1)} %pad_maximum_fusion.8), channel_id=1, source_target_pairs={{0,4},{4,0},{8,12},{12,8},{16,20},{20,16},{24,28},{28,24},{1,5},{5... | collective-permute-start | bytes 589832 | tf_op jit(solution)/shard_map/ppermute | solution.py:633
  263.9 9.0 %collective-permute-start.53 = (bf16[1,4,72,768]{3,2,1,0:T(8,128)(2,1)S(1)}, bf16[1,4,72,768]{3,2,1,0:T(8,128)(2,1)S(1)}, u32[]{:S(2)}, u32[]{:S(2)}) collective-permute-start(bf16[1,4,72,768]{3,2,1,0:T(8,128)(2,1)S(1)} %constant_dynamic-update-slice_fusion.3), channel_id=1, source_target_pairs={{0,4},{4,0},{8,12},{12,8},{16,20},{20,16},{24,28},{28,24},{1,5},{5... | collective-permute-start | bytes 1327112 | tf_op jit(solution)/shard_map/ppermute | solution.py:633
  268.7 10.2 %collective-permute-start.42 = (bf16[512,768]{1,0:T(8,128)(2,1)S(1)}, bf16[512,768]{1,0:T(8,128)(2,1)S(1)}, u32[]{:S(2)}, u32[]{:S(2)}) collective-permute-start(bf16[512,768]{1,0:T(8,128)(2,1)S(1)} %add_convert_fusion.refs_2_), channel_id=1, source_target_pairs={{0,1},{1,0},{2,3},{3,2},{4,5},{5,4},{6,7},{7,6},{8,9},{9,8},{10,11... | collective-permute-start | bytes 2359304 | tf_op jit(solution)/shard_map/ppermute | solution.py:630
  (84 other events, 529.3 us)

commit v5 on v4

--- a/solution.py
+++ b/solution.py
@@ -685,6 +685,10 @@
                     self.state = self.state.reshape(-1, d)
             self.parts = (self.state,)
 
+    def sum_dp(value, turn):
+        members = list(range(groups))
+        return lax.psum(value, "dp", axis_index_groups=[members[turn:] + members[:turn]])
+
     scalars = jnp.concatenate([core.reshape(1), lengths])
     token = []
 
@@ -732,21 +736,9 @@
         return done(entry_back(meta(), tokens, grads, qkv_w, before, u, frames, dtype))
 
 
-    pairs = [(b, 1) for b in range(bits)]
     stages = [(0, 1)] + [(b, 2) for b in range(1, bits - 1, 2)] + ([(bits - 1, 1)] if bits % 2 == 0 else [])
-    out_rows = [b[0] for b in back]
-    out_other = [swap(r, 1) for r in out_rows]
-    inner, near, crossed, so_far = [], [], [], ()
-    ffn, chains = [], []
-
-    def finish(group, *after):
-        for chain in group:
-            chain.finish(*after)
-        return [chain.state for chain in group]
-
-    def start(group):
-        for chain in group:
-            chain.start()
+    out_rows = jnp.stack([b[0] for b in back])
+    inner, near, crossed, so_far, entry, spare = [], [], [], (), [], []
 
     def together(group, *others):
         values = lax.optimization_barrier((*(chain.state for chain in group), *others))
@@ -758,60 +750,45 @@
         last = u == seqs - 1
         if u == 0:
             up_own, up_other, down_own, down_other = lax.optimization_barrier((*back[-1][6:], far_grad[0]))[:4]
-            ffn.append(Chain((down_own, swap(down_other, 1)), pairs))
-            ffn.append(Chain((up_own, swap(up_other, 1)), pairs[1:2] + pairs[:1] + pairs[2:], pairs[::-1]))
             res, grads = inner_step(0, ())
-            start(ffn)
             inner.append(res)
             far_grad.append(swap(lax.optimization_barrier((back[-1][4], res[0]))[0], 2))
-            token.extend(out_other)
+            down_sum, up_sum = total((down_own, swap(down_other, 1))), total((up_own, swap(up_other, 1)))
+            token.extend([down_sum, up_sum])
+            down_sum, up_sum = sum_dp(down_sum, 0), sum_dp(up_sum, 1)
         dqkv = attend_step(u, grads)
-        token.extend(finish(ffn + chains, dqkv[0]))
-        start(ffn + chains)
         if not last:
             before = ()
             if u + 1 == seqs - 1:
                 before = (inner[0][3], inner[0][4], inner[0][5], back[0][5], back[1][5])
             res, grads = inner_step(u + 1, before)
             inner.append(res)
-            merge = Chain((res[3], swap(res[4], 1)), pairs)
-            token.extend([grads[1], merge.parts[1]])
-            merge.start()
-        else:
-            token.extend(crossed)
         out = entry_step(u, dqkv, so_far, BF if last else F32)
         so_far = (out[2],)
-        got = swap(out[0], 1)
-        if not last:
-            chains.append(merge)
-            finish(ffn + chains, out[0])
-            (got,) = together(ffn + chains, got)
-            start(ffn + chains)
-            token.extend([chain.state for chain in ffn + chains])
-            near.append(out[1].astype(F32) + got.astype(F32))
-            crossed.append(swap(near[u].astype(BF), 2))
+        entry.append(out)
     qkv = Chain((so_far[0],), stages)
     qkv.start()
-    finish(ffn + [merge], out[0])
-    together(ffn + [merge])
-    start(ffn + [merge])
-    near.append(out[1].astype(F32) + got.astype(F32))
-    chains = ffn + [merge, qkv]
-    finish(chains)
-    (arrived,) = together(chains, near[-1].astype(BF))
-    crossed.append(swap(arrived, 2))
-    start(chains)
-    finish(chains)
-    together(chains, crossed[-1])
-    start(chains)
+    merge_sum = sum_dp(lax.optimization_barrier((total((res[3], swap(res[4], 1))), entry[0][0]))[0], 2)
+    for u in range(seqs):
+        got = swap(entry[u][0], 1)
+        near.append(entry[u][1].astype(F32) + got.astype(F32))
+        crossed.append(swap(near[u].astype(BF), 2))
+    chains = [qkv]
     while any(chain.steps for chain in chains):
-        finish(chains)
-        together(chains)
-        start(chains)
-    down_sum, up_sum, merge_sum, qkv_sum = (chain.state for chain in chains)
+        for chain in chains:
+            chain.finish()
+        if len(qkv.steps) == 1:
+            down_sum, up_sum = together(chains, down_sum, up_sum)
+        else:
+            together(chains)
+        for chain in chains:
+            chain.start()
+    qkv_sum = qkv.state
+    merge_sum, qkv_sum = lax.optimization_barrier((merge_sum, qkv_sum))
 
     ready = [(inner[u][0] + (near[u] + crossed[u].astype(F32))).astype(BF) for u in range(seqs)]
-    layer_output = place(meta(), out_rows, out_other)
+    pairs = [[i, i + 1] for i in range(0, 4, 2)]
+    layer_output = lax.all_gather(out_rows, "tensor", axis=1, tiled=True, axis_index_groups=pairs).reshape(rows, d)
     input_grad = place(scalars, ready, [swap(r, 1) for r in ready])
 
     small = merge_sum[192:196].astype(F32)

time: 286 us -> 383 us (1.34)
  waiting for transfers between devices: 69.9 us -> 176 us
  starting transfers between devices: 51.2 us -> 37 us
  between operations: 2.25 us -> 16.2 us
  local copies, waits for them, and re-layouts: 28.9 us -> 18.8 us
  other arithmetic: 21.5 us -> 27.2 us
  Pallas kernels: 108 us -> 103 us
    psum x0 -> x3, waiting for transfers between devices: none -> 132 us  [sum_dp(): lax.psum(value, 'dp', axis_index_groups=[members[turn:] + members[:turn]])]
    ppermute x26 -> x8, waiting for transfers between devices: 57.3 us -> 24.1 us  [swap_dp(): return lax.ppermute(value, 'dp', [(i, i ^ k) for i in range(groups)])]
    ppermute x26 -> x8, starting transfers between devices: 34.6 us -> 18.5 us  [swap_dp(): return lax.ppermute(value, 'dp', [(i, i ^ k) for i in range(groups)])]
    unnamed x156 -> x135, local copies, waits for them, and re-layouts: 25.6 us -> 13.9 us
    ppermute x28 -> x26, waiting for transfers between devices: 12.7 us -> 19.4 us  [swap(): return lax.ppermute(value, 'tensor', [(i, i ^ k) for i in range(4)])]
    pallas_call x16 -> x15, Pallas kernels: 108 us -> 103 us  [call(): pl.pallas_call(kernel, grid_spec=pltpu.PrefetchScalarGridSpec(num_scalar_...]
    convert_element_type x9 -> x4, other arithmetic: 10.7 us -> 7.17 us  [total(): sum((piece.astype(F32) for piece in pieces)).astype(BF)]
    ppermute x28 -> x26, starting transfers between devices: 16.6 us -> 18.3 us  [swap(): return lax.ppermute(value, 'tensor', [(i, i ^ k) for i in range(4)])]
  transfers between devices with their start and end apart: 54 -> 38, of which waited for: 22 -> 13; matrix products, arithmetic and copies ran while one was open for 8% -> 8% of each run, Pallas kernels for 36% -> 26%
where the time goes in v5:
time: 383 us; the launch traced here: 379 us
  waiting for transfers between devices  176 us (46%)
  Pallas kernels  103 us (27%)
  starting transfers between devices  37 us (10%)
  other arithmetic  27.2 us (7%)
  local copies, waits for them, and re-layouts  18.8 us (5%)
  between operations  16.2 us (4%)
    psum x3, waiting for transfers between devices, sum_dp(): lax.psum(value, 'dp', axis_index_groups=[members[turn:] + members[:turn]])  132 us
    pallas_call x15, Pallas kernels, call(): pl.pallas_call(kernel, grid_spec=pltpu.PrefetchScalarGridSpec(num_scalar_...  103 us
    ppermute x8, waiting for transfers between devices, swap_dp(): return lax.ppermute(value, 'dp', [(i, i ^ k) for i in range(groups)])  24.1 us
    ppermute x26, waiting for transfers between devices, swap(): return lax.ppermute(value, 'tensor', [(i, i ^ k) for i in range(4)])  19.4 us
    ppermute x8, starting transfers between devices, swap_dp(): return lax.ppermute(value, 'dp', [(i, i ^ k) for i in range(groups)])  18.5 us
    ppermute x26, starting transfers between devices, swap(): return lax.ppermute(value, 'tensor', [(i, i ^ k) for i in range(4)])  18.3 us
    unnamed x135, local copies, waits for them, and re-layouts  13.9 us
  transfers between devices with their start and end apart: 38, of which 13 were waited for; matrix products, arithmetic and copies ran while one was open for 8% of the time, Pallas kernels for 26%

profile of v5, /device:TPU:0, one launch (start us, length us, event | category | flops | bytes accessed | tf_op | source)
XLA Modules:
  0.0 378.5 jit_solution(15953153302049125456)
XLA Ops:
  8.6 2.6 collective-permute-start.1
  12.5 7.4 %project.1 = (bf16[2048,256]{1,0:T(8,128)(2,1)S(1)}, bf16[2048,256]{1,0:T(8,128)(2,1)S(1)}, bf16[2048,256]{1,0:T(8,128)(2,1)S(1)}) custom-call(s32[3]{0:T(128)S(1)} %pad_add_fusion.meta_ref, bf16[2048,768]{1,0:T(8,128)(2,1)} %x_ref.5, bf16[192,768]{1,0:T(8,128)(2,1)} %bitcast.20, bf16[192,768]{1,0:T(8,128)(2,1)} %bitcast.23, bf16[192,768]{1,0:T(8,128)(2,1)} %bitcast.26), custom_call_target="tpu_custom_call" | custom-call | flops 3300000000 | bytes 1024 | tf_op jit(solution)/shard_map/project/pallas_call | solution.py:68
  19.9 7.7 %attend_forward.2 = (bf16[192,512]{1,0:T(8,128)(2,1)S(1)}, bf16[192,512]{1,0:T(8,128)(2,1)S(1)}, f32[2,8,512]{2,1,0:T(8,128)S(1)}) custom-call(s32[3]{0:T(128)S(1)} %pad_add_fusion.meta_ref, bf16[2048,256]{1,0:T(8,128)(2,1)S(1)} %get-tuple-element.99.q_ref, bf16[2048,256]{1,0:T(8,128)(2,1)S(1)} %get-tuple-element.100.k_ref, ...), custom_call_target="tpu_custom_call" | custom-call | flops 8800000000 | bytes 1024 | tf_op jit(solution)/shard_map/attend_forward/pallas_call | solution.py:68
  28.6 1.7 collective-permute-start.7
  30.7 4.5 %attend_forward.3 = (bf16[192,512]{1,0:T(8,128)(2,1)S(1)}, bf16[192,512]{1,0:T(8,128)(2,1)S(1)}, f32[2,8,512]{2,1,0:T(8,128)S(1)}) custom-call(s32[3]{0:T(128)S(1)} %pad_add_fusion.meta_ref, bf16[2048,256]{1,0:T(8,128)(2,1)S(1)} %get-tuple-element.99.q_ref, bf16[2048,256]{1,0:T(8,128)(2,1)S(1)} %get-tuple-element.100.k_ref, ...), custom_call_target="tpu_custom_call" | custom-call | flops 8800000000 | bytes 1024 | tf_op jit(solution)/shard_map/attend_forward/pallas_call | solution.py:68
  37.4 3.0 collective-permute-done.6.a2
  40.5 9.3 %ahead.2 = (f32[512,768]{1,0:T(8,128)S(1)}, f32[512,128]{1,0:T(8,128)S(1)}, bf16[512,768]{1,0:T(8,128)(2,1)S(1)}, bf16[512,1536]{1,0:T(8,128)(2,1)S(1)}, bf16[51...) custom-call(s32[3]{0:T(128)S(1)} %pad_add_fusion.meta_ref, bf16[2048,768]{1,0:T(8,128)(2,1)} %x_ref.5, ...), custom_call_target="tpu_custom_call" | custom-call | flops 9900000256 | bytes 1024 | tf_op jit(solution)/shard_map/ahead/pallas_call | solution.py:68
  49.9 1.9 collective-permute-start.11
  51.8 9.5 %ahead.3 = (f32[512,768]{1,0:T(8,128)S(1)}, f32[512,128]{1,0:T(8,128)S(1)}, bf16[512,768]{1,0:T(8,128)(2,1)S(1)}, bf16[512,1536]{1,0:T(8,128)(2,1)S(1)}, bf16[51...) custom-call(s32[3]{0:T(128)S(1)} %pad_add_fusion.meta_ref, bf16[2048,768]{1,0:T(8,128)(2,1)} %x_ref.5, ...), custom_call_target="tpu_custom_call" | custom-call | flops 9900000256 | bytes 1024 | tf_op jit(solution)/shard_map/ahead/pallas_call | solution.py:68
  62.7 7.7 %collective-permute-done.11.far_ref = bf16[512,768]{1,0:T(8,128)(2,1)S(1)} collective-permute-done((bf16[512,768]{1,0:T(8,128)(2,1)S(1)}, bf16[512,768]{1,0:T(8,128)(2,1)S(1)}, u32[]{:S(2)}, u32[]{:S(2)}) %collective-permute-start.11) | collective-permute-done | bytes 786464 | tf_op jit(solution)/shard_map/ppermute | solution.py:630
  70.4 8.3 %astern.2 = (bf16[512,768]{1,0:T(8,128)(2,1)S(1)}, bf16[512,768]{1,0:T(8,128)(2,1)S(1)}, bf16[512,1536]{1,0:T(8,128)(2,1)S(1)}, f32[512,768]{1,0:T(8,128)S(1)}, ...) custom-call(s32[3]{0:T(128)S(1)} %pad_add_fusion.meta_ref, f32[512,768]{1,0:T(8,128)S(1)} %get-tuple-element.112.own_ref, ...), custom_call_target="tpu_custom_call" | custom-call | flops 11000000512 | bytes 1024 | tf_op jit(solution)/shard_map/astern/pallas_call | solution.py:68
  78.8 3.2 weight_grads.1
  82.0 1.9 collective-permute-start.13
  83.9 3.4 collective-permute-done.12.far_ref
  87.3 12.3 %astern.3 = (bf16[512,768]{1,0:T(8,128)(2,1)S(1)}, bf16[512,768]{1,0:T(8,128)(2,1)}, bf16[512,1536]{1,0:T(8,128)(2,1)}, f32[512,768]{1,0:T(8,128)S(1)}, bf16[512...) custom-call(s32[3]{0:T(128)S(1)} %pad_add_fusion.meta_ref, ...), custom_call_target="tpu_custom_call" | custom-call | flops 11000000512 | bytes 1024 | tf_op jit(solution)/shard_map/astern/pallas_call | solution.py:68
  100.1 2.5 collective-permute-done.13.far_ref
  103.1 2.4 inner_norm.2
  110.5 2.7 add_convert_fusion.1
  116.8 1.7 collective-permute-start.17
  122.5 11.2 %attend_backward.2 = (bf16[1024,256]{1,0:T(8,128)(2,1)S(1)}, bf16[1024,256]{1,0:T(8,128)(2,1)S(1)}, bf16[1024,256]{1,0:T(8,128)(2,1)S(1)}) custom-call(s32[3]{0:T(128)S(1)} %pad_add_fusion.meta_ref, bf16[2048,256]{1,0:T(8,128)(2,1)S(1)} %copy-done.39, bf16[2048,256]{1,0:T(8,128)(2,1)S(1)} %copy-done.42, bf16[2048,256]{1,0:T(8,128)(2,1)S(1)} %copy-done.45, ...), custom_call_target="tpu_custom_call" | custom-call | flops 13200000000 | bytes 1024 | tf_op jit(solution)/shard_map/attend_backward/pallas_call | solution.py:68
  133.7 2.7 collective-permute-done.17.far_ref
  136.6 3.2 inner_norm.3
  139.8 7.7 %entry_back.2 = (bf16[512,768]{1,0:T(8,128)(2,1)}, bf16[512,768]{1,0:T(8,128)(2,1)S(1)}, f32[576,768]{1,0:T(8,128)S(1)}) custom-call(s32[3]{0:T(128)S(1)} %pad_add_fusion.meta_ref, bf16[2048,768]{1,0:T(8,128)(2,1)} %x_ref.5, bf16[1024,256]{1,0:T(8,128)(2,1)S(1)} %get-tuple-element.149.dq_ref, bf16[1024,256]{1,0:T(8,128)(2,1)S(1)} %get-tuple-element.162.dk_ref, ...), custom_call_target="tpu_custom_call" | custom-call | flops 5500000256 | bytes 1024 | tf_op jit(solution)/shard_map/entry_back/pallas_call | solution.py:68
  147.6 6.3 %attend_backward.3 = (bf16[1024,256]{1,0:T(8,128)(2,1)S(1)}, bf16[1024,256]{1,0:T(8,128)(2,1)S(1)}, bf16[1024,256]{1,0:T(8,128)(2,1)S(1)}) custom-call(s32[3]{0:T(128)S(1)} %pad_add_fusion.meta_ref, bf16[2048,256]{1,0:T(8,128)(2,1)S(1)} %copy-done.40, bf16[2048,256]{1,0:T(8,128)(2,1)S(1)} %copy-done.43, bf16[2048,256]{1,0:T(8,128)(2,1)S(1)} %copy-done.46, ...), custom_call_target="tpu_custom_call" | custom-call | flops 13200000000 | bytes 1024 | tf_op jit(solution)/shard_map/attend_backward/pallas_call | solution.py:68
  153.8 6.3 %entry_back.3 = (bf16[512,768]{1,0:T(8,128)(2,1)S(1)}, bf16[512,768]{1,0:T(8,128)(2,1)S(1)}, bf16[576,768]{1,0:T(8,128)(2,1)S(1)}) custom-call(s32[3]{0:T(128)S(1)} %pad_add_fusion.meta_ref, bf16[2048,768]{1,0:T(8,128)(2,1)} %x_ref.5, bf16[1024,256]{1,0:T(8,128)(2,1)S(1)} %get-tuple-element.170.dq_ref, bf16[1024,256]{1,0:T(8,128)(2,1)S(1)} %get-tuple-element.172.dk_ref, ...), custom_call_target="tpu_custom_call" | custom-call | flops 5500000256 | bytes 1024 | tf_op jit(solution)/shard_map/entry_back/pallas_call | solution.py:68
  161.8 1.8 collective-permute-start.26
  164.1 1.9 add_convert_fusion.5
  166.0 8.7 %collective-permute-done.26 = bf16[288,768]{1,0:T(8,128)(2,1)} collective-permute-done((bf16[288,768]{1,0:T(8,128)(2,1)}, bf16[288,768]{1,0:T(8,128)(2,1)}, u32[]{:S(2)}, u32[]{:S(2)}) %collective-permute-start.26) | collective-permute-done | bytes 442400 | tf_op jit(solution)/shard_map/ppermute | solution.py:633
  176.0 4.1 %collective-permute-start.27 = (bf16[72,768]{1,0:T(8,128)(2,1)S(1)}, bf16[72,768]{1,0:T(8,128)(2,1)S(1)}, u32[]{:S(2)}, u32[]{:S(2)}) collective-permute-start(bf16[72,768]{1,0:T(8,128)(2,1)S(1)} %get-tuple-element.195), channel_id=1, source_target_pairs={{0,8},{4,12},{8,0},{12,4},{16,24},{20,28},{24,16},{28,20},{1,9},{5... | collective-permute-start | bytes 331784 | tf_op jit(solution)/shard_map/ppermute | solution.py:633
  180.1 2.8 collective-permute-start.28
  183.0 2.2 fusion
  186.6 4.1 %collective-permute-done.27 = bf16[72,768]{1,0:T(8,128)(2,1)S(1)} collective-permute-done((bf16[72,768]{1,0:T(8,128)(2,1)S(1)}, bf16[72,768]{1,0:T(8,128)(2,1)S(1)}, u32[]{:S(2)}, u32[]{:S(2)}) %collective-permute-start.27) | collective-permute-done | bytes 110624 | tf_op jit(solution)/shard_map/ppermute | solution.py:633
  190.7 4.5 %collective-permute-done.28 = bf16[72,768]{1,0:T(8,128)(2,1)S(1)} collective-permute-done((bf16[72,768]{1,0:T(8,128)(2,1)S(1)}, bf16[72,768]{1,0:T(8,128)(2,1)S(1)}, u32[]{:S(2)}, u32[]{:S(2)}) %collective-permute-start.28) | collective-permute-done | bytes 110624 | tf_op jit(solution)/shard_map/ppermute | solution.py:633
  195.2 2.5 collective-permute-done.29
  197.8 5.9 %collective-permute-start.30 = (bf16[1,1,72,768]{3,2,1,0:T(8,128)(2,1)S(1)}, bf16[1,1,72,768]{3,2,1,0:T(8,128)(2,1)S(1)}, u32[]{:S(2)}, u32[]{:S(2)}) collective-permute-start(bf16[1,1,72,768]{3,2,1,0:T(8,128)(2,1)S(1)} %fusion.2), channel_id=1, source_target_pairs={{0,8},{4,12},{8,0},{12,4},{16,24},{20,28},{24,16},{28,20},{1,9},{5... | collective-permute-start | bytes 331784 | tf_op jit(solution)/shard_map/ppermute | solution.py:633
  203.7 2.4 collective-permute-start.32
  206.1 2.3 fusion.1
  212.0 2.3 collective-permute-done.31
  215.6 71.5 %all-reduce.6.cloned.1.call-done = bf16[768,768]{1,0:T(8,128)(2,1)} async-done(((bf16[768,768]{1,0:T(8,128)(2,1)}), bf16[768,768]{1,0:T(8,128)(2,1)}) %all-reduce.6.cloned.1.call-update) | async-done | bytes 1179664 | tf_op jit(solution)/shard_map/psum | solution.py:690
  288.5 2.8 convert_element_type.124
  291.4 1.6 convert_element_type.125
  293.0 2.8 add_convert_fusion.3.refs_0_
  295.8 1.8 add_convert_fusion.2.refs_2_
  298.1 2.0 collective-permute-done.33
  301.4 60.2 %all-reduce.4.cloned.1.call-done = bf16[256,768]{1,0:T(8,128)(2,1)} async-done(((bf16[256,768]{1,0:T(8,128)(2,1)}), bf16[256,768]{1,0:T(8,128)(2,1)}) %all-reduce.4.cloned.1.call-update) | async-done | bytes 393232 | tf_op jit(solution)/shard_map/psum | solution.py:690
  363.0 2.4 convert_bitcast_fusion
  365.4 4.1 %place.1 = bf16[2048,768]{1,0:T(8,128)(2,1)} custom-call(s32[3]{0:T(128)S(1)} %pad_add_fusion.meta_ref, bf16[512,768]{1,0:T(8,128)(2,1)} %add_convert_fusion.3.refs_0_, bf16[512,768]{1,0:T(8,128)(2,1)S(1)} %collective-permute-done.20.refs_1_, bf16[512,768]{1,0:T(8,128)(2,1)S(1)} %add_convert_fusion.2.refs_2_, ...), custom_call_target="tpu_custom_call" | custom-call | flops 3300000000 | bytes 1024 | tf_op jit(solution)/shard_map/place/pallas_call | solution.py:68
  369.5 1.7 copy.34
  (212 shorter events, 34.9 us)
Async XLA Ops:
  8.0 207.6 %all-reduce.8.cloned.1.call-start = ((), (), s32[]{:S(2)}) async-start(), calls=%async_computation.3 | async-start | bytes 2359296 | tf_op jit(solution)/shard_map/psum | solution.py:690
  8.1 20.3 %collective-permute-start = (bf16[192,768]{1,0:T(8,128)(2,1)}, bf16[192,768]{1,0:T(8,128)(2,1)S(1)}, u32[]{:S(2)}, u32[]{:S(2)}) collective-permute-start(bf16[192,768]{1,0:T(8,128)(2,1)} %w0.7), channel_id=1, source_target_pairs={{0,1},{1,0},{2,3},{3,2},{4,5},{5,4},{6,7},{7,6},{8,9},{9,8},{10,11... | collective-permute-start | bytes 884744 | tf_op jit(solution)/shard_map/ppermute | solution.py:630
  8.6 20.0 %collective-permute-start.1 = (bf16[192,768]{1,0:T(8,128)(2,1)}, bf16[192,768]{1,0:T(8,128)(2,1)S(1)}, u32[]{:S(2)}, u32[]{:S(2)}) collective-permute-start(bf16[192,768]{1,0:T(8,128)(2,1)} %w0.7), channel_id=1, source_target_pairs={{0,2},{1,3},{2,0},{3,1},{4,6},{5,7},{6,4},{7,5},{8,10},{9,11},{10,... | collective-permute-start | bytes 884744 | tf_op jit(solution)/shard_map/ppermute | solution.py:630
  11.1 19.1 %collective-permute-start.2 = (bf16[192,768]{1,0:T(8,128)(2,1)}, bf16[192,768]{1,0:T(8,128)(2,1)S(1)}, u32[]{:S(2)}, u32[]{:S(2)}) collective-permute-start(bf16[192,768]{1,0:T(8,128)(2,1)} %w0.7), channel_id=1, source_target_pairs={{0,3},{1,2},{2,1},{3,0},{4,7},{5,6},{6,5},{7,4},{8,11},{9,10},{10,... | collective-permute-start | bytes 884744 | tf_op jit(solution)/shard_map/ppermute | solution.py:630
  11.2 19.5 %collective-permute-start.3 = (bf16[768,768]{1,0:T(8,128)(2,1)}, bf16[768,768]{1,0:T(8,128)(2,1)S(1)}, u32[]{:S(2)}, u32[]{:S(2)}) collective-permute-start(bf16[768,768]{1,0:T(8,128)(2,1)} %ua_ref.7), channel_id=1, source_target_pairs={{0,1},{1,0},{2,3},{3,2},{4,5},{5,4},{6,7},{7,6},{8,9},{9,8},{10,11... | collective-permute-start | bytes 3538952 | tf_op jit(solution)/shard_map/ppermute | solution.py:630
  11.4 19.3 %collective-permute-start.4 = (bf16[768,768]{1,0:T(8,128)(2,1)}, bf16[768,768]{1,0:T(8,128)(2,1)}, u32[]{:S(2)}, u32[]{:S(2)}) collective-permute-start(bf16[768,768]{1,0:T(8,128)(2,1)} %da_ref.7), channel_id=1, source_target_pairs={{0,1},{1,0},{2,3},{3,2},{4,5},{5,4},{6,7},{7,6},{8,9},{9,8},{10,11... | collective-permute-start | bytes 3538952 | tf_op jit(solution)/shard_map/ppermute | solution.py:630
  28.3 74.8 %copy-start.21 = (bf16[192,512]{1,0:T(8,128)(2,1)}, bf16[192,512]{1,0:T(8,128)(2,1)S(1)}, u32[]{:S(2)}) copy-start(bf16[192,512]{1,0:T(8,128)(2,1)S(1)} %get-tuple-element.102.a0.o0_ref) | copy-start | bytes 589828
  28.4 23.4 %copy-start.14 = (bf16[192,768]{1,0:T(8,128)(2,1)}, bf16[192,768]{1,0:T(8,128)(2,1)S(1)}, u32[]{:S(2)}) copy-start(bf16[192,768]{1,0:T(8,128)(2,1)S(1)} %collective-permute-done.w1) | copy-start | bytes 884740
  28.4 8.8 %collective-permute-start.5 = (bf16[192,512]{1,0:T(8,128)(2,1)S(1)}, bf16[192,512]{1,0:T(8,128)(2,1)S(1)}, u32[]{:S(2)}, u32[]{:S(2)}) collective-permute-start(bf16[192,512]{1,0:T(8,128)(2,1)S(1)} %get-tuple-element.106.o1_ref), channel_id=1, source_target_pairs={{0,1},{1,0},{2,3},{3,2},{4,5},{5,4},{6,7},{7,6},{8,9},{9,8},{10,11... | collective-permute-start | bytes 589832 | tf_op jit(solution)/shard_map/ppermute | solution.py:630
  28.6 11.9 %collective-permute-start.7 = (bf16[192,512]{1,0:T(8,128)(2,1)S(1)}, bf16[192,512]{1,0:T(8,128)(2,1)S(1)}, u32[]{:S(2)}, u32[]{:S(2)}) collective-permute-start(bf16[192,512]{1,0:T(8,128)(2,1)S(1)} %get-tuple-element.106.o1_ref), channel_id=1, source_target_pairs={{0,3},{1,2},{2,1},{3,0},{4,7},{5,6},{6,5},{7,4},{8,11},{9,10},{10,... | collective-permute-start | bytes 589832 | tf_op jit(solution)/shard_map/ppermute | solution.py:630
  30.3 10.2 %collective-permute-start.6 = (bf16[192,512]{1,0:T(8,128)(2,1)S(1)}, bf16[192,512]{1,0:T(8,128)(2,1)S(1)}, u32[]{:S(2)}, u32[]{:S(2)}) collective-permute-start(bf16[192,512]{1,0:T(8,128)(2,1)S(1)} %get-tuple-element.102.a0.o0_ref), channel_id=1, source_target_pairs={{0,2},{1,3},{2,0},{3,1},{4,6},{5,7},{6,4},{7,5},{8,10},{9,11},{10,... | collective-permute-start | bytes 589832 | tf_op jit(solution)/shard_map/ppermute | solution.py:630
  30.7 39.7 %copy-start.7 = (bf16[768,768]{1,0:T(8,128)(2,1)}, bf16[768,768]{1,0:T(8,128)(2,1)S(1)}, u32[]{:S(2)}) copy-start(bf16[768,768]{1,0:T(8,128)(2,1)S(1)} %collective-permute-done.3.ub_ref) | copy-start | bytes 3538948
  35.2 14.6 %copy-start.19 = (bf16[192,512]{1,0:T(8,128)(2,1)}, bf16[192,512]{1,0:T(8,128)(2,1)S(1)}, u32[]{:S(2)}) copy-start(bf16[192,512]{1,0:T(8,128)(2,1)S(1)} %get-tuple-element.109.o1_ref) | copy-start | bytes 589828
  35.2 14.6 %copy-start.57 = (f32[2,8,512]{2,1,0:T(8,128)}, f32[2,8,512]{2,1,0:T(8,128)S(1)}, u32[]{:S(2)}) copy-start(f32[2,8,512]{2,1,0:T(8,128)S(1)} %get-tuple-element.169.lse_ref) | copy-start | bytes 98308
  35.2 16.5 %copy-start.17 = (bf16[192,512]{1,0:T(8,128)(2,1)}, bf16[192,512]{1,0:T(8,128)(2,1)S(1)}, u32[]{:S(2)}) copy-start(bf16[192,512]{1,0:T(8,128)(2,1)S(1)} %get-tuple-element.104.a0.o0_ref) | copy-start | bytes 589828
  35.2 16.5 %collective-permute-start.10 = (bf16[192,512]{1,0:T(8,128)(2,1)S(1)}, bf16[192,512]{1,0:T(8,128)(2,1)S(1)}, u32[]{:S(2)}, u32[]{:S(2)}) collective-permute-start(bf16[192,512]{1,0:T(8,128)(2,1)S(1)} %get-tuple-element.109.o1_ref), channel_id=1, source_target_pairs={{0,3},{1,2},{2,1},{3,0},{4,7},{5,6},{6,5},{7,4},{8,11},{9,10},{10,... | collective-permute-start | bytes 589832 | tf_op jit(solution)/shard_map/ppermute | solution.py:630
  36.7 15.0 %collective-permute-start.8 = (bf16[192,512]{1,0:T(8,128)(2,1)S(1)}, bf16[192,512]{1,0:T(8,128)(2,1)S(1)}, u32[]{:S(2)}, u32[]{:S(2)}) collective-permute-start(bf16[192,512]{1,0:T(8,128)(2,1)S(1)} %get-tuple-element.109.o1_ref), channel_id=1, source_target_pairs={{0,1},{1,0},{2,3},{3,2},{4,5},{5,4},{6,7},{7,6},{8,9},{9,8},{10,11... | collective-permute-start | bytes 589832 | tf_op jit(solution)/shard_map/ppermute | solution.py:630
  37.1 14.6 %collective-permute-start.9 = (bf16[192,512]{1,0:T(8,128)(2,1)S(1)}, bf16[192,512]{1,0:T(8,128)(2,1)S(1)}, u32[]{:S(2)}, u32[]{:S(2)}) collective-permute-start(bf16[192,512]{1,0:T(8,128)(2,1)S(1)} %get-tuple-element.104.a0.o0_ref), channel_id=1, source_target_pairs={{0,2},{1,3},{2,0},{3,1},{4,6},{5,7},{6,4},{7,5},{8,10},{9,11},{10,... | collective-permute-start | bytes 589832 | tf_op jit(solution)/shard_map/ppermute | solution.py:630
  49.8 20.6 %copy-start.29 = (s32[2,64]{1,0:T(2,128)S(1)}, s32[2,64]{1,0:T(2,128)}, u32[]{:S(2)}) copy-start(s32[2,64]{1,0:T(2,128)} %span_ref.3) | copy-start | bytes 1540
  49.9 20.5 %collective-permute-start.11 = (bf16[512,768]{1,0:T(8,128)(2,1)S(1)}, bf16[512,768]{1,0:T(8,128)(2,1)S(1)}, u32[]{:S(2)}, u32[]{:S(2)}) collective-permute-start(bf16[512,768]{1,0:T(8,128)(2,1)S(1)} %get-tuple-element.113), channel_id=1, source_target_pairs={{0,2},{1,3},{2,0},{3,1},{4,6},{5,7},{6,4},{7,5},{8,10},{9,11},{10,... | collective-permute-start | bytes 2359304 | tf_op jit(solution)/shard_map/ppermute | solution.py:630
  62.5 16.3 %copy-start.47 = (f32[512,128]{1,0:T(8,128)}, f32[512,128]{1,0:T(8,128)S(1)}, u32[]{:S(2)}) copy-start(f32[512,128]{1,0:T(8,128)S(1)} %get-tuple-element.154.rstd_ref) | copy-start | bytes 786436
  62.5 24.8 %collective-permute-start.12 = (bf16[512,768]{1,0:T(8,128)(2,1)S(1)}, bf16[512,768]{1,0:T(8,128)(2,1)S(1)}, u32[]{:S(2)}, u32[]{:S(2)}) collective-permute-start(bf16[512,768]{1,0:T(8,128)(2,1)S(1)} %get-tuple-element.124), channel_id=1, source_target_pairs={{0,2},{1,3},{2,0},{3,1},{4,6},{5,7},{6,4},{7,5},{8,10},{9,11},{10,... | collective-permute-start | bytes 2359304 | tf_op jit(solution)/shard_map/ppermute | solution.py:630
  82.0 20.5 %collective-permute-start.13 = (bf16[512,768]{1,0:T(8,128)(2,1)S(1)}, bf16[512,768]{1,0:T(8,128)(2,1)S(1)}, u32[]{:S(2)}, u32[]{:S(2)}) collective-permute-start(bf16[512,768]{1,0:T(8,128)(2,1)S(1)} %get-tuple-element.134), channel_id=1, source_target_pairs={{0,2},{1,3},{2,0},{3,1},{4,6},{5,7},{6,4},{7,5},{8,10},{9,11},{10,... | collective-permute-start | bytes 2359304 | tf_op jit(solution)/shard_map/ppermute | solution.py:630
  87.2 15.8 %copy-start.15 = (bf16[192,768]{1,0:T(8,128)(2,1)S(1)}, bf16[192,768]{1,0:T(8,128)(2,1)}, u32[]{:S(2)}) copy-start(bf16[192,768]{1,0:T(8,128)(2,1)} %copy-done.14) | copy-start | bytes 884740
  102.6 6.5 %collective-permute-start.15 = (bf16[768,768]{1,0:T(8,128)(2,1)S(1)}, bf16[768,768]{1,0:T(8,128)(2,1)S(1)}, u32[]{:S(2)}, u32[]{:S(2)}) collective-permute-start(bf16[768,768]{1,0:T(8,128)(2,1)S(1)} %get-tuple-element.144), channel_id=1, source_target_pairs={{0,1},{1,0},{2,3},{3,2},{4,5},{5,4},{6,7},{7,6},{8,9},{9,8},{10,11... | collective-permute-start | bytes 3538952 | tf_op jit(solution)/shard_map/ppermute | solution.py:630
  102.6 7.9 %collective-permute-start.14 = (bf16[768,768]{1,0:T(8,128)(2,1)}, bf16[768,768]{1,0:T(8,128)(2,1)}, u32[]{:S(2)}, u32[]{:S(2)}) collective-permute-start(bf16[768,768]{1,0:T(8,128)(2,1)} %get-tuple-element.142), channel_id=1, source_target_pairs={{0,1},{1,0},{2,3},{3,2},{4,5},{5,4},{6,7},{7,6},{8,9},{9,8},{10,11... | collective-permute-start | bytes 3538952 | tf_op jit(solution)/shard_map/ppermute | solution.py:630
  113.2 173.9 %all-reduce.6.cloned.1.call-start = ((), (), s32[]{:S(2)}) async-start(), calls=%async_computation.2 | async-start | bytes 2359296 | tf_op jit(solution)/shard_map/psum | solution.py:690
  113.9 179.0 %all-gather.2.cloned.1.call-start = ((), (), s32[]{:S(2)}) async-start(), calls=%async_computation | async-start | bytes 4718592 | tf_op jit(solution)/shard_map/all_gather | solution.py:791
  114.1 4.5 %collective-permute-start.16 = (bf16[192,512]{1,0:T(8,128)(2,1)S(1)}, bf16[192,512]{1,0:T(8,128)(2,1)S(1)}, u32[]{:S(2)}, u32[]{:S(2)}) collective-permute-start(bf16[192,512]{1,0:T(8,128)(2,1)S(1)} %copy-done.28), channel_id=1, source_target_pairs={{0,1},{1,0},{2,3},{3,2},{4,5},{5,4},{6,7},{7,6},{8,9},{9,8},{10,11... | collective-permute-start | bytes 589832 | tf_op jit(solution)/shard_map/ppermute | solution.py:630
  115.7 245.9 %all-reduce.4.cloned.1.call-start = ((), (), s32[]{:S(2)}) async-start(), calls=%async_computation.1 | async-start | bytes 786432 | tf_op jit(solution)/shard_map/psum | solution.py:690
  116.8 19.6 %collective-permute-start.17 = (bf16[512,768]{1,0:T(8,128)(2,1)S(1)}, bf16[512,768]{1,0:T(8,128)(2,1)S(1)}, u32[]{:S(2)}, u32[]{:S(2)}) collective-permute-start(bf16[512,768]{1,0:T(8,128)(2,1)S(1)} %copy-done.11), channel_id=1, source_target_pairs={{0,2},{1,3},{2,0},{3,1},{4,6},{5,7},{6,4},{7,5},{8,10},{9,11},{10,... | collective-permute-start | bytes 2359304 | tf_op jit(solution)/shard_map/ppermute | solution.py:630
  122.4 14.1 %copy-start.31 = (f32[512,768]{1,0:T(8,128)S(1)}, f32[512,768]{1,0:T(8,128)}, u32[]{:S(2)}) copy-start(f32[512,768]{1,0:T(8,128)} %copy-done.30) | copy-start | bytes 4718596
  139.8 7.8 %collective-permute-start.21 = (bf16[192,512]{1,0:T(8,128)(2,1)S(1)}, bf16[192,512]{1,0:T(8,128)(2,1)S(1)}, u32[]{:S(2)}, u32[]{:S(2)}) collective-permute-start(bf16[192,512]{1,0:T(8,128)(2,1)S(1)} %get-tuple-element.168), channel_id=1, source_target_pairs={{0,1},{1,0},{2,3},{3,2},{4,5},{5,4},{6,7},{7,6},{8,9},{9,8},{10,11... | collective-permute-start | bytes 589832 | tf_op jit(solution)/shard_map/ppermute | solution.py:630
  147.5 16.6 %collective-permute-start.25 = (bf16[256,768]{1,0:T(8,128)(2,1)}, bf16[256,768]{1,0:T(8,128)(2,1)}, u32[]{:S(2)}, u32[]{:S(2)}) collective-permute-start(bf16[256,768]{1,0:T(8,128)(2,1)} %get-tuple-element.178), channel_id=1, source_target_pairs={{0,1},{1,0},{2,3},{3,2},{4,5},{5,4},{6,7},{7,6},{8,9},{9,8},{10,11... | collective-permute-start | bytes 1179656 | tf_op jit(solution)/shard_map/ppermute | solution.py:630
  161.8 12.9 %collective-permute-start.26 = (bf16[288,768]{1,0:T(8,128)(2,1)}, bf16[288,768]{1,0:T(8,128)(2,1)}, u32[]{:S(2)}, u32[]{:S(2)}) collective-permute-start(bf16[288,768]{1,0:T(8,128)(2,1)} %constant_dynamic-slice_fusion.3), channel_id=1, source_target_pairs={{0,4},{4,0},{8,12},{12,8},{16,20},{20,16},{24,28},{28,24},{1,5},{5... | collective-permute-start | bytes 1327112 | tf_op jit(solution)/shard_map/ppermute | solution.py:633
  163.6 19.4 %collective-permute-start.18 = (bf16[512,768]{1,0:T(8,128)(2,1)}, bf16[512,768]{1,0:T(8,128)(2,1)}, u32[]{:S(2)}, u32[]{:S(2)}) collective-permute-start(bf16[512,768]{1,0:T(8,128)(2,1)} %get-tuple-element.165), channel_id=1, source_target_pairs={{0,1},{1,0},{2,3},{3,2},{4,5},{5,4},{6,7},{7,6},{8,9},{9,8},{10,11... | collective-permute-start | bytes 2359304 | tf_op jit(solution)/shard_map/ppermute | solution.py:630
  163.8 42.3 %collective-permute-start.22 = (bf16[512,768]{1,0:T(8,128)(2,1)}, bf16[512,768]{1,0:T(8,128)(2,1)}, u32[]{:S(2)}, u32[]{:S(2)}) collective-permute-start(bf16[512,768]{1,0:T(8,128)(2,1)} %copy-done.9), channel_id=1, source_target_pairs={{0,1},{1,0},{2,3},{3,2},{4,5},{5,4},{6,7},{7,6},{8,9},{9,8},{10,11... | collective-permute-start | bytes 2359304 | tf_op jit(solution)/shard_map/ppermute | solution.py:630
  176.0 14.7 %collective-permute-start.27 = (bf16[72,768]{1,0:T(8,128)(2,1)S(1)}, bf16[72,768]{1,0:T(8,128)(2,1)S(1)}, u32[]{:S(2)}, u32[]{:S(2)}) collective-permute-start(bf16[72,768]{1,0:T(8,128)(2,1)S(1)} %get-tuple-element.195), channel_id=1, source_target_pairs={{0,8},{4,12},{8,0},{12,4},{16,24},{20,28},{24,16},{28,20},{1,9},{5... | collective-permute-start | bytes 331784 | tf_op jit(solution)/shard_map/ppermute | solution.py:633
  180.1 15.1 %collective-permute-start.28 = (bf16[72,768]{1,0:T(8,128)(2,1)S(1)}, bf16[72,768]{1,0:T(8,128)(2,1)S(1)}, u32[]{:S(2)}, u32[]{:S(2)}) collective-permute-start(bf16[72,768]{1,0:T(8,128)(2,1)S(1)} %get-tuple-element.197), channel_id=1, source_target_pairs={{0,16},{4,20},{8,24},{12,28},{16,0},{20,4},{24,8},{28,12},{1,17},{... | collective-permute-start | bytes 331784 | tf_op jit(solution)/shard_map/ppermute | solution.py:633
  183.0 14.7 %collective-permute-start.29 = (bf16[72,768]{1,0:T(8,128)(2,1)S(1)}, bf16[72,768]{1,0:T(8,128)(2,1)S(1)}, u32[]{:S(2)}, u32[]{:S(2)}) collective-permute-start(bf16[72,768]{1,0:T(8,128)(2,1)S(1)} %get-tuple-element.196), channel_id=1, source_target_pairs={{0,24},{4,28},{8,16},{12,20},{16,8},{20,12},{24,0},{28,4},{1,25},{... | collective-permute-start | bytes 331784 | tf_op jit(solution)/shard_map/ppermute | solution.py:633
  185.2 107.8 %collective-permute-start.19 = (bf16[512,768]{1,0:T(8,128)(2,1)}, bf16[512,768]{1,0:T(8,128)(2,1)}, u32[]{:S(2)}, u32[]{:S(2)}) collective-permute-start(bf16[512,768]{1,0:T(8,128)(2,1)} %fusion), channel_id=1, source_target_pairs={{0,2},{1,3},{2,0},{3,1},{4,6},{5,7},{6,4},{7,5},{8,10},{9,11},{10,... | collective-permute-start | bytes 2359304 | tf_op jit(solution)/shard_map/ppermute | solution.py:630
  197.8 13.5 %collective-permute-start.30 = (bf16[1,1,72,768]{3,2,1,0:T(8,128)(2,1)S(1)}, bf16[1,1,72,768]{3,2,1,0:T(8,128)(2,1)S(1)}, u32[]{:S(2)}, u32[]{:S(2)}) collective-permute-start(bf16[1,1,72,768]{3,2,1,0:T(8,128)(2,1)S(1)} %fusion.2), channel_id=1, source_target_pairs={{0,8},{4,12},{8,0},{12,4},{16,24},{20,28},{24,16},{28,20},{1,9},{5... | collective-permute-start | bytes 331784 | tf_op jit(solution)/shard_map/ppermute | solution.py:633
  203.7 10.6 %collective-permute-start.31 = (bf16[1,1,72,768]{3,2,1,0:T(8,128)(2,1)S(1)}, bf16[1,1,72,768]{3,2,1,0:T(8,128)(2,1)S(1)}, u32[]{:S(2)}, u32[]{:S(2)}) collective-permute-start(bf16[1,1,72,768]{3,2,1,0:T(8,128)(2,1)S(1)} %fusion.2), channel_id=1, source_target_pairs={{0,16},{4,20},{8,24},{12,28},{16,0},{20,4},{24,8},{28,12},{1,17},{... | collective-permute-start | bytes 331784 | tf_op jit(solution)/shard_map/ppermute | solution.py:633
  203.7 11.2 %collective-permute-start.32 = (bf16[1,1,72,768]{3,2,1,0:T(8,128)(2,1)S(1)}, bf16[1,1,72,768]{3,2,1,0:T(8,128)(2,1)S(1)}, u32[]{:S(2)}, u32[]{:S(2)}) collective-permute-start(bf16[1,1,72,768]{3,2,1,0:T(8,128)(2,1)S(1)} %fusion.2), channel_id=1, source_target_pairs={{0,24},{4,28},{8,16},{12,20},{16,8},{20,12},{24,0},{28,4},{1,25},{... | collective-permute-start | bytes 331784 | tf_op jit(solution)/shard_map/ppermute | solution.py:633
  208.4 87.4 %collective-permute-start.23 = (bf16[512,768]{1,0:T(8,128)(2,1)}, bf16[512,768]{1,0:T(8,128)(2,1)}, u32[]{:S(2)}, u32[]{:S(2)}) collective-permute-start(bf16[512,768]{1,0:T(8,128)(2,1)} %fusion.1), channel_id=1, source_target_pairs={{0,2},{1,3},{2,0},{3,1},{4,6},{5,7},{6,4},{7,5},{8,10},{9,11},{10,... | collective-permute-start | bytes 2359304 | tf_op jit(solution)/shard_map/ppermute | solution.py:630
  287.1 13.1 %collective-permute-start.33 = (bf16[1,4,72,768]{3,2,1,0:T(8,128)(2,1)}, bf16[1,4,72,768]{3,2,1,0:T(8,128)(2,1)}, u32[]{:S(2)}, u32[]{:S(2)}) collective-permute-start(bf16[1,4,72,768]{3,2,1,0:T(8,128)(2,1)} %constant_dynamic-update-slice_fusion), channel_id=1, source_target_pairs={{0,4},{4,0},{8,12},{12,8},{16,20},{20,16},{24,28},{28,24},{1,5},{5... | collective-permute-start | bytes 1327112 | tf_op jit(solution)/shard_map/ppermute | solution.py:633
  295.8 69.6 %collective-permute-start.20 = (bf16[512,768]{1,0:T(8,128)(2,1)}, bf16[512,768]{1,0:T(8,128)(2,1)S(1)}, u32[]{:S(2)}, u32[]{:S(2)}) collective-permute-start(bf16[512,768]{1,0:T(8,128)(2,1)} %add_convert_fusion.3.refs_0_), channel_id=1, source_target_pairs={{0,1},{1,0},{2,3},{3,2},{4,5},{5,4},{6,7},{7,6},{8,9},{9,8},{10,11... | collective-permute-start | bytes 2359304 | tf_op jit(solution)/shard_map/ppermute | solution.py:630
  297.6 67.8 %collective-permute-start.24 = (bf16[512,768]{1,0:T(8,128)(2,1)S(1)}, bf16[512,768]{1,0:T(8,128)(2,1)S(1)}, u32[]{:S(2)}, u32[]{:S(2)}) collective-permute-start(bf16[512,768]{1,0:T(8,128)(2,1)S(1)} %add_convert_fusion.2.refs_2_), channel_id=1, source_target_pairs={{0,1},{1,0},{2,3},{3,2},{4,5},{5,4},{6,7},{7,6},{8,9},{9,8},{10,11... | collective-permute-start | bytes 2359304 | tf_op jit(solution)/shard_map/ppermute | solution.py:630
  (57 other events, 380.5 us)
Sparse Core Ops, SparseCore 0:
  113.3 90.2 all-reduce.7
  207.5 79.4 all-reduce.5
  291.0 70.6 all-reduce.3
Sparse Core Ops, SparseCore 1:
  116.5 12.5 all-gather.1

commit v6 on v5

--- a/solution.py
+++ b/solution.py
@@ -12,7 +12,7 @@
 EPS = 1e-05
 LOG2E = 1.4426950408889634
 KB = 256
-VMEM = 16
+VMEM = 10
 RB = 128
 HB = 256
 BF = jnp.bfloat16
@@ -523,7 +523,7 @@
             like((2, d), F32),
         ]
         + [like(shape, BF) for shape in grads],
-        limit=24 if before else VMEM,
+        limit=12 if before else VMEM,
         hold=(0, -3, 8, *range(10, 10 + len(before))),
         out=(3,) if before else (1, 2, 3),
     )
@@ -685,10 +685,6 @@
                     self.state = self.state.reshape(-1, d)
             self.parts = (self.state,)
 
-    def sum_dp(value, turn):
-        members = list(range(groups))
-        return lax.psum(value, "dp", axis_index_groups=[members[turn:] + members[:turn]])
-
     scalars = jnp.concatenate([core.reshape(1), lengths])
     token = []
 
@@ -737,7 +733,6 @@
 
 
     stages = [(0, 1)] + [(b, 2) for b in range(1, bits - 1, 2)] + ([(bits - 1, 1)] if bits % 2 == 0 else [])
-    out_rows = jnp.stack([b[0] for b in back])
     inner, near, crossed, so_far, entry, spare = [], [], [], (), [], []
 
     def together(group, *others):
@@ -755,7 +750,7 @@
             far_grad.append(swap(lax.optimization_barrier((back[-1][4], res[0]))[0], 2))
             down_sum, up_sum = total((down_own, swap(down_other, 1))), total((up_own, swap(up_other, 1)))
             token.extend([down_sum, up_sum])
-            down_sum, up_sum = sum_dp(down_sum, 0), sum_dp(up_sum, 1)
+            down_sum, up_sum = lax.psum((down_sum, up_sum), "dp")
         dqkv = attend_step(u, grads)
         if not last:
             before = ()
@@ -767,29 +762,32 @@
         so_far = (out[2],)
         entry.append(out)
     qkv = Chain((so_far[0],), stages)
-    qkv.start()
-    merge_sum = sum_dp(lax.optimization_barrier((total((res[3], swap(res[4], 1))), entry[0][0]))[0], 2)
+    merge = Chain((res[3], swap(lax.optimization_barrier((res[4], entry[0][0]))[0], 1)), stages[1:] + stages[:1])
     for u in range(seqs):
         got = swap(entry[u][0], 1)
         near.append(entry[u][1].astype(F32) + got.astype(F32))
         crossed.append(swap(near[u].astype(BF), 2))
-    chains = [qkv]
+    chains = [qkv, merge]
+    for chain in chains:
+        chain.start()
     while any(chain.steps for chain in chains):
         for chain in chains:
             chain.finish()
-        if len(qkv.steps) == 1:
-            down_sum, up_sum = together(chains, down_sum, up_sum)
-        else:
-            together(chains)
+        together(chains)
         for chain in chains:
             chain.start()
-    qkv_sum = qkv.state
-    merge_sum, qkv_sum = lax.optimization_barrier((merge_sum, qkv_sum))
-
-    ready = [(inner[u][0] + (near[u] + crossed[u].astype(F32))).astype(BF) for u in range(seqs)]
+    merge_sum, qkv_sum = merge.state, qkv.state
+
     pairs = [[i, i + 1] for i in range(0, 4, 2)]
-    layer_output = lax.all_gather(out_rows, "tensor", axis=1, tiled=True, axis_index_groups=pairs).reshape(rows, d)
-    input_grad = place(scalars, ready, [swap(r, 1) for r in ready])
+
+    def both_cores(blocks):
+        whole = lax.all_gather(jnp.stack(blocks), "tensor", axis=1, tiled=True, axis_index_groups=pairs)
+        return whole.reshape(rows, d)
+
+    down_sum, up_sum = down_sum.astype(F32), up_sum.astype(F32)
+    layer_output = both_cores(list(lax.optimization_barrier((*(b[0] for b in back), inner[0][0]))[:seqs]))
+    layer_output, down_sum, up_sum = lax.optimization_barrier((layer_output, down_sum, up_sum))
+    input_grad = both_cores([(inner[u][0] + (near[u] + crossed[u].astype(F32))).astype(BF) for u in range(seqs)])
 
     small = merge_sum[192:196].astype(F32)
     query_grad, key_grad, value_grad = (qkv_sum[192 * i : 192 * (i + 1)].astype(F32).T for i in range(3))
@@ -800,8 +798,8 @@
         key_grad,
         value_grad,
         merge_sum[:192].astype(F32),
-        up_sum.astype(F32),
-        down_sum.astype(F32),
+        up_sum,
+        down_sum,
         small[0],
         small[1],
         small[2],

time: 383 us -> 282 us (0.74)
  waiting for transfers between devices: 176 us -> 59.2 us
  starting transfers between devices: 37 us -> 59.1 us
  other arithmetic: 27.2 us -> 21.8 us
    psum x3 -> x1, waiting for transfers between devices: 132 us -> 0.01 us  [local(): down_sum, up_sum = lax.psum((down_sum, up_sum), 'dp')]
    ppermute x8 -> x16, starting transfers between devices: 18.5 us -> 41.6 us  [swap_dp(): return lax.ppermute(value, 'dp', [(i, i ^ k) for i in range(groups)])]
    ppermute x26 -> x24, waiting for transfers between devices: 19.4 us -> 28.1 us  [swap(): return lax.ppermute(value, 'tensor', [(i, i ^ k) for i in range(4)])]
    ppermute x8 -> x16, waiting for transfers between devices: 24.1 us -> 31 us  [swap_dp(): return lax.ppermute(value, 'dp', [(i, i ^ k) for i in range(groups)])]
    another operation x1 -> x4, other arithmetic: 1.28 us -> 5.85 us  [both_cores(): jnp.stack(blocks)]
    convert_element_type x4 -> x2, other arithmetic: 9 us -> 4.52 us  [local(): down_sum, up_sum = (down_sum.astype(F32), up_sum.astype(F32))]
    unnamed x135 -> x136, local copies, waits for them, and re-layouts: 13.9 us -> 18.2 us
    pallas_call x15 -> x14, Pallas kernels: 103 us -> 102 us  [call(): pl.pallas_call(kernel, grid_spec=pltpu.PrefetchScalarGridSpec(num_scalar_...]
  transfers between devices with their start and end apart: 38 -> 43, of which waited for: 13 -> 12; matrix products, arithmetic and copies ran while one was open for 8% -> 8% of each run, Pallas kernels for 26% -> 37%
where the time goes in v6:
time: 282 us; the launch traced here: 279 us
  Pallas kernels  102 us (36%)
  waiting for transfers between devices  59.2 us (21%)
  starting transfers between devices  59.1 us (21%)
  other arithmetic  21.8 us (8%)
  local copies, waits for them, and re-layouts  19.8 us (7%)
  between operations  16.6 us (6%)
    pallas_call x14, Pallas kernels, call(): pl.pallas_call(kernel, grid_spec=pltpu.PrefetchScalarGridSpec(num_scalar_...  102 us
    ppermute x16, starting transfers between devices, swap_dp(): return lax.ppermute(value, 'dp', [(i, i ^ k) for i in range(groups)])  41.6 us
    ppermute x16, waiting for transfers between devices, swap_dp(): return lax.ppermute(value, 'dp', [(i, i ^ k) for i in range(groups)])  31 us
    ppermute x24, waiting for transfers between devices, swap(): return lax.ppermute(value, 'tensor', [(i, i ^ k) for i in range(4)])  28.1 us
    unnamed x136, local copies, waits for them, and re-layouts  18.2 us
    ppermute x24, starting transfers between devices, swap(): return lax.ppermute(value, 'tensor', [(i, i ^ k) for i in range(4)])  17.3 us
    convert_element_type x5, other arithmetic, total(): sum((piece.astype(F32) for piece in pieces)).astype(BF)  6.54 us
    another operation x4, other arithmetic, both_cores(): jnp.stack(blocks)  5.85 us
  transfers between devices with their start and end apart: 43, of which 12 were waited for; matrix products, arithmetic and copies ran while one was open for 8% of the time, Pallas kernels for 37%

profile of v6, /device:TPU:0, one launch (start us, length us, event | category | flops | bytes accessed | tf_op | source)
XLA Modules:
  0.0 279.0 jit_solution(1997644358103788789)
XLA Ops:
  8.6 2.6 collective-permute-start.1
  12.4 7.4 %project.1 = (bf16[2048,256]{1,0:T(8,128)(2,1)S(1)}, bf16[2048,256]{1,0:T(8,128)(2,1)S(1)}, bf16[2048,256]{1,0:T(8,128)(2,1)S(1)}) custom-call(s32[3]{0:T(128)S(1)} %pad_add_fusion.meta_ref, bf16[2048,768]{1,0:T(8,128)(2,1)} %x_ref.5, bf16[192,768]{1,0:T(8,128)(2,1)} %bitcast.31, bf16[192,768]{1,0:T(8,128)(2,1)} %bitcast.34, bf16[192,768]{1,0:T(8,128)(2,1)} %bitcast.37), custom_call_target="tpu_custom_call" | custom-call | flops 3300000000 | bytes 1024 | tf_op jit(solution)/shard_map/project/pallas_call | solution.py:68
  19.9 7.7 %attend_forward.2 = (bf16[192,512]{1,0:T(8,128)(2,1)S(1)}, bf16[192,512]{1,0:T(8,128)(2,1)S(1)}, f32[2,8,512]{2,1,0:T(8,128)S(1)}) custom-call(s32[3]{0:T(128)S(1)} %pad_add_fusion.meta_ref, bf16[2048,256]{1,0:T(8,128)(2,1)S(1)} %get-tuple-element.107.q_ref, bf16[2048,256]{1,0:T(8,128)(2,1)S(1)} %get-tuple-element.108.k_ref, ...), custom_call_target="tpu_custom_call" | custom-call | flops 8800000000 | bytes 1024 | tf_op jit(solution)/shard_map/attend_forward/pallas_call | solution.py:68
  28.6 1.7 collective-permute-start.7
  30.7 4.5 %attend_forward.3 = (bf16[192,512]{1,0:T(8,128)(2,1)S(1)}, bf16[192,512]{1,0:T(8,128)(2,1)S(1)}, f32[2,8,512]{2,1,0:T(8,128)S(1)}) custom-call(s32[3]{0:T(128)S(1)} %pad_add_fusion.meta_ref, bf16[2048,256]{1,0:T(8,128)(2,1)S(1)} %get-tuple-element.107.q_ref, bf16[2048,256]{1,0:T(8,128)(2,1)S(1)} %get-tuple-element.108.k_ref, ...), custom_call_target="tpu_custom_call" | custom-call | flops 8800000000 | bytes 1024 | tf_op jit(solution)/shard_map/attend_forward/pallas_call | solution.py:68
  35.3 1.5 collective-permute-start.10
  37.5 3.0 %collective-permute-done.6.a2 = bf16[192,512]{1,0:T(8,128)(2,1)S(1)} collective-permute-done((bf16[192,512]{1,0:T(8,128)(2,1)S(1)}, bf16[192,512]{1,0:T(8,128)(2,1)S(1)}, u32[]{:S(2)}, u32[]{:S(2)}) %collective-permute-start.6) | collective-permute-done | bytes 196640 | tf_op jit(solution)/shard_map/ppermute | solution.py:630
  40.5 9.3 %ahead.2 = (f32[512,768]{1,0:T(8,128)S(1)}, f32[512,128]{1,0:T(8,128)S(1)}, bf16[512,768]{1,0:T(8,128)(2,1)S(1)}, bf16[512,1536]{1,0:T(8,128)(2,1)S(1)}, bf16[51...) custom-call(s32[3]{0:T(128)S(1)} %pad_add_fusion.meta_ref, bf16[2048,768]{1,0:T(8,128)(2,1)} %x_ref.5, ...), custom_call_target="tpu_custom_call" | custom-call | flops 9900000256 | bytes 1024 | tf_op jit(solution)/shard_map/ahead/pallas_call | solution.py:68
  49.9 1.9 collective-permute-start.11
  51.8 9.6 %ahead.3 = (f32[512,768]{1,0:T(8,128)S(1)}, f32[512,128]{1,0:T(8,128)S(1)}, bf16[512,768]{1,0:T(8,128)(2,1)S(1)}, bf16[512,1536]{1,0:T(8,128)(2,1)S(1)}, bf16[51...) custom-call(s32[3]{0:T(128)S(1)} %pad_add_fusion.meta_ref, bf16[2048,768]{1,0:T(8,128)(2,1)} %x_ref.5, ...), custom_call_target="tpu_custom_call" | custom-call | flops 9900000256 | bytes 1024 | tf_op jit(solution)/shard_map/ahead/pallas_call | solution.py:68
  62.8 7.6 %collective-permute-done.11.far_ref = bf16[512,768]{1,0:T(8,128)(2,1)S(1)} collective-permute-done((bf16[512,768]{1,0:T(8,128)(2,1)S(1)}, bf16[512,768]{1,0:T(8,128)(2,1)S(1)}, u32[]{:S(2)}, u32[]{:S(2)}) %collective-permute-start.11) | collective-permute-done | bytes 786464 | tf_op jit(solution)/shard_map/ppermute | solution.py:630
  71.7 8.3 %astern.2 = (bf16[512,768]{1,0:T(8,128)(2,1)S(1)}, bf16[512,768]{1,0:T(8,128)(2,1)S(1)}, bf16[512,1536]{1,0:T(8,128)(2,1)S(1)}, f32[512,768]{1,0:T(8,128)S(1)}, ...) custom-call(s32[3]{0:T(128)S(1)} %pad_add_fusion.meta_ref, f32[512,768]{1,0:T(8,128)S(1)} %get-tuple-element.120.own_ref, ...), custom_call_target="tpu_custom_call" | custom-call | flops 11000000512 | bytes 1024 | tf_op jit(solution)/shard_map/astern/pallas_call | solution.py:68
  80.1 3.2 %weight_grads.1 = (bf16[768,768]{1,0:T(8,128)(2,1)S(1)}, bf16[768,768]{1,0:T(8,128)(2,1)S(1)}, bf16[768,768]{1,0:T(8,128)(2,1)S(1)}, bf16[768,768]{1,0:T(8,128)(2,1)S(1)}) custom-call(s32[3]{0:T(128)S(1)} %pad_add_fusion.meta_ref, bf16[512,768]{1,0:T(8,128)(2,1)S(1)} %get-tuple-element.125.x_ref, bf16[512,768]{1,0:T(8,128)(2,1)S(1)} %get-tuple-element.126.g_ref, ...), custom_call_target="tpu_custom_call" | custom-call | flops 5500000256 | bytes 1024 | tf_op jit(solution)/shard_map/weight_grads/pallas_call | solution.py:68
  83.3 1.9 collective-permute-start.13
  85.2 2.1 collective-permute-done.12.far_ref
  87.3 12.2 %astern.3 = (bf16[512,768]{1,0:T(8,128)(2,1)S(1)}, bf16[512,768]{1,0:T(8,128)(2,1)}, bf16[512,1536]{1,0:T(8,128)(2,1)}, f32[512,768]{1,0:T(8,128)S(1)}, bf16[512...) custom-call(s32[3]{0:T(128)S(1)} %pad_add_fusion.meta_ref, ...), custom_call_target="tpu_custom_call" | custom-call | flops 11000000512 | bytes 1024 | tf_op jit(solution)/shard_map/astern/pallas_call | solution.py:68
  99.5 3.1 %collective-permute-done.13.far_ref = bf16[512,768]{1,0:T(8,128)(2,1)S(1)} collective-permute-done((bf16[512,768]{1,0:T(8,128)(2,1)S(1)}, bf16[512,768]{1,0:T(8,128)(2,1)S(1)}, u32[]{:S(2)}, u32[]{:S(2)}) %collective-permute-start.13) | collective-permute-done | bytes 786464 | tf_op jit(solution)/shard_map/ppermute | solution.py:630
  103.1 2.9 %inner_norm.2 = (f32[512,768]{1,0:T(8,128)S(1)}, bf16[192,512]{1,0:T(8,128)(2,1)S(1)}, bf16[192,512]{1,0:T(8,128)(2,1)}, f32[192,768]{1,0:T(8,128)S(1)}, f32[192,768]{1,0:T(8,128)S(1)}, /*index=5*/f32[2,768]{1,0:T(2,128)S(1)}) custom-call(s32[3]{0:T(128)S(1)} %pad_add_fusion.meta_ref, f32[512,768]{1,0:T(8,128)S(1)} %get-tuple-element.141.own_ref, ...), custom_call_target="tpu_custom_call" | custom-call | flops 3300000000 | bytes 1024 | tf_op jit(solution)/shard_map/inner_norm/pallas_call | solution.py:68
  110.6 1.8 collective-permute-start.17
  118.6 12.8 %attend_backward.2 = (bf16[1024,256]{1,0:T(8,128)(2,1)S(1)}, bf16[1024,256]{1,0:T(8,128)(2,1)S(1)}, bf16[1024,256]{1,0:T(8,128)(2,1)S(1)}) custom-call(s32[3]{0:T(128)S(1)} %pad_add_fusion.meta_ref, bf16[2048,256]{1,0:T(8,128)(2,1)S(1)} %copy-done.36, bf16[2048,256]{1,0:T(8,128)(2,1)S(1)} %copy-done.39, bf16[2048,256]{1,0:T(8,128)(2,1)S(1)} %copy-done.42, ...), custom_call_target="tpu_custom_call" | custom-call | flops 13200000000 | bytes 1024 | tf_op jit(solution)/shard_map/attend_backward/pallas_call | solution.py:68
  131.6 4.2 %inner_norm.3 = (f32[512,768]{1,0:T(8,128)S(1)}, bf16[192,512]{1,0:T(8,128)(2,1)S(1)}, bf16[192,512]{1,0:T(8,128)(2,1)S(1)}, bf16[256,768]{1,0:T(8,128)(2,1)S(1)...) custom-call(s32[3]{0:T(128)S(1)} %pad_add_fusion.meta_ref, f32[512,768]{1,0:T(8,128)S(1)} %copy-done.30, ...), custom_call_target="tpu_custom_call" | custom-call | flops 3300000000 | bytes 1024 | tf_op jit(solution)/shard_map/inner_norm/pallas_call | solution.py:68
  135.9 6.8 %entry_back.2 = (bf16[512,768]{1,0:T(8,128)(2,1)S(1)}, bf16[512,768]{1,0:T(8,128)(2,1)S(1)}, f32[576,768]{1,0:T(8,128)S(1)}) custom-call(s32[3]{0:T(128)S(1)} %pad_add_fusion.meta_ref, bf16[2048,768]{1,0:T(8,128)(2,1)} %x_ref.5, bf16[1024,256]{1,0:T(8,128)(2,1)S(1)} %get-tuple-element.160.dq_ref, bf16[1024,256]{1,0:T(8,128)(2,1)S(1)} %get-tuple-element.173.dk_ref, ...), custom_call_target="tpu_custom_call" | custom-call | flops 5500000256 | bytes 1024 | tf_op jit(solution)/shard_map/entry_back/pallas_call | solution.py:68
  142.8 6.3 %attend_backward.3 = (bf16[1024,256]{1,0:T(8,128)(2,1)S(1)}, bf16[1024,256]{1,0:T(8,128)(2,1)S(1)}, bf16[1024,256]{1,0:T(8,128)(2,1)S(1)}) custom-call(s32[3]{0:T(128)S(1)} %pad_add_fusion.meta_ref, bf16[2048,256]{1,0:T(8,128)(2,1)S(1)} %copy-done.37, bf16[2048,256]{1,0:T(8,128)(2,1)S(1)} %copy-done.40, bf16[2048,256]{1,0:T(8,128)(2,1)S(1)} %copy-done.43, ...), custom_call_target="tpu_custom_call" | custom-call | flops 13200000000 | bytes 1024 | tf_op jit(solution)/shard_map/attend_backward/pallas_call | solution.py:68
  149.1 7.1 %entry_back.3 = (bf16[512,768]{1,0:T(8,128)(2,1)}, bf16[512,768]{1,0:T(8,128)(2,1)S(1)}, bf16[576,768]{1,0:T(8,128)(2,1)S(1)}) custom-call(s32[3]{0:T(128)S(1)} %pad_add_fusion.meta_ref, bf16[2048,768]{1,0:T(8,128)(2,1)} %x_ref.5, bf16[1024,256]{1,0:T(8,128)(2,1)S(1)} %get-tuple-element.181.dq_ref, bf16[1024,256]{1,0:T(8,128)(2,1)S(1)} %get-tuple-element.183.dk_ref, ...), custom_call_target="tpu_custom_call" | custom-call | flops 5500000256 | bytes 1024 | tf_op jit(solution)/shard_map/entry_back/pallas_call | solution.py:68
  164.4 4.9 %collective-permute-start.26 = (bf16[64,768]{1,0:T(8,128)(2,1)S(1)}, bf16[64,768]{1,0:T(8,128)(2,1)S(1)}, u32[]{:S(2)}, u32[]{:S(2)}) collective-permute-start(bf16[64,768]{1,0:T(8,128)(2,1)S(1)} %get-tuple-element.215), channel_id=1, source_target_pairs={{0,16},{4,20},{8,24},{12,28},{16,0},{20,4},{24,8},{28,12},{1,17},{... | collective-permute-start | bytes 294920 | tf_op jit(solution)/shard_map/ppermute | solution.py:633
  171.5 9.8 %collective-permute-start.23 = (bf16[288,768]{1,0:T(8,128)(2,1)}, bf16[288,768]{1,0:T(8,128)(2,1)}, u32[]{:S(2)}, u32[]{:S(2)}) collective-permute-start(bf16[288,768]{1,0:T(8,128)(2,1)} %constant_dynamic-slice_fusion.4), channel_id=1, source_target_pairs={{0,4},{4,0},{8,12},{12,8},{16,20},{20,16},{24,28},{28,24},{1,5},{5... | collective-permute-start | bytes 1327112 | tf_op jit(solution)/shard_map/ppermute | solution.py:633
  181.3 1.6 add_convert_fusion.6
  182.9 1.7 fusion.2
  184.6 12.2 %collective-permute-done.22 = bf16[512,768]{1,0:T(8,128)(2,1)S(1)} collective-permute-done((bf16[512,768]{1,0:T(8,128)(2,1)S(1)}, bf16[512,768]{1,0:T(8,128)(2,1)S(1)}, u32[]{:S(2)}, u32[]{:S(2)}) %collective-permute-start.22) | collective-permute-done | bytes 786464 | tf_op jit(solution)/shard_map/ppermute | solution.py:630
  196.8 1.6 fusion.3
  202.0 7.3 %collective-permute-start.31 = (bf16[32,768]{1,0:T(8,128)(2,1)S(1)}, bf16[32,768]{1,0:T(8,128)(2,1)S(1)}, u32[]{:S(2)}, u32[]{:S(2)}) collective-permute-start(bf16[32,768]{1,0:T(8,128)(2,1)S(1)} %constant_dynamic-slice_fusion), channel_id=1, source_target_pairs={{0,4},{4,0},{8,12},{12,8},{16,20},{20,16},{24,28},{28,24},{1,5},{5... | collective-permute-start | bytes 147464 | tf_op jit(solution)/shard_map/ppermute | solution.py:633
  209.4 2.7 collective-permute-start.29
  212.1 1.7 collective-permute-start.30
  213.8 8.5 %collective-permute-done.28 = bf16[72,768]{1,0:T(8,128)(2,1)S(1)} collective-permute-done((bf16[72,768]{1,0:T(8,128)(2,1)S(1)}, bf16[72,768]{1,0:T(8,128)(2,1)S(1)}, u32[]{:S(2)}, u32[]{:S(2)}) %collective-permute-start.28) | collective-permute-done | bytes 110624 | tf_op jit(solution)/shard_map/ppermute | solution.py:633
  222.3 2.4 collective-permute-done.29
  224.7 4.0 %collective-permute-done.30 = bf16[72,768]{1,0:T(8,128)(2,1)S(1)} collective-permute-done((bf16[72,768]{1,0:T(8,128)(2,1)S(1)}, bf16[72,768]{1,0:T(8,128)(2,1)S(1)}, u32[]{:S(2)}, u32[]{:S(2)}) %collective-permute-start.30) | collective-permute-done | bytes 110624 | tf_op jit(solution)/shard_map/ppermute | solution.py:633
  228.7 4.7 %collective-permute-start.32 = (bf16[1,1,72,768]{3,2,1,0:T(8,128)(2,1)S(1)}, bf16[1,1,72,768]{3,2,1,0:T(8,128)(2,1)S(1)}, u32[]{:S(2)}, u32[]{:S(2)}) collective-permute-start(bf16[1,1,72,768]{3,2,1,0:T(8,128)(2,1)S(1)} %fusion.4), channel_id=1, source_target_pairs={{0,8},{4,12},{8,0},{12,4},{16,24},{20,28},{24,16},{28,20},{1,9},{5... | collective-permute-start | bytes 331784 | tf_op jit(solution)/shard_map/ppermute | solution.py:633
  233.4 2.4 collective-permute-start.34
  236.7 3.2 %collective-permute-done.35 = bf16[1,1,32,768]{3,2,1,0:T(8,128)(2,1)S(1)} collective-permute-done((bf16[1,1,32,768]{3,2,1,0:T(8,128)(2,1)S(1)}, bf16[1,1,32,768]{3,2,1,0:T(8,128)(2,1)S(1)}, u32[]{:S(2)}, u32[]{:S(2)}) %collective-permute-start.35) | collective-permute-done | bytes 49184 | tf_op jit(solution)/shard_map/ppermute | solution.py:633
  240.0 4.0 %collective-permute-done.33 = bf16[1,1,72,768]{3,2,1,0:T(8,128)(2,1)S(1)} collective-permute-done((bf16[1,1,72,768]{3,2,1,0:T(8,128)(2,1)S(1)}, bf16[1,1,72,768]{3,2,1,0:T(8,128)(2,1)S(1)}, u32[]{:S(2)}, u32[]{:S(2)}) %collective-permute-start.33) | collective-permute-done | bytes 110624 | tf_op jit(solution)/shard_map/ppermute | solution.py:633
  244.1 1.9 collective-permute-start.37
  246.3 2.2 collective-permute-start.39
  250.0 5.5 %collective-permute-done.38 = bf16[1,2,32,768]{3,2,1,0:T(8,128)(2,1)S(1)} collective-permute-done((bf16[1,2,32,768]{3,2,1,0:T(8,128)(2,1)S(1)}, bf16[1,2,32,768]{3,2,1,0:T(8,128)(2,1)S(1)}, u32[]{:S(2)}, u32[]{:S(2)}) %collective-permute-start.38) | collective-permute-done | bytes 98336 | tf_op jit(solution)/shard_map/ppermute | solution.py:633
  255.5 3.5 %collective-permute-done.36 = bf16[1,4,72,768]{3,2,1,0:T(8,128)(2,1)S(1)} collective-permute-done((bf16[1,4,72,768]{3,2,1,0:T(8,128)(2,1)S(1)}, bf16[1,4,72,768]{3,2,1,0:T(8,128)(2,1)S(1)}, u32[]{:S(2)}, u32[]{:S(2)}) %collective-permute-start.36) | collective-permute-done | bytes 442400 | tf_op jit(solution)/shard_map/ppermute | solution.py:633
  261.2 2.9 %convert_element_type.144 = f32[768,768]{1,0:T(8,128)} convert(bf16[768,768]{1,0:T(8,128)(2,1)} %get-tuple-element.206) | non-fusion elementwise | flops 589824 | bytes 3538944 | tf_op jit(solution)/shard_map/convert_element_type | solution.py:787
  264.2 1.6 convert_element_type.148
  265.7 3.9 %copy.38 = bf16[2048,768]{1,0:T(8,128)(2,1)} copy(bf16[2048,768]{1,0:T(8,128)(2,1)} %bitcast.27) | data formatting | bytes 6291456
  269.7 1.7 copy.39
  (232 shorter events, 37.0 us)
Async XLA Ops:
  8.0 253.2 %all-reduce.3.cloned.1.call-start = ((), (), s32[]{:S(2)}) async-start(), calls=%async_computation.2 | async-start | bytes 4718592 | tf_op jit(solution)/shard_map/psum | solution.py:753
  8.1 20.3 %collective-permute-start = (bf16[192,768]{1,0:T(8,128)(2,1)}, bf16[192,768]{1,0:T(8,128)(2,1)S(1)}, u32[]{:S(2)}, u32[]{:S(2)}) collective-permute-start(bf16[192,768]{1,0:T(8,128)(2,1)} %w0.7), channel_id=1, source_target_pairs={{0,1},{1,0},{2,3},{3,2},{4,5},{5,4},{6,7},{7,6},{8,9},{9,8},{10,11... | collective-permute-start | bytes 884744 | tf_op jit(solution)/shard_map/ppermute | solution.py:630
  8.6 20.0 %collective-permute-start.1 = (bf16[192,768]{1,0:T(8,128)(2,1)}, bf16[192,768]{1,0:T(8,128)(2,1)S(1)}, u32[]{:S(2)}, u32[]{:S(2)}) collective-permute-start(bf16[192,768]{1,0:T(8,128)(2,1)} %w0.7), channel_id=1, source_target_pairs={{0,2},{1,3},{2,0},{3,1},{4,6},{5,7},{6,4},{7,5},{8,10},{9,11},{10,... | collective-permute-start | bytes 884744 | tf_op jit(solution)/shard_map/ppermute | solution.py:630
  11.1 19.2 %collective-permute-start.2 = (bf16[192,768]{1,0:T(8,128)(2,1)}, bf16[192,768]{1,0:T(8,128)(2,1)S(1)}, u32[]{:S(2)}, u32[]{:S(2)}) collective-permute-start(bf16[192,768]{1,0:T(8,128)(2,1)} %w0.7), channel_id=1, source_target_pairs={{0,3},{1,2},{2,1},{3,0},{4,7},{5,6},{6,5},{7,4},{8,11},{9,10},{10,... | collective-permute-start | bytes 884744 | tf_op jit(solution)/shard_map/ppermute | solution.py:630
  11.2 19.5 %collective-permute-start.3 = (bf16[768,768]{1,0:T(8,128)(2,1)}, bf16[768,768]{1,0:T(8,128)(2,1)S(1)}, u32[]{:S(2)}, u32[]{:S(2)}) collective-permute-start(bf16[768,768]{1,0:T(8,128)(2,1)} %ua_ref.7), channel_id=1, source_target_pairs={{0,1},{1,0},{2,3},{3,2},{4,5},{5,4},{6,7},{7,6},{8,9},{9,8},{10,11... | collective-permute-start | bytes 3538952 | tf_op jit(solution)/shard_map/ppermute | solution.py:630
  11.4 19.3 %collective-permute-start.4 = (bf16[768,768]{1,0:T(8,128)(2,1)}, bf16[768,768]{1,0:T(8,128)(2,1)}, u32[]{:S(2)}, u32[]{:S(2)}) collective-permute-start(bf16[768,768]{1,0:T(8,128)(2,1)} %da_ref.7), channel_id=1, source_target_pairs={{0,1},{1,0},{2,3},{3,2},{4,5},{5,4},{6,7},{7,6},{8,9},{9,8},{10,11... | collective-permute-start | bytes 3538952 | tf_op jit(solution)/shard_map/ppermute | solution.py:630
  28.3 74.8 %copy-start.20 = (bf16[192,512]{1,0:T(8,128)(2,1)}, bf16[192,512]{1,0:T(8,128)(2,1)S(1)}, u32[]{:S(2)}) copy-start(bf16[192,512]{1,0:T(8,128)(2,1)S(1)} %get-tuple-element.110.a0.o0_ref) | copy-start | bytes 589828
  28.4 23.4 %copy-start.13 = (bf16[192,768]{1,0:T(8,128)(2,1)}, bf16[192,768]{1,0:T(8,128)(2,1)S(1)}, u32[]{:S(2)}) copy-start(bf16[192,768]{1,0:T(8,128)(2,1)S(1)} %collective-permute-done.w1) | copy-start | bytes 884740
  28.4 8.8 %collective-permute-start.5 = (bf16[192,512]{1,0:T(8,128)(2,1)S(1)}, bf16[192,512]{1,0:T(8,128)(2,1)S(1)}, u32[]{:S(2)}, u32[]{:S(2)}) collective-permute-start(bf16[192,512]{1,0:T(8,128)(2,1)S(1)} %get-tuple-element.114.o1_ref), channel_id=1, source_target_pairs={{0,1},{1,0},{2,3},{3,2},{4,5},{5,4},{6,7},{7,6},{8,9},{9,8},{10,11... | collective-permute-start | bytes 589832 | tf_op jit(solution)/shard_map/ppermute | solution.py:630
  28.6 11.9 %collective-permute-start.7 = (bf16[192,512]{1,0:T(8,128)(2,1)S(1)}, bf16[192,512]{1,0:T(8,128)(2,1)S(1)}, u32[]{:S(2)}, u32[]{:S(2)}) collective-permute-start(bf16[192,512]{1,0:T(8,128)(2,1)S(1)} %get-tuple-element.114.o1_ref), channel_id=1, source_target_pairs={{0,3},{1,2},{2,1},{3,0},{4,7},{5,6},{6,5},{7,4},{8,11},{9,10},{10,... | collective-permute-start | bytes 589832 | tf_op jit(solution)/shard_map/ppermute | solution.py:630
  30.3 10.2 %collective-permute-start.6 = (bf16[192,512]{1,0:T(8,128)(2,1)S(1)}, bf16[192,512]{1,0:T(8,128)(2,1)S(1)}, u32[]{:S(2)}, u32[]{:S(2)}) collective-permute-start(bf16[192,512]{1,0:T(8,128)(2,1)S(1)} %get-tuple-element.110.a0.o0_ref), channel_id=1, source_target_pairs={{0,2},{1,3},{2,0},{3,1},{4,6},{5,7},{6,4},{7,5},{8,10},{9,11},{10,... | collective-permute-start | bytes 589832 | tf_op jit(solution)/shard_map/ppermute | solution.py:630
  30.7 21.1 %copy-start.7 = (bf16[768,768]{1,0:T(8,128)(2,1)}, bf16[768,768]{1,0:T(8,128)(2,1)S(1)}, u32[]{:S(2)}) copy-start(bf16[768,768]{1,0:T(8,128)(2,1)S(1)} %collective-permute-done.3.ub_ref) | copy-start | bytes 3538948
  35.3 16.4 %collective-permute-start.10 = (bf16[192,512]{1,0:T(8,128)(2,1)S(1)}, bf16[192,512]{1,0:T(8,128)(2,1)S(1)}, u32[]{:S(2)}, u32[]{:S(2)}) collective-permute-start(bf16[192,512]{1,0:T(8,128)(2,1)S(1)} %get-tuple-element.117.o1_ref), channel_id=1, source_target_pairs={{0,3},{1,2},{2,1},{3,0},{4,7},{5,6},{6,5},{7,4},{8,11},{9,10},{10,... | collective-permute-start | bytes 589832 | tf_op jit(solution)/shard_map/ppermute | solution.py:630
  36.8 15.0 %collective-permute-start.8 = (bf16[192,512]{1,0:T(8,128)(2,1)S(1)}, bf16[192,512]{1,0:T(8,128)(2,1)S(1)}, u32[]{:S(2)}, u32[]{:S(2)}) collective-permute-start(bf16[192,512]{1,0:T(8,128)(2,1)S(1)} %get-tuple-element.117.o1_ref), channel_id=1, source_target_pairs={{0,1},{1,0},{2,3},{3,2},{4,5},{5,4},{6,7},{7,6},{8,9},{9,8},{10,11... | collective-permute-start | bytes 589832 | tf_op jit(solution)/shard_map/ppermute | solution.py:630
  37.2 14.6 %collective-permute-start.9 = (bf16[192,512]{1,0:T(8,128)(2,1)S(1)}, bf16[192,512]{1,0:T(8,128)(2,1)S(1)}, u32[]{:S(2)}, u32[]{:S(2)}) collective-permute-start(bf16[192,512]{1,0:T(8,128)(2,1)S(1)} %get-tuple-element.112.a0.o0_ref), channel_id=1, source_target_pairs={{0,2},{1,3},{2,0},{3,1},{4,6},{5,7},{6,4},{7,5},{8,10},{9,11},{10,... | collective-permute-start | bytes 589832 | tf_op jit(solution)/shard_map/ppermute | solution.py:630
  49.8 20.6 %copy-start.26 = (s32[2,64]{1,0:T(2,128)S(1)}, s32[2,64]{1,0:T(2,128)}, u32[]{:S(2)}) copy-start(s32[2,64]{1,0:T(2,128)} %span_ref.3) | copy-start | bytes 1540
  49.9 20.5 %collective-permute-start.11 = (bf16[512,768]{1,0:T(8,128)(2,1)S(1)}, bf16[512,768]{1,0:T(8,128)(2,1)S(1)}, u32[]{:S(2)}, u32[]{:S(2)}) collective-permute-start(bf16[512,768]{1,0:T(8,128)(2,1)S(1)} %get-tuple-element.121), channel_id=1, source_target_pairs={{0,2},{1,3},{2,0},{3,1},{4,6},{5,7},{6,4},{7,5},{8,10},{9,11},{10,... | collective-permute-start | bytes 2359304 | tf_op jit(solution)/shard_map/ppermute | solution.py:630
  62.5 24.7 %collective-permute-start.12 = (bf16[512,768]{1,0:T(8,128)(2,1)S(1)}, bf16[512,768]{1,0:T(8,128)(2,1)S(1)}, u32[]{:S(2)}, u32[]{:S(2)}) collective-permute-start(bf16[512,768]{1,0:T(8,128)(2,1)S(1)} %get-tuple-element.132), channel_id=1, source_target_pairs={{0,2},{1,3},{2,0},{3,1},{4,6},{5,7},{6,4},{7,5},{8,10},{9,11},{10,... | collective-permute-start | bytes 2359304 | tf_op jit(solution)/shard_map/ppermute | solution.py:630
  83.3 19.3 %collective-permute-start.13 = (bf16[512,768]{1,0:T(8,128)(2,1)S(1)}, bf16[512,768]{1,0:T(8,128)(2,1)S(1)}, u32[]{:S(2)}, u32[]{:S(2)}) collective-permute-start(bf16[512,768]{1,0:T(8,128)(2,1)S(1)} %get-tuple-element.142), channel_id=1, source_target_pairs={{0,2},{1,3},{2,0},{3,1},{4,6},{5,7},{6,4},{7,5},{8,10},{9,11},{10,... | collective-permute-start | bytes 2359304 | tf_op jit(solution)/shard_map/ppermute | solution.py:630
  102.6 5.0 %collective-permute-start.15 = (bf16[768,768]{1,0:T(8,128)(2,1)S(1)}, bf16[768,768]{1,0:T(8,128)(2,1)S(1)}, u32[]{:S(2)}, u32[]{:S(2)}) collective-permute-start(bf16[768,768]{1,0:T(8,128)(2,1)S(1)} %get-tuple-element.154), channel_id=1, source_target_pairs={{0,1},{1,0},{2,3},{3,2},{4,5},{5,4},{6,7},{7,6},{8,9},{9,8},{10,11... | collective-permute-start | bytes 3538952 | tf_op jit(solution)/shard_map/ppermute | solution.py:630
  102.6 6.4 %collective-permute-start.14 = (bf16[768,768]{1,0:T(8,128)(2,1)S(1)}, bf16[768,768]{1,0:T(8,128)(2,1)S(1)}, u32[]{:S(2)}, u32[]{:S(2)}) collective-permute-start(bf16[768,768]{1,0:T(8,128)(2,1)S(1)} %get-tuple-element.152), channel_id=1, source_target_pairs={{0,1},{1,0},{2,3},{3,2},{4,5},{5,4},{6,7},{7,6},{8,9},{9,8},{10,11... | collective-permute-start | bytes 3538952 | tf_op jit(solution)/shard_map/ppermute | solution.py:630
  110.4 155.3 %all-gather.3.cloned.1.call-start = ((), (), s32[]{:S(2)}) async-start(), calls=%async_computation | async-start | bytes 4718592 | tf_op jit(solution)/shard_map/all_gather | solution.py:784
  110.5 3.3 %collective-permute-start.16 = (bf16[192,512]{1,0:T(8,128)(2,1)}, bf16[192,512]{1,0:T(8,128)(2,1)}, u32[]{:S(2)}, u32[]{:S(2)}) collective-permute-start(bf16[192,512]{1,0:T(8,128)(2,1)} %get-tuple-element.158), channel_id=1, source_target_pairs={{0,1},{1,0},{2,3},{3,2},{4,5},{5,4},{6,7},{7,6},{8,9},{9,8},{10,11... | collective-permute-start | bytes 589832 | tf_op jit(solution)/shard_map/ppermute | solution.py:630
  110.6 20.9 %collective-permute-start.17 = (bf16[512,768]{1,0:T(8,128)(2,1)}, bf16[512,768]{1,0:T(8,128)(2,1)}, u32[]{:S(2)}, u32[]{:S(2)}) collective-permute-start(bf16[512,768]{1,0:T(8,128)(2,1)} %copy-done.10), channel_id=1, source_target_pairs={{0,2},{1,3},{2,0},{3,1},{4,6},{5,7},{6,4},{7,5},{8,10},{9,11},{10,... | collective-permute-start | bytes 2359304 | tf_op jit(solution)/shard_map/ppermute | solution.py:630
  113.7 152.1 %all-gather.5.cloned.1.call-start = ((), (), s32[]{:S(2)}) async-start(), calls=%async_computation.1 | async-start | bytes 4718592 | tf_op jit(solution)/shard_map/all_gather | solution.py:784
  135.8 7.0 %collective-permute-start.20 = (bf16[192,512]{1,0:T(8,128)(2,1)S(1)}, bf16[192,512]{1,0:T(8,128)(2,1)S(1)}, u32[]{:S(2)}, u32[]{:S(2)}) collective-permute-start(bf16[192,512]{1,0:T(8,128)(2,1)S(1)} %get-tuple-element.179), channel_id=1, source_target_pairs={{0,1},{1,0},{2,3},{3,2},{4,5},{5,4},{6,7},{7,6},{8,9},{9,8},{10,11... | collective-permute-start | bytes 589832 | tf_op jit(solution)/shard_map/ppermute | solution.py:630
  142.7 15.1 %collective-permute-start.18 = (bf16[512,768]{1,0:T(8,128)(2,1)S(1)}, bf16[512,768]{1,0:T(8,128)(2,1)S(1)}, u32[]{:S(2)}, u32[]{:S(2)}) collective-permute-start(bf16[512,768]{1,0:T(8,128)(2,1)S(1)} %get-tuple-element.176), channel_id=1, source_target_pairs={{0,1},{1,0},{2,3},{3,2},{4,5},{5,4},{6,7},{7,6},{8,9},{9,8},{10,11... | collective-permute-start | bytes 2359304 | tf_op jit(solution)/shard_map/ppermute | solution.py:630
  157.2 3.6 %collective-permute-start.21 = (bf16[512,768]{1,0:T(8,128)(2,1)}, bf16[512,768]{1,0:T(8,128)(2,1)}, u32[]{:S(2)}, u32[]{:S(2)}) collective-permute-start(bf16[512,768]{1,0:T(8,128)(2,1)} %get-tuple-element.187), channel_id=1, source_target_pairs={{0,1},{1,0},{2,3},{3,2},{4,5},{5,4},{6,7},{7,6},{8,9},{9,8},{10,11... | collective-permute-start | bytes 2359304 | tf_op jit(solution)/shard_map/ppermute | solution.py:630
  157.8 5.5 %collective-permute-start.24 = (bf16[256,768]{1,0:T(8,128)(2,1)}, bf16[256,768]{1,0:T(8,128)(2,1)}, u32[]{:S(2)}, u32[]{:S(2)}) collective-permute-start(bf16[256,768]{1,0:T(8,128)(2,1)} %get-tuple-element.191), channel_id=1, source_target_pairs={{0,1},{1,0},{2,3},{3,2},{4,5},{5,4},{6,7},{7,6},{8,9},{9,8},{10,11... | collective-permute-start | bytes 1179656 | tf_op jit(solution)/shard_map/ppermute | solution.py:630
  159.8 23.1 %collective-permute-start.19 = (bf16[512,768]{1,0:T(8,128)(2,1)}, bf16[512,768]{1,0:T(8,128)(2,1)}, u32[]{:S(2)}, u32[]{:S(2)}) collective-permute-start(bf16[512,768]{1,0:T(8,128)(2,1)} %fusion), channel_id=1, source_target_pairs={{0,2},{1,3},{2,0},{3,1},{4,6},{5,7},{6,4},{7,5},{8,10},{9,11},{10,... | collective-permute-start | bytes 2359304 | tf_op jit(solution)/shard_map/ppermute | solution.py:630
  162.2 20.7 %copy-start.60 = (bf16[512,768]{1,0:T(8,128)(2,1)S(1)}, bf16[512,768]{1,0:T(8,128)(2,1)}, u32[]{:S(2)}) copy-start(bf16[512,768]{1,0:T(8,128)(2,1)} %copy-done.59) | copy-start | bytes 2359300
  162.2 34.6 %collective-permute-start.22 = (bf16[512,768]{1,0:T(8,128)(2,1)S(1)}, bf16[512,768]{1,0:T(8,128)(2,1)S(1)}, u32[]{:S(2)}, u32[]{:S(2)}) collective-permute-start(bf16[512,768]{1,0:T(8,128)(2,1)S(1)} %fusion.1), channel_id=1, source_target_pairs={{0,2},{1,3},{2,0},{3,1},{4,6},{5,7},{6,4},{7,5},{8,10},{9,11},{10,... | collective-permute-start | bytes 2359304 | tf_op jit(solution)/shard_map/ppermute | solution.py:630
  164.4 7.2 %collective-permute-start.25 = (bf16[64,768]{1,0:T(8,128)(2,1)S(1)}, bf16[64,768]{1,0:T(8,128)(2,1)S(1)}, u32[]{:S(2)}, u32[]{:S(2)}) collective-permute-start(bf16[64,768]{1,0:T(8,128)(2,1)S(1)} %get-tuple-element.213), channel_id=1, source_target_pairs={{0,8},{4,12},{8,0},{12,4},{16,24},{20,28},{24,16},{28,20},{1,9},{5... | collective-permute-start | bytes 294920 | tf_op jit(solution)/shard_map/ppermute | solution.py:633
  164.4 16.9 %collective-permute-start.26 = (bf16[64,768]{1,0:T(8,128)(2,1)S(1)}, bf16[64,768]{1,0:T(8,128)(2,1)S(1)}, u32[]{:S(2)}, u32[]{:S(2)}) collective-permute-start(bf16[64,768]{1,0:T(8,128)(2,1)S(1)} %get-tuple-element.215), channel_id=1, source_target_pairs={{0,16},{4,20},{8,24},{12,28},{16,0},{20,4},{24,8},{28,12},{1,17},{... | collective-permute-start | bytes 294920 | tf_op jit(solution)/shard_map/ppermute | solution.py:633
  169.3 12.0 %collective-permute-start.27 = (bf16[64,768]{1,0:T(8,128)(2,1)S(1)}, bf16[64,768]{1,0:T(8,128)(2,1)S(1)}, u32[]{:S(2)}, u32[]{:S(2)}) collective-permute-start(bf16[64,768]{1,0:T(8,128)(2,1)S(1)} %get-tuple-element.214), channel_id=1, source_target_pairs={{0,24},{4,28},{8,16},{12,20},{16,8},{20,12},{24,0},{28,4},{1,25},{... | collective-permute-start | bytes 294920 | tf_op jit(solution)/shard_map/ppermute | solution.py:633
  171.5 28.2 %collective-permute-start.23 = (bf16[288,768]{1,0:T(8,128)(2,1)}, bf16[288,768]{1,0:T(8,128)(2,1)}, u32[]{:S(2)}, u32[]{:S(2)}) collective-permute-start(bf16[288,768]{1,0:T(8,128)(2,1)} %constant_dynamic-slice_fusion.4), channel_id=1, source_target_pairs={{0,4},{4,0},{8,12},{12,8},{16,20},{20,16},{24,28},{28,24},{1,5},{5... | collective-permute-start | bytes 1327112 | tf_op jit(solution)/shard_map/ppermute | solution.py:633
  202.0 11.8 %collective-permute-start.31 = (bf16[32,768]{1,0:T(8,128)(2,1)S(1)}, bf16[32,768]{1,0:T(8,128)(2,1)S(1)}, u32[]{:S(2)}, u32[]{:S(2)}) collective-permute-start(bf16[32,768]{1,0:T(8,128)(2,1)S(1)} %constant_dynamic-slice_fusion), channel_id=1, source_target_pairs={{0,4},{4,0},{8,12},{12,8},{16,20},{20,16},{24,28},{28,24},{1,5},{5... | collective-permute-start | bytes 147464 | tf_op jit(solution)/shard_map/ppermute | solution.py:633
  209.3 13.0 %collective-permute-start.28 = (bf16[72,768]{1,0:T(8,128)(2,1)S(1)}, bf16[72,768]{1,0:T(8,128)(2,1)S(1)}, u32[]{:S(2)}, u32[]{:S(2)}) collective-permute-start(bf16[72,768]{1,0:T(8,128)(2,1)S(1)} %get-tuple-element.216), channel_id=1, source_target_pairs={{0,8},{4,12},{8,0},{12,4},{16,24},{20,28},{24,16},{28,20},{1,9},{5... | collective-permute-start | bytes 331784 | tf_op jit(solution)/shard_map/ppermute | solution.py:633
  209.4 15.3 %collective-permute-start.29 = (bf16[72,768]{1,0:T(8,128)(2,1)S(1)}, bf16[72,768]{1,0:T(8,128)(2,1)S(1)}, u32[]{:S(2)}, u32[]{:S(2)}) collective-permute-start(bf16[72,768]{1,0:T(8,128)(2,1)S(1)} %get-tuple-element.218), channel_id=1, source_target_pairs={{0,16},{4,20},{8,24},{12,28},{16,0},{20,4},{24,8},{28,12},{1,17},{... | collective-permute-start | bytes 331784 | tf_op jit(solution)/shard_map/ppermute | solution.py:633
  212.1 16.6 %collective-permute-start.30 = (bf16[72,768]{1,0:T(8,128)(2,1)S(1)}, bf16[72,768]{1,0:T(8,128)(2,1)S(1)}, u32[]{:S(2)}, u32[]{:S(2)}) collective-permute-start(bf16[72,768]{1,0:T(8,128)(2,1)S(1)} %get-tuple-element.217), channel_id=1, source_target_pairs={{0,24},{4,28},{8,16},{12,20},{16,8},{20,12},{24,0},{28,4},{1,25},{... | collective-permute-start | bytes 331784 | tf_op jit(solution)/shard_map/ppermute | solution.py:633
  228.7 11.3 %collective-permute-start.32 = (bf16[1,1,72,768]{3,2,1,0:T(8,128)(2,1)S(1)}, bf16[1,1,72,768]{3,2,1,0:T(8,128)(2,1)S(1)}, u32[]{:S(2)}, u32[]{:S(2)}) collective-permute-start(bf16[1,1,72,768]{3,2,1,0:T(8,128)(2,1)S(1)} %fusion.4), channel_id=1, source_target_pairs={{0,8},{4,12},{8,0},{12,4},{16,24},{20,28},{24,16},{28,20},{1,9},{5... | collective-permute-start | bytes 331784 | tf_op jit(solution)/shard_map/ppermute | solution.py:633
  233.4 10.6 %collective-permute-start.33 = (bf16[1,1,72,768]{3,2,1,0:T(8,128)(2,1)S(1)}, bf16[1,1,72,768]{3,2,1,0:T(8,128)(2,1)S(1)}, u32[]{:S(2)}, u32[]{:S(2)}) collective-permute-start(bf16[1,1,72,768]{3,2,1,0:T(8,128)(2,1)S(1)} %fusion.4), channel_id=1, source_target_pairs={{0,16},{4,20},{8,24},{12,28},{16,0},{20,4},{24,8},{28,12},{1,17},{... | collective-permute-start | bytes 331784 | tf_op jit(solution)/shard_map/ppermute | solution.py:633
  233.4 10.6 %collective-permute-start.34 = (bf16[1,1,72,768]{3,2,1,0:T(8,128)(2,1)S(1)}, bf16[1,1,72,768]{3,2,1,0:T(8,128)(2,1)S(1)}, u32[]{:S(2)}, u32[]{:S(2)}) collective-permute-start(bf16[1,1,72,768]{3,2,1,0:T(8,128)(2,1)S(1)} %fusion.4), channel_id=1, source_target_pairs={{0,24},{4,28},{8,16},{12,20},{16,8},{20,12},{24,0},{28,4},{1,25},{... | collective-permute-start | bytes 331784 | tf_op jit(solution)/shard_map/ppermute | solution.py:633
  235.9 4.1 %collective-permute-start.35 = (bf16[1,1,32,768]{3,2,1,0:T(8,128)(2,1)S(1)}, bf16[1,1,32,768]{3,2,1,0:T(8,128)(2,1)S(1)}, u32[]{:S(2)}, u32[]{:S(2)}) collective-permute-start(bf16[1,1,32,768]{3,2,1,0:T(8,128)(2,1)S(1)} %fusion.5), channel_id=1, source_target_pairs={{0,4},{4,0},{8,12},{12,8},{16,20},{20,16},{24,28},{28,24},{1,5},{5... | collective-permute-start | bytes 147464 | tf_op jit(solution)/shard_map/ppermute | solution.py:633
  244.1 5.9 %collective-permute-start.37 = (bf16[1,2,32,768]{3,2,1,0:T(8,128)(2,1)S(1)}, bf16[1,2,32,768]{3,2,1,0:T(8,128)(2,1)S(1)}, u32[]{:S(2)}, u32[]{:S(2)}) collective-permute-start(bf16[1,2,32,768]{3,2,1,0:T(8,128)(2,1)S(1)} %pad_maximum_fusion.3), channel_id=1, source_target_pairs={{0,8},{4,12},{8,0},{12,4},{16,24},{20,28},{24,16},{28,20},{1,9},{5... | collective-permute-start | bytes 294920 | tf_op jit(solution)/shard_map/ppermute | solution.py:633
  246.0 9.5 %collective-permute-start.38 = (bf16[1,2,32,768]{3,2,1,0:T(8,128)(2,1)S(1)}, bf16[1,2,32,768]{3,2,1,0:T(8,128)(2,1)S(1)}, u32[]{:S(2)}, u32[]{:S(2)}) collective-permute-start(bf16[1,2,32,768]{3,2,1,0:T(8,128)(2,1)S(1)} %pad_maximum_fusion.3), channel_id=1, source_target_pairs={{0,16},{4,20},{8,24},{12,28},{16,0},{20,4},{24,8},{28,12},{1,17},{... | collective-permute-start | bytes 294920 | tf_op jit(solution)/shard_map/ppermute | solution.py:633
  246.3 9.2 %collective-permute-start.39 = (bf16[1,2,32,768]{3,2,1,0:T(8,128)(2,1)S(1)}, bf16[1,2,32,768]{3,2,1,0:T(8,128)(2,1)S(1)}, u32[]{:S(2)}, u32[]{:S(2)}) collective-permute-start(bf16[1,2,32,768]{3,2,1,0:T(8,128)(2,1)S(1)} %pad_maximum_fusion.3), channel_id=1, source_target_pairs={{0,24},{4,28},{8,16},{12,20},{16,8},{20,12},{24,0},{28,4},{1,25},{... | collective-permute-start | bytes 294920 | tf_op jit(solution)/shard_map/ppermute | solution.py:633
  248.5 10.5 %collective-permute-start.36 = (bf16[1,4,72,768]{3,2,1,0:T(8,128)(2,1)S(1)}, bf16[1,4,72,768]{3,2,1,0:T(8,128)(2,1)S(1)}, u32[]{:S(2)}, u32[]{:S(2)}) collective-permute-start(bf16[1,4,72,768]{3,2,1,0:T(8,128)(2,1)S(1)} %constant_dynamic-update-slice_fusion.2), channel_id=1, source_target_pairs={{0,4},{4,0},{8,12},{12,8},{16,20},{20,16},{24,28},{28,24},{1,5},{5... | collective-permute-start | bytes 1327112 | tf_op jit(solution)/shard_map/ppermute | solution.py:633
  (62 other events, 470.9 us)
Sparse Core Ops, SparseCore 0:
  110.6 122.7 all-reduce.2
Sparse Core Ops, SparseCore 1:
  113.8 12.4 all-gather.2
  199.8 17.1 all-gather.4

commit v7 on v6

--- a/solution.py
+++ b/solution.py
@@ -292,13 +292,14 @@
             pltpu.VMEM((192, half), BF),
             pltpu.VMEM((192, half), BF),
         ],
-        hold=(0, 1, 2, 7),
+        hold=(-1, -2, -3, 7),
         out=(0, 1, 2),
     )
 
 
 def entry_kernel(meta_ref, x_ref, dq_ref, dk_ref, dv_ref, wq_ref, wk_ref, wv_ref, *refs):
-    before_ref = refs[0] if len(refs) == 5 else None
+    last = len(refs) == 7
+    before_ref = refs[0] if last else None
     send_ref, keep_ref, sum_ref, acc = refs[-4:]
     step = pl.program_id(0)
     x = x_ref[...]
@@ -322,15 +323,19 @@
     @pl.when(step == 0)
     def _():
         send_ref[...] = low
+        if last:
+            merged = refs[1][...].astype(F32) + refs[2][...].astype(F32)
+            sum_ref[576:, :] = merged.astype(sum_ref.dtype)
 
     @pl.when(step == 1)
     def _():
         keep_ref[...] = low
 
 
-def entry_back(meta, tokens, grads, weights, before, u, frames, dtype):
+def entry_back(meta, tokens, grads, weights, before, u, frames):
     half = frames // 2
     d = tokens.shape[1]
+    rows, dtype = (832, BF) if before else (576, F32)
     return call(
         entry_kernel,
         "entry_back",
@@ -340,9 +345,9 @@
         [pl.BlockSpec((half, d), lambda i, m: (u * 2 + (1 - i ^ m[0]), 0))]
         + [pl.BlockSpec((half, 256), lambda i, m: (1 - i ^ m[0], 0))] * 3
         + [fixed(192, d)] * 3
-        + [fixed(576, d)] * len(before),
-        [fixed(half, d), fixed(half, d), fixed(576, d)],
-        [like((half, d), BF), like((half, d), BF), like((576, d), dtype)],
+        + [fixed(*value.shape) for value in before],
+        [fixed(half, d), fixed(half, d), fixed(rows, d)],
+        [like((half, d), BF), like((half, d), BF), like((rows, d), dtype)],
         [pltpu.VMEM((576, d), F32)],
         hold=(-1, 1, 2, 3, -5, -6, -7),
     )
@@ -635,55 +640,41 @@
     def add(a, b):
         return (a.astype(F32) + b.astype(F32)).astype(BF)
 
-    def cut(array, index, count):
-        size = array.shape[0] // count
-        return lax.dynamic_slice_in_dim(array, index * size, size, 0)
-
     def total(pieces):
         return sum(piece.astype(F32) for piece in pieces).astype(BF) if len(pieces) > 1 else pieces[0]
 
-    class Chain:
-        def __init__(self, parts, order, back=None):
-            self.parts = parts
-            self.order = order
-            self.held = list(order)
-            self.steps = [(True, *stage) for stage in order] + [(False, *stage) for stage in back or reversed(order)]
+    stages = [(0, 1)] + [(b, 2) for b in range(1, bits - 1, 2)] + ([(bits - 1, 1)] if bits % 2 == 0 else [])
+
+    class Scatter:
+        def __init__(self, parts, turned):
+            shape = [1 << width for _, width in reversed(stages)]
+            self.parts = [part.reshape(*shape, -1, d) for part in parts]
+            self.turned = turned
+            self.steps = list(enumerate(stages))
+
+        def cut(self, j):
+            k, (low_bit, width) = self.steps[0]
+            flip = (1 << width) - 1 if self.turned else 0
+            spot = ((place_dp >> low_bit) & ((1 << width) - 1)) ^ flip ^ j
+            return [lax.dynamic_slice_in_dim(part, spot, 1, len(stages) - 1 - k) for part in self.parts]
 
         def start(self):
             if self.steps:
-                scatter, low_bit, width = self.steps[0]
-                count = 1 << width
-                spot = (place_dp >> low_bit) & (count - 1)
-                pick = lambda j: total([cut(part, spot ^ j, count) if scatter else part for part in self.parts])
-                self.pending = [swap_dp(pick(j), j << low_bit) for j in range(1, count)]
+                low_bit, width = self.steps[0][1]
+                self.pending = [swap_dp(total(self.cut(j)), j << low_bit) for j in range(1, 1 << width)]
 
         def finish(self, *after):
-            if not self.steps:
-                return
-            scatter, low_bit, width = self.steps.pop(0)
-            got = self.pending
-            if after:
-                got = list(lax.optimization_barrier((*got, *after))[: len(got)])
-            count = 1 << width
-            spot = (place_dp >> low_bit) & (count - 1)
-            if scatter:
-                self.state = total([cut(part, spot, count) for part in self.parts] + got)
-                if all(step[0] is False for step in self.steps):
-                    self.state = self.state.reshape((1,) * len(self.order) + self.state.shape)
-            else:
-                axis = self.order.index((low_bit, width))
-                mine = self.parts[0]
-                if count == 2:
-                    halves = [jnp.where(spot, got[0], mine), jnp.where(spot, mine, got[0])]
-                    self.state = jnp.concatenate(halves, axis=axis)
-                else:
-                    whole = jnp.zeros(mine.shape[:axis] + (count,) + mine.shape[axis + 1 :], BF)
-                    for j, piece in enumerate([mine] + got):
-                        whole = lax.dynamic_update_slice_in_dim(whole, piece, spot ^ j, axis)
-                    self.state = whole
-                if not self.steps:
-                    self.state = self.state.reshape(-1, d)
-            self.parts = (self.state,)
+            if self.steps:
+                got = self.pending
+                if after:
+                    got = list(lax.optimization_barrier((*got, *after))[: len(got)])
+                self.parts = [total(self.cut(0) + got)]
+                self.steps.pop(0)
+
+        def gather(self):
+            members = list(range(groups))[:: -1 if self.turned else 1]
+            block = self.parts[0].reshape(-1, d)
+            return lax.all_gather(block, "dp", axis=0, tiled=True, axis_index_groups=[members])
 
     scalars = jnp.concatenate([core.reshape(1), lengths])
     token = []
@@ -728,19 +719,11 @@
     def attend_step(u, grads):
         return done(attend_backward(meta(), q, k, v, grads, fwd[u][:2], fwd[u][2], u, frames))
 
-    def entry_step(u, grads, before, dtype):
-        return done(entry_back(meta(), tokens, grads, qkv_w, before, u, frames, dtype))
-
-
-    stages = [(0, 1)] + [(b, 2) for b in range(1, bits - 1, 2)] + ([(bits - 1, 1)] if bits % 2 == 0 else [])
-    inner, near, crossed, so_far, entry, spare = [], [], [], (), [], []
-
-    def together(group, *others):
-        values = lax.optimization_barrier((*(chain.state for chain in group), *others))
-        for chain, value in zip(group, values):
-            chain.state, chain.parts = value, (value,)
-        return values[len(group) :]
-
+    def entry_step(u, grads, before):
+        return done(entry_back(meta(), tokens, grads, qkv_w, before, u, frames))
+
+
+    inner, entry, so_far = [], [], ()
     for u in range(seqs):
         last = u == seqs - 1
         if u == 0:
@@ -748,9 +731,11 @@
             res, grads = inner_step(0, ())
             inner.append(res)
             far_grad.append(swap(lax.optimization_barrier((back[-1][4], res[0]))[0], 2))
-            down_sum, up_sum = total((down_own, swap(down_other, 1))), total((up_own, swap(up_other, 1)))
-            token.extend([down_sum, up_sum])
-            down_sum, up_sum = lax.psum((down_sum, up_sum), "dp")
+            up_sum = total((up_own, swap(up_other, 1)))
+            token.append(up_sum)
+            up_sum = lax.psum(up_sum, "dp")
+            down = Scatter((down_own, swap(down_other, 1)), False)
+            down.start()
         dqkv = attend_step(u, grads)
         if not last:
             before = ()
@@ -758,37 +743,43 @@
                 before = (inner[0][3], inner[0][4], inner[0][5], back[0][5], back[1][5])
             res, grads = inner_step(u + 1, before)
             inner.append(res)
-        out = entry_step(u, dqkv, so_far, BF if last else F32)
-        so_far = (out[2],)
+            down.finish(res[0])
+            down.start()
+            token.append(down.parts[0])
+        else:
+            down.finish(dqkv[0])
+            token.append(down.parts[0])
+            down.start()
+        out = entry_step(u, dqkv, so_far)
+        if not last:
+            merge_got = swap(lax.optimization_barrier((res[4], out[0]))[0], 1)
+            so_far = (out[2], res[3], merge_got)
         entry.append(out)
-    qkv = Chain((so_far[0],), stages)
-    merge = Chain((res[3], swap(lax.optimization_barrier((res[4], entry[0][0]))[0], 1)), stages[1:] + stages[:1])
+    qkv = Scatter((out[2],), True)
+    qkv.start()
+
+    ready = []
     for u in range(seqs):
         got = swap(entry[u][0], 1)
-        near.append(entry[u][1].astype(F32) + got.astype(F32))
-        crossed.append(swap(near[u].astype(BF), 2))
-    chains = [qkv, merge]
-    for chain in chains:
-        chain.start()
-    while any(chain.steps for chain in chains):
-        for chain in chains:
-            chain.finish()
-        together(chains)
-        for chain in chains:
-            chain.start()
-    merge_sum, qkv_sum = merge.state, qkv.state
-
+        crossed = swap(total((entry[u][1], got)), 2)
+        rest = entry[u][1].astype(F32) + got.astype(F32) + crossed.astype(F32)
+        ready.append((inner[u][0] + rest).astype(BF))
+    while qkv.steps or down.steps:
+        for scatter in (qkv, down):
+            scatter.finish()
+            scatter.start()
+
+    up_sum = up_sum.astype(F32)
     pairs = [[i, i + 1] for i in range(0, 4, 2)]
-
-    def both_cores(blocks):
-        whole = lax.all_gather(jnp.stack(blocks), "tensor", axis=1, tiled=True, axis_index_groups=pairs)
-        return whole.reshape(rows, d)
-
-    down_sum, up_sum = down_sum.astype(F32), up_sum.astype(F32)
-    layer_output = both_cores(list(lax.optimization_barrier((*(b[0] for b in back), inner[0][0]))[:seqs]))
-    layer_output, down_sum, up_sum = lax.optimization_barrier((layer_output, down_sum, up_sum))
-    input_grad = both_cores([(inner[u][0] + (near[u] + crossed[u].astype(F32))).astype(BF) for u in range(seqs)])
-
+    out_rows = lax.optimization_barrier((*(b[0] for b in back), inner[0][0]))[:seqs]
+    layer_output = lax.all_gather(jnp.stack(out_rows), "tensor", axis=1, tiled=True, axis_index_groups=pairs)
+    layer_output, up_sum = lax.optimization_barrier((layer_output.reshape(rows, d), up_sum))
+    down_sum = down.gather()
+    layer_output, down_sum = lax.optimization_barrier((layer_output, down_sum))
+    joint = qkv.gather()
+    down_sum, joint = lax.optimization_barrier((down_sum, joint))
+    input_grad = place(scalars, ready, [swap(r, 1) for r in ready])
+    qkv_sum, merge_sum = joint[:576], joint[576:]
     small = merge_sum[192:196].astype(F32)
     query_grad, key_grad, value_grad = (qkv_sum[192 * i : 192 * (i + 1)].astype(F32).T for i in range(3))
     return (
@@ -799,7 +790,7 @@
         value_grad,
         merge_sum[:192].astype(F32),
         up_sum,
-        down_sum,
+        down_sum.astype(F32),
         small[0],
         small[1],
         small[2],

time: 282 us -> 284 us (level)
  starting transfers between devices: 59.1 us -> 35 us
  waiting for transfers between devices: 59.2 us -> 78.7 us
  other arithmetic: 21.8 us -> 25.6 us
    ppermute x16 -> x8, starting transfers between devices: 41.6 us -> 16.7 us  [swap_dp(): return lax.ppermute(value, 'dp', [(i, i ^ k) for i in range(groups)])]
    all_gather x2 -> x3, waiting for transfers between devices: 0.01 us -> 6.58 us  [the longest x2 6.58 us: gather(): lax.all_gather(block, 'dp', axis=0, tiled=True, axis_index_groups=[members])]
    ppermute x16 -> x8, waiting for transfers between devices: 31 us -> 37.5 us  [swap_dp(): return lax.ppermute(value, 'dp', [(i, i ^ k) for i in range(groups)])]
    ppermute x24 -> x26, waiting for transfers between devices: 28.1 us -> 34.5 us  [swap(): return lax.ppermute(value, 'tensor', [(i, i ^ k) for i in range(4)])]
    convert_element_type x4 -> x5, other arithmetic: 7.02 us -> 11.4 us  [the longest x2 4.18 us: local(): ready.append((inner[u][0] + rest).astype(BF))]
    convert_element_type x5 -> x8, other arithmetic: 6.54 us -> 10.4 us  [total(): sum((piece.astype(F32) for piece in pieces)).astype(BF)]
    another operation x4 -> x1, other arithmetic: 5.85 us -> 2.42 us  [local(): jnp.stack(out_rows)]
    unnamed x136 -> x139, local copies, waits for them, and re-layouts: 18.2 us -> 19.5 us
  transfers between devices with their start and end apart: 43 -> 38, of which waited for: 12 -> 12; matrix products, arithmetic and copies ran while one was open for 8% -> 7% of each run, Pallas kernels for 37% -> 37%
where the time goes in v7:
time: 284 us; the launch traced here: 279 us
  Pallas kernels  102 us (36%)
  waiting for transfers between devices  78.7 us (28%)
  starting transfers between devices  35 us (12%)
  other arithmetic  25.6 us (9%)
  local copies, waits for them, and re-layouts  21.1 us (7%)
  between operations  16.7 us (6%)
    pallas_call x15, Pallas kernels, call(): pl.pallas_call(kernel, grid_spec=pltpu.PrefetchScalarGridSpec(num_scalar_...  102 us
    ppermute x8, waiting for transfers between devices, swap_dp(): return lax.ppermute(value, 'dp', [(i, i ^ k) for i in range(groups)])  37.5 us
    ppermute x26, waiting for transfers between devices, swap(): return lax.ppermute(value, 'tensor', [(i, i ^ k) for i in range(4)])  34.5 us
    unnamed x139, local copies, waits for them, and re-layouts  19.5 us
    ppermute x26, starting transfers between devices, swap(): return lax.ppermute(value, 'tensor', [(i, i ^ k) for i in range(4)])  18.1 us
    ppermute x8, starting transfers between devices, swap_dp(): return lax.ppermute(value, 'dp', [(i, i ^ k) for i in range(groups)])  16.7 us
    convert_element_type x8, other arithmetic, total(): sum((piece.astype(F32) for piece in pieces)).astype(BF)  10.4 us
    all_gather x2, waiting for transfers between devices, gather(): lax.all_gather(block, 'dp', axis=0, tiled=True, axis_index_groups=[members])  6.58 us
  transfers between devices with their start and end apart: 38, of which 12 were waited for; matrix products, arithmetic and copies ran while one was open for 7% of the time, Pallas kernels for 37%

profile of v7, /device:TPU:0, one launch (start us, length us, event | category | flops | bytes accessed | tf_op | source)
XLA Modules:
  0.0 279.0 jit_solution(10577248829886131887)
XLA Ops:
  8.6 2.6 collective-permute-start.1
  12.4 7.4 %project.1 = (bf16[2048,256]{1,0:T(8,128)(2,1)S(1)}, bf16[2048,256]{1,0:T(8,128)(2,1)S(1)}, bf16[2048,256]{1,0:T(8,128)(2,1)S(1)}) custom-call(s32[3]{0:T(128)S(1)} %pad_add_fusion.meta_ref, bf16[2048,768]{1,0:T(8,128)(2,1)} %x_ref.5, bf16[192,768]{1,0:T(8,128)(2,1)} %bitcast.28, bf16[192,768]{1,0:T(8,128)(2,1)} %bitcast.31, bf16[192,768]{1,0:T(8,128)(2,1)} %bitcast.34), custom_call_target="tpu_custom_call" | custom-call | flops 3300000000 | bytes 1024 | tf_op jit(solution)/shard_map/project/pallas_call | solution.py:68
  19.9 4.3 %attend_forward.2 = (bf16[192,512]{1,0:T(8,128)(2,1)S(1)}, bf16[192,512]{1,0:T(8,128)(2,1)S(1)}, f32[2,8,512]{2,1,0:T(8,128)S(1)}) custom-call(s32[3]{0:T(128)S(1)} %pad_add_fusion.meta_ref, bf16[2048,256]{1,0:T(8,128)(2,1)S(1)} %get-tuple-element.106.q_ref, bf16[2048,256]{1,0:T(8,128)(2,1)S(1)} %get-tuple-element.107.k_ref, ...), custom_call_target="tpu_custom_call" | custom-call | flops 8800000000 | bytes 1024 | tf_op jit(solution)/shard_map/attend_forward/pallas_call | solution.py:68
  25.2 1.7 collective-permute-start.7
  27.3 6.2 %attend_forward.3 = (bf16[192,512]{1,0:T(8,128)(2,1)S(1)}, bf16[192,512]{1,0:T(8,128)(2,1)S(1)}, f32[2,8,512]{2,1,0:T(8,128)S(1)}) custom-call(s32[3]{0:T(128)S(1)} %pad_add_fusion.meta_ref, bf16[2048,256]{1,0:T(8,128)(2,1)S(1)} %get-tuple-element.106.q_ref, bf16[2048,256]{1,0:T(8,128)(2,1)S(1)} %get-tuple-element.107.k_ref, ...), custom_call_target="tpu_custom_call" | custom-call | flops 8800000000 | bytes 1024 | tf_op jit(solution)/shard_map/attend_forward/pallas_call | solution.py:68
  33.5 1.5 collective-permute-start.10
  36.6 9.3 %ahead.2 = (f32[512,768]{1,0:T(8,128)S(1)}, f32[512,128]{1,0:T(8,128)S(1)}, bf16[512,768]{1,0:T(8,128)(2,1)S(1)}, bf16[512,1536]{1,0:T(8,128)(2,1)S(1)}, bf16[51...) custom-call(s32[3]{0:T(128)S(1)} %pad_add_fusion.meta_ref, bf16[2048,768]{1,0:T(8,128)(2,1)} %x_ref.5, ...), custom_call_target="tpu_custom_call" | custom-call | flops 9900000256 | bytes 1024 | tf_op jit(solution)/shard_map/ahead/pallas_call | solution.py:68
  46.0 2.1 collective-permute-start.11
  48.2 9.6 %ahead.3 = (f32[512,768]{1,0:T(8,128)S(1)}, f32[512,128]{1,0:T(8,128)S(1)}, bf16[512,768]{1,0:T(8,128)(2,1)S(1)}, bf16[512,1536]{1,0:T(8,128)(2,1)S(1)}, bf16[51...) custom-call(s32[3]{0:T(128)S(1)} %pad_add_fusion.meta_ref, bf16[2048,768]{1,0:T(8,128)(2,1)} %x_ref.5, ...), custom_call_target="tpu_custom_call" | custom-call | flops 9900000256 | bytes 1024 | tf_op jit(solution)/shard_map/ahead/pallas_call | solution.py:68
  59.0 7.6 %collective-permute-done.11.far_ref = bf16[512,768]{1,0:T(8,128)(2,1)S(1)} collective-permute-done((bf16[512,768]{1,0:T(8,128)(2,1)S(1)}, bf16[512,768]{1,0:T(8,128)(2,1)S(1)}, u32[]{:S(2)}, u32[]{:S(2)}) %collective-permute-start.11) | collective-permute-done | bytes 786464 | tf_op jit(solution)/shard_map/ppermute | solution.py:635
  66.6 8.2 %astern.2 = (bf16[512,768]{1,0:T(8,128)(2,1)S(1)}, bf16[512,768]{1,0:T(8,128)(2,1)S(1)}, bf16[512,1536]{1,0:T(8,128)(2,1)S(1)}, f32[512,768]{1,0:T(8,128)S(1)}, ...) custom-call(s32[3]{0:T(128)S(1)} %pad_add_fusion.meta_ref, f32[512,768]{1,0:T(8,128)S(1)} %get-tuple-element.119.own_ref, ...), custom_call_target="tpu_custom_call" | custom-call | flops 11000000512 | bytes 1024 | tf_op jit(solution)/shard_map/astern/pallas_call | solution.py:68
  74.8 3.2 %weight_grads.1 = (bf16[768,768]{1,0:T(8,128)(2,1)S(1)}, bf16[768,768]{1,0:T(8,128)(2,1)S(1)}, bf16[768,768]{1,0:T(8,128)(2,1)S(1)}, bf16[768,768]{1,0:T(8,128)(2,1)S(1)}) custom-call(s32[3]{0:T(128)S(1)} %pad_add_fusion.meta_ref, bf16[512,768]{1,0:T(8,128)(2,1)S(1)} %get-tuple-element.124.x_ref, bf16[512,768]{1,0:T(8,128)(2,1)S(1)} %get-tuple-element.125.g_ref, ...), custom_call_target="tpu_custom_call" | custom-call | flops 5500000256 | bytes 1024 | tf_op jit(solution)/shard_map/weight_grads/pallas_call | solution.py:68
  78.1 2.1 collective-permute-start.13
  80.2 3.2 %collective-permute-done.12.far_ref = bf16[512,768]{1,0:T(8,128)(2,1)S(1)} collective-permute-done((bf16[512,768]{1,0:T(8,128)(2,1)S(1)}, bf16[512,768]{1,0:T(8,128)(2,1)S(1)}, u32[]{:S(2)}, u32[]{:S(2)}) %collective-permute-start.12) | collective-permute-done | bytes 786464 | tf_op jit(solution)/shard_map/ppermute | solution.py:635
  83.4 12.1 %astern.3 = (bf16[512,768]{1,0:T(8,128)(2,1)S(1)}, bf16[512,768]{1,0:T(8,128)(2,1)}, bf16[512,1536]{1,0:T(8,128)(2,1)}, f32[512,768]{1,0:T(8,128)S(1)}, bf16[512...) custom-call(s32[3]{0:T(128)S(1)} %pad_add_fusion.meta_ref, ...), custom_call_target="tpu_custom_call" | custom-call | flops 11000000512 | bytes 1024 | tf_op jit(solution)/shard_map/astern/pallas_call | solution.py:68
  96.1 3.1 %collective-permute-done.13.far_ref = bf16[512,768]{1,0:T(8,128)(2,1)S(1)} collective-permute-done((bf16[512,768]{1,0:T(8,128)(2,1)S(1)}, bf16[512,768]{1,0:T(8,128)(2,1)S(1)}, u32[]{:S(2)}, u32[]{:S(2)}) %collective-permute-start.13) | collective-permute-done | bytes 786464 | tf_op jit(solution)/shard_map/ppermute | solution.py:635
  99.2 2.3 inner_norm.2
  107.1 1.7 collective-permute-start.18
  108.8 2.4 pad_maximum_fusion
  111.4 1.4 add_convert_fusion.5
  112.7 5.0 %collective-permute-start.16 = (bf16[4,1,96,768]{3,2,1,0:T(8,128)(2,1)S(1)}, bf16[4,1,96,768]{3,2,1,0:T(8,128)(2,1)S(1)}, u32[]{:S(2)}, u32[]{:S(2)}) collective-permute-start(bf16[4,1,96,768]{3,2,1,0:T(8,128)(2,1)S(1)} %add_convert_fusion.5), channel_id=1, source_target_pairs={{0,4},{4,0},{8,12},{12,8},{16,20},{20,16},{24,28},{28,24},{1,5},{5... | collective-permute-start | bytes 1769480 | tf_op jit(solution)/shard_map/ppermute | solution.py:638
  117.9 8.3 %attend_backward.2 = (bf16[1024,256]{1,0:T(8,128)(2,1)S(1)}, bf16[1024,256]{1,0:T(8,128)(2,1)S(1)}, bf16[1024,256]{1,0:T(8,128)(2,1)S(1)}) custom-call(s32[3]{0:T(128)S(1)} %pad_add_fusion.meta_ref, bf16[2048,256]{1,0:T(8,128)(2,1)} %copy-done.36, bf16[2048,256]{1,0:T(8,128)(2,1)} %copy-done.37, bf16[2048,256]{1,0:T(8,128)(2,1)} %copy-done.38, ...), custom_call_target="tpu_custom_call" | custom-call | flops 13200000000 | bytes 1024 | tf_op jit(solution)/shard_map/attend_backward/pallas_call | solution.py:68
  127.1 4.0 %inner_norm.3 = (f32[512,768]{1,0:T(8,128)S(1)}, bf16[192,512]{1,0:T(8,128)(2,1)S(1)}, bf16[192,512]{1,0:T(8,128)(2,1)S(1)}, bf16[256,768]{1,0:T(8,128)(2,1)S(1)...) custom-call(s32[3]{0:T(128)S(1)} %pad_add_fusion.meta_ref, f32[512,768]{1,0:T(8,128)S(1)} %copy-done.31, ...), custom_call_target="tpu_custom_call" | custom-call | flops 3300000000 | bytes 1024 | tf_op jit(solution)/shard_map/inner_norm/pallas_call | solution.py:68
  131.1 3.9 %collective-permute-done.16 = bf16[4,1,96,768]{3,2,1,0:T(8,128)(2,1)S(1)} collective-permute-done((bf16[4,1,96,768]{3,2,1,0:T(8,128)(2,1)S(1)}, bf16[4,1,96,768]{3,2,1,0:T(8,128)(2,1)S(1)}, u32[]{:S(2)}, u32[]{:S(2)}) %collective-permute-start.16) | collective-permute-done | bytes 589856 | tf_op jit(solution)/shard_map/ppermute | solution.py:638
  136.3 6.8 %entry_back.2 = (bf16[512,768]{1,0:T(8,128)(2,1)}, bf16[512,768]{1,0:T(8,128)(2,1)S(1)}, f32[576,768]{1,0:T(8,128)S(1)}) custom-call(s32[3]{0:T(128)S(1)} %pad_add_fusion.meta_ref, bf16[2048,768]{1,0:T(8,128)(2,1)} %x_ref.5, bf16[1024,256]{1,0:T(8,128)(2,1)S(1)} %get-tuple-element.159.dq_ref, bf16[1024,256]{1,0:T(8,128)(2,1)S(1)} %get-tuple-element.173.dk_ref, ...), custom_call_target="tpu_custom_call" | custom-call | flops 5500000256 | bytes 1024 | tf_op jit(solution)/shard_map/entry_back/pallas_call | solution.py:68
  144.4 1.6 collective-permute-start.19
  146.0 2.9 %collective-permute-start.20 = (bf16[1,1,96,768]{3,2,1,0:T(8,128)(2,1)S(1)}, bf16[1,1,96,768]{3,2,1,0:T(8,128)(2,1)S(1)}, u32[]{:S(2)}, u32[]{:S(2)}) collective-permute-start(bf16[1,1,96,768]{3,2,1,0:T(8,128)(2,1)S(1)} %get-tuple-element.212), channel_id=1, source_target_pairs={{0,16},{4,20},{8,24},{12,28},{16,0},{20,4},{24,8},{28,12},{1,17},{... | collective-permute-start | bytes 442376 | tf_op jit(solution)/shard_map/ppermute | solution.py:638
  148.9 10.0 %attend_backward.3 = (bf16[1024,256]{1,0:T(8,128)(2,1)S(1)}, bf16[1024,256]{1,0:T(8,128)(2,1)S(1)}, bf16[1024,256]{1,0:T(8,128)(2,1)S(1)}) custom-call(s32[3]{0:T(128)S(1)} %pad_add_fusion.meta_ref, bf16[2048,256]{1,0:T(8,128)(2,1)} %copy-done.36, bf16[2048,256]{1,0:T(8,128)(2,1)} %copy-done.37, bf16[2048,256]{1,0:T(8,128)(2,1)} %copy-done.38, ...), custom_call_target="tpu_custom_call" | custom-call | flops 13200000000 | bytes 1024 | tf_op jit(solution)/shard_map/attend_backward/pallas_call | solution.py:68
  162.1 1.5 copy-done.40
  167.7 6.3 %entry_back.3 = (bf16[512,768]{1,0:T(8,128)(2,1)S(1)}, bf16[512,768]{1,0:T(8,128)(2,1)S(1)}, bf16[832,768]{1,0:T(8,128)(2,1)S(1)}) custom-call(s32[3]{0:T(128)S(1)} %pad_add_fusion.meta_ref, bf16[2048,768]{1,0:T(8,128)(2,1)} %x_ref.5, bf16[1024,256]{1,0:T(8,128)(2,1)S(1)} %copy-done.48, bf16[1024,256]{1,0:T(8,128)(2,1)S(1)} %copy-done.50, ...), custom_call_target="tpu_custom_call" | custom-call | flops 5500000256 | bytes 1024 | tf_op jit(solution)/shard_map/entry_back/pallas_call | solution.py:68
  178.2 24.9 %collective-permute-done.30 = bf16[4,1,104,768]{3,2,1,0:T(8,128)(2,1)} collective-permute-done((bf16[4,1,104,768]{3,2,1,0:T(8,128)(2,1)}, bf16[4,1,104,768]{3,2,1,0:T(8,128)(2,1)}, u32[]{:S(2)}, u32[]{:S(2)}) %collective-permute-start.30) | collective-permute-done | bytes 639008 | tf_op jit(solution)/shard_map/ppermute | solution.py:638
  203.1 1.4 add_convert_fusion.3
  204.6 3.7 %collective-permute-start.31 = (bf16[1,1,104,768]{3,2,1,0:T(8,128)(2,1)S(1)}, bf16[1,1,104,768]{3,2,1,0:T(8,128)(2,1)S(1)}, u32[]{:S(2)}, u32[]{:S(2)}) collective-permute-start(bf16[1,1,104,768]{3,2,1,0:T(8,128)(2,1)S(1)} %get-tuple-element.208), channel_id=1, source_target_pairs={{0,8},{4,12},{8,0},{12,4},{16,24},{20,28},{24,16},{28,20},{1,9},{5... | collective-permute-start | bytes 479240 | tf_op jit(solution)/shard_map/ppermute | solution.py:638
  209.6 1.4 collective-permute-start.33
  211.0 2.2 fusion
  214.3 3.4 %collective-permute-done.31 = bf16[1,1,104,768]{3,2,1,0:T(8,128)(2,1)S(1)} collective-permute-done((bf16[1,1,104,768]{3,2,1,0:T(8,128)(2,1)S(1)}, bf16[1,1,104,768]{3,2,1,0:T(8,128)(2,1)S(1)}, u32[]{:S(2)}, u32[]{:S(2)}) %collective-permute-start.31) | collective-permute-done | bytes 159776 | tf_op jit(solution)/shard_map/ppermute | solution.py:638
  217.7 5.3 %collective-permute-done.32 = bf16[1,1,104,768]{3,2,1,0:T(8,128)(2,1)S(1)} collective-permute-done((bf16[1,1,104,768]{3,2,1,0:T(8,128)(2,1)S(1)}, bf16[1,1,104,768]{3,2,1,0:T(8,128)(2,1)S(1)}, u32[]{:S(2)}, u32[]{:S(2)}) %collective-permute-start.32) | collective-permute-done | bytes 159776 | tf_op jit(solution)/shard_map/ppermute | solution.py:638
  225.2 1.6 collective-permute-start.28
  226.7 7.3 %collective-permute-done.24 = bf16[512,768]{1,0:T(8,128)(2,1)} collective-permute-done((bf16[512,768]{1,0:T(8,128)(2,1)}, bf16[512,768]{1,0:T(8,128)(2,1)}, u32[]{:S(2)}, u32[]{:S(2)}) %collective-permute-start.24) | collective-permute-done | bytes 786464 | tf_op jit(solution)/shard_map/ppermute | solution.py:635
  234.0 2.6 add_convert_fusion.2.refs_0_
  236.6 11.7 %collective-permute-done.28 = bf16[512,768]{1,0:T(8,128)(2,1)S(1)} collective-permute-done((bf16[512,768]{1,0:T(8,128)(2,1)S(1)}, bf16[512,768]{1,0:T(8,128)(2,1)S(1)}, u32[]{:S(2)}, u32[]{:S(2)}) %collective-permute-start.28) | collective-permute-done | bytes 786464 | tf_op jit(solution)/shard_map/ppermute | solution.py:635
  248.3 1.6 add_convert_fusion.1.refs_2_
  250.0 2.9 %convert_element_type.121 = f32[768,768]{1,0:T(8,128)} convert(bf16[768,768]{1,0:T(8,128)(2,1)} %all-reduce.2.cloned.1.call-done) | non-fusion elementwise | flops 589824 | bytes 3538944 | tf_op jit(solution)/shard_map/convert_element_type | solution.py:772
  252.9 3.8 %place.1 = bf16[2048,768]{1,0:T(8,128)(2,1)} custom-call(s32[3]{0:T(128)S(1)} %pad_add_fusion.meta_ref, bf16[512,768]{1,0:T(8,128)(2,1)} %add_convert_fusion.2.refs_0_, bf16[512,768]{1,0:T(8,128)(2,1)S(1)} %collective-permute-done.25.refs_1_, bf16[512,768]{1,0:T(8,128)(2,1)S(1)} %add_convert_fusion.1.refs_2_, ...), custom_call_target="tpu_custom_call" | custom-call | flops 3300000000 | bytes 1024 | tf_op jit(solution)/shard_map/place/pallas_call | solution.py:68
  256.7 6.6 %all-gather.10.cloned.1.call-done = bf16[1,1,832,768]{3,2,1,0:T(8,128)(2,1)} async-done(((bf16[1,1,104,768]{3,2,1,0:T(8,128)(2,1)}), bf16[1,1,832,768]{3,2,1,0:T(8,128)(2,1)}) %all-gather.10.cloned.1.call-update) | async-done | bytes 1277968 | tf_op jit(solution)/shard_map/all_gather | solution.py:677
  263.3 2.8 slice_convert_fusion
  266.8 1.6 convert_element_type.153
  269.5 1.7 copy.28
  (211 shorter events, 33.7 us)
Async XLA Ops:
  8.0 242.0 %all-reduce.2.cloned.1.call-start = ((), (), s32[]{:S(2)}) async-start(), calls=%async_computation.1 | async-start | bytes 2359296 | tf_op jit(solution)/shard_map/psum | solution.py:736
  8.1 16.9 %collective-permute-start = (bf16[192,768]{1,0:T(8,128)(2,1)}, bf16[192,768]{1,0:T(8,128)(2,1)S(1)}, u32[]{:S(2)}, u32[]{:S(2)}) collective-permute-start(bf16[192,768]{1,0:T(8,128)(2,1)} %w0.7), channel_id=1, source_target_pairs={{0,1},{1,0},{2,3},{3,2},{4,5},{5,4},{6,7},{7,6},{8,9},{9,8},{10,11... | collective-permute-start | bytes 884744 | tf_op jit(solution)/shard_map/ppermute | solution.py:635
  8.6 16.6 %collective-permute-start.1 = (bf16[192,768]{1,0:T(8,128)(2,1)}, bf16[192,768]{1,0:T(8,128)(2,1)S(1)}, u32[]{:S(2)}, u32[]{:S(2)}) collective-permute-start(bf16[192,768]{1,0:T(8,128)(2,1)} %w0.7), channel_id=1, source_target_pairs={{0,2},{1,3},{2,0},{3,1},{4,6},{5,7},{6,4},{7,5},{8,10},{9,11},{10,... | collective-permute-start | bytes 884744 | tf_op jit(solution)/shard_map/ppermute | solution.py:635
  11.1 15.8 %collective-permute-start.2 = (bf16[192,768]{1,0:T(8,128)(2,1)}, bf16[192,768]{1,0:T(8,128)(2,1)}, u32[]{:S(2)}, u32[]{:S(2)}) collective-permute-start(bf16[192,768]{1,0:T(8,128)(2,1)} %w0.7), channel_id=1, source_target_pairs={{0,3},{1,2},{2,1},{3,0},{4,7},{5,6},{6,5},{7,4},{8,11},{9,10},{10,... | collective-permute-start | bytes 884744 | tf_op jit(solution)/shard_map/ppermute | solution.py:635
  11.2 16.1 %collective-permute-start.3 = (bf16[768,768]{1,0:T(8,128)(2,1)}, bf16[768,768]{1,0:T(8,128)(2,1)S(1)}, u32[]{:S(2)}, u32[]{:S(2)}) collective-permute-start(bf16[768,768]{1,0:T(8,128)(2,1)} %ua_ref.7), channel_id=1, source_target_pairs={{0,1},{1,0},{2,3},{3,2},{4,5},{5,4},{6,7},{7,6},{8,9},{9,8},{10,11... | collective-permute-start | bytes 3538952 | tf_op jit(solution)/shard_map/ppermute | solution.py:635
  11.4 15.9 %collective-permute-start.4 = (bf16[768,768]{1,0:T(8,128)(2,1)}, bf16[768,768]{1,0:T(8,128)(2,1)}, u32[]{:S(2)}, u32[]{:S(2)}) collective-permute-start(bf16[768,768]{1,0:T(8,128)(2,1)} %da_ref.7), channel_id=1, source_target_pairs={{0,1},{1,0},{2,3},{3,2},{4,5},{5,4},{6,7},{7,6},{8,9},{9,8},{10,11... | collective-permute-start | bytes 3538952 | tf_op jit(solution)/shard_map/ppermute | solution.py:635
  24.9 74.3 %copy-start.20 = (bf16[192,512]{1,0:T(8,128)(2,1)}, bf16[192,512]{1,0:T(8,128)(2,1)S(1)}, u32[]{:S(2)}) copy-start(bf16[192,512]{1,0:T(8,128)(2,1)S(1)} %get-tuple-element.109.a0.o0_ref) | copy-start | bytes 589828
  25.0 23.2 %copy-start.13 = (bf16[192,768]{1,0:T(8,128)(2,1)}, bf16[192,768]{1,0:T(8,128)(2,1)S(1)}, u32[]{:S(2)}) copy-start(bf16[192,768]{1,0:T(8,128)(2,1)S(1)} %collective-permute-done.w1) | copy-start | bytes 884740
  25.0 10.5 %collective-permute-start.5 = (bf16[192,512]{1,0:T(8,128)(2,1)S(1)}, bf16[192,512]{1,0:T(8,128)(2,1)S(1)}, u32[]{:S(2)}, u32[]{:S(2)}) collective-permute-start(bf16[192,512]{1,0:T(8,128)(2,1)S(1)} %get-tuple-element.113.o1_ref), channel_id=1, source_target_pairs={{0,1},{1,0},{2,3},{3,2},{4,5},{5,4},{6,7},{7,6},{8,9},{9,8},{10,11... | collective-permute-start | bytes 589832 | tf_op jit(solution)/shard_map/ppermute | solution.py:635
  25.2 11.4 %collective-permute-start.7 = (bf16[192,512]{1,0:T(8,128)(2,1)S(1)}, bf16[192,512]{1,0:T(8,128)(2,1)S(1)}, u32[]{:S(2)}, u32[]{:S(2)}) collective-permute-start(bf16[192,512]{1,0:T(8,128)(2,1)S(1)} %get-tuple-element.113.o1_ref), channel_id=1, source_target_pairs={{0,3},{1,2},{2,1},{3,0},{4,7},{5,6},{6,5},{7,4},{8,11},{9,10},{10,... | collective-permute-start | bytes 589832 | tf_op jit(solution)/shard_map/ppermute | solution.py:635
  26.9 9.7 %collective-permute-start.6 = (bf16[192,512]{1,0:T(8,128)(2,1)S(1)}, bf16[192,512]{1,0:T(8,128)(2,1)S(1)}, u32[]{:S(2)}, u32[]{:S(2)}) collective-permute-start(bf16[192,512]{1,0:T(8,128)(2,1)S(1)} %get-tuple-element.109.a0.o0_ref), channel_id=1, source_target_pairs={{0,2},{1,3},{2,0},{3,1},{4,6},{5,7},{6,4},{7,5},{8,10},{9,11},{10,... | collective-permute-start | bytes 589832 | tf_op jit(solution)/shard_map/ppermute | solution.py:635
  27.3 39.3 %copy-start.6 = (bf16[768,768]{1,0:T(8,128)(2,1)}, bf16[768,768]{1,0:T(8,128)(2,1)S(1)}, u32[]{:S(2)}) copy-start(bf16[768,768]{1,0:T(8,128)(2,1)S(1)} %collective-permute-done.3.ub_ref) | copy-start | bytes 3538948
  33.5 14.7 %copy-start.16 = (bf16[192,512]{1,0:T(8,128)(2,1)}, bf16[192,512]{1,0:T(8,128)(2,1)S(1)}, u32[]{:S(2)}) copy-start(bf16[192,512]{1,0:T(8,128)(2,1)S(1)} %get-tuple-element.111.a0.o0_ref) | copy-start | bytes 589828
  33.5 14.6 %collective-permute-start.10 = (bf16[192,512]{1,0:T(8,128)(2,1)S(1)}, bf16[192,512]{1,0:T(8,128)(2,1)S(1)}, u32[]{:S(2)}, u32[]{:S(2)}) collective-permute-start(bf16[192,512]{1,0:T(8,128)(2,1)S(1)} %get-tuple-element.116.o1_ref), channel_id=1, source_target_pairs={{0,3},{1,2},{2,1},{3,0},{4,7},{5,6},{6,5},{7,4},{8,11},{9,10},{10,... | collective-permute-start | bytes 589832 | tf_op jit(solution)/shard_map/ppermute | solution.py:635
  35.0 13.2 %collective-permute-start.8 = (bf16[192,512]{1,0:T(8,128)(2,1)S(1)}, bf16[192,512]{1,0:T(8,128)(2,1)S(1)}, u32[]{:S(2)}, u32[]{:S(2)}) collective-permute-start(bf16[192,512]{1,0:T(8,128)(2,1)S(1)} %get-tuple-element.116.o1_ref), channel_id=1, source_target_pairs={{0,1},{1,0},{2,3},{3,2},{4,5},{5,4},{6,7},{7,6},{8,9},{9,8},{10,11... | collective-permute-start | bytes 589832 | tf_op jit(solution)/shard_map/ppermute | solution.py:635
  35.5 12.7 %collective-permute-start.9 = (bf16[192,512]{1,0:T(8,128)(2,1)S(1)}, bf16[192,512]{1,0:T(8,128)(2,1)S(1)}, u32[]{:S(2)}, u32[]{:S(2)}) collective-permute-start(bf16[192,512]{1,0:T(8,128)(2,1)S(1)} %get-tuple-element.111.a0.o0_ref), channel_id=1, source_target_pairs={{0,2},{1,3},{2,0},{3,1},{4,6},{5,7},{6,4},{7,5},{8,10},{9,11},{10,... | collective-permute-start | bytes 589832 | tf_op jit(solution)/shard_map/ppermute | solution.py:635
  46.0 20.6 %copy-start.27 = (s32[2,64]{1,0:T(2,128)S(1)}, s32[2,64]{1,0:T(2,128)}, u32[]{:S(2)}) copy-start(s32[2,64]{1,0:T(2,128)} %span_ref.3) | copy-start | bytes 1540
  46.0 20.5 %collective-permute-start.11 = (bf16[512,768]{1,0:T(8,128)(2,1)S(1)}, bf16[512,768]{1,0:T(8,128)(2,1)S(1)}, u32[]{:S(2)}, u32[]{:S(2)}) collective-permute-start(bf16[512,768]{1,0:T(8,128)(2,1)S(1)} %get-tuple-element.120), channel_id=1, source_target_pairs={{0,2},{1,3},{2,0},{3,1},{4,6},{5,7},{6,4},{7,5},{8,10},{9,11},{10,... | collective-permute-start | bytes 2359304 | tf_op jit(solution)/shard_map/ppermute | solution.py:635
  58.9 15.9 %copy-start.43 = (f32[512,128]{1,0:T(8,128)}, f32[512,128]{1,0:T(8,128)S(1)}, u32[]{:S(2)}) copy-start(f32[512,128]{1,0:T(8,128)S(1)} %get-tuple-element.164.rstd_ref) | copy-start | bytes 786436
  58.9 24.5 %collective-permute-start.12 = (bf16[512,768]{1,0:T(8,128)(2,1)S(1)}, bf16[512,768]{1,0:T(8,128)(2,1)S(1)}, u32[]{:S(2)}, u32[]{:S(2)}) collective-permute-start(bf16[512,768]{1,0:T(8,128)(2,1)S(1)} %get-tuple-element.131), channel_id=1, source_target_pairs={{0,2},{1,3},{2,0},{3,1},{4,6},{5,7},{6,4},{7,5},{8,10},{9,11},{10,... | collective-permute-start | bytes 2359304 | tf_op jit(solution)/shard_map/ppermute | solution.py:635
  78.1 21.1 %collective-permute-start.13 = (bf16[512,768]{1,0:T(8,128)(2,1)S(1)}, bf16[512,768]{1,0:T(8,128)(2,1)S(1)}, u32[]{:S(2)}, u32[]{:S(2)}) collective-permute-start(bf16[512,768]{1,0:T(8,128)(2,1)S(1)} %get-tuple-element.141), channel_id=1, source_target_pairs={{0,2},{1,3},{2,0},{3,1},{4,6},{5,7},{6,4},{7,5},{8,10},{9,11},{10,... | collective-permute-start | bytes 2359304 | tf_op jit(solution)/shard_map/ppermute | solution.py:635
  83.4 15.8 %copy-start.14 = (bf16[192,768]{1,0:T(8,128)(2,1)S(1)}, bf16[192,768]{1,0:T(8,128)(2,1)}, u32[]{:S(2)}) copy-start(bf16[192,768]{1,0:T(8,128)(2,1)} %copy-done.13) | copy-start | bytes 884740
  99.2 6.0 %collective-permute-start.14 = (bf16[768,768]{1,0:T(8,128)(2,1)S(1)}, bf16[768,768]{1,0:T(8,128)(2,1)S(1)}, u32[]{:S(2)}, u32[]{:S(2)}) collective-permute-start(bf16[768,768]{1,0:T(8,128)(2,1)S(1)} %get-tuple-element.151), channel_id=1, source_target_pairs={{0,1},{1,0},{2,3},{3,2},{4,5},{5,4},{6,7},{7,6},{8,9},{9,8},{10,11... | collective-permute-start | bytes 3538952 | tf_op jit(solution)/shard_map/ppermute | solution.py:635
  106.5 146.4 %all-gather.6.cloned.1.call-start = ((), (), s32[]{:S(2)}) async-start(), calls=%async_computation | async-start | bytes 4718592 | tf_op jit(solution)/shard_map/all_gather | solution.py:775
  106.5 4.8 %collective-permute-start.15 = (bf16[768,768]{1,0:T(8,128)(2,1)}, bf16[768,768]{1,0:T(8,128)(2,1)}, u32[]{:S(2)}, u32[]{:S(2)}) collective-permute-start(bf16[768,768]{1,0:T(8,128)(2,1)} %copy-done.8), channel_id=1, source_target_pairs={{0,1},{1,0},{2,3},{3,2},{4,5},{5,4},{6,7},{7,6},{8,9},{9,8},{10,11... | collective-permute-start | bytes 3538952 | tf_op jit(solution)/shard_map/ppermute | solution.py:635
  107.1 19.9 %collective-permute-start.18 = (bf16[512,768]{1,0:T(8,128)(2,1)}, bf16[512,768]{1,0:T(8,128)(2,1)}, u32[]{:S(2)}, u32[]{:S(2)}) collective-permute-start(bf16[512,768]{1,0:T(8,128)(2,1)} %copy-done.9), channel_id=1, source_target_pairs={{0,2},{1,3},{2,0},{3,1},{4,6},{5,7},{6,4},{7,5},{8,10},{9,11},{10,... | collective-permute-start | bytes 2359304 | tf_op jit(solution)/shard_map/ppermute | solution.py:635
  108.8 8.9 %collective-permute-start.17 = (bf16[192,512]{1,0:T(8,128)(2,1)}, bf16[192,512]{1,0:T(8,128)(2,1)}, u32[]{:S(2)}, u32[]{:S(2)}) collective-permute-start(bf16[192,512]{1,0:T(8,128)(2,1)} %copy-done.26), channel_id=1, source_target_pairs={{0,1},{1,0},{2,3},{3,2},{4,5},{5,4},{6,7},{7,6},{8,9},{9,8},{10,11... | collective-permute-start | bytes 589832 | tf_op jit(solution)/shard_map/ppermute | solution.py:635
  111.3 141.6 %all-gather.8.cloned.1.call-start = ((), (), s32[]{:S(2)}) async-start(), calls=%async_computation.2 | async-start | bytes 1327104 | tf_op jit(solution)/shard_map/all_gather | solution.py:677
  112.7 22.3 %collective-permute-start.16 = (bf16[4,1,96,768]{3,2,1,0:T(8,128)(2,1)S(1)}, bf16[4,1,96,768]{3,2,1,0:T(8,128)(2,1)S(1)}, u32[]{:S(2)}, u32[]{:S(2)}) collective-permute-start(bf16[4,1,96,768]{3,2,1,0:T(8,128)(2,1)S(1)} %add_convert_fusion.5), channel_id=1, source_target_pairs={{0,4},{4,0},{8,12},{12,8},{16,20},{20,16},{24,28},{28,24},{1,5},{5... | collective-permute-start | bytes 1769480 | tf_op jit(solution)/shard_map/ppermute | solution.py:638
  131.1 17.8 %collective-permute-start.22 = (bf16[192,512]{1,0:T(8,128)(2,1)S(1)}, bf16[192,512]{1,0:T(8,128)(2,1)S(1)}, u32[]{:S(2)}, u32[]{:S(2)}) collective-permute-start(bf16[192,512]{1,0:T(8,128)(2,1)S(1)} %get-tuple-element.178), channel_id=1, source_target_pairs={{0,1},{1,0},{2,3},{3,2},{4,5},{5,4},{6,7},{7,6},{8,9},{9,8},{10,11... | collective-permute-start | bytes 589832 | tf_op jit(solution)/shard_map/ppermute | solution.py:635
  136.3 12.6 %copy-start.19 = (bf16[192,512]{1,0:T(8,128)(2,1)S(1)}, bf16[192,512]{1,0:T(8,128)(2,1)}, u32[]{:S(2)}) copy-start(bf16[192,512]{1,0:T(8,128)(2,1)} %copy-done.18) | copy-start | bytes 589828
  136.3 12.6 %copy-start.60 = (f32[2,8,512]{2,1,0:T(8,128)S(1)}, f32[2,8,512]{2,1,0:T(8,128)}, u32[]{:S(2)}) copy-start(f32[2,8,512]{2,1,0:T(8,128)} %copy-done.59) | copy-start | bytes 98308
  144.3 17.8 %collective-permute-start.26 = (bf16[256,768]{1,0:T(8,128)(2,1)S(1)}, bf16[256,768]{1,0:T(8,128)(2,1)S(1)}, u32[]{:S(2)}, u32[]{:S(2)}) collective-permute-start(bf16[256,768]{1,0:T(8,128)(2,1)S(1)} %get-tuple-element.192), channel_id=1, source_target_pairs={{0,1},{1,0},{2,3},{3,2},{4,5},{5,4},{6,7},{7,6},{8,9},{9,8},{10,11... | collective-permute-start | bytes 1179656 | tf_op jit(solution)/shard_map/ppermute | solution.py:635
  144.4 16.9 %collective-permute-start.19 = (bf16[1,1,96,768]{3,2,1,0:T(8,128)(2,1)S(1)}, bf16[1,1,96,768]{3,2,1,0:T(8,128)(2,1)S(1)}, u32[]{:S(2)}, u32[]{:S(2)}) collective-permute-start(bf16[1,1,96,768]{3,2,1,0:T(8,128)(2,1)S(1)} %get-tuple-element.213), channel_id=1, source_target_pairs={{0,8},{4,12},{8,0},{12,4},{16,24},{20,28},{24,16},{28,20},{1,9},{5... | collective-permute-start | bytes 442376 | tf_op jit(solution)/shard_map/ppermute | solution.py:638
  146.0 15.3 %collective-permute-start.20 = (bf16[1,1,96,768]{3,2,1,0:T(8,128)(2,1)S(1)}, bf16[1,1,96,768]{3,2,1,0:T(8,128)(2,1)S(1)}, u32[]{:S(2)}, u32[]{:S(2)}) collective-permute-start(bf16[1,1,96,768]{3,2,1,0:T(8,128)(2,1)S(1)} %get-tuple-element.212), channel_id=1, source_target_pairs={{0,16},{4,20},{8,24},{12,28},{16,0},{20,4},{24,8},{28,12},{1,17},{... | collective-permute-start | bytes 442376 | tf_op jit(solution)/shard_map/ppermute | solution.py:638
  148.9 12.4 %collective-permute-start.21 = (bf16[1,1,96,768]{3,2,1,0:T(8,128)(2,1)S(1)}, bf16[1,1,96,768]{3,2,1,0:T(8,128)(2,1)S(1)}, u32[]{:S(2)}, u32[]{:S(2)}) collective-permute-start(bf16[1,1,96,768]{3,2,1,0:T(8,128)(2,1)S(1)} %get-tuple-element.211), channel_id=1, source_target_pairs={{0,24},{4,28},{8,16},{12,20},{16,8},{20,12},{24,0},{28,4},{1,25},{... | collective-permute-start | bytes 442376 | tf_op jit(solution)/shard_map/ppermute | solution.py:638
  162.1 101.2 %all-gather.10.cloned.1.call-start = ((), (), s32[]{:S(2)}) async-start(), calls=%async_computation.3 | async-start | bytes 1437696 | tf_op jit(solution)/shard_map/all_gather | solution.py:677
  176.9 26.2 %collective-permute-start.30 = (bf16[4,1,104,768]{3,2,1,0:T(8,128)(2,1)}, bf16[4,1,104,768]{3,2,1,0:T(8,128)(2,1)}, u32[]{:S(2)}, u32[]{:S(2)}) collective-permute-start(bf16[4,1,104,768]{3,2,1,0:T(8,128)(2,1)} %constant_dynamic-slice_fusion.3), channel_id=1, source_target_pairs={{0,4},{4,0},{8,12},{12,8},{16,20},{20,16},{24,28},{28,24},{1,5},{5... | collective-permute-start | bytes 1916936 | tf_op jit(solution)/shard_map/ppermute | solution.py:638
  177.7 33.3 %collective-permute-start.23 = (bf16[512,768]{1,0:T(8,128)(2,1)}, bf16[512,768]{1,0:T(8,128)(2,1)}, u32[]{:S(2)}, u32[]{:S(2)}) collective-permute-start(bf16[512,768]{1,0:T(8,128)(2,1)} %get-tuple-element.175), channel_id=1, source_target_pairs={{0,1},{1,0},{2,3},{3,2},{4,5},{5,4},{6,7},{7,6},{8,9},{9,8},{10,11... | collective-permute-start | bytes 2359304 | tf_op jit(solution)/shard_map/ppermute | solution.py:635
  177.7 46.1 %collective-permute-start.27 = (bf16[512,768]{1,0:T(8,128)(2,1)}, bf16[512,768]{1,0:T(8,128)(2,1)}, u32[]{:S(2)}, u32[]{:S(2)}) collective-permute-start(bf16[512,768]{1,0:T(8,128)(2,1)} %copy-done.10), channel_id=1, source_target_pairs={{0,1},{1,0},{2,3},{3,2},{4,5},{5,4},{6,7},{7,6},{8,9},{9,8},{10,11... | collective-permute-start | bytes 2359304 | tf_op jit(solution)/shard_map/ppermute | solution.py:635
  204.6 13.2 %collective-permute-start.31 = (bf16[1,1,104,768]{3,2,1,0:T(8,128)(2,1)S(1)}, bf16[1,1,104,768]{3,2,1,0:T(8,128)(2,1)S(1)}, u32[]{:S(2)}, u32[]{:S(2)}) collective-permute-start(bf16[1,1,104,768]{3,2,1,0:T(8,128)(2,1)S(1)} %get-tuple-element.208), channel_id=1, source_target_pairs={{0,8},{4,12},{8,0},{12,4},{16,24},{20,28},{24,16},{28,20},{1,9},{5... | collective-permute-start | bytes 479240 | tf_op jit(solution)/shard_map/ppermute | solution.py:638
  208.2 14.8 %collective-permute-start.32 = (bf16[1,1,104,768]{3,2,1,0:T(8,128)(2,1)S(1)}, bf16[1,1,104,768]{3,2,1,0:T(8,128)(2,1)S(1)}, u32[]{:S(2)}, u32[]{:S(2)}) collective-permute-start(bf16[1,1,104,768]{3,2,1,0:T(8,128)(2,1)S(1)} %get-tuple-element.210), channel_id=1, source_target_pairs={{0,16},{4,20},{8,24},{12,28},{16,0},{20,4},{24,8},{28,12},{1,17},{... | collective-permute-start | bytes 479240 | tf_op jit(solution)/shard_map/ppermute | solution.py:638
  209.6 13.5 %collective-permute-start.33 = (bf16[1,1,104,768]{3,2,1,0:T(8,128)(2,1)S(1)}, bf16[1,1,104,768]{3,2,1,0:T(8,128)(2,1)S(1)}, u32[]{:S(2)}, u32[]{:S(2)}) collective-permute-start(bf16[1,1,104,768]{3,2,1,0:T(8,128)(2,1)S(1)} %get-tuple-element.209), channel_id=1, source_target_pairs={{0,24},{4,28},{8,16},{12,20},{16,8},{20,12},{24,0},{28,4},{1,25},{... | collective-permute-start | bytes 479240 | tf_op jit(solution)/shard_map/ppermute | solution.py:638
  213.2 20.8 %collective-permute-start.24 = (bf16[512,768]{1,0:T(8,128)(2,1)}, bf16[512,768]{1,0:T(8,128)(2,1)}, u32[]{:S(2)}, u32[]{:S(2)}) collective-permute-start(bf16[512,768]{1,0:T(8,128)(2,1)} %fusion), channel_id=1, source_target_pairs={{0,2},{1,3},{2,0},{3,1},{4,6},{5,7},{6,4},{7,5},{8,10},{9,11},{10,... | collective-permute-start | bytes 2359304 | tf_op jit(solution)/shard_map/ppermute | solution.py:635
  225.2 23.1 %copy-start.1 = (f32[512,768]{1,0:T(8,128)S(1)}, f32[512,768]{1,0:T(8,128)}, u32[]{:S(2)}) copy-start(f32[512,768]{1,0:T(8,128)} %copy-done) | copy-start | bytes 4718596
  225.2 23.1 %collective-permute-start.28 = (bf16[512,768]{1,0:T(8,128)(2,1)S(1)}, bf16[512,768]{1,0:T(8,128)(2,1)S(1)}, u32[]{:S(2)}, u32[]{:S(2)}) collective-permute-start(bf16[512,768]{1,0:T(8,128)(2,1)S(1)} %fusion.1), channel_id=1, source_target_pairs={{0,2},{1,3},{2,0},{3,1},{4,6},{5,7},{6,4},{7,5},{8,10},{9,11},{10,... | collective-permute-start | bytes 2359304 | tf_op jit(solution)/shard_map/ppermute | solution.py:635
  236.6 16.3 %collective-permute-start.25 = (bf16[512,768]{1,0:T(8,128)(2,1)}, bf16[512,768]{1,0:T(8,128)(2,1)S(1)}, u32[]{:S(2)}, u32[]{:S(2)}) collective-permute-start(bf16[512,768]{1,0:T(8,128)(2,1)} %add_convert_fusion.2.refs_0_), channel_id=1, source_target_pairs={{0,1},{1,0},{2,3},{3,2},{4,5},{5,4},{6,7},{7,6},{8,9},{9,8},{10,11... | collective-permute-start | bytes 2359304 | tf_op jit(solution)/shard_map/ppermute | solution.py:635
  249.9 3.0 %collective-permute-start.29 = (bf16[512,768]{1,0:T(8,128)(2,1)S(1)}, bf16[512,768]{1,0:T(8,128)(2,1)S(1)}, u32[]{:S(2)}, u32[]{:S(2)}) collective-permute-start(bf16[512,768]{1,0:T(8,128)(2,1)S(1)} %add_convert_fusion.1.refs_2_), channel_id=1, source_target_pairs={{0,1},{1,0},{2,3},{3,2},{4,5},{5,4},{6,7},{7,6},{8,9},{9,8},{10,11... | collective-permute-start | bytes 2359304 | tf_op jit(solution)/shard_map/ppermute | solution.py:635
  (59 other events, 331.8 us)
Sparse Core Ops, SparseCore 0:
  106.6 94.7 all-reduce.1
Sparse Core Ops, SparseCore 1:
  111.4 14.9 all-gather.5
  162.1 53.8 all-gather.7
  223.9 39.3 all-gather.9

commit v8 on v7

--- a/solution.py
+++ b/solution.py
@@ -96,8 +96,8 @@
         o_ref[:, 192:] = jnp.zeros((x.shape[0], HEAD_DIM), BF)
 
 
-def project(meta, tokens, weights):
-    rows, d = tokens.shape
+def project(meta, tokens, weights, u, frames):
+    rows, d = frames, tokens.shape[1]
     block = 256
     return call(
         project_kernel,
@@ -105,7 +105,7 @@
         (rows // block,),
         meta,
         (tokens, *weights),
-        [pl.BlockSpec((block, d), lambda i, m: (i, 0))] + [fixed(192, d)] * 3,
+        [pl.BlockSpec((block, d), lambda i, m: (u * (rows // block) + i, 0))] + [fixed(192, d)] * 3,
         [pl.BlockSpec((block, 256), lambda i, m: (i, 0))] * 3,
         [like((rows, 256), BF)] * 3,
         hold=(-1, -2, -3, -4),
@@ -174,9 +174,9 @@
         meta,
         (q, k, v),
         [
-            pl.BlockSpec((half, 256), lambda i, m: (u * 2 + (i ^ m[0]), 0)),
-            pl.BlockSpec((frames, 256), lambda i, m: (u, 0)),
-            pl.BlockSpec((frames, 256), lambda i, m: (u, 0)),
+            pl.BlockSpec((half, 256), lambda i, m: (i ^ m[0], 0)),
+            fixed(frames, 256),
+            fixed(frames, 256),
         ],
         [
             fixed(192, half),
@@ -270,9 +270,9 @@
         meta,
         (q, k, v, *grads, *outs, lse),
         [
-            pl.BlockSpec((half, 256), lambda i, m: (u * 2 + (i ^ m[0]), 0)),
-            pl.BlockSpec((frames, 256), lambda i, m: (u, 0)),
-            pl.BlockSpec((frames, 256), lambda i, m: (u, 0)),
+            pl.BlockSpec((half, 256), lambda i, m: (i ^ m[0], 0)),
+            fixed(frames, 256),
+            fixed(frames, 256),
             fixed(192, half),
             fixed(192, half),
             fixed(192, half),
@@ -573,7 +573,16 @@
 
 
 def inner_kernel(meta_ref, own_ref, far_ref, xhat_ref, rstd_ref, vec_ref, a0, a1, w0, w1, *refs):
-    last = len(refs) == 11
+    last, cuts = len(refs) == 11, len(refs) == 14
+    if cuts:
+        for i in range(2):
+            here, there, send, keep = refs[2 * i], refs[2 * i + 1], refs[-4 + 2 * i], refs[-3 + 2 * i]
+            half = send.shape[0]
+            bit = meta_ref[meta_ref.shape[0] - 2 + i]
+            for part, j in ((send, 1 - bit), (keep, bit)):
+                rows = pl.ds(pl.multiple_of(j * half, 128), half)
+                part[...] = (here[rows, :].astype(F32) + there[rows, :].astype(F32)).astype(BF)
+        refs = refs[4:-4]
     out_ref, g0, g1, m0, m1, small_ref = refs[-6:]
     grad = own_ref[...] + far_ref[...].astype(F32)
     xhat = xhat_ref[...]
@@ -602,23 +611,28 @@
         m1[...] = nn(a1[...], low)
 
 
-def inner_norm(meta, own, far, xhat, rstd, vectors, att, weights, before):
+def inner_norm(meta, own, far, xhat, rstd, vectors, att, weights, before=(), sums=()):
     rows, d = xhat.shape
     merge = like((256, d), BF) if before else like((192, d), F32)
+    half = like((sums[0].shape[0] // 2, d), BF) if sums else None
     return call(
         inner_kernel,
         "inner_norm",
         (1,),
         meta,
-        (own, far, xhat, rstd, vectors, *att, *weights, *before),
+        (own, far, xhat, rstd, vectors, *att, *weights, *before, *sums),
         [fixed(rows, d)] * 3
         + [fixed(rows, 128), fixed(4, d)]
         + [fixed(192, rows)] * 2
         + [fixed(192, d)] * 2
-        + ([fixed(192, d)] * 2 + [fixed(2, d)] * 3 if before else []),
-        [fixed(rows, d), fixed(192, rows), fixed(192, rows), fixed(*merge.shape), fixed(*merge.shape), fixed(2, d)],
-        [like((rows, d), F32), like((192, rows), BF), like((192, rows), BF), merge, merge, like((2, d), F32)],
+        + ([fixed(192, d)] * 2 + [fixed(2, d)] * 3 if before else [])
+        + [fixed(*value.shape) for value in sums],
+        [fixed(rows, d), fixed(192, rows), fixed(192, rows), fixed(*merge.shape), fixed(*merge.shape), fixed(2, d)]
+        + ([fixed(*half.shape)] * 4 if sums else []),
+        [like((rows, d), F32), like((192, rows), BF), like((192, rows), BF), merge, merge, like((2, d), F32)]
+        + ([half] * 4 if sums else []),
         hold=(0, 2, 3),
+        limit=20 if sums else VMEM,
     )
 
 
@@ -643,40 +657,75 @@
     def total(pieces):
         return sum(piece.astype(F32) for piece in pieces).astype(BF) if len(pieces) > 1 else pieces[0]
 
+    pairs = [(b, 1) for b in range(bits)]
     stages = [(0, 1)] + [(b, 2) for b in range(1, bits - 1, 2)] + ([(bits - 1, 1)] if bits % 2 == 0 else [])
-
-    class Scatter:
-        def __init__(self, parts, turned):
-            shape = [1 << width for _, width in reversed(stages)]
-            self.parts = [part.reshape(*shape, -1, d) for part in parts]
-            self.turned = turned
-            self.steps = list(enumerate(stages))
-
-        def cut(self, j):
-            k, (low_bit, width) = self.steps[0]
-            flip = (1 << width) - 1 if self.turned else 0
-            spot = ((place_dp >> low_bit) & ((1 << width) - 1)) ^ flip ^ j
-            return [lax.dynamic_slice_in_dim(part, spot, 1, len(stages) - 1 - k) for part in self.parts]
+    orders = (pairs, pairs[1:2] + pairs[:1] + pairs[2:])
+
+    def spot_of(stage):
+        return (place_dp >> stage[0]) & ((1 << stage[1]) - 1)
+
+    class Chain:
+        def __init__(self, parts, order, back=None, halves=None):
+            self.parts = parts
+            self.halves = halves
+            self.order = order
+            self.steps = [(True, stage) for stage in order] + [(False, stage) for stage in back or reversed(order)]
+
+        def cut(self, stage, j):
+            count = 1 << stage[1]
+            size = self.parts[0].shape[0] // count
+            return [lax.dynamic_slice_in_dim(p, (spot_of(stage) ^ j) * size, size, 0) for p in self.parts]
 
         def start(self):
             if self.steps:
-                low_bit, width = self.steps[0][1]
-                self.pending = [swap_dp(total(self.cut(j)), j << low_bit) for j in range(1, 1 << width)]
+                scatter, stage = self.steps[0]
+                others = range(1, 1 << stage[1])
+                if self.halves:
+                    sent = [self.halves[0]]
+                else:
+                    sent = [total(self.cut(stage, j)) if scatter else self.parts[0] for j in others]
+                self.pending = [swap_dp(piece, j << stage[0]) for j, piece in zip(others, sent)]
 
         def finish(self, *after):
-            if self.steps:
-                got = self.pending
-                if after:
-                    got = list(lax.optimization_barrier((*got, *after))[: len(got)])
-                self.parts = [total(self.cut(0) + got)]
-                self.steps.pop(0)
-
-        def gather(self):
-            members = list(range(groups))[:: -1 if self.turned else 1]
-            block = self.parts[0].reshape(-1, d)
-            return lax.all_gather(block, "dp", axis=0, tiled=True, axis_index_groups=[members])
-
-    scalars = jnp.concatenate([core.reshape(1), lengths])
+            if not self.steps:
+                return
+            scatter, stage = self.steps.pop(0)
+            got = self.pending
+            if after:
+                got = list(lax.optimization_barrier((*got, *after))[: len(got)])
+            if scatter:
+                state = total(([self.halves[1]] if self.halves else self.cut(stage, 0)) + got)
+                self.halves = None
+                if not self.steps[0][0]:
+                    state = state.reshape((1,) * len(self.order) + state.shape)
+            else:
+                axis = self.order.index(stage)
+                spot = spot_of(stage)
+                mine = self.parts[0]
+                if len(got) == 1:
+                    laid = [jnp.where(spot, got[0], mine), jnp.where(spot, mine, got[0])]
+                    state = jnp.concatenate(laid, axis=axis)
+                else:
+                    state = jnp.zeros(mine.shape[:axis] + (1 + len(got),) + mine.shape[axis + 1 :], BF)
+                    for j, piece in enumerate([mine] + got):
+                        state = lax.dynamic_update_slice_in_dim(state, piece, spot ^ j, axis)
+                if not self.steps:
+                    state = state.reshape(-1, d)
+            self.parts = [state]
+
+    def finish(group, *after):
+        for chain in group:
+            chain.finish(*after)
+
+    def start(group):
+        for chain in group:
+            chain.start()
+
+    def together(group):
+        for chain, value in zip(group, lax.optimization_barrier(tuple(chain.parts[0] for chain in group))):
+            chain.parts = [value]
+
+    scalars = jnp.concatenate([core.reshape(1), lengths, *(spot_of(order[0]).reshape(1) for order in orders)])
     token = []
 
     def meta():
@@ -692,13 +741,14 @@
     vectors = jnp.stack([ig, ib, og, ob])
     qkv_w = (wq.T, wk.T, wv.T)
 
-    q, k, v = project(scalars, tokens, qkv_w)
-    fwd, att = [], []
+    fwd, att, front, far = [], [], [], []
+    qkv_of = [done(project(scalars, tokens, qkv_w, 0, frames))]
     for u in range(seqs):
-        fwd.append(done(attend_forward(meta(), q, k, v, u, frames), *merge_w[1:], up_w[1], down_w[1]))
+        fwd.append(done(attend_forward(meta(), *qkv_of[u], u, frames), *(merge_w[1:] if u == 0 else ())))
         own, other = fwd[u][:2]
         att.append((own, swap(other, 1), swap(own, 2), swap(other, 3)))
-    front, far = [], []
+        if u + 1 < seqs:
+            qkv_of.append(done(project(meta(), tokens, qkv_w, u + 1, frames), up_w[1], down_w[1]))
     for u in range(seqs):
         front.append(done(ahead(meta(), tokens, att[u], merge_w, up_w, down_w, vectors, u)))
         far.append(swap(front[u][6], 2))
@@ -712,12 +762,12 @@
             far_grad.append(swap(back[u][4], 2))
             sums = done(weight_grads(meta(), front[u][2], back[u][1], front[u][3], back[u][2], sums))
 
-    def inner_step(u, before):
-        res = done(inner_norm(meta(), back[u][3], far_grad[u], front[u][0], front[u][1], vectors, att[u][:2], merge_w[:2], before))
+    def inner_step(u, **more):
+        res = done(inner_norm(meta(), back[u][3], far_grad[u], front[u][0], front[u][1], vectors, att[u][:2], merge_w[:2], **more))
         return res, (res[1], swap(res[2], 1))
 
     def attend_step(u, grads):
-        return done(attend_backward(meta(), q, k, v, grads, fwd[u][:2], fwd[u][2], u, frames))
+        return done(attend_backward(meta(), *qkv_of[u], grads, fwd[u][:2], fwd[u][2], u, frames))
 
     def entry_step(u, grads, before):
         return done(entry_back(meta(), tokens, grads, qkv_w, before, u, frames))
@@ -728,34 +778,31 @@
         last = u == seqs - 1
         if u == 0:
             up_own, up_other, down_own, down_other = lax.optimization_barrier((*back[-1][6:], far_grad[0]))[:4]
-            res, grads = inner_step(0, ())
+            sums = (down_own, swap(down_other, 1), up_own, swap(up_other, 1))
+            res, grads = inner_step(0, sums=sums)
             inner.append(res)
             far_grad.append(swap(lax.optimization_barrier((back[-1][4], res[0]))[0], 2))
-            up_sum = total((up_own, swap(up_other, 1)))
-            token.append(up_sum)
-            up_sum = lax.psum(up_sum, "dp")
-            down = Scatter((down_own, swap(down_other, 1)), False)
-            down.start()
+            ffn = [Chain(None, order, None, res[6 + 2 * i : 8 + 2 * i]) for i, order in enumerate(orders)]
+            start(ffn)
         dqkv = attend_step(u, grads)
+        finish(ffn, dqkv[0])
+        token.extend(chain.parts[0] for chain in ffn)
+        start(ffn)
         if not last:
             before = ()
             if u + 1 == seqs - 1:
                 before = (inner[0][3], inner[0][4], inner[0][5], back[0][5], back[1][5])
-            res, grads = inner_step(u + 1, before)
+            res, grads = inner_step(u + 1, before=before)
             inner.append(res)
-            down.finish(res[0])
-            down.start()
-            token.append(down.parts[0])
-        else:
-            down.finish(dqkv[0])
-            token.append(down.parts[0])
-            down.start()
         out = entry_step(u, dqkv, so_far)
+        entry.append(out)
         if not last:
             merge_got = swap(lax.optimization_barrier((res[4], out[0]))[0], 1)
             so_far = (out[2], res[3], merge_got)
-        entry.append(out)
-    qkv = Scatter((out[2],), True)
+            finish(ffn, out[0])
+            token.extend(chain.parts[0] for chain in ffn)
+            start(ffn)
+    qkv = Chain([out[2]], stages)
     qkv.start()
 
     ready = []
@@ -764,20 +811,23 @@
         crossed = swap(total((entry[u][1], got)), 2)
         rest = entry[u][1].astype(F32) + got.astype(F32) + crossed.astype(F32)
         ready.append((inner[u][0] + rest).astype(BF))
-    while qkv.steps or down.steps:
-        for scatter in (qkv, down):
-            scatter.finish()
-            scatter.start()
-
-    up_sum = up_sum.astype(F32)
-    pairs = [[i, i + 1] for i in range(0, 4, 2)]
+
+    first, second = ffn
+    finish(ffn, got)
+    for group, sending in (((qkv,), (qkv, first, second)), ((qkv, first, second), (qkv, first)), ((qkv, first), (qkv, second))):
+        finish(group)
+        together([qkv, first, second])
+        start(sending)
+    finish([qkv, second])
+    while qkv.steps or first.steps or second.steps:
+        start([qkv, first, second])
+        finish([qkv, first, second])
+        together([qkv, first, second])
+    down_sum, up_sum, joint = (chain.parts[0] for chain in ffn + [qkv])
+    chips = [[i, i + 1] for i in range(0, 4, 2)]
     out_rows = lax.optimization_barrier((*(b[0] for b in back), inner[0][0]))[:seqs]
-    layer_output = lax.all_gather(jnp.stack(out_rows), "tensor", axis=1, tiled=True, axis_index_groups=pairs)
-    layer_output, up_sum = lax.optimization_barrier((layer_output.reshape(rows, d), up_sum))
-    down_sum = down.gather()
-    layer_output, down_sum = lax.optimization_barrier((layer_output, down_sum))
-    joint = qkv.gather()
-    down_sum, joint = lax.optimization_barrier((down_sum, joint))
+    layer_output = lax.all_gather(jnp.stack(out_rows), "tensor", axis=1, tiled=True, axis_index_groups=chips)
+    layer_output = layer_output.reshape(rows, d)
     input_grad = place(scalars, ready, [swap(r, 1) for r in ready])
     qkv_sum, merge_sum = joint[:576], joint[576:]
     small = merge_sum[192:196].astype(F32)
@@ -789,7 +839,7 @@
         key_grad,
         value_grad,
         merge_sum[:192].astype(F32),
-        up_sum,
+        up_sum.astype(F32),
         down_sum.astype(F32),
         small[0],
         small[1],

time: 284 us -> 279 us (0.982)
  starting transfers between devices: 35 us -> 49 us
  waiting for transfers between devices: 78.7 us -> 65.2 us
  other arithmetic: 25.6 us -> 18.6 us
  Pallas kernels: 102 us -> 107 us
    ppermute x26, waiting for transfers between devices: 34.5 us -> 19.2 us  [swap(): return lax.ppermute(value, 'tensor', [(i, i ^ k) for i in range(4)])]
    ppermute x8 -> x20, starting transfers between devices: 16.7 us -> 30.9 us  [swap_dp(): return lax.ppermute(value, 'dp', [(i, i ^ k) for i in range(groups)])]
    ppermute x8 -> x20, waiting for transfers between devices: 37.5 us -> 45.9 us  [swap_dp(): return lax.ppermute(value, 'dp', [(i, i ^ k) for i in range(groups)])]
    convert_element_type x8 -> x6, other arithmetic: 10.4 us -> 3.41 us  [total(): sum((piece.astype(F32) for piece in pieces)).astype(BF)]
    all_gather x2 -> x0, waiting for transfers between devices: 6.58 us -> none  [gather(): lax.all_gather(block, 'dp', axis=0, tiled=True, axis_index_groups=[members])]
    pallas_call x15 -> x16, Pallas kernels: 102 us -> 107 us  [call(): pl.pallas_call(kernel, grid_spec=pltpu.PrefetchScalarGridSpec(num_scalar_...]
    unnamed x139 -> x119, local copies, waits for them, and re-layouts: 19.5 us -> 15.2 us
  transfers between devices with their start and end apart: 38 -> 47, of which waited for: 12 -> 17; matrix products, arithmetic and copies ran while one was open for 7% -> 8% of each run, Pallas kernels for 37% -> 33%
where the time goes in v8:
time: 279 us; the launch traced here: 275 us
  Pallas kernels  107 us (38%)
  waiting for transfers between devices  65.2 us (23%)
  starting transfers between devices  49 us (18%)
  local copies, waits for them, and re-layouts  20.4 us (7%)
  other arithmetic  18.6 us (7%)
  between operations  15.4 us (6%)
    pallas_call x16, Pallas kernels, call(): pl.pallas_call(kernel, grid_spec=pltpu.PrefetchScalarGridSpec(num_scalar_...  107 us
    ppermute x20, waiting for transfers between devices, swap_dp(): return lax.ppermute(value, 'dp', [(i, i ^ k) for i in range(groups)])  45.9 us
    ppermute x20, starting transfers between devices, swap_dp(): return lax.ppermute(value, 'dp', [(i, i ^ k) for i in range(groups)])  30.9 us
    ppermute x26, waiting for transfers between devices, swap(): return lax.ppermute(value, 'tensor', [(i, i ^ k) for i in range(4)])  19.2 us
    ppermute x26, starting transfers between devices, swap(): return lax.ppermute(value, 'tensor', [(i, i ^ k) for i in range(4)])  18 us
    unnamed x119, local copies, waits for them, and re-layouts  15.2 us
  transfers between devices with their start and end apart: 47, of which 17 were waited for; matrix products, arithmetic and copies ran while one was open for 8% of the time, Pallas kernels for 33%

profile of v8, /device:TPU:0, one launch (start us, length us, event | category | flops | bytes accessed | tf_op | source)
XLA Modules:
  0.0 275.4 jit_solution(3462680235353562352)
XLA Ops:
  7.7 2.6 collective-permute-start.1
  11.6 4.3 %project.2 = (bf16[1024,256]{1,0:T(8,128)(2,1)S(1)}, bf16[1024,256]{1,0:T(8,128)(2,1)S(1)}, bf16[1024,256]{1,0:T(8,128)(2,1)S(1)}) custom-call(s32[5]{0:T(128)S(1)} %pad_add_fusion.meta_ref, bf16[2048,768]{1,0:T(8,128)(2,1)} %x_ref.7, bf16[192,768]{1,0:T(8,128)(2,1)} %bitcast.32, bf16[192,768]{1,0:T(8,128)(2,1)} %bitcast.36, bf16[192,768]{1,0:T(8,128)(2,1)} %bitcast.40), custom_call_target="tpu_custom_call" | custom-call | flops 3300000000 | bytes 1024 | tf_op jit(solution)/shard_map/project/pallas_call | solution.py:68
  16.0 6.0 %attend_forward.2 = (bf16[192,512]{1,0:T(8,128)(2,1)S(1)}, bf16[192,512]{1,0:T(8,128)(2,1)S(1)}, f32[2,8,512]{2,1,0:T(8,128)S(1)}) custom-call(s32[5]{0:T(128)S(1)} %pad_add_fusion.meta_ref, bf16[1024,256]{1,0:T(8,128)(2,1)S(1)} %get-tuple-element.122.q_ref, bf16[1024,256]{1,0:T(8,128)(2,1)S(1)} %get-tuple-element.124.k_ref, ...), custom_call_target="tpu_custom_call" | custom-call | flops 8800000000 | bytes 1024 | tf_op jit(solution)/shard_map/attend_forward/pallas_call | solution.py:68
  24.0 1.7 collective-permute-start.7
  26.0 4.4 %project.3 = (bf16[1024,256]{1,0:T(8,128)(2,1)S(1)}, bf16[1024,256]{1,0:T(8,128)(2,1)S(1)}, bf16[1024,256]{1,0:T(8,128)(2,1)S(1)}) custom-call(s32[5]{0:T(128)S(1)} %pad_add_fusion.meta_ref, bf16[2048,768]{1,0:T(8,128)(2,1)} %x_ref.7, bf16[192,768]{1,0:T(8,128)(2,1)} %bitcast.33, bf16[192,768]{1,0:T(8,128)(2,1)} %bitcast.37, bf16[192,768]{1,0:T(8,128)(2,1)} %bitcast.41), custom_call_target="tpu_custom_call" | custom-call | flops 3300000000 | bytes 1024 | tf_op jit(solution)/shard_map/project/pallas_call | solution.py:68
  30.5 6.5 %attend_forward.3 = (bf16[192,512]{1,0:T(8,128)(2,1)S(1)}, bf16[192,512]{1,0:T(8,128)(2,1)S(1)}, f32[2,8,512]{2,1,0:T(8,128)S(1)}) custom-call(s32[5]{0:T(128)S(1)} %pad_add_fusion.meta_ref, bf16[1024,256]{1,0:T(8,128)(2,1)S(1)} %get-tuple-element.128.q_ref, bf16[1024,256]{1,0:T(8,128)(2,1)S(1)} %get-tuple-element.130.k_ref, ...), custom_call_target="tpu_custom_call" | custom-call | flops 8800000000 | bytes 1024 | tf_op jit(solution)/shard_map/attend_forward/pallas_call | solution.py:68
  39.3 9.1 %ahead.2 = (f32[512,768]{1,0:T(8,128)S(1)}, f32[512,128]{1,0:T(8,128)S(1)}, bf16[512,768]{1,0:T(8,128)(2,1)S(1)}, bf16[512,1536]{1,0:T(8,128)(2,1)S(1)}, bf16[51...) custom-call(s32[5]{0:T(128)S(1)} %pad_add_fusion.meta_ref, bf16[2048,768]{1,0:T(8,128)(2,1)} %x_ref.7, ...), custom_call_target="tpu_custom_call" | custom-call | flops 9900000256 | bytes 1024 | tf_op jit(solution)/shard_map/ahead/pallas_call | solution.py:68
  48.4 1.8 collective-permute-start.11
  50.2 9.2 %ahead.3 = (f32[512,768]{1,0:T(8,128)S(1)}, f32[512,128]{1,0:T(8,128)S(1)}, bf16[512,768]{1,0:T(8,128)(2,1)S(1)}, bf16[512,1536]{1,0:T(8,128)(2,1)S(1)}, bf16[51...) custom-call(s32[5]{0:T(128)S(1)} %pad_add_fusion.meta_ref, bf16[2048,768]{1,0:T(8,128)(2,1)} %x_ref.7, ...), custom_call_target="tpu_custom_call" | custom-call | flops 9900000256 | bytes 1024 | tf_op jit(solution)/shard_map/ahead/pallas_call | solution.py:68
  60.9 8.0 %collective-permute-done.11.far_ref = bf16[512,768]{1,0:T(8,128)(2,1)S(1)} collective-permute-done((bf16[512,768]{1,0:T(8,128)(2,1)S(1)}, bf16[512,768]{1,0:T(8,128)(2,1)S(1)}, u32[]{:S(2)}, u32[]{:S(2)}) %collective-permute-start.11) | collective-permute-done | bytes 786464 | tf_op jit(solution)/shard_map/ppermute | solution.py:649
  68.9 8.0 %astern.2 = (bf16[512,768]{1,0:T(8,128)(2,1)S(1)}, bf16[512,768]{1,0:T(8,128)(2,1)S(1)}, bf16[512,1536]{1,0:T(8,128)(2,1)S(1)}, f32[512,768]{1,0:T(8,128)S(1)}, ...) custom-call(s32[5]{0:T(128)S(1)} %pad_add_fusion.meta_ref, f32[512,768]{1,0:T(8,128)S(1)} %get-tuple-element.140.own_ref, ...), custom_call_target="tpu_custom_call" | custom-call | flops 11000000512 | bytes 1024 | tf_op jit(solution)/shard_map/astern/pallas_call | solution.py:68
  76.9 3.2 %weight_grads.1 = (bf16[768,768]{1,0:T(8,128)(2,1)S(1)}, bf16[768,768]{1,0:T(8,128)(2,1)S(1)}, bf16[768,768]{1,0:T(8,128)(2,1)S(1)}, bf16[768,768]{1,0:T(8,128)(2,1)S(1)}) custom-call(s32[5]{0:T(128)S(1)} %pad_add_fusion.meta_ref, bf16[512,768]{1,0:T(8,128)(2,1)S(1)} %get-tuple-element.145.x_ref, bf16[512,768]{1,0:T(8,128)(2,1)S(1)} %get-tuple-element.146.g_ref, ...), custom_call_target="tpu_custom_call" | custom-call | flops 5500000256 | bytes 1024 | tf_op jit(solution)/shard_map/weight_grads/pallas_call | solution.py:68
  80.1 1.8 collective-permute-start.13
  81.9 3.8 %collective-permute-done.12.far_ref = bf16[512,768]{1,0:T(8,128)(2,1)S(1)} collective-permute-done((bf16[512,768]{1,0:T(8,128)(2,1)S(1)}, bf16[512,768]{1,0:T(8,128)(2,1)S(1)}, u32[]{:S(2)}, u32[]{:S(2)}) %collective-permute-start.12) | collective-permute-done | bytes 786464 | tf_op jit(solution)/shard_map/ppermute | solution.py:649
  85.7 11.7 %astern.3 = (bf16[512,768]{1,0:T(8,128)(2,1)S(1)}, bf16[512,768]{1,0:T(8,128)(2,1)}, bf16[512,1536]{1,0:T(8,128)(2,1)}, f32[512,768]{1,0:T(8,128)S(1)}, bf16[512...) custom-call(s32[5]{0:T(128)S(1)} %pad_add_fusion.meta_ref, ...), custom_call_target="tpu_custom_call" | custom-call | flops 11000000512 | bytes 1024 | tf_op jit(solution)/shard_map/astern/pallas_call | solution.py:68
  98.0 3.4 %collective-permute-done.13.far_ref = bf16[512,768]{1,0:T(8,128)(2,1)S(1)} collective-permute-done((bf16[512,768]{1,0:T(8,128)(2,1)S(1)}, bf16[512,768]{1,0:T(8,128)(2,1)S(1)}, u32[]{:S(2)}, u32[]{:S(2)}) %collective-permute-start.13) | collective-permute-done | bytes 786464 | tf_op jit(solution)/shard_map/ppermute | solution.py:649
  102.0 2.3 collective-permute-done.14.refs_1_
  104.3 1.7 collective-permute-done.15.refs_3_
  106.0 4.1 %inner_norm.2 = (f32[512,768]{1,0:T(8,128)S(1)}, bf16[192,512]{1,0:T(8,128)(2,1)S(1)}, bf16[192,512]{1,0:T(8,128)(2,1)}, f32[192,768]{1,0:T(8,128)S(1)}, f32[192...) custom-call(s32[5]{0:T(128)S(1)} %pad_add_fusion.meta_ref, ...), custom_call_target="tpu_custom_call" | custom-call | flops 3300000000 | bytes 1024 | tf_op jit(solution)/shard_map/inner_norm/pallas_call | solution.py:68
  114.7 1.6 collective-permute-start.19
  116.4 5.0 %collective-permute-start.18 = (bf16[384,768]{1,0:T(8,128)(2,1)}, bf16[384,768]{1,0:T(8,128)(2,1)S(1)}, u32[]{:S(2)}, u32[]{:S(2)}) collective-permute-start(bf16[384,768]{1,0:T(8,128)(2,1)} %copy-done.9), channel_id=1, source_target_pairs={{0,8},{4,12},{8,0},{12,4},{16,24},{20,28},{24,16},{28,20},{1,9},{5... | collective-permute-start | bytes 1769480 | tf_op jit(solution)/shard_map/ppermute | solution.py:652
  126.4 10.0 %attend_backward.2 = (bf16[1024,256]{1,0:T(8,128)(2,1)S(1)}, bf16[1024,256]{1,0:T(8,128)(2,1)S(1)}, bf16[1024,256]{1,0:T(8,128)(2,1)S(1)}) custom-call(s32[5]{0:T(128)S(1)} %pad_add_fusion.meta_ref, bf16[1024,256]{1,0:T(8,128)(2,1)} %copy-done.39, bf16[1024,256]{1,0:T(8,128)(2,1)} %copy-done.40, bf16[1024,256]{1,0:T(8,128)(2,1)} %copy-done.41, ...), custom_call_target="tpu_custom_call" | custom-call | flops 13200000000 | bytes 1024 | tf_op jit(solution)/shard_map/attend_backward/pallas_call | solution.py:68
  137.1 2.8 %collective-permute-start.23 = (bf16[192,768]{1,0:T(8,128)(2,1)S(1)}, bf16[192,768]{1,0:T(8,128)(2,1)S(1)}, u32[]{:S(2)}, u32[]{:S(2)}) collective-permute-start(bf16[192,768]{1,0:T(8,128)(2,1)S(1)} %constant_dynamic-slice_fusion.7), channel_id=1, source_target_pairs={{0,8},{4,12},{8,0},{12,4},{16,24},{20,28},{24,16},{28,20},{1,9},{5... | collective-permute-start | bytes 884744 | tf_op jit(solution)/shard_map/ppermute | solution.py:652
  140.1 3.0 %inner_norm.3 = (f32[512,768]{1,0:T(8,128)S(1)}, bf16[192,512]{1,0:T(8,128)(2,1)S(1)}, bf16[192,512]{1,0:T(8,128)(2,1)S(1)}, bf16[256,768]{1,0:T(8,128)(2,1)S(1)...) custom-call(s32[5]{0:T(128)S(1)} %pad_add_fusion.meta_ref, f32[512,768]{1,0:T(8,128)S(1)} %copy-done.33, ...), custom_call_target="tpu_custom_call" | custom-call | flops 3300000000 | bytes 1024 | tf_op jit(solution)/shard_map/inner_norm/pallas_call | solution.py:68
  143.1 6.2 %entry_back.2 = (bf16[512,768]{1,0:T(8,128)(2,1)S(1)}, bf16[512,768]{1,0:T(8,128)(2,1)S(1)}, f32[576,768]{1,0:T(8,128)S(1)}) custom-call(s32[5]{0:T(128)S(1)} %pad_add_fusion.meta_ref, bf16[2048,768]{1,0:T(8,128)(2,1)} %x_ref.7, bf16[1024,256]{1,0:T(8,128)(2,1)S(1)} %get-tuple-element.179.dq_ref, bf16[1024,256]{1,0:T(8,128)(2,1)S(1)} %get-tuple-element.198.dk_ref, ...), custom_call_target="tpu_custom_call" | custom-call | flops 5500000256 | bytes 1024 | tf_op jit(solution)/shard_map/entry_back/pallas_call | solution.py:68
  151.1 3.0 %collective-permute-start.26 = (bf16[96,768]{1,0:T(8,128)(2,1)S(1)}, bf16[96,768]{1,0:T(8,128)(2,1)S(1)}, u32[]{:S(2)}, u32[]{:S(2)}) collective-permute-start(bf16[96,768]{1,0:T(8,128)(2,1)S(1)} %constant_dynamic-slice_fusion.5), channel_id=1, source_target_pairs={{0,16},{4,20},{8,24},{12,28},{16,0},{20,4},{24,8},{28,12},{1,17},{... | collective-permute-start | bytes 442376 | tf_op jit(solution)/shard_map/ppermute | solution.py:652
  154.0 10.0 %attend_backward.3 = (bf16[1024,256]{1,0:T(8,128)(2,1)S(1)}, bf16[1024,256]{1,0:T(8,128)(2,1)S(1)}, bf16[1024,256]{1,0:T(8,128)(2,1)S(1)}) custom-call(s32[5]{0:T(128)S(1)} %pad_add_fusion.meta_ref, bf16[1024,256]{1,0:T(8,128)(2,1)} %copy-done.36, bf16[1024,256]{1,0:T(8,128)(2,1)} %copy-done.37, bf16[1024,256]{1,0:T(8,128)(2,1)} %copy-done.38, ...), custom_call_target="tpu_custom_call" | custom-call | flops 13200000000 | bytes 1024 | tf_op jit(solution)/shard_map/attend_backward/pallas_call | solution.py:68
  164.9 2.2 collective-permute-done.26
  167.3 7.0 %entry_back.3 = (bf16[512,768]{1,0:T(8,128)(2,1)}, bf16[512,768]{1,0:T(8,128)(2,1)S(1)}, bf16[832,768]{1,0:T(8,128)(2,1)S(1)}) custom-call(s32[5]{0:T(128)S(1)} %pad_add_fusion.meta_ref, bf16[2048,768]{1,0:T(8,128)(2,1)} %x_ref.7, bf16[1024,256]{1,0:T(8,128)(2,1)S(1)} %get-tuple-element.208.dq_ref, bf16[1024,256]{1,0:T(8,128)(2,1)S(1)} %get-tuple-element.212.dk_ref, ...), custom_call_target="tpu_custom_call" | custom-call | flops 5500000256 | bytes 1024 | tf_op jit(solution)/shard_map/entry_back/pallas_call | solution.py:68
  177.7 2.7 pad_maximum_fusion
  180.9 2.9 %collective-permute-start.33 = (bf16[1,1,1,96,768]{4,3,2,1,0:T(8,128)(2,1)S(1)}, bf16[1,1,1,96,768]{4,3,2,1,0:T(8,128)(2,1)S(1)}, u32[]{:S(2)}, u32[]{:S(2)}) collective-permute-start(bf16[1,1,1,96,768]{4,3,2,1,0:T(8,128)(2,1)S(1)} %fusion.3), channel_id=1, source_target_pairs={{0,16},{4,20},{8,24},{12,28},{16,0},{20,4},{24,8},{28,12},{1,17},{... | collective-permute-start | bytes 442376 | tf_op jit(solution)/shard_map/ppermute | solution.py:652
  183.8 8.7 %collective-permute-done.32 = bf16[416,768]{1,0:T(8,128)(2,1)} collective-permute-done((bf16[416,768]{1,0:T(8,128)(2,1)}, bf16[416,768]{1,0:T(8,128)(2,1)}, u32[]{:S(2)}, u32[]{:S(2)}) %collective-permute-start.32) | collective-permute-done | bytes 639008 | tf_op jit(solution)/shard_map/ppermute | solution.py:652
  194.0 2.4 collective-permute-done.33
  198.0 1.7 collective-permute-start.36
  199.7 2.6 collective-permute-start.37
  205.2 7.5 %collective-permute-done.36 = bf16[104,768]{1,0:T(8,128)(2,1)S(1)} collective-permute-done((bf16[104,768]{1,0:T(8,128)(2,1)S(1)}, bf16[104,768]{1,0:T(8,128)(2,1)S(1)}, u32[]{:S(2)}, u32[]{:S(2)}) %collective-permute-start.36) | collective-permute-done | bytes 159776 | tf_op jit(solution)/shard_map/ppermute | solution.py:652
  213.8 3.5 %collective-permute-done.38 = bf16[1,1,2,96,768]{4,3,2,1,0:T(8,128)(2,1)S(1)} collective-permute-done((bf16[1,1,2,96,768]{4,3,2,1,0:T(8,128)(2,1)S(1)}, bf16[1,1,2,96,768]{4,3,2,1,0:T(8,128)(2,1)S(1)}, u32[]{:S(2)}, u32[]{:S(2)}) %collective-permute-start.38) | collective-permute-done | bytes 294944 | tf_op jit(solution)/shard_map/ppermute | solution.py:652
  220.8 1.9 collective-permute-start.41
  225.1 1.6 collective-permute-start.42
  227.4 7.8 %collective-permute-done.41 = bf16[1,1,104,768]{3,2,1,0:T(8,128)(2,1)S(1)} collective-permute-done((bf16[1,1,104,768]{3,2,1,0:T(8,128)(2,1)S(1)}, bf16[1,1,104,768]{3,2,1,0:T(8,128)(2,1)S(1)}, u32[]{:S(2)}, u32[]{:S(2)}) %collective-permute-start.41) | collective-permute-done | bytes 159776 | tf_op jit(solution)/shard_map/ppermute | solution.py:652
  236.8 2.1 collective-permute-start.45
  240.2 1.6 add_convert_fusion.refs_2_
  243.8 1.6 convert_element_type.169
  245.4 6.1 %collective-permute-done.45 = bf16[1,2,2,96,768]{4,3,2,1,0:T(8,128)(2,1)} collective-permute-done((bf16[1,2,2,96,768]{4,3,2,1,0:T(8,128)(2,1)}, bf16[1,2,2,96,768]{4,3,2,1,0:T(8,128)(2,1)}, u32[]{:S(2)}, u32[]{:S(2)}) %collective-permute-start.45) | collective-permute-done | bytes 589856 | tf_op jit(solution)/shard_map/ppermute | solution.py:652
  252.9 1.7 bitcast_convert_fusion
  254.6 4.3 %collective-permute-done.44 = bf16[1,4,104,768]{3,2,1,0:T(8,128)(2,1)S(1)} collective-permute-done((bf16[1,4,104,768]{3,2,1,0:T(8,128)(2,1)}, bf16[1,4,104,768]{3,2,1,0:T(8,128)(2,1)S(1)}, u32[]{:S(2)}, u32[]{:S(2)}) %collective-permute-start.44) | collective-permute-done | bytes 639008 | tf_op jit(solution)/shard_map/ppermute | solution.py:652
  262.3 4.1 %place.1 = bf16[2048,768]{1,0:T(8,128)(2,1)} custom-call(s32[5]{0:T(128)S(1)} %pad_add_fusion.meta_ref, bf16[512,768]{1,0:T(8,128)(2,1)} %add_convert_fusion.1.refs_0_, bf16[512,768]{1,0:T(8,128)(2,1)S(1)} %collective-permute-done.22.refs_1_, bf16[512,768]{1,0:T(8,128)(2,1)S(1)} %add_convert_fusion.refs_2_, bf16[512,768]{1,0:T(8,128)(2,1)S(1)} %collective-permute-done.31.refs_3_), custom_call_target="tpu_custom_call" | custom-call | flops 3300000000 | bytes 1024 | tf_op jit(solution)/shard_map/place/pallas_call | solution.py:68
  266.4 1.7 copy.31
  (230 shorter events, 49.2 us)
Async XLA Ops:
  7.2 238.2 %all-gather.2.cloned.1.call-start = ((), (), s32[]{:S(2)}) async-start(), calls=%async_computation | async-start | bytes 4718592 | tf_op jit(solution)/shard_map/all_gather | solution.py:829
  7.2 16.6 %collective-permute-start = (bf16[192,768]{1,0:T(8,128)(2,1)}, bf16[192,768]{1,0:T(8,128)(2,1)S(1)}, u32[]{:S(2)}, u32[]{:S(2)}) collective-permute-start(bf16[192,768]{1,0:T(8,128)(2,1)} %w0.7), channel_id=1, source_target_pairs={{0,1},{1,0},{2,3},{3,2},{4,5},{5,4},{6,7},{7,6},{8,9},{9,8},{10,11... | collective-permute-start | bytes 884744 | tf_op jit(solution)/shard_map/ppermute | solution.py:649
  7.7 16.3 %collective-permute-start.1 = (bf16[192,768]{1,0:T(8,128)(2,1)}, bf16[192,768]{1,0:T(8,128)(2,1)S(1)}, u32[]{:S(2)}, u32[]{:S(2)}) collective-permute-start(bf16[192,768]{1,0:T(8,128)(2,1)} %w0.7), channel_id=1, source_target_pairs={{0,2},{1,3},{2,0},{3,1},{4,6},{5,7},{6,4},{7,5},{8,10},{9,11},{10,... | collective-permute-start | bytes 884744 | tf_op jit(solution)/shard_map/ppermute | solution.py:649
  10.3 15.4 %collective-permute-start.2 = (bf16[192,768]{1,0:T(8,128)(2,1)}, bf16[192,768]{1,0:T(8,128)(2,1)}, u32[]{:S(2)}, u32[]{:S(2)}) collective-permute-start(bf16[192,768]{1,0:T(8,128)(2,1)} %w0.7), channel_id=1, source_target_pairs={{0,3},{1,2},{2,1},{3,0},{4,7},{5,6},{6,5},{7,4},{8,11},{9,10},{10,... | collective-permute-start | bytes 884744 | tf_op jit(solution)/shard_map/ppermute | solution.py:649
  10.4 20.1 %collective-permute-start.3 = (bf16[768,768]{1,0:T(8,128)(2,1)}, bf16[768,768]{1,0:T(8,128)(2,1)S(1)}, u32[]{:S(2)}, u32[]{:S(2)}) collective-permute-start(bf16[768,768]{1,0:T(8,128)(2,1)} %ua_ref.7), channel_id=1, source_target_pairs={{0,1},{1,0},{2,3},{3,2},{4,5},{5,4},{6,7},{7,6},{8,9},{9,8},{10,11... | collective-permute-start | bytes 3538952 | tf_op jit(solution)/shard_map/ppermute | solution.py:649
  10.5 19.9 %collective-permute-start.4 = (bf16[768,768]{1,0:T(8,128)(2,1)}, bf16[768,768]{1,0:T(8,128)(2,1)S(1)}, u32[]{:S(2)}, u32[]{:S(2)}) collective-permute-start(bf16[768,768]{1,0:T(8,128)(2,1)} %da_ref.7), channel_id=1, source_target_pairs={{0,1},{1,0},{2,3},{3,2},{4,5},{5,4},{6,7},{7,6},{8,9},{9,8},{10,11... | collective-permute-start | bytes 3538952 | tf_op jit(solution)/shard_map/ppermute | solution.py:649
  23.7 82.3 %copy-start.19 = (bf16[192,512]{1,0:T(8,128)(2,1)}, bf16[192,512]{1,0:T(8,128)(2,1)S(1)}, u32[]{:S(2)}) copy-start(bf16[192,512]{1,0:T(8,128)(2,1)S(1)} %get-tuple-element.126.a0.o0_ref) | copy-start | bytes 589828
  23.8 15.1 %collective-permute-start.5 = (bf16[192,512]{1,0:T(8,128)(2,1)S(1)}, bf16[192,512]{1,0:T(8,128)(2,1)S(1)}, u32[]{:S(2)}, u32[]{:S(2)}) collective-permute-start(bf16[192,512]{1,0:T(8,128)(2,1)S(1)} %get-tuple-element.134.o1_ref), channel_id=1, source_target_pairs={{0,1},{1,0},{2,3},{3,2},{4,5},{5,4},{6,7},{7,6},{8,9},{9,8},{10,11... | collective-permute-start | bytes 589832 | tf_op jit(solution)/shard_map/ppermute | solution.py:649
  24.0 15.2 %collective-permute-start.7 = (bf16[192,512]{1,0:T(8,128)(2,1)S(1)}, bf16[192,512]{1,0:T(8,128)(2,1)S(1)}, u32[]{:S(2)}, u32[]{:S(2)}) collective-permute-start(bf16[192,512]{1,0:T(8,128)(2,1)S(1)} %get-tuple-element.134.o1_ref), channel_id=1, source_target_pairs={{0,3},{1,2},{2,1},{3,0},{4,7},{5,6},{6,5},{7,4},{8,11},{9,10},{10,... | collective-permute-start | bytes 589832 | tf_op jit(solution)/shard_map/ppermute | solution.py:649
  25.7 13.5 %collective-permute-start.6 = (bf16[192,512]{1,0:T(8,128)(2,1)S(1)}, bf16[192,512]{1,0:T(8,128)(2,1)S(1)}, u32[]{:S(2)}, u32[]{:S(2)}) collective-permute-start(bf16[192,512]{1,0:T(8,128)(2,1)S(1)} %get-tuple-element.126.a0.o0_ref), channel_id=1, source_target_pairs={{0,2},{1,3},{2,0},{3,1},{4,6},{5,7},{6,4},{7,5},{8,10},{9,11},{10,... | collective-permute-start | bytes 589832 | tf_op jit(solution)/shard_map/ppermute | solution.py:649
  37.0 13.1 %collective-permute-start.10 = (bf16[192,512]{1,0:T(8,128)(2,1)S(1)}, bf16[192,512]{1,0:T(8,128)(2,1)S(1)}, u32[]{:S(2)}, u32[]{:S(2)}) collective-permute-start(bf16[192,512]{1,0:T(8,128)(2,1)S(1)} %get-tuple-element.137.o1_ref), channel_id=1, source_target_pairs={{0,3},{1,2},{2,1},{3,0},{4,7},{5,6},{6,5},{7,4},{8,11},{9,10},{10,... | collective-permute-start | bytes 589832 | tf_op jit(solution)/shard_map/ppermute | solution.py:649
  38.5 11.7 %collective-permute-start.8 = (bf16[192,512]{1,0:T(8,128)(2,1)S(1)}, bf16[192,512]{1,0:T(8,128)(2,1)S(1)}, u32[]{:S(2)}, u32[]{:S(2)}) collective-permute-start(bf16[192,512]{1,0:T(8,128)(2,1)S(1)} %get-tuple-element.137.o1_ref), channel_id=1, source_target_pairs={{0,1},{1,0},{2,3},{3,2},{4,5},{5,4},{6,7},{7,6},{8,9},{9,8},{10,11... | collective-permute-start | bytes 589832 | tf_op jit(solution)/shard_map/ppermute | solution.py:649
  38.9 11.2 %collective-permute-start.9 = (bf16[192,512]{1,0:T(8,128)(2,1)S(1)}, bf16[192,512]{1,0:T(8,128)(2,1)S(1)}, u32[]{:S(2)}, u32[]{:S(2)}) collective-permute-start(bf16[192,512]{1,0:T(8,128)(2,1)S(1)} %get-tuple-element.132.a0.o0_ref), channel_id=1, source_target_pairs={{0,2},{1,3},{2,0},{3,1},{4,6},{5,7},{6,4},{7,5},{8,10},{9,11},{10,... | collective-permute-start | bytes 589832 | tf_op jit(solution)/shard_map/ppermute | solution.py:649
  48.4 20.5 %collective-permute-start.11 = (bf16[512,768]{1,0:T(8,128)(2,1)S(1)}, bf16[512,768]{1,0:T(8,128)(2,1)S(1)}, u32[]{:S(2)}, u32[]{:S(2)}) collective-permute-start(bf16[512,768]{1,0:T(8,128)(2,1)S(1)} %get-tuple-element.141), channel_id=1, source_target_pairs={{0,2},{1,3},{2,0},{3,1},{4,6},{5,7},{6,4},{7,5},{8,10},{9,11},{10,... | collective-permute-start | bytes 2359304 | tf_op jit(solution)/shard_map/ppermute | solution.py:649
  60.6 25.1 %collective-permute-start.12 = (bf16[512,768]{1,0:T(8,128)(2,1)S(1)}, bf16[512,768]{1,0:T(8,128)(2,1)S(1)}, u32[]{:S(2)}, u32[]{:S(2)}) collective-permute-start(bf16[512,768]{1,0:T(8,128)(2,1)S(1)} %get-tuple-element.152), channel_id=1, source_target_pairs={{0,2},{1,3},{2,0},{3,1},{4,6},{5,7},{6,4},{7,5},{8,10},{9,11},{10,... | collective-permute-start | bytes 2359304 | tf_op jit(solution)/shard_map/ppermute | solution.py:649
  80.1 21.3 %collective-permute-start.13 = (bf16[512,768]{1,0:T(8,128)(2,1)S(1)}, bf16[512,768]{1,0:T(8,128)(2,1)S(1)}, u32[]{:S(2)}, u32[]{:S(2)}) collective-permute-start(bf16[512,768]{1,0:T(8,128)(2,1)S(1)} %get-tuple-element.162), channel_id=1, source_target_pairs={{0,2},{1,3},{2,0},{3,1},{4,6},{5,7},{6,4},{7,5},{8,10},{9,11},{10,... | collective-permute-start | bytes 2359304 | tf_op jit(solution)/shard_map/ppermute | solution.py:649
  101.4 2.8 %collective-permute-start.14 = (bf16[768,768]{1,0:T(8,128)(2,1)S(1)}, bf16[768,768]{1,0:T(8,128)(2,1)S(1)}, u32[]{:S(2)}, u32[]{:S(2)}) collective-permute-start(bf16[768,768]{1,0:T(8,128)(2,1)S(1)} %get-tuple-element.169), channel_id=1, source_target_pairs={{0,1},{1,0},{2,3},{3,2},{4,5},{5,4},{6,7},{7,6},{8,9},{9,8},{10,11... | collective-permute-start | bytes 3538952 | tf_op jit(solution)/shard_map/ppermute | solution.py:649
  101.4 4.5 %collective-permute-start.15 = (bf16[768,768]{1,0:T(8,128)(2,1)S(1)}, bf16[768,768]{1,0:T(8,128)(2,1)S(1)}, u32[]{:S(2)}, u32[]{:S(2)}) collective-permute-start(bf16[768,768]{1,0:T(8,128)(2,1)S(1)} %get-tuple-element.171), channel_id=1, source_target_pairs={{0,1},{1,0},{2,3},{3,2},{4,5},{5,4},{6,7},{7,6},{8,9},{9,8},{10,11... | collective-permute-start | bytes 3538952 | tf_op jit(solution)/shard_map/ppermute | solution.py:649
  114.6 8.3 %collective-permute-start.16 = (bf16[192,512]{1,0:T(8,128)(2,1)}, bf16[192,512]{1,0:T(8,128)(2,1)}, u32[]{:S(2)}, u32[]{:S(2)}) collective-permute-start(bf16[192,512]{1,0:T(8,128)(2,1)} %get-tuple-element.177), channel_id=1, source_target_pairs={{0,1},{1,0},{2,3},{3,2},{4,5},{5,4},{6,7},{7,6},{8,9},{9,8},{10,11... | collective-permute-start | bytes 589832 | tf_op jit(solution)/shard_map/ppermute | solution.py:649
  114.7 25.3 %collective-permute-start.19 = (bf16[512,768]{1,0:T(8,128)(2,1)S(1)}, bf16[512,768]{1,0:T(8,128)(2,1)S(1)}, u32[]{:S(2)}, u32[]{:S(2)}) collective-permute-start(bf16[512,768]{1,0:T(8,128)(2,1)S(1)} %get-tuple-element.189), channel_id=1, source_target_pairs={{0,2},{1,3},{2,0},{3,1},{4,6},{5,7},{6,4},{7,5},{8,10},{9,11},{10,... | collective-permute-start | bytes 2359304 | tf_op jit(solution)/shard_map/ppermute | solution.py:649
  116.4 20.1 %collective-permute-start.18 = (bf16[384,768]{1,0:T(8,128)(2,1)}, bf16[384,768]{1,0:T(8,128)(2,1)S(1)}, u32[]{:S(2)}, u32[]{:S(2)}) collective-permute-start(bf16[384,768]{1,0:T(8,128)(2,1)} %copy-done.9), channel_id=1, source_target_pairs={{0,8},{4,12},{8,0},{12,4},{16,24},{20,28},{24,16},{28,20},{1,9},{5... | collective-permute-start | bytes 1769480 | tf_op jit(solution)/shard_map/ppermute | solution.py:652
  121.4 15.2 %collective-permute-start.17 = (bf16[384,768]{1,0:T(8,128)(2,1)}, bf16[384,768]{1,0:T(8,128)(2,1)S(1)}, u32[]{:S(2)}, u32[]{:S(2)}) collective-permute-start(bf16[384,768]{1,0:T(8,128)(2,1)} %copy-done.8), channel_id=1, source_target_pairs={{0,4},{4,0},{8,12},{12,8},{16,20},{20,16},{24,28},{28,24},{1,5},{5... | collective-permute-start | bytes 1769480 | tf_op jit(solution)/shard_map/ppermute | solution.py:652
  137.1 13.7 %collective-permute-start.23 = (bf16[192,768]{1,0:T(8,128)(2,1)S(1)}, bf16[192,768]{1,0:T(8,128)(2,1)S(1)}, u32[]{:S(2)}, u32[]{:S(2)}) collective-permute-start(bf16[192,768]{1,0:T(8,128)(2,1)S(1)} %constant_dynamic-slice_fusion.7), channel_id=1, source_target_pairs={{0,8},{4,12},{8,0},{12,4},{16,24},{20,28},{24,16},{28,20},{1,9},{5... | collective-permute-start | bytes 884744 | tf_op jit(solution)/shard_map/ppermute | solution.py:652
  139.9 10.9 %collective-permute-start.24 = (bf16[192,768]{1,0:T(8,128)(2,1)S(1)}, bf16[192,768]{1,0:T(8,128)(2,1)S(1)}, u32[]{:S(2)}, u32[]{:S(2)}) collective-permute-start(bf16[192,768]{1,0:T(8,128)(2,1)S(1)} %constant_dynamic-slice_fusion.6), channel_id=1, source_target_pairs={{0,4},{4,0},{8,12},{12,8},{16,20},{20,16},{24,28},{28,24},{1,5},{5... | collective-permute-start | bytes 884744 | tf_op jit(solution)/shard_map/ppermute | solution.py:652
  150.2 17.0 %collective-permute-start.28 = (bf16[256,768]{1,0:T(8,128)(2,1)S(1)}, bf16[256,768]{1,0:T(8,128)(2,1)S(1)}, u32[]{:S(2)}, u32[]{:S(2)}) collective-permute-start(bf16[256,768]{1,0:T(8,128)(2,1)S(1)} %get-tuple-element.217), channel_id=1, source_target_pairs={{0,1},{1,0},{2,3},{3,2},{4,5},{5,4},{6,7},{7,6},{8,9},{9,8},{10,11... | collective-permute-start | bytes 1179656 | tf_op jit(solution)/shard_map/ppermute | solution.py:649
  150.3 3.8 %collective-permute-start.25 = (bf16[192,512]{1,0:T(8,128)(2,1)S(1)}, bf16[192,512]{1,0:T(8,128)(2,1)S(1)}, u32[]{:S(2)}, u32[]{:S(2)}) collective-permute-start(bf16[192,512]{1,0:T(8,128)(2,1)S(1)} %get-tuple-element.206), channel_id=1, source_target_pairs={{0,1},{1,0},{2,3},{3,2},{4,5},{5,4},{6,7},{7,6},{8,9},{9,8},{10,11... | collective-permute-start | bytes 589832 | tf_op jit(solution)/shard_map/ppermute | solution.py:649
  150.9 14.0 %collective-permute-start.27 = (bf16[96,768]{1,0:T(8,128)(2,1)S(1)}, bf16[96,768]{1,0:T(8,128)(2,1)S(1)}, u32[]{:S(2)}, u32[]{:S(2)}) collective-permute-start(bf16[96,768]{1,0:T(8,128)(2,1)S(1)} %constant_dynamic-slice_fusion.4), channel_id=1, source_target_pairs={{0,16},{4,20},{8,24},{12,28},{16,0},{20,4},{24,8},{28,12},{1,17},{... | collective-permute-start | bytes 442376 | tf_op jit(solution)/shard_map/ppermute | solution.py:652
  151.1 16.1 %collective-permute-start.26 = (bf16[96,768]{1,0:T(8,128)(2,1)S(1)}, bf16[96,768]{1,0:T(8,128)(2,1)S(1)}, u32[]{:S(2)}, u32[]{:S(2)}) collective-permute-start(bf16[96,768]{1,0:T(8,128)(2,1)S(1)} %constant_dynamic-slice_fusion.5), channel_id=1, source_target_pairs={{0,16},{4,20},{8,24},{12,28},{16,0},{20,4},{24,8},{28,12},{1,17},{... | collective-permute-start | bytes 442376 | tf_op jit(solution)/shard_map/ppermute | solution.py:652
  176.2 16.4 %collective-permute-start.32 = (bf16[416,768]{1,0:T(8,128)(2,1)}, bf16[416,768]{1,0:T(8,128)(2,1)}, u32[]{:S(2)}, u32[]{:S(2)}) collective-permute-start(bf16[416,768]{1,0:T(8,128)(2,1)} %constant_dynamic-slice_fusion.3), channel_id=1, source_target_pairs={{0,4},{4,0},{8,12},{12,8},{16,20},{20,16},{24,28},{28,24},{1,5},{5... | collective-permute-start | bytes 1916936 | tf_op jit(solution)/shard_map/ppermute | solution.py:652
  177.7 16.3 %collective-permute-start.29 = (bf16[512,768]{1,0:T(8,128)(2,1)}, bf16[512,768]{1,0:T(8,128)(2,1)}, u32[]{:S(2)}, u32[]{:S(2)}) collective-permute-start(bf16[512,768]{1,0:T(8,128)(2,1)} %get-tuple-element.219), channel_id=1, source_target_pairs={{0,1},{1,0},{2,3},{3,2},{4,5},{5,4},{6,7},{7,6},{8,9},{9,8},{10,11... | collective-permute-start | bytes 2359304 | tf_op jit(solution)/shard_map/ppermute | solution.py:649
  180.3 22.0 %collective-permute-start.20 = (bf16[512,768]{1,0:T(8,128)(2,1)}, bf16[512,768]{1,0:T(8,128)(2,1)S(1)}, u32[]{:S(2)}, u32[]{:S(2)}) collective-permute-start(bf16[512,768]{1,0:T(8,128)(2,1)} %copy-done.7), channel_id=1, source_target_pairs={{0,1},{1,0},{2,3},{3,2},{4,5},{5,4},{6,7},{7,6},{8,9},{9,8},{10,11... | collective-permute-start | bytes 2359304 | tf_op jit(solution)/shard_map/ppermute | solution.py:649
  180.9 13.1 %collective-permute-start.34 = (bf16[1,1,1,96,768]{4,3,2,1,0:T(8,128)(2,1)S(1)}, bf16[1,1,1,96,768]{4,3,2,1,0:T(8,128)(2,1)S(1)}, u32[]{:S(2)}, u32[]{:S(2)}) collective-permute-start(bf16[1,1,1,96,768]{4,3,2,1,0:T(8,128)(2,1)S(1)} %fusion.4), channel_id=1, source_target_pairs={{0,16},{4,20},{8,24},{12,28},{16,0},{20,4},{24,8},{28,12},{1,17},{... | collective-permute-start | bytes 442376 | tf_op jit(solution)/shard_map/ppermute | solution.py:652
  180.9 15.5 %collective-permute-start.33 = (bf16[1,1,1,96,768]{4,3,2,1,0:T(8,128)(2,1)S(1)}, bf16[1,1,1,96,768]{4,3,2,1,0:T(8,128)(2,1)S(1)}, u32[]{:S(2)}, u32[]{:S(2)}) collective-permute-start(bf16[1,1,1,96,768]{4,3,2,1,0:T(8,128)(2,1)S(1)} %fusion.3), channel_id=1, source_target_pairs={{0,16},{4,20},{8,24},{12,28},{16,0},{20,4},{24,8},{28,12},{1,17},{... | collective-permute-start | bytes 442376 | tf_op jit(solution)/shard_map/ppermute | solution.py:652
  196.5 16.3 %collective-permute-start.39 = (bf16[1,1,2,96,768]{4,3,2,1,0:T(8,128)(2,1)S(1)}, bf16[1,1,2,96,768]{4,3,2,1,0:T(8,128)(2,1)S(1)}, u32[]{:S(2)}, u32[]{:S(2)}) collective-permute-start(bf16[1,1,2,96,768]{4,3,2,1,0:T(8,128)(2,1)S(1)} %pad_maximum_fusion.7), channel_id=1, source_target_pairs={{0,4},{4,0},{8,12},{12,8},{16,20},{20,16},{24,28},{28,24},{1,5},{5... | collective-permute-start | bytes 884744 | tf_op jit(solution)/shard_map/ppermute | solution.py:652
  197.9 7.3 %collective-permute-start.35 = (bf16[104,768]{1,0:T(8,128)(2,1)S(1)}, bf16[104,768]{1,0:T(8,128)(2,1)S(1)}, u32[]{:S(2)}, u32[]{:S(2)}) collective-permute-start(bf16[104,768]{1,0:T(8,128)(2,1)S(1)} %get-tuple-element.246), channel_id=1, source_target_pairs={{0,8},{4,12},{8,0},{12,4},{16,24},{20,28},{24,16},{28,20},{1,9},{5... | collective-permute-start | bytes 479240 | tf_op jit(solution)/shard_map/ppermute | solution.py:652
  198.0 14.7 %collective-permute-start.36 = (bf16[104,768]{1,0:T(8,128)(2,1)S(1)}, bf16[104,768]{1,0:T(8,128)(2,1)S(1)}, u32[]{:S(2)}, u32[]{:S(2)}) collective-permute-start(bf16[104,768]{1,0:T(8,128)(2,1)S(1)} %get-tuple-element.248), channel_id=1, source_target_pairs={{0,16},{4,20},{8,24},{12,28},{16,0},{20,4},{24,8},{28,12},{1,17},{... | collective-permute-start | bytes 479240 | tf_op jit(solution)/shard_map/ppermute | solution.py:652
  199.7 13.0 %collective-permute-start.37 = (bf16[104,768]{1,0:T(8,128)(2,1)S(1)}, bf16[104,768]{1,0:T(8,128)(2,1)S(1)}, u32[]{:S(2)}, u32[]{:S(2)}) collective-permute-start(bf16[104,768]{1,0:T(8,128)(2,1)S(1)} %get-tuple-element.247), channel_id=1, source_target_pairs={{0,24},{4,28},{8,16},{12,20},{16,8},{20,12},{24,0},{28,4},{1,25},{... | collective-permute-start | bytes 479240 | tf_op jit(solution)/shard_map/ppermute | solution.py:652
  202.6 36.2 %collective-permute-start.21 = (bf16[512,768]{1,0:T(8,128)(2,1)S(1)}, bf16[512,768]{1,0:T(8,128)(2,1)S(1)}, u32[]{:S(2)}, u32[]{:S(2)}) collective-permute-start(bf16[512,768]{1,0:T(8,128)(2,1)S(1)} %fusion), channel_id=1, source_target_pairs={{0,2},{1,3},{2,0},{3,1},{4,6},{5,7},{6,4},{7,5},{8,10},{9,11},{10,... | collective-permute-start | bytes 2359304 | tf_op jit(solution)/shard_map/ppermute | solution.py:649
  205.2 12.0 %collective-permute-start.38 = (bf16[1,1,2,96,768]{4,3,2,1,0:T(8,128)(2,1)S(1)}, bf16[1,1,2,96,768]{4,3,2,1,0:T(8,128)(2,1)S(1)}, u32[]{:S(2)}, u32[]{:S(2)}) collective-permute-start(bf16[1,1,2,96,768]{4,3,2,1,0:T(8,128)(2,1)S(1)} %pad_maximum_fusion.6), channel_id=1, source_target_pairs={{0,8},{4,12},{8,0},{12,4},{16,24},{20,28},{24,16},{28,20},{1,9},{5... | collective-permute-start | bytes 884744 | tf_op jit(solution)/shard_map/ppermute | solution.py:652
  217.4 19.2 %collective-permute-start.43 = (bf16[1,2,2,96,768]{4,3,2,1,0:T(8,128)(2,1)S(1)}, bf16[1,2,2,96,768]{4,3,2,1,0:T(8,128)(2,1)S(1)}, u32[]{:S(2)}, u32[]{:S(2)}) collective-permute-start(bf16[1,2,2,96,768]{4,3,2,1,0:T(8,128)(2,1)S(1)} %pad_maximum_fusion.4), channel_id=1, source_target_pairs={{0,4},{4,0},{8,12},{12,8},{16,20},{20,16},{24,28},{28,24},{1,5},{5... | collective-permute-start | bytes 1769480 | tf_op jit(solution)/shard_map/ppermute | solution.py:652
  218.5 6.6 %collective-permute-start.40 = (bf16[1,1,104,768]{3,2,1,0:T(8,128)(2,1)S(1)}, bf16[1,1,104,768]{3,2,1,0:T(8,128)(2,1)S(1)}, u32[]{:S(2)}, u32[]{:S(2)}) collective-permute-start(bf16[1,1,104,768]{3,2,1,0:T(8,128)(2,1)S(1)} %fusion.2), channel_id=1, source_target_pairs={{0,8},{4,12},{8,0},{12,4},{16,24},{20,28},{24,16},{28,20},{1,9},{5... | collective-permute-start | bytes 479240 | tf_op jit(solution)/shard_map/ppermute | solution.py:652
  219.9 20.3 %collective-permute-start.30 = (bf16[512,768]{1,0:T(8,128)(2,1)S(1)}, bf16[512,768]{1,0:T(8,128)(2,1)S(1)}, u32[]{:S(2)}, u32[]{:S(2)}) collective-permute-start(bf16[512,768]{1,0:T(8,128)(2,1)S(1)} %fusion.1), channel_id=1, source_target_pairs={{0,2},{1,3},{2,0},{3,1},{4,6},{5,7},{6,4},{7,5},{8,10},{9,11},{10,... | collective-permute-start | bytes 2359304 | tf_op jit(solution)/shard_map/ppermute | solution.py:649
  220.8 14.4 %collective-permute-start.41 = (bf16[1,1,104,768]{3,2,1,0:T(8,128)(2,1)S(1)}, bf16[1,1,104,768]{3,2,1,0:T(8,128)(2,1)S(1)}, u32[]{:S(2)}, u32[]{:S(2)}) collective-permute-start(bf16[1,1,104,768]{3,2,1,0:T(8,128)(2,1)S(1)} %fusion.2), channel_id=1, source_target_pairs={{0,16},{4,20},{8,24},{12,28},{16,0},{20,4},{24,8},{28,12},{1,17},{... | collective-permute-start | bytes 479240 | tf_op jit(solution)/shard_map/ppermute | solution.py:652
  225.1 10.8 %collective-permute-start.42 = (bf16[1,1,104,768]{3,2,1,0:T(8,128)(2,1)S(1)}, bf16[1,1,104,768]{3,2,1,0:T(8,128)(2,1)S(1)}, u32[]{:S(2)}, u32[]{:S(2)}) collective-permute-start(bf16[1,1,104,768]{3,2,1,0:T(8,128)(2,1)S(1)} %fusion.2), channel_id=1, source_target_pairs={{0,24},{4,28},{8,16},{12,20},{16,8},{20,12},{24,0},{28,4},{1,25},{... | collective-permute-start | bytes 479240 | tf_op jit(solution)/shard_map/ppermute | solution.py:652
  236.8 14.7 %collective-permute-start.45 = (bf16[1,2,2,96,768]{4,3,2,1,0:T(8,128)(2,1)}, bf16[1,2,2,96,768]{4,3,2,1,0:T(8,128)(2,1)}, u32[]{:S(2)}, u32[]{:S(2)}) collective-permute-start(bf16[1,2,2,96,768]{4,3,2,1,0:T(8,128)(2,1)} %pad_maximum_fusion.5), channel_id=1, source_target_pairs={{0,8},{4,12},{8,0},{12,4},{16,24},{20,28},{24,16},{28,20},{1,9},{5... | collective-permute-start | bytes 1769480 | tf_op jit(solution)/shard_map/ppermute | solution.py:652
  240.2 22.1 %collective-permute-start.22 = (bf16[512,768]{1,0:T(8,128)(2,1)}, bf16[512,768]{1,0:T(8,128)(2,1)S(1)}, u32[]{:S(2)}, u32[]{:S(2)}) collective-permute-start(bf16[512,768]{1,0:T(8,128)(2,1)} %add_convert_fusion.1.refs_0_), channel_id=1, source_target_pairs={{0,1},{1,0},{2,3},{3,2},{4,5},{5,4},{6,7},{7,6},{8,9},{9,8},{10,11... | collective-permute-start | bytes 2359304 | tf_op jit(solution)/shard_map/ppermute | solution.py:649
  241.8 20.5 %collective-permute-start.31 = (bf16[512,768]{1,0:T(8,128)(2,1)S(1)}, bf16[512,768]{1,0:T(8,128)(2,1)S(1)}, u32[]{:S(2)}, u32[]{:S(2)}) collective-permute-start(bf16[512,768]{1,0:T(8,128)(2,1)S(1)} %add_convert_fusion.refs_2_), channel_id=1, source_target_pairs={{0,1},{1,0},{2,3},{3,2},{4,5},{5,4},{6,7},{7,6},{8,9},{9,8},{10,11... | collective-permute-start | bytes 2359304 | tf_op jit(solution)/shard_map/ppermute | solution.py:649
  242.3 16.6 %collective-permute-start.44 = (bf16[1,4,104,768]{3,2,1,0:T(8,128)(2,1)}, bf16[1,4,104,768]{3,2,1,0:T(8,128)(2,1)S(1)}, u32[]{:S(2)}, u32[]{:S(2)}) collective-permute-start(bf16[1,4,104,768]{3,2,1,0:T(8,128)(2,1)} %constant_dynamic-update-slice_fusion), channel_id=1, source_target_pairs={{0,4},{4,0},{8,12},{12,8},{16,20},{20,16},{24,28},{28,24},{1,5},{5... | collective-permute-start | bytes 1916936 | tf_op jit(solution)/shard_map/ppermute | solution.py:652
  (58 other events, 339.5 us)
Sparse Core Ops, SparseCore 0:
  180.5 9.7 all-gather.1

commit v9 on v8

--- a/solution.py
+++ b/solution.py
@@ -12,7 +12,7 @@
 EPS = 1e-05
 LOG2E = 1.4426950408889634
 KB = 256
-VMEM = 10
+VMEM = 12
 RB = 128
 HB = 256
 BF = jnp.bfloat16
@@ -40,7 +40,7 @@
     return pl.CostEstimate(flops=int(micros * 1.1e9), bytes_accessed=1024, transcendentals=0)
 
 
-MICROS = {"project": 3, "attend_forward": 8, "attend_backward": 12, "entry_back": 5, "place": 3, "ahead": 9, "astern": 10, "inner_norm": 3, "weight_grads": 5}
+MICROS = {"project": 3, "attend_forward": 8, "attend_backward": 12, "entry_back": 5, "place": 3, "ahead": 9, "astern": 10, "inner_norm": 3, "weight_grads": 4, "fold": 2}
 
 
 def lane_parts(block):
@@ -57,14 +57,16 @@
 TILE = (0, 0, 1)
 
 
-def call(kernel, name, grid, meta, args, in_specs, out_specs, out_shape, scratch=(), limit=VMEM, hold=(), out=()):
-    args = list(args)
-    for i in hold:
-        space = pltpu.VMEM if i >= 0 else pltpu.HBM
-        spot = i if i >= 0 else -1 - i
-        args[spot] = pltpu.with_memory_space_constraint(args[spot], space)
-    if isinstance(out_shape, list):
-        out_shape = [pltpu.VMEM(o.shape, o.dtype) if i in out else o for i, o in enumerate(out_shape)]
+def call(kernel, name, grid, meta, args, in_specs, out_specs, out_shape, scratch=(), limit=VMEM, hold=(), far=(), out=(), out_far=()):
+    def place_input(i, value):
+        space = pltpu.VMEM if i in hold else pltpu.HBM if i in far else None
+        return value if space is None else pltpu.with_memory_space_constraint(value, space)
+
+    def place_output(i, value):
+        space = pltpu.VMEM if i in out else pltpu.HBM if i in out_far else None
+        return value if space is None else space(value.shape, value.dtype)
+
+    single = not isinstance(out_shape, list)
     return pl.pallas_call(
         kernel,
         grid_spec=pltpu.PrefetchScalarGridSpec(
@@ -74,11 +76,11 @@
             out_specs=out_specs,
             scratch_shapes=scratch,
         ),
-        out_shape=out_shape,
+        out_shape=place_output(0, out_shape) if single else [place_output(i, o) for i, o in enumerate(out_shape)],
         compiler_params=params(limit),
         cost_estimate=cost(MICROS[name]),
         name=name,
-    )(meta, *args)
+    )(meta, *(place_input(i, value) for i, value in enumerate(args)))
 
 
 def fixed(*shape):
@@ -108,7 +110,7 @@
         [pl.BlockSpec((block, d), lambda i, m: (u * (rows // block) + i, 0))] + [fixed(192, d)] * 3,
         [pl.BlockSpec((block, 256), lambda i, m: (i, 0))] * 3,
         [like((rows, 256), BF)] * 3,
-        hold=(-1, -2, -3, -4),
+        far=range(4),
         out=(0, 1, 2),
     )
 
@@ -190,7 +192,6 @@
         ],
         [pltpu.VMEM((3, frames, half), F32)],
         hold=(0, 1, 2),
-        out=(2,),
     )
 
 
@@ -292,7 +293,8 @@
             pltpu.VMEM((192, half), BF),
             pltpu.VMEM((192, half), BF),
         ],
-        hold=(-1, -2, -3, 7),
+        hold=(3,),
+        far=(0, 1, 2),
         out=(0, 1, 2),
     )
 
@@ -349,7 +351,8 @@
         [fixed(half, d), fixed(half, d), fixed(rows, d)],
         [like((half, d), BF), like((half, d), BF), like((rows, d), dtype)],
         [pltpu.VMEM((576, d), F32)],
-        hold=(-1, 1, 2, 3, -5, -6, -7),
+        hold=(1, 2, 3),
+        far=(0, 4, 5, 6),
     )
 
 
@@ -450,8 +453,9 @@
             like((half, d), F32),
             like((half, d), BF),
         ],
-        hold=(-1,),
-        out=(0, 1, 2, 3, 4, 5),
+        far=(0,),
+        out=(1, 2, 3, 4, 5),
+        out_far=(0,),
     )
 
 
@@ -529,7 +533,8 @@
         ]
         + [like(shape, BF) for shape in grads],
         limit=12 if before else VMEM,
-        hold=(0, -3, 8, *range(10, 10 + len(before))),
+        hold=(0, 8, *range(10, 10 + len(before))),
+        far=(2,),
         out=(3,) if before else (1, 2, 3),
     )
 
@@ -573,16 +578,7 @@
 
 
 def inner_kernel(meta_ref, own_ref, far_ref, xhat_ref, rstd_ref, vec_ref, a0, a1, w0, w1, *refs):
-    last, cuts = len(refs) == 11, len(refs) == 14
-    if cuts:
-        for i in range(2):
-            here, there, send, keep = refs[2 * i], refs[2 * i + 1], refs[-4 + 2 * i], refs[-3 + 2 * i]
-            half = send.shape[0]
-            bit = meta_ref[meta_ref.shape[0] - 2 + i]
-            for part, j in ((send, 1 - bit), (keep, bit)):
-                rows = pl.ds(pl.multiple_of(j * half, 128), half)
-                part[...] = (here[rows, :].astype(F32) + there[rows, :].astype(F32)).astype(BF)
-        refs = refs[4:-4]
+    last = len(refs) == 11
     out_ref, g0, g1, m0, m1, small_ref = refs[-6:]
     grad = own_ref[...] + far_ref[...].astype(F32)
     xhat = xhat_ref[...]
@@ -611,28 +607,57 @@
         m1[...] = nn(a1[...], low)
 
 
-def inner_norm(meta, own, far, xhat, rstd, vectors, att, weights, before=(), sums=()):
+def inner_norm(meta, own, far, xhat, rstd, vectors, att, weights, before):
     rows, d = xhat.shape
     merge = like((256, d), BF) if before else like((192, d), F32)
-    half = like((sums[0].shape[0] // 2, d), BF) if sums else None
     return call(
         inner_kernel,
         "inner_norm",
         (1,),
         meta,
-        (own, far, xhat, rstd, vectors, *att, *weights, *before, *sums),
+        (own, far, xhat, rstd, vectors, *att, *weights, *before),
         [fixed(rows, d)] * 3
         + [fixed(rows, 128), fixed(4, d)]
         + [fixed(192, rows)] * 2
         + [fixed(192, d)] * 2
-        + ([fixed(192, d)] * 2 + [fixed(2, d)] * 3 if before else [])
-        + [fixed(*value.shape) for value in sums],
-        [fixed(rows, d), fixed(192, rows), fixed(192, rows), fixed(*merge.shape), fixed(*merge.shape), fixed(2, d)]
-        + ([fixed(*half.shape)] * 4 if sums else []),
-        [like((rows, d), F32), like((192, rows), BF), like((192, rows), BF), merge, merge, like((2, d), F32)]
-        + ([half] * 4 if sums else []),
-        hold=(0, 2, 3),
-        limit=20 if sums else VMEM,
+        + ([fixed(192, d)] * 2 + [fixed(2, d)] * 3 if before else []),
+        [fixed(rows, d), fixed(192, rows), fixed(192, rows), fixed(*merge.shape), fixed(*merge.shape), fixed(2, d)],
+        [like((rows, d), F32), like((192, rows), BF), like((192, rows), BF), merge, merge, like((2, d), F32)],
+        hold=(0, 3, 9, 10) if before else (0, 3),
+        far=(2,),
+        out=(1,) if before else (1, 3, 4),
+        out_far=(0,),
+    )
+
+
+def fold_kernel(bits, meta_ref, *refs):
+    for i in range(2):
+        here, there = refs[2 * i : 2 * i + 2]
+        if bits:
+            send, keep = refs[4 + 2 * i : 6 + 2 * i]
+            half = send.shape[0]
+            bit = meta_ref[bits[i]]
+            for part, j in ((send, 1 - bit), (keep, bit)):
+                rows = pl.ds(pl.multiple_of(j * half, 16), half)
+                part[...] = (here[rows, :].astype(F32) + there[rows, :].astype(F32)).astype(BF)
+        else:
+            refs[4 + i][...] = (here[...].astype(F32) + there[...].astype(F32)).astype(BF)
+
+
+def fold(meta, pairs, bits, hold=()):
+    args = [value for pair in pairs for value in pair]
+    rows, d = args[0].shape
+    shapes = [like((rows // 2, d), BF)] * 4 if bits else [like((rows, d), BF)] * 2
+    return call(
+        functools.partial(fold_kernel, bits),
+        "fold",
+        (1,),
+        meta,
+        args,
+        [fixed(rows, d)] * 4,
+        [fixed(*shape.shape) for shape in shapes],
+        shapes,
+        hold=hold,
     )
 
 
@@ -657,34 +682,28 @@
     def total(pieces):
         return sum(piece.astype(F32) for piece in pieces).astype(BF) if len(pieces) > 1 else pieces[0]
 
-    pairs = [(b, 1) for b in range(bits)]
     stages = [(0, 1)] + [(b, 2) for b in range(1, bits - 1, 2)] + ([(bits - 1, 1)] if bits % 2 == 0 else [])
-    orders = (pairs, pairs[1:2] + pairs[:1] + pairs[2:])
+    bit_orders = (list(range(bits)), [1, 0, *range(2, bits)])
 
     def spot_of(stage):
         return (place_dp >> stage[0]) & ((1 << stage[1]) - 1)
 
     class Chain:
-        def __init__(self, parts, order, back=None, halves=None):
-            self.parts = parts
-            self.halves = halves
+        def __init__(self, part, order, cut_already=False):
+            self.part = part.reshape((1,) * len(order) + part.shape) if cut_already else part
             self.order = order
-            self.steps = [(True, stage) for stage in order] + [(False, stage) for stage in back or reversed(order)]
+            self.steps = [] if cut_already else [(True, stage) for stage in order]
+            self.steps += [(False, stage) for stage in reversed(order)]
 
         def cut(self, stage, j):
-            count = 1 << stage[1]
-            size = self.parts[0].shape[0] // count
-            return [lax.dynamic_slice_in_dim(p, (spot_of(stage) ^ j) * size, size, 0) for p in self.parts]
+            size = self.part.shape[0] >> stage[1]
+            return lax.dynamic_slice_in_dim(self.part, (spot_of(stage) ^ j) * size, size, 0)
 
         def start(self):
             if self.steps:
                 scatter, stage = self.steps[0]
                 others = range(1, 1 << stage[1])
-                if self.halves:
-                    sent = [self.halves[0]]
-                else:
-                    sent = [total(self.cut(stage, j)) if scatter else self.parts[0] for j in others]
-                self.pending = [swap_dp(piece, j << stage[0]) for j, piece in zip(others, sent)]
+                self.pending = [swap_dp(self.cut(stage, j) if scatter else self.part, j << stage[0]) for j in others]
 
         def finish(self, *after):
             if not self.steps:
@@ -694,14 +713,13 @@
             if after:
                 got = list(lax.optimization_barrier((*got, *after))[: len(got)])
             if scatter:
-                state = total(([self.halves[1]] if self.halves else self.cut(stage, 0)) + got)
-                self.halves = None
+                state = total([self.cut(stage, 0)] + got)
                 if not self.steps[0][0]:
                     state = state.reshape((1,) * len(self.order) + state.shape)
             else:
                 axis = self.order.index(stage)
                 spot = spot_of(stage)
-                mine = self.parts[0]
+                mine = self.part
                 if len(got) == 1:
                     laid = [jnp.where(spot, got[0], mine), jnp.where(spot, mine, got[0])]
                     state = jnp.concatenate(laid, axis=axis)
@@ -711,7 +729,7 @@
                         state = lax.dynamic_update_slice_in_dim(state, piece, spot ^ j, axis)
                 if not self.steps:
                     state = state.reshape(-1, d)
-            self.parts = [state]
+            self.part = state
 
     def finish(group, *after):
         for chain in group:
@@ -722,10 +740,11 @@
             chain.start()
 
     def together(group):
-        for chain, value in zip(group, lax.optimization_barrier(tuple(chain.parts[0] for chain in group))):
-            chain.parts = [value]
-
-    scalars = jnp.concatenate([core.reshape(1), lengths, *(spot_of(order[0]).reshape(1) for order in orders)])
+        for chain, value in zip(group, lax.optimization_barrier(tuple(chain.part for chain in group))):
+            chain.part = value
+
+    all_bits = [((place_dp >> b) & 1).reshape(1) for b in range(bits)]
+    scalars = jnp.concatenate([core.reshape(1), lengths, *all_bits])
     token = []
 
     def meta():
@@ -762,8 +781,8 @@
             far_grad.append(swap(back[u][4], 2))
             sums = done(weight_grads(meta(), front[u][2], back[u][1], front[u][3], back[u][2], sums))
 
-    def inner_step(u, **more):
-        res = done(inner_norm(meta(), back[u][3], far_grad[u], front[u][0], front[u][1], vectors, att[u][:2], merge_w[:2], **more))
+    def inner_step(u, before):
+        res = done(inner_norm(meta(), back[u][3], far_grad[u], front[u][0], front[u][1], vectors, att[u][:2], merge_w[:2], before))
         return res, (res[1], swap(res[2], 1))
 
     def attend_step(u, grads):
@@ -772,37 +791,48 @@
     def entry_step(u, grads, before):
         return done(entry_back(meta(), tokens, grads, qkv_w, before, u, frames))
 
+
+    first_bit = 1 + seqs
+
+    def scatter(step, pairs, after, hold=()):
+        pairs = [tuple(lax.optimization_barrier((*pair, after))[:2]) for pair in pairs]
+        if step == bits:
+            return done(fold(meta(), pairs, (), hold))
+        out = done(fold(meta(), pairs, tuple(first_bit + order[step] for order in bit_orders), hold))
+        return [(out[2 * i + 1], swap_dp(out[2 * i], 1 << bit_orders[i][step])) for i in range(2)]
 
     inner, entry, so_far = [], [], ()
     for u in range(seqs):
         last = u == seqs - 1
         if u == 0:
             up_own, up_other, down_own, down_other = lax.optimization_barrier((*back[-1][6:], far_grad[0]))[:4]
-            sums = (down_own, swap(down_other, 1), up_own, swap(up_other, 1))
-            res, grads = inner_step(0, sums=sums)
+            moving = [(down_own, swap(down_other, 1)), (up_own, swap(up_other, 1))]
+            res, grads = inner_step(0, ())
             inner.append(res)
             far_grad.append(swap(lax.optimization_barrier((back[-1][4], res[0]))[0], 2))
-            ffn = [Chain(None, order, None, res[6 + 2 * i : 8 + 2 * i]) for i, order in enumerate(orders)]
-            start(ffn)
+            moving = scatter(0, moving, res[0], (0, 2))
         dqkv = attend_step(u, grads)
-        finish(ffn, dqkv[0])
-        token.extend(chain.parts[0] for chain in ffn)
-        start(ffn)
+        moving = scatter(1 + 2 * u, moving, dqkv[0])
         if not last:
             before = ()
             if u + 1 == seqs - 1:
                 before = (inner[0][3], inner[0][4], inner[0][5], back[0][5], back[1][5])
-            res, grads = inner_step(u + 1, before=before)
+            res, grads = inner_step(u + 1, before)
             inner.append(res)
+        else:
+            for step in range(4, bits + 1):
+                moving = scatter(step, moving, moving[0][0])
+            first, second = (
+                Chain(moving[i], [(b, 1) for b in order], True) for i, order in enumerate(bit_orders)
+            )
+            start([first, second])
         out = entry_step(u, dqkv, so_far)
         entry.append(out)
         if not last:
             merge_got = swap(lax.optimization_barrier((res[4], out[0]))[0], 1)
             so_far = (out[2], res[3], merge_got)
-            finish(ffn, out[0])
-            token.extend(chain.parts[0] for chain in ffn)
-            start(ffn)
-    qkv = Chain([out[2]], stages)
+            moving = scatter(2, moving, out[0])
+    qkv = Chain(out[2], stages)
     qkv.start()
 
     ready = []
@@ -811,24 +841,21 @@
         crossed = swap(total((entry[u][1], got)), 2)
         rest = entry[u][1].astype(F32) + got.astype(F32) + crossed.astype(F32)
         ready.append((inner[u][0] + rest).astype(BF))
-
-    first, second = ffn
-    finish(ffn, got)
+    out_rows = [b[0] for b in back]
+    layer_output = place(meta(), out_rows, [swap(r, 1) for r in out_rows])
+
+    finish([first, second], got)
     for group, sending in (((qkv,), (qkv, first, second)), ((qkv, first, second), (qkv, first)), ((qkv, first), (qkv, second))):
         finish(group)
         together([qkv, first, second])
         start(sending)
-    finish([qkv, second])
+    input_grad = place(scalars, ready, [swap(r, 1) for r in ready])
+    finish([qkv, second], input_grad, layer_output)
     while qkv.steps or first.steps or second.steps:
         start([qkv, first, second])
         finish([qkv, first, second])
         together([qkv, first, second])
-    down_sum, up_sum, joint = (chain.parts[0] for chain in ffn + [qkv])
-    chips = [[i, i + 1] for i in range(0, 4, 2)]
-    out_rows = lax.optimization_barrier((*(b[0] for b in back), inner[0][0]))[:seqs]
-    layer_output = lax.all_gather(jnp.stack(out_rows), "tensor", axis=1, tiled=True, axis_index_groups=chips)
-    layer_output = layer_output.reshape(rows, d)
-    input_grad = place(scalars, ready, [swap(r, 1) for r in ready])
+    down_sum, up_sum, joint = (chain.part for chain in (first, second, qkv))
     qkv_sum, merge_sum = joint[:576], joint[576:]
     small = merge_sum[192:196].astype(F32)
     query_grad, key_grad, value_grad = (qkv_sum[192 * i : 192 * (i + 1)].astype(F32).T for i in range(3))

time: 279 us -> 270 us (0.968)
  between operations: 15.4 us -> 1.97 us
  Pallas kernels: 107 us -> 119 us
  starting transfers between devices: 49 us -> 39 us
  waiting for transfers between devices: 65.2 us -> 73.2 us
  other arithmetic: 18.6 us -> 12.7 us
    pallas_call x16 -> x21, Pallas kernels: 107 us -> 119 us  [call(): pl.pallas_call(kernel, grid_spec=pltpu.PrefetchScalarGridSpec(num_scalar_...]
    ppermute x20, starting transfers between devices: 30.9 us -> 22.2 us  [swap_dp(): return lax.ppermute(value, 'dp', [(i, i ^ k) for i in range(groups)])]
    ppermute x26 -> x28, waiting for transfers between devices: 19.2 us -> 25.8 us  [swap(): return lax.ppermute(value, 'tensor', [(i, i ^ k) for i in range(4)])]
    unnamed x119 -> x112, local copies, waits for them, and re-layouts: 15.2 us -> 19.7 us
    ppermute x26 -> x28, starting transfers between devices: 18 us -> 16.8 us  [swap(): return lax.ppermute(value, 'tensor', [(i, i ^ k) for i in range(4)])]
  transfers between devices with their start and end apart: 47 -> 48, of which waited for: 17 -> 14; matrix products, arithmetic and copies ran while one was open for 8% -> 5% of each run, Pallas kernels for 33% -> 44%
where the time goes in v9:
time: 270 us; the launch traced here: 267 us
  Pallas kernels  119 us (44%)
  waiting for transfers between devices  73.2 us (27%)
  starting transfers between devices  39 us (14%)
  local copies, waits for them, and re-layouts  22.1 us (8%)
  other arithmetic  12.7 us (5%)
    pallas_call x21, Pallas kernels, call(): pl.pallas_call(kernel, grid_spec=pltpu.PrefetchScalarGridSpec(num_scalar_...  119 us
    ppermute x20, waiting for transfers between devices, swap_dp(): return lax.ppermute(value, 'dp', [(i, i ^ k) for i in range(groups)])  47.4 us
    ppermute x28, waiting for transfers between devices, swap(): return lax.ppermute(value, 'tensor', [(i, i ^ k) for i in range(4)])  25.8 us
    ppermute x20, starting transfers between devices, swap_dp(): return lax.ppermute(value, 'dp', [(i, i ^ k) for i in range(groups)])  22.2 us
    unnamed x112, local copies, waits for them, and re-layouts  19.7 us
    ppermute x28, starting transfers between devices, swap(): return lax.ppermute(value, 'tensor', [(i, i ^ k) for i in range(4)])  16.8 us
  transfers between devices with their start and end apart: 48, of which 14 were waited for; matrix products, arithmetic and copies ran while one was open for 5% of the time, Pallas kernels for 44%

profile of v9, /device:TPU:0, one launch (start us, length us, event | category | flops | bytes accessed | tf_op | source)
XLA Modules:
  0.0 267.4 jit_solution(15239228609510679428)
XLA Ops:
  1.2 2.6 collective-permute-start.1
  5.0 4.4 %project.2 = (bf16[1024,256]{1,0:T(8,128)(2,1)S(1)}, bf16[1024,256]{1,0:T(8,128)(2,1)S(1)}, bf16[1024,256]{1,0:T(8,128)(2,1)S(1)}) custom-call(s32[6]{0:T(128)S(1)} %concatenate.24.meta_ref, bf16[2048,768]{1,0:T(8,128)(2,1)} %x_ref.7, bf16[192,768]{1,0:T(8,128)(2,1)} %bitcast.31, bf16[192,768]{1,0:T(8,128)(2,1)} %bitcast.35, bf16[192,768]{1,0:T(8,128)(2,1)} %bitcast.39), custom_call_target="tpu_custom_call" | custom-call | flops 3300000000 | bytes 1024 | tf_op jit(solution)/shard_map/project/pallas_call | solution.py:70
  9.5 7.7 %attend_forward.2 = (bf16[192,512]{1,0:T(8,128)(2,1)S(1)}, bf16[192,512]{1,0:T(8,128)(2,1)S(1)}, f32[2,8,512]{2,1,0:T(8,128)S(1)}) custom-call(s32[6]{0:T(128)S(1)} %concatenate.24.meta_ref, bf16[1024,256]{1,0:T(8,128)(2,1)S(1)} %get-tuple-element.147.q_ref, bf16[1024,256]{1,0:T(8,128)(2,1)S(1)} %get-tuple-element.149.k_ref, ...), custom_call_target="tpu_custom_call" | custom-call | flops 8800000000 | bytes 1024 | tf_op jit(solution)/shard_map/attend_forward/pallas_call | solution.py:70
  17.6 1.7 collective-permute-start.7
  19.6 4.4 %project.3 = (bf16[1024,256]{1,0:T(8,128)(2,1)S(1)}, bf16[1024,256]{1,0:T(8,128)(2,1)S(1)}, bf16[1024,256]{1,0:T(8,128)(2,1)S(1)}) custom-call(s32[6]{0:T(128)S(1)} %concatenate.24.meta_ref, bf16[2048,768]{1,0:T(8,128)(2,1)} %x_ref.7, bf16[192,768]{1,0:T(8,128)(2,1)} %bitcast.32, bf16[192,768]{1,0:T(8,128)(2,1)} %bitcast.36, bf16[192,768]{1,0:T(8,128)(2,1)} %bitcast.40), custom_call_target="tpu_custom_call" | custom-call | flops 3300000000 | bytes 1024 | tf_op jit(solution)/shard_map/project/pallas_call | solution.py:70
  26.1 6.5 %attend_forward.3 = (bf16[192,512]{1,0:T(8,128)(2,1)S(1)}, bf16[192,512]{1,0:T(8,128)(2,1)S(1)}, f32[2,8,512]{2,1,0:T(8,128)S(1)}) custom-call(s32[6]{0:T(128)S(1)} %concatenate.24.meta_ref, bf16[1024,256]{1,0:T(8,128)(2,1)S(1)} %get-tuple-element.153.q_ref, bf16[1024,256]{1,0:T(8,128)(2,1)S(1)} %get-tuple-element.155.k_ref, ...), custom_call_target="tpu_custom_call" | custom-call | flops 8800000000 | bytes 1024 | tf_op jit(solution)/shard_map/attend_forward/pallas_call | solution.py:70
  35.0 1.4 collective-permute-start.10
  37.2 9.0 %ahead.2 = (f32[512,768]{1,0:T(8,128)}, f32[512,128]{1,0:T(8,128)S(1)}, bf16[512,768]{1,0:T(8,128)(2,1)S(1)}, bf16[512,1536]{1,0:T(8,128)(2,1)S(1)}, bf16[512,15...) custom-call(s32[6]{0:T(128)S(1)} %concatenate.24.meta_ref, bf16[2048,768]{1,0:T(8,128)(2,1)} %x_ref.7, ...), custom_call_target="tpu_custom_call" | custom-call | flops 9900000256 | bytes 1024 | tf_op jit(solution)/shard_map/ahead/pallas_call | solution.py:70
  46.9 1.7 collective-permute-start.11
  48.6 9.1 %ahead.3 = (f32[512,768]{1,0:T(8,128)}, f32[512,128]{1,0:T(8,128)S(1)}, bf16[512,768]{1,0:T(8,128)(2,1)S(1)}, bf16[512,1536]{1,0:T(8,128)(2,1)S(1)}, bf16[512,15...) custom-call(s32[6]{0:T(128)S(1)} %concatenate.24.meta_ref, bf16[2048,768]{1,0:T(8,128)(2,1)} %x_ref.7, ...), custom_call_target="tpu_custom_call" | custom-call | flops 9900000256 | bytes 1024 | tf_op jit(solution)/shard_map/ahead/pallas_call | solution.py:70
  58.8 8.5 %collective-permute-done.11.far_ref = bf16[512,768]{1,0:T(8,128)(2,1)S(1)} collective-permute-done((bf16[512,768]{1,0:T(8,128)(2,1)S(1)}, bf16[512,768]{1,0:T(8,128)(2,1)S(1)}, u32[]{:S(2)}, u32[]{:S(2)}) %collective-permute-start.11) | collective-permute-done | bytes 786464 | tf_op jit(solution)/shard_map/ppermute | solution.py:674
  67.3 8.0 %astern.2 = (bf16[512,768]{1,0:T(8,128)(2,1)S(1)}, bf16[512,768]{1,0:T(8,128)(2,1)S(1)}, bf16[512,1536]{1,0:T(8,128)(2,1)S(1)}, f32[512,768]{1,0:T(8,128)S(1)}, ...) custom-call(s32[6]{0:T(128)S(1)} %concatenate.24.meta_ref, f32[512,768]{1,0:T(8,128)S(1)} %get-tuple-element.165.own_ref, ...), custom_call_target="tpu_custom_call" | custom-call | flops 11000000512 | bytes 1024 | tf_op jit(solution)/shard_map/astern/pallas_call | solution.py:70
  76.3 3.2 %weight_grads.1 = (bf16[768,768]{1,0:T(8,128)(2,1)S(1)}, bf16[768,768]{1,0:T(8,128)(2,1)S(1)}, bf16[768,768]{1,0:T(8,128)(2,1)S(1)}, bf16[768,768]{1,0:T(8,128)(2,1)S(1)}) custom-call(s32[6]{0:T(128)S(1)} %concatenate.24.meta_ref, bf16[512,768]{1,0:T(8,128)(2,1)S(1)} %get-tuple-element.170.x_ref, bf16[512,768]{1,0:T(8,128)(2,1)S(1)} %get-tuple-element.171.g_ref, ...), custom_call_target="tpu_custom_call" | custom-call | flops 4400000000 | bytes 1024 | tf_op jit(solution)/shard_map/weight_grads/pallas_call | solution.py:70
  79.5 1.8 collective-permute-start.13
  81.3 2.9 %collective-permute-done.12.far_ref = bf16[512,768]{1,0:T(8,128)(2,1)S(1)} collective-permute-done((bf16[512,768]{1,0:T(8,128)(2,1)S(1)}, bf16[512,768]{1,0:T(8,128)(2,1)S(1)}, u32[]{:S(2)}, u32[]{:S(2)}) %collective-permute-start.12) | collective-permute-done | bytes 786464 | tf_op jit(solution)/shard_map/ppermute | solution.py:674
  84.2 12.2 %astern.3 = (bf16[512,768]{1,0:T(8,128)(2,1)S(1)}, bf16[512,768]{1,0:T(8,128)(2,1)}, bf16[512,1536]{1,0:T(8,128)(2,1)}, f32[512,768]{1,0:T(8,128)S(1)}, bf16[512...) custom-call(s32[6]{0:T(128)S(1)} %concatenate.24.meta_ref, ...), custom_call_target="tpu_custom_call" | custom-call | flops 11000000512 | bytes 1024 | tf_op jit(solution)/shard_map/astern/pallas_call | solution.py:70
  105.9 1.4 copy-done.39
  108.3 4.9 %inner_norm.2 = (f32[512,768]{1,0:T(8,128)}, bf16[192,512]{1,0:T(8,128)(2,1)S(1)}, bf16[192,512]{1,0:T(8,128)(2,1)S(1)}, f32[192,768]{1,0:T(8,128)S(1)}, f32[192,768]{1,0:T(8,128)S(1)}, /*index=5*/f32[2,768]{1,0:T(2,128)S(1)}) custom-call(s32[6]{0:T(128)S(1)} %concatenate.24.meta_ref, f32[512,768]{1,0:T(8,128)S(1)} %copy-done.39, ...), custom_call_target="tpu_custom_call" | custom-call | flops 3300000000 | bytes 1024 | tf_op jit(solution)/shard_map/inner_norm/pallas_call | solution.py:70
  113.2 1.7 collective-permute-start.19
  116.3 12.3 %attend_backward.2 = (bf16[1024,256]{1,0:T(8,128)(2,1)S(1)}, bf16[1024,256]{1,0:T(8,128)(2,1)S(1)}, bf16[1024,256]{1,0:T(8,128)(2,1)S(1)}) custom-call(s32[6]{0:T(128)S(1)} %concatenate.24.meta_ref, bf16[1024,256]{1,0:T(8,128)(2,1)} %copy-done.43, bf16[1024,256]{1,0:T(8,128)(2,1)} %copy-done.44, bf16[1024,256]{1,0:T(8,128)(2,1)} %copy-done.45, ...), custom_call_target="tpu_custom_call" | custom-call | flops 13200000000 | bytes 1024 | tf_op jit(solution)/shard_map/attend_backward/pallas_call | solution.py:70
  128.7 3.2 %collective-permute-done.18.refs_3_ = bf16[384,768]{1,0:T(8,128)(2,1)S(1)} collective-permute-done((bf16[384,768]{1,0:T(8,128)(2,1)S(1)}, bf16[384,768]{1,0:T(8,128)(2,1)S(1)}, u32[]{:S(2)}, u32[]{:S(2)}) %collective-permute-start.18) | collective-permute-done | bytes 589856 | tf_op jit(solution)/shard_map/ppermute | solution.py:677
  133.6 4.3 %inner_norm.3 = (f32[512,768]{1,0:T(8,128)}, bf16[192,512]{1,0:T(8,128)(2,1)S(1)}, bf16[192,512]{1,0:T(8,128)(2,1)S(1)}, bf16[256,768]{1,0:T(8,128)(2,1)S(1)}, b...) custom-call(s32[6]{0:T(128)S(1)} %concatenate.24.meta_ref, f32[512,768]{1,0:T(8,128)S(1)} %copy-done.37, ...), custom_call_target="tpu_custom_call" | custom-call | flops 3300000000 | bytes 1024 | tf_op jit(solution)/shard_map/inner_norm/pallas_call | solution.py:70
  137.9 1.7 collective-permute-start.21
  139.6 7.0 %entry_back.2 = (bf16[512,768]{1,0:T(8,128)(2,1)}, bf16[512,768]{1,0:T(8,128)(2,1)S(1)}, f32[576,768]{1,0:T(8,128)S(1)}) custom-call(s32[6]{0:T(128)S(1)} %concatenate.24.meta_ref, bf16[2048,768]{1,0:T(8,128)(2,1)} %x_ref.7, bf16[1024,256]{1,0:T(8,128)(2,1)S(1)} %get-tuple-element.208.dq_ref, bf16[1024,256]{1,0:T(8,128)(2,1)S(1)} %get-tuple-element.230.dk_ref, ...), custom_call_target="tpu_custom_call" | custom-call | flops 5500000256 | bytes 1024 | tf_op jit(solution)/shard_map/entry_back/pallas_call | solution.py:70
  147.9 5.2 %collective-permute-start.23 = (bf16[96,768]{1,0:T(8,128)(2,1)S(1)}, bf16[96,768]{1,0:T(8,128)(2,1)S(1)}, u32[]{:S(2)}, u32[]{:S(2)}) collective-permute-start(bf16[96,768]{1,0:T(8,128)(2,1)S(1)} %get-tuple-element.241), channel_id=1, source_target_pairs={{0,16},{4,20},{8,24},{12,28},{16,0},{20,4},{24,8},{28,12},{1,17},{... | collective-permute-start | bytes 442376 | tf_op jit(solution)/shard_map/ppermute | solution.py:677
  153.1 10.0 %attend_backward.3 = (bf16[1024,256]{1,0:T(8,128)(2,1)S(1)}, bf16[1024,256]{1,0:T(8,128)(2,1)S(1)}, bf16[1024,256]{1,0:T(8,128)(2,1)S(1)}) custom-call(s32[6]{0:T(128)S(1)} %concatenate.24.meta_ref, bf16[1024,256]{1,0:T(8,128)(2,1)} %copy-done.40, bf16[1024,256]{1,0:T(8,128)(2,1)} %copy-done.41, bf16[1024,256]{1,0:T(8,128)(2,1)} %copy-done.42, ...), custom_call_target="tpu_custom_call" | custom-call | flops 13200000000 | bytes 1024 | tf_op jit(solution)/shard_map/attend_backward/pallas_call | solution.py:70
  163.1 3.9 %collective-permute-done.24.refs_3_ = bf16[96,768]{1,0:T(8,128)(2,1)S(1)} collective-permute-done((bf16[96,768]{1,0:T(8,128)(2,1)S(1)}, bf16[96,768]{1,0:T(8,128)(2,1)S(1)}, u32[]{:S(2)}, u32[]{:S(2)}) %collective-permute-start.24) | collective-permute-done | bytes 147488 | tf_op jit(solution)/shard_map/ppermute | solution.py:677
  167.7 7.0 %entry_back.3 = (bf16[512,768]{1,0:T(8,128)(2,1)}, bf16[512,768]{1,0:T(8,128)(2,1)S(1)}, bf16[832,768]{1,0:T(8,128)(2,1)S(1)}) custom-call(s32[6]{0:T(128)S(1)} %concatenate.24.meta_ref, bf16[2048,768]{1,0:T(8,128)(2,1)} %x_ref.7, bf16[1024,256]{1,0:T(8,128)(2,1)S(1)} %get-tuple-element.246.dq_ref, bf16[1024,256]{1,0:T(8,128)(2,1)S(1)} %get-tuple-element.257.dk_ref, ...), custom_call_target="tpu_custom_call" | custom-call | flops 5500000256 | bytes 1024 | tf_op jit(solution)/shard_map/entry_back/pallas_call | solution.py:70
  176.4 2.9 %collective-permute-start.35 = (bf16[1,1,1,96,768]{4,3,2,1,0:T(8,128)(2,1)S(1)}, bf16[1,1,1,96,768]{4,3,2,1,0:T(8,128)(2,1)S(1)}, u32[]{:S(2)}, u32[]{:S(2)}) collective-permute-start(bf16[1,1,1,96,768]{4,3,2,1,0:T(8,128)(2,1)S(1)} %bitcast.26), channel_id=1, source_target_pairs={{0,16},{4,20},{8,24},{12,28},{16,0},{20,4},{24,8},{28,12},{1,17},{... | collective-permute-start | bytes 442376 | tf_op jit(solution)/shard_map/ppermute | solution.py:677
  180.7 11.4 %collective-permute-done.34 = bf16[416,768]{1,0:T(8,128)(2,1)} collective-permute-done((bf16[416,768]{1,0:T(8,128)(2,1)}, bf16[416,768]{1,0:T(8,128)(2,1)}, u32[]{:S(2)}, u32[]{:S(2)}) %collective-permute-start.34) | collective-permute-done | bytes 639008 | tf_op jit(solution)/shard_map/ppermute | solution.py:677
  194.5 2.6 collective-permute-start.38
  197.1 1.8 collective-permute-start.39
  200.2 2.1 collective-permute-done.37
  202.3 6.8 %collective-permute-done.38 = bf16[104,768]{1,0:T(8,128)(2,1)S(1)} collective-permute-done((bf16[104,768]{1,0:T(8,128)(2,1)S(1)}, bf16[104,768]{1,0:T(8,128)(2,1)S(1)}, u32[]{:S(2)}, u32[]{:S(2)}) %collective-permute-start.38) | collective-permute-done | bytes 159776 | tf_op jit(solution)/shard_map/ppermute | solution.py:677
  209.7 2.2 collective-permute-start.40
  212.7 5.2 %collective-permute-done.40 = bf16[1,1,2,96,768]{4,3,2,1,0:T(8,128)(2,1)S(1)} collective-permute-done((bf16[1,1,2,96,768]{4,3,2,1,0:T(8,128)(2,1)S(1)}, bf16[1,1,2,96,768]{4,3,2,1,0:T(8,128)(2,1)S(1)}, u32[]{:S(2)}, u32[]{:S(2)}) %collective-permute-start.40) | collective-permute-done | bytes 294944 | tf_op jit(solution)/shard_map/ppermute | solution.py:677
  218.1 1.8 collective-permute-start.42
  220.0 9.7 %collective-permute-done.29 = bf16[512,768]{1,0:T(8,128)(2,1)S(1)} collective-permute-done((bf16[512,768]{1,0:T(8,128)(2,1)S(1)}, bf16[512,768]{1,0:T(8,128)(2,1)S(1)}, u32[]{:S(2)}, u32[]{:S(2)}) %collective-permute-start.29) | collective-permute-done | bytes 786464 | tf_op jit(solution)/shard_map/ppermute | solution.py:674
  229.7 1.6 add_convert_fusion.1.refs_0_
  232.1 5.3 %collective-permute-done.43 = bf16[1,1,104,768]{3,2,1,0:T(8,128)(2,1)S(1)} collective-permute-done((bf16[1,1,104,768]{3,2,1,0:T(8,128)(2,1)S(1)}, bf16[1,1,104,768]{3,2,1,0:T(8,128)(2,1)S(1)}, u32[]{:S(2)}, u32[]{:S(2)}) %collective-permute-start.43) | collective-permute-done | bytes 159776 | tf_op jit(solution)/shard_map/ppermute | solution.py:677
  238.6 4.5 %collective-permute-done.32 = bf16[512,768]{1,0:T(8,128)(2,1)S(1)} collective-permute-done((bf16[512,768]{1,0:T(8,128)(2,1)S(1)}, bf16[512,768]{1,0:T(8,128)(2,1)S(1)}, u32[]{:S(2)}, u32[]{:S(2)}) %collective-permute-start.32) | collective-permute-done | bytes 786464 | tf_op jit(solution)/shard_map/ppermute | solution.py:674
  243.1 1.6 add_convert_fusion.refs_2_
  246.6 2.7 %place.2 = bf16[2048,768]{1,0:T(8,128)(2,1)} custom-call(s32[6]{0:T(128)S(1)} %concatenate.24.meta_ref, bf16[512,768]{1,0:T(8,128)(2,1)S(1)} %copy-done.7, bf16[512,768]{1,0:T(8,128)(2,1)S(1)} %collective-permute-done.26.refs_1_, bf16[512,768]{1,0:T(8,128)(2,1)S(1)} %copy-done.9, bf16[512,768]{1,0:T(8,128)(2,1)S(1)} %collective-permute-done.27.refs_3_), custom_call_target="tpu_custom_call" | custom-call | flops 3300000000 | bytes 1024 | tf_op jit(solution)/shard_map/place/pallas_call | solution.py:70
  249.3 1.6 convert_element_type.97
  250.9 2.7 %place.3 = bf16[2048,768]{1,0:T(8,128)(2,1)} custom-call(s32[6]{0:T(128)S(1)} %concatenate.24.meta_ref, bf16[512,768]{1,0:T(8,128)(2,1)S(1)} %add_convert_fusion.1.refs_0_, bf16[512,768]{1,0:T(8,128)(2,1)S(1)} %collective-permute-done.30.refs_1_, bf16[512,768]{1,0:T(8,128)(2,1)S(1)} %add_convert_fusion.refs_2_, ...), custom_call_target="tpu_custom_call" | custom-call | flops 3300000000 | bytes 1024 | tf_op jit(solution)/shard_map/place/pallas_call | solution.py:70
  253.6 8.4 %collective-permute-done.46 = bf16[1,4,104,768]{3,2,1,0:T(8,128)(2,1)S(1)} collective-permute-done((bf16[1,4,104,768]{3,2,1,0:T(8,128)(2,1)S(1)}, bf16[1,4,104,768]{3,2,1,0:T(8,128)(2,1)S(1)}, u32[]{:S(2)}, u32[]{:S(2)}) %collective-permute-start.46) | collective-permute-done | bytes 639008 | tf_op jit(solution)/shard_map/ppermute | solution.py:677
  262.2 1.4 slice_convert_fusion
  264.7 1.7 bitcast_convert_fusion
  (218 shorter events, 39.9 us)
Async XLA Ops:
  0.6 16.7 %collective-permute-start = (bf16[192,768]{1,0:T(8,128)(2,1)}, bf16[192,768]{1,0:T(8,128)(2,1)S(1)}, u32[]{:S(2)}, u32[]{:S(2)}) collective-permute-start(bf16[192,768]{1,0:T(8,128)(2,1)} %w0.7), channel_id=1, source_target_pairs={{0,1},{1,0},{2,3},{3,2},{4,5},{5,4},{6,7},{7,6},{8,9},{9,8},{10,11... | collective-permute-start | bytes 884744 | tf_op jit(solution)/shard_map/ppermute | solution.py:674
  1.2 16.4 %collective-permute-start.1 = (bf16[192,768]{1,0:T(8,128)(2,1)}, bf16[192,768]{1,0:T(8,128)(2,1)S(1)}, u32[]{:S(2)}, u32[]{:S(2)}) collective-permute-start(bf16[192,768]{1,0:T(8,128)(2,1)} %w0.7), channel_id=1, source_target_pairs={{0,2},{1,3},{2,0},{3,1},{4,6},{5,7},{6,4},{7,5},{8,10},{9,11},{10,... | collective-permute-start | bytes 884744 | tf_op jit(solution)/shard_map/ppermute | solution.py:674
  3.7 15.6 %collective-permute-start.2 = (bf16[192,768]{1,0:T(8,128)(2,1)}, bf16[192,768]{1,0:T(8,128)(2,1)S(1)}, u32[]{:S(2)}, u32[]{:S(2)}) collective-permute-start(bf16[192,768]{1,0:T(8,128)(2,1)} %w0.7), channel_id=1, source_target_pairs={{0,3},{1,2},{2,1},{3,0},{4,7},{5,6},{6,5},{7,4},{8,11},{9,10},{10,... | collective-permute-start | bytes 884744 | tf_op jit(solution)/shard_map/ppermute | solution.py:674
  3.8 20.2 %collective-permute-start.3 = (bf16[768,768]{1,0:T(8,128)(2,1)}, bf16[768,768]{1,0:T(8,128)(2,1)S(1)}, u32[]{:S(2)}, u32[]{:S(2)}) collective-permute-start(bf16[768,768]{1,0:T(8,128)(2,1)} %ua_ref.7), channel_id=1, source_target_pairs={{0,1},{1,0},{2,3},{3,2},{4,5},{5,4},{6,7},{7,6},{8,9},{9,8},{10,11... | collective-permute-start | bytes 3538952 | tf_op jit(solution)/shard_map/ppermute | solution.py:674
  3.9 21.1 %collective-permute-start.4 = (bf16[768,768]{1,0:T(8,128)(2,1)}, bf16[768,768]{1,0:T(8,128)(2,1)S(1)}, u32[]{:S(2)}, u32[]{:S(2)}) collective-permute-start(bf16[768,768]{1,0:T(8,128)(2,1)} %da_ref.7), channel_id=1, source_target_pairs={{0,1},{1,0},{2,3},{3,2},{4,5},{5,4},{6,7},{7,6},{8,9},{9,8},{10,11... | collective-permute-start | bytes 3538952 | tf_op jit(solution)/shard_map/ppermute | solution.py:674
  17.4 19.4 %collective-permute-start.5 = (bf16[192,512]{1,0:T(8,128)(2,1)S(1)}, bf16[192,512]{1,0:T(8,128)(2,1)S(1)}, u32[]{:S(2)}, u32[]{:S(2)}) collective-permute-start(bf16[192,512]{1,0:T(8,128)(2,1)S(1)} %get-tuple-element.159.o1_ref), channel_id=1, source_target_pairs={{0,1},{1,0},{2,3},{3,2},{4,5},{5,4},{6,7},{7,6},{8,9},{9,8},{10,11... | collective-permute-start | bytes 589832 | tf_op jit(solution)/shard_map/ppermute | solution.py:674
  17.6 19.5 %collective-permute-start.7 = (bf16[192,512]{1,0:T(8,128)(2,1)S(1)}, bf16[192,512]{1,0:T(8,128)(2,1)S(1)}, u32[]{:S(2)}, u32[]{:S(2)}) collective-permute-start(bf16[192,512]{1,0:T(8,128)(2,1)S(1)} %get-tuple-element.159.o1_ref), channel_id=1, source_target_pairs={{0,3},{1,2},{2,1},{3,0},{4,7},{5,6},{6,5},{7,4},{8,11},{9,10},{10,... | collective-permute-start | bytes 589832 | tf_op jit(solution)/shard_map/ppermute | solution.py:674
  19.3 17.8 %collective-permute-start.6 = (bf16[192,512]{1,0:T(8,128)(2,1)S(1)}, bf16[192,512]{1,0:T(8,128)(2,1)S(1)}, u32[]{:S(2)}, u32[]{:S(2)}) collective-permute-start(bf16[192,512]{1,0:T(8,128)(2,1)S(1)} %get-tuple-element.151.a0.o0_ref), channel_id=1, source_target_pairs={{0,2},{1,3},{2,0},{3,1},{4,6},{5,7},{6,4},{7,5},{8,10},{9,11},{10,... | collective-permute-start | bytes 589832 | tf_op jit(solution)/shard_map/ppermute | solution.py:674
  35.0 13.6 %collective-permute-start.10 = (bf16[192,512]{1,0:T(8,128)(2,1)S(1)}, bf16[192,512]{1,0:T(8,128)(2,1)S(1)}, u32[]{:S(2)}, u32[]{:S(2)}) collective-permute-start(bf16[192,512]{1,0:T(8,128)(2,1)S(1)} %get-tuple-element.162.o1_ref), channel_id=1, source_target_pairs={{0,3},{1,2},{2,1},{3,0},{4,7},{5,6},{6,5},{7,4},{8,11},{9,10},{10,... | collective-permute-start | bytes 589832 | tf_op jit(solution)/shard_map/ppermute | solution.py:674
  36.4 12.2 %collective-permute-start.8 = (bf16[192,512]{1,0:T(8,128)(2,1)S(1)}, bf16[192,512]{1,0:T(8,128)(2,1)S(1)}, u32[]{:S(2)}, u32[]{:S(2)}) collective-permute-start(bf16[192,512]{1,0:T(8,128)(2,1)S(1)} %get-tuple-element.162.o1_ref), channel_id=1, source_target_pairs={{0,1},{1,0},{2,3},{3,2},{4,5},{5,4},{6,7},{7,6},{8,9},{9,8},{10,11... | collective-permute-start | bytes 589832 | tf_op jit(solution)/shard_map/ppermute | solution.py:674
  36.8 11.8 %collective-permute-start.9 = (bf16[192,512]{1,0:T(8,128)(2,1)S(1)}, bf16[192,512]{1,0:T(8,128)(2,1)S(1)}, u32[]{:S(2)}, u32[]{:S(2)}) collective-permute-start(bf16[192,512]{1,0:T(8,128)(2,1)S(1)} %get-tuple-element.157.a0.o0_ref), channel_id=1, source_target_pairs={{0,2},{1,3},{2,0},{3,1},{4,6},{5,7},{6,4},{7,5},{8,10},{9,11},{10,... | collective-permute-start | bytes 589832 | tf_op jit(solution)/shard_map/ppermute | solution.py:674
  46.9 20.4 %collective-permute-start.11 = (bf16[512,768]{1,0:T(8,128)(2,1)S(1)}, bf16[512,768]{1,0:T(8,128)(2,1)S(1)}, u32[]{:S(2)}, u32[]{:S(2)}) collective-permute-start(bf16[512,768]{1,0:T(8,128)(2,1)S(1)} %get-tuple-element.166), channel_id=1, source_target_pairs={{0,2},{1,3},{2,0},{3,1},{4,6},{5,7},{6,4},{7,5},{8,10},{9,11},{10,... | collective-permute-start | bytes 2359304 | tf_op jit(solution)/shard_map/ppermute | solution.py:674
  58.5 25.7 %collective-permute-start.12 = (bf16[512,768]{1,0:T(8,128)(2,1)S(1)}, bf16[512,768]{1,0:T(8,128)(2,1)S(1)}, u32[]{:S(2)}, u32[]{:S(2)}) collective-permute-start(bf16[512,768]{1,0:T(8,128)(2,1)S(1)} %get-tuple-element.177), channel_id=1, source_target_pairs={{0,2},{1,3},{2,0},{3,1},{4,6},{5,7},{6,4},{7,5},{8,10},{9,11},{10,... | collective-permute-start | bytes 2359304 | tf_op jit(solution)/shard_map/ppermute | solution.py:674
  79.5 21.0 %collective-permute-start.13 = (bf16[512,768]{1,0:T(8,128)(2,1)S(1)}, bf16[512,768]{1,0:T(8,128)(2,1)S(1)}, u32[]{:S(2)}, u32[]{:S(2)}) collective-permute-start(bf16[512,768]{1,0:T(8,128)(2,1)S(1)} %get-tuple-element.187), channel_id=1, source_target_pairs={{0,2},{1,3},{2,0},{3,1},{4,6},{5,7},{6,4},{7,5},{8,10},{9,11},{10,... | collective-permute-start | bytes 2359304 | tf_op jit(solution)/shard_map/ppermute | solution.py:674
  101.4 13.5 %collective-permute-start.15 = (bf16[768,768]{1,0:T(8,128)(2,1)}, bf16[768,768]{1,0:T(8,128)(2,1)S(1)}, u32[]{:S(2)}, u32[]{:S(2)}) collective-permute-start(bf16[768,768]{1,0:T(8,128)(2,1)} %get-tuple-element.200), channel_id=1, source_target_pairs={{0,1},{1,0},{2,3},{3,2},{4,5},{5,4},{6,7},{7,6},{8,9},{9,8},{10,11... | collective-permute-start | bytes 3538952 | tf_op jit(solution)/shard_map/ppermute | solution.py:674
  101.4 13.5 %collective-permute-start.14 = (bf16[768,768]{1,0:T(8,128)(2,1)}, bf16[768,768]{1,0:T(8,128)(2,1)S(1)}, u32[]{:S(2)}, u32[]{:S(2)}) collective-permute-start(bf16[768,768]{1,0:T(8,128)(2,1)} %get-tuple-element.196), channel_id=1, source_target_pairs={{0,1},{1,0},{2,3},{3,2},{4,5},{5,4},{6,7},{7,6},{8,9},{9,8},{10,11... | collective-permute-start | bytes 3538952 | tf_op jit(solution)/shard_map/ppermute | solution.py:674
  113.2 19.9 %collective-permute-start.19 = (bf16[512,768]{1,0:T(8,128)(2,1)S(1)}, bf16[512,768]{1,0:T(8,128)(2,1)S(1)}, u32[]{:S(2)}, u32[]{:S(2)}) collective-permute-start(bf16[512,768]{1,0:T(8,128)(2,1)S(1)} %get-tuple-element.221), channel_id=1, source_target_pairs={{0,2},{1,3},{2,0},{3,1},{4,6},{5,7},{6,4},{7,5},{8,10},{9,11},{10,... | collective-permute-start | bytes 2359304 | tf_op jit(solution)/shard_map/ppermute | solution.py:674
  114.9 1.4 collective-permute-start.16
  116.0 15.9 %collective-permute-start.17 = (bf16[384,768]{1,0:T(8,128)(2,1)S(1)}, bf16[384,768]{1,0:T(8,128)(2,1)S(1)}, u32[]{:S(2)}, u32[]{:S(2)}) collective-permute-start(bf16[384,768]{1,0:T(8,128)(2,1)S(1)} %get-tuple-element.203), channel_id=1, source_target_pairs={{0,4},{4,0},{8,12},{12,8},{16,20},{20,16},{24,28},{28,24},{1,5},{5... | collective-permute-start | bytes 1769480 | tf_op jit(solution)/shard_map/ppermute | solution.py:677
  116.1 15.8 %collective-permute-start.18 = (bf16[384,768]{1,0:T(8,128)(2,1)S(1)}, bf16[384,768]{1,0:T(8,128)(2,1)S(1)}, u32[]{:S(2)}, u32[]{:S(2)}) collective-permute-start(bf16[384,768]{1,0:T(8,128)(2,1)S(1)} %get-tuple-element.214), channel_id=1, source_target_pairs={{0,8},{4,12},{8,0},{12,4},{16,24},{20,28},{24,16},{28,20},{1,9},{5... | collective-permute-start | bytes 1769480 | tf_op jit(solution)/shard_map/ppermute | solution.py:677
  132.7 14.4 %collective-permute-start.20 = (bf16[192,768]{1,0:T(8,128)(2,1)S(1)}, bf16[192,768]{1,0:T(8,128)(2,1)S(1)}, u32[]{:S(2)}, u32[]{:S(2)}) collective-permute-start(bf16[192,768]{1,0:T(8,128)(2,1)S(1)} %get-tuple-element.217), channel_id=1, source_target_pairs={{0,8},{4,12},{8,0},{12,4},{16,24},{20,28},{24,16},{28,20},{1,9},{5... | collective-permute-start | bytes 884744 | tf_op jit(solution)/shard_map/ppermute | solution.py:677
  137.9 9.2 %collective-permute-start.21 = (bf16[192,768]{1,0:T(8,128)(2,1)S(1)}, bf16[192,768]{1,0:T(8,128)(2,1)S(1)}, u32[]{:S(2)}, u32[]{:S(2)}) collective-permute-start(bf16[192,768]{1,0:T(8,128)(2,1)S(1)} %get-tuple-element.238), channel_id=1, source_target_pairs={{0,4},{4,0},{8,12},{12,8},{16,20},{20,16},{24,28},{28,24},{1,5},{5... | collective-permute-start | bytes 884744 | tf_op jit(solution)/shard_map/ppermute | solution.py:677
  146.6 29.8 %collective-permute-start.28 = (bf16[512,768]{1,0:T(8,128)(2,1)}, bf16[512,768]{1,0:T(8,128)(2,1)}, u32[]{:S(2)}, u32[]{:S(2)}) collective-permute-start(bf16[512,768]{1,0:T(8,128)(2,1)} %get-tuple-element.232), channel_id=1, source_target_pairs={{0,1},{1,0},{2,3},{3,2},{4,5},{5,4},{6,7},{7,6},{8,9},{9,8},{10,11... | collective-permute-start | bytes 2359304 | tf_op jit(solution)/shard_map/ppermute | solution.py:674
  146.6 21.0 %collective-permute-start.25 = (bf16[256,768]{1,0:T(8,128)(2,1)S(1)}, bf16[256,768]{1,0:T(8,128)(2,1)S(1)}, u32[]{:S(2)}, u32[]{:S(2)}) collective-permute-start(bf16[256,768]{1,0:T(8,128)(2,1)S(1)} %get-tuple-element.262), channel_id=1, source_target_pairs={{0,1},{1,0},{2,3},{3,2},{4,5},{5,4},{6,7},{7,6},{8,9},{9,8},{10,11... | collective-permute-start | bytes 1179656 | tf_op jit(solution)/shard_map/ppermute | solution.py:674
  147.1 6.0 %collective-permute-start.22 = (bf16[192,512]{1,0:T(8,128)(2,1)S(1)}, bf16[192,512]{1,0:T(8,128)(2,1)S(1)}, u32[]{:S(2)}, u32[]{:S(2)}) collective-permute-start(bf16[192,512]{1,0:T(8,128)(2,1)S(1)} %get-tuple-element.244), channel_id=1, source_target_pairs={{0,1},{1,0},{2,3},{3,2},{4,5},{5,4},{6,7},{7,6},{8,9},{9,8},{10,11... | collective-permute-start | bytes 589832 | tf_op jit(solution)/shard_map/ppermute | solution.py:674
  147.9 19.2 %collective-permute-start.23 = (bf16[96,768]{1,0:T(8,128)(2,1)S(1)}, bf16[96,768]{1,0:T(8,128)(2,1)S(1)}, u32[]{:S(2)}, u32[]{:S(2)}) collective-permute-start(bf16[96,768]{1,0:T(8,128)(2,1)S(1)} %get-tuple-element.241), channel_id=1, source_target_pairs={{0,16},{4,20},{8,24},{12,28},{16,0},{20,4},{24,8},{28,12},{1,17},{... | collective-permute-start | bytes 442376 | tf_op jit(solution)/shard_map/ppermute | solution.py:677
  153.0 14.0 %collective-permute-start.24 = (bf16[96,768]{1,0:T(8,128)(2,1)S(1)}, bf16[96,768]{1,0:T(8,128)(2,1)S(1)}, u32[]{:S(2)}, u32[]{:S(2)}) collective-permute-start(bf16[96,768]{1,0:T(8,128)(2,1)S(1)} %get-tuple-element.252), channel_id=1, source_target_pairs={{0,16},{4,20},{8,24},{12,28},{16,0},{20,4},{24,8},{28,12},{1,17},{... | collective-permute-start | bytes 442376 | tf_op jit(solution)/shard_map/ppermute | solution.py:677
  175.5 16.5 %collective-permute-start.34 = (bf16[416,768]{1,0:T(8,128)(2,1)}, bf16[416,768]{1,0:T(8,128)(2,1)}, u32[]{:S(2)}, u32[]{:S(2)}) collective-permute-start(bf16[416,768]{1,0:T(8,128)(2,1)} %constant_dynamic-slice_fusion.3), channel_id=1, source_target_pairs={{0,4},{4,0},{8,12},{12,8},{16,20},{20,16},{24,28},{28,24},{1,5},{5... | collective-permute-start | bytes 1916936 | tf_op jit(solution)/shard_map/ppermute | solution.py:677
  175.9 17.4 %collective-permute-start.31 = (bf16[512,768]{1,0:T(8,128)(2,1)}, bf16[512,768]{1,0:T(8,128)(2,1)}, u32[]{:S(2)}, u32[]{:S(2)}) collective-permute-start(bf16[512,768]{1,0:T(8,128)(2,1)} %get-tuple-element.263), channel_id=1, source_target_pairs={{0,1},{1,0},{2,3},{3,2},{4,5},{5,4},{6,7},{7,6},{8,9},{9,8},{10,11... | collective-permute-start | bytes 2359304 | tf_op jit(solution)/shard_map/ppermute | solution.py:674
  175.9 69.7 %collective-permute-start.26 = (bf16[512,768]{1,0:T(8,128)(2,1)}, bf16[512,768]{1,0:T(8,128)(2,1)S(1)}, u32[]{:S(2)}, u32[]{:S(2)}) collective-permute-start(bf16[512,768]{1,0:T(8,128)(2,1)} %copy-done.6), channel_id=1, source_target_pairs={{0,1},{1,0},{2,3},{3,2},{4,5},{5,4},{6,7},{7,6},{8,9},{9,8},{10,11... | collective-permute-start | bytes 2359304 | tf_op jit(solution)/shard_map/ppermute | solution.py:674
  176.4 16.9 %collective-permute-start.36 = (bf16[1,1,1,96,768]{4,3,2,1,0:T(8,128)(2,1)S(1)}, bf16[1,1,1,96,768]{4,3,2,1,0:T(8,128)(2,1)S(1)}, u32[]{:S(2)}, u32[]{:S(2)}) collective-permute-start(bf16[1,1,1,96,768]{4,3,2,1,0:T(8,128)(2,1)S(1)} %bitcast.27), channel_id=1, source_target_pairs={{0,16},{4,20},{8,24},{12,28},{16,0},{20,4},{24,8},{28,12},{1,17},{... | collective-permute-start | bytes 442376 | tf_op jit(solution)/shard_map/ppermute | solution.py:677
  176.4 16.9 %collective-permute-start.35 = (bf16[1,1,1,96,768]{4,3,2,1,0:T(8,128)(2,1)S(1)}, bf16[1,1,1,96,768]{4,3,2,1,0:T(8,128)(2,1)S(1)}, u32[]{:S(2)}, u32[]{:S(2)}) collective-permute-start(bf16[1,1,1,96,768]{4,3,2,1,0:T(8,128)(2,1)S(1)} %bitcast.26), channel_id=1, source_target_pairs={{0,16},{4,20},{8,24},{12,28},{16,0},{20,4},{24,8},{28,12},{1,17},{... | collective-permute-start | bytes 442376 | tf_op jit(solution)/shard_map/ppermute | solution.py:677
  193.5 18.5 %collective-permute-start.41 = (bf16[1,1,2,96,768]{4,3,2,1,0:T(8,128)(2,1)S(1)}, bf16[1,1,2,96,768]{4,3,2,1,0:T(8,128)(2,1)S(1)}, u32[]{:S(2)}, u32[]{:S(2)}) collective-permute-start(bf16[1,1,2,96,768]{4,3,2,1,0:T(8,128)(2,1)S(1)} %get-tuple-element.273), channel_id=1, source_target_pairs={{0,4},{4,0},{8,12},{12,8},{16,20},{20,16},{24,28},{28,24},{1,5},{5... | collective-permute-start | bytes 884744 | tf_op jit(solution)/shard_map/ppermute | solution.py:677
  194.4 7.9 %collective-permute-start.37 = (bf16[104,768]{1,0:T(8,128)(2,1)S(1)}, bf16[104,768]{1,0:T(8,128)(2,1)S(1)}, u32[]{:S(2)}, u32[]{:S(2)}) collective-permute-start(bf16[104,768]{1,0:T(8,128)(2,1)S(1)} %get-tuple-element.296), channel_id=1, source_target_pairs={{0,8},{4,12},{8,0},{12,4},{16,24},{20,28},{24,16},{28,20},{1,9},{5... | collective-permute-start | bytes 479240 | tf_op jit(solution)/shard_map/ppermute | solution.py:677
  194.5 14.7 %collective-permute-start.38 = (bf16[104,768]{1,0:T(8,128)(2,1)S(1)}, bf16[104,768]{1,0:T(8,128)(2,1)S(1)}, u32[]{:S(2)}, u32[]{:S(2)}) collective-permute-start(bf16[104,768]{1,0:T(8,128)(2,1)S(1)} %get-tuple-element.298), channel_id=1, source_target_pairs={{0,16},{4,20},{8,24},{12,28},{16,0},{20,4},{24,8},{28,12},{1,17},{... | collective-permute-start | bytes 479240 | tf_op jit(solution)/shard_map/ppermute | solution.py:677
  197.1 12.6 %collective-permute-start.39 = (bf16[104,768]{1,0:T(8,128)(2,1)S(1)}, bf16[104,768]{1,0:T(8,128)(2,1)S(1)}, u32[]{:S(2)}, u32[]{:S(2)}) collective-permute-start(bf16[104,768]{1,0:T(8,128)(2,1)S(1)} %get-tuple-element.297), channel_id=1, source_target_pairs={{0,24},{4,28},{8,16},{12,20},{16,8},{20,12},{24,0},{28,4},{1,25},{... | collective-permute-start | bytes 479240 | tf_op jit(solution)/shard_map/ppermute | solution.py:677
  202.3 43.3 %collective-permute-start.27 = (bf16[512,768]{1,0:T(8,128)(2,1)S(1)}, bf16[512,768]{1,0:T(8,128)(2,1)S(1)}, u32[]{:S(2)}, u32[]{:S(2)}) collective-permute-start(bf16[512,768]{1,0:T(8,128)(2,1)S(1)} %copy-done.9), channel_id=1, source_target_pairs={{0,1},{1,0},{2,3},{3,2},{4,5},{5,4},{6,7},{7,6},{8,9},{9,8},{10,11... | collective-permute-start | bytes 2359304 | tf_op jit(solution)/shard_map/ppermute | solution.py:674
  209.2 20.5 %collective-permute-start.29 = (bf16[512,768]{1,0:T(8,128)(2,1)S(1)}, bf16[512,768]{1,0:T(8,128)(2,1)S(1)}, u32[]{:S(2)}, u32[]{:S(2)}) collective-permute-start(bf16[512,768]{1,0:T(8,128)(2,1)S(1)} %fusion), channel_id=1, source_target_pairs={{0,2},{1,3},{2,0},{3,1},{4,6},{5,7},{6,4},{7,5},{8,10},{9,11},{10,... | collective-permute-start | bytes 2359304 | tf_op jit(solution)/shard_map/ppermute | solution.py:674
  209.7 8.2 %collective-permute-start.40 = (bf16[1,1,2,96,768]{4,3,2,1,0:T(8,128)(2,1)S(1)}, bf16[1,1,2,96,768]{4,3,2,1,0:T(8,128)(2,1)S(1)}, u32[]{:S(2)}, u32[]{:S(2)}) collective-permute-start(bf16[1,1,2,96,768]{4,3,2,1,0:T(8,128)(2,1)S(1)} %get-tuple-element.272), channel_id=1, source_target_pairs={{0,8},{4,12},{8,0},{12,4},{16,24},{20,28},{24,16},{28,20},{1,9},{5... | collective-permute-start | bytes 884744 | tf_op jit(solution)/shard_map/ppermute | solution.py:677
  212.0 31.1 %collective-permute-start.32 = (bf16[512,768]{1,0:T(8,128)(2,1)S(1)}, bf16[512,768]{1,0:T(8,128)(2,1)S(1)}, u32[]{:S(2)}, u32[]{:S(2)}) collective-permute-start(bf16[512,768]{1,0:T(8,128)(2,1)S(1)} %fusion.1), channel_id=1, source_target_pairs={{0,2},{1,3},{2,0},{3,1},{4,6},{5,7},{6,4},{7,5},{8,10},{9,11},{10,... | collective-permute-start | bytes 2359304 | tf_op jit(solution)/shard_map/ppermute | solution.py:674
  218.1 13.2 %collective-permute-start.42 = (bf16[1,1,104,768]{3,2,1,0:T(8,128)(2,1)S(1)}, bf16[1,1,104,768]{3,2,1,0:T(8,128)(2,1)S(1)}, u32[]{:S(2)}, u32[]{:S(2)}) collective-permute-start(bf16[1,1,104,768]{3,2,1,0:T(8,128)(2,1)S(1)} %fusion.2), channel_id=1, source_target_pairs={{0,8},{4,12},{8,0},{12,4},{16,24},{20,28},{24,16},{28,20},{1,9},{5... | collective-permute-start | bytes 479240 | tf_op jit(solution)/shard_map/ppermute | solution.py:677
  229.7 7.8 %collective-permute-start.43 = (bf16[1,1,104,768]{3,2,1,0:T(8,128)(2,1)S(1)}, bf16[1,1,104,768]{3,2,1,0:T(8,128)(2,1)S(1)}, u32[]{:S(2)}, u32[]{:S(2)}) collective-permute-start(bf16[1,1,104,768]{3,2,1,0:T(8,128)(2,1)S(1)} %fusion.2), channel_id=1, source_target_pairs={{0,16},{4,20},{8,24},{12,28},{16,0},{20,4},{24,8},{28,12},{1,17},{... | collective-permute-start | bytes 479240 | tf_op jit(solution)/shard_map/ppermute | solution.py:677
  231.2 14.0 %collective-permute-start.45 = (bf16[1,2,2,96,768]{4,3,2,1,0:T(8,128)(2,1)S(1)}, bf16[1,2,2,96,768]{4,3,2,1,0:T(8,128)(2,1)S(1)}, u32[]{:S(2)}, u32[]{:S(2)}) collective-permute-start(bf16[1,2,2,96,768]{4,3,2,1,0:T(8,128)(2,1)S(1)} %pad_maximum_fusion.3), channel_id=1, source_target_pairs={{0,4},{4,0},{8,12},{12,8},{16,20},{20,16},{24,28},{28,24},{1,5},{5... | collective-permute-start | bytes 1769480 | tf_op jit(solution)/shard_map/ppermute | solution.py:677
  237.5 7.2 %collective-permute-start.44 = (bf16[1,1,104,768]{3,2,1,0:T(8,128)(2,1)S(1)}, bf16[1,1,104,768]{3,2,1,0:T(8,128)(2,1)S(1)}, u32[]{:S(2)}, u32[]{:S(2)}) collective-permute-start(bf16[1,1,104,768]{3,2,1,0:T(8,128)(2,1)S(1)} %fusion.2), channel_id=1, source_target_pairs={{0,24},{4,28},{8,16},{12,20},{16,8},{20,12},{24,0},{28,4},{1,25},{... | collective-permute-start | bytes 479240 | tf_op jit(solution)/shard_map/ppermute | solution.py:677
  243.1 7.8 %collective-permute-start.30 = (bf16[512,768]{1,0:T(8,128)(2,1)S(1)}, bf16[512,768]{1,0:T(8,128)(2,1)S(1)}, u32[]{:S(2)}, u32[]{:S(2)}) collective-permute-start(bf16[512,768]{1,0:T(8,128)(2,1)S(1)} %add_convert_fusion.1.refs_0_), channel_id=1, source_target_pairs={{0,1},{1,0},{2,3},{3,2},{4,5},{5,4},{6,7},{7,6},{8,9},{9,8},{10,11... | collective-permute-start | bytes 2359304 | tf_op jit(solution)/shard_map/ppermute | solution.py:674
  244.7 6.2 %collective-permute-start.33 = (bf16[512,768]{1,0:T(8,128)(2,1)S(1)}, bf16[512,768]{1,0:T(8,128)(2,1)S(1)}, u32[]{:S(2)}, u32[]{:S(2)}) collective-permute-start(bf16[512,768]{1,0:T(8,128)(2,1)S(1)} %add_convert_fusion.refs_2_), channel_id=1, source_target_pairs={{0,1},{1,0},{2,3},{3,2},{4,5},{5,4},{6,7},{7,6},{8,9},{9,8},{10,11... | collective-permute-start | bytes 2359304 | tf_op jit(solution)/shard_map/ppermute | solution.py:674
  245.6 16.4 %collective-permute-start.46 = (bf16[1,4,104,768]{3,2,1,0:T(8,128)(2,1)S(1)}, bf16[1,4,104,768]{3,2,1,0:T(8,128)(2,1)S(1)}, u32[]{:S(2)}, u32[]{:S(2)}) collective-permute-start(bf16[1,4,104,768]{3,2,1,0:T(8,128)(2,1)S(1)} %constant_dynamic-update-slice_fusion), channel_id=1, source_target_pairs={{0,4},{4,0},{8,12},{12,8},{16,20},{20,16},{24,28},{28,24},{1,5},{5... | collective-permute-start | bytes 1916936 | tf_op jit(solution)/shard_map/ppermute | solution.py:677
  249.3 15.3 %collective-permute-start.47 = (bf16[1,2,2,96,768]{4,3,2,1,0:T(8,128)(2,1)S(1)}, bf16[1,2,2,96,768]{4,3,2,1,0:T(8,128)(2,1)S(1)}, u32[]{:S(2)}, u32[]{:S(2)}) collective-permute-start(bf16[1,2,2,96,768]{4,3,2,1,0:T(8,128)(2,1)S(1)} %pad_maximum_fusion.4), channel_id=1, source_target_pairs={{0,8},{4,12},{8,0},{12,4},{16,24},{20,28},{24,16},{28,20},{1,9},{5... | collective-permute-start | bytes 1769480 | tf_op jit(solution)/shard_map/ppermute | solution.py:677
  (56 other events, 348.6 us)

commit v10 on v9

--- a/solution.py
+++ b/solution.py
@@ -454,15 +454,18 @@
             like((half, d), BF),
         ],
         far=(0,),
-        out=(1, 2, 3, 4, 5),
-        out_far=(0,),
+        out=(2, 3, 4, 5),
+        out_far=(0, 1),
     )
 
 
 def astern_kernel(u, meta_ref, own_ref, far_ref, grad_ref, span_ref, ua_ref, ub_ref, da_ref, db_ref, slope_ref, vec_ref, *refs):
     last = len(refs) > 6
-    before = refs[: len(refs) - 10] if last else ()
-    out_ref, g_ref, pre_ref, back_ref, sent_ref, small_ref = refs[len(before) : len(before) + 6]
+    if last:
+        before = refs[:-10]
+        out_ref, back_ref, sent_ref, small_ref, *sums, g_ref, pre_ref = refs[-10:]
+    else:
+        out_ref, g_ref, pre_ref, back_ref, sent_ref, small_ref = refs
     gain, bias = vec_ref[2:3, :], vec_ref[3:4, :]
     half, d = own_ref.shape
     hidden = ua_ref.shape[1]
@@ -500,7 +503,7 @@
     small_ref[1:2, :] = bias_grad
     if last:
         x_ref, act_ref = before[:2]
-        weight_sums(x_ref[...], g_ref[...], act_ref, pre_ref, before[2:], refs[-4:])
+        weight_sums(x_ref[...], g_ref[...], act_ref, pre_ref, before[2:], sums)
 
 
 def astern(meta, own, far, grad, spans, up, down, slope, vectors, u, before):
@@ -510,6 +513,9 @@
     wide = fixed(half, 2 * hidden)
     grads = [] if not before else [(d, hidden)] * 2 + [(hidden, d)] * 2
     extra = [] if not before else [rows, wide] + [fixed(*shape) for shape in grads[: len(before) - 2]]
+    made = [like((half, d), BF), like((half, 2 * hidden), BF)]
+    others = [like((half, d), F32), like((half, d), BF), like((2, d), F32)]
+    shapes = [like((half, d), BF)] + ([] if before else made) + others + [like(shape, BF) for shape in grads]
     return call(
         functools.partial(astern_kernel, u),
         "astern",
@@ -522,20 +528,14 @@
         + [fixed(hidden, d)] * 2
         + [wide, fixed(4, d)]
         + extra,
-        [rows, rows, wide, rows, rows, fixed(2, d)] + [fixed(*shape) for shape in grads],
-        [
-            like((half, d), BF),
-            like((half, d), BF),
-            like((half, 2 * hidden), BF),
-            like((half, d), F32),
-            like((half, d), BF),
-            like((2, d), F32),
-        ]
-        + [like(shape, BF) for shape in grads],
-        limit=12 if before else VMEM,
+        [fixed(*shape.shape) for shape in shapes],
+        shapes,
+        [pltpu.VMEM(shape.shape, shape.dtype) for shape in made] if before else (),
+        limit=20 if before else VMEM,
         hold=(0, 8, *range(10, 10 + len(before))),
         far=(2,),
-        out=(3,) if before else (1, 2, 3),
+        out=() if before else (1, 2),
+        out_far=(0, 1) if before else (0, 3),
     )
 
 
@@ -623,10 +623,9 @@
         + ([fixed(192, d)] * 2 + [fixed(2, d)] * 3 if before else []),
         [fixed(rows, d), fixed(192, rows), fixed(192, rows), fixed(*merge.shape), fixed(*merge.shape), fixed(2, d)],
         [like((rows, d), F32), like((192, rows), BF), like((192, rows), BF), merge, merge, like((2, d), F32)],
-        hold=(0, 3, 9, 10) if before else (0, 3),
-        far=(2,),
-        out=(1,) if before else (1, 3, 4),
-        out_far=(0,),
+        far=(0, 2, 3, 5, 6, 7, 8, *((9, 10) if before else ())),
+        out=(1,),
+        out_far=(0,) if before else (0, 3, 4),
     )
 
 
@@ -771,18 +770,22 @@
     for u in range(seqs):
         front.append(done(ahead(meta(), tokens, att[u], merge_w, up_w, down_w, vectors, u)))
         far.append(swap(front[u][6], 2))
-    back, far_grad, sums = [], [], ()
+    out_rows, back, far_grad, smalls, sums = [], [], [], [], ()
     for u in range(seqs):
-        before = (front[u][2], front[u][3], *sums) if u == seqs - 1 else ()
-        back.append(
-            done(astern(meta(), front[u][5], far[u], out_grad, span_starts, up_w, down_w, front[u][4], vectors, u, before))
-        )
-        if u < seqs - 1:
-            far_grad.append(swap(back[u][4], 2))
-            sums = done(weight_grads(meta(), front[u][2], back[u][1], front[u][3], back[u][2], sums))
+        last = u == seqs - 1
+        before = (front[u][2], front[u][3], *sums) if last else ()
+        res = done(astern(meta(), front[u][5], far[u], out_grad, span_starts, up_w, down_w, front[u][4], vectors, u, before))
+        out_rows.append(res[0])
+        back.append(res[1 if last else 3])
+        smalls.append(res[3 if last else 5])
+        if last:
+            sent, sums = res[2], res[4:]
+        else:
+            far_grad.append(swap(res[4], 2))
+            sums = done(weight_grads(meta(), front[u][2], res[1], front[u][3], res[2], sums))
 
     def inner_step(u, before):
-        res = done(inner_norm(meta(), back[u][3], far_grad[u], front[u][0], front[u][1], vectors, att[u][:2], merge_w[:2], before))
+        res = done(inner_norm(meta(), back[u], far_grad[u], front[u][0], front[u][1], vectors, att[u][:2], merge_w[:2], before))
         return res, (res[1], swap(res[2], 1))
 
     def attend_step(u, grads):
@@ -801,22 +804,30 @@
         out = done(fold(meta(), pairs, tuple(first_bit + order[step] for order in bit_orders), hold))
         return [(out[2 * i + 1], swap_dp(out[2 * i], 1 << bit_orders[i][step])) for i in range(2)]
 
-    inner, entry, so_far = [], [], ()
+    inner, entry, so_far, near, crossed = [], [], (), [], []
+    out_other = [swap(r, 1) for r in out_rows]
+
+    def exchange(out):
+        got = swap(out[0], 1)
+        near.append((out[1], got))
+        crossed.append(swap(total(near[-1]), 2))
+        return got
+
     for u in range(seqs):
         last = u == seqs - 1
         if u == 0:
-            up_own, up_other, down_own, down_other = lax.optimization_barrier((*back[-1][6:], far_grad[0]))[:4]
+            up_own, up_other, down_own, down_other = lax.optimization_barrier((*sums, far_grad[0]))[:4]
             moving = [(down_own, swap(down_other, 1)), (up_own, swap(up_other, 1))]
             res, grads = inner_step(0, ())
             inner.append(res)
-            far_grad.append(swap(lax.optimization_barrier((back[-1][4], res[0]))[0], 2))
-            moving = scatter(0, moving, res[0], (0, 2))
+            far_grad.append(swap(lax.optimization_barrier((sent, res[0]))[0], 2))
+            moving = scatter(0, moving, res[0])
         dqkv = attend_step(u, grads)
         moving = scatter(1 + 2 * u, moving, dqkv[0])
         if not last:
             before = ()
             if u + 1 == seqs - 1:
-                before = (inner[0][3], inner[0][4], inner[0][5], back[0][5], back[1][5])
+                before = (inner[0][3], inner[0][4], inner[0][5], *smalls)
             res, grads = inner_step(u + 1, before)
             inner.append(res)
         else:
@@ -826,31 +837,36 @@
                 Chain(moving[i], [(b, 1) for b in order], True) for i, order in enumerate(bit_orders)
             )
             start([first, second])
+            token.extend(out_other)
         out = entry_step(u, dqkv, so_far)
         entry.append(out)
         if not last:
             merge_got = swap(lax.optimization_barrier((res[4], out[0]))[0], 1)
             so_far = (out[2], res[3], merge_got)
             moving = scatter(2, moving, out[0])
+            exchange(out)
     qkv = Chain(out[2], stages)
     qkv.start()
 
+    got = exchange(out)
+    layer_output = place(meta(), out_rows, out_other)
+
+    finish([first, second], got)
+    finish([qkv], crossed[0])
+    together([qkv, first, second])
+    start([qkv, first, second])
+    finish([qkv, first, second], crossed[-1])
+    together([qkv, first, second])
+    start([qkv, first])
     ready = []
     for u in range(seqs):
-        got = swap(entry[u][0], 1)
-        crossed = swap(total((entry[u][1], got)), 2)
-        rest = entry[u][1].astype(F32) + got.astype(F32) + crossed.astype(F32)
+        rest = near[u][0].astype(F32) + near[u][1].astype(F32) + crossed[u].astype(F32)
         ready.append((inner[u][0] + rest).astype(BF))
-    out_rows = [b[0] for b in back]
-    layer_output = place(meta(), out_rows, [swap(r, 1) for r in out_rows])
-
-    finish([first, second], got)
-    for group, sending in (((qkv,), (qkv, first, second)), ((qkv, first, second), (qkv, first)), ((qkv, first), (qkv, second))):
-        finish(group)
-        together([qkv, first, second])
-        start(sending)
     input_grad = place(scalars, ready, [swap(r, 1) for r in ready])
-    finish([qkv, second], input_grad, layer_output)
+    finish([qkv, first], layer_output)
+    together([qkv, first, second])
+    start([qkv, second])
+    finish([qkv, second], input_grad)
     while qkv.steps or first.steps or second.steps:
         start([qkv, first, second])
         finish([qkv, first, second])

time: 270 us -> 247 us (0.915)
  local copies, waits for them, and re-layouts: 22.1 us -> 2.65 us
  Pallas kernels: 119 us -> 111 us
  starting transfers between devices: 39 us -> 44.6 us
    unnamed x112 -> x68, local copies, waits for them, and re-layouts: 19.7 us -> 1.08 us
    pallas_call x21, Pallas kernels: 119 us -> 111 us  [call(): pl.pallas_call(kernel, grid_spec=pltpu.PrefetchScalarGridSpec(num_scalar_...]
    ppermute x20, waiting for transfers between devices: 47.4 us -> 40.2 us  [swap_dp(): return lax.ppermute(value, 'dp', [(i, i ^ k) for i in range(groups)])]
    ppermute x20, starting transfers between devices: 22.2 us -> 29 us  [swap_dp(): return lax.ppermute(value, 'dp', [(i, i ^ k) for i in range(groups)])]
    ppermute x28, waiting for transfers between devices: 25.8 us -> 31.3 us  [swap(): return lax.ppermute(value, 'tensor', [(i, i ^ k) for i in range(4)])]
  transfers between devices with their start and end apart: 48 -> 48, of which waited for: 14 -> 20; matrix products, arithmetic and copies ran while one was open for 5% -> 5% of each run, Pallas kernels for 44% -> 46%
where the time goes in v10:
time: 247 us; the launch traced here: 243 us
  Pallas kernels  111 us (45%)
  waiting for transfers between devices  71.5 us (29%)
  starting transfers between devices  44.6 us (18%)
  other arithmetic  11.7 us (5%)
  local copies, waits for them, and re-layouts  2.65 us (1%)
    pallas_call x21, Pallas kernels, call(): pl.pallas_call(kernel, grid_spec=pltpu.PrefetchScalarGridSpec(num_scalar_...  111 us
    ppermute x20, waiting for transfers between devices, swap_dp(): return lax.ppermute(value, 'dp', [(i, i ^ k) for i in range(groups)])  40.2 us
    ppermute x28, waiting for transfers between devices, swap(): return lax.ppermute(value, 'tensor', [(i, i ^ k) for i in range(4)])  31.3 us
    ppermute x20, starting transfers between devices, swap_dp(): return lax.ppermute(value, 'dp', [(i, i ^ k) for i in range(groups)])  29 us
    ppermute x28, starting transfers between devices, swap(): return lax.ppermute(value, 'tensor', [(i, i ^ k) for i in range(4)])  15.6 us
  transfers between devices with their start and end apart: 48, of which 20 were waited for; matrix products, arithmetic and copies ran while one was open for 5% of the time, Pallas kernels for 46%

profile of v10, /device:TPU:0, one launch (start us, length us, event | category | flops | bytes accessed | tf_op | source)
XLA Modules:
  0.0 243.3 jit_solution(318828300419238486)
XLA Ops:
  1.2 2.6 %collective-permute-start.1 = (bf16[192,768]{1,0:T(8,128)(2,1)}, bf16[192,768]{1,0:T(8,128)(2,1)S(1)}, u32[]{:S(2)}, u32[]{:S(2)}) collective-permute-start(bf16[192,768]{1,0:T(8,128)(2,1)} %w0.7), channel_id=1, source_target_pairs={{0,2},{1,3},{2,0},{3,1},{4,6},{5,7},{6,4},{7,5},{8,10},{9,11},{10,... | collective-permute-start | bytes 884744 | tf_op jit(solution)/shard_map/ppermute | solution.py:673
  5.0 4.4 %project.2 = (bf16[1024,256]{1,0:T(8,128)(2,1)S(1)}, bf16[1024,256]{1,0:T(8,128)(2,1)S(1)}, bf16[1024,256]{1,0:T(8,128)(2,1)S(1)}) custom-call(s32[6]{0:T(128)S(1)} %concatenate.24.meta_ref, bf16[2048,768]{1,0:T(8,128)(2,1)} %x_ref.7, bf16[192,768]{1,0:T(8,128)(2,1)} %bitcast.31, bf16[192,768]{1,0:T(8,128)(2,1)} %bitcast.35, bf16[192,768]{1,0:T(8,128)(2,1)} %bitcast.39), custom_call_target="tpu_custom_call" | custom-call | flops 3300000000 | bytes 1024 | tf_op jit(solution)/shard_map/project/pallas_call | solution.py:70
  9.5 4.3 %attend_forward.2 = (bf16[192,512]{1,0:T(8,128)(2,1)S(1)}, bf16[192,512]{1,0:T(8,128)(2,1)S(1)}, f32[2,8,512]{2,1,0:T(8,128)S(1)}) custom-call(s32[6]{0:T(128)S(1)} %concatenate.24.meta_ref, bf16[1024,256]{1,0:T(8,128)(2,1)S(1)} %get-tuple-element.157.q_ref, bf16[1024,256]{1,0:T(8,128)(2,1)S(1)} %get-tuple-element.159.k_ref, ...), custom_call_target="tpu_custom_call" | custom-call | flops 8800000000 | bytes 1024 | tf_op jit(solution)/shard_map/attend_forward/pallas_call | solution.py:70
  14.2 1.7 collective-permute-start.7
  15.9 1.8 collective-permute-done.2.w3
  19.2 4.4 %project.3 = (bf16[1024,256]{1,0:T(8,128)(2,1)S(1)}, bf16[1024,256]{1,0:T(8,128)(2,1)S(1)}, bf16[1024,256]{1,0:T(8,128)(2,1)S(1)}) custom-call(s32[6]{0:T(128)S(1)} %concatenate.24.meta_ref, bf16[2048,768]{1,0:T(8,128)(2,1)} %x_ref.7, bf16[192,768]{1,0:T(8,128)(2,1)} %bitcast.32, bf16[192,768]{1,0:T(8,128)(2,1)} %bitcast.36, bf16[192,768]{1,0:T(8,128)(2,1)} %bitcast.40), custom_call_target="tpu_custom_call" | custom-call | flops 3300000000 | bytes 1024 | tf_op jit(solution)/shard_map/project/pallas_call | solution.py:70
  23.7 4.8 %attend_forward.3 = (bf16[192,512]{1,0:T(8,128)(2,1)S(1)}, bf16[192,512]{1,0:T(8,128)(2,1)S(1)}, f32[2,8,512]{2,1,0:T(8,128)S(1)}) custom-call(s32[6]{0:T(128)S(1)} %concatenate.24.meta_ref, bf16[1024,256]{1,0:T(8,128)(2,1)S(1)} %get-tuple-element.163.q_ref, bf16[1024,256]{1,0:T(8,128)(2,1)S(1)} %get-tuple-element.165.k_ref, ...), custom_call_target="tpu_custom_call" | custom-call | flops 8800000000 | bytes 1024 | tf_op jit(solution)/shard_map/attend_forward/pallas_call | solution.py:70
  29.4 1.6 collective-permute-start.9
  31.1 10.1 %ahead.2 = (f32[512,768]{1,0:T(8,128)}, f32[512,128]{1,0:T(8,128)}, bf16[512,768]{1,0:T(8,128)(2,1)S(1)}, bf16[512,1536]{1,0:T(8,128)(2,1)S(1)}, bf16[512,1536]{...) custom-call(s32[6]{0:T(128)S(1)} %concatenate.24.meta_ref, bf16[2048,768]{1,0:T(8,128)(2,1)} %x_ref.7, ...), custom_call_target="tpu_custom_call" | custom-call | flops 9900000256 | bytes 1024 | tf_op jit(solution)/shard_map/ahead/pallas_call | solution.py:70
  41.6 10.2 %ahead.3 = (f32[512,768]{1,0:T(8,128)}, f32[512,128]{1,0:T(8,128)}, bf16[512,768]{1,0:T(8,128)(2,1)S(1)}, bf16[512,1536]{1,0:T(8,128)(2,1)S(1)}, bf16[512,1536]{...) custom-call(s32[6]{0:T(128)S(1)} %concatenate.24.meta_ref, bf16[2048,768]{1,0:T(8,128)(2,1)} %x_ref.7, ...), custom_call_target="tpu_custom_call" | custom-call | flops 9900000256 | bytes 1024 | tf_op jit(solution)/shard_map/ahead/pallas_call | solution.py:70
  51.8 1.7 collective-permute-start.12
  53.5 8.1 %collective-permute-done.11.far_ref = bf16[512,768]{1,0:T(8,128)(2,1)S(1)} collective-permute-done((bf16[512,768]{1,0:T(8,128)(2,1)S(1)}, bf16[512,768]{1,0:T(8,128)(2,1)S(1)}, u32[]{:S(2)}, u32[]{:S(2)}) %collective-permute-start.11) | collective-permute-done | bytes 786464 | tf_op jit(solution)/shard_map/ppermute | solution.py:673
  61.5 9.2 %astern.2 = (bf16[512,768]{1,0:T(8,128)(2,1)}, bf16[512,768]{1,0:T(8,128)(2,1)S(1)}, bf16[512,1536]{1,0:T(8,128)(2,1)S(1)}, f32[512,768]{1,0:T(8,128)}, bf16[512...) custom-call(s32[6]{0:T(128)S(1)} %concatenate.24.meta_ref, f32[512,768]{1,0:T(8,128)S(1)} %get-tuple-element.175.own_ref, ...), custom_call_target="tpu_custom_call" | custom-call | flops 11000000512 | bytes 1024 | tf_op jit(solution)/shard_map/astern/pallas_call | solution.py:70
  70.7 3.2 %weight_grads.1 = (bf16[768,768]{1,0:T(8,128)(2,1)S(1)}, bf16[768,768]{1,0:T(8,128)(2,1)S(1)}, bf16[768,768]{1,0:T(8,128)(2,1)S(1)}, bf16[768,768]{1,0:T(8,128)(2,1)S(1)}) custom-call(s32[6]{0:T(128)S(1)} %concatenate.24.meta_ref, bf16[512,768]{1,0:T(8,128)(2,1)S(1)} %get-tuple-element.180.x_ref, bf16[512,768]{1,0:T(8,128)(2,1)S(1)} %get-tuple-element.181.g_ref, ...), custom_call_target="tpu_custom_call" | custom-call | flops 4400000000 | bytes 1024 | tf_op jit(solution)/shard_map/weight_grads/pallas_call | solution.py:70
  74.4 4.0 %collective-permute-done.12.far_ref = bf16[512,768]{1,0:T(8,128)(2,1)S(1)} collective-permute-done((bf16[512,768]{1,0:T(8,128)(2,1)S(1)}, bf16[512,768]{1,0:T(8,128)(2,1)S(1)}, u32[]{:S(2)}, u32[]{:S(2)}) %collective-permute-start.12) | collective-permute-done | bytes 786464 | tf_op jit(solution)/shard_map/ppermute | solution.py:673
  78.4 11.8 %astern.3 = (bf16[512,768]{1,0:T(8,128)(2,1)}, f32[512,768]{1,0:T(8,128)}, bf16[512,768]{1,0:T(8,128)(2,1)S(1)}, f32[2,768]{1,0:T(2,128)S(1)}, bf16[768,768]{1,0...) custom-call(s32[6]{0:T(128)S(1)} %concatenate.24.meta_ref, ...), custom_call_target="tpu_custom_call" | custom-call | flops 11000000512 | bytes 1024 | tf_op jit(solution)/shard_map/astern/pallas_call | solution.py:70
  90.2 4.2 %collective-permute-done.13.far_ref = bf16[512,768]{1,0:T(8,128)(2,1)S(1)} collective-permute-done((bf16[512,768]{1,0:T(8,128)(2,1)S(1)}, bf16[512,768]{1,0:T(8,128)(2,1)S(1)}, u32[]{:S(2)}, u32[]{:S(2)}) %collective-permute-start.13) | collective-permute-done | bytes 786464 | tf_op jit(solution)/shard_map/ppermute | solution.py:673
  95.5 5.3 %inner_norm.2 = (f32[512,768]{1,0:T(8,128)}, bf16[192,512]{1,0:T(8,128)(2,1)S(1)}, bf16[192,512]{1,0:T(8,128)(2,1)S(1)}, f32[192,768]{1,0:T(8,128)}, f32[192,768]{1,0:T(8,128)}, /*index=5*/f32[2,768]{1,0:T(2,128)S(1)}) custom-call(s32[6]{0:T(128)S(1)} %concatenate.24.meta_ref, f32[512,768]{1,0:T(8,128)} %get-tuple-element.196.own_ref, ...), custom_call_target="tpu_custom_call" | custom-call | flops 3300000000 | bytes 1024 | tf_op jit(solution)/shard_map/inner_norm/pallas_call | solution.py:70
  102.2 4.5 %collective-permute-start.17 = (bf16[384,768]{1,0:T(8,128)(2,1)S(1)}, bf16[384,768]{1,0:T(8,128)(2,1)S(1)}, u32[]{:S(2)}, u32[]{:S(2)}) collective-permute-start(bf16[384,768]{1,0:T(8,128)(2,1)S(1)} %get-tuple-element.213), channel_id=1, source_target_pairs={{0,4},{4,0},{8,12},{12,8},{16,20},{20,16},{24,28},{28,24},{1,5},{5... | collective-permute-start | bytes 1769480 | tf_op jit(solution)/shard_map/ppermute | solution.py:676
  106.8 2.0 collective-permute-start.18
  108.8 7.6 %attend_backward.2 = (bf16[1024,256]{1,0:T(8,128)(2,1)S(1)}, bf16[1024,256]{1,0:T(8,128)(2,1)S(1)}, bf16[1024,256]{1,0:T(8,128)(2,1)S(1)}) custom-call(s32[6]{0:T(128)S(1)} %concatenate.24.meta_ref, bf16[1024,256]{1,0:T(8,128)(2,1)} %copy-done.25, bf16[1024,256]{1,0:T(8,128)(2,1)} %copy-done.26, bf16[1024,256]{1,0:T(8,128)(2,1)} %copy-done.27, ...), custom_call_target="tpu_custom_call" | custom-call | flops 13200000000 | bytes 1024 | tf_op jit(solution)/shard_map/attend_backward/pallas_call | solution.py:70
  116.4 6.2 %collective-permute-done.18.refs_3_ = bf16[384,768]{1,0:T(8,128)(2,1)S(1)} collective-permute-done((bf16[384,768]{1,0:T(8,128)(2,1)S(1)}, bf16[384,768]{1,0:T(8,128)(2,1)S(1)}, u32[]{:S(2)}, u32[]{:S(2)}) %collective-permute-start.18) | collective-permute-done | bytes 589856 | tf_op jit(solution)/shard_map/ppermute | solution.py:676
  123.4 1.8 collective-permute-start.20
  125.2 5.5 %inner_norm.3 = (f32[512,768]{1,0:T(8,128)}, bf16[192,512]{1,0:T(8,128)(2,1)S(1)}, bf16[192,512]{1,0:T(8,128)(2,1)S(1)}, bf16[256,768]{1,0:T(8,128)(2,1)S(1)}, b...) custom-call(s32[6]{0:T(128)S(1)} %concatenate.24.meta_ref, f32[512,768]{1,0:T(8,128)} %get-tuple-element.229.own_ref, ...), custom_call_target="tpu_custom_call" | custom-call | flops 3300000000 | bytes 1024 | tf_op jit(solution)/shard_map/inner_norm/pallas_call | solution.py:70
  130.7 1.7 collective-permute-start.21
  132.4 7.1 %entry_back.2 = (bf16[512,768]{1,0:T(8,128)(2,1)}, bf16[512,768]{1,0:T(8,128)(2,1)S(1)}, f32[576,768]{1,0:T(8,128)S(1)}) custom-call(s32[6]{0:T(128)S(1)} %concatenate.24.meta_ref, bf16[2048,768]{1,0:T(8,128)(2,1)} %x_ref.7, bf16[1024,256]{1,0:T(8,128)(2,1)S(1)} %get-tuple-element.218.dq_ref, bf16[1024,256]{1,0:T(8,128)(2,1)S(1)} %get-tuple-element.240.dk_ref, ...), custom_call_target="tpu_custom_call" | custom-call | flops 5500000256 | bytes 1024 | tf_op jit(solution)/shard_map/entry_back/pallas_call | solution.py:70
  141.5 2.2 collective-permute-start.24
  143.7 7.6 %attend_backward.3 = (bf16[1024,256]{1,0:T(8,128)(2,1)S(1)}, bf16[1024,256]{1,0:T(8,128)(2,1)S(1)}, bf16[1024,256]{1,0:T(8,128)(2,1)S(1)}) custom-call(s32[6]{0:T(128)S(1)} %concatenate.24.meta_ref, bf16[1024,256]{1,0:T(8,128)(2,1)} %copy-done.22, bf16[1024,256]{1,0:T(8,128)(2,1)} %copy-done.23, bf16[1024,256]{1,0:T(8,128)(2,1)} %copy-done.24, ...), custom_call_target="tpu_custom_call" | custom-call | flops 13200000000 | bytes 1024 | tf_op jit(solution)/shard_map/attend_backward/pallas_call | solution.py:70
  151.3 5.4 %collective-permute-done.24.refs_3_ = bf16[96,768]{1,0:T(8,128)(2,1)S(1)} collective-permute-done((bf16[96,768]{1,0:T(8,128)(2,1)S(1)}, bf16[96,768]{1,0:T(8,128)(2,1)S(1)}, u32[]{:S(2)}, u32[]{:S(2)}) %collective-permute-start.24) | collective-permute-done | bytes 147488 | tf_op jit(solution)/shard_map/ppermute | solution.py:676
  158.3 7.0 %entry_back.3 = (bf16[512,768]{1,0:T(8,128)(2,1)}, bf16[512,768]{1,0:T(8,128)(2,1)S(1)}, bf16[832,768]{1,0:T(8,128)(2,1)S(1)}) custom-call(s32[6]{0:T(128)S(1)} %concatenate.24.meta_ref, bf16[2048,768]{1,0:T(8,128)(2,1)} %x_ref.7, bf16[1024,256]{1,0:T(8,128)(2,1)S(1)} %get-tuple-element.256.dq_ref, bf16[1024,256]{1,0:T(8,128)(2,1)S(1)} %get-tuple-element.267.dk_ref, ...), custom_call_target="tpu_custom_call" | custom-call | flops 5500000256 | bytes 1024 | tf_op jit(solution)/shard_map/entry_back/pallas_call | solution.py:70
  165.7 2.9 %collective-permute-start.35 = (bf16[1,1,1,96,768]{4,3,2,1,0:T(8,128)(2,1)S(1)}, bf16[1,1,1,96,768]{4,3,2,1,0:T(8,128)(2,1)S(1)}, u32[]{:S(2)}, u32[]{:S(2)}) collective-permute-start(bf16[1,1,1,96,768]{4,3,2,1,0:T(8,128)(2,1)S(1)} %bitcast.26), channel_id=1, source_target_pairs={{0,16},{4,20},{8,24},{12,28},{16,0},{20,4},{24,8},{28,12},{1,17},{... | collective-permute-start | bytes 442376 | tf_op jit(solution)/shard_map/ppermute | solution.py:676
  173.2 4.8 %collective-permute-done.36 = bf16[1,1,1,96,768]{4,3,2,1,0:T(8,128)(2,1)S(1)} collective-permute-done((bf16[1,1,1,96,768]{4,3,2,1,0:T(8,128)(2,1)S(1)}, bf16[1,1,1,96,768]{4,3,2,1,0:T(8,128)(2,1)S(1)}, u32[]{:S(2)}, u32[]{:S(2)}) %collective-permute-start.36) | collective-permute-done | bytes 147488 | tf_op jit(solution)/shard_map/ppermute | solution.py:676
  178.0 3.1 %collective-permute-done.35 = bf16[1,1,1,96,768]{4,3,2,1,0:T(8,128)(2,1)S(1)} collective-permute-done((bf16[1,1,1,96,768]{4,3,2,1,0:T(8,128)(2,1)S(1)}, bf16[1,1,1,96,768]{4,3,2,1,0:T(8,128)(2,1)S(1)}, u32[]{:S(2)}, u32[]{:S(2)}) %collective-permute-start.35) | collective-permute-done | bytes 147488 | tf_op jit(solution)/shard_map/ppermute | solution.py:676
  181.8 2.8 %collective-permute-done.34 = bf16[416,768]{1,0:T(8,128)(2,1)S(1)} collective-permute-done((bf16[416,768]{1,0:T(8,128)(2,1)S(1)}, bf16[416,768]{1,0:T(8,128)(2,1)S(1)}, u32[]{:S(2)}, u32[]{:S(2)}) %collective-permute-start.34) | collective-permute-done | bytes 639008 | tf_op jit(solution)/shard_map/ppermute | solution.py:676
  184.6 7.3 %collective-permute-done.29 = bf16[512,768]{1,0:T(8,128)(2,1)S(1)} collective-permute-done((bf16[512,768]{1,0:T(8,128)(2,1)S(1)}, bf16[512,768]{1,0:T(8,128)(2,1)S(1)}, u32[]{:S(2)}, u32[]{:S(2)}) %collective-permute-start.29) | collective-permute-done | bytes 786464 | tf_op jit(solution)/shard_map/ppermute | solution.py:673
  192.9 2.7 %place.2 = bf16[2048,768]{1,0:T(8,128)(2,1)} custom-call(s32[6]{0:T(128)S(1)} %concatenate.24.meta_ref, bf16[512,768]{1,0:T(8,128)(2,1)S(1)} %copy-done.3, bf16[512,768]{1,0:T(8,128)(2,1)S(1)} %copy-done.6, bf16[512,768]{1,0:T(8,128)(2,1)S(1)} %copy-done.4, bf16[512,768]{1,0:T(8,128)(2,1)S(1)} %copy-done.8), custom_call_target="tpu_custom_call" | custom-call | flops 3300000000 | bytes 1024 | tf_op jit(solution)/shard_map/place/pallas_call | solution.py:70
  195.7 2.1 collective-permute-start.37
  201.7 5.2 %collective-permute-done.32 = bf16[512,768]{1,0:T(8,128)(2,1)S(1)} collective-permute-done((bf16[512,768]{1,0:T(8,128)(2,1)S(1)}, bf16[512,768]{1,0:T(8,128)(2,1)S(1)}, u32[]{:S(2)}, u32[]{:S(2)}) %collective-permute-start.32) | collective-permute-done | bytes 786464 | tf_op jit(solution)/shard_map/ppermute | solution.py:673
  207.6 1.7 collective-permute-done.37
  209.3 2.9 %collective-permute-done.39 = bf16[104,768]{1,0:T(8,128)(2,1)S(1)} collective-permute-done((bf16[104,768]{1,0:T(8,128)(2,1)S(1)}, bf16[104,768]{1,0:T(8,128)(2,1)S(1)}, u32[]{:S(2)}, u32[]{:S(2)}) %collective-permute-start.39) | collective-permute-done | bytes 159776 | tf_op jit(solution)/shard_map/ppermute | solution.py:676
  212.6 2.0 collective-permute-start.43
  214.6 2.4 collective-permute-start.44
  220.3 3.5 %collective-permute-done.43 = bf16[1,1,104,768]{3,2,1,0:T(8,128)(2,1)S(1)} collective-permute-done((bf16[1,1,104,768]{3,2,1,0:T(8,128)(2,1)S(1)}, bf16[1,1,104,768]{3,2,1,0:T(8,128)(2,1)S(1)}, u32[]{:S(2)}, u32[]{:S(2)}) %collective-permute-start.43) | collective-permute-done | bytes 159776 | tf_op jit(solution)/shard_map/ppermute | solution.py:676
  223.9 3.0 %collective-permute-done.45 = bf16[1,2,2,96,768]{4,3,2,1,0:T(8,128)(2,1)S(1)} collective-permute-done((bf16[1,2,2,96,768]{4,3,2,1,0:T(8,128)(2,1)S(1)}, bf16[1,2,2,96,768]{4,3,2,1,0:T(8,128)(2,1)S(1)}, u32[]{:S(2)}, u32[]{:S(2)}) %collective-permute-start.45) | collective-permute-done | bytes 589856 | tf_op jit(solution)/shard_map/ppermute | solution.py:676
  227.2 2.1 collective-permute-start.46
  230.9 2.7 %place.3 = bf16[2048,768]{1,0:T(8,128)(2,1)} custom-call(s32[6]{0:T(128)S(1)} %concatenate.24.meta_ref, bf16[512,768]{1,0:T(8,128)(2,1)S(1)} %add_convert_fusion.1.refs_0_, bf16[512,768]{1,0:T(8,128)(2,1)S(1)} %collective-permute-done.30.refs_1_, bf16[512,768]{1,0:T(8,128)(2,1)S(1)} %add_convert_fusion.refs_2_, ...), custom_call_target="tpu_custom_call" | custom-call | flops 3300000000 | bytes 1024 | tf_op jit(solution)/shard_map/place/pallas_call | solution.py:70
  233.6 4.4 %collective-permute-done.47 = bf16[1,2,2,96,768]{4,3,2,1,0:T(8,128)(2,1)S(1)} collective-permute-done((bf16[1,2,2,96,768]{4,3,2,1,0:T(8,128)(2,1)S(1)}, bf16[1,2,2,96,768]{4,3,2,1,0:T(8,128)(2,1)S(1)}, u32[]{:S(2)}, u32[]{:S(2)}) %collective-permute-start.47) | collective-permute-done | bytes 589856 | tf_op jit(solution)/shard_map/ppermute | solution.py:676
  238.3 1.7 bitcast_convert_fusion
  (174 shorter events, 32.4 us)
Async XLA Ops:
  0.6 13.3 %collective-permute-start = (bf16[192,768]{1,0:T(8,128)(2,1)}, bf16[192,768]{1,0:T(8,128)(2,1)S(1)}, u32[]{:S(2)}, u32[]{:S(2)}) collective-permute-start(bf16[192,768]{1,0:T(8,128)(2,1)} %w0.7), channel_id=1, source_target_pairs={{0,1},{1,0},{2,3},{3,2},{4,5},{5,4},{6,7},{7,6},{8,9},{9,8},{10,11... | collective-permute-start | bytes 884744 | tf_op jit(solution)/shard_map/ppermute | solution.py:673
  1.2 13.0 %collective-permute-start.1 = (bf16[192,768]{1,0:T(8,128)(2,1)}, bf16[192,768]{1,0:T(8,128)(2,1)S(1)}, u32[]{:S(2)}, u32[]{:S(2)}) collective-permute-start(bf16[192,768]{1,0:T(8,128)(2,1)} %w0.7), channel_id=1, source_target_pairs={{0,2},{1,3},{2,0},{3,1},{4,6},{5,7},{6,4},{7,5},{8,10},{9,11},{10,... | collective-permute-start | bytes 884744 | tf_op jit(solution)/shard_map/ppermute | solution.py:673
  3.7 14.0 %collective-permute-start.2 = (bf16[192,768]{1,0:T(8,128)(2,1)}, bf16[192,768]{1,0:T(8,128)(2,1)S(1)}, u32[]{:S(2)}, u32[]{:S(2)}) collective-permute-start(bf16[192,768]{1,0:T(8,128)(2,1)} %w0.7), channel_id=1, source_target_pairs={{0,3},{1,2},{2,1},{3,0},{4,7},{5,6},{6,5},{7,4},{8,11},{9,10},{10,... | collective-permute-start | bytes 884744 | tf_op jit(solution)/shard_map/ppermute | solution.py:673
  3.8 19.8 %collective-permute-start.3 = (bf16[768,768]{1,0:T(8,128)(2,1)}, bf16[768,768]{1,0:T(8,128)(2,1)S(1)}, u32[]{:S(2)}, u32[]{:S(2)}) collective-permute-start(bf16[768,768]{1,0:T(8,128)(2,1)} %ua_ref.7), channel_id=1, source_target_pairs={{0,1},{1,0},{2,3},{3,2},{4,5},{5,4},{6,7},{7,6},{8,9},{9,8},{10,11... | collective-permute-start | bytes 3538952 | tf_op jit(solution)/shard_map/ppermute | solution.py:673
  3.9 19.6 %collective-permute-start.4 = (bf16[768,768]{1,0:T(8,128)(2,1)}, bf16[768,768]{1,0:T(8,128)(2,1)S(1)}, u32[]{:S(2)}, u32[]{:S(2)}) collective-permute-start(bf16[768,768]{1,0:T(8,128)(2,1)} %da_ref.7), channel_id=1, source_target_pairs={{0,1},{1,0},{2,3},{3,2},{4,5},{5,4},{6,7},{7,6},{8,9},{9,8},{10,11... | collective-permute-start | bytes 3538952 | tf_op jit(solution)/shard_map/ppermute | solution.py:673
  14.0 15.4 %collective-permute-start.5 = (bf16[192,512]{1,0:T(8,128)(2,1)S(1)}, bf16[192,512]{1,0:T(8,128)(2,1)S(1)}, u32[]{:S(2)}, u32[]{:S(2)}) collective-permute-start(bf16[192,512]{1,0:T(8,128)(2,1)S(1)} %get-tuple-element.169.o1_ref), channel_id=1, source_target_pairs={{0,1},{1,0},{2,3},{3,2},{4,5},{5,4},{6,7},{7,6},{8,9},{9,8},{10,11... | collective-permute-start | bytes 589832 | tf_op jit(solution)/shard_map/ppermute | solution.py:673
  14.2 16.8 %collective-permute-start.7 = (bf16[192,512]{1,0:T(8,128)(2,1)S(1)}, bf16[192,512]{1,0:T(8,128)(2,1)S(1)}, u32[]{:S(2)}, u32[]{:S(2)}) collective-permute-start(bf16[192,512]{1,0:T(8,128)(2,1)S(1)} %get-tuple-element.169.o1_ref), channel_id=1, source_target_pairs={{0,3},{1,2},{2,1},{3,0},{4,7},{5,6},{6,5},{7,4},{8,11},{9,10},{10,... | collective-permute-start | bytes 589832 | tf_op jit(solution)/shard_map/ppermute | solution.py:673
  17.7 13.3 %collective-permute-start.6 = (bf16[192,512]{1,0:T(8,128)(2,1)S(1)}, bf16[192,512]{1,0:T(8,128)(2,1)S(1)}, u32[]{:S(2)}, u32[]{:S(2)}) collective-permute-start(bf16[192,512]{1,0:T(8,128)(2,1)S(1)} %get-tuple-element.161.a0.o0_ref), channel_id=1, source_target_pairs={{0,2},{1,3},{2,0},{3,1},{4,6},{5,7},{6,4},{7,5},{8,10},{9,11},{10,... | collective-permute-start | bytes 589832 | tf_op jit(solution)/shard_map/ppermute | solution.py:673
  28.5 13.0 %collective-permute-start.10 = (bf16[192,512]{1,0:T(8,128)(2,1)S(1)}, bf16[192,512]{1,0:T(8,128)(2,1)S(1)}, u32[]{:S(2)}, u32[]{:S(2)}) collective-permute-start(bf16[192,512]{1,0:T(8,128)(2,1)S(1)} %get-tuple-element.172.o1_ref), channel_id=1, source_target_pairs={{0,3},{1,2},{2,1},{3,0},{4,7},{5,6},{6,5},{7,4},{8,11},{9,10},{10,... | collective-permute-start | bytes 589832 | tf_op jit(solution)/shard_map/ppermute | solution.py:673
  29.2 12.3 %collective-permute-start.8 = (bf16[192,512]{1,0:T(8,128)(2,1)S(1)}, bf16[192,512]{1,0:T(8,128)(2,1)S(1)}, u32[]{:S(2)}, u32[]{:S(2)}) collective-permute-start(bf16[192,512]{1,0:T(8,128)(2,1)S(1)} %get-tuple-element.172.o1_ref), channel_id=1, source_target_pairs={{0,1},{1,0},{2,3},{3,2},{4,5},{5,4},{6,7},{7,6},{8,9},{9,8},{10,11... | collective-permute-start | bytes 589832 | tf_op jit(solution)/shard_map/ppermute | solution.py:673
  29.4 12.1 %collective-permute-start.9 = (bf16[192,512]{1,0:T(8,128)(2,1)S(1)}, bf16[192,512]{1,0:T(8,128)(2,1)S(1)}, u32[]{:S(2)}, u32[]{:S(2)}) collective-permute-start(bf16[192,512]{1,0:T(8,128)(2,1)S(1)} %get-tuple-element.167.a0.o0_ref), channel_id=1, source_target_pairs={{0,2},{1,3},{2,0},{3,1},{4,6},{5,7},{6,4},{7,5},{8,10},{9,11},{10,... | collective-permute-start | bytes 589832 | tf_op jit(solution)/shard_map/ppermute | solution.py:673
  41.1 20.4 %collective-permute-start.11 = (bf16[512,768]{1,0:T(8,128)(2,1)S(1)}, bf16[512,768]{1,0:T(8,128)(2,1)S(1)}, u32[]{:S(2)}, u32[]{:S(2)}) collective-permute-start(bf16[512,768]{1,0:T(8,128)(2,1)S(1)} %get-tuple-element.176), channel_id=1, source_target_pairs={{0,2},{1,3},{2,0},{3,1},{4,6},{5,7},{6,4},{7,5},{8,10},{9,11},{10,... | collective-permute-start | bytes 2359304 | tf_op jit(solution)/shard_map/ppermute | solution.py:673
  51.8 26.6 %collective-permute-start.12 = (bf16[512,768]{1,0:T(8,128)(2,1)S(1)}, bf16[512,768]{1,0:T(8,128)(2,1)S(1)}, u32[]{:S(2)}, u32[]{:S(2)}) collective-permute-start(bf16[512,768]{1,0:T(8,128)(2,1)S(1)} %get-tuple-element.187), channel_id=1, source_target_pairs={{0,2},{1,3},{2,0},{3,1},{4,6},{5,7},{6,4},{7,5},{8,10},{9,11},{10,... | collective-permute-start | bytes 2359304 | tf_op jit(solution)/shard_map/ppermute | solution.py:673
  73.9 20.5 %collective-permute-start.13 = (bf16[512,768]{1,0:T(8,128)(2,1)S(1)}, bf16[512,768]{1,0:T(8,128)(2,1)S(1)}, u32[]{:S(2)}, u32[]{:S(2)}) collective-permute-start(bf16[512,768]{1,0:T(8,128)(2,1)S(1)} %get-tuple-element.197), channel_id=1, source_target_pairs={{0,2},{1,3},{2,0},{3,1},{4,6},{5,7},{6,4},{7,5},{8,10},{9,11},{10,... | collective-permute-start | bytes 2359304 | tf_op jit(solution)/shard_map/ppermute | solution.py:673
  94.4 6.7 %collective-permute-start.15 = (bf16[768,768]{1,0:T(8,128)(2,1)S(1)}, bf16[768,768]{1,0:T(8,128)(2,1)S(1)}, u32[]{:S(2)}, u32[]{:S(2)}) collective-permute-start(bf16[768,768]{1,0:T(8,128)(2,1)S(1)} %get-tuple-element.210), channel_id=1, source_target_pairs={{0,1},{1,0},{2,3},{3,2},{4,5},{5,4},{6,7},{7,6},{8,9},{9,8},{10,11... | collective-permute-start | bytes 3538952 | tf_op jit(solution)/shard_map/ppermute | solution.py:673
  94.4 6.7 %collective-permute-start.14 = (bf16[768,768]{1,0:T(8,128)(2,1)S(1)}, bf16[768,768]{1,0:T(8,128)(2,1)S(1)}, u32[]{:S(2)}, u32[]{:S(2)}) collective-permute-start(bf16[768,768]{1,0:T(8,128)(2,1)S(1)} %get-tuple-element.206), channel_id=1, source_target_pairs={{0,1},{1,0},{2,3},{3,2},{4,5},{5,4},{6,7},{7,6},{8,9},{9,8},{10,11... | collective-permute-start | bytes 3538952 | tf_op jit(solution)/shard_map/ppermute | solution.py:673
  94.9 62.4 %collective-permute-start.25 = (bf16[512,768]{1,0:T(8,128)(2,1)S(1)}, bf16[512,768]{1,0:T(8,128)(2,1)S(1)}, u32[]{:S(2)}, u32[]{:S(2)}) collective-permute-start(bf16[512,768]{1,0:T(8,128)(2,1)S(1)} %copy-done.2), channel_id=1, source_target_pairs={{0,1},{1,0},{2,3},{3,2},{4,5},{5,4},{6,7},{7,6},{8,9},{9,8},{10,11... | collective-permute-start | bytes 2359304 | tf_op jit(solution)/shard_map/ppermute | solution.py:673
  94.9 62.4 %collective-permute-start.26 = (bf16[512,768]{1,0:T(8,128)(2,1)}, bf16[512,768]{1,0:T(8,128)(2,1)S(1)}, u32[]{:S(2)}, u32[]{:S(2)}) collective-permute-start(bf16[512,768]{1,0:T(8,128)(2,1)} %get-tuple-element.194.refs_2_), channel_id=1, source_target_pairs={{0,1},{1,0},{2,3},{3,2},{4,5},{5,4},{6,7},{7,6},{8,9},{9,8},{10,11... | collective-permute-start | bytes 2359304 | tf_op jit(solution)/shard_map/ppermute | solution.py:673
  100.8 24.4 %collective-permute-start.19 = (bf16[512,768]{1,0:T(8,128)(2,1)S(1)}, bf16[512,768]{1,0:T(8,128)(2,1)S(1)}, u32[]{:S(2)}, u32[]{:S(2)}) collective-permute-start(bf16[512,768]{1,0:T(8,128)(2,1)S(1)} %get-tuple-element.231), channel_id=1, source_target_pairs={{0,2},{1,3},{2,0},{3,1},{4,6},{5,7},{6,4},{7,5},{8,10},{9,11},{10,... | collective-permute-start | bytes 2359304 | tf_op jit(solution)/shard_map/ppermute | solution.py:673
  101.1 5.7 %collective-permute-start.16 = (bf16[192,512]{1,0:T(8,128)(2,1)S(1)}, bf16[192,512]{1,0:T(8,128)(2,1)S(1)}, u32[]{:S(2)}, u32[]{:S(2)}) collective-permute-start(bf16[192,512]{1,0:T(8,128)(2,1)S(1)} %get-tuple-element.216), channel_id=1, source_target_pairs={{0,1},{1,0},{2,3},{3,2},{4,5},{5,4},{6,7},{7,6},{8,9},{9,8},{10,11... | collective-permute-start | bytes 589832 | tf_op jit(solution)/shard_map/ppermute | solution.py:673
  102.2 20.4 %collective-permute-start.17 = (bf16[384,768]{1,0:T(8,128)(2,1)S(1)}, bf16[384,768]{1,0:T(8,128)(2,1)S(1)}, u32[]{:S(2)}, u32[]{:S(2)}) collective-permute-start(bf16[384,768]{1,0:T(8,128)(2,1)S(1)} %get-tuple-element.213), channel_id=1, source_target_pairs={{0,4},{4,0},{8,12},{12,8},{16,20},{20,16},{24,28},{28,24},{1,5},{5... | collective-permute-start | bytes 1769480 | tf_op jit(solution)/shard_map/ppermute | solution.py:676
  106.8 15.8 %collective-permute-start.18 = (bf16[384,768]{1,0:T(8,128)(2,1)S(1)}, bf16[384,768]{1,0:T(8,128)(2,1)S(1)}, u32[]{:S(2)}, u32[]{:S(2)}) collective-permute-start(bf16[384,768]{1,0:T(8,128)(2,1)S(1)} %get-tuple-element.224), channel_id=1, source_target_pairs={{0,8},{4,12},{8,0},{12,4},{16,24},{20,28},{24,16},{28,20},{1,9},{5... | collective-permute-start | bytes 1769480 | tf_op jit(solution)/shard_map/ppermute | solution.py:676
  123.4 16.5 %collective-permute-start.20 = (bf16[192,768]{1,0:T(8,128)(2,1)S(1)}, bf16[192,768]{1,0:T(8,128)(2,1)S(1)}, u32[]{:S(2)}, u32[]{:S(2)}) collective-permute-start(bf16[192,768]{1,0:T(8,128)(2,1)S(1)} %get-tuple-element.227), channel_id=1, source_target_pairs={{0,8},{4,12},{8,0},{12,4},{16,24},{20,28},{24,16},{28,20},{1,9},{5... | collective-permute-start | bytes 884744 | tf_op jit(solution)/shard_map/ppermute | solution.py:676
  130.7 8.7 %collective-permute-start.21 = (bf16[192,768]{1,0:T(8,128)(2,1)S(1)}, bf16[192,768]{1,0:T(8,128)(2,1)S(1)}, u32[]{:S(2)}, u32[]{:S(2)}) collective-permute-start(bf16[192,768]{1,0:T(8,128)(2,1)S(1)} %get-tuple-element.248), channel_id=1, source_target_pairs={{0,4},{4,0},{8,12},{12,8},{16,20},{20,16},{24,28},{28,24},{1,5},{5... | collective-permute-start | bytes 884744 | tf_op jit(solution)/shard_map/ppermute | solution.py:676
  139.5 18.8 %collective-permute-start.27 = (bf16[256,768]{1,0:T(8,128)(2,1)S(1)}, bf16[256,768]{1,0:T(8,128)(2,1)S(1)}, u32[]{:S(2)}, u32[]{:S(2)}) collective-permute-start(bf16[256,768]{1,0:T(8,128)(2,1)S(1)} %get-tuple-element.272), channel_id=1, source_target_pairs={{0,1},{1,0},{2,3},{3,2},{4,5},{5,4},{6,7},{7,6},{8,9},{9,8},{10,11... | collective-permute-start | bytes 1179656 | tf_op jit(solution)/shard_map/ppermute | solution.py:673
  139.5 2.0 collective-permute-start.22
  140.7 16.0 %collective-permute-start.23 = (bf16[96,768]{1,0:T(8,128)(2,1)S(1)}, bf16[96,768]{1,0:T(8,128)(2,1)S(1)}, u32[]{:S(2)}, u32[]{:S(2)}) collective-permute-start(bf16[96,768]{1,0:T(8,128)(2,1)S(1)} %get-tuple-element.251), channel_id=1, source_target_pairs={{0,16},{4,20},{8,24},{12,28},{16,0},{20,4},{24,8},{28,12},{1,17},{... | collective-permute-start | bytes 442376 | tf_op jit(solution)/shard_map/ppermute | solution.py:676
  141.5 15.2 %collective-permute-start.24 = (bf16[96,768]{1,0:T(8,128)(2,1)S(1)}, bf16[96,768]{1,0:T(8,128)(2,1)S(1)}, u32[]{:S(2)}, u32[]{:S(2)}) collective-permute-start(bf16[96,768]{1,0:T(8,128)(2,1)S(1)} %get-tuple-element.262), channel_id=1, source_target_pairs={{0,16},{4,20},{8,24},{12,28},{16,0},{20,4},{24,8},{28,12},{1,17},{... | collective-permute-start | bytes 442376 | tf_op jit(solution)/shard_map/ppermute | solution.py:676
  156.7 13.3 %collective-permute-start.28 = (bf16[512,768]{1,0:T(8,128)(2,1)}, bf16[512,768]{1,0:T(8,128)(2,1)}, u32[]{:S(2)}, u32[]{:S(2)}) collective-permute-start(bf16[512,768]{1,0:T(8,128)(2,1)} %get-tuple-element.242), channel_id=1, source_target_pairs={{0,1},{1,0},{2,3},{3,2},{4,5},{5,4},{6,7},{7,6},{8,9},{9,8},{10,11... | collective-permute-start | bytes 2359304 | tf_op jit(solution)/shard_map/ppermute | solution.py:673
  165.3 6.6 %collective-permute-start.31 = (bf16[512,768]{1,0:T(8,128)(2,1)}, bf16[512,768]{1,0:T(8,128)(2,1)}, u32[]{:S(2)}, u32[]{:S(2)}) collective-permute-start(bf16[512,768]{1,0:T(8,128)(2,1)} %get-tuple-element.273), channel_id=1, source_target_pairs={{0,1},{1,0},{2,3},{3,2},{4,5},{5,4},{6,7},{7,6},{8,9},{9,8},{10,11... | collective-permute-start | bytes 2359304 | tf_op jit(solution)/shard_map/ppermute | solution.py:673
  165.7 12.3 %collective-permute-start.36 = (bf16[1,1,1,96,768]{4,3,2,1,0:T(8,128)(2,1)S(1)}, bf16[1,1,1,96,768]{4,3,2,1,0:T(8,128)(2,1)S(1)}, u32[]{:S(2)}, u32[]{:S(2)}) collective-permute-start(bf16[1,1,1,96,768]{4,3,2,1,0:T(8,128)(2,1)S(1)} %bitcast.27), channel_id=1, source_target_pairs={{0,16},{4,20},{8,24},{12,28},{16,0},{20,4},{24,8},{28,12},{1,17},{... | collective-permute-start | bytes 442376 | tf_op jit(solution)/shard_map/ppermute | solution.py:676
  165.7 15.3 %collective-permute-start.35 = (bf16[1,1,1,96,768]{4,3,2,1,0:T(8,128)(2,1)S(1)}, bf16[1,1,1,96,768]{4,3,2,1,0:T(8,128)(2,1)S(1)}, u32[]{:S(2)}, u32[]{:S(2)}) collective-permute-start(bf16[1,1,1,96,768]{4,3,2,1,0:T(8,128)(2,1)S(1)} %bitcast.26), channel_id=1, source_target_pairs={{0,16},{4,20},{8,24},{12,28},{16,0},{20,4},{24,8},{28,12},{1,17},{... | collective-permute-start | bytes 442376 | tf_op jit(solution)/shard_map/ppermute | solution.py:676
  168.7 15.9 %collective-permute-start.34 = (bf16[416,768]{1,0:T(8,128)(2,1)S(1)}, bf16[416,768]{1,0:T(8,128)(2,1)S(1)}, u32[]{:S(2)}, u32[]{:S(2)}) collective-permute-start(bf16[416,768]{1,0:T(8,128)(2,1)S(1)} %constant_dynamic-slice_fusion.3), channel_id=1, source_target_pairs={{0,4},{4,0},{8,12},{12,8},{16,20},{20,16},{24,28},{28,24},{1,5},{5... | collective-permute-start | bytes 1916936 | tf_op jit(solution)/shard_map/ppermute | solution.py:676
  171.3 20.5 %collective-permute-start.29 = (bf16[512,768]{1,0:T(8,128)(2,1)S(1)}, bf16[512,768]{1,0:T(8,128)(2,1)S(1)}, u32[]{:S(2)}, u32[]{:S(2)}) collective-permute-start(bf16[512,768]{1,0:T(8,128)(2,1)S(1)} %fusion), channel_id=1, source_target_pairs={{0,2},{1,3},{2,0},{3,1},{4,6},{5,7},{6,4},{7,5},{8,10},{9,11},{10,... | collective-permute-start | bytes 2359304 | tf_op jit(solution)/shard_map/ppermute | solution.py:673
  181.1 25.8 %collective-permute-start.32 = (bf16[512,768]{1,0:T(8,128)(2,1)S(1)}, bf16[512,768]{1,0:T(8,128)(2,1)S(1)}, u32[]{:S(2)}, u32[]{:S(2)}) collective-permute-start(bf16[512,768]{1,0:T(8,128)(2,1)S(1)} %fusion.1), channel_id=1, source_target_pairs={{0,2},{1,3},{2,0},{3,1},{4,6},{5,7},{6,4},{7,5},{8,10},{9,11},{10,... | collective-permute-start | bytes 2359304 | tf_op jit(solution)/shard_map/ppermute | solution.py:673
  192.0 6.8 %collective-permute-start.41 = (bf16[1,1,2,96,768]{4,3,2,1,0:T(8,128)(2,1)S(1)}, bf16[1,1,2,96,768]{4,3,2,1,0:T(8,128)(2,1)S(1)}, u32[]{:S(2)}, u32[]{:S(2)}) collective-permute-start(bf16[1,1,2,96,768]{4,3,2,1,0:T(8,128)(2,1)S(1)} %get-tuple-element.288), channel_id=1, source_target_pairs={{0,4},{4,0},{8,12},{12,8},{16,20},{20,16},{24,28},{28,24},{1,5},{5... | collective-permute-start | bytes 884744 | tf_op jit(solution)/shard_map/ppermute | solution.py:676
  195.6 12.0 %collective-permute-start.40 = (bf16[1,1,2,96,768]{4,3,2,1,0:T(8,128)(2,1)S(1)}, bf16[1,1,2,96,768]{4,3,2,1,0:T(8,128)(2,1)S(1)}, u32[]{:S(2)}, u32[]{:S(2)}) collective-permute-start(bf16[1,1,2,96,768]{4,3,2,1,0:T(8,128)(2,1)S(1)} %get-tuple-element.286), channel_id=1, source_target_pairs={{0,8},{4,12},{8,0},{12,4},{16,24},{20,28},{24,16},{28,20},{1,9},{5... | collective-permute-start | bytes 884744 | tf_op jit(solution)/shard_map/ppermute | solution.py:676
  195.7 13.6 %collective-permute-start.37 = (bf16[104,768]{1,0:T(8,128)(2,1)S(1)}, bf16[104,768]{1,0:T(8,128)(2,1)S(1)}, u32[]{:S(2)}, u32[]{:S(2)}) collective-permute-start(bf16[104,768]{1,0:T(8,128)(2,1)S(1)} %get-tuple-element.318), channel_id=1, source_target_pairs={{0,8},{4,12},{8,0},{12,4},{16,24},{20,28},{24,16},{28,20},{1,9},{5... | collective-permute-start | bytes 479240 | tf_op jit(solution)/shard_map/ppermute | solution.py:676
  197.8 11.6 %collective-permute-start.38 = (bf16[104,768]{1,0:T(8,128)(2,1)S(1)}, bf16[104,768]{1,0:T(8,128)(2,1)S(1)}, u32[]{:S(2)}, u32[]{:S(2)}) collective-permute-start(bf16[104,768]{1,0:T(8,128)(2,1)S(1)} %get-tuple-element.317), channel_id=1, source_target_pairs={{0,16},{4,20},{8,24},{12,28},{16,0},{20,4},{24,8},{28,12},{1,17},{... | collective-permute-start | bytes 479240 | tf_op jit(solution)/shard_map/ppermute | solution.py:676
  198.8 13.4 %collective-permute-start.39 = (bf16[104,768]{1,0:T(8,128)(2,1)S(1)}, bf16[104,768]{1,0:T(8,128)(2,1)S(1)}, u32[]{:S(2)}, u32[]{:S(2)}) collective-permute-start(bf16[104,768]{1,0:T(8,128)(2,1)S(1)} %get-tuple-element.316), channel_id=1, source_target_pairs={{0,24},{4,28},{8,16},{12,20},{16,8},{20,12},{24,0},{28,4},{1,25},{... | collective-permute-start | bytes 479240 | tf_op jit(solution)/shard_map/ppermute | solution.py:676
  206.9 24.0 %collective-permute-start.30 = (bf16[512,768]{1,0:T(8,128)(2,1)S(1)}, bf16[512,768]{1,0:T(8,128)(2,1)S(1)}, u32[]{:S(2)}, u32[]{:S(2)}) collective-permute-start(bf16[512,768]{1,0:T(8,128)(2,1)S(1)} %add_convert_fusion.1.refs_0_), channel_id=1, source_target_pairs={{0,1},{1,0},{2,3},{3,2},{4,5},{5,4},{6,7},{7,6},{8,9},{9,8},{10,11... | collective-permute-start | bytes 2359304 | tf_op jit(solution)/shard_map/ppermute | solution.py:673
  212.5 7.6 %collective-permute-start.42 = (bf16[1,1,104,768]{3,2,1,0:T(8,128)(2,1)S(1)}, bf16[1,1,104,768]{3,2,1,0:T(8,128)(2,1)S(1)}, u32[]{:S(2)}, u32[]{:S(2)}) collective-permute-start(bf16[1,1,104,768]{3,2,1,0:T(8,128)(2,1)S(1)} %fusion.2), channel_id=1, source_target_pairs={{0,8},{4,12},{8,0},{12,4},{16,24},{20,28},{24,16},{28,20},{1,9},{5... | collective-permute-start | bytes 479240 | tf_op jit(solution)/shard_map/ppermute | solution.py:676
  212.6 11.2 %collective-permute-start.43 = (bf16[1,1,104,768]{3,2,1,0:T(8,128)(2,1)S(1)}, bf16[1,1,104,768]{3,2,1,0:T(8,128)(2,1)S(1)}, u32[]{:S(2)}, u32[]{:S(2)}) collective-permute-start(bf16[1,1,104,768]{3,2,1,0:T(8,128)(2,1)S(1)} %fusion.2), channel_id=1, source_target_pairs={{0,16},{4,20},{8,24},{12,28},{16,0},{20,4},{24,8},{28,12},{1,17},{... | collective-permute-start | bytes 479240 | tf_op jit(solution)/shard_map/ppermute | solution.py:676
  214.6 9.1 %collective-permute-start.44 = (bf16[1,1,104,768]{3,2,1,0:T(8,128)(2,1)S(1)}, bf16[1,1,104,768]{3,2,1,0:T(8,128)(2,1)S(1)}, u32[]{:S(2)}, u32[]{:S(2)}) collective-permute-start(bf16[1,1,104,768]{3,2,1,0:T(8,128)(2,1)S(1)} %fusion.2), channel_id=1, source_target_pairs={{0,24},{4,28},{8,16},{12,20},{16,8},{20,12},{24,0},{28,4},{1,25},{... | collective-permute-start | bytes 479240 | tf_op jit(solution)/shard_map/ppermute | solution.py:676
  217.0 9.9 %collective-permute-start.45 = (bf16[1,2,2,96,768]{4,3,2,1,0:T(8,128)(2,1)S(1)}, bf16[1,2,2,96,768]{4,3,2,1,0:T(8,128)(2,1)S(1)}, u32[]{:S(2)}, u32[]{:S(2)}) collective-permute-start(bf16[1,2,2,96,768]{4,3,2,1,0:T(8,128)(2,1)S(1)} %pad_maximum_fusion.3), channel_id=1, source_target_pairs={{0,4},{4,0},{8,12},{12,8},{16,20},{20,16},{24,28},{28,24},{1,5},{5... | collective-permute-start | bytes 1769480 | tf_op jit(solution)/shard_map/ppermute | solution.py:676
  220.2 10.7 %collective-permute-start.33 = (bf16[512,768]{1,0:T(8,128)(2,1)S(1)}, bf16[512,768]{1,0:T(8,128)(2,1)S(1)}, u32[]{:S(2)}, u32[]{:S(2)}) collective-permute-start(bf16[512,768]{1,0:T(8,128)(2,1)S(1)} %add_convert_fusion.refs_2_), channel_id=1, source_target_pairs={{0,1},{1,0},{2,3},{3,2},{4,5},{5,4},{6,7},{7,6},{8,9},{9,8},{10,11... | collective-permute-start | bytes 2359304 | tf_op jit(solution)/shard_map/ppermute | solution.py:673
  227.2 10.9 %collective-permute-start.47 = (bf16[1,2,2,96,768]{4,3,2,1,0:T(8,128)(2,1)S(1)}, bf16[1,2,2,96,768]{4,3,2,1,0:T(8,128)(2,1)S(1)}, u32[]{:S(2)}, u32[]{:S(2)}) collective-permute-start(bf16[1,2,2,96,768]{4,3,2,1,0:T(8,128)(2,1)S(1)} %pad_maximum_fusion.4), channel_id=1, source_target_pairs={{0,8},{4,12},{8,0},{12,4},{16,24},{20,28},{24,16},{28,20},{1,9},{5... | collective-permute-start | bytes 1769480 | tf_op jit(solution)/shard_map/ppermute | solution.py:676
  227.2 13.4 %collective-permute-start.46 = (bf16[1,4,104,768]{3,2,1,0:T(8,128)(2,1)S(1)}, bf16[1,4,104,768]{3,2,1,0:T(8,128)(2,1)S(1)}, u32[]{:S(2)}, u32[]{:S(2)}) collective-permute-start(bf16[1,4,104,768]{3,2,1,0:T(8,128)(2,1)S(1)} %constant_dynamic-update-slice_fusion), channel_id=1, source_target_pairs={{0,4},{4,0},{8,12},{12,8},{16,20},{20,16},{24,28},{28,24},{1,5},{5... | collective-permute-start | bytes 1916936 | tf_op jit(solution)/shard_map/ppermute | solution.py:676
  (34 other events, 293.3 us)

commit v11 on v10

--- a/solution.py
+++ b/solution.py
@@ -11,7 +11,8 @@
 SPAN = 10
 EPS = 1e-05
 LOG2E = 1.4426950408889634
-KB = 256
+KF = 1024
+KB = 512
 VMEM = 12
 RB = 128
 HB = 256
@@ -118,14 +119,14 @@
 def forward_kernel(u, meta_ref, q_ref, k_ref, v_ref, own_ref, other_ref, lse_ref, s_ref):
     length = meta_ref[1 + u]
     step = pl.program_id(0)
-    blocks = lax.div(length + KB - 1, KB)
+    blocks = lax.div(length + KF - 1, KF)
     parts = lane_parts(q_ref[...] * jnp.asarray(0.125, BF))
     width = q_ref.shape[0]
 
     def first(kb, highest):
-        start = pl.multiple_of(kb * KB, KB)
-        rows = pl.ds(start, KB)
-        live = start + lax.broadcasted_iota(jnp.int32, (KB, width), 0) < length
+        start = pl.multiple_of(kb * KF, KF)
+        rows = pl.ds(start, KF)
+        live = start + lax.broadcasted_iota(jnp.int32, (KF, width), 0) < length
         out = []
         for h in range(3):
             tile = pl.ds(128 * TILE[h], 128)
@@ -139,7 +140,7 @@
     highest = lax.fori_loop(0, blocks, first, (floor,) * 3)
 
     def second(kb, carry):
-        rows = pl.ds(pl.multiple_of(kb * KB, KB), KB)
+        rows = pl.ds(pl.multiple_of(kb * KF, KF), KF)
         out = []
         for h in range(3):
             total, result = carry[h]
@@ -358,23 +359,33 @@
 
 def place_kernel(meta_ref, *refs):
     o_ref = refs[-1]
-    for i, r_ref in enumerate(refs[:-1]):
-
-        @pl.when(pl.program_id(0) == i)
+    for j in range(2):
+
+        @pl.when(pl.program_id(0) % 2 == j)
         def _():
-            o_ref[...] = r_ref[...]
-
-
-def place(meta, own, other):
-    half, d = own[0].shape
-    count = 2 * len(own)
+            if len(refs) == 3:
+                o_ref[...] = refs[j][...]
+            else:
+                count = (len(refs) - 1) // 2
+                for u in range(count):
+
+                    @pl.when(pl.program_id(0) // 2 == u)
+                    def _():
+                        o_ref[...] = refs[j * count + u][...]
+
+
+def place(meta, own, other, half):
+    d = own[0].shape[1]
+    count = 2 * sum(block.shape[0] for block in own) // half
+    one = len(own) == 1
+    spec = pl.BlockSpec((half, d), lambda i, m: (i // 2 if one else 0, 0))
     return call(
         place_kernel,
         "place",
         (count,),
         meta,
-        [block for pair in zip(own, other) for block in pair],
-        [fixed(half, d)] * count,
+        (*own, *other),
+        [spec] * (2 * len(own)),
         pl.BlockSpec((half, d), lambda i, m: (i ^ m[0], 0)),
         like((count * half, d), own[0].dtype),
     )
@@ -804,14 +815,8 @@
         out = done(fold(meta(), pairs, tuple(first_bit + order[step] for order in bit_orders), hold))
         return [(out[2 * i + 1], swap_dp(out[2 * i], 1 << bit_orders[i][step])) for i in range(2)]
 
-    inner, entry, so_far, near, crossed = [], [], (), [], []
+    inner, so_far, near = [], (), []
     out_other = [swap(r, 1) for r in out_rows]
-
-    def exchange(out):
-        got = swap(out[0], 1)
-        near.append((out[1], got))
-        crossed.append(swap(total(near[-1]), 2))
-        return got
 
     for u in range(seqs):
         last = u == seqs - 1
@@ -839,34 +844,33 @@
             start([first, second])
             token.extend(out_other)
         out = entry_step(u, dqkv, so_far)
-        entry.append(out)
+        near.append((out[1], swap(out[0], 1)))
         if not last:
             merge_got = swap(lax.optimization_barrier((res[4], out[0]))[0], 1)
             so_far = (out[2], res[3], merge_got)
             moving = scatter(2, moving, out[0])
-            exchange(out)
     qkv = Chain(out[2], stages)
     qkv.start()
 
-    got = exchange(out)
-    layer_output = place(meta(), out_rows, out_other)
-
-    finish([first, second], got)
-    finish([qkv], crossed[0])
+    layer_output = place(meta(), out_rows, out_other, half)
+
+    here = jnp.concatenate([total(pair) for pair in near], axis=0)
+    crossed = swap(here, 2)
+    finish([first, second], near[-1][1])
+    finish([qkv])
     together([qkv, first, second])
     start([qkv, first, second])
-    finish([qkv, first, second], crossed[-1])
+    finish([qkv, first, second])
     together([qkv, first, second])
     start([qkv, first])
-    ready = []
-    for u in range(seqs):
-        rest = near[u][0].astype(F32) + near[u][1].astype(F32) + crossed[u].astype(F32)
-        ready.append((inner[u][0] + rest).astype(BF))
-    input_grad = place(scalars, ready, [swap(r, 1) for r in ready])
-    finish([qkv, first], layer_output)
+    finish([qkv, first])
     together([qkv, first, second])
     start([qkv, second])
-    finish([qkv, second], input_grad)
+    crossed = lax.optimization_barrier((crossed, qkv.part))[0]
+    rest = jnp.concatenate([pair[0].astype(F32) + pair[1].astype(F32) for pair in near], axis=0)
+    ready = (jnp.concatenate([res[0] for res in inner], axis=0) + (rest + crossed.astype(F32))).astype(BF)
+    input_grad = place(scalars, [ready], [swap(ready, 1)], half)
+    finish([qkv, second], input_grad, layer_output)
     while qkv.steps or first.steps or second.steps:
         start([qkv, first, second])
         finish([qkv, first, second])

time: 247 us -> 269 us (1.089)
  local copies, waits for them, and re-layouts: 2.65 us -> 13.7 us
  Pallas kernels: 111 us -> 122 us
  starting transfers between devices: 44.6 us -> 40.2 us
    pallas_call x21, Pallas kernels: 111 us -> 122 us  [call(): pl.pallas_call(kernel, grid_spec=pltpu.PrefetchScalarGridSpec(num_scalar_...]
    unnamed x68 -> x98, local copies, waits for them, and re-layouts: 1.08 us -> 10.4 us
    ppermute x20, starting transfers between devices: 29 us -> 24.9 us  [swap_dp(): return lax.ppermute(value, 'dp', [(i, i ^ k) for i in range(groups)])]
    ppermute x20, waiting for transfers between devices: 40.2 us -> 43.4 us  [swap_dp(): return lax.ppermute(value, 'dp', [(i, i ^ k) for i in range(groups)])]
    ppermute x28 -> x26, waiting for transfers between devices: 31.3 us -> 28.4 us  [swap(): return lax.ppermute(value, 'tensor', [(i, i ^ k) for i in range(4)])]
    ppermute x28 -> x26, starting transfers between devices: 15.6 us -> 15.3 us  [swap(): return lax.ppermute(value, 'tensor', [(i, i ^ k) for i in range(4)])]
  transfers between devices with their start and end apart: 48 -> 46, of which waited for: 20 -> 15; matrix products, arithmetic and copies ran while one was open for 5% -> 5% of each run, Pallas kernels for 46% -> 46%
where the time goes in v11:
time: 269 us; the launch traced here: 264 us
  Pallas kernels  122 us (45%)
  waiting for transfers between devices  71.8 us (27%)
  starting transfers between devices  40.2 us (15%)
  other arithmetic  14.2 us (5%)
  local copies, waits for them, and re-layouts  13.7 us (5%)
    pallas_call x21, Pallas kernels, call(): pl.pallas_call(kernel, grid_spec=pltpu.PrefetchScalarGridSpec(num_scalar_...  122 us
    ppermute x20, waiting for transfers between devices, swap_dp(): return lax.ppermute(value, 'dp', [(i, i ^ k) for i in range(groups)])  43.4 us
    ppermute x26, waiting for transfers between devices, swap(): return lax.ppermute(value, 'tensor', [(i, i ^ k) for i in range(4)])  28.4 us
    ppermute x20, starting transfers between devices, swap_dp(): return lax.ppermute(value, 'dp', [(i, i ^ k) for i in range(groups)])  24.9 us
    ppermute x26, starting transfers between devices, swap(): return lax.ppermute(value, 'tensor', [(i, i ^ k) for i in range(4)])  15.3 us
    unnamed x98, local copies, waits for them, and re-layouts  10.4 us
  transfers between devices with their start and end apart: 46, of which 15 were waited for; matrix products, arithmetic and copies ran while one was open for 5% of the time, Pallas kernels for 46%

profile of v11, /device:TPU:0, one launch (start us, length us, event | category | flops | bytes accessed | tf_op | source)
XLA Modules:
  0.0 263.8 jit_solution(9517220887114584199)
XLA Ops:
  1.2 2.6 collective-permute-start.1
  5.0 4.4 %project.2 = (bf16[1024,256]{1,0:T(8,128)(2,1)S(1)}, bf16[1024,256]{1,0:T(8,128)(2,1)S(1)}, bf16[1024,256]{1,0:T(8,128)(2,1)S(1)}) custom-call(s32[6]{0:T(128)S(1)} %concatenate.33.meta_ref, bf16[2048,768]{1,0:T(8,128)(2,1)} %x_ref.7, bf16[192,768]{1,0:T(8,128)(2,1)} %bitcast.31, bf16[192,768]{1,0:T(8,128)(2,1)} %bitcast.35, bf16[192,768]{1,0:T(8,128)(2,1)} %bitcast.39), custom_call_target="tpu_custom_call" | custom-call | flops 3300000000 | bytes 1024 | tf_op jit(solution)/shard_map/project/pallas_call | solution.py:71
  9.5 5.6 %attend_forward.2 = (bf16[192,512]{1,0:T(8,128)(2,1)S(1)}, bf16[192,512]{1,0:T(8,128)(2,1)S(1)}, f32[2,8,512]{2,1,0:T(8,128)S(1)}) custom-call(s32[6]{0:T(128)S(1)} %concatenate.33.meta_ref, bf16[1024,256]{1,0:T(8,128)(2,1)S(1)} %get-tuple-element.148.q_ref, bf16[1024,256]{1,0:T(8,128)(2,1)S(1)} %get-tuple-element.150.k_ref, ...), custom_call_target="tpu_custom_call" | custom-call | flops 8800000000 | bytes 1024 | tf_op jit(solution)/shard_map/attend_forward/pallas_call | solution.py:71
  15.5 1.7 collective-permute-start.7
  17.6 1.6 collective-permute-start.6
  19.2 4.4 %project.3 = (bf16[1024,256]{1,0:T(8,128)(2,1)S(1)}, bf16[1024,256]{1,0:T(8,128)(2,1)S(1)}, bf16[1024,256]{1,0:T(8,128)(2,1)S(1)}) custom-call(s32[6]{0:T(128)S(1)} %concatenate.33.meta_ref, bf16[2048,768]{1,0:T(8,128)(2,1)} %x_ref.7, bf16[192,768]{1,0:T(8,128)(2,1)} %bitcast.32, bf16[192,768]{1,0:T(8,128)(2,1)} %bitcast.36, bf16[192,768]{1,0:T(8,128)(2,1)} %bitcast.40), custom_call_target="tpu_custom_call" | custom-call | flops 3300000000 | bytes 1024 | tf_op jit(solution)/shard_map/project/pallas_call | solution.py:71
  25.6 6.0 %attend_forward.3 = (bf16[192,512]{1,0:T(8,128)(2,1)S(1)}, bf16[192,512]{1,0:T(8,128)(2,1)S(1)}, f32[2,8,512]{2,1,0:T(8,128)S(1)}) custom-call(s32[6]{0:T(128)S(1)} %concatenate.33.meta_ref, bf16[1024,256]{1,0:T(8,128)(2,1)S(1)} %get-tuple-element.154.q_ref, bf16[1024,256]{1,0:T(8,128)(2,1)S(1)} %get-tuple-element.156.k_ref, ...), custom_call_target="tpu_custom_call" | custom-call | flops 8800000000 | bytes 1024 | tf_op jit(solution)/shard_map/attend_forward/pallas_call | solution.py:71
  34.7 1.6 collective-permute-start.9
  36.3 10.0 %ahead.2 = (f32[512,768]{1,0:T(8,128)}, f32[512,128]{1,0:T(8,128)}, bf16[512,768]{1,0:T(8,128)(2,1)S(1)}, bf16[512,1536]{1,0:T(8,128)(2,1)S(1)}, bf16[512,1536]{...) custom-call(s32[6]{0:T(128)S(1)} %concatenate.33.meta_ref, bf16[2048,768]{1,0:T(8,128)(2,1)} %x_ref.7, ...), custom_call_target="tpu_custom_call" | custom-call | flops 9900000256 | bytes 1024 | tf_op jit(solution)/shard_map/ahead/pallas_call | solution.py:71
  46.9 10.2 %ahead.3 = (f32[512,768]{1,0:T(8,128)}, f32[512,128]{1,0:T(8,128)}, bf16[512,768]{1,0:T(8,128)(2,1)S(1)}, bf16[512,1536]{1,0:T(8,128)(2,1)S(1)}, bf16[512,1536]{...) custom-call(s32[6]{0:T(128)S(1)} %concatenate.33.meta_ref, bf16[2048,768]{1,0:T(8,128)(2,1)} %x_ref.7, ...), custom_call_target="tpu_custom_call" | custom-call | flops 9900000256 | bytes 1024 | tf_op jit(solution)/shard_map/ahead/pallas_call | solution.py:71
  57.1 1.6 collective-permute-start.12
  58.7 8.1 %collective-permute-done.11.far_ref = bf16[512,768]{1,0:T(8,128)(2,1)S(1)} collective-permute-done((bf16[512,768]{1,0:T(8,128)(2,1)S(1)}, bf16[512,768]{1,0:T(8,128)(2,1)S(1)}, u32[]{:S(2)}, u32[]{:S(2)}) %collective-permute-start.11) | collective-permute-done | bytes 786464 | tf_op jit(solution)/shard_map/ppermute | solution.py:684
  66.8 9.2 %astern.2 = (bf16[512,768]{1,0:T(8,128)(2,1)}, bf16[512,768]{1,0:T(8,128)(2,1)S(1)}, bf16[512,1536]{1,0:T(8,128)(2,1)S(1)}, f32[512,768]{1,0:T(8,128)}, bf16[512...) custom-call(s32[6]{0:T(128)S(1)} %concatenate.33.meta_ref, f32[512,768]{1,0:T(8,128)S(1)} %get-tuple-element.166.own_ref, ...), custom_call_target="tpu_custom_call" | custom-call | flops 11000000512 | bytes 1024 | tf_op jit(solution)/shard_map/astern/pallas_call | solution.py:71
  76.0 3.2 %weight_grads.1 = (bf16[768,768]{1,0:T(8,128)(2,1)S(1)}, bf16[768,768]{1,0:T(8,128)(2,1)S(1)}, bf16[768,768]{1,0:T(8,128)(2,1)S(1)}, bf16[768,768]{1,0:T(8,128)(2,1)S(1)}) custom-call(s32[6]{0:T(128)S(1)} %concatenate.33.meta_ref, bf16[512,768]{1,0:T(8,128)(2,1)S(1)} %get-tuple-element.171.x_ref, bf16[512,768]{1,0:T(8,128)(2,1)S(1)} %get-tuple-element.172.g_ref, ...), custom_call_target="tpu_custom_call" | custom-call | flops 4400000000 | bytes 1024 | tf_op jit(solution)/shard_map/weight_grads/pallas_call | solution.py:71
  79.8 3.9 %collective-permute-done.12.far_ref = bf16[512,768]{1,0:T(8,128)(2,1)S(1)} collective-permute-done((bf16[512,768]{1,0:T(8,128)(2,1)S(1)}, bf16[512,768]{1,0:T(8,128)(2,1)S(1)}, u32[]{:S(2)}, u32[]{:S(2)}) %collective-permute-start.12) | collective-permute-done | bytes 786464 | tf_op jit(solution)/shard_map/ppermute | solution.py:684
  83.7 12.1 %astern.3 = (bf16[512,768]{1,0:T(8,128)(2,1)}, f32[512,768]{1,0:T(8,128)}, bf16[512,768]{1,0:T(8,128)(2,1)S(1)}, f32[2,768]{1,0:T(2,128)S(1)}, bf16[768,768]{1,0...) custom-call(s32[6]{0:T(128)S(1)} %concatenate.33.meta_ref, ...), custom_call_target="tpu_custom_call" | custom-call | flops 11000000512 | bytes 1024 | tf_op jit(solution)/shard_map/astern/pallas_call | solution.py:71
  102.4 5.6 %inner_norm.2 = (f32[512,768]{1,0:T(8,128)}, bf16[192,512]{1,0:T(8,128)(2,1)S(1)}, bf16[192,512]{1,0:T(8,128)(2,1)S(1)}, f32[192,768]{1,0:T(8,128)}, f32[192,768]{1,0:T(8,128)}, /*index=5*/f32[2,768]{1,0:T(2,128)S(1)}) custom-call(s32[6]{0:T(128)S(1)} %concatenate.33.meta_ref, f32[512,768]{1,0:T(8,128)} %get-tuple-element.187.own_ref, ...), custom_call_target="tpu_custom_call" | custom-call | flops 3300000000 | bytes 1024 | tf_op jit(solution)/shard_map/inner_norm/pallas_call | solution.py:71
  109.6 1.7 collective-permute-start.17
  111.3 1.6 collective-permute-start.18
  112.9 11.6 %attend_backward.2 = (bf16[1024,256]{1,0:T(8,128)(2,1)S(1)}, bf16[1024,256]{1,0:T(8,128)(2,1)S(1)}, bf16[1024,256]{1,0:T(8,128)(2,1)S(1)}) custom-call(s32[6]{0:T(128)S(1)} %concatenate.33.meta_ref, bf16[1024,256]{1,0:T(8,128)(2,1)} %copy-done.39, bf16[1024,256]{1,0:T(8,128)(2,1)} %copy-done.40, bf16[1024,256]{1,0:T(8,128)(2,1)} %copy-done.41, ...), custom_call_target="tpu_custom_call" | custom-call | flops 13200000000 | bytes 1024 | tf_op jit(solution)/shard_map/attend_backward/pallas_call | solution.py:71
  124.5 2.3 collective-permute-done.18.refs_3_
  127.6 1.6 collective-permute-start.20
  129.2 5.5 %inner_norm.3 = (f32[512,768]{1,0:T(8,128)}, bf16[192,512]{1,0:T(8,128)(2,1)S(1)}, bf16[192,512]{1,0:T(8,128)(2,1)S(1)}, bf16[256,768]{1,0:T(8,128)(2,1)S(1)}, b...) custom-call(s32[6]{0:T(128)S(1)} %concatenate.33.meta_ref, f32[512,768]{1,0:T(8,128)} %get-tuple-element.220.own_ref, ...), custom_call_target="tpu_custom_call" | custom-call | flops 3300000000 | bytes 1024 | tf_op jit(solution)/shard_map/inner_norm/pallas_call | solution.py:71
  135.2 7.0 %entry_back.2 = (bf16[512,768]{1,0:T(8,128)(2,1)}, bf16[512,768]{1,0:T(8,128)(2,1)S(1)}, f32[576,768]{1,0:T(8,128)S(1)}) custom-call(s32[6]{0:T(128)S(1)} %concatenate.33.meta_ref, bf16[2048,768]{1,0:T(8,128)(2,1)} %x_ref.7, bf16[1024,256]{1,0:T(8,128)(2,1)S(1)} %get-tuple-element.209.dq_ref, bf16[1024,256]{1,0:T(8,128)(2,1)S(1)} %get-tuple-element.231.dk_ref, ...), custom_call_target="tpu_custom_call" | custom-call | flops 5500000256 | bytes 1024 | tf_op jit(solution)/shard_map/entry_back/pallas_call | solution.py:71
  143.5 2.7 %collective-permute-start.23 = (bf16[96,768]{1,0:T(8,128)(2,1)S(1)}, bf16[96,768]{1,0:T(8,128)(2,1)S(1)}, u32[]{:S(2)}, u32[]{:S(2)}) collective-permute-start(bf16[96,768]{1,0:T(8,128)(2,1)S(1)} %get-tuple-element.242), channel_id=1, source_target_pairs={{0,16},{4,20},{8,24},{12,28},{16,0},{20,4},{24,8},{28,12},{1,17},{... | collective-permute-start | bytes 442376 | tf_op jit(solution)/shard_map/ppermute | solution.py:687
  146.9 11.6 %attend_backward.3 = (bf16[1024,256]{1,0:T(8,128)(2,1)S(1)}, bf16[1024,256]{1,0:T(8,128)(2,1)S(1)}, bf16[1024,256]{1,0:T(8,128)(2,1)S(1)}) custom-call(s32[6]{0:T(128)S(1)} %concatenate.33.meta_ref, bf16[1024,256]{1,0:T(8,128)(2,1)} %copy-done.36, bf16[1024,256]{1,0:T(8,128)(2,1)} %copy-done.37, bf16[1024,256]{1,0:T(8,128)(2,1)} %copy-done.38, ...), custom_call_target="tpu_custom_call" | custom-call | flops 13200000000 | bytes 1024 | tf_op jit(solution)/shard_map/attend_backward/pallas_call | solution.py:71
  158.4 1.6 collective-permute-done.24.refs_3_
  161.6 7.0 %entry_back.3 = (bf16[512,768]{1,0:T(8,128)(2,1)}, bf16[512,768]{1,0:T(8,128)(2,1)S(1)}, bf16[832,768]{1,0:T(8,128)(2,1)S(1)}) custom-call(s32[6]{0:T(128)S(1)} %concatenate.33.meta_ref, bf16[2048,768]{1,0:T(8,128)(2,1)} %x_ref.7, bf16[1024,256]{1,0:T(8,128)(2,1)S(1)} %get-tuple-element.247.dq_ref, bf16[1024,256]{1,0:T(8,128)(2,1)S(1)} %get-tuple-element.258.dk_ref, ...), custom_call_target="tpu_custom_call" | custom-call | flops 5500000256 | bytes 1024 | tf_op jit(solution)/shard_map/entry_back/pallas_call | solution.py:71
  171.8 1.9 collective-permute-start.32
  173.7 2.5 fusion.2
  176.2 10.4 %collective-permute-done.31 = bf16[416,768]{1,0:T(8,128)(2,1)} collective-permute-done((bf16[416,768]{1,0:T(8,128)(2,1)}, bf16[416,768]{1,0:T(8,128)(2,1)}, u32[]{:S(2)}, u32[]{:S(2)}) %collective-permute-start.31) | collective-permute-done | bytes 639008 | tf_op jit(solution)/shard_map/ppermute | solution.py:687
  189.2 2.1 collective-permute-start.34
  192.4 1.4 collective-permute-start.36
  193.8 1.3 fusion.3
  196.4 8.3 %collective-permute-done.34 = bf16[104,768]{1,0:T(8,128)(2,1)S(1)} collective-permute-done((bf16[104,768]{1,0:T(8,128)(2,1)S(1)}, bf16[104,768]{1,0:T(8,128)(2,1)S(1)}, u32[]{:S(2)}, u32[]{:S(2)}) %collective-permute-start.34) | collective-permute-done | bytes 159776 | tf_op jit(solution)/shard_map/ppermute | solution.py:687
  204.7 1.5 collective-permute-start.30
  206.2 2.4 collective-permute-done.36
  209.9 3.8 %collective-permute-start.40 = (bf16[1,1,104,768]{3,2,1,0:T(8,128)(2,1)S(1)}, bf16[1,1,104,768]{3,2,1,0:T(8,128)(2,1)S(1)}, u32[]{:S(2)}, u32[]{:S(2)}) collective-permute-start(bf16[1,1,104,768]{3,2,1,0:T(8,128)(2,1)S(1)} %fusion.1), channel_id=1, source_target_pairs={{0,16},{4,20},{8,24},{12,28},{16,0},{20,4},{24,8},{28,12},{1,17},{... | collective-permute-start | bytes 479240 | tf_op jit(solution)/shard_map/ppermute | solution.py:687
  214.4 4.3 %collective-permute-done.39 = bf16[1,1,104,768]{3,2,1,0:T(8,128)(2,1)} collective-permute-done((bf16[1,1,104,768]{3,2,1,0:T(8,128)(2,1)S(1)}, bf16[1,1,104,768]{3,2,1,0:T(8,128)(2,1)}, u32[]{:S(2)}, u32[]{:S(2)}) %collective-permute-start.39) | collective-permute-done | bytes 159776 | tf_op jit(solution)/shard_map/ppermute | solution.py:687
  219.6 4.2 %collective-permute-done.40 = bf16[1,1,104,768]{3,2,1,0:T(8,128)(2,1)S(1)} collective-permute-done((bf16[1,1,104,768]{3,2,1,0:T(8,128)(2,1)S(1)}, bf16[1,1,104,768]{3,2,1,0:T(8,128)(2,1)S(1)}, u32[]{:S(2)}, u32[]{:S(2)}) %collective-permute-start.40) | collective-permute-done | bytes 159776 | tf_op jit(solution)/shard_map/ppermute | solution.py:687
  224.1 15.3 %collective-permute-done.30 = bf16[1024,768]{1,0:T(8,128)(2,1)} collective-permute-done((bf16[1024,768]{1,0:T(8,128)(2,1)}, bf16[1024,768]{1,0:T(8,128)(2,1)}, u32[]{:S(2)}, u32[]{:S(2)}) %collective-permute-start.30) | collective-permute-done | bytes 1572896 | tf_op jit(solution)/shard_map/ppermute | solution.py:684
  239.5 2.3 fusion.refs_0_
  242.8 2.7 %place.2 = bf16[2048,768]{1,0:T(8,128)(2,1)} custom-call(s32[6]{0:T(128)S(1)} %concatenate.33.meta_ref, bf16[512,768]{1,0:T(8,128)(2,1)S(1)} %copy-done.7, bf16[512,768]{1,0:T(8,128)(2,1)S(1)} %copy-done.8, bf16[512,768]{1,0:T(8,128)(2,1)S(1)} %copy-done.10, bf16[512,768]{1,0:T(8,128)(2,1)S(1)} %copy-done.12), custom_call_target="tpu_custom_call" | custom-call | flops 3300000000 | bytes 1024 | tf_op jit(solution)/shard_map/place/pallas_call | solution.py:71
  245.5 1.6 convert_element_type.89
  247.1 2.7 %place.3 = bf16[2048,768]{1,0:T(8,128)(2,1)} custom-call(s32[6]{0:T(128)S(1)} %concatenate.33.meta_ref, bf16[1024,768]{1,0:T(8,128)(2,1)S(1)} %fusion.refs_0_, bf16[1024,768]{1,0:T(8,128)(2,1)S(1)} %collective-permute-done.43.refs_1_), custom_call_target="tpu_custom_call" | custom-call | flops 3300000000 | bytes 1024 | tf_op jit(solution)/shard_map/place/pallas_call | solution.py:71
  249.8 8.9 %collective-permute-done.44 = bf16[1,4,104,768]{3,2,1,0:T(8,128)(2,1)S(1)} collective-permute-done((bf16[1,4,104,768]{3,2,1,0:T(8,128)(2,1)S(1)}, bf16[1,4,104,768]{3,2,1,0:T(8,128)(2,1)S(1)}, u32[]{:S(2)}, u32[]{:S(2)}) %collective-permute-start.44) | collective-permute-done | bytes 639008 | tf_op jit(solution)/shard_map/ppermute | solution.py:687
  258.9 1.4 slice_convert_fusion
  261.1 1.7 bitcast_convert_fusion
  (200 shorter events, 35.5 us)
Async XLA Ops:
  0.6 14.6 %collective-permute-start = (bf16[192,768]{1,0:T(8,128)(2,1)}, bf16[192,768]{1,0:T(8,128)(2,1)S(1)}, u32[]{:S(2)}, u32[]{:S(2)}) collective-permute-start(bf16[192,768]{1,0:T(8,128)(2,1)} %w0.7), channel_id=1, source_target_pairs={{0,1},{1,0},{2,3},{3,2},{4,5},{5,4},{6,7},{7,6},{8,9},{9,8},{10,11... | collective-permute-start | bytes 884744 | tf_op jit(solution)/shard_map/ppermute | solution.py:684
  1.2 14.3 %collective-permute-start.1 = (bf16[192,768]{1,0:T(8,128)(2,1)}, bf16[192,768]{1,0:T(8,128)(2,1)S(1)}, u32[]{:S(2)}, u32[]{:S(2)}) collective-permute-start(bf16[192,768]{1,0:T(8,128)(2,1)} %w0.7), channel_id=1, source_target_pairs={{0,2},{1,3},{2,0},{3,1},{4,6},{5,7},{6,4},{7,5},{8,10},{9,11},{10,... | collective-permute-start | bytes 884744 | tf_op jit(solution)/shard_map/ppermute | solution.py:684
  3.7 13.9 %collective-permute-start.2 = (bf16[192,768]{1,0:T(8,128)(2,1)}, bf16[192,768]{1,0:T(8,128)(2,1)S(1)}, u32[]{:S(2)}, u32[]{:S(2)}) collective-permute-start(bf16[192,768]{1,0:T(8,128)(2,1)} %w0.7), channel_id=1, source_target_pairs={{0,3},{1,2},{2,1},{3,0},{4,7},{5,6},{6,5},{7,4},{8,11},{9,10},{10,... | collective-permute-start | bytes 884744 | tf_op jit(solution)/shard_map/ppermute | solution.py:684
  3.8 19.8 %collective-permute-start.3 = (bf16[768,768]{1,0:T(8,128)(2,1)}, bf16[768,768]{1,0:T(8,128)(2,1)S(1)}, u32[]{:S(2)}, u32[]{:S(2)}) collective-permute-start(bf16[768,768]{1,0:T(8,128)(2,1)} %ua_ref.7), channel_id=1, source_target_pairs={{0,1},{1,0},{2,3},{3,2},{4,5},{5,4},{6,7},{7,6},{8,9},{9,8},{10,11... | collective-permute-start | bytes 3538952 | tf_op jit(solution)/shard_map/ppermute | solution.py:684
  3.9 20.6 %collective-permute-start.4 = (bf16[768,768]{1,0:T(8,128)(2,1)}, bf16[768,768]{1,0:T(8,128)(2,1)S(1)}, u32[]{:S(2)}, u32[]{:S(2)}) collective-permute-start(bf16[768,768]{1,0:T(8,128)(2,1)} %da_ref.7), channel_id=1, source_target_pairs={{0,1},{1,0},{2,3},{3,2},{4,5},{5,4},{6,7},{7,6},{8,9},{9,8},{10,11... | collective-permute-start | bytes 3538952 | tf_op jit(solution)/shard_map/ppermute | solution.py:684
  15.1 21.1 %copy-start.25 = (bf16[192,512]{1,0:T(8,128)(2,1)}, bf16[192,512]{1,0:T(8,128)(2,1)S(1)}, u32[]{:S(2)}) copy-start(bf16[192,512]{1,0:T(8,128)(2,1)S(1)} %get-tuple-element.152.a0.o0_ref) | copy-start | bytes 589828
  15.2 31.6 %copy-start.18 = (bf16[192,768]{1,0:T(8,128)(2,1)}, bf16[192,768]{1,0:T(8,128)(2,1)S(1)}, u32[]{:S(2)}) copy-start(bf16[192,768]{1,0:T(8,128)(2,1)S(1)} %collective-permute-done.w1) | copy-start | bytes 884740
  15.3 19.4 %collective-permute-start.5 = (bf16[192,512]{1,0:T(8,128)(2,1)S(1)}, bf16[192,512]{1,0:T(8,128)(2,1)S(1)}, u32[]{:S(2)}, u32[]{:S(2)}) collective-permute-start(bf16[192,512]{1,0:T(8,128)(2,1)S(1)} %get-tuple-element.160.o1_ref), channel_id=1, source_target_pairs={{0,1},{1,0},{2,3},{3,2},{4,5},{5,4},{6,7},{7,6},{8,9},{9,8},{10,11... | collective-permute-start | bytes 589832 | tf_op jit(solution)/shard_map/ppermute | solution.py:684
  15.5 20.8 %collective-permute-start.7 = (bf16[192,512]{1,0:T(8,128)(2,1)S(1)}, bf16[192,512]{1,0:T(8,128)(2,1)S(1)}, u32[]{:S(2)}, u32[]{:S(2)}) collective-permute-start(bf16[192,512]{1,0:T(8,128)(2,1)S(1)} %get-tuple-element.160.o1_ref), channel_id=1, source_target_pairs={{0,3},{1,2},{2,1},{3,0},{4,7},{5,6},{6,5},{7,4},{8,11},{9,10},{10,... | collective-permute-start | bytes 589832 | tf_op jit(solution)/shard_map/ppermute | solution.py:684
  17.6 18.6 %collective-permute-start.6 = (bf16[192,512]{1,0:T(8,128)(2,1)S(1)}, bf16[192,512]{1,0:T(8,128)(2,1)S(1)}, u32[]{:S(2)}, u32[]{:S(2)}) collective-permute-start(bf16[192,512]{1,0:T(8,128)(2,1)S(1)} %get-tuple-element.152.a0.o0_ref), channel_id=1, source_target_pairs={{0,2},{1,3},{2,0},{3,1},{4,6},{5,7},{6,4},{7,5},{8,10},{9,11},{10,... | collective-permute-start | bytes 589832 | tf_op jit(solution)/shard_map/ppermute | solution.py:684
  34.1 12.8 %collective-permute-start.10 = (bf16[192,512]{1,0:T(8,128)(2,1)S(1)}, bf16[192,512]{1,0:T(8,128)(2,1)S(1)}, u32[]{:S(2)}, u32[]{:S(2)}) collective-permute-start(bf16[192,512]{1,0:T(8,128)(2,1)S(1)} %get-tuple-element.163.o1_ref), channel_id=1, source_target_pairs={{0,3},{1,2},{2,1},{3,0},{4,7},{5,6},{6,5},{7,4},{8,11},{9,10},{10,... | collective-permute-start | bytes 589832 | tf_op jit(solution)/shard_map/ppermute | solution.py:684
  34.1 12.8 %collective-permute-start.8 = (bf16[192,512]{1,0:T(8,128)(2,1)S(1)}, bf16[192,512]{1,0:T(8,128)(2,1)S(1)}, u32[]{:S(2)}, u32[]{:S(2)}) collective-permute-start(bf16[192,512]{1,0:T(8,128)(2,1)S(1)} %get-tuple-element.163.o1_ref), channel_id=1, source_target_pairs={{0,1},{1,0},{2,3},{3,2},{4,5},{5,4},{6,7},{7,6},{8,9},{9,8},{10,11... | collective-permute-start | bytes 589832 | tf_op jit(solution)/shard_map/ppermute | solution.py:684
  34.7 12.2 %collective-permute-start.9 = (bf16[192,512]{1,0:T(8,128)(2,1)S(1)}, bf16[192,512]{1,0:T(8,128)(2,1)S(1)}, u32[]{:S(2)}, u32[]{:S(2)}) collective-permute-start(bf16[192,512]{1,0:T(8,128)(2,1)S(1)} %get-tuple-element.158.a0.o0_ref), channel_id=1, source_target_pairs={{0,2},{1,3},{2,0},{3,1},{4,6},{5,7},{6,4},{7,5},{8,10},{9,11},{10,... | collective-permute-start | bytes 589832 | tf_op jit(solution)/shard_map/ppermute | solution.py:684
  46.3 20.5 %collective-permute-start.11 = (bf16[512,768]{1,0:T(8,128)(2,1)S(1)}, bf16[512,768]{1,0:T(8,128)(2,1)S(1)}, u32[]{:S(2)}, u32[]{:S(2)}) collective-permute-start(bf16[512,768]{1,0:T(8,128)(2,1)S(1)} %get-tuple-element.167), channel_id=1, source_target_pairs={{0,2},{1,3},{2,0},{3,1},{4,6},{5,7},{6,4},{7,5},{8,10},{9,11},{10,... | collective-permute-start | bytes 2359304 | tf_op jit(solution)/shard_map/ppermute | solution.py:684
  57.1 26.6 %collective-permute-start.12 = (bf16[512,768]{1,0:T(8,128)(2,1)S(1)}, bf16[512,768]{1,0:T(8,128)(2,1)S(1)}, u32[]{:S(2)}, u32[]{:S(2)}) collective-permute-start(bf16[512,768]{1,0:T(8,128)(2,1)S(1)} %get-tuple-element.178), channel_id=1, source_target_pairs={{0,2},{1,3},{2,0},{3,1},{4,6},{5,7},{6,4},{7,5},{8,10},{9,11},{10,... | collective-permute-start | bytes 2359304 | tf_op jit(solution)/shard_map/ppermute | solution.py:684
  79.2 20.1 %collective-permute-start.13 = (bf16[512,768]{1,0:T(8,128)(2,1)S(1)}, bf16[512,768]{1,0:T(8,128)(2,1)S(1)}, u32[]{:S(2)}, u32[]{:S(2)}) collective-permute-start(bf16[512,768]{1,0:T(8,128)(2,1)S(1)} %get-tuple-element.188), channel_id=1, source_target_pairs={{0,2},{1,3},{2,0},{3,1},{4,6},{5,7},{6,4},{7,5},{8,10},{9,11},{10,... | collective-permute-start | bytes 2359304 | tf_op jit(solution)/shard_map/ppermute | solution.py:684
  100.2 8.3 %collective-permute-start.15 = (bf16[768,768]{1,0:T(8,128)(2,1)}, bf16[768,768]{1,0:T(8,128)(2,1)S(1)}, u32[]{:S(2)}, u32[]{:S(2)}) collective-permute-start(bf16[768,768]{1,0:T(8,128)(2,1)} %get-tuple-element.201), channel_id=1, source_target_pairs={{0,1},{1,0},{2,3},{3,2},{4,5},{5,4},{6,7},{7,6},{8,9},{9,8},{10,11... | collective-permute-start | bytes 3538952 | tf_op jit(solution)/shard_map/ppermute | solution.py:684
  100.2 8.3 %collective-permute-start.14 = (bf16[768,768]{1,0:T(8,128)(2,1)}, bf16[768,768]{1,0:T(8,128)(2,1)S(1)}, u32[]{:S(2)}, u32[]{:S(2)}) collective-permute-start(bf16[768,768]{1,0:T(8,128)(2,1)} %get-tuple-element.197), channel_id=1, source_target_pairs={{0,1},{1,0},{2,3},{3,2},{4,5},{5,4},{6,7},{7,6},{8,9},{9,8},{10,11... | collective-permute-start | bytes 3538952 | tf_op jit(solution)/shard_map/ppermute | solution.py:684
  100.7 60.0 %collective-permute-start.25 = (bf16[512,768]{1,0:T(8,128)(2,1)S(1)}, bf16[512,768]{1,0:T(8,128)(2,1)S(1)}, u32[]{:S(2)}, u32[]{:S(2)}) collective-permute-start(bf16[512,768]{1,0:T(8,128)(2,1)S(1)} %copy-done.6), channel_id=1, source_target_pairs={{0,1},{1,0},{2,3},{3,2},{4,5},{5,4},{6,7},{7,6},{8,9},{9,8},{10,11... | collective-permute-start | bytes 2359304 | tf_op jit(solution)/shard_map/ppermute | solution.py:684
  100.7 60.9 %collective-permute-start.26 = (bf16[512,768]{1,0:T(8,128)(2,1)}, bf16[512,768]{1,0:T(8,128)(2,1)S(1)}, u32[]{:S(2)}, u32[]{:S(2)}) collective-permute-start(bf16[512,768]{1,0:T(8,128)(2,1)} %get-tuple-element.185.refs_1_), channel_id=1, source_target_pairs={{0,1},{1,0},{2,3},{3,2},{4,5},{5,4},{6,7},{7,6},{8,9},{9,8},{10,11... | collective-permute-start | bytes 2359304 | tf_op jit(solution)/shard_map/ppermute | solution.py:684
  108.0 21.2 %collective-permute-start.19 = (bf16[512,768]{1,0:T(8,128)(2,1)S(1)}, bf16[512,768]{1,0:T(8,128)(2,1)S(1)}, u32[]{:S(2)}, u32[]{:S(2)}) collective-permute-start(bf16[512,768]{1,0:T(8,128)(2,1)S(1)} %copy-done.14), channel_id=1, source_target_pairs={{0,2},{1,3},{2,0},{3,1},{4,6},{5,7},{6,4},{7,5},{8,10},{9,11},{10,... | collective-permute-start | bytes 2359304 | tf_op jit(solution)/shard_map/ppermute | solution.py:684
  108.5 2.9 %collective-permute-start.16 = (bf16[192,512]{1,0:T(8,128)(2,1)S(1)}, bf16[192,512]{1,0:T(8,128)(2,1)S(1)}, u32[]{:S(2)}, u32[]{:S(2)}) collective-permute-start(bf16[192,512]{1,0:T(8,128)(2,1)S(1)} %get-tuple-element.207), channel_id=1, source_target_pairs={{0,1},{1,0},{2,3},{3,2},{4,5},{5,4},{6,7},{7,6},{8,9},{9,8},{10,11... | collective-permute-start | bytes 589832 | tf_op jit(solution)/shard_map/ppermute | solution.py:684
  109.6 17.1 %collective-permute-start.17 = (bf16[384,768]{1,0:T(8,128)(2,1)S(1)}, bf16[384,768]{1,0:T(8,128)(2,1)S(1)}, u32[]{:S(2)}, u32[]{:S(2)}) collective-permute-start(bf16[384,768]{1,0:T(8,128)(2,1)S(1)} %get-tuple-element.204), channel_id=1, source_target_pairs={{0,4},{4,0},{8,12},{12,8},{16,20},{20,16},{24,28},{28,24},{1,5},{5... | collective-permute-start | bytes 1769480 | tf_op jit(solution)/shard_map/ppermute | solution.py:687
  111.3 15.4 %collective-permute-start.18 = (bf16[384,768]{1,0:T(8,128)(2,1)S(1)}, bf16[384,768]{1,0:T(8,128)(2,1)S(1)}, u32[]{:S(2)}, u32[]{:S(2)}) collective-permute-start(bf16[384,768]{1,0:T(8,128)(2,1)S(1)} %get-tuple-element.215), channel_id=1, source_target_pairs={{0,8},{4,12},{8,0},{12,4},{16,24},{20,28},{24,16},{28,20},{1,9},{5... | collective-permute-start | bytes 1769480 | tf_op jit(solution)/shard_map/ppermute | solution.py:687
  127.6 15.2 %collective-permute-start.20 = (bf16[192,768]{1,0:T(8,128)(2,1)S(1)}, bf16[192,768]{1,0:T(8,128)(2,1)S(1)}, u32[]{:S(2)}, u32[]{:S(2)}) collective-permute-start(bf16[192,768]{1,0:T(8,128)(2,1)S(1)} %get-tuple-element.218), channel_id=1, source_target_pairs={{0,8},{4,12},{8,0},{12,4},{16,24},{20,28},{24,16},{28,20},{1,9},{5... | collective-permute-start | bytes 884744 | tf_op jit(solution)/shard_map/ppermute | solution.py:687
  134.7 8.0 %collective-permute-start.21 = (bf16[192,768]{1,0:T(8,128)(2,1)S(1)}, bf16[192,768]{1,0:T(8,128)(2,1)S(1)}, u32[]{:S(2)}, u32[]{:S(2)}) collective-permute-start(bf16[192,768]{1,0:T(8,128)(2,1)S(1)} %get-tuple-element.239), channel_id=1, source_target_pairs={{0,4},{4,0},{8,12},{12,8},{16,20},{20,16},{24,28},{28,24},{1,5},{5... | collective-permute-start | bytes 884744 | tf_op jit(solution)/shard_map/ppermute | solution.py:687
  142.3 19.4 %collective-permute-start.27 = (bf16[256,768]{1,0:T(8,128)(2,1)S(1)}, bf16[256,768]{1,0:T(8,128)(2,1)S(1)}, u32[]{:S(2)}, u32[]{:S(2)}) collective-permute-start(bf16[256,768]{1,0:T(8,128)(2,1)S(1)} %get-tuple-element.263), channel_id=1, source_target_pairs={{0,1},{1,0},{2,3},{3,2},{4,5},{5,4},{6,7},{7,6},{8,9},{9,8},{10,11... | collective-permute-start | bytes 1179656 | tf_op jit(solution)/shard_map/ppermute | solution.py:684
  142.7 3.4 %collective-permute-start.22 = (bf16[192,512]{1,0:T(8,128)(2,1)S(1)}, bf16[192,512]{1,0:T(8,128)(2,1)S(1)}, u32[]{:S(2)}, u32[]{:S(2)}) collective-permute-start(bf16[192,512]{1,0:T(8,128)(2,1)S(1)} %get-tuple-element.245), channel_id=1, source_target_pairs={{0,1},{1,0},{2,3},{3,2},{4,5},{5,4},{6,7},{7,6},{8,9},{9,8},{10,11... | collective-permute-start | bytes 589832 | tf_op jit(solution)/shard_map/ppermute | solution.py:684
  143.5 16.6 %collective-permute-start.23 = (bf16[96,768]{1,0:T(8,128)(2,1)S(1)}, bf16[96,768]{1,0:T(8,128)(2,1)S(1)}, u32[]{:S(2)}, u32[]{:S(2)}) collective-permute-start(bf16[96,768]{1,0:T(8,128)(2,1)S(1)} %get-tuple-element.242), channel_id=1, source_target_pairs={{0,16},{4,20},{8,24},{12,28},{16,0},{20,4},{24,8},{28,12},{1,17},{... | collective-permute-start | bytes 442376 | tf_op jit(solution)/shard_map/ppermute | solution.py:687
  146.1 13.9 %collective-permute-start.24 = (bf16[96,768]{1,0:T(8,128)(2,1)S(1)}, bf16[96,768]{1,0:T(8,128)(2,1)S(1)}, u32[]{:S(2)}, u32[]{:S(2)}) collective-permute-start(bf16[96,768]{1,0:T(8,128)(2,1)S(1)} %get-tuple-element.253), channel_id=1, source_target_pairs={{0,16},{4,20},{8,24},{12,28},{16,0},{20,4},{24,8},{28,12},{1,17},{... | collective-permute-start | bytes 442376 | tf_op jit(solution)/shard_map/ppermute | solution.py:687
  160.0 13.7 %collective-permute-start.28 = (bf16[512,768]{1,0:T(8,128)(2,1)}, bf16[512,768]{1,0:T(8,128)(2,1)}, u32[]{:S(2)}, u32[]{:S(2)}) collective-permute-start(bf16[512,768]{1,0:T(8,128)(2,1)} %get-tuple-element.233), channel_id=1, source_target_pairs={{0,1},{1,0},{2,3},{3,2},{4,5},{5,4},{6,7},{7,6},{8,9},{9,8},{10,11... | collective-permute-start | bytes 2359304 | tf_op jit(solution)/shard_map/ppermute | solution.py:684
  169.5 17.1 %collective-permute-start.31 = (bf16[416,768]{1,0:T(8,128)(2,1)}, bf16[416,768]{1,0:T(8,128)(2,1)}, u32[]{:S(2)}, u32[]{:S(2)}) collective-permute-start(bf16[416,768]{1,0:T(8,128)(2,1)} %constant_dynamic-slice_fusion.3), channel_id=1, source_target_pairs={{0,4},{4,0},{8,12},{12,8},{16,20},{20,16},{24,28},{28,24},{1,5},{5... | collective-permute-start | bytes 1916936 | tf_op jit(solution)/shard_map/ppermute | solution.py:687
  170.6 17.2 %collective-permute-start.29 = (bf16[512,768]{1,0:T(8,128)(2,1)}, bf16[512,768]{1,0:T(8,128)(2,1)}, u32[]{:S(2)}, u32[]{:S(2)}) collective-permute-start(bf16[512,768]{1,0:T(8,128)(2,1)} %get-tuple-element.264), channel_id=1, source_target_pairs={{0,1},{1,0},{2,3},{3,2},{4,5},{5,4},{6,7},{7,6},{8,9},{9,8},{10,11... | collective-permute-start | bytes 2359304 | tf_op jit(solution)/shard_map/ppermute | solution.py:684
  170.8 17.0 %collective-permute-start.33 = (bf16[1,1,1,96,768]{4,3,2,1,0:T(8,128)(2,1)S(1)}, bf16[1,1,1,96,768]{4,3,2,1,0:T(8,128)(2,1)S(1)}, u32[]{:S(2)}, u32[]{:S(2)}) collective-permute-start(bf16[1,1,1,96,768]{4,3,2,1,0:T(8,128)(2,1)S(1)} %bitcast.27), channel_id=1, source_target_pairs={{0,16},{4,20},{8,24},{12,28},{16,0},{20,4},{24,8},{28,12},{1,17},{... | collective-permute-start | bytes 442376 | tf_op jit(solution)/shard_map/ppermute | solution.py:687
  171.8 16.0 %collective-permute-start.32 = (bf16[1,1,1,96,768]{4,3,2,1,0:T(8,128)(2,1)S(1)}, bf16[1,1,1,96,768]{4,3,2,1,0:T(8,128)(2,1)S(1)}, u32[]{:S(2)}, u32[]{:S(2)}) collective-permute-start(bf16[1,1,1,96,768]{4,3,2,1,0:T(8,128)(2,1)S(1)} %bitcast.26), channel_id=1, source_target_pairs={{0,16},{4,20},{8,24},{12,28},{16,0},{20,4},{24,8},{28,12},{1,17},{... | collective-permute-start | bytes 442376 | tf_op jit(solution)/shard_map/ppermute | solution.py:687
  187.9 20.7 %collective-permute-start.38 = (bf16[1,1,2,96,768]{4,3,2,1,0:T(8,128)(2,1)S(1)}, bf16[1,1,2,96,768]{4,3,2,1,0:T(8,128)(2,1)S(1)}, u32[]{:S(2)}, u32[]{:S(2)}) collective-permute-start(bf16[1,1,2,96,768]{4,3,2,1,0:T(8,128)(2,1)S(1)} %get-tuple-element.274), channel_id=1, source_target_pairs={{0,4},{4,0},{8,12},{12,8},{16,20},{20,16},{24,28},{28,24},{1,5},{5... | collective-permute-start | bytes 884744 | tf_op jit(solution)/shard_map/ppermute | solution.py:687
  189.1 19.7 %collective-permute-start.37 = (bf16[1,1,2,96,768]{4,3,2,1,0:T(8,128)(2,1)S(1)}, bf16[1,1,2,96,768]{4,3,2,1,0:T(8,128)(2,1)S(1)}, u32[]{:S(2)}, u32[]{:S(2)}) collective-permute-start(bf16[1,1,2,96,768]{4,3,2,1,0:T(8,128)(2,1)S(1)} %get-tuple-element.273), channel_id=1, source_target_pairs={{0,8},{4,12},{8,0},{12,4},{16,24},{20,28},{24,16},{28,20},{1,9},{5... | collective-permute-start | bytes 884744 | tf_op jit(solution)/shard_map/ppermute | solution.py:687
  189.2 15.6 %collective-permute-start.34 = (bf16[104,768]{1,0:T(8,128)(2,1)S(1)}, bf16[104,768]{1,0:T(8,128)(2,1)S(1)}, u32[]{:S(2)}, u32[]{:S(2)}) collective-permute-start(bf16[104,768]{1,0:T(8,128)(2,1)S(1)} %get-tuple-element.302), channel_id=1, source_target_pairs={{0,8},{4,12},{8,0},{12,4},{16,24},{20,28},{24,16},{28,20},{1,9},{5... | collective-permute-start | bytes 479240 | tf_op jit(solution)/shard_map/ppermute | solution.py:687
  191.2 15.0 %collective-permute-start.35 = (bf16[104,768]{1,0:T(8,128)(2,1)S(1)}, bf16[104,768]{1,0:T(8,128)(2,1)S(1)}, u32[]{:S(2)}, u32[]{:S(2)}) collective-permute-start(bf16[104,768]{1,0:T(8,128)(2,1)S(1)} %get-tuple-element.304), channel_id=1, source_target_pairs={{0,16},{4,20},{8,24},{12,28},{16,0},{20,4},{24,8},{28,12},{1,17},{... | collective-permute-start | bytes 479240 | tf_op jit(solution)/shard_map/ppermute | solution.py:687
  192.4 16.1 %collective-permute-start.36 = (bf16[104,768]{1,0:T(8,128)(2,1)S(1)}, bf16[104,768]{1,0:T(8,128)(2,1)S(1)}, u32[]{:S(2)}, u32[]{:S(2)}) collective-permute-start(bf16[104,768]{1,0:T(8,128)(2,1)S(1)} %get-tuple-element.303), channel_id=1, source_target_pairs={{0,24},{4,28},{8,16},{12,20},{16,8},{20,12},{24,0},{28,4},{1,25},{... | collective-permute-start | bytes 479240 | tf_op jit(solution)/shard_map/ppermute | solution.py:687
  204.7 34.7 %collective-permute-start.30 = (bf16[1024,768]{1,0:T(8,128)(2,1)}, bf16[1024,768]{1,0:T(8,128)(2,1)}, u32[]{:S(2)}, u32[]{:S(2)}) collective-permute-start(bf16[1024,768]{1,0:T(8,128)(2,1)} %pad_maximum_fusion), channel_id=1, source_target_pairs={{0,2},{1,3},{2,0},{3,1},{4,6},{5,7},{6,4},{7,5},{8,10},{9,11},{10,... | collective-permute-start | bytes 4718600 | tf_op jit(solution)/shard_map/ppermute | solution.py:684
  208.9 14.9 %collective-permute-start.42 = (bf16[1,2,2,96,768]{4,3,2,1,0:T(8,128)(2,1)S(1)}, bf16[1,2,2,96,768]{4,3,2,1,0:T(8,128)(2,1)S(1)}, u32[]{:S(2)}, u32[]{:S(2)}) collective-permute-start(bf16[1,2,2,96,768]{4,3,2,1,0:T(8,128)(2,1)S(1)} %pad_maximum_fusion.4), channel_id=1, source_target_pairs={{0,4},{4,0},{8,12},{12,8},{16,20},{20,16},{24,28},{28,24},{1,5},{5... | collective-permute-start | bytes 1769480 | tf_op jit(solution)/shard_map/ppermute | solution.py:687
  209.9 8.8 %collective-permute-start.39 = (bf16[1,1,104,768]{3,2,1,0:T(8,128)(2,1)S(1)}, bf16[1,1,104,768]{3,2,1,0:T(8,128)(2,1)}, u32[]{:S(2)}, u32[]{:S(2)}) collective-permute-start(bf16[1,1,104,768]{3,2,1,0:T(8,128)(2,1)S(1)} %fusion.1), channel_id=1, source_target_pairs={{0,8},{4,12},{8,0},{12,4},{16,24},{20,28},{24,16},{28,20},{1,9},{5... | collective-permute-start | bytes 479240 | tf_op jit(solution)/shard_map/ppermute | solution.py:687
  209.9 13.9 %collective-permute-start.40 = (bf16[1,1,104,768]{3,2,1,0:T(8,128)(2,1)S(1)}, bf16[1,1,104,768]{3,2,1,0:T(8,128)(2,1)S(1)}, u32[]{:S(2)}, u32[]{:S(2)}) collective-permute-start(bf16[1,1,104,768]{3,2,1,0:T(8,128)(2,1)S(1)} %fusion.1), channel_id=1, source_target_pairs={{0,16},{4,20},{8,24},{12,28},{16,0},{20,4},{24,8},{28,12},{1,17},{... | collective-permute-start | bytes 479240 | tf_op jit(solution)/shard_map/ppermute | solution.py:687
  213.7 10.1 %collective-permute-start.41 = (bf16[1,1,104,768]{3,2,1,0:T(8,128)(2,1)S(1)}, bf16[1,1,104,768]{3,2,1,0:T(8,128)(2,1)S(1)}, u32[]{:S(2)}, u32[]{:S(2)}) collective-permute-start(bf16[1,1,104,768]{3,2,1,0:T(8,128)(2,1)S(1)} %fusion.1), channel_id=1, source_target_pairs={{0,24},{4,28},{8,16},{12,20},{16,8},{20,12},{24,0},{28,4},{1,25},{... | collective-permute-start | bytes 479240 | tf_op jit(solution)/shard_map/ppermute | solution.py:687
  241.8 5.3 %collective-permute-start.43 = (bf16[1024,768]{1,0:T(8,128)(2,1)S(1)}, bf16[1024,768]{1,0:T(8,128)(2,1)S(1)}, u32[]{:S(2)}, u32[]{:S(2)}) collective-permute-start(bf16[1024,768]{1,0:T(8,128)(2,1)S(1)} %fusion.refs_0_), channel_id=1, source_target_pairs={{0,1},{1,0},{2,3},{3,2},{4,5},{5,4},{6,7},{7,6},{8,9},{9,8},{10,11... | collective-permute-start | bytes 4718600 | tf_op jit(solution)/shard_map/ppermute | solution.py:684
  241.8 16.8 %collective-permute-start.44 = (bf16[1,4,104,768]{3,2,1,0:T(8,128)(2,1)S(1)}, bf16[1,4,104,768]{3,2,1,0:T(8,128)(2,1)S(1)}, u32[]{:S(2)}, u32[]{:S(2)}) collective-permute-start(bf16[1,4,104,768]{3,2,1,0:T(8,128)(2,1)S(1)} %constant_dynamic-update-slice_fusion), channel_id=1, source_target_pairs={{0,4},{4,0},{8,12},{12,8},{16,20},{20,16},{24,28},{28,24},{1,5},{5... | collective-permute-start | bytes 1916936 | tf_op jit(solution)/shard_map/ppermute | solution.py:687
  245.5 15.4 %collective-permute-start.45 = (bf16[1,2,2,96,768]{4,3,2,1,0:T(8,128)(2,1)S(1)}, bf16[1,2,2,96,768]{4,3,2,1,0:T(8,128)(2,1)S(1)}, u32[]{:S(2)}, u32[]{:S(2)}) collective-permute-start(bf16[1,2,2,96,768]{4,3,2,1,0:T(8,128)(2,1)S(1)} %pad_maximum_fusion.5), channel_id=1, source_target_pairs={{0,8},{4,12},{8,0},{12,4},{16,24},{20,28},{24,16},{28,20},{1,9},{5... | collective-permute-start | bytes 1769480 | tf_op jit(solution)/shard_map/ppermute | solution.py:687
  (47 other events, 314.7 us)

commit v12 on v10

--- a/solution.py
+++ b/solution.py
@@ -40,7 +40,7 @@
     return pl.CostEstimate(flops=int(micros * 1.1e9), bytes_accessed=1024, transcendentals=0)
 
 
-MICROS = {"project": 3, "attend_forward": 8, "attend_backward": 12, "entry_back": 5, "place": 3, "ahead": 9, "astern": 10, "inner_norm": 3, "weight_grads": 4, "fold": 2}
+MICROS = {"project": 3, "attend_forward": 8, "attend_backward": 12, "entry_back": 5, "place": 3, "ahead": 9, "astern": 10, "inner_norm": 3, "weight_grads": 4, "fold": 2, "joint_grads": 4, "entry_rows": 3}
 
 
 def lane_parts(block):
@@ -299,10 +299,7 @@
     )
 
 
-def entry_kernel(meta_ref, x_ref, dq_ref, dk_ref, dv_ref, wq_ref, wk_ref, wv_ref, *refs):
-    last = len(refs) == 7
-    before_ref = refs[0] if last else None
-    send_ref, keep_ref, sum_ref, acc = refs[-4:]
+def entry_kernel(meta_ref, x_ref, dq_ref, dk_ref, dv_ref, wq_ref, wk_ref, wv_ref, send_ref, keep_ref, sum_ref, acc):
     step = pl.program_id(0)
     x = x_ref[...]
     total = jnp.zeros(x.shape, F32)
@@ -314,45 +311,106 @@
 
         @pl.when(step == 0)
         def _():
-            acc[rows, :] = product if before_ref is None else product + before_ref[rows, :]
+            acc[rows, :] = product
 
         @pl.when(step == 1)
         def _():
-            sum_ref[rows, :] = (product + acc[rows, :]).astype(sum_ref.dtype)
+            sum_ref[rows, :] = product + acc[rows, :]
 
     low = total.astype(BF)
 
     @pl.when(step == 0)
     def _():
         send_ref[...] = low
-        if last:
-            merged = refs[1][...].astype(F32) + refs[2][...].astype(F32)
-            sum_ref[576:, :] = merged.astype(sum_ref.dtype)
 
     @pl.when(step == 1)
     def _():
         keep_ref[...] = low
 
 
-def entry_back(meta, tokens, grads, weights, before, u, frames):
+def entry_back(meta, tokens, grads, weights, u, frames):
     half = frames // 2
     d = tokens.shape[1]
-    rows, dtype = (832, BF) if before else (576, F32)
     return call(
         entry_kernel,
         "entry_back",
         (2,),
         meta,
-        (tokens, *grads, *weights, *before),
+        (tokens, *grads, *weights),
         [pl.BlockSpec((half, d), lambda i, m: (u * 2 + (1 - i ^ m[0]), 0))]
         + [pl.BlockSpec((half, 256), lambda i, m: (1 - i ^ m[0], 0))] * 3
-        + [fixed(192, d)] * 3
-        + [fixed(*value.shape) for value in before],
-        [fixed(half, d), fixed(half, d), fixed(rows, d)],
-        [like((half, d), BF), like((half, d), BF), like((rows, d), dtype)],
+        + [fixed(192, d)] * 3,
+        [fixed(half, d), fixed(half, d), fixed(576, d)],
+        [like((half, d), BF), like((half, d), BF), like((576, d), F32)],
         [pltpu.VMEM((576, d), F32)],
         hold=(1, 2, 3),
         far=(0, 4, 5, 6),
+    )
+
+
+def joint_kernel(meta_ref, x_ref, dq_ref, dk_ref, dv_ref, before_ref, m0_ref, m1_ref, sum_ref, acc):
+    step = pl.program_id(0)
+    x = x_ref[...]
+    for i, g_ref in enumerate((dq_ref, dk_ref, dv_ref)):
+        rows = pl.ds(192 * i, 192)
+        product = tn(g_ref[:, :192], x)
+
+        @pl.when(step == 0)
+        def _():
+            acc[rows, :] = product
+
+        @pl.when(step == 1)
+        def _():
+            sum_ref[rows, :] = (product + acc[rows, :] + before_ref[rows, :]).astype(BF)
+
+    @pl.when(step == 0)
+    def _():
+        sum_ref[576:, :] = (m0_ref[...].astype(F32) + m1_ref[...].astype(F32)).astype(BF)
+
+
+def joint_grads(meta, tokens, grads, before, u, frames):
+    half = frames // 2
+    d = tokens.shape[1]
+    return call(
+        joint_kernel,
+        "joint_grads",
+        (2,),
+        meta,
+        (tokens, *grads, *before),
+        [pl.BlockSpec((half, d), lambda i, m: (u * 2 + i, 0))]
+        + [pl.BlockSpec((half, 256), lambda i, m: (i, 0))] * 3
+        + [fixed(*value.shape) for value in before],
+        [fixed(832, d)],
+        [like((832, d), BF)],
+        [pltpu.VMEM((576, d), F32)],
+        hold=(1, 2, 3),
+        far=(0,),
+    )
+
+
+def rows_kernel(meta_ref, dq_ref, dk_ref, dv_ref, wq_ref, wk_ref, wv_ref, send_ref, keep_ref):
+    total = sum(nn(g[:, :192], w[...]) for g, w in ((dq_ref, wq_ref), (dk_ref, wk_ref), (dv_ref, wv_ref)))
+    for j, o_ref in enumerate((send_ref, keep_ref)):
+
+        @pl.when(pl.program_id(0) == j)
+        def _():
+            o_ref[...] = total.astype(BF)
+
+
+def entry_rows(meta, grads, weights, frames):
+    half = frames // 2
+    d = weights[0].shape[1]
+    return call(
+        rows_kernel,
+        "entry_rows",
+        (2,),
+        meta,
+        (*grads, *weights),
+        [pl.BlockSpec((half, 256), lambda i, m: (1 - i ^ m[0], 0))] * 3 + [fixed(192, d)] * 3,
+        [fixed(half, d), fixed(half, d)],
+        [like((half, d), BF), like((half, d), BF)],
+        hold=(0, 1, 2),
+        far=(3, 4, 5),
     )
 
 
@@ -791,8 +849,8 @@
     def attend_step(u, grads):
         return done(attend_backward(meta(), *qkv_of[u], grads, fwd[u][:2], fwd[u][2], u, frames))
 
-    def entry_step(u, grads, before):
-        return done(entry_back(meta(), tokens, grads, qkv_w, before, u, frames))
+    def entry_step(u, grads):
+        return done(entry_back(meta(), tokens, grads, qkv_w, u, frames))
 
 
     first_bit = 1 + seqs
@@ -804,7 +862,7 @@
         out = done(fold(meta(), pairs, tuple(first_bit + order[step] for order in bit_orders), hold))
         return [(out[2 * i + 1], swap_dp(out[2 * i], 1 << bit_orders[i][step])) for i in range(2)]
 
-    inner, entry, so_far, near, crossed = [], [], (), [], []
+    inner, so_far, near, crossed = [], (), [], []
     out_other = [swap(r, 1) for r in out_rows]
 
     def exchange(out):
@@ -838,35 +896,36 @@
             )
             start([first, second])
             token.extend(out_other)
-        out = entry_step(u, dqkv, so_far)
-        entry.append(out)
-        if not last:
+        if last:
+            qkv = Chain(done(joint_grads(meta(), tokens, dqkv, so_far, u, frames))[0], stages)
+            qkv.start()
+            out = done(entry_rows(meta(), dqkv, qkv_w, frames))
+        else:
+            out = entry_step(u, dqkv)
             merge_got = swap(lax.optimization_barrier((res[4], out[0]))[0], 1)
             so_far = (out[2], res[3], merge_got)
             moving = scatter(2, moving, out[0])
             exchange(out)
-    qkv = Chain(out[2], stages)
-    qkv.start()
 
     got = exchange(out)
     layer_output = place(meta(), out_rows, out_other)
 
     finish([first, second], got)
-    finish([qkv], crossed[0])
+    finish([qkv])
     together([qkv, first, second])
     start([qkv, first, second])
-    finish([qkv, first, second], crossed[-1])
+    finish([qkv, first, second], crossed[0])
     together([qkv, first, second])
     start([qkv, first])
+    finish([qkv, first], crossed[1])
+    together([qkv, first, second])
+    start([qkv, second])
     ready = []
     for u in range(seqs):
         rest = near[u][0].astype(F32) + near[u][1].astype(F32) + crossed[u].astype(F32)
         ready.append((inner[u][0] + rest).astype(BF))
     input_grad = place(scalars, ready, [swap(r, 1) for r in ready])
-    finish([qkv, first], layer_output)
-    together([qkv, first, second])
-    start([qkv, second])
-    finish([qkv, second], input_grad)
+    finish([qkv, second], input_grad, layer_output)
     while qkv.steps or first.steps or second.steps:
         start([qkv, first, second])
         finish([qkv, first, second])

time: 247 us -> 255 us (1.032)
  waiting for transfers between devices: 71.5 us -> 52.8 us
  Pallas kernels: 111 us -> 126 us
  local copies, waits for them, and re-layouts: 2.65 us -> 11.9 us
  other arithmetic: 11.7 us -> 14.7 us
    ppermute x28, waiting for transfers between devices: 31.3 us -> 11.4 us  [swap(): return lax.ppermute(value, 'tensor', [(i, i ^ k) for i in range(4)])]
    pallas_call x21 -> x22, Pallas kernels: 111 us -> 126 us  [call(): pl.pallas_call(kernel, grid_spec=pltpu.PrefetchScalarGridSpec(num_scalar_...]
    unnamed x68 -> x98, local copies, waits for them, and re-layouts: 1.08 us -> 9.54 us
    ppermute x20, starting transfers between devices: 29 us -> 25.7 us  [swap_dp(): return lax.ppermute(value, 'dp', [(i, i ^ k) for i in range(groups)])]
    convert_element_type x3, other arithmetic: 2.78 us -> 5.57 us  [total(): sum((piece.astype(F32) for piece in pieces)).astype(BF)]
  transfers between devices with their start and end apart: 48 -> 48, of which waited for: 20 -> 15; matrix products, arithmetic and copies ran while one was open for 5% -> 6% of each run, Pallas kernels for 46% -> 50%
where the time goes in v12:
time: 255 us; the launch traced here: 251 us
  Pallas kernels  126 us (49%)
  waiting for transfers between devices  52.8 us (21%)
  starting transfers between devices  43.7 us (17%)
  other arithmetic  14.7 us (6%)
  local copies, waits for them, and re-layouts  11.9 us (5%)
    pallas_call x22, Pallas kernels, call(): pl.pallas_call(kernel, grid_spec=pltpu.PrefetchScalarGridSpec(num_scalar_...  126 us
    ppermute x20, waiting for transfers between devices, swap_dp(): return lax.ppermute(value, 'dp', [(i, i ^ k) for i in range(groups)])  41.3 us
    ppermute x20, starting transfers between devices, swap_dp(): return lax.ppermute(value, 'dp', [(i, i ^ k) for i in range(groups)])  25.7 us
    ppermute x28, starting transfers between devices, swap(): return lax.ppermute(value, 'tensor', [(i, i ^ k) for i in range(4)])  18.1 us
    ppermute x28, waiting for transfers between devices, swap(): return lax.ppermute(value, 'tensor', [(i, i ^ k) for i in range(4)])  11.4 us
    unnamed x98, local copies, waits for them, and re-layouts  9.54 us
    convert_element_type x3, other arithmetic, total(): sum((piece.astype(F32) for piece in pieces)).astype(BF)  5.57 us
  transfers between devices with their start and end apart: 48, of which 15 were waited for; matrix products, arithmetic and copies ran while one was open for 6% of the time, Pallas kernels for 50%

profile of v12, /device:TPU:0, one launch (start us, length us, event | category | flops | bytes accessed | tf_op | source)
XLA Modules:
  0.0 250.7 jit_solution(12161609265222126086)
XLA Ops:
  1.2 2.6 %collective-permute-start.1 = (bf16[192,768]{1,0:T(8,128)(2,1)}, bf16[192,768]{1,0:T(8,128)(2,1)S(1)}, u32[]{:S(2)}, u32[]{:S(2)}) collective-permute-start(bf16[192,768]{1,0:T(8,128)(2,1)} %w0.7), channel_id=1, source_target_pairs={{0,2},{1,3},{2,0},{3,1},{4,6},{5,7},{6,4},{7,5},{8,10},{9,11},{10,... | collective-permute-start | bytes 884744 | tf_op jit(solution)/shard_map/ppermute | solution.py:731
  5.0 4.4 %project.2 = (bf16[1024,256]{1,0:T(8,128)(2,1)S(1)}, bf16[1024,256]{1,0:T(8,128)(2,1)S(1)}, bf16[1024,256]{1,0:T(8,128)(2,1)S(1)}) custom-call(s32[6]{0:T(128)S(1)} %concatenate.24.meta_ref, bf16[2048,768]{1,0:T(8,128)(2,1)} %x_ref.7, bf16[192,768]{1,0:T(8,128)(2,1)} %bitcast.31, bf16[192,768]{1,0:T(8,128)(2,1)} %bitcast.35, bf16[192,768]{1,0:T(8,128)(2,1)} %bitcast.39), custom_call_target="tpu_custom_call" | custom-call | flops 3300000000 | bytes 1024 | tf_op jit(solution)/shard_map/project/pallas_call | solution.py:70
  9.5 7.7 %attend_forward.2 = (bf16[192,512]{1,0:T(8,128)(2,1)S(1)}, bf16[192,512]{1,0:T(8,128)(2,1)S(1)}, f32[2,8,512]{2,1,0:T(8,128)S(1)}) custom-call(s32[6]{0:T(128)S(1)} %concatenate.24.meta_ref, bf16[1024,256]{1,0:T(8,128)(2,1)S(1)} %get-tuple-element.156.q_ref, bf16[1024,256]{1,0:T(8,128)(2,1)S(1)} %get-tuple-element.158.k_ref, ...), custom_call_target="tpu_custom_call" | custom-call | flops 8800000000 | bytes 1024 | tf_op jit(solution)/shard_map/attend_forward/pallas_call | solution.py:70
  17.6 1.7 collective-permute-start.7
  19.6 4.4 %project.3 = (bf16[1024,256]{1,0:T(8,128)(2,1)S(1)}, bf16[1024,256]{1,0:T(8,128)(2,1)S(1)}, bf16[1024,256]{1,0:T(8,128)(2,1)S(1)}) custom-call(s32[6]{0:T(128)S(1)} %concatenate.24.meta_ref, bf16[2048,768]{1,0:T(8,128)(2,1)} %x_ref.7, bf16[192,768]{1,0:T(8,128)(2,1)} %bitcast.32, bf16[192,768]{1,0:T(8,128)(2,1)} %bitcast.36, bf16[192,768]{1,0:T(8,128)(2,1)} %bitcast.40), custom_call_target="tpu_custom_call" | custom-call | flops 3300000000 | bytes 1024 | tf_op jit(solution)/shard_map/project/pallas_call | solution.py:70
  26.1 6.5 %attend_forward.3 = (bf16[192,512]{1,0:T(8,128)(2,1)S(1)}, bf16[192,512]{1,0:T(8,128)(2,1)S(1)}, f32[2,8,512]{2,1,0:T(8,128)S(1)}) custom-call(s32[6]{0:T(128)S(1)} %concatenate.24.meta_ref, bf16[1024,256]{1,0:T(8,128)(2,1)S(1)} %get-tuple-element.162.q_ref, bf16[1024,256]{1,0:T(8,128)(2,1)S(1)} %get-tuple-element.164.k_ref, ...), custom_call_target="tpu_custom_call" | custom-call | flops 8800000000 | bytes 1024 | tf_op jit(solution)/shard_map/attend_forward/pallas_call | solution.py:70
  37.2 10.0 %ahead.2 = (f32[512,768]{1,0:T(8,128)}, f32[512,128]{1,0:T(8,128)}, bf16[512,768]{1,0:T(8,128)(2,1)S(1)}, bf16[512,1536]{1,0:T(8,128)(2,1)S(1)}, bf16[512,1536]{...) custom-call(s32[6]{0:T(128)S(1)} %concatenate.24.meta_ref, bf16[2048,768]{1,0:T(8,128)(2,1)} %x_ref.7, ...), custom_call_target="tpu_custom_call" | custom-call | flops 9900000256 | bytes 1024 | tf_op jit(solution)/shard_map/ahead/pallas_call | solution.py:70
  47.2 1.8 collective-permute-start.11
  49.0 10.2 %ahead.3 = (f32[512,768]{1,0:T(8,128)}, f32[512,128]{1,0:T(8,128)}, bf16[512,768]{1,0:T(8,128)(2,1)S(1)}, bf16[512,1536]{1,0:T(8,128)(2,1)S(1)}, bf16[512,1536]{...) custom-call(s32[6]{0:T(128)S(1)} %concatenate.24.meta_ref, bf16[2048,768]{1,0:T(8,128)(2,1)} %x_ref.7, ...), custom_call_target="tpu_custom_call" | custom-call | flops 9900000256 | bytes 1024 | tf_op jit(solution)/shard_map/ahead/pallas_call | solution.py:70
  59.5 8.2 %collective-permute-done.11.far_ref = bf16[512,768]{1,0:T(8,128)(2,1)S(1)} collective-permute-done((bf16[512,768]{1,0:T(8,128)(2,1)S(1)}, bf16[512,768]{1,0:T(8,128)(2,1)S(1)}, u32[]{:S(2)}, u32[]{:S(2)}) %collective-permute-start.11) | collective-permute-done | bytes 786464 | tf_op jit(solution)/shard_map/ppermute | solution.py:731
  67.7 9.2 %astern.2 = (bf16[512,768]{1,0:T(8,128)(2,1)}, bf16[512,768]{1,0:T(8,128)(2,1)S(1)}, bf16[512,1536]{1,0:T(8,128)(2,1)S(1)}, f32[512,768]{1,0:T(8,128)}, bf16[512...) custom-call(s32[6]{0:T(128)S(1)} %concatenate.24.meta_ref, f32[512,768]{1,0:T(8,128)S(1)} %get-tuple-element.174.own_ref, ...), custom_call_target="tpu_custom_call" | custom-call | flops 11000000512 | bytes 1024 | tf_op jit(solution)/shard_map/astern/pallas_call | solution.py:70
  76.8 3.2 %weight_grads.1 = (bf16[768,768]{1,0:T(8,128)(2,1)S(1)}, bf16[768,768]{1,0:T(8,128)(2,1)S(1)}, bf16[768,768]{1,0:T(8,128)(2,1)S(1)}, bf16[768,768]{1,0:T(8,128)(2,1)S(1)}) custom-call(s32[6]{0:T(128)S(1)} %concatenate.24.meta_ref, bf16[512,768]{1,0:T(8,128)(2,1)S(1)} %get-tuple-element.179.x_ref, bf16[512,768]{1,0:T(8,128)(2,1)S(1)} %get-tuple-element.180.g_ref, ...), custom_call_target="tpu_custom_call" | custom-call | flops 4400000000 | bytes 1024 | tf_op jit(solution)/shard_map/weight_grads/pallas_call | solution.py:70
  80.1 1.8 collective-permute-start.13
  81.9 2.7 %collective-permute-done.12.far_ref = bf16[512,768]{1,0:T(8,128)(2,1)S(1)} collective-permute-done((bf16[512,768]{1,0:T(8,128)(2,1)S(1)}, bf16[512,768]{1,0:T(8,128)(2,1)S(1)}, u32[]{:S(2)}, u32[]{:S(2)}) %collective-permute-start.12) | collective-permute-done | bytes 786464 | tf_op jit(solution)/shard_map/ppermute | solution.py:731
  84.5 12.2 %astern.3 = (bf16[512,768]{1,0:T(8,128)(2,1)}, f32[512,768]{1,0:T(8,128)}, bf16[512,768]{1,0:T(8,128)(2,1)S(1)}, f32[2,768]{1,0:T(2,128)S(1)}, bf16[768,768]{1,0...) custom-call(s32[6]{0:T(128)S(1)} %concatenate.24.meta_ref, ...), custom_call_target="tpu_custom_call" | custom-call | flops 11000000512 | bytes 1024 | tf_op jit(solution)/shard_map/astern/pallas_call | solution.py:70
  103.3 5.6 %inner_norm.2 = (f32[512,768]{1,0:T(8,128)}, bf16[192,512]{1,0:T(8,128)(2,1)S(1)}, bf16[192,512]{1,0:T(8,128)(2,1)S(1)}, f32[192,768]{1,0:T(8,128)}, f32[192,768]{1,0:T(8,128)}, /*index=5*/f32[2,768]{1,0:T(2,128)S(1)}) custom-call(s32[6]{0:T(128)S(1)} %concatenate.24.meta_ref, f32[512,768]{1,0:T(8,128)} %get-tuple-element.195.own_ref, ...), custom_call_target="tpu_custom_call" | custom-call | flops 3300000000 | bytes 1024 | tf_op jit(solution)/shard_map/inner_norm/pallas_call | solution.py:70
  108.9 1.7 collective-permute-start.19
  111.8 1.7 collective-permute-start.17
  113.4 1.6 collective-permute-start.18
  115.0 12.3 %attend_backward.2 = (bf16[1024,256]{1,0:T(8,128)(2,1)S(1)}, bf16[1024,256]{1,0:T(8,128)(2,1)S(1)}, bf16[1024,256]{1,0:T(8,128)(2,1)S(1)}) custom-call(s32[6]{0:T(128)S(1)} %concatenate.24.meta_ref, bf16[1024,256]{1,0:T(8,128)(2,1)} %copy-done.39, bf16[1024,256]{1,0:T(8,128)(2,1)} %copy-done.40, bf16[1024,256]{1,0:T(8,128)(2,1)} %copy-done.41, ...), custom_call_target="tpu_custom_call" | custom-call | flops 13200000000 | bytes 1024 | tf_op jit(solution)/shard_map/attend_backward/pallas_call | solution.py:70
  129.7 1.6 collective-permute-start.20
  131.3 5.5 %inner_norm.3 = (f32[512,768]{1,0:T(8,128)}, bf16[192,512]{1,0:T(8,128)(2,1)S(1)}, bf16[192,512]{1,0:T(8,128)(2,1)S(1)}, bf16[256,768]{1,0:T(8,128)(2,1)S(1)}, b...) custom-call(s32[6]{0:T(128)S(1)} %concatenate.24.meta_ref, f32[512,768]{1,0:T(8,128)} %get-tuple-element.228.own_ref, ...), custom_call_target="tpu_custom_call" | custom-call | flops 3300000000 | bytes 1024 | tf_op jit(solution)/shard_map/inner_norm/pallas_call | solution.py:70
  137.2 7.0 %entry_back.1 = (bf16[512,768]{1,0:T(8,128)(2,1)}, bf16[512,768]{1,0:T(8,128)(2,1)S(1)}, f32[576,768]{1,0:T(8,128)S(1)}) custom-call(s32[6]{0:T(128)S(1)} %concatenate.24.meta_ref, bf16[2048,768]{1,0:T(8,128)(2,1)} %x_ref.7, bf16[1024,256]{1,0:T(8,128)(2,1)S(1)} %get-tuple-element.217.dq_ref, bf16[1024,256]{1,0:T(8,128)(2,1)S(1)} %get-tuple-element.239.dk_ref, ...), custom_call_target="tpu_custom_call" | custom-call | flops 5500000256 | bytes 1024 | tf_op jit(solution)/shard_map/entry_back/pallas_call | solution.py:70
  145.6 2.7 %collective-permute-start.23 = (bf16[96,768]{1,0:T(8,128)(2,1)S(1)}, bf16[96,768]{1,0:T(8,128)(2,1)S(1)}, u32[]{:S(2)}, u32[]{:S(2)}) collective-permute-start(bf16[96,768]{1,0:T(8,128)(2,1)S(1)} %get-tuple-element.250), channel_id=1, source_target_pairs={{0,16},{4,20},{8,24},{12,28},{16,0},{20,4},{24,8},{28,12},{1,17},{... | collective-permute-start | bytes 442376 | tf_op jit(solution)/shard_map/ppermute | solution.py:734
  149.0 10.0 %attend_backward.3 = (bf16[1024,256]{1,0:T(8,128)(2,1)S(1)}, bf16[1024,256]{1,0:T(8,128)(2,1)S(1)}, bf16[1024,256]{1,0:T(8,128)(2,1)S(1)}) custom-call(s32[6]{0:T(128)S(1)} %concatenate.24.meta_ref, bf16[1024,256]{1,0:T(8,128)(2,1)} %copy-done.36, bf16[1024,256]{1,0:T(8,128)(2,1)} %copy-done.37, bf16[1024,256]{1,0:T(8,128)(2,1)} %copy-done.38, ...), custom_call_target="tpu_custom_call" | custom-call | flops 13200000000 | bytes 1024 | tf_op jit(solution)/shard_map/attend_backward/pallas_call | solution.py:70
  159.0 3.2 %collective-permute-done.24.refs_3_ = bf16[96,768]{1,0:T(8,128)(2,1)S(1)} collective-permute-done((bf16[96,768]{1,0:T(8,128)(2,1)S(1)}, bf16[96,768]{1,0:T(8,128)(2,1)S(1)}, u32[]{:S(2)}, u32[]{:S(2)}) %collective-permute-start.24) | collective-permute-done | bytes 147488 | tf_op jit(solution)/shard_map/ppermute | solution.py:734
  162.9 4.5 %joint_grads.1 = bf16[832,768]{1,0:T(8,128)(2,1)S(1)} custom-call(s32[6]{0:T(128)S(1)} %concatenate.24.meta_ref, bf16[2048,768]{1,0:T(8,128)(2,1)} %x_ref.7, bf16[1024,256]{1,0:T(8,128)(2,1)S(1)} %get-tuple-element.255.dq_ref, bf16[1024,256]{1,0:T(8,128)(2,1)S(1)} %get-tuple-element.266.dk_ref, bf16[1024,256]{1,0:T(8,128)(2,1)S(1)} %get-tuple-element.267.dv_ref, ...), custom_call_target="tpu_custom_call" | custom-call | flops 4400000000 | bytes 1024 | tf_op jit(solution)/shard_map/joint_grads/pallas_call | solution.py:70
  169.4 4.3 %entry_rows.1 = (bf16[512,768]{1,0:T(8,128)(2,1)}, bf16[512,768]{1,0:T(8,128)(2,1)S(1)}) custom-call(s32[6]{0:T(128)S(1)} %concatenate.24.meta_ref, bf16[1024,256]{1,0:T(8,128)(2,1)S(1)} %get-tuple-element.255.dq_ref, bf16[1024,256]{1,0:T(8,128)(2,1)S(1)} %get-tuple-element.266.dk_ref, bf16[1024,256]{1,0:T(8,128)(2,1)S(1)} %get-tuple-element.267.dv_ref, ...), custom_call_target="tpu_custom_call" | custom-call | flops 3300000000 | bytes 1024 | tf_op jit(solution)/shard_map/entry_rows/pallas_call | solution.py:70
  174.7 2.1 collective-permute-start.35
  176.8 2.2 fusion
  180.5 4.8 %collective-permute-done.34 = bf16[416,768]{1,0:T(8,128)(2,1)} collective-permute-done((bf16[416,768]{1,0:T(8,128)(2,1)}, bf16[416,768]{1,0:T(8,128)(2,1)}, u32[]{:S(2)}, u32[]{:S(2)}) %collective-permute-start.34) | collective-permute-done | bytes 639008 | tf_op jit(solution)/shard_map/ppermute | solution.py:734
  185.4 2.1 add_convert_fusion.2
  187.4 2.8 %collective-permute-done.35 = bf16[1,1,1,96,768]{4,3,2,1,0:T(8,128)(2,1)S(1)} collective-permute-done((bf16[1,1,1,96,768]{4,3,2,1,0:T(8,128)(2,1)S(1)}, bf16[1,1,1,96,768]{4,3,2,1,0:T(8,128)(2,1)S(1)}, u32[]{:S(2)}, u32[]{:S(2)}) %collective-permute-start.35) | collective-permute-done | bytes 147488 | tf_op jit(solution)/shard_map/ppermute | solution.py:734
  191.4 2.1 collective-permute-start.37
  193.5 5.9 %collective-permute-done.41 = bf16[1,1,2,96,768]{4,3,2,1,0:T(8,128)(2,1)S(1)} collective-permute-done((bf16[1,1,2,96,768]{4,3,2,1,0:T(8,128)(2,1)S(1)}, bf16[1,1,2,96,768]{4,3,2,1,0:T(8,128)(2,1)S(1)}, u32[]{:S(2)}, u32[]{:S(2)}) %collective-permute-start.41) | collective-permute-done | bytes 294944 | tf_op jit(solution)/shard_map/ppermute | solution.py:734
  199.4 1.8 collective-permute-start.39
  202.5 1.6 collective-permute-start.32
  204.7 5.6 %collective-permute-done.37 = bf16[104,768]{1,0:T(8,128)(2,1)S(1)} collective-permute-done((bf16[104,768]{1,0:T(8,128)(2,1)S(1)}, bf16[104,768]{1,0:T(8,128)(2,1)S(1)}, u32[]{:S(2)}, u32[]{:S(2)}) %collective-permute-start.37) | collective-permute-done | bytes 159776 | tf_op jit(solution)/shard_map/ppermute | solution.py:734
  210.7 2.6 %collective-permute-start.43 = (bf16[1,1,104,768]{3,2,1,0:T(8,128)(2,1)S(1)}, bf16[1,1,104,768]{3,2,1,0:T(8,128)(2,1)S(1)}, u32[]{:S(2)}, u32[]{:S(2)}) collective-permute-start(bf16[1,1,104,768]{3,2,1,0:T(8,128)(2,1)S(1)} %fusion.2), channel_id=1, source_target_pairs={{0,16},{4,20},{8,24},{12,28},{16,0},{20,4},{24,8},{28,12},{1,17},{... | collective-permute-start | bytes 479240 | tf_op jit(solution)/shard_map/ppermute | solution.py:734
  213.4 1.8 collective-permute-start.44
  216.3 1.9 add_convert_fusion.1.refs_0_
  218.4 6.8 %collective-permute-done.43 = bf16[1,1,104,768]{3,2,1,0:T(8,128)(2,1)S(1)} collective-permute-done((bf16[1,1,104,768]{3,2,1,0:T(8,128)(2,1)S(1)}, bf16[1,1,104,768]{3,2,1,0:T(8,128)(2,1)S(1)}, u32[]{:S(2)}, u32[]{:S(2)}) %collective-permute-start.43) | collective-permute-done | bytes 159776 | tf_op jit(solution)/shard_map/ppermute | solution.py:734
  228.5 1.6 collective-permute-start.46
  230.2 2.7 %place.2 = bf16[2048,768]{1,0:T(8,128)(2,1)} custom-call(s32[6]{0:T(128)S(1)} %concatenate.24.meta_ref, bf16[512,768]{1,0:T(8,128)(2,1)S(1)} %copy-done.7, bf16[512,768]{1,0:T(8,128)(2,1)S(1)} %copy-done.10, bf16[512,768]{1,0:T(8,128)(2,1)S(1)} %copy-done.8, bf16[512,768]{1,0:T(8,128)(2,1)S(1)} %copy-done.12), custom_call_target="tpu_custom_call" | custom-call | flops 3300000000 | bytes 1024 | tf_op jit(solution)/shard_map/place/pallas_call | solution.py:70
  235.3 2.7 %place.3 = bf16[2048,768]{1,0:T(8,128)(2,1)} custom-call(s32[6]{0:T(128)S(1)} %concatenate.24.meta_ref, bf16[512,768]{1,0:T(8,128)(2,1)S(1)} %add_convert_fusion.1.refs_0_, bf16[512,768]{1,0:T(8,128)(2,1)S(1)} %collective-permute-done.30.refs_1_, bf16[512,768]{1,0:T(8,128)(2,1)S(1)} %add_convert_fusion.refs_2_, ...), custom_call_target="tpu_custom_call" | custom-call | flops 3300000000 | bytes 1024 | tf_op jit(solution)/shard_map/place/pallas_call | solution.py:70
  238.1 5.9 %collective-permute-done.46 = bf16[1,4,104,768]{3,2,1,0:T(8,128)(2,1)S(1)} collective-permute-done((bf16[1,4,104,768]{3,2,1,0:T(8,128)(2,1)S(1)}, bf16[1,4,104,768]{3,2,1,0:T(8,128)(2,1)S(1)}, u32[]{:S(2)}, u32[]{:S(2)}) %collective-permute-start.46) | collective-permute-done | bytes 639008 | tf_op jit(solution)/shard_map/ppermute | solution.py:734
  245.7 2.1 collective-permute-done.47
  247.9 1.7 bitcast_convert_fusion
  (205 shorter events, 39.9 us)
Async XLA Ops:
  0.6 16.7 %collective-permute-start = (bf16[192,768]{1,0:T(8,128)(2,1)}, bf16[192,768]{1,0:T(8,128)(2,1)S(1)}, u32[]{:S(2)}, u32[]{:S(2)}) collective-permute-start(bf16[192,768]{1,0:T(8,128)(2,1)} %w0.7), channel_id=1, source_target_pairs={{0,1},{1,0},{2,3},{3,2},{4,5},{5,4},{6,7},{7,6},{8,9},{9,8},{10,11... | collective-permute-start | bytes 884744 | tf_op jit(solution)/shard_map/ppermute | solution.py:731
  1.2 16.4 %collective-permute-start.1 = (bf16[192,768]{1,0:T(8,128)(2,1)}, bf16[192,768]{1,0:T(8,128)(2,1)S(1)}, u32[]{:S(2)}, u32[]{:S(2)}) collective-permute-start(bf16[192,768]{1,0:T(8,128)(2,1)} %w0.7), channel_id=1, source_target_pairs={{0,2},{1,3},{2,0},{3,1},{4,6},{5,7},{6,4},{7,5},{8,10},{9,11},{10,... | collective-permute-start | bytes 884744 | tf_op jit(solution)/shard_map/ppermute | solution.py:731
  3.7 15.6 %collective-permute-start.2 = (bf16[192,768]{1,0:T(8,128)(2,1)}, bf16[192,768]{1,0:T(8,128)(2,1)S(1)}, u32[]{:S(2)}, u32[]{:S(2)}) collective-permute-start(bf16[192,768]{1,0:T(8,128)(2,1)} %w0.7), channel_id=1, source_target_pairs={{0,3},{1,2},{2,1},{3,0},{4,7},{5,6},{6,5},{7,4},{8,11},{9,10},{10,... | collective-permute-start | bytes 884744 | tf_op jit(solution)/shard_map/ppermute | solution.py:731
  3.8 20.2 %collective-permute-start.3 = (bf16[768,768]{1,0:T(8,128)(2,1)}, bf16[768,768]{1,0:T(8,128)(2,1)S(1)}, u32[]{:S(2)}, u32[]{:S(2)}) collective-permute-start(bf16[768,768]{1,0:T(8,128)(2,1)} %ua_ref.7), channel_id=1, source_target_pairs={{0,1},{1,0},{2,3},{3,2},{4,5},{5,4},{6,7},{7,6},{8,9},{9,8},{10,11... | collective-permute-start | bytes 3538952 | tf_op jit(solution)/shard_map/ppermute | solution.py:731
  3.9 21.1 %collective-permute-start.4 = (bf16[768,768]{1,0:T(8,128)(2,1)}, bf16[768,768]{1,0:T(8,128)(2,1)S(1)}, u32[]{:S(2)}, u32[]{:S(2)}) collective-permute-start(bf16[768,768]{1,0:T(8,128)(2,1)} %da_ref.7), channel_id=1, source_target_pairs={{0,1},{1,0},{2,3},{3,2},{4,5},{5,4},{6,7},{7,6},{8,9},{9,8},{10,11... | collective-permute-start | bytes 3538952 | tf_op jit(solution)/shard_map/ppermute | solution.py:731
  17.4 19.4 %collective-permute-start.5 = (bf16[192,512]{1,0:T(8,128)(2,1)S(1)}, bf16[192,512]{1,0:T(8,128)(2,1)S(1)}, u32[]{:S(2)}, u32[]{:S(2)}) collective-permute-start(bf16[192,512]{1,0:T(8,128)(2,1)S(1)} %get-tuple-element.168.o1_ref), channel_id=1, source_target_pairs={{0,1},{1,0},{2,3},{3,2},{4,5},{5,4},{6,7},{7,6},{8,9},{9,8},{10,11... | collective-permute-start | bytes 589832 | tf_op jit(solution)/shard_map/ppermute | solution.py:731
  17.6 19.5 %collective-permute-start.7 = (bf16[192,512]{1,0:T(8,128)(2,1)S(1)}, bf16[192,512]{1,0:T(8,128)(2,1)S(1)}, u32[]{:S(2)}, u32[]{:S(2)}) collective-permute-start(bf16[192,512]{1,0:T(8,128)(2,1)S(1)} %get-tuple-element.168.o1_ref), channel_id=1, source_target_pairs={{0,3},{1,2},{2,1},{3,0},{4,7},{5,6},{6,5},{7,4},{8,11},{9,10},{10,... | collective-permute-start | bytes 589832 | tf_op jit(solution)/shard_map/ppermute | solution.py:731
  19.3 17.8 %collective-permute-start.6 = (bf16[192,512]{1,0:T(8,128)(2,1)S(1)}, bf16[192,512]{1,0:T(8,128)(2,1)S(1)}, u32[]{:S(2)}, u32[]{:S(2)}) collective-permute-start(bf16[192,512]{1,0:T(8,128)(2,1)S(1)} %get-tuple-element.160.a0.o0_ref), channel_id=1, source_target_pairs={{0,2},{1,3},{2,0},{3,1},{4,6},{5,7},{6,4},{7,5},{8,10},{9,11},{10,... | collective-permute-start | bytes 589832 | tf_op jit(solution)/shard_map/ppermute | solution.py:731
  34.9 14.0 %collective-permute-start.10 = (bf16[192,512]{1,0:T(8,128)(2,1)S(1)}, bf16[192,512]{1,0:T(8,128)(2,1)S(1)}, u32[]{:S(2)}, u32[]{:S(2)}) collective-permute-start(bf16[192,512]{1,0:T(8,128)(2,1)S(1)} %get-tuple-element.171.o1_ref), channel_id=1, source_target_pairs={{0,3},{1,2},{2,1},{3,0},{4,7},{5,6},{6,5},{7,4},{8,11},{9,10},{10,... | collective-permute-start | bytes 589832 | tf_op jit(solution)/shard_map/ppermute | solution.py:731
  36.3 12.6 %collective-permute-start.8 = (bf16[192,512]{1,0:T(8,128)(2,1)S(1)}, bf16[192,512]{1,0:T(8,128)(2,1)S(1)}, u32[]{:S(2)}, u32[]{:S(2)}) collective-permute-start(bf16[192,512]{1,0:T(8,128)(2,1)S(1)} %get-tuple-element.171.o1_ref), channel_id=1, source_target_pairs={{0,1},{1,0},{2,3},{3,2},{4,5},{5,4},{6,7},{7,6},{8,9},{9,8},{10,11... | collective-permute-start | bytes 589832 | tf_op jit(solution)/shard_map/ppermute | solution.py:731
  36.8 12.2 %collective-permute-start.9 = (bf16[192,512]{1,0:T(8,128)(2,1)S(1)}, bf16[192,512]{1,0:T(8,128)(2,1)S(1)}, u32[]{:S(2)}, u32[]{:S(2)}) collective-permute-start(bf16[192,512]{1,0:T(8,128)(2,1)S(1)} %get-tuple-element.166.a0.o0_ref), channel_id=1, source_target_pairs={{0,2},{1,3},{2,0},{3,1},{4,6},{5,7},{6,4},{7,5},{8,10},{9,11},{10,... | collective-permute-start | bytes 589832 | tf_op jit(solution)/shard_map/ppermute | solution.py:731
  47.2 20.5 %collective-permute-start.11 = (bf16[512,768]{1,0:T(8,128)(2,1)S(1)}, bf16[512,768]{1,0:T(8,128)(2,1)S(1)}, u32[]{:S(2)}, u32[]{:S(2)}) collective-permute-start(bf16[512,768]{1,0:T(8,128)(2,1)S(1)} %get-tuple-element.175), channel_id=1, source_target_pairs={{0,2},{1,3},{2,0},{3,1},{4,6},{5,7},{6,4},{7,5},{8,10},{9,11},{10,... | collective-permute-start | bytes 2359304 | tf_op jit(solution)/shard_map/ppermute | solution.py:731
  59.2 25.3 %collective-permute-start.12 = (bf16[512,768]{1,0:T(8,128)(2,1)S(1)}, bf16[512,768]{1,0:T(8,128)(2,1)S(1)}, u32[]{:S(2)}, u32[]{:S(2)}) collective-permute-start(bf16[512,768]{1,0:T(8,128)(2,1)S(1)} %get-tuple-element.186), channel_id=1, source_target_pairs={{0,2},{1,3},{2,0},{3,1},{4,6},{5,7},{6,4},{7,5},{8,10},{9,11},{10,... | collective-permute-start | bytes 2359304 | tf_op jit(solution)/shard_map/ppermute | solution.py:731
  80.1 20.1 %collective-permute-start.13 = (bf16[512,768]{1,0:T(8,128)(2,1)S(1)}, bf16[512,768]{1,0:T(8,128)(2,1)S(1)}, u32[]{:S(2)}, u32[]{:S(2)}) collective-permute-start(bf16[512,768]{1,0:T(8,128)(2,1)S(1)} %get-tuple-element.196), channel_id=1, source_target_pairs={{0,2},{1,3},{2,0},{3,1},{4,6},{5,7},{6,4},{7,5},{8,10},{9,11},{10,... | collective-permute-start | bytes 2359304 | tf_op jit(solution)/shard_map/ppermute | solution.py:731
  101.1 9.5 %collective-permute-start.15 = (bf16[768,768]{1,0:T(8,128)(2,1)}, bf16[768,768]{1,0:T(8,128)(2,1)S(1)}, u32[]{:S(2)}, u32[]{:S(2)}) collective-permute-start(bf16[768,768]{1,0:T(8,128)(2,1)} %get-tuple-element.209), channel_id=1, source_target_pairs={{0,1},{1,0},{2,3},{3,2},{4,5},{5,4},{6,7},{7,6},{8,9},{9,8},{10,11... | collective-permute-start | bytes 3538952 | tf_op jit(solution)/shard_map/ppermute | solution.py:731
  101.1 9.5 %collective-permute-start.14 = (bf16[768,768]{1,0:T(8,128)(2,1)}, bf16[768,768]{1,0:T(8,128)(2,1)S(1)}, u32[]{:S(2)}, u32[]{:S(2)}) collective-permute-start(bf16[768,768]{1,0:T(8,128)(2,1)} %get-tuple-element.205), channel_id=1, source_target_pairs={{0,1},{1,0},{2,3},{3,2},{4,5},{5,4},{6,7},{7,6},{8,9},{9,8},{10,11... | collective-permute-start | bytes 3538952 | tf_op jit(solution)/shard_map/ppermute | solution.py:731
  101.6 61.2 %collective-permute-start.25 = (bf16[512,768]{1,0:T(8,128)(2,1)S(1)}, bf16[512,768]{1,0:T(8,128)(2,1)S(1)}, u32[]{:S(2)}, u32[]{:S(2)}) collective-permute-start(bf16[512,768]{1,0:T(8,128)(2,1)S(1)} %copy-done.6), channel_id=1, source_target_pairs={{0,1},{1,0},{2,3},{3,2},{4,5},{5,4},{6,7},{7,6},{8,9},{9,8},{10,11... | collective-permute-start | bytes 2359304 | tf_op jit(solution)/shard_map/ppermute | solution.py:731
  101.6 61.2 %collective-permute-start.26 = (bf16[512,768]{1,0:T(8,128)(2,1)}, bf16[512,768]{1,0:T(8,128)(2,1)S(1)}, u32[]{:S(2)}, u32[]{:S(2)}) collective-permute-start(bf16[512,768]{1,0:T(8,128)(2,1)} %get-tuple-element.193.refs_2_), channel_id=1, source_target_pairs={{0,1},{1,0},{2,3},{3,2},{4,5},{5,4},{6,7},{7,6},{8,9},{9,8},{10,11... | collective-permute-start | bytes 2359304 | tf_op jit(solution)/shard_map/ppermute | solution.py:731
  108.9 22.4 %collective-permute-start.19 = (bf16[512,768]{1,0:T(8,128)(2,1)S(1)}, bf16[512,768]{1,0:T(8,128)(2,1)S(1)}, u32[]{:S(2)}, u32[]{:S(2)}) collective-permute-start(bf16[512,768]{1,0:T(8,128)(2,1)S(1)} %copy-done.14), channel_id=1, source_target_pairs={{0,2},{1,3},{2,0},{3,1},{4,6},{5,7},{6,4},{7,5},{8,10},{9,11},{10,... | collective-permute-start | bytes 2359304 | tf_op jit(solution)/shard_map/ppermute | solution.py:731
  110.6 2.8 %collective-permute-start.16 = (bf16[192,512]{1,0:T(8,128)(2,1)S(1)}, bf16[192,512]{1,0:T(8,128)(2,1)S(1)}, u32[]{:S(2)}, u32[]{:S(2)}) collective-permute-start(bf16[192,512]{1,0:T(8,128)(2,1)S(1)} %get-tuple-element.215), channel_id=1, source_target_pairs={{0,1},{1,0},{2,3},{3,2},{4,5},{5,4},{6,7},{7,6},{8,9},{9,8},{10,11... | collective-permute-start | bytes 589832 | tf_op jit(solution)/shard_map/ppermute | solution.py:731
  111.8 17.1 %collective-permute-start.17 = (bf16[384,768]{1,0:T(8,128)(2,1)S(1)}, bf16[384,768]{1,0:T(8,128)(2,1)S(1)}, u32[]{:S(2)}, u32[]{:S(2)}) collective-permute-start(bf16[384,768]{1,0:T(8,128)(2,1)S(1)} %get-tuple-element.212), channel_id=1, source_target_pairs={{0,4},{4,0},{8,12},{12,8},{16,20},{20,16},{24,28},{28,24},{1,5},{5... | collective-permute-start | bytes 1769480 | tf_op jit(solution)/shard_map/ppermute | solution.py:734
  113.4 15.4 %collective-permute-start.18 = (bf16[384,768]{1,0:T(8,128)(2,1)S(1)}, bf16[384,768]{1,0:T(8,128)(2,1)S(1)}, u32[]{:S(2)}, u32[]{:S(2)}) collective-permute-start(bf16[384,768]{1,0:T(8,128)(2,1)S(1)} %get-tuple-element.223), channel_id=1, source_target_pairs={{0,8},{4,12},{8,0},{12,4},{16,24},{20,28},{24,16},{28,20},{1,9},{5... | collective-permute-start | bytes 1769480 | tf_op jit(solution)/shard_map/ppermute | solution.py:734
  129.7 15.2 %collective-permute-start.20 = (bf16[192,768]{1,0:T(8,128)(2,1)S(1)}, bf16[192,768]{1,0:T(8,128)(2,1)S(1)}, u32[]{:S(2)}, u32[]{:S(2)}) collective-permute-start(bf16[192,768]{1,0:T(8,128)(2,1)S(1)} %get-tuple-element.226), channel_id=1, source_target_pairs={{0,8},{4,12},{8,0},{12,4},{16,24},{20,28},{24,16},{28,20},{1,9},{5... | collective-permute-start | bytes 884744 | tf_op jit(solution)/shard_map/ppermute | solution.py:734
  136.8 8.0 %collective-permute-start.21 = (bf16[192,768]{1,0:T(8,128)(2,1)S(1)}, bf16[192,768]{1,0:T(8,128)(2,1)S(1)}, u32[]{:S(2)}, u32[]{:S(2)}) collective-permute-start(bf16[192,768]{1,0:T(8,128)(2,1)S(1)} %get-tuple-element.247), channel_id=1, source_target_pairs={{0,4},{4,0},{8,12},{12,8},{16,20},{20,16},{24,28},{28,24},{1,5},{5... | collective-permute-start | bytes 884744 | tf_op jit(solution)/shard_map/ppermute | solution.py:734
  144.2 18.6 %collective-permute-start.27 = (bf16[256,768]{1,0:T(8,128)(2,1)S(1)}, bf16[256,768]{1,0:T(8,128)(2,1)S(1)}, u32[]{:S(2)}, u32[]{:S(2)}) collective-permute-start(bf16[256,768]{1,0:T(8,128)(2,1)S(1)} %get-tuple-element.271), channel_id=1, source_target_pairs={{0,1},{1,0},{2,3},{3,2},{4,5},{5,4},{6,7},{7,6},{8,9},{9,8},{10,11... | collective-permute-start | bytes 1179656 | tf_op jit(solution)/shard_map/ppermute | solution.py:731
  144.9 3.4 %collective-permute-start.22 = (bf16[192,512]{1,0:T(8,128)(2,1)S(1)}, bf16[192,512]{1,0:T(8,128)(2,1)S(1)}, u32[]{:S(2)}, u32[]{:S(2)}) collective-permute-start(bf16[192,512]{1,0:T(8,128)(2,1)S(1)} %get-tuple-element.253), channel_id=1, source_target_pairs={{0,1},{1,0},{2,3},{3,2},{4,5},{5,4},{6,7},{7,6},{8,9},{9,8},{10,11... | collective-permute-start | bytes 589832 | tf_op jit(solution)/shard_map/ppermute | solution.py:731
  145.6 16.7 %collective-permute-start.23 = (bf16[96,768]{1,0:T(8,128)(2,1)S(1)}, bf16[96,768]{1,0:T(8,128)(2,1)S(1)}, u32[]{:S(2)}, u32[]{:S(2)}) collective-permute-start(bf16[96,768]{1,0:T(8,128)(2,1)S(1)} %get-tuple-element.250), channel_id=1, source_target_pairs={{0,16},{4,20},{8,24},{12,28},{16,0},{20,4},{24,8},{28,12},{1,17},{... | collective-permute-start | bytes 442376 | tf_op jit(solution)/shard_map/ppermute | solution.py:734
  148.2 13.9 %collective-permute-start.24 = (bf16[96,768]{1,0:T(8,128)(2,1)S(1)}, bf16[96,768]{1,0:T(8,128)(2,1)S(1)}, u32[]{:S(2)}, u32[]{:S(2)}) collective-permute-start(bf16[96,768]{1,0:T(8,128)(2,1)S(1)} %get-tuple-element.261), channel_id=1, source_target_pairs={{0,16},{4,20},{8,24},{12,28},{16,0},{20,4},{24,8},{28,12},{1,17},{... | collective-permute-start | bytes 442376 | tf_op jit(solution)/shard_map/ppermute | solution.py:734
  162.1 14.7 %collective-permute-start.28 = (bf16[512,768]{1,0:T(8,128)(2,1)}, bf16[512,768]{1,0:T(8,128)(2,1)}, u32[]{:S(2)}, u32[]{:S(2)}) collective-permute-start(bf16[512,768]{1,0:T(8,128)(2,1)} %get-tuple-element.241), channel_id=1, source_target_pairs={{0,1},{1,0},{2,3},{3,2},{4,5},{5,4},{6,7},{7,6},{8,9},{9,8},{10,11... | collective-permute-start | bytes 2359304 | tf_op jit(solution)/shard_map/ppermute | solution.py:731
  168.3 17.0 %collective-permute-start.34 = (bf16[416,768]{1,0:T(8,128)(2,1)}, bf16[416,768]{1,0:T(8,128)(2,1)}, u32[]{:S(2)}, u32[]{:S(2)}) collective-permute-start(bf16[416,768]{1,0:T(8,128)(2,1)} %constant_dynamic-slice_fusion.3), channel_id=1, source_target_pairs={{0,4},{4,0},{8,12},{12,8},{16,20},{20,16},{24,28},{28,24},{1,5},{5... | collective-permute-start | bytes 1916936 | tf_op jit(solution)/shard_map/ppermute | solution.py:734
  173.7 13.7 %collective-permute-start.31 = (bf16[512,768]{1,0:T(8,128)(2,1)}, bf16[512,768]{1,0:T(8,128)(2,1)}, u32[]{:S(2)}, u32[]{:S(2)}) collective-permute-start(bf16[512,768]{1,0:T(8,128)(2,1)} %get-tuple-element.273), channel_id=1, source_target_pairs={{0,1},{1,0},{2,3},{3,2},{4,5},{5,4},{6,7},{7,6},{8,9},{9,8},{10,11... | collective-permute-start | bytes 2359304 | tf_op jit(solution)/shard_map/ppermute | solution.py:731
  173.9 13.5 %collective-permute-start.36 = (bf16[1,1,1,96,768]{4,3,2,1,0:T(8,128)(2,1)S(1)}, bf16[1,1,1,96,768]{4,3,2,1,0:T(8,128)(2,1)S(1)}, u32[]{:S(2)}, u32[]{:S(2)}) collective-permute-start(bf16[1,1,1,96,768]{4,3,2,1,0:T(8,128)(2,1)S(1)} %bitcast.27), channel_id=1, source_target_pairs={{0,16},{4,20},{8,24},{12,28},{16,0},{20,4},{24,8},{28,12},{1,17},{... | collective-permute-start | bytes 442376 | tf_op jit(solution)/shard_map/ppermute | solution.py:734
  174.7 15.5 %collective-permute-start.35 = (bf16[1,1,1,96,768]{4,3,2,1,0:T(8,128)(2,1)S(1)}, bf16[1,1,1,96,768]{4,3,2,1,0:T(8,128)(2,1)S(1)}, u32[]{:S(2)}, u32[]{:S(2)}) collective-permute-start(bf16[1,1,1,96,768]{4,3,2,1,0:T(8,128)(2,1)S(1)} %bitcast.26), channel_id=1, source_target_pairs={{0,16},{4,20},{8,24},{12,28},{16,0},{20,4},{24,8},{28,12},{1,17},{... | collective-permute-start | bytes 442376 | tf_op jit(solution)/shard_map/ppermute | solution.py:734
  179.0 23.5 %collective-permute-start.29 = (bf16[512,768]{1,0:T(8,128)(2,1)}, bf16[512,768]{1,0:T(8,128)(2,1)}, u32[]{:S(2)}, u32[]{:S(2)}) collective-permute-start(bf16[512,768]{1,0:T(8,128)(2,1)} %fusion), channel_id=1, source_target_pairs={{0,2},{1,3},{2,0},{3,1},{4,6},{5,7},{6,4},{7,5},{8,10},{9,11},{10,... | collective-permute-start | bytes 2359304 | tf_op jit(solution)/shard_map/ppermute | solution.py:731
  190.4 9.0 %collective-permute-start.41 = (bf16[1,1,2,96,768]{4,3,2,1,0:T(8,128)(2,1)S(1)}, bf16[1,1,2,96,768]{4,3,2,1,0:T(8,128)(2,1)S(1)}, u32[]{:S(2)}, u32[]{:S(2)}) collective-permute-start(bf16[1,1,2,96,768]{4,3,2,1,0:T(8,128)(2,1)S(1)} %get-tuple-element.286), channel_id=1, source_target_pairs={{0,4},{4,0},{8,12},{12,8},{16,20},{20,16},{24,28},{28,24},{1,5},{5... | collective-permute-start | bytes 884744 | tf_op jit(solution)/shard_map/ppermute | solution.py:734
  191.3 13.3 %collective-permute-start.40 = (bf16[1,1,2,96,768]{4,3,2,1,0:T(8,128)(2,1)S(1)}, bf16[1,1,2,96,768]{4,3,2,1,0:T(8,128)(2,1)S(1)}, u32[]{:S(2)}, u32[]{:S(2)}) collective-permute-start(bf16[1,1,2,96,768]{4,3,2,1,0:T(8,128)(2,1)S(1)} %get-tuple-element.284), channel_id=1, source_target_pairs={{0,8},{4,12},{8,0},{12,4},{16,24},{20,28},{24,16},{28,20},{1,9},{5... | collective-permute-start | bytes 884744 | tf_op jit(solution)/shard_map/ppermute | solution.py:734
  191.4 18.9 %collective-permute-start.37 = (bf16[104,768]{1,0:T(8,128)(2,1)S(1)}, bf16[104,768]{1,0:T(8,128)(2,1)S(1)}, u32[]{:S(2)}, u32[]{:S(2)}) collective-permute-start(bf16[104,768]{1,0:T(8,128)(2,1)S(1)} %get-tuple-element.316), channel_id=1, source_target_pairs={{0,8},{4,12},{8,0},{12,4},{16,24},{20,28},{24,16},{28,20},{1,9},{5... | collective-permute-start | bytes 479240 | tf_op jit(solution)/shard_map/ppermute | solution.py:734
  193.5 16.8 %collective-permute-start.38 = (bf16[104,768]{1,0:T(8,128)(2,1)S(1)}, bf16[104,768]{1,0:T(8,128)(2,1)S(1)}, u32[]{:S(2)}, u32[]{:S(2)}) collective-permute-start(bf16[104,768]{1,0:T(8,128)(2,1)S(1)} %get-tuple-element.315), channel_id=1, source_target_pairs={{0,16},{4,20},{8,24},{12,28},{16,0},{20,4},{24,8},{28,12},{1,17},{... | collective-permute-start | bytes 479240 | tf_op jit(solution)/shard_map/ppermute | solution.py:734
  199.4 10.9 %collective-permute-start.39 = (bf16[104,768]{1,0:T(8,128)(2,1)S(1)}, bf16[104,768]{1,0:T(8,128)(2,1)S(1)}, u32[]{:S(2)}, u32[]{:S(2)}) collective-permute-start(bf16[104,768]{1,0:T(8,128)(2,1)S(1)} %get-tuple-element.314), channel_id=1, source_target_pairs={{0,24},{4,28},{8,16},{12,20},{16,8},{20,12},{24,0},{28,4},{1,25},{... | collective-permute-start | bytes 479240 | tf_op jit(solution)/shard_map/ppermute | solution.py:734
  202.5 22.6 %collective-permute-start.32 = (bf16[512,768]{1,0:T(8,128)(2,1)S(1)}, bf16[512,768]{1,0:T(8,128)(2,1)S(1)}, u32[]{:S(2)}, u32[]{:S(2)}) collective-permute-start(bf16[512,768]{1,0:T(8,128)(2,1)S(1)} %fusion.1), channel_id=1, source_target_pairs={{0,2},{1,3},{2,0},{3,1},{4,6},{5,7},{6,4},{7,5},{8,10},{9,11},{10,... | collective-permute-start | bytes 2359304 | tf_op jit(solution)/shard_map/ppermute | solution.py:731
  210.7 7.6 %collective-permute-start.42 = (bf16[1,1,104,768]{3,2,1,0:T(8,128)(2,1)S(1)}, bf16[1,1,104,768]{3,2,1,0:T(8,128)(2,1)S(1)}, u32[]{:S(2)}, u32[]{:S(2)}) collective-permute-start(bf16[1,1,104,768]{3,2,1,0:T(8,128)(2,1)S(1)} %fusion.2), channel_id=1, source_target_pairs={{0,8},{4,12},{8,0},{12,4},{16,24},{20,28},{24,16},{28,20},{1,9},{5... | collective-permute-start | bytes 479240 | tf_op jit(solution)/shard_map/ppermute | solution.py:734
  210.7 14.4 %collective-permute-start.43 = (bf16[1,1,104,768]{3,2,1,0:T(8,128)(2,1)S(1)}, bf16[1,1,104,768]{3,2,1,0:T(8,128)(2,1)S(1)}, u32[]{:S(2)}, u32[]{:S(2)}) collective-permute-start(bf16[1,1,104,768]{3,2,1,0:T(8,128)(2,1)S(1)} %fusion.2), channel_id=1, source_target_pairs={{0,16},{4,20},{8,24},{12,28},{16,0},{20,4},{24,8},{28,12},{1,17},{... | collective-permute-start | bytes 479240 | tf_op jit(solution)/shard_map/ppermute | solution.py:734
  213.4 11.8 %collective-permute-start.44 = (bf16[1,1,104,768]{3,2,1,0:T(8,128)(2,1)S(1)}, bf16[1,1,104,768]{3,2,1,0:T(8,128)(2,1)S(1)}, u32[]{:S(2)}, u32[]{:S(2)}) collective-permute-start(bf16[1,1,104,768]{3,2,1,0:T(8,128)(2,1)S(1)} %fusion.2), channel_id=1, source_target_pairs={{0,24},{4,28},{8,16},{12,20},{16,8},{20,12},{24,0},{28,4},{1,25},{... | collective-permute-start | bytes 479240 | tf_op jit(solution)/shard_map/ppermute | solution.py:734
  215.1 13.2 %collective-permute-start.45 = (bf16[1,2,2,96,768]{4,3,2,1,0:T(8,128)(2,1)S(1)}, bf16[1,2,2,96,768]{4,3,2,1,0:T(8,128)(2,1)S(1)}, u32[]{:S(2)}, u32[]{:S(2)}) collective-permute-start(bf16[1,2,2,96,768]{4,3,2,1,0:T(8,128)(2,1)S(1)} %pad_maximum_fusion.3), channel_id=1, source_target_pairs={{0,4},{4,0},{8,12},{12,8},{16,20},{20,16},{24,28},{28,24},{1,5},{5... | collective-permute-start | bytes 1769480 | tf_op jit(solution)/shard_map/ppermute | solution.py:734
  218.3 17.1 %collective-permute-start.30 = (bf16[512,768]{1,0:T(8,128)(2,1)S(1)}, bf16[512,768]{1,0:T(8,128)(2,1)S(1)}, u32[]{:S(2)}, u32[]{:S(2)}) collective-permute-start(bf16[512,768]{1,0:T(8,128)(2,1)S(1)} %add_convert_fusion.1.refs_0_), channel_id=1, source_target_pairs={{0,1},{1,0},{2,3},{3,2},{4,5},{5,4},{6,7},{7,6},{8,9},{9,8},{10,11... | collective-permute-start | bytes 2359304 | tf_op jit(solution)/shard_map/ppermute | solution.py:731
  226.7 8.6 %collective-permute-start.33 = (bf16[512,768]{1,0:T(8,128)(2,1)S(1)}, bf16[512,768]{1,0:T(8,128)(2,1)S(1)}, u32[]{:S(2)}, u32[]{:S(2)}) collective-permute-start(bf16[512,768]{1,0:T(8,128)(2,1)S(1)} %add_convert_fusion.refs_2_), channel_id=1, source_target_pairs={{0,1},{1,0},{2,3},{3,2},{4,5},{5,4},{6,7},{7,6},{8,9},{9,8},{10,11... | collective-permute-start | bytes 2359304 | tf_op jit(solution)/shard_map/ppermute | solution.py:731
  228.5 15.5 %collective-permute-start.46 = (bf16[1,4,104,768]{3,2,1,0:T(8,128)(2,1)S(1)}, bf16[1,4,104,768]{3,2,1,0:T(8,128)(2,1)S(1)}, u32[]{:S(2)}, u32[]{:S(2)}) collective-permute-start(bf16[1,4,104,768]{3,2,1,0:T(8,128)(2,1)S(1)} %constant_dynamic-update-slice_fusion), channel_id=1, source_target_pairs={{0,4},{4,0},{8,12},{12,8},{16,20},{20,16},{24,28},{28,24},{1,5},{5... | collective-permute-start | bytes 1916936 | tf_op jit(solution)/shard_map/ppermute | solution.py:734
  232.9 14.8 %collective-permute-start.47 = (bf16[1,2,2,96,768]{4,3,2,1,0:T(8,128)(2,1)S(1)}, bf16[1,2,2,96,768]{4,3,2,1,0:T(8,128)(2,1)S(1)}, u32[]{:S(2)}, u32[]{:S(2)}) collective-permute-start(bf16[1,2,2,96,768]{4,3,2,1,0:T(8,128)(2,1)S(1)} %pad_maximum_fusion.4), channel_id=1, source_target_pairs={{0,8},{4,12},{8,0},{12,4},{16,24},{20,28},{24,16},{28,20},{1,9},{5... | collective-permute-start | bytes 1769480 | tf_op jit(solution)/shard_map/ppermute | solution.py:734
  (49 other events, 350.5 us)
